TPU v7x, 32 devices: a whole 2x2x4 slice. The times are simulated.
32 devices in a mesh: groups: 2 (over x), dp: 8 (over z, y), tensor: 2 (over core).
Axes of the slice: x: 2, y: 2, z: 4, core: 2. Of those that a mesh axis runs over, the one named last changes fastest.
Arguments:
- tokens: bfloat16 [14336, 8192], P(('groups', 'dp'), 'tensor'), parts along dimension 0, may hold values from -6 to 6
- base_weight: bfloat16 [8192, 1024], P('tensor'), may hold values from -0.0625 to 0.0625
- adapter_down: bfloat16 [32, 8192, 16], P('dp', 'tensor'), may hold values from -0.0625 to 0.0625
- adapter_up: bfloat16 [32, 16, 1024], P('dp', None, 'tensor'), may hold values from -0.75 to 0.75
- out_cotangent: bfloat16 [14336, 1024], P(('groups', 'dp'), 'tensor'), parts along dimension 0, may hold values from -6 to 6
- block_tenant: int32 [112], P(('groups', 'dp')), parts along dimension 0, may hold values from 0 to 31, as said below
- block_valid: int32 [112], P(('groups', 'dp')), parts along dimension 0, may hold values from 1 to 128, as said below
- tenant_slot: int32 [64], P('groups'), parts along dimension 0, may hold values from 0 to 31, as said below
Outputs:
- projected: bfloat16 [14336, 1024], P(('groups', 'dp'), 'tensor'), parts along dimension 0
- grad_tokens: bfloat16 [14336, 8192], P(('groups', 'dp'), 'tensor'), parts along dimension 0
- grad_down: float32 [64, 8192, 16], P(('groups', 'dp'), 'tensor'), parts along dimension 0
- grad_up: float32 [64, 16, 1024], P(('groups', 'dp'), None, 'tensor'), parts along dimension 0
There are 2 independent parts, one for each index of `groups`. A program takes and returns all parts, laid end to end along the dimension named above; an argument that names none is the same for every part. Nothing has to cross between parts.
Inputs may be any that keep to these rules, and one draw needn't show every extreme that they name: `tenant_slot`: a permutation; slot s is held by dp index s // 4. `block_tenant`: among the blocks of one dp index, at most 2 name tenants whose slots are held by one same dp index; some dp index reaches 2 in every draw. `block_valid`: the valid tokens of a block come first in it.
All inputs are finite; a program needn't handle non-finite values.
Results may differ from a plain program's by a relative error of at most 0.0045.
Values may be sent and summed in bfloat16 or wider, within the bound.
No kernel may reach another device: no remote copies, remote signals or barrier semaphores. Data moves between devices by JAX's collectives and lax.ppermute only.
A program may use at most 192 MiB of HBM per device.

v0:
```python
import jax
import jax.numpy as jnp
from jax import lax
from jax.sharding import PartitionSpec as P

TENANT_BLOCK = 128


adapter_scale = 2.0


def on_device(
    tokens,
    base_weight,
    adapter_down,
    adapter_up,
    out_cotangent,
    block_tenant,
    block_valid,
    tenant_slot,
):
    float_single = jnp.float32
    bfloat_half = jnp.bfloat16
    highest = lax.Precision.HIGHEST
    token_blocks = block_tenant.shape[0]
    token_rows = tokens.shape[0]
    half_width = tokens.shape[1]
    local_output = out_cotangent.shape[1]
    tenants = tenant_slot.shape[0]
    tenant_match = block_tenant[:, None] == jnp.arange(tenants, dtype=jnp.int32)[None, :]
    slots_used = jnp.sum(jnp.where(tenant_match, tenant_slot[None, :], 0), axis=1)
    validity_mask = (
        jnp.arange(TENANT_BLOCK, dtype=jnp.int32)[None, :] < block_valid[:, None]
    ).astype(float_single)
    x_blocks = tokens.reshape(token_blocks, TENANT_BLOCK, half_width)
    every_down, every_up = (
        lax.all_gather(adapter_down, "dp", axis=0, tiled=True),
        lax.all_gather(adapter_up, "dp", axis=0, tiled=True),
    )
    block_down = jnp.take(every_down, slots_used, axis=0)
    block_up_weight = jnp.take(every_up, slots_used, axis=0)
    base_part = jnp.dot(tokens, base_weight, preferred_element_type=float_single)
    shrink_part = jnp.einsum(
        "btd,bdr->btr", x_blocks, block_down, preferred_element_type=float_single
    )
    frozen_output_local = lax.psum_scatter(base_part, "tensor", scatter_dimension=1, tiled=True)
    narrowed_rows = lax.psum(shrink_part, "tensor").astype(bfloat_half)
    widened_rows = jnp.einsum(
        "btr,brk->btk", narrowed_rows, block_up_weight, preferred_element_type=float_single
    )
    projected = (
        (
            validity_mask[:, :, None]
            * (
                frozen_output_local.reshape(token_blocks, TENANT_BLOCK, local_output)
                + adapter_scale * widened_rows
            )
        )
        .astype(bfloat_half)
        .reshape(token_rows, local_output)
    )
    output_gradient = out_cotangent.reshape(
        token_blocks, TENANT_BLOCK, local_output
    ) * validity_mask[:, :, None].astype(bfloat_half)
    backward_piece = jnp.einsum(
        "oml,opl->omp", output_gradient, block_up_weight, preferred_element_type=float_single
    )
    backward_narrowed = (adapter_scale * lax.psum(backward_piece, "tensor")).astype(bfloat_half)
    flat_grad = output_gradient.reshape(token_rows, local_output)
    through = lax.dot_general(
        lax.all_gather(flat_grad, "tensor", axis=1, tiled=True),
        base_weight,
        (((1,), (1,)), ((), ())),
        preferred_element_type=float_single,
    )
    adapter_back = jnp.einsum(
        "btr,bdr->btd", backward_narrowed, block_down, preferred_element_type=float_single
    )
    grad_tokens = (
        (through.reshape(token_blocks, TENANT_BLOCK, half_width) + adapter_back)
        .astype(bfloat_half)
        .reshape(token_rows, half_width)
    )
    down_blocks = jnp.einsum(
        "btd,btr->bdr", x_blocks, backward_narrowed, preferred_element_type=float_single
    )
    up_weight_blocks = adapter_scale * jnp.einsum(
        "qsh,qsc->qhc", narrowed_rows, output_gradient, preferred_element_type=float_single
    )
    slot_match = (slots_used[:, None] == jnp.arange(tenants, dtype=jnp.int32)[None, :]).astype(
        float_single
    )
    dense_down = jnp.einsum("bs,bdr->sdr", slot_match, down_blocks, precision=highest)
    dense_up = jnp.einsum("bs,brk->srk", slot_match, up_weight_blocks, precision=highest)
    grad_down, grad_up = (
        lax.psum_scatter(dense_down, "dp", scatter_dimension=0, tiled=True),
        lax.psum_scatter(dense_up, "dp", scatter_dimension=0, tiled=True),
    )
    return (projected, grad_tokens, grad_down, grad_up)


def solution(mesh):
    in_specs = (
        P(("groups", "dp"), "tensor"),
        P("tensor", None),
        P("dp", "tensor", None),
        P("dp", None, "tensor"),
        P(("groups", "dp"), "tensor"),
        P(("groups", "dp")),
        P(("groups", "dp")),
        P("groups"),
    )
    out_specs = (
        P(("groups", "dp"), "tensor"),
        P(("groups", "dp"), "tensor"),
        P(("groups", "dp"), "tensor", None),
        P(("groups", "dp"), None, "tensor"),
    )
    return jax.shard_map(
        on_device, mesh=mesh, in_specs=in_specs, out_specs=out_specs, check_vma=False
    )
```

profile of v0, /device:TPU:0, one launch (start us, length us, event | category | flops | bytes accessed | tf_op | source)
XLA Modules:
  0.0 344.2 jit_solution(4590639244834750476)
XLA Ops:
  7.2 0.0 all-gather.3.cloned.1.call-start
  7.2 0.7 all-gather.3.cloned.1.call-update
  7.9 0.0 all-gather.5.cloned.1.call-start
  7.9 0.7 fusion.19
  8.7 2.3 broadcast_multiply_fusion
  11.0 0.0 all-gather.5.cloned.1.call-update
  11.0 0.0 reduce-scatter.4.cloned.1.call-start
  11.1 13.6 %fusion.26 = f32[896,1024]{1,0:T(8,128)} fusion(bf16[896,4096]{1,0:T(8,128)(2,1)} %param.8, bf16[4096,1024]{1,0:T(8,128)(2,1)} %param.9), kind=kOutput, calls=%fused_computation.43 | convolution fusion | flops 7516192768 | bytes 19398656 | tf_op jit(solution)/shard_map/dot_general | solution.py:42
  24.6 0.0 reduce-scatter.4.cloned.1.call-update
  24.7 0.0 reduce-scatter.8.cloned.1.call-start
  24.7 0.2 select_reduce_fusion
  25.0 34.8 %all_gather.10 = bf16[32,16,512]{2,1,0:T(8,128)(2,1)S(1)} all-gather(bf16[4,16,512]{2,1,0:T(8,128)(2,1)S(1)} %copy-done.1), channel_id=1, replica_groups=mesh['groups'=2,'dp'=8,'tensor'=2] {'dp'}, dimensions={0}, use_global_device_ids=true | all-gather | bytes 589824 | tf_op jit(solution)/shard_map/all_gather | solution.py:38
  59.7 0.6 gather_fusion.1
  60.3 0.4 fusion.3
  60.7 29.4 %all-gather.3.cloned.1.call-done = bf16[32,4096,16]{1,2,0:T(8,128)(2,1)} async-done(((bf16[4,4096,16]{1,2,0:T(8,128)(2,1)}), bf16[32,4096,16]{1,2,0:T(8,128)(2,1)}) %all-gather.3.cloned.1.call-update) | async-done | bytes 4194320 | tf_op jit(solution)/shard_map/all_gather | solution.py:37
  90.2 2.8 gather_fusion
  93.0 5.1 %convolution_bitcast_fusion.1 = f32[7,128,16]{1,2,0:T(8,128)S(1)} fusion(bf16[7,128,4096]{2,1,0:T(8,128)(2,1)} %bitcast.28, bf16[7,4096,16]{1,2,0:T(8,128)(2,1)S(1)} %gather_fusion, pred[7]{0:T(512)(128)(4,1)S(1)} %compare_and_fusion), kind=kOutput, calls=%fused_computation.8 | convolution fusion | flops 117899264 | bytes 8314887 | tf_op jit(solution)/shard_map/btd,bdr->btr/dot_general | solution.py:43
  98.1 3.9 %all-reduce.2 = (bf16[7,128,16]{1,2,0:T(8,128)(2,1)S(1)}, f32[7,128,16]{1,2,0:T(8,128)S(1)}) all-reduce(f32[7,128,16]{1,2,0:T(8,128)S(1)} %convolution_bitcast_fusion.1, f32[7,128,16]{1,2,0:T(8,128)S(1)} %fusion.3), channel_id=1, replica_groups=mesh['groups'=2,'dp'=8,'tensor'=2] {'tensor'}, use_global_device_ids=true, to_apply=%region_2.3 | all-reduce | flops 28672 | bytes 200704 | tf_op jit(solution)/shard_map/psum | solution.py:47
  101.9 0.3 convolution_multiply_fusion
  102.2 0.7 fusion.7
  103.0 1.6 copy.19
  104.6 0.0 reduce-scatter.8.cloned.1.call-update
  104.6 0.2 reduce-scatter.6.cloned.1.call-start
  104.8 4.2 %convolution_bitcast_fusion = f32[7,4096,16]{1,2,0:T(8,128)S(1)} fusion(bf16[7,128,4096]{2,1,0:T(8,128)(2,1)} %bitcast.29, f32[7,128,16]{1,2,0:T(8,128)S(1)} %get-tuple-element.9), kind=kOutput, calls=%fused_computation.3 | convolution fusion | flops 117469184 | bytes 9232384 | tf_op jit(solution)/shard_map/btd,btr->bdr/dot_general | solution.py:84
  109.0 4.2 %fusion = f32[32,4096,16]{1,0,2:T(8,128)S(1)} fusion(f32[7,4096,16]{1,2,0:T(8,128)S(1)} %convolution_bitcast_fusion, s32[7]{0:T(128)S(1)} %select_reduce_fusion), kind=kOutput, calls=%fused_computation.4 | convolution fusion | flops 176160992 | bytes 10223644 | tf_op jit(solution)/shard_map/bs,bdr->sdr/dot_general | solution.py:93
  113.2 8.1 %copy.17 = f32[32,4096,16]{1,2,0:T(8,128)} copy(f32[32,4096,16]{1,0,2:T(8,128)S(1)} %fusion) | data formatting | bytes 16777216 | tf_op jit(solution)/shard_map/bs,bdr->sdr/dot_general | solution.py:93
  121.3 0.0 all-gather.5.cloned.1.call-done
  121.3 14.9 %fusion.27 = f32[896,4096]{1,0:T(8,128)} fusion(bf16[896,1024]{1,0:T(8,128)(2,1)} %all-gather.5.cloned.1.call-done, bf16[4096,1024]{1,0:T(8,128)(2,1)} %param.9), kind=kOutput, calls=%fused_computation.44 | convolution fusion | flops 7516192768 | bytes 24903680 | tf_op jit(solution)/shard_map/dot_general | solution.py:70
  136.3 2.9 multiply_convert_fusion
  139.2 10.5 %add_convert_fusion = bf16[7,128,4096]{2,1,0:T(8,128)(2,1)} fusion(f32[7,128,4096]{2,1,0:T(8,128)} %bitcast.30, bf16[7,4096,16]{1,2,0:T(8,128)(2,1)S(1)} %gather_fusion, pred[7]{0:T(512)(128)(4,1)S(1)} %compare_and_fusion, f32[7,128,16]{1,2,0:T(8,128)S(1)} %get-tuple-element.9), kind=kOutput, calls=%fused_computation.2 | convolution fusion | flops 125267968 | bytes 22994952 | tf_op jit(solution)/shard_map/btr,bdr->btd/dot_general | solution.py:76
  149.7 35.9 %reduce-scatter.8.cloned.1.call-done = f32[4,16,512]{2,1,0:T(8,128)} async-done(((f32[32,16,512]{2,1,0:T(8,128)}), f32[4,16,512]{2,1,0:T(8,128)}) %reduce-scatter.8.cloned.1.call-update) | async-done | bytes 131088 | tf_op jit(solution)/shard_map/reduce_scatter | solution.py:97
  185.6 152.1 %reduce-scatter.6.cloned.1.call-done = f32[4,4096,16]{1,2,0:T(8,128)} async-done(((f32[32,4096,16]{1,2,0:T(8,128)}), f32[4,4096,16]{1,2,0:T(8,128)}) %reduce-scatter.6.cloned.1.call-update) | async-done | bytes 1048592 | tf_op jit(solution)/shard_map/reduce_scatter | solution.py:96
  (13 shorter events, 0.1 us)
Async XLA Ops:
  7.2 83.0 %all-gather.3.cloned.1.call-start = ((), (), s32[]{:S(2)}) async-start(), calls=%async_computation.4 | async-start | bytes 4718592 | tf_op jit(solution)/shard_map/all_gather | solution.py:37
  7.9 113.4 %all-gather.5.cloned.1.call-start = ((), (), s32[]{:S(2)}) async-start(), calls=%async_computation.5 | async-start | bytes 2752512 | tf_op jit(solution)/shard_map/all_gather | solution.py:71
  11.0 13.7 %copy-start.2 = (s32[32]{0:T(128)S(1)}, s32[32]{0:T(128)}, u32[]{:S(2)}) copy-start(s32[32]{0:T(128)} %param.15) | copy-start | bytes 388
  11.0 13.7 %copy-start.3 = (s32[7]{0:T(128)S(1)}, s32[7]{0:T(128)}, u32[]{:S(2)}) copy-start(s32[7]{0:T(128)} %param.13) | copy-start | bytes 88
  11.0 13.9 %copy-start.1 = (bf16[4,16,512]{2,1,0:T(8,128)(2,1)S(1)}, bf16[4,16,512]{2,1,0:T(8,128)(2,1)}, u32[]{:S(2)}) copy-start(bf16[4,16,512]{2,1,0:T(8,128)(2,1)} %param.11) | copy-start | bytes 196612
  11.0 49.3 %copy-start = (bf16[896,512]{1,0:T(8,128)(2,1)S(1)}, bf16[896,512]{1,0:T(8,128)(2,1)}, u32[]{:S(2)}) copy-start(bf16[896,512]{1,0:T(8,128)(2,1)} %param.12) | copy-start | bytes 2752516
  11.0 125.2 %reduce-scatter.4.cloned.1.call-start = ((), (), s32[]{:S(2)}) async-start(), calls=%async_computation.3 | async-start | bytes 5505024 | tf_op jit(solution)/shard_map/reduce_scatter | solution.py:46
  24.7 160.9 %reduce-scatter.8.cloned.1.call-start = ((), (), s32[]{:S(2)}) async-start(), calls=%async_computation.7 | async-start | bytes 1179648 | tf_op jit(solution)/shard_map/reduce_scatter | solution.py:97
  104.6 233.1 %reduce-scatter.6.cloned.1.call-start = ((), (), s32[]{:S(2)}) async-start(), calls=%async_computation.6 | async-start | bytes 9437184 | tf_op jit(solution)/shard_map/reduce_scatter | solution.py:96
Sparse Core Ops, SparseCore 0:
  10.1 79.9 all-gather.2
  92.3 9.0 all-gather.4
  104.2 12.6 reduce-scatter.3
  121.1 64.5 reduce-scatter.7
  189.7 147.9 reduce-scatter.5
where the time goes:
time: 345 us; the launch traced here: 344 us
  waiting for transfers between devices  218 us (63%)
  matrix products  56.8 us (16%)
  blocking collectives  38.6 us (11%)
  between operations  13.9 us (4%)
  local copies, waits for them, and re-layouts  13.1 us (4%)
    reduce_scatter x1, waiting for transfers between devices, on_device(): lax.psum_scatter(dense_down, 'dp', scatter_dimension=0, tiled=True)  152 us
    reduce_scatter x1, waiting for transfers between devices, on_device(): lax.psum_scatter(dense_up, 'dp', scatter_dimension=0, tiled=True)  35.9 us
    all_gather x1, blocking collectives, on_device(): lax.all_gather(adapter_up, 'dp', axis=0, tiled=True)  34.8 us
    all_gather x1, waiting for transfers between devices, on_device(): lax.all_gather(adapter_down, 'dp', axis=0, tiled=True)  29.4 us
    dot_general x1, matrix products, on_device(): lax.dot_general(lax.all_gather(flat_grad, 'tensor', axis=1, tiled=True),...  14.9 us
    dot_general x1, matrix products, on_device(): jnp.dot(tokens, base_weight, preferred_element_type=float_single)  13.6 us
    dot_general x1, matrix products, on_device(): jnp.einsum('btr,bdr->btd', backward_narrowed, block_down, preferred_eleme...  10.5 us
    dot_general x1, local copies, waits for them, and re-layouts, on_device(): jnp.einsum('bs,bdr->sdr', slot_match, down_blocks, precision=highest)  8.14 us
  transfers between devices with their start and end apart: 5, of which 3 were waited for; matrix products, arithmetic and copies ran while one was open for 21% of the time, Pallas kernels for 0%

commit v1 on v0

v1 whole, which is shorter than its diff:
```python
import jax
import jax.numpy as jnp
from jax import lax
from jax.sharding import PartitionSpec as P

TENANT_BLOCK = 128
CAP = 2
NEAR = 4

adapter_scale = 2.0


def _swap(x, axis):
    return lax.ppermute(x, axis, [(0, 1), (1, 0)])


def _xor(x, n, k):
    return lax.ppermute(x, "dp", [(i, i ^ k) for i in range(n)])


def _owners(slots, ten_dev):
    owner = slots // ten_dev
    n = slots.shape[0]
    earlier = jnp.arange(n)[None, :] < jnp.arange(n)[:, None]
    rank = jnp.sum((owner[None, :] == owner[:, None]) & earlier, axis=1)
    return owner, rank.astype(jnp.int32)


def on_device(
    n_groups,
    n_dp,
    tokens,
    base_weight,
    adapter_down,
    adapter_up,
    out_cotangent,
    block_tenant,
    block_valid,
    tenant_slot,
):
    f32 = jnp.float32
    bf16 = jnp.bfloat16
    i32 = jnp.int32
    nb = block_tenant.shape[0]
    rows, width = tokens.shape
    cols = out_cotangent.shape[1]
    tenants = tenant_slot.shape[0]
    ten_dev, _, rank_dim = adapter_down.shape
    n_far = n_dp // NEAR
    me = lax.axis_index("dp")
    core = lax.axis_index("tensor")
    group = lax.axis_index("groups")

    tenant_match = block_tenant[:, None] == jnp.arange(tenants, dtype=i32)[None, :]
    slots = jnp.sum(jnp.where(tenant_match, tenant_slot[None, :], 0), axis=1).astype(i32)
    valid = jnp.arange(TENANT_BLOCK, dtype=i32)[None, :] < block_valid[:, None]
    valid_rows = valid.reshape(rows, 1)

    grad_out = out_cotangent * valid_rows.astype(bf16)
    grad_other = _swap(grad_out, "tensor")

    down_t = jnp.swapaxes(adapter_down, 1, 2)

    ups = [adapter_up] + [_xor(adapter_up, n_dp, NEAR * j) for j in range(1, n_far)]
    mine = jnp.concatenate(ups, axis=0).reshape(n_far * ten_dev * rank_dim, cols)
    tag = jnp.zeros((16, cols), bf16).at[0, :nb].set(slots.astype(bf16))
    packet = jnp.concatenate([mine, tag], axis=0)
    packets = [packet] + [_xor(packet, n_dp, k) for k in range(1, NEAR)]
    near_slots = [slots] + [p[-16, :nb].astype(i32) for p in packets[1:]]
    all_up = jnp.stack([p[:-16] for p in packets]).reshape(
        NEAR, n_far, ten_dev, rank_dim, cols
    )

    def up_row(s):
        rel = (s // ten_dev) ^ me
        return ((rel % NEAR) * n_far + rel // NEAR) * ten_dev + s % ten_dev

    block_up = jnp.take(
        all_up.reshape(n_dp * ten_dev, rank_dim, cols), up_row(slots), axis=0
    )

    if n_groups == 2 and n_dp == 8:
        quarter = width // 4
        mine_q = group * 2 + me % 2
        own = lax.dynamic_slice_in_dim(down_t, mine_q * quarter, quarter, axis=2)
        to_y = lax.dynamic_slice_in_dim(down_t, (mine_q ^ 1) * quarter, quarter, axis=2)
        shard = jnp.concatenate([own, _xor(to_y, n_dp, 1)], axis=0)
        pair = jnp.concatenate([shard, _xor(shard, n_dp, 4)], axis=0)
        every = jnp.concatenate([pair, _xor(pair, n_dp, 2)], axis=0)

        def down_row(s):
            rel = (s // ten_dev) ^ me
            z = rel // 2
            place = (z % 2) * 4 + (z // 2) * 2 + rel % 2
            return place * ten_dev + s % ten_dev

        both = jnp.stack([slots, near_slots[1]])
        both_x = _swap(both, "groups")
        need_y = jnp.take(every, down_row(near_slots[1]), axis=0)
        need_x = jnp.take(every, down_row(both_x[0]), axis=0)
        need_d = jnp.take(every, down_row(both_x[1]), axis=0)
        got_0 = jnp.take(every, down_row(slots), axis=0)
        got_y = _xor(need_y, n_dp, 1)
        got_x = _swap(need_x, "groups")
        got_d = lax.ppermute(
            need_d,
            ("groups", "dp"),
            [(g * n_dp + d, (1 - g) * n_dp + (d ^ 1)) for g in range(2) for d in range(n_dp)],
        )
        parts = jnp.stack([got_0, got_y, got_x, got_d])
        parts = jnp.take(parts, jnp.arange(4) ^ mine_q, axis=0)
        block_down = jnp.transpose(parts, (1, 2, 0, 3)).reshape(nb * rank_dim, width)
    else:
        every = lax.all_gather(down_t, "dp", axis=0, tiled=True)
        block_down = jnp.take(every, slots, axis=0).reshape(nb * rank_dim, width)

    same_block = (
        jnp.arange(nb)[:, None, None, None] == jnp.arange(nb)[None, None, :, None]
    )

    def pick(full):
        x = full.reshape(nb, TENANT_BLOCK, nb, rank_dim)
        return jnp.sum(jnp.where(same_block, x, 0.0), axis=2)

    def spread(x):
        y = jnp.where(same_block, x[:, :, None, :], jnp.zeros((), x.dtype))
        return y.reshape(rows, nb * rank_dim)

    up_2d = block_up.reshape(nb * rank_dim, cols)
    back_part = pick(
        lax.dot_general(grad_out, up_2d, (((1,), (1,)), ((), ())), preferred_element_type=f32)
    )
    back_shrink = (adapter_scale * (back_part + _swap(back_part, "tensor"))).astype(bf16)

    owner, order = _owners(slots, ten_dev)
    rel = owner ^ me
    place = ((rel % NEAR) * n_far + rel // NEAR) * CAP + order
    sel = (place[None, :] == jnp.arange(n_dp * CAP)[:, None]).astype(bf16)
    back_t = jnp.transpose(back_shrink, (2, 0, 1))
    packed_back = (sel[:, None, :, None] * back_t[None]).reshape(n_dp * CAP * rank_dim, rows)
    near_rows = n_far * CAP * rank_dim
    sends = lax.dot_general(
        packed_back, tokens, (((1,), (0,)), ((), ())), preferred_element_type=f32
    ).astype(bf16)

    hot = []
    for k in range(NEAR):
        o, r = _owners(near_slots[k], ten_dev)
        hit = (
            (o[None, None, :] == (me ^ (NEAR * jnp.arange(n_far)))[:, None, None])
            & (r[None, None, :] == jnp.arange(CAP)[None, :, None])
        )
        local = jnp.sum(jnp.where(hit, near_slots[k][None, None, :] % ten_dev, 0), axis=2)
        hot.append(local)
    hot = jnp.stack(hot, axis=1).reshape(n_far, NEAR * CAP)
    one_hot = (hot[:, None, :] == jnp.arange(ten_dev)[None, :, None]).astype(bf16)
    eye = jnp.eye(rank_dim, dtype=bf16)
    summing = (one_hot[:, :, None, :, None] * eye[None, None, :, None, :]).reshape(
        n_far, ten_dev * rank_dim, NEAR * CAP * rank_dim
    )

    def scatter(sends):
        wide = sends.shape[1]
        packs = sends.reshape(NEAR, near_rows, wide)
        got = [packs[0]] + [_xor(packs[k], n_dp, k) for k in range(1, NEAR)]
        got = [g.reshape(n_far, CAP * rank_dim, wide) for g in got]

        def dense(j):
            stacked = jnp.concatenate([g[j] for g in got], axis=0)
            return jnp.dot(summing[j], stacked, preferred_element_type=f32)

        arrived = [_xor(dense(j).astype(bf16), n_dp, NEAR * j) for j in range(1, n_far)]
        total = dense(0)
        for a in arrived:
            total = total + a.astype(f32)
        return total.reshape(ten_dev, rank_dim, wide)

    grad_down = jnp.swapaxes(scatter(sends), 1, 2)

    w_own = lax.dynamic_slice_in_dim(base_weight, core * cols, cols, axis=1)
    w_other = lax.dynamic_slice_in_dim(base_weight, (1 - core) * cols, cols, axis=1)
    base_other = jnp.dot(tokens, w_other, preferred_element_type=f32).astype(bf16)
    base_own = jnp.dot(tokens, w_own, preferred_element_type=f32)
    base = base_own + _swap(base_other, "tensor").astype(f32)

    shrink_part = pick(
        lax.dot_general(tokens, block_down, (((1,), (1,)), ((), ())), preferred_element_type=f32)
    )
    shrink = (shrink_part + _swap(shrink_part, "tensor")).astype(bf16)
    widened = jnp.dot(spread(shrink), up_2d, preferred_element_type=f32)
    projected = jnp.where(valid_rows, base + adapter_scale * widened, 0.0).astype(bf16)

    shrink_t = jnp.transpose(shrink, (2, 0, 1))
    packed_shrink = (sel[:, None, :, None] * shrink_t[None]).reshape(
        n_dp * CAP * rank_dim, rows
    )
    up_sends = (
        adapter_scale * jnp.dot(packed_shrink, grad_out, preferred_element_type=f32)
    ).astype(bf16)
    grad_up = scatter(up_sends)

    through = lax.dot_general(
        grad_out, w_own, (((1,), (1,)), ((), ())), preferred_element_type=f32
    ) + lax.dot_general(
        grad_other, w_other, (((1,), (1,)), ((), ())), preferred_element_type=f32
    )
    grad_tokens = (
        through + jnp.dot(spread(back_shrink), block_down, preferred_element_type=f32)
    ).astype(bf16)
    return projected, grad_tokens, grad_down, grad_up


def solution(mesh):
    n_groups, n_dp = mesh.shape["groups"], mesh.shape["dp"]
    in_specs = (
        P(("groups", "dp"), "tensor"),
        P("tensor", None),
        P("dp", "tensor", None),
        P("dp", None, "tensor"),
        P(("groups", "dp"), "tensor"),
        P(("groups", "dp")),
        P(("groups", "dp")),
        P("groups"),
    )
    out_specs = (
        P(("groups", "dp"), "tensor"),
        P(("groups", "dp"), "tensor"),
        P(("groups", "dp"), "tensor", None),
        P(("groups", "dp"), None, "tensor"),
    )

    def run(*args):
        return on_device(n_groups, n_dp, *args)

    return jax.shard_map(
        run, mesh=mesh, in_specs=in_specs, out_specs=out_specs, check_vma=False
    )
```

time: 345 us -> 188 us (0.54)
  waiting for transfers between devices: 218 us -> 61.3 us
  blocking collectives: 38.6 us -> 0 us
  starting transfers between devices: 0.38 us -> 23.6 us
  matrix products: 56.8 us -> 76.1 us
  between operations: 13.9 us -> 1.17 us
  local copies, waits for them, and re-layouts: 13.1 us -> 17.9 us
  other arithmetic: 3.22 us -> 7.47 us
    reduce_scatter x3 -> x0, waiting for transfers between devices: 188 us -> none  [the longest x1 152 us: on_device(): lax.psum_scatter(dense_down, 'dp', scatter_dimension=0, tiled=True)]
    ppermute x0 -> x23, waiting for transfers between devices: none -> 61.3 us  [the longest x16 52.7 us: _xor(): return lax.ppermute(x, 'dp', [(i, i ^ k) for i in range(n)])]
    all_gather x1 -> x0, blocking collectives: 34.8 us -> none  [on_device(): lax.all_gather(adapter_up, 'dp', axis=0, tiled=True)]
    all_gather x2 -> x0, waiting for transfers between devices: 29.5 us -> none  [the longest x1 29.4 us: on_device(): lax.all_gather(adapter_down, 'dp', axis=0, tiled=True)]
    ppermute x0 -> x23, starting transfers between devices: none -> 23.6 us  [the longest x16 17.9 us: _xor(): return lax.ppermute(x, 'dp', [(i, i ^ k) for i in range(n)])]
    dot_general x10 -> x14, matrix products: 56.8 us -> 76.1 us  [the longest x1 15.8 us: on_device(): lax.dot_general(grad_other, w_other, (((1,), (1,)), ((), ())), preferred_...]
    slice x0 -> x11, local copies, waits for them, and re-layouts: none -> 9.77 us  [the longest x8 7.85 us: dense(): stacked = jnp.concatenate([g[j] for g in got], axis=0)]
    dot_general x2 -> x0, local copies, waits for them, and re-layouts: 9.74 us -> none  [the longest x1 8.14 us: on_device(): jnp.einsum('bs,bdr->sdr', slot_match, down_blocks, precision=highest)]
  transfers between devices with their start and end apart: 5 -> 23, of which waited for: 3 -> 10; matrix products, arithmetic and copies ran while one was open for 21% -> 53% of each run, Pallas kernels for 0% -> 0%
where the time goes in v1:
time: 188 us; the launch traced here: 187 us
  matrix products  76.1 us (40%)
  waiting for transfers between devices  61.3 us (33%)
  starting transfers between devices  23.6 us (13%)
  local copies, waits for them, and re-layouts  17.9 us (10%)
  other arithmetic  7.47 us (4%)
    ppermute x16, waiting for transfers between devices, _xor(): return lax.ppermute(x, 'dp', [(i, i ^ k) for i in range(n)])  52.7 us
    ppermute x16, starting transfers between devices, _xor(): return lax.ppermute(x, 'dp', [(i, i ^ k) for i in range(n)])  17.9 us
    dot_general x1, matrix products, on_device(): lax.dot_general(grad_other, w_other, (((1,), (1,)), ((), ())), preferred_...  15.8 us
    dot_general x1, matrix products, on_device(): lax.dot_general(grad_out, w_own, (((1,), (1,)), ((), ())), preferred_elem...  11.7 us
    dot_general x1, matrix products, on_device(): jnp.dot(tokens, w_other, preferred_element_type=f32).astype(bf16)  9.85 us
    dot_general x1, matrix products, on_device(): base_own = jnp.dot(tokens, w_own, preferred_element_type=f32)  9.17 us
    slice x8, local copies, waits for them, and re-layouts, dense(): stacked = jnp.concatenate([g[j] for g in got], axis=0)  7.85 us
    dot_general x4, matrix products, dense(): return jnp.dot(summing[j], stacked, preferred_element_type=f32)  7.68 us
  transfers between devices with their start and end apart: 23, of which 10 were waited for; matrix products, arithmetic and copies ran while one was open for 53% of the time, Pallas kernels for 0%

profile of v1, /device:TPU:0, one launch (start us, length us, event | category | flops | bytes accessed | tf_op | source)
XLA Modules:
  0.0 187.5 jit_solution(13108786416516300151)
XLA Ops:
  0.6 4.1 %collective-permute-start.4 = (bf16[4,16,512]{2,1,0:T(8,128)(2,1)}, bf16[4,16,512]{2,1,0:T(8,128)(2,1)S(1)}, u32[]{:S(2)}, u32[]{:S(2)}) collective-permute-start(bf16[4,16,512]{2,1,0:T(8,128)(2,1)} %param.15), channel_id=1, source_target_pairs={{0,8},{2,10},{4,12},{6,14},{8,0},{10,2},{12,4},{14,6},{1,9},{3,11}... | collective-permute-start | bytes 196616 | tf_op jit(solution)/shard_map/ppermute | solution.py:18
  5.7 1.6 collective-permute-start.1
  8.6 2.3 %broadcast_multiply_fusion = bf16[896,512]{1,0:T(8,128)(2,1)} fusion(bf16[896,512]{1,0:T(8,128)(2,1)} %param.16, bf16[896]{0:T(1024)(128)(2,1)S(1)} %get-tuple-element.84), kind=kLoop, calls=%fused_computation.53 | loop fusion | flops 458752 | bytes 1836800 | tf_op jit(solution)/shard_map/mul | solution.py:59
  10.9 9.9 %fusion.15 = bf16[896,512]{0,1:T(8,128)(2,1)} fusion(bf16[896,4096]{1,0:T(8,128)(2,1)} %param.12, bf16[4096,1024]{1,0:T(8,128)(2,1)} %param.13, s32[]{:T(128)S(6)} %select_n.382), kind=kOutput, calls=%fused_computation.22 | convolution fusion | flops 3758555136 | bytes 12451844 | tf_op jit(solution)/shard_map/dot_general | solution.py:182
  21.8 11.7 %fusion.3 = f32[896,4096]{1,0:T(8,128)} fusion(bf16[896,512]{1,0:T(8,128)(2,1)} %broadcast_multiply_fusion, bf16[4096,1024]{1,0:T(8,128)(2,1)} %param.13, s32[]{:T(128)S(6)} %select_n.381), kind=kOutput, calls=%fused_computation.13 | convolution fusion | flops 3758096384 | bytes 19791876 | tf_op jit(solution)/shard_map/dot_general | solution.py:202
  34.2 2.5 %collective-permute-start.12 = (bf16[144,512]{1,0:T(8,128)(2,1)S(1)}, bf16[144,512]{1,0:T(8,128)(2,1)S(1)}, u32[]{:S(2)}, u32[]{:S(2)}) collective-permute-start(bf16[144,512]{1,0:T(8,128)(2,1)S(1)} %fusion.46), channel_id=1, source_target_pairs={{0,6},{2,4},{4,2},{6,0},{8,14},{10,12},{12,10},{14,8},{1,7},{3,5},... | collective-permute-start | bytes 442376 | tf_op jit(solution)/shard_map/ppermute | solution.py:18
  37.2 5.4 %collective-permute-done.5 = bf16[144,512]{1,0:T(8,128)(2,1)S(1)} collective-permute-done((bf16[144,512]{1,0:T(8,128)(2,1)S(1)}, bf16[144,512]{1,0:T(8,128)(2,1)S(1)}, u32[]{:S(2)}, u32[]{:S(2)}) %collective-permute-start.5) | collective-permute-done | bytes 147488 | tf_op jit(solution)/shard_map/ppermute | solution.py:18
  45.5 1.6 collective-permute-start.7
  47.8 1.6 fusion.19
  49.4 6.9 %collective-permute-done.2 = bf16[8,16,1024]{2,1,0:T(8,128)(2,1)S(1)} collective-permute-done((bf16[8,16,1024]{2,1,0:T(8,128)(2,1)S(1)}, bf16[8,16,1024]{2,1,0:T(8,128)(2,1)S(1)}, u32[]{:S(2)}, u32[]{:S(2)}) %collective-permute-start.2) | collective-permute-done | bytes 262176 | tf_op jit(solution)/shard_map/ppermute | solution.py:18
  56.7 12.5 %collective-permute-done.3 = bf16[16,16,1024]{2,1,0:T(8,128)(2,1)S(1)} collective-permute-done((bf16[16,16,1024]{2,1,0:T(8,128)(2,1)S(1)}, bf16[16,16,1024]{2,1,0:T(8,128)(2,1)S(1)}, u32[]{:S(2)}, u32[]{:S(2)}) %collective-permute-start.3) | collective-permute-done | bytes 524320 | tf_op jit(solution)/shard_map/ppermute | solution.py:18
  72.0 1.5 collective-permute-start.8
  74.2 2.0 %collective-permute-start.9 = (bf16[7,16,1024]{2,1,0:T(8,128)(2,1)S(1)}, bf16[7,16,1024]{2,1,0:T(8,128)(2,1)S(1)}, u32[]{:S(2)}, u32[]{:S(2)}) collective-permute-start(bf16[7,16,1024]{2,1,0:T(8,128)(2,1)S(1)} %broadcast_select_fusion), channel_id=1, source_target_pairs={{0,18},{2,16},{4,22},{6,20},{8,26},{10,24},{12,30},{14,28},{16,2},... | collective-permute-start | bytes 688136 | tf_op jit(solution)/shard_map/ppermute | solution.py:105
  76.4 4.3 %collective-permute-done.8 = bf16[7,16,1024]{2,1,0:T(8,128)(2,1)S(1)} collective-permute-done((bf16[7,16,1024]{2,1,0:T(8,128)(2,1)}, bf16[7,16,1024]{2,1,0:T(8,128)(2,1)S(1)}, u32[]{:S(2)}, u32[]{:S(2)}) %collective-permute-start.8) | collective-permute-done | bytes 229408 | tf_op jit(solution)/shard_map/ppermute | solution.py:14
  80.7 3.2 %collective-permute-done.9 = bf16[7,16,1024]{2,1,0:T(8,128)(2,1)S(1)} collective-permute-done((bf16[7,16,1024]{2,1,0:T(8,128)(2,1)S(1)}, bf16[7,16,1024]{2,1,0:T(8,128)(2,1)S(1)}, u32[]{:S(2)}, u32[]{:S(2)}) %collective-permute-start.9) | collective-permute-done | bytes 229408 | tf_op jit(solution)/shard_map/ppermute | solution.py:105
  85.9 5.5 %convolution_bitcast_fusion = f32[896,112]{0,1:T(8,128)S(1)} fusion(bf16[112,4096]{1,0:T(8,128)(2,1)S(1)} %bitcast.199, bf16[896,4096]{1,0:T(8,128)(2,1)} %param.12), kind=kOutput, calls=%fused_computation.25 | convolution fusion | flops 822083584 | bytes 8658944 | tf_op jit(solution)/shard_map/dot_general | solution.py:187
  93.2 1.6 fusion.18
  96.7 2.4 %collective-permute-start.21 = (bf16[64,512]{1,0:T(8,128)(2,1)}, bf16[64,512]{1,0:T(8,128)(2,1)}, u32[]{:S(2)}, u32[]{:S(2)}) collective-permute-start(bf16[64,512]{1,0:T(8,128)(2,1)} %get-tuple-element.64), channel_id=1, source_target_pairs={{0,6},{2,4},{4,2},{6,0},{8,14},{10,12},{12,10},{14,8},{1,7},{3,5},... | collective-permute-start | bytes 196616 | tf_op jit(solution)/shard_map/ppermute | solution.py:18
  99.1 5.4 %convolution_convert_fusion = bf16[256,4096]{1,0:T(8,128)(2,1)S(1)} fusion(bf16[896,4096]{1,0:T(8,128)(2,1)} %param.12, bf16[32,8,7,128]{3,2,1,0:T(8,128)(2,1)S(1)} %bitcast.207), kind=kOutput, calls=%fused_computation.7 | convolution fusion | flops 1880096768 | bytes 9895936 | tf_op jit(solution)/shard_map/dot_general | solution.py:142
  105.8 7.3 %fusion.40 = f32[896,4096]{1,0:T(8,128)} fusion(bf16[112,4096]{1,0:T(8,128)(2,1)S(1)} %bitcast.200, bf16[14,8,7,128]{3,2,1,0:T(8,128)(2,1)S(1)} %bitcast.202), kind=kOutput, calls=%fused_computation.65 | convolution fusion | flops 822083584 | bytes 15798272 | tf_op jit(solution)/shard_map/dot_general | solution.py:208
  115.0 15.8 %add_convert_fusion = bf16[896,4096]{1,0:T(8,128)(2,1)} fusion(f32[896,4096]{1,0:T(8,128)} %fusion.40, f32[896,4096]{1,0:T(8,128)} %fusion.3, bf16[896,512]{1,0:T(8,128)(2,1)S(1)} %collective-permute-done.13, bf16[4096,1024]{1,0:T(8,128)(2,1)} %param.13, s32[]{:T(128)S(6)} %select_n.382), kind=kOutput, calls=%fused_computation.6 | convolution fusion | flops 3769106432 | bytes 41811972 | tf_op jit(solution)/shard_map/dot_general | solution.py:204
  130.9 1.4 fusion.113
  134.0 2.4 %collective-permute-start.17 = (bf16[64,4096]{1,0:T(8,128)(2,1)}, bf16[64,4096]{1,0:T(8,128)(2,1)S(1)}, u32[]{:S(2)}, u32[]{:S(2)}) collective-permute-start(bf16[64,4096]{1,0:T(8,128)(2,1)} %get-tuple-element.51), channel_id=1, source_target_pairs={{0,6},{2,4},{4,2},{6,0},{8,14},{10,12},{12,10},{14,8},{1,7},{3,5},... | collective-permute-start | bytes 1572872 | tf_op jit(solution)/shard_map/ppermute | solution.py:18
  137.8 1.4 fusion.118
  139.2 1.5 convolution_convert_fusion.2
  142.3 6.4 %collective-permute-done.16 = bf16[64,4096]{1,0:T(8,128)(2,1)S(1)} collective-permute-done((bf16[64,4096]{1,0:T(8,128)(2,1)}, bf16[64,4096]{1,0:T(8,128)(2,1)S(1)}, u32[]{:S(2)}, u32[]{:S(2)}) %collective-permute-start.16) | collective-permute-done | bytes 524320 | tf_op jit(solution)/shard_map/ppermute | solution.py:18
  148.8 9.9 %collective-permute-done.17 = bf16[64,4096]{1,0:T(8,128)(2,1)S(1)} collective-permute-done((bf16[64,4096]{1,0:T(8,128)(2,1)}, bf16[64,4096]{1,0:T(8,128)(2,1)S(1)}, u32[]{:S(2)}, u32[]{:S(2)}) %collective-permute-start.17) | collective-permute-done | bytes 524320 | tf_op jit(solution)/shard_map/ppermute | solution.py:18
  159.4 2.1 %convolution_convert_fusion.1 = bf16[64,4096]{1,0:T(8,128)(2,1)} fusion(bf16[64,128]{1,0:T(8,128)(2,1)} %squeeze.11, bf16[32,4096]{1,0:T(8,128)(2,1)S(1)} %get-tuple-element.57, bf16[32,4096]{1,0:T(8,128)(2,1)S(1)} %get-tuple-element.55, bf16[32,4096]{1,0:T(8,128)(2,1)S(1)} %get-tuple-element.53, bf16[32,4096]{1,0:T(8,128)(2,1)} %get-tuple-element.48), kind=kOutput, calls=%fused_computation.9 | convolution fusion | flops 71565312 | bytes 1589248 | tf_op jit(solution)/shard_map/dot_general | solution.py:170
  161.7 9.2 %fusion.9 = bf16[896,512]{0,1:T(8,128)(2,1)S(1)} fusion(f32[896,512]{0,1:T(8,128)S(1)} %fusion.43, bf16[896,512]{0,1:T(8,128)(2,1)} %collective-permute-done, bf16[896,4096]{1,0:T(8,128)(2,1)} %param.12, bf16[4096,1024]{1,0:T(8,128)(2,1)} %param.13, s32[]{:T(128)S(6)} %select_n.381, pred[896]{0:T(1024)(128)(4,1)S(1)} %copy-done.3), kind=kOutput, calls=%fused_computation.20 | convolution fusion | flops 3760848896 | bytes 15205252 | tf_op jit(solution)/shard_map/dot_general | solution.py:183
  172.2 1.7 convolution_add_fusion.1
  173.9 11.1 %collective-permute-done.18 = bf16[64,4096]{1,0:T(8,128)(2,1)} collective-permute-done((bf16[64,4096]{1,0:T(8,128)(2,1)}, bf16[64,4096]{1,0:T(8,128)(2,1)}, u32[]{:S(2)}, u32[]{:S(2)}) %collective-permute-start.18) | collective-permute-done | bytes 524320 | tf_op jit(solution)/shard_map/ppermute | solution.py:18
  185.1 2.4 %convolution_add_fusion = f32[64,4096]{1,0:T(8,128)} fusion(bf16[64,128]{1,0:T(8,128)(2,1)S(1)} %squeeze.10, bf16[32,4096]{1,0:T(8,128)(2,1)} %get-tuple-element.58, bf16[32,4096]{1,0:T(8,128)(2,1)S(1)} %get-tuple-element.56, bf16[32,4096]{1,0:T(8,128)(2,1)S(1)} %copy-done.1, bf16[32,4096]{1,0:T(8,128)(2,1)S(1)} %get-tuple-element.49, ...), kind=kOutput, calls=%fused_computation.8 | convolution fusion | flops 71827456 | bytes 2637824 | tf_op jit(solution)/shard_map/dot_general | solution.py:170
  (137 shorter events, 27.8 us)
Async XLA Ops:
  0.6 32.9 %collective-permute-start.4 = (bf16[4,16,512]{2,1,0:T(8,128)(2,1)}, bf16[4,16,512]{2,1,0:T(8,128)(2,1)S(1)}, u32[]{:S(2)}, u32[]{:S(2)}) collective-permute-start(bf16[4,16,512]{2,1,0:T(8,128)(2,1)} %param.15), channel_id=1, source_target_pairs={{0,8},{2,10},{4,12},{6,14},{8,0},{10,2},{12,4},{14,6},{1,9},{3,11}... | collective-permute-start | bytes 196616 | tf_op jit(solution)/shard_map/ppermute | solution.py:18
  5.7 31.0 %collective-permute-start.1 = (bf16[4,16,1024]{2,1,0:T(8,128)(2,1)S(1)}, bf16[4,16,1024]{2,1,0:T(8,128)(2,1)S(1)}, u32[]{:S(2)}, u32[]{:S(2)}) collective-permute-start(bf16[4,16,1024]{2,1,0:T(8,128)(2,1)S(1)} %get-tuple-element.60), channel_id=1, source_target_pairs={{0,2},{2,0},{4,6},{6,4},{8,10},{10,8},{12,14},{14,12},{1,3},{3,1},... | collective-permute-start | bytes 393224 | tf_op jit(solution)/shard_map/ppermute | solution.py:18
  10.9 103.4 %collective-permute-start.13 = (bf16[896,512]{1,0:T(8,128)(2,1)}, bf16[896,512]{1,0:T(8,128)(2,1)S(1)}, u32[]{:S(2)}, u32[]{:S(2)}) collective-permute-start(bf16[896,512]{1,0:T(8,128)(2,1)} %broadcast_multiply_fusion), channel_id=1, source_target_pairs={{0,1},{1,0},{2,3},{3,2},{4,5},{5,4},{6,7},{7,6},{8,9},{9,8},{10,11... | collective-permute-start | bytes 2752520 | tf_op jit(solution)/shard_map/ppermute | solution.py:14
  10.9 10.4 %copy-start.2 = (bf16[4,16,512]{2,1,0:T(8,128)(2,1)S(1)}, bf16[4,16,512]{2,1,0:T(8,128)(2,1)}, u32[]{:S(2)}) copy-start(bf16[4,16,512]{2,1,0:T(8,128)(2,1)} %param.15) | copy-start | bytes 196612
  10.9 10.4 %copy-start.4 = (s32[32]{0:T(128)S(1)}, s32[32]{0:T(128)}, u32[]{:S(2)}) copy-start(s32[32]{0:T(128)} %param.19) | copy-start | bytes 388
  10.9 10.4 %copy-start.5 = (s32[7]{0:T(128)S(1)}, s32[7]{0:T(128)}, u32[]{:S(2)}) copy-start(s32[7]{0:T(128)} %param.17) | copy-start | bytes 88
  20.8 141.0 %collective-permute-start = (bf16[896,512]{0,1:T(8,128)(2,1)}, bf16[896,512]{0,1:T(8,128)(2,1)}, u32[]{:S(2)}, u32[]{:S(2)}) collective-permute-start(bf16[896,512]{0,1:T(8,128)(2,1)} %fusion.15), channel_id=1, source_target_pairs={{0,1},{1,0},{2,3},{3,2},{4,5},{5,4},{6,7},{7,6},{8,9},{9,8},{10,11... | collective-permute-start | bytes 2752520 | tf_op jit(solution)/shard_map/ppermute | solution.py:14
  33.6 9.0 %collective-permute-start.5 = (bf16[144,512]{1,0:T(8,128)(2,1)S(1)}, bf16[144,512]{1,0:T(8,128)(2,1)S(1)}, u32[]{:S(2)}, u32[]{:S(2)}) collective-permute-start(bf16[144,512]{1,0:T(8,128)(2,1)S(1)} %fusion.46), channel_id=1, source_target_pairs={{0,2},{2,0},{4,6},{6,4},{8,10},{10,8},{12,14},{14,12},{1,3},{3,1},... | collective-permute-start | bytes 442376 | tf_op jit(solution)/shard_map/ppermute | solution.py:18
  34.2 9.0 %collective-permute-start.12 = (bf16[144,512]{1,0:T(8,128)(2,1)S(1)}, bf16[144,512]{1,0:T(8,128)(2,1)S(1)}, u32[]{:S(2)}, u32[]{:S(2)}) collective-permute-start(bf16[144,512]{1,0:T(8,128)(2,1)S(1)} %fusion.46), channel_id=1, source_target_pairs={{0,6},{2,4},{4,2},{6,0},{8,14},{10,12},{12,10},{14,8},{1,7},{3,5},... | collective-permute-start | bytes 442376 | tf_op jit(solution)/shard_map/ppermute | solution.py:18
  36.7 7.1 %collective-permute-start.11 = (bf16[144,512]{1,0:T(8,128)(2,1)S(1)}, bf16[144,512]{1,0:T(8,128)(2,1)S(1)}, u32[]{:S(2)}, u32[]{:S(2)}) collective-permute-start(bf16[144,512]{1,0:T(8,128)(2,1)S(1)} %fusion.46), channel_id=1, source_target_pairs={{0,4},{2,6},{4,0},{6,2},{8,12},{10,14},{12,8},{14,10},{1,5},{3,7},... | collective-permute-start | bytes 442376 | tf_op jit(solution)/shard_map/ppermute | solution.py:18
  42.6 13.7 %collective-permute-start.2 = (bf16[8,16,1024]{2,1,0:T(8,128)(2,1)S(1)}, bf16[8,16,1024]{2,1,0:T(8,128)(2,1)S(1)}, u32[]{:S(2)}, u32[]{:S(2)}) collective-permute-start(bf16[8,16,1024]{2,1,0:T(8,128)(2,1)S(1)} %pad_maximum_fusion.4), channel_id=1, source_target_pairs={{0,8},{2,10},{4,12},{6,14},{8,0},{10,2},{12,4},{14,6},{1,9},{3,11}... | collective-permute-start | bytes 786440 | tf_op jit(solution)/shard_map/ppermute | solution.py:18
  45.5 11.2 %collective-permute-start.7 = (s32[2,7]{1,0:T(2,128)S(1)}, s32[2,7]{1,0:T(2,128)S(1)}, u32[]{:S(2)}, u32[]{:S(2)}) collective-permute-start(s32[2,7]{1,0:T(2,128)S(1)} %pad_add_fusion.1), channel_id=1, source_target_pairs={{0,16},{16,0},{1,17},{17,1},{2,18},{18,2},{3,19},{19,3},{4,20},{20... | collective-permute-start | bytes 176 | tf_op jit(solution)/shard_map/ppermute | solution.py:14
  56.4 12.8 %collective-permute-start.3 = (bf16[16,16,1024]{2,1,0:T(8,128)(2,1)S(1)}, bf16[16,16,1024]{2,1,0:T(8,128)(2,1)S(1)}, u32[]{:S(2)}, u32[]{:S(2)}) collective-permute-start(bf16[16,16,1024]{2,1,0:T(8,128)(2,1)S(1)} %pad_maximum_fusion.2), channel_id=1, source_target_pairs={{0,4},{2,6},{4,0},{6,2},{8,12},{10,14},{12,8},{14,10},{1,5},{3,7},... | collective-permute-start | bytes 1572872 | tf_op jit(solution)/shard_map/ppermute | solution.py:18
  70.0 6.3 %collective-permute-start.6 = (bf16[7,16,1024]{2,1,0:T(8,128)(2,1)S(1)}, bf16[7,16,1024]{2,1,0:T(8,128)(2,1)S(1)}, u32[]{:S(2)}, u32[]{:S(2)}) collective-permute-start(bf16[7,16,1024]{2,1,0:T(8,128)(2,1)S(1)} %broadcast_select_fusion.2), channel_id=1, source_target_pairs={{0,2},{2,0},{4,6},{6,4},{8,10},{10,8},{12,14},{14,12},{1,3},{3,1},... | collective-permute-start | bytes 688136 | tf_op jit(solution)/shard_map/ppermute | solution.py:18
  72.0 8.6 %collective-permute-start.8 = (bf16[7,16,1024]{2,1,0:T(8,128)(2,1)}, bf16[7,16,1024]{2,1,0:T(8,128)(2,1)S(1)}, u32[]{:S(2)}, u32[]{:S(2)}) collective-permute-start(bf16[7,16,1024]{2,1,0:T(8,128)(2,1)} %broadcast_select_fusion.1), channel_id=1, source_target_pairs={{0,16},{16,0},{1,17},{17,1},{2,18},{18,2},{3,19},{19,3},{4,20},{20... | collective-permute-start | bytes 688136 | tf_op jit(solution)/shard_map/ppermute | solution.py:14
  74.2 9.6 %collective-permute-start.9 = (bf16[7,16,1024]{2,1,0:T(8,128)(2,1)S(1)}, bf16[7,16,1024]{2,1,0:T(8,128)(2,1)S(1)}, u32[]{:S(2)}, u32[]{:S(2)}) collective-permute-start(bf16[7,16,1024]{2,1,0:T(8,128)(2,1)S(1)} %broadcast_select_fusion), channel_id=1, source_target_pairs={{0,18},{2,16},{4,22},{6,20},{8,26},{10,24},{12,30},{14,28},{16,2},... | collective-permute-start | bytes 688136 | tf_op jit(solution)/shard_map/ppermute | solution.py:105
  76.3 15.4 %collective-permute-start.14 = (f32[7,128,16]{1,2,0:T(8,128)S(1)}, f32[7,128,16]{1,2,0:T(8,128)S(1)}, u32[]{:S(2)}, u32[]{:S(2)}) collective-permute-start(f32[7,128,16]{1,2,0:T(8,128)S(1)} %fusion.19), channel_id=1, source_target_pairs={{0,1},{1,0},{2,3},{3,2},{4,5},{5,4},{6,7},{7,6},{8,9},{9,8},{10,11... | collective-permute-start | bytes 172040 | tf_op jit(solution)/shard_map/ppermute | solution.py:14
  91.6 1.3 collective-permute-start.10
  94.9 9.7 %copy-start = (bf16[256,512]{1,0:T(8,128)(2,1)}, bf16[256,512]{1,0:T(8,128)(2,1)S(1)}, u32[]{:S(2)}) copy-start(bf16[256,512]{1,0:T(8,128)(2,1)S(1)} %fusion.18) | copy-start | bytes 786436
  95.6 36.6 %collective-permute-start.19 = (bf16[64,512]{1,0:T(8,128)(2,1)}, bf16[64,512]{1,0:T(8,128)(2,1)}, u32[]{:S(2)}, u32[]{:S(2)}) collective-permute-start(bf16[64,512]{1,0:T(8,128)(2,1)} %get-tuple-element.63), channel_id=1, source_target_pairs={{0,2},{2,0},{4,6},{6,4},{8,10},{10,8},{12,14},{14,12},{1,3},{3,1},... | collective-permute-start | bytes 196616 | tf_op jit(solution)/shard_map/ppermute | solution.py:18
  96.4 37.6 %collective-permute-start.20 = (bf16[64,512]{1,0:T(8,128)(2,1)}, bf16[64,512]{1,0:T(8,128)(2,1)}, u32[]{:S(2)}, u32[]{:S(2)}) collective-permute-start(bf16[64,512]{1,0:T(8,128)(2,1)} %get-tuple-element.65), channel_id=1, source_target_pairs={{0,4},{2,6},{4,0},{6,2},{8,12},{10,14},{12,8},{14,10},{1,5},{3,7},... | collective-permute-start | bytes 196616 | tf_op jit(solution)/shard_map/ppermute | solution.py:18
  96.7 41.1 %collective-permute-start.21 = (bf16[64,512]{1,0:T(8,128)(2,1)}, bf16[64,512]{1,0:T(8,128)(2,1)}, u32[]{:S(2)}, u32[]{:S(2)}) collective-permute-start(bf16[64,512]{1,0:T(8,128)(2,1)} %get-tuple-element.64), channel_id=1, source_target_pairs={{0,6},{2,4},{4,2},{6,0},{8,14},{10,12},{12,10},{14,8},{1,7},{3,5},... | collective-permute-start | bytes 196616 | tf_op jit(solution)/shard_map/ppermute | solution.py:18
  114.3 27.3 %collective-permute-start.15 = (bf16[64,4096]{1,0:T(8,128)(2,1)}, bf16[64,4096]{1,0:T(8,128)(2,1)S(1)}, u32[]{:S(2)}, u32[]{:S(2)}) collective-permute-start(bf16[64,4096]{1,0:T(8,128)(2,1)} %get-tuple-element.50), channel_id=1, source_target_pairs={{0,2},{2,0},{4,6},{6,4},{8,10},{10,8},{12,14},{14,12},{1,3},{3,1},... | collective-permute-start | bytes 1572872 | tf_op jit(solution)/shard_map/ppermute | solution.py:18
  130.8 30.9 %copy-start.3 = (pred[896]{0:T(1024)(128)(4,1)S(1)}, pred[896]{0:T(1024)(128)(4,1)}, u32[]{:S(2)}) copy-start(pred[896]{0:T(1024)(128)(4,1)} %get-tuple-element.85) | copy-start | bytes 2692
  132.2 16.5 %collective-permute-start.16 = (bf16[64,4096]{1,0:T(8,128)(2,1)}, bf16[64,4096]{1,0:T(8,128)(2,1)S(1)}, u32[]{:S(2)}, u32[]{:S(2)}) collective-permute-start(bf16[64,4096]{1,0:T(8,128)(2,1)} %get-tuple-element.52), channel_id=1, source_target_pairs={{0,4},{2,6},{4,0},{6,2},{8,12},{10,14},{12,8},{14,10},{1,5},{3,7},... | collective-permute-start | bytes 1572872 | tf_op jit(solution)/shard_map/ppermute | solution.py:18
  134.0 24.7 %collective-permute-start.17 = (bf16[64,4096]{1,0:T(8,128)(2,1)}, bf16[64,4096]{1,0:T(8,128)(2,1)S(1)}, u32[]{:S(2)}, u32[]{:S(2)}) collective-permute-start(bf16[64,4096]{1,0:T(8,128)(2,1)} %get-tuple-element.51), channel_id=1, source_target_pairs={{0,6},{2,4},{4,2},{6,0},{8,14},{10,12},{12,10},{14,8},{1,7},{3,5},... | collective-permute-start | bytes 1572872 | tf_op jit(solution)/shard_map/ppermute | solution.py:18
  140.7 31.5 %collective-permute-start.22 = (bf16[64,512]{1,0:T(8,128)(2,1)}, bf16[64,512]{1,0:T(8,128)(2,1)}, u32[]{:S(2)}, u32[]{:S(2)}) collective-permute-start(bf16[64,512]{1,0:T(8,128)(2,1)} %convolution_convert_fusion.2), channel_id=1, source_target_pairs={{0,8},{2,10},{4,12},{6,14},{8,0},{10,2},{12,4},{14,6},{1,9},{3,11}... | collective-permute-start | bytes 196616 | tf_op jit(solution)/shard_map/ppermute | solution.py:18
  161.5 23.6 %collective-permute-start.18 = (bf16[64,4096]{1,0:T(8,128)(2,1)}, bf16[64,4096]{1,0:T(8,128)(2,1)}, u32[]{:S(2)}, u32[]{:S(2)}) collective-permute-start(bf16[64,4096]{1,0:T(8,128)(2,1)} %convolution_convert_fusion.1), channel_id=1, source_target_pairs={{0,8},{2,10},{4,12},{6,14},{8,0},{10,2},{12,4},{14,6},{1,9},{3,11}... | collective-permute-start | bytes 1572872 | tf_op jit(solution)/shard_map/ppermute | solution.py:18
  161.7 23.3 %copy-start.1 = (bf16[32,4096]{1,0:T(8,128)(2,1)S(1)}, bf16[32,4096]{1,0:T(8,128)(2,1)}, u32[]{:S(2)}) copy-start(bf16[32,4096]{1,0:T(8,128)(2,1)} %get-tuple-element.54) | copy-start | bytes 786436

commit v2 on v0

v2 whole, which is shorter than its diff:
```python
import functools

import jax
import jax.numpy as jnp
from jax import lax
from jax.experimental import pallas as pl
from jax.experimental.pallas import tpu as pltpu
from jax.sharding import PartitionSpec as P

TENANT_BLOCK = 128
CAP = 2
NEAR = 4
VMEM_LIMIT = 48 * 1024 * 1024

adapter_scale = 2.0
f32 = jnp.float32
bf16 = jnp.bfloat16
i32 = jnp.int32

NT = (((1,), (1,)), ((), ()))
TN = (((0,), (0,)), ((), ()))
NN = (((1,), (0,)), ((), ()))


def _dot(a, b, dims):
    return lax.dot_general(a, b, dims, preferred_element_type=f32)


def _swap(x, axis):
    return lax.ppermute(x, axis, [(0, 1), (1, 0)])


def _xor(x, n, k):
    return lax.ppermute(x, "dp", [(i, i ^ k) for i in range(n)])


def _call(body, n_scalars, grid, in_specs, out_specs, out_shape, scratch, flops, moved):
    return pl.pallas_call(
        body,
        grid_spec=pltpu.PrefetchScalarGridSpec(
            num_scalar_prefetch=n_scalars,
            grid=grid,
            in_specs=in_specs,
            out_specs=out_specs,
            scratch_shapes=scratch,
        ),
        out_shape=out_shape,
        compiler_params=pltpu.CompilerParams(vmem_limit_bytes=VMEM_LIMIT),
        cost_estimate=pl.CostEstimate(flops=flops, bytes_accessed=moved, transcendentals=0),
    )


def _whole(shape):
    return pl.BlockSpec(shape, lambda *_: (0,) * len(shape))


class Sizes:
    def __init__(self, n_dp, nb, ten_dev, rank, cols, width):
        self.n_dp, self.nb, self.ten_dev = n_dp, nb, ten_dev
        self.rank, self.cols, self.width = rank, cols, width
        self.n_far = n_dp // NEAR
        self.rows = nb * TENANT_BLOCK
        self.me, self.core, self.quarter = 6 * nb, 6 * nb + 1, 6 * nb + 2
        self.valid = 6 * nb + 3

    def slot(self, info, which, b):
        return info[which * self.nb + b]

    def owner_and_order(self, info, which):
        owners = [self.slot(info, which, b) // self.ten_dev for b in range(self.nb)]
        orders = []
        for b in range(self.nb):
            n = jnp.int32(0)
            for c in range(b):
                n = n + jnp.where(owners[c] == owners[b], 1, 0)
            orders.append(n)
        return owners, orders

    def places(self, info):
        owners, orders = self.owner_and_order(info, 0)
        out = []
        for o, r in zip(owners, orders):
            rel = o ^ info[self.me]
            out.append(((rel % NEAR) * self.n_far + rel // NEAR) * CAP + r)
        return out


def _masked(x, valid):
    row = lax.broadcasted_iota(i32, x.shape, 0)
    return jnp.where(row < valid, x, jnp.zeros((), x.dtype))


def back_kernel(z, info, g_ref, *refs):
    packets, (up_ref, part_ref) = refs[:NEAR], refs[NEAR:]
    t = TENANT_BLOCK
    for b in range(z.nb):
        s = z.slot(info, 0, b)
        rel = (s // z.ten_dev) ^ info[z.me]
        at = pl.multiple_of(((rel // NEAR) * z.ten_dev + s % z.ten_dev) * z.rank, z.rank)
        near = rel % NEAR
        u = packets[0][pl.ds(at, z.rank), :]
        for k in range(1, NEAR):
            u = jnp.where(near == k, packets[k][pl.ds(at, z.rank), :], u)
        up_ref[b * z.rank : (b + 1) * z.rank, :] = u
        g = _masked(g_ref[b * t : (b + 1) * t, :], info[z.valid + b])
        part_ref[:, b * t : (b + 1) * t] = _dot(u, g, NT)


def pack_kernel(z, n_out, info, mine_ref, other_ref, right_ref, *refs):
    outs, packed = refs[:n_out], refs[n_out]
    t = TENANT_BLOCK

    @pl.when(pl.program_id(0) == 0)
    def _():
        packed[...] = jnp.zeros_like(packed)
        for b, place in enumerate(z.places(info)):
            cut = slice(b * t, (b + 1) * t)
            v = (mine_ref[:, cut] + other_ref[:, cut]) * adapter_scale
            packed[pl.ds(pl.multiple_of(place * z.rank, z.rank), z.rank), cut] = v.astype(bf16)

    res = jnp.dot(packed[...], right_ref[...], preferred_element_type=f32).astype(bf16)
    each = res.shape[0] // n_out
    for k in range(n_out):
        outs[k][...] = res[k * each : (k + 1) * each]


def pack_up_kernel(z, n_out, info, mine_ref, other_ref, g_ref, *refs):
    outs, packed, g = refs[:n_out], refs[n_out], refs[n_out + 1]
    t = TENANT_BLOCK
    packed[...] = jnp.zeros_like(packed)
    for b, place in enumerate(z.places(info)):
        cut = slice(b * t, (b + 1) * t)
        v = mine_ref[:, cut] + other_ref[:, cut]
        packed[pl.ds(pl.multiple_of(place * z.rank, z.rank), z.rank), cut] = v.astype(bf16)
        g[cut, :] = _masked(g_ref[cut, :], info[z.valid + b])
    res = adapter_scale * jnp.dot(packed[...], g[...], preferred_element_type=f32)
    each = res.shape[0] // n_out
    for k in range(n_out):
        outs[k][...] = res[k * each : (k + 1) * each].astype(bf16)


def dense_kernel(z, info, *refs):
    got, near_ref, far_refs = refs[:NEAR], refs[NEAR], refs[NEAR + 1 :]
    n = CAP * z.rank
    shape = (z.ten_dev * z.rank, n)
    row = lax.broadcasted_iota(i32, shape, 0)
    col = lax.broadcasted_iota(i32, shape, 1)
    same = (row % z.rank) == (col % z.rank)
    tables = [z.owner_and_order(info, k) for k in range(NEAR)]
    for j in range(z.n_far):
        holder = info[z.me] ^ (NEAR * j)
        total = None
        for k in range(NEAR):
            owners, orders = tables[k]
            local = []
            for r in range(CAP):
                found = jnp.int32(0)
                for b in range(z.nb):
                    hit = (owners[b] == holder) & (orders[b] == r)
                    found = jnp.where(hit, z.slot(info, k, b) % z.ten_dev, found)
                local.append(found)
            wanted = jnp.where(col < z.rank, local[0], local[1])
            one_hot = jnp.where(same & (row // z.rank == wanted), 1.0, 0.0).astype(bf16)
            term = jnp.dot(
                one_hot, got[k][j * n : (j + 1) * n, :], preferred_element_type=f32
            )
            total = term if total is None else total + term
        if j == 0:
            near_ref[...] = total
        else:
            far_refs[j - 1][...] = total.astype(bf16)


def final_kernel(near_ref, *refs):
    total = near_ref[...]
    for r in refs[:-1]:
        total = total + r[...].astype(f32)
    refs[-1][...] = total


def choose_kernel(z, info, pair_ref, far_ref, *outs):
    half = pair_ref.shape[0]
    for which, out in zip((0, 1, 4, 5), outs):
        for b in range(z.nb):
            s = z.slot(info, which, b)
            rel = (s // z.ten_dev) ^ info[z.me]
            line = rel // 2
            at = ((line // 2) * 2 + rel % 2) * z.ten_dev + s % z.ten_dev
            out[b] = jnp.where(line % 2 == 1, far_ref[at % half], pair_ref[at % half])


def other_kernel(info, x_ref, w_ref, out_ref, acc):
    k = pl.program_id(0)

    @pl.when(k == 0)
    def _():
        acc[...] = jnp.zeros_like(acc)

    acc[...] += jnp.dot(x_ref[...], w_ref[...], preferred_element_type=f32)

    @pl.when(k == pl.num_programs(0) - 1)
    def _():
        out_ref[...] = acc[...].astype(bf16)


def shrink_kernel(z, info, x_ref, d_ref, out_ref):
    k = pl.program_id(0)
    t = TENANT_BLOCK
    for b in range(z.nb):
        cut = slice(b * t, (b + 1) * t)
        v = _dot(d_ref[0, b], x_ref[cut, :], NT)

        @pl.when(k == 0)
        def _():
            out_ref[:, cut] = v

        @pl.when(k > 0)
        def _():
            out_ref[:, cut] += v


def projected_kernel(z, info, x_ref, w_ref, base_ref, mine_ref, other_ref, up_ref, out_ref, acc):
    k = pl.program_id(0)
    t = TENANT_BLOCK

    @pl.when(k == 0)
    def _():
        acc[...] = base_ref[...].astype(f32)

    acc[...] += jnp.dot(x_ref[...], w_ref[...], preferred_element_type=f32)

    @pl.when(k == pl.num_programs(0) - 1)
    def _():
        for b in range(z.nb):
            cut = slice(b * t, (b + 1) * t)
            s = (mine_ref[:, cut] + other_ref[:, cut]).astype(bf16)
            wide = _dot(s, up_ref[b * z.rank : (b + 1) * z.rank, :], TN)
            full = acc[cut, :] + adapter_scale * wide
            out_ref[cut, :] = _masked(full, info[z.valid + b]).astype(bf16)


def tokens_kernel(z, info, g_ref, h_ref, w_ref, mine_ref, other_ref, d_ref, out_ref, g_full, back):
    t = TENANT_BLOCK

    @pl.when(pl.program_id(0) == 0)
    def _():
        own = pl.ds(pl.multiple_of(info[z.core] * z.cols, z.cols), z.cols)
        far = pl.ds(pl.multiple_of((1 - info[z.core]) * z.cols, z.cols), z.cols)
        for b in range(z.nb):
            cut = slice(b * t, (b + 1) * t)
            g_full[cut, own] = _masked(g_ref[cut, :], info[z.valid + b])
            g_full[cut, far] = _masked(h_ref[cut, :], info[z.valid + b])
        back[...] = ((mine_ref[...] + other_ref[...]) * adapter_scale).astype(bf16)

    through = _dot(g_full[...], w_ref[...], NT)
    for b in range(z.nb):
        cut = slice(b * t, (b + 1) * t)
        out_ref[cut, :] = (through[cut] + _dot(back[:, cut], d_ref[0, b], TN)).astype(bf16)


def on_device(
    n_groups,
    n_dp,
    tokens,
    base_weight,
    adapter_down,
    adapter_up,
    out_cotangent,
    block_tenant,
    block_valid,
    tenant_slot,
):
    nb = block_tenant.shape[0]
    rows, width = tokens.shape
    cols = out_cotangent.shape[1]
    tenants = tenant_slot.shape[0]
    ten_dev, _, rank = adapter_down.shape
    z = Sizes(n_dp, nb, ten_dev, rank, cols, width)
    n_far = z.n_far
    me = lax.axis_index("dp")
    core = lax.axis_index("tensor")
    group = lax.axis_index("groups")
    shared = n_groups == 2 and n_dp == 8
    n_quarters = 4 if shared else 1
    mine_q = group * 2 + me % 2 if shared else jnp.int32(0)

    far_up = [_xor(adapter_up, n_dp, NEAR * j) for j in range(1, n_far)]
    cotangent_other = _swap(out_cotangent, "tensor")

    tenant_match = block_tenant[:, None] == jnp.arange(tenants, dtype=i32)[None, :]
    slots = jnp.sum(jnp.where(tenant_match, tenant_slot[None, :], 0), axis=1).astype(i32)
    slots_x = _swap(slots, "groups") if shared else slots

    down_t = jnp.swapaxes(adapter_down, 1, 2)
    if shared:
        quarter = width // 4
        own = lax.dynamic_slice_in_dim(down_t, mine_q * quarter, quarter, axis=2)
        to_y = lax.dynamic_slice_in_dim(down_t, (mine_q ^ 1) * quarter, quarter, axis=2)
        shard = jnp.concatenate([own, _xor(to_y, n_dp, 1)], axis=0)
        pair = jnp.concatenate([shard, _xor(shard, n_dp, 4)], axis=0)

    tag = jnp.zeros((16, cols), bf16)
    tag = tag.at[0, :nb].set(slots.astype(bf16)).at[1, :nb].set(slots_x.astype(bf16))
    ups = [u.reshape(ten_dev * rank, cols) for u in [adapter_up] + far_up]
    packet = jnp.concatenate(ups + [tag], axis=0)
    packets = [packet] + [_xor(packet, n_dp, k) for k in range(1, NEAR)]
    tags = [p[-16:-14, :nb].astype(i32) for p in packets]
    info = jnp.concatenate(
        [tags[k][0] for k in range(NEAR)]
        + [tags[0][1], tags[1][1], jnp.stack([me, core, mine_q]), block_valid]
    ).astype(i32)

    part_width = width // n_quarters
    part = (rank, rows)
    block_up, back_part = _call(
        functools.partial(back_kernel, z), 1, (1,),
        [_whole((rows, cols))] + [_whole(packet.shape)] * NEAR,
        [_whole((nb * rank, cols)), _whole(part)],
        [jax.ShapeDtypeStruct((nb * rank, cols), bf16), jax.ShapeDtypeStruct(part, f32)],
        [], 2 * rows * cols * rank * 8, 2 * rows * cols,
    )(info, out_cotangent, *packets)
    back_other = _swap(back_part, "tensor")

    packed_rows = n_dp * CAP * rank
    near_rows = packed_rows // NEAR
    tile = min(1024, part_width)
    sends = _call(
        functools.partial(pack_kernel, z, NEAR), 1, (width // tile,),
        [_whole(part), _whole(part), pl.BlockSpec((rows, tile), lambda i, *_: (0, i))],
        [pl.BlockSpec((near_rows, tile), lambda i, *_: (0, i))] * NEAR,
        [jax.ShapeDtypeStruct((near_rows, width), bf16)] * NEAR,
        [pltpu.VMEM((packed_rows, rows), bf16)],
        2 * packed_rows * rows * width, 2 * rows * width + 2 * packed_rows * width,
    )(info, back_part, back_other, tokens)

    def collect(sends):
        wide = sends[0].shape[1]
        cut = min(wide, tile)
        got = [sends[0]] + [_xor(sends[k], n_dp, k) for k in range(1, NEAR)]
        spec = pl.BlockSpec((ten_dev * rank, cut), lambda i, *_: (0, i))
        dense = _call(
            functools.partial(dense_kernel, z), 1, (wide // cut,),
            [pl.BlockSpec((near_rows, cut), lambda i, *_: (0, i))] * NEAR,
            [spec] * n_far,
            [jax.ShapeDtypeStruct((ten_dev * rank, wide), f32)]
            + [jax.ShapeDtypeStruct((ten_dev * rank, wide), bf16)] * (n_far - 1),
            [], 2 * packed_rows * ten_dev * rank * wide, 2 * packed_rows * wide,
        )(info, *got)
        far = [_xor(dense[j], n_dp, NEAR * j) for j in range(1, n_far)]
        spec = pl.BlockSpec((ten_dev * rank, cut), lambda i: (0, i))
        total = _call(
            final_kernel, 0, (wide // cut,), [spec] * n_far, spec,
            jax.ShapeDtypeStruct((ten_dev * rank, wide), f32),
            [], ten_dev * rank * wide, 10 * ten_dev * rank * wide,
        )(dense[0], *far)
        return total.reshape(ten_dev, rank, wide)

    grad_down = jnp.swapaxes(collect(sends), 1, 2)

    deep = min(1024, width)
    base_other = _call(
        other_kernel, 1, (width // deep,),
        [
            pl.BlockSpec((rows, deep), lambda k, s: (0, k)),
            pl.BlockSpec((deep, cols), lambda k, s: (k, 1 - s[0])),
        ],
        _whole((rows, cols)), jax.ShapeDtypeStruct((rows, cols), bf16),
        [pltpu.VMEM((rows, cols), f32)],
        2 * rows * cols * width, 2 * rows * width + 2 * cols * width,
    )(jnp.full((1,), core, i32), tokens, base_weight)
    base_arrived = _swap(base_other, "tensor")

    if shared:
        every = _xor(pair, n_dp, 2)
        block = (nb, rank, quarter)
        chosen = _call(
            functools.partial(choose_kernel, z), 1, (1,),
            [_whole(pair.shape)] * 2, [_whole(block)] * 4,
            [jax.ShapeDtypeStruct(block, bf16)] * 4,
            [], 0, 6 * pair.size,
        )(info, pair, every)
        got = [
            chosen[0],
            _xor(chosen[1], n_dp, 1),
            _swap(chosen[2], "groups"),
            lax.ppermute(
                chosen[3],
                ("groups", "dp"),
                [(g * n_dp + d, (1 - g) * n_dp + (d ^ 1)) for g in range(2) for d in range(n_dp)],
            ),
        ]
        block_down = jnp.stack(got)
    else:
        every = lax.all_gather(down_t, "dp", axis=0, tiled=True)
        block_down = jnp.take(every, slots, axis=0)[None]

    def down_spec(cut):
        per = part_width // cut
        return pl.BlockSpec(
            (1, nb, rank, cut), lambda i, s: ((i // per) ^ s[z.quarter], 0, 0, i % per)
        )

    cut = min(1024, part_width)
    shrink_part = _call(
        functools.partial(shrink_kernel, z), 1, (width // cut,),
        [pl.BlockSpec((rows, cut), lambda i, s: (0, i)), down_spec(cut)],
        _whole(part), jax.ShapeDtypeStruct(part, f32),
        [], 2 * rows * width * 128, 2 * rows * width,
    )(info, tokens, block_down)
    shrink_other = _swap(shrink_part, "tensor")

    up_sends = _call(
        functools.partial(pack_up_kernel, z, NEAR), 1, (1,),
        [_whole(part), _whole(part), _whole((rows, cols))],
        [_whole((near_rows, cols))] * NEAR,
        [jax.ShapeDtypeStruct((near_rows, cols), bf16)] * NEAR,
        [pltpu.VMEM((packed_rows, rows), bf16), pltpu.VMEM((rows, cols), bf16)],
        2 * packed_rows * rows * cols, 2 * rows * cols + 2 * packed_rows * cols,
    )(info, shrink_part, shrink_other, out_cotangent)
    grad_up = collect(up_sends)

    projected = _call(
        functools.partial(projected_kernel, z), 1, (width // deep,),
        [
            pl.BlockSpec((rows, deep), lambda k, s: (0, k)),
            pl.BlockSpec((deep, cols), lambda k, s: (k, s[z.core])),
            _whole((rows, cols)), _whole(part), _whole(part), _whole((nb * rank, cols)),
        ],
        _whole((rows, cols)), jax.ShapeDtypeStruct((rows, cols), bf16),
        [pltpu.VMEM((rows, cols), f32)],
        2 * rows * cols * width, 2 * rows * width + 2 * cols * width,
    )(info, tokens, base_weight, base_arrived, shrink_part, shrink_other, block_up)

    cut = min(512, part_width)
    grad_tokens = _call(
        functools.partial(tokens_kernel, z), 1, (width // cut,),
        [
            _whole((rows, cols)), _whole((rows, cols)),
            pl.BlockSpec((cut, 2 * cols), lambda i, s: (i, 0)),
            _whole(part), _whole(part), down_spec(cut),
        ],
        pl.BlockSpec((rows, cut), lambda i, s: (0, i)),
        jax.ShapeDtypeStruct((rows, width), bf16),
        [pltpu.VMEM((rows, 2 * cols), bf16), pltpu.VMEM(part, bf16)],
        4 * rows * cols * width, 2 * rows * width + 4 * cols * width,
    )(info, out_cotangent, cotangent_other, base_weight, back_part, back_other, block_down)
    return projected, grad_tokens, grad_down, grad_up


def solution(mesh):
    n_groups, n_dp = mesh.shape["groups"], mesh.shape["dp"]
    in_specs = (
        P(("groups", "dp"), "tensor"),
        P("tensor", None),
        P("dp", "tensor", None),
        P("dp", None, "tensor"),
        P(("groups", "dp"), "tensor"),
        P(("groups", "dp")),
        P(("groups", "dp")),
        P("groups"),
    )
    out_specs = (
        P(("groups", "dp"), "tensor"),
        P(("groups", "dp"), "tensor"),
        P(("groups", "dp"), "tensor", None),
        P(("groups", "dp"), None, "tensor"),
    )

    def run(*args):
        return on_device(n_groups, n_dp, *args)

    return jax.shard_map(
        run, mesh=mesh, in_specs=in_specs, out_specs=out_specs, check_vma=False
    )
```

time: 345 us -> 117 us (0.34)
  waiting for transfers between devices: 218 us -> 25.6 us
  matrix products: 56.8 us -> 0 us
  Pallas kernels: 0 us -> 56.5 us
  blocking collectives: 38.6 us -> 0 us
  starting transfers between devices: 0.38 us -> 28.5 us
  between operations: 13.9 us -> 0.87 us
  local copies, waits for them, and re-layouts: 13.1 us -> 3.11 us
    reduce_scatter x3 -> x0, waiting for transfers between devices: 188 us -> none  [the longest x1 152 us: on_device(): lax.psum_scatter(dense_down, 'dp', scatter_dimension=0, tiled=True)]
    dot_general x10 -> x0, matrix products: 56.8 us -> none  [the longest x1 14.9 us: on_device(): lax.dot_general(lax.all_gather(flat_grad, 'tensor', axis=1, tiled=True),...]
    pallas_call x0 -> x12, Pallas kernels: none -> 56.5 us  [the longest x1 14.8 us: on_device(): _call(functools.partial(tokens_kernel, z), 1, (width // cut,), [_whole((r...]
    all_gather x1 -> x0, blocking collectives: 34.8 us -> none  [on_device(): lax.all_gather(adapter_up, 'dp', axis=0, tiled=True)]
    all_gather x2 -> x0, waiting for transfers between devices: 29.5 us -> none  [the longest x1 29.4 us: on_device(): lax.all_gather(adapter_down, 'dp', axis=0, tiled=True)]
    ppermute x0 -> x23, starting transfers between devices: none -> 28.5 us  [the longest x16 25.3 us: _xor(): return lax.ppermute(x, 'dp', [(i, i ^ k) for i in range(n)])]
    ppermute x0 -> x23, waiting for transfers between devices: none -> 25.6 us  [the longest x16 25.6 us: _xor(): return lax.ppermute(x, 'dp', [(i, i ^ k) for i in range(n)])]
    dot_general x2 -> x0, local copies, waits for them, and re-layouts: 9.74 us -> none  [the longest x1 8.14 us: on_device(): jnp.einsum('bs,bdr->sdr', slot_match, down_blocks, precision=highest)]
  transfers between devices with their start and end apart: 5 -> 23, of which waited for: 3 -> 5; matrix products, arithmetic and copies ran while one was open for 21% -> 2% of each run, Pallas kernels for 0% -> 48%
where the time goes in v2:
time: 117 us; the launch traced here: 116 us
  Pallas kernels  56.5 us (48%)
  starting transfers between devices  28.5 us (24%)
  waiting for transfers between devices  25.6 us (22%)
  local copies, waits for them, and re-layouts  3.11 us (3%)
  other arithmetic  1.93 us (2%)
    ppermute x16, waiting for transfers between devices, _xor(): return lax.ppermute(x, 'dp', [(i, i ^ k) for i in range(n)])  25.6 us
    ppermute x16, starting transfers between devices, _xor(): return lax.ppermute(x, 'dp', [(i, i ^ k) for i in range(n)])  25.3 us
    pallas_call x1, Pallas kernels, on_device(): _call(functools.partial(tokens_kernel, z), 1, (width // cut,), [_whole((r...  14.8 us
    pallas_call x1, Pallas kernels, on_device(): _call(functools.partial(projected_kernel, z), 1, (width // deep,), [pl.Bl...  9.13 us
    pallas_call x1, Pallas kernels, on_device(): _call(functools.partial(shrink_kernel, z), 1, (width // cut,), [pl.BlockS...  8.92 us
    pallas_call x1, Pallas kernels, on_device(): _call(other_kernel, 1, (width // deep,), [pl.BlockSpec((rows, deep), lamb...  7.33 us
    pallas_call x1, Pallas kernels, on_device(): _call(functools.partial(pack_kernel, z, NEAR), 1, (width // tile,), [_who...  6.12 us
    pallas_call x2, Pallas kernels, collect(): _call(functools.partial(dense_kernel, z), 1, (wide // cut,), [pl.BlockSpe...  4.75 us
  transfers between devices with their start and end apart: 23, of which 5 were waited for; matrix products, arithmetic and copies ran while one was open for 2% of the time, Pallas kernels for 48%

profile of v2, /device:TPU:0, one launch (start us, length us, event | category | flops | bytes accessed | tf_op | source)
XLA Modules:
  0.0 116.4 jit_solution(17356567297552278513)
XLA Ops:
  0.7 1.0 dynamic-slice_bitcast_fusion.1
  1.6 3.0 %collective-permute-start.6 = (bf16[4,16,1024]{2,1,0:T(8,128)(2,1)S(1)}, bf16[4,16,1024]{2,1,0:T(8,128)(2,1)S(1)}, u32[]{:S(2)}, u32[]{:S(2)}) collective-permute-start(bf16[4,16,1024]{2,1,0:T(8,128)(2,1)S(1)} %get-tuple-element.65), channel_id=1, source_target_pairs={{0,2},{2,0},{4,6},{6,4},{8,10},{10,8},{12,14},{14,12},{1,3},{3,1},... | collective-permute-start | bytes 393224 | tf_op jit(solution)/shard_map/ppermute | solution.py:34
  4.7 0.9 select_reduce_fusion
  5.5 1.5 %collective-permute-start = (s32[7]{0:T(128)S(1)}, s32[7]{0:T(128)S(1)}, u32[]{:S(2)}, u32[]{:S(2)}) collective-permute-start(s32[7]{0:T(128)S(1)} %select_reduce_fusion), channel_id=1, source_target_pairs={{0,16},{16,0},{1,17},{17,1},{2,18},{18,2},{3,19},{19,3},{4,20},{20... | collective-permute-start | bytes 92 | tf_op jit(solution)/shard_map/ppermute | solution.py:30
  7.1 2.6 %collective-permute-start.1 = (bf16[4,16,512]{2,1,0:T(8,128)(2,1)}, bf16[4,16,512]{2,1,0:T(8,128)(2,1)S(1)}, u32[]{:S(2)}, u32[]{:S(2)}) collective-permute-start(bf16[4,16,512]{2,1,0:T(8,128)(2,1)} %param.15), channel_id=1, source_target_pairs={{0,8},{2,10},{4,12},{6,14},{8,0},{10,2},{12,4},{14,6},{1,9},{3,11}... | collective-permute-start | bytes 196616 | tf_op jit(solution)/shard_map/ppermute | solution.py:34
  9.9 2.6 %collective-permute-done.1 = bf16[4,16,512]{2,1,0:T(8,128)(2,1)S(1)} collective-permute-done((bf16[4,16,512]{2,1,0:T(8,128)(2,1)}, bf16[4,16,512]{2,1,0:T(8,128)(2,1)S(1)}, u32[]{:S(2)}, u32[]{:S(2)}) %collective-permute-start.1) | collective-permute-done | bytes 65568 | tf_op jit(solution)/shard_map/ppermute | solution.py:34
  12.5 0.8 pad_maximum_fusion.3.refs_0_
  13.3 1.6 %collective-permute-start.4 = (bf16[144,512]{1,0:T(8,128)(2,1)S(1)}, bf16[144,512]{1,0:T(8,128)(2,1)S(1)}, u32[]{:S(2)}, u32[]{:S(2)}) collective-permute-start(bf16[144,512]{1,0:T(8,128)(2,1)S(1)} %pad_maximum_fusion.3.refs_0_), channel_id=1, source_target_pairs={{0,6},{2,4},{4,2},{6,0},{8,14},{10,12},{12,10},{14,8},{1,7},{3,5},... | collective-permute-start | bytes 442376 | tf_op jit(solution)/shard_map/ppermute | solution.py:34
  14.9 3.2 %collective-permute-start.7 = (bf16[8,16,1024]{2,1,0:T(8,128)(2,1)S(1)}, bf16[8,16,1024]{2,1,0:T(8,128)(2,1)S(1)}, u32[]{:S(2)}, u32[]{:S(2)}) collective-permute-start(bf16[8,16,1024]{2,1,0:T(8,128)(2,1)S(1)} %pad_maximum_fusion.2), channel_id=1, source_target_pairs={{0,8},{2,10},{4,12},{6,14},{8,0},{10,2},{12,4},{14,6},{1,9},{3,11}... | collective-permute-start | bytes 786440 | tf_op jit(solution)/shard_map/ppermute | solution.py:34
  18.2 1.5 %collective-permute-start.2 = (bf16[144,512]{1,0:T(8,128)(2,1)S(1)}, bf16[144,512]{1,0:T(8,128)(2,1)S(1)}, u32[]{:S(2)}, u32[]{:S(2)}) collective-permute-start(bf16[144,512]{1,0:T(8,128)(2,1)S(1)} %pad_maximum_fusion.3.refs_0_), channel_id=1, source_target_pairs={{0,2},{2,0},{4,6},{6,4},{8,10},{10,8},{12,14},{14,12},{1,3},{3,1},... | collective-permute-start | bytes 442376 | tf_op jit(solution)/shard_map/ppermute | solution.py:34
  19.7 2.4 %collective-permute-done.4.refs_3_ = bf16[144,512]{1,0:T(8,128)(2,1)S(1)} collective-permute-done((bf16[144,512]{1,0:T(8,128)(2,1)S(1)}, bf16[144,512]{1,0:T(8,128)(2,1)S(1)}, u32[]{:S(2)}, u32[]{:S(2)}) %collective-permute-start.4) | collective-permute-done | bytes 147488 | tf_op jit(solution)/shard_map/ppermute | solution.py:34
  22.1 6.0 %collective-permute-done.7 = bf16[8,16,1024]{2,1,0:T(8,128)(2,1)S(1)} collective-permute-done((bf16[8,16,1024]{2,1,0:T(8,128)(2,1)S(1)}, bf16[8,16,1024]{2,1,0:T(8,128)(2,1)S(1)}, u32[]{:S(2)}, u32[]{:S(2)}) %collective-permute-start.7) | collective-permute-done | bytes 262176 | tf_op jit(solution)/shard_map/ppermute | solution.py:34
  28.3 0.7 concatenate.18.info
  29.1 1.2 %copy-done = bf16[896,512]{1,0:T(8,128)(2,1)S(1)} copy-done((bf16[896,512]{1,0:T(8,128)(2,1)S(1)}, bf16[896,512]{1,0:T(8,128)(2,1)}, u32[]{:S(2)}) %copy-start) | copy-done | bytes 917528
  30.3 0.9 shard_map.114
  31.1 8.2 %collective-permute-done.8.far_ref = bf16[16,16,1024]{2,1,0:T(8,128)(2,1)S(1)} collective-permute-done((bf16[16,16,1024]{2,1,0:T(8,128)(2,1)S(1)}, bf16[16,16,1024]{2,1,0:T(8,128)(2,1)S(1)}, u32[]{:S(2)}, u32[]{:S(2)}) %collective-permute-start.8) | collective-permute-done | bytes 524320 | tf_op jit(solution)/shard_map/ppermute | solution.py:34
  39.3 1.1 shard_map.112
  40.5 3.1 %collective-permute-start.9 = (bf16[7,16,1024]{2,1,0:T(8,128)(2,1)S(1)}, bf16[7,16,1024]{2,1,0:T(8,128)(2,1)S(1)}, u32[]{:S(2)}, u32[]{:S(2)}) collective-permute-start(bf16[7,16,1024]{2,1,0:T(8,128)(2,1)S(1)} %get-tuple-element.47), channel_id=1, source_target_pairs={{0,2},{2,0},{4,6},{6,4},{8,10},{10,8},{12,14},{14,12},{1,3},{3,1},... | collective-permute-start | bytes 688136 | tf_op jit(solution)/shard_map/ppermute | solution.py:34
  44.2 6.1 %shard_map.117 = (bf16[64,4096]{1,0:T(8,128)(2,1)S(1)}, bf16[64,4096]{1,0:T(8,128)(2,1)S(1)}, bf16[64,4096]{1,0:T(8,128)(2,1)S(1)}, bf16[64,4096]{1,0:T(8,128)(2,1)S(1)}) custom-call(s32[52]{0:T(128)S(1)} %concatenate.18.info, f32[16,896]{1,0:T(8,128)S(1)} %get-tuple-element.51.mine_ref, f32[16,896]{1,0:T(8,128)S(1)} %collective-permute-done.14.other_ref, ...), custom_call_target="tpu_custom_call" | custom-call | flops 1879048192 | bytes 9437184 | tf_op jit(solution)/shard_map/pallas_call | solution.py:327
  50.7 3.1 %collective-permute-start.17 = (bf16[64,4096]{1,0:T(8,128)(2,1)S(1)}, bf16[64,4096]{1,0:T(8,128)(2,1)S(1)}, u32[]{:S(2)}, u32[]{:S(2)}) collective-permute-start(bf16[64,4096]{1,0:T(8,128)(2,1)S(1)} %get-tuple-element.55), channel_id=1, source_target_pairs={{0,6},{2,4},{4,2},{6,0},{8,14},{10,12},{12,10},{14,8},{1,7},{3,5},... | collective-permute-start | bytes 1572872 | tf_op jit(solution)/shard_map/ppermute | solution.py:34
  53.8 1.0 collective-permute-start.11
  54.8 7.3 %shard_map.111 = bf16[896,512]{1,0:T(8,128)(2,1)S(1)} custom-call(s32[1]{0:T(128)} %bitcast.11.info, bf16[896,4096]{1,0:T(8,128)(2,1)} %right_ref.1, bf16[4096,1024]{1,0:T(8,128)(2,1)} %w_ref.5), custom_call_target="tpu_custom_call" | custom-call | flops 3758096384 | bytes 11534336 | tf_op jit(solution)/shard_map/pallas_call | solution.py:361
  62.4 8.9 %shard_map.113.mine_ref = f32[16,896]{1,0:T(8,128)S(1)} custom-call(s32[52]{0:T(128)S(1)} %concatenate.18.info, bf16[896,4096]{1,0:T(8,128)(2,1)} %right_ref.1, bf16[4,7,16,1024]{3,2,1,0:T(8,128)(2,1)S(1)} %pad_maximum_fusion.d_ref), custom_call_target="tpu_custom_call" | custom-call | flops 939524096 | bytes 7340032 | tf_op jit(solution)/shard_map/pallas_call | solution.py:404
  71.3 6.3 %collective-permute-done.15.refs_1_ = bf16[64,4096]{1,0:T(8,128)(2,1)S(1)} collective-permute-done((bf16[64,4096]{1,0:T(8,128)(2,1)S(1)}, bf16[64,4096]{1,0:T(8,128)(2,1)S(1)}, u32[]{:S(2)}, u32[]{:S(2)}) %collective-permute-start.15) | collective-permute-done | bytes 524320 | tf_op jit(solution)/shard_map/ppermute | solution.py:34
  77.7 3.6 %shard_map.118 = (f32[64,4096]{1,0:T(8,128)S(1)}, bf16[64,4096]{1,0:T(8,128)(2,1)S(1)}) custom-call(s32[52]{0:T(128)S(1)} %concatenate.18.info, bf16[64,4096]{1,0:T(8,128)(2,1)S(1)} %get-tuple-element.52.refs_0_, bf16[64,4096]{1,0:T(8,128)(2,1)S(1)} %collective-permute-done.15.refs_1_, bf16[64,4096]{1,0:T(8,128)(2,1)S(1)} %collective-permute-done.16.refs_2_, ...), custom_call_target="tpu_custom_call" | custom-call | flops 134217728 | bytes 2097152 | tf_op jit(solution)/shard_map/pallas_call | solution.py:341
  81.4 1.1 shard_map.120
  83.4 2.6 %collective-permute-start.21 = (bf16[64,512]{1,0:T(8,128)(2,1)S(1)}, bf16[64,512]{1,0:T(8,128)(2,1)S(1)}, u32[]{:S(2)}, u32[]{:S(2)}) collective-permute-start(bf16[64,512]{1,0:T(8,128)(2,1)S(1)} %get-tuple-element.61), channel_id=1, source_target_pairs={{0,6},{2,4},{4,2},{6,0},{8,14},{10,12},{12,10},{14,8},{1,7},{3,5},... | collective-permute-start | bytes 196616 | tf_op jit(solution)/shard_map/ppermute | solution.py:34
  86.0 14.8 %shard_map.116 = bf16[896,4096]{1,0:T(8,128)(2,1)} custom-call(s32[52]{0:T(128)S(1)} %concatenate.18.info, bf16[896,512]{1,0:T(8,128)(2,1)S(1)} %copy-done.1, bf16[896,512]{1,0:T(8,128)(2,1)S(1)} %collective-permute-done.13.h_ref, bf16[4096,1024]{1,0:T(8,128)(2,1)} %w_ref.5, f32[16,896]{1,0:T(8,128)S(1)} %get-tuple-element.51.mine_ref, ...), custom_call_target="tpu_custom_call" | custom-call | flops 7516192768 | bytes 15728640 | tf_op jit(solution)/shard_map/pallas_call | solution.py:435
  100.9 1.2 shard_map.121
  102.0 3.0 %collective-permute-start.22 = (bf16[64,512]{1,0:T(8,128)(2,1)S(1)}, bf16[64,512]{1,0:T(8,128)(2,1)S(1)}, u32[]{:S(2)}, u32[]{:S(2)}) collective-permute-start(bf16[64,512]{1,0:T(8,128)(2,1)S(1)} %get-tuple-element.63), channel_id=1, source_target_pairs={{0,8},{2,10},{4,12},{6,14},{8,0},{10,2},{12,4},{14,6},{1,9},{3,11}... | collective-permute-start | bytes 196616 | tf_op jit(solution)/shard_map/ppermute | solution.py:34
  105.0 9.1 %shard_map.115 = bf16[896,512]{1,0:T(8,128)(2,1)} custom-call(s32[52]{0:T(128)S(1)} %concatenate.18.info, bf16[896,4096]{1,0:T(8,128)(2,1)} %right_ref.1, bf16[4096,1024]{1,0:T(8,128)(2,1)} %w_ref.5, bf16[896,512]{1,0:T(8,128)(2,1)S(1)} %collective-permute-done.5.base_ref, f32[16,896]{1,0:T(8,128)S(1)} %shard_map.113.mine_ref, ...), custom_call_target="tpu_custom_call" | custom-call | flops 3758096384 | bytes 11534336 | tf_op jit(solution)/shard_map/pallas_call | solution.py:422
  114.1 1.6 %shard_map.119 = f32[64,4096]{1,0:T(8,128)} custom-call(f32[64,4096]{1,0:T(8,128)S(1)} %get-tuple-element.56.near_ref, bf16[64,4096]{1,0:T(8,128)(2,1)S(1)} %collective-permute-done.18.refs_0_), custom_call_target="tpu_custom_call" | custom-call | flops 262144 | bytes 2621440 | tf_op jit(solution)/shard_map/pallas_call | solution.py:351
  (47 shorter events, 3.3 us)
Async XLA Ops:
  1.6 13.3 %collective-permute-start.6 = (bf16[4,16,1024]{2,1,0:T(8,128)(2,1)S(1)}, bf16[4,16,1024]{2,1,0:T(8,128)(2,1)S(1)}, u32[]{:S(2)}, u32[]{:S(2)}) collective-permute-start(bf16[4,16,1024]{2,1,0:T(8,128)(2,1)S(1)} %get-tuple-element.65), channel_id=1, source_target_pairs={{0,2},{2,0},{4,6},{6,4},{8,10},{10,8},{12,14},{14,12},{1,3},{3,1},... | collective-permute-start | bytes 393224 | tf_op jit(solution)/shard_map/ppermute | solution.py:34
  5.5 4.2 %collective-permute-start = (s32[7]{0:T(128)S(1)}, s32[7]{0:T(128)S(1)}, u32[]{:S(2)}, u32[]{:S(2)}) collective-permute-start(s32[7]{0:T(128)S(1)} %select_reduce_fusion), channel_id=1, source_target_pairs={{0,16},{16,0},{1,17},{17,1},{2,18},{18,2},{3,19},{19,3},{4,20},{20... | collective-permute-start | bytes 92 | tf_op jit(solution)/shard_map/ppermute | solution.py:30
  7.1 5.4 %collective-permute-start.1 = (bf16[4,16,512]{2,1,0:T(8,128)(2,1)}, bf16[4,16,512]{2,1,0:T(8,128)(2,1)S(1)}, u32[]{:S(2)}, u32[]{:S(2)}) collective-permute-start(bf16[4,16,512]{2,1,0:T(8,128)(2,1)} %param.15), channel_id=1, source_target_pairs={{0,8},{2,10},{4,12},{6,14},{8,0},{10,2},{12,4},{14,6},{1,9},{3,11}... | collective-permute-start | bytes 196616 | tf_op jit(solution)/shard_map/ppermute | solution.py:34
  9.7 73.7 %collective-permute-start.13 = (bf16[896,512]{1,0:T(8,128)(2,1)}, bf16[896,512]{1,0:T(8,128)(2,1)S(1)}, u32[]{:S(2)}, u32[]{:S(2)}) collective-permute-start(bf16[896,512]{1,0:T(8,128)(2,1)} %g_ref.5), channel_id=1, source_target_pairs={{0,1},{1,0},{2,3},{3,2},{4,5},{5,4},{6,7},{7,6},{8,9},{9,8},{10,11... | collective-permute-start | bytes 2752520 | tf_op jit(solution)/shard_map/ppermute | solution.py:30
  13.3 8.7 %collective-permute-start.4 = (bf16[144,512]{1,0:T(8,128)(2,1)S(1)}, bf16[144,512]{1,0:T(8,128)(2,1)S(1)}, u32[]{:S(2)}, u32[]{:S(2)}) collective-permute-start(bf16[144,512]{1,0:T(8,128)(2,1)S(1)} %pad_maximum_fusion.3.refs_0_), channel_id=1, source_target_pairs={{0,6},{2,4},{4,2},{6,0},{8,14},{10,12},{12,10},{14,8},{1,7},{3,5},... | collective-permute-start | bytes 442376 | tf_op jit(solution)/shard_map/ppermute | solution.py:34
  14.9 13.2 %collective-permute-start.7 = (bf16[8,16,1024]{2,1,0:T(8,128)(2,1)S(1)}, bf16[8,16,1024]{2,1,0:T(8,128)(2,1)S(1)}, u32[]{:S(2)}, u32[]{:S(2)}) collective-permute-start(bf16[8,16,1024]{2,1,0:T(8,128)(2,1)S(1)} %pad_maximum_fusion.2), channel_id=1, source_target_pairs={{0,8},{2,10},{4,12},{6,14},{8,0},{10,2},{12,4},{14,6},{1,9},{3,11}... | collective-permute-start | bytes 786440 | tf_op jit(solution)/shard_map/ppermute | solution.py:34
  18.2 10.1 %collective-permute-start.2 = (bf16[144,512]{1,0:T(8,128)(2,1)S(1)}, bf16[144,512]{1,0:T(8,128)(2,1)S(1)}, u32[]{:S(2)}, u32[]{:S(2)}) collective-permute-start(bf16[144,512]{1,0:T(8,128)(2,1)S(1)} %pad_maximum_fusion.3.refs_0_), channel_id=1, source_target_pairs={{0,2},{2,0},{4,6},{6,4},{8,10},{10,8},{12,14},{14,12},{1,3},{3,1},... | collective-permute-start | bytes 442376 | tf_op jit(solution)/shard_map/ppermute | solution.py:34
  19.7 8.6 %collective-permute-start.3 = (bf16[144,512]{1,0:T(8,128)(2,1)S(1)}, bf16[144,512]{1,0:T(8,128)(2,1)S(1)}, u32[]{:S(2)}, u32[]{:S(2)}) collective-permute-start(bf16[144,512]{1,0:T(8,128)(2,1)S(1)} %pad_maximum_fusion.3.refs_0_), channel_id=1, source_target_pairs={{0,4},{2,6},{4,0},{6,2},{8,12},{10,14},{12,8},{14,10},{1,5},{3,7},... | collective-permute-start | bytes 442376 | tf_op jit(solution)/shard_map/ppermute | solution.py:34
  28.2 11.2 %collective-permute-start.8 = (bf16[16,16,1024]{2,1,0:T(8,128)(2,1)S(1)}, bf16[16,16,1024]{2,1,0:T(8,128)(2,1)S(1)}, u32[]{:S(2)}, u32[]{:S(2)}) collective-permute-start(bf16[16,16,1024]{2,1,0:T(8,128)(2,1)S(1)} %pad_maximum_fusion.1.pair_ref), channel_id=1, source_target_pairs={{0,4},{2,6},{4,0},{6,2},{8,12},{10,14},{12,8},{14,10},{1,5},{3,7},... | collective-permute-start | bytes 1572872 | tf_op jit(solution)/shard_map/ppermute | solution.py:34
  29.1 1.2 %copy-start = (bf16[896,512]{1,0:T(8,128)(2,1)S(1)}, bf16[896,512]{1,0:T(8,128)(2,1)}, u32[]{:S(2)}) copy-start(bf16[896,512]{1,0:T(8,128)(2,1)} %g_ref.5) | copy-start | bytes 2752516
  31.1 13.0 %collective-permute-start.14 = (f32[16,896]{1,0:T(8,128)S(1)}, f32[16,896]{1,0:T(8,128)S(1)}, u32[]{:S(2)}, u32[]{:S(2)}) collective-permute-start(f32[16,896]{1,0:T(8,128)S(1)} %get-tuple-element.51.mine_ref), channel_id=1, source_target_pairs={{0,1},{1,0},{2,3},{3,2},{4,5},{5,4},{6,7},{7,6},{8,9},{9,8},{10,11... | collective-permute-start | bytes 172040 | tf_op jit(solution)/shard_map/ppermute | solution.py:30
  40.5 10.2 %collective-permute-start.9 = (bf16[7,16,1024]{2,1,0:T(8,128)(2,1)S(1)}, bf16[7,16,1024]{2,1,0:T(8,128)(2,1)S(1)}, u32[]{:S(2)}, u32[]{:S(2)}) collective-permute-start(bf16[7,16,1024]{2,1,0:T(8,128)(2,1)S(1)} %get-tuple-element.47), channel_id=1, source_target_pairs={{0,2},{2,0},{4,6},{6,4},{8,10},{10,8},{12,14},{14,12},{1,3},{3,1},... | collective-permute-start | bytes 688136 | tf_op jit(solution)/shard_map/ppermute | solution.py:34
  43.6 10.2 %collective-permute-start.10 = (bf16[7,16,1024]{2,1,0:T(8,128)(2,1)S(1)}, bf16[7,16,1024]{2,1,0:T(8,128)(2,1)S(1)}, u32[]{:S(2)}, u32[]{:S(2)}) collective-permute-start(bf16[7,16,1024]{2,1,0:T(8,128)(2,1)S(1)} %get-tuple-element.48), channel_id=1, source_target_pairs={{0,16},{16,0},{1,17},{17,1},{2,18},{18,2},{3,19},{19,3},{4,20},{20... | collective-permute-start | bytes 688136 | tf_op jit(solution)/shard_map/ppermute | solution.py:30
  50.3 27.4 %collective-permute-start.15 = (bf16[64,4096]{1,0:T(8,128)(2,1)S(1)}, bf16[64,4096]{1,0:T(8,128)(2,1)S(1)}, u32[]{:S(2)}, u32[]{:S(2)}) collective-permute-start(bf16[64,4096]{1,0:T(8,128)(2,1)S(1)} %get-tuple-element.53), channel_id=1, source_target_pairs={{0,2},{2,0},{4,6},{6,4},{8,10},{10,8},{12,14},{14,12},{1,3},{3,1},... | collective-permute-start | bytes 1572872 | tf_op jit(solution)/shard_map/ppermute | solution.py:34
  50.4 27.3 %collective-permute-start.16 = (bf16[64,4096]{1,0:T(8,128)(2,1)S(1)}, bf16[64,4096]{1,0:T(8,128)(2,1)S(1)}, u32[]{:S(2)}, u32[]{:S(2)}) collective-permute-start(bf16[64,4096]{1,0:T(8,128)(2,1)S(1)} %get-tuple-element.54), channel_id=1, source_target_pairs={{0,4},{2,6},{4,0},{6,2},{8,12},{10,14},{12,8},{14,10},{1,5},{3,7},... | collective-permute-start | bytes 1572872 | tf_op jit(solution)/shard_map/ppermute | solution.py:34
  50.7 27.0 %collective-permute-start.17 = (bf16[64,4096]{1,0:T(8,128)(2,1)S(1)}, bf16[64,4096]{1,0:T(8,128)(2,1)S(1)}, u32[]{:S(2)}, u32[]{:S(2)}) collective-permute-start(bf16[64,4096]{1,0:T(8,128)(2,1)S(1)} %get-tuple-element.55), channel_id=1, source_target_pairs={{0,6},{2,4},{4,2},{6,0},{8,14},{10,12},{12,10},{14,8},{1,7},{3,5},... | collective-permute-start | bytes 1572872 | tf_op jit(solution)/shard_map/ppermute | solution.py:34
  53.8 8.4 %collective-permute-start.11 = (bf16[7,16,1024]{2,1,0:T(8,128)(2,1)S(1)}, bf16[7,16,1024]{2,1,0:T(8,128)(2,1)S(1)}, u32[]{:S(2)}, u32[]{:S(2)}) collective-permute-start(bf16[7,16,1024]{2,1,0:T(8,128)(2,1)S(1)} %get-tuple-element.49), channel_id=1, source_target_pairs={{0,18},{2,16},{4,22},{6,20},{8,26},{10,24},{12,30},{14,28},{16,2},... | collective-permute-start | bytes 688136 | tf_op jit(solution)/shard_map/ppermute | solution.py:386
  62.2 19.2 %copy-start.1 = (bf16[896,512]{1,0:T(8,128)(2,1)S(1)}, bf16[896,512]{1,0:T(8,128)(2,1)}, u32[]{:S(2)}) copy-start(bf16[896,512]{1,0:T(8,128)(2,1)} %g_ref.5) | copy-start | bytes 2752516
  62.2 42.8 %collective-permute-start.5 = (bf16[896,512]{1,0:T(8,128)(2,1)S(1)}, bf16[896,512]{1,0:T(8,128)(2,1)S(1)}, u32[]{:S(2)}, u32[]{:S(2)}) collective-permute-start(bf16[896,512]{1,0:T(8,128)(2,1)S(1)} %shard_map.111), channel_id=1, source_target_pairs={{0,1},{1,0},{2,3},{3,2},{4,5},{5,4},{6,7},{7,6},{8,9},{9,8},{10,11... | collective-permute-start | bytes 2752520 | tf_op jit(solution)/shard_map/ppermute | solution.py:30
  77.7 3.7 %collective-permute-start.12 = (f32[16,896]{1,0:T(8,128)S(1)}, f32[16,896]{1,0:T(8,128)S(1)}, u32[]{:S(2)}, u32[]{:S(2)}) collective-permute-start(f32[16,896]{1,0:T(8,128)S(1)} %shard_map.113.mine_ref), channel_id=1, source_target_pairs={{0,1},{1,0},{2,3},{3,2},{4,5},{5,4},{6,7},{7,6},{8,9},{9,8},{10,11... | collective-permute-start | bytes 172040 | tf_op jit(solution)/shard_map/ppermute | solution.py:30
  81.3 32.8 %collective-permute-start.18 = (bf16[64,4096]{1,0:T(8,128)(2,1)S(1)}, bf16[64,4096]{1,0:T(8,128)(2,1)S(1)}, u32[]{:S(2)}, u32[]{:S(2)}) collective-permute-start(bf16[64,4096]{1,0:T(8,128)(2,1)S(1)} %get-tuple-element.57), channel_id=1, source_target_pairs={{0,8},{2,10},{4,12},{6,14},{8,0},{10,2},{12,4},{14,6},{1,9},{3,11}... | collective-permute-start | bytes 1572872 | tf_op jit(solution)/shard_map/ppermute | solution.py:34
  82.5 18.4 %collective-permute-start.19 = (bf16[64,512]{1,0:T(8,128)(2,1)S(1)}, bf16[64,512]{1,0:T(8,128)(2,1)S(1)}, u32[]{:S(2)}, u32[]{:S(2)}) collective-permute-start(bf16[64,512]{1,0:T(8,128)(2,1)S(1)} %get-tuple-element.59), channel_id=1, source_target_pairs={{0,2},{2,0},{4,6},{6,4},{8,10},{10,8},{12,14},{14,12},{1,3},{3,1},... | collective-permute-start | bytes 196616 | tf_op jit(solution)/shard_map/ppermute | solution.py:34
  82.9 18.0 %collective-permute-start.20 = (bf16[64,512]{1,0:T(8,128)(2,1)S(1)}, bf16[64,512]{1,0:T(8,128)(2,1)S(1)}, u32[]{:S(2)}, u32[]{:S(2)}) collective-permute-start(bf16[64,512]{1,0:T(8,128)(2,1)S(1)} %get-tuple-element.60), channel_id=1, source_target_pairs={{0,4},{2,6},{4,0},{6,2},{8,12},{10,14},{12,8},{14,10},{1,5},{3,7},... | collective-permute-start | bytes 196616 | tf_op jit(solution)/shard_map/ppermute | solution.py:34
  83.4 17.4 %collective-permute-start.21 = (bf16[64,512]{1,0:T(8,128)(2,1)S(1)}, bf16[64,512]{1,0:T(8,128)(2,1)S(1)}, u32[]{:S(2)}, u32[]{:S(2)}) collective-permute-start(bf16[64,512]{1,0:T(8,128)(2,1)S(1)} %get-tuple-element.61), channel_id=1, source_target_pairs={{0,6},{2,4},{4,2},{6,0},{8,14},{10,12},{12,10},{14,8},{1,7},{3,5},... | collective-permute-start | bytes 196616 | tf_op jit(solution)/shard_map/ppermute | solution.py:34
  102.0 13.8 %collective-permute-start.22 = (bf16[64,512]{1,0:T(8,128)(2,1)S(1)}, bf16[64,512]{1,0:T(8,128)(2,1)S(1)}, u32[]{:S(2)}, u32[]{:S(2)}) collective-permute-start(bf16[64,512]{1,0:T(8,128)(2,1)S(1)} %get-tuple-element.63), channel_id=1, source_target_pairs={{0,8},{2,10},{4,12},{6,14},{8,0},{10,2},{12,4},{14,6},{1,9},{3,11}... | collective-permute-start | bytes 196616 | tf_op jit(solution)/shard_map/ppermute | solution.py:34

commit v3 on v2

v3 whole, which is shorter than its diff:
```python
import functools

import jax
import jax.numpy as jnp
from jax import lax
from jax.experimental import pallas as pl
from jax.experimental.pallas import tpu as pltpu
from jax.sharding import PartitionSpec as P

TENANT_BLOCK = 128
CAP = 2
NEAR = 4
VMEM_LIMIT = 24 * 1024 * 1024

adapter_scale = 2.0
f32 = jnp.float32
bf16 = jnp.bfloat16
i32 = jnp.int32

NT = (((1,), (1,)), ((), ()))
TN = (((0,), (0,)), ((), ()))
NN = (((1,), (0,)), ((), ()))


def _dot(a, b, dims):
    return lax.dot_general(a, b, dims, preferred_element_type=f32)


def _swap(x, axis):
    return lax.ppermute(x, axis, [(0, 1), (1, 0)])


def _xor(x, n, k):
    return lax.ppermute(x, "dp", [(i, i ^ k) for i in range(n)])


def _tie(x, *after):
    return lax.optimization_barrier((x,) + after)[0]


def _div(a, n):
    return a >> (n.bit_length() - 1) if n & (n - 1) == 0 else lax.div(a, jnp.int32(n))


def _rem(a, n):
    return a & (n - 1) if n & (n - 1) == 0 else lax.rem(a, jnp.int32(n))


VMEM = pl.BlockSpec(memory_space=pltpu.VMEM)


def _shape(shape, dtype):
    return jax.ShapeDtypeStruct(shape, dtype)


def _call(body, name, grid, in_specs, out_specs, out_shape, scratch, flops, moved, aliases=None):
    return pl.pallas_call(
        body,
        name=name,
        grid_spec=pltpu.PrefetchScalarGridSpec(
            num_scalar_prefetch=1,
            grid=grid,
            in_specs=in_specs,
            out_specs=out_specs,
            scratch_shapes=scratch,
        ),
        out_shape=out_shape,
        input_output_aliases=aliases or {},
        compiler_params=pltpu.CompilerParams(vmem_limit_bytes=VMEM_LIMIT),
        cost_estimate=pl.CostEstimate(flops=flops, bytes_accessed=moved, transcendentals=0),
    )


def _whole(shape):
    return pl.BlockSpec(shape, lambda *_: (0,) * len(shape))


class Sizes:
    def __init__(self, n_dp, nb, ten_dev, rank, cols, width):
        self.n_dp, self.nb, self.ten_dev = n_dp, nb, ten_dev
        self.rank, self.cols, self.width = rank, cols, width
        self.n_far = n_dp // NEAR
        self.rows = nb * TENANT_BLOCK
        self.me, self.core, self.quarter = 6 * nb, 6 * nb + 1, 6 * nb + 2
        self.valid = 6 * nb + 3

    def block(self, b):
        return slice(b * TENANT_BLOCK, (b + 1) * TENANT_BLOCK)

    def ranks(self, b):
        return slice(b * self.rank, (b + 1) * self.rank)

    def slot(self, info, which, b):
        return info[which * self.nb + b]

    def owner_and_order(self, info, which):
        owners = [_div(self.slot(info, which, b), self.ten_dev) for b in range(self.nb)]
        orders = []
        for b in range(self.nb):
            n = jnp.int32(0)
            for c in range(b):
                n = n + jnp.where(owners[c] == owners[b], 1, 0)
            orders.append(n)
        return owners, orders

    def places(self, info):
        owners, orders = self.owner_and_order(info, 0)
        out = []
        for o, r in zip(owners, orders):
            rel = o ^ info[self.me]
            place = (_rem(rel, NEAR) * self.n_far + _div(rel, NEAR)) * CAP + r
            out.append(pl.ds(pl.multiple_of(place * self.rank, self.rank), self.rank))
        return out


def _masked(x, valid):
    row = lax.broadcasted_iota(i32, x.shape, 0)
    return jnp.where(row < valid, x, jnp.zeros((), x.dtype))


def other_kernel(z, me, x_ref, w_ref, out_ref):
    far = pl.ds(pl.multiple_of((1 - me[0]) * z.cols, z.cols), z.cols)
    out_ref[...] = _dot(x_ref[...], w_ref[:, far], NN).astype(bf16)


def own_kernel(z, info, x_ref, w_ref, g_ref, h_ref, out_ref, full_ref):
    own = pl.ds(pl.multiple_of(info[z.core] * z.cols, z.cols), z.cols)
    far = pl.ds(pl.multiple_of((1 - info[z.core]) * z.cols, z.cols), z.cols)
    out_ref[...] = _dot(x_ref[...], w_ref[:, own], NN)
    for b in range(z.nb):
        cut = z.block(b)
        full_ref[cut, own] = _masked(g_ref[cut, :], info[z.valid + b])
        full_ref[cut, far] = _masked(h_ref[cut, :], info[z.valid + b])


def back_kernel(z, info, g_ref, *refs):
    packets, (up_ref, part_ref) = refs[:NEAR], refs[NEAR:]
    for b in range(z.nb):
        s = z.slot(info, 0, b)
        rel = _div(s, z.ten_dev) ^ info[z.me]
        at = _div(rel, NEAR) * z.ten_dev + _rem(s, z.ten_dev)
        at = pl.ds(pl.multiple_of(at * z.rank, z.rank), z.rank)
        near = _rem(rel, NEAR)
        u = packets[0][at, :]
        for k in range(1, NEAR):
            u = jnp.where(near == k, packets[k][at, :], u)
        up_ref[z.ranks(b), :] = u
        g = _masked(g_ref[z.block(b), :], info[z.valid + b])
        part_ref[:, z.block(b)] = _dot(u, g, NT)


def pack_kernel(z, n_out, start, info, mine_ref, other_ref, x_ref, *refs):
    outs, packed = refs[:n_out], refs[n_out]
    packed[...] = jnp.zeros_like(packed)
    for b, place in enumerate(z.places(info)):
        cut = z.block(b)
        v = (mine_ref[:, cut] + other_ref[:, cut]) * adapter_scale
        packed[place, cut] = v.astype(bf16)
    wide = outs[0].shape[1]
    res = _dot(packed[...], x_ref[:, start : start + wide], NN).astype(bf16)
    each = res.shape[0] // n_out
    for k in range(n_out):
        outs[k][...] = res[k * each : (k + 1) * each]


def pack_up_kernel(z, n_out, info, mine_ref, other_ref, g_ref, *refs):
    outs, packed = refs[:n_out], refs[n_out]
    own = pl.ds(pl.multiple_of(info[z.core] * z.cols, z.cols), z.cols)
    packed[...] = jnp.zeros_like(packed)
    for b, place in enumerate(z.places(info)):
        cut = z.block(b)
        packed[place, cut] = (mine_ref[:, cut] + other_ref[:, cut]).astype(bf16)
    res = (adapter_scale * _dot(packed[...], g_ref[:, own], NN)).astype(bf16)
    each = res.shape[0] // n_out
    for k in range(n_out):
        outs[k][...] = res[k * each : (k + 1) * each]


def dense_kernel(z, info, *refs):
    got, near_ref, far_refs = refs[:NEAR], refs[NEAR], refs[NEAR + 1 :]
    n = CAP * z.rank
    shape = (z.ten_dev * z.rank, n)
    row = lax.broadcasted_iota(i32, shape, 0)
    col = lax.broadcasted_iota(i32, shape, 1)
    same = _rem(row, z.rank) == _rem(col, z.rank)
    row_slot = _div(row, z.rank)
    tables = [z.owner_and_order(info, k) for k in range(NEAR)]
    for j in range(z.n_far):
        holder = info[z.me] ^ (NEAR * j)
        total = None
        for k in range(NEAR):
            owners, orders = tables[k]
            local = []
            for r in range(CAP):
                found = jnp.int32(0)
                for b in range(z.nb):
                    hit = (owners[b] == holder) & (orders[b] == r)
                    found = jnp.where(hit, _rem(z.slot(info, k, b), z.ten_dev), found)
                local.append(found)
            wanted = jnp.where(col < z.rank, local[0], local[1])
            one_hot = jnp.where(same & (row_slot == wanted), 1.0, 0.0).astype(bf16)
            term = _dot(one_hot, got[k][j * n : (j + 1) * n, :], NN)
            total = term if total is None else total + term
        if j == 0:
            near_ref[...] = total
        else:
            far_refs[j - 1][...] = total.astype(bf16)


def final_kernel(n_parts, n_far, info, *refs):
    out = refs[-1]
    at = 0
    for p in range(n_parts):
        near, far = refs[p * n_far], refs[p * n_far + 1 : (p + 1) * n_far]
        total = near[...]
        for r in far:
            total = total + r[...].astype(f32)
        out[:, at : at + total.shape[1]] = total
        at += total.shape[1]


def choose_kernel(z, info, own_ref, near_ref, far_ref, farther_ref, *outs):
    sources = (own_ref, near_ref, far_ref, farther_ref)
    for which, out in zip((0, 1, 4, 5), outs):
        for b in range(z.nb):
            s = z.slot(info, which, b)
            rel = _div(s, z.ten_dev) ^ info[z.me]
            at = _rem(rel, 2) * z.ten_dev + _rem(s, z.ten_dev)
            line = _div(rel, 2)
            v = sources[0][at]
            for k in range(1, 4):
                v = jnp.where(line == k, sources[k][at], v)
            out[z.ranks(b), :] = v


def shrink_kernel(z, n_parts, info, x_ref, *refs):
    parts, (full_ref, out_ref) = refs[:n_parts], refs[n_parts:]
    wide = z.width // n_parts
    total = None
    for j in range(n_parts):
        if n_parts == 1:
            cut = slice(0, wide)
        else:
            cut = pl.ds(pl.multiple_of((info[z.quarter] ^ j) * wide, wide), wide)
        full_ref[:, cut] = parts[j][...]
        term = _dot(x_ref[:, cut], parts[j][...], NT)
        total = term if total is None else total + term
    for b in range(z.nb):
        out_ref[:, z.block(b)] = total[z.block(b), :].T[z.ranks(b), :]


def projected_kernel(z, info, base_ref, far_ref, mine_ref, other_ref, up_ref, out_ref, spread):
    spread[...] = jnp.zeros_like(spread)
    for b in range(z.nb):
        cut = z.block(b)
        spread[z.ranks(b), cut] = (mine_ref[:, cut] + other_ref[:, cut]).astype(bf16)
    wide = _dot(spread[...], up_ref[...], TN)
    for b in range(z.nb):
        cut = z.block(b)
        full = base_ref[cut, :] + far_ref[cut, :].astype(f32) + adapter_scale * wide[cut]
        out_ref[cut, :] = _masked(full, info[z.valid + b]).astype(bf16)


def tokens_kernel(z, first, info, g_ref, w_ref, mine_ref, other_ref, d_ref, *refs):
    out_ref, spread = refs[-2:]
    step = pl.program_id(0)

    @pl.when(step == 0)
    def _():
        spread[...] = jnp.zeros_like(spread)
        for b in range(z.nb):
            cut = z.block(b)
            v = (mine_ref[:, cut] + other_ref[:, cut]) * adapter_scale
            spread[z.ranks(b), cut] = v.astype(bf16)

    wide = out_ref.shape[1]
    cut = pl.ds(pl.multiple_of((first + step) * wide, wide), wide)
    through = _dot(g_ref[...], w_ref[cut, :], NT)
    out_ref[...] = (through + _dot(spread[...], d_ref[:, cut], TN)).astype(bf16)


def on_device(
    n_groups,
    n_dp,
    tokens,
    base_weight,
    adapter_down,
    adapter_up,
    out_cotangent,
    block_tenant,
    block_valid,
    tenant_slot,
):
    nb = block_tenant.shape[0]
    rows, width = tokens.shape
    cols = out_cotangent.shape[1]
    tenants = tenant_slot.shape[0]
    ten_dev, _, rank = adapter_down.shape
    z = Sizes(n_dp, nb, ten_dev, rank, cols, width)
    n_far = z.n_far
    me = lax.axis_index("dp")
    core = lax.axis_index("tensor")
    group = lax.axis_index("groups")
    shared = n_groups == 2 and n_dp == 8
    n_parts = 4 if shared else 1
    mine_q = group * 2 + me % 2 if shared else jnp.int32(0)
    quarter = width // n_parts

    far_up = [_xor(adapter_up, n_dp, NEAR * j) for j in range(1, n_far)]
    down_t = jnp.swapaxes(adapter_down, 1, 2)
    if shared:
        to_y = lax.dynamic_slice_in_dim(down_t, (mine_q ^ 1) * quarter, quarter, axis=2)
        from_y = _xor(to_y, n_dp, 1)
    tenant_match = block_tenant[:, None] == jnp.arange(tenants, dtype=i32)[None, :]
    slots = jnp.sum(jnp.where(tenant_match, tenant_slot[None, :], 0), axis=1).astype(i32)
    slots_x = _swap(slots, "groups") if shared else slots
    cotangent_other = _swap(out_cotangent, "tensor")

    tag = jnp.zeros((16, cols), bf16)
    tag = tag.at[0, :nb].set(slots.astype(bf16)).at[1, :nb].set(slots_x.astype(bf16))
    ups = [u.reshape(ten_dev * rank, cols) for u in [adapter_up] + far_up]
    packet = jnp.concatenate(ups + [tag], axis=0)
    packets = [packet] + [_xor(packet, n_dp, k) for k in range(1, NEAR)]

    gate = packet
    if shared:
        own = lax.dynamic_slice_in_dim(down_t, mine_q * quarter, quarter, axis=2)
        shard = _tie(jnp.concatenate([own, from_y], axis=0), packet)
        shard_far = _xor(shard, n_dp, 4)
        shard_near = _xor(shard, n_dp, 2)
        gate = shard

    base_other = _call(
        functools.partial(other_kernel, z), "base_other", (1,),
        [VMEM, VMEM], _whole((rows, cols)), _shape((rows, cols), bf16), [],
        2 * rows * cols * width, 2 * rows * cols,
    )(_tie(jnp.full((1,), core, i32), gate), tokens, base_weight)
    base_arrived = _swap(base_other, "tensor")

    tags = [p[-16:-14, :nb].astype(i32) for p in packets]
    info = jnp.concatenate(
        [tags[k][0] for k in range(NEAR)]
        + [tags[0][1], tags[1][1], jnp.stack([me, core, mine_q]), block_valid]
    ).astype(i32)

    part = (rank, rows)
    block_up, back_part = _call(
        functools.partial(back_kernel, z), "back", (1,),
        [VMEM] * (1 + NEAR), [VMEM, _whole(part)],
        [_shape((nb * rank, cols), bf16), _shape(part, f32)], [],
        2 * rows * cols * rank * 8, 2 * rows * cols,
    )(_tie(info, base_other), out_cotangent, *packets)
    back_other = _swap(back_part, "tensor")

    packed_rows = n_dp * CAP * rank
    near_rows = packed_rows // NEAR

    def pack(info, start, wide):
        return _call(
            functools.partial(pack_kernel, z, NEAR, start), "pack_down", (1,),
            [VMEM] * 3, [_whole((near_rows, wide))] * NEAR,
            [_shape((near_rows, wide), bf16)] * NEAR,
            [pltpu.VMEM((packed_rows, rows), bf16)],
            2 * packed_rows * rows * wide, 2 * packed_rows * wide,
        )(info, back_part, back_other, tokens)

    def to_near(sends):
        return [sends[0]] + [_xor(sends[k], n_dp, k) for k in range(1, NEAR)]

    def dense(info, got):
        wide = got[0].shape[1]
        out = (ten_dev * rank, wide)
        return _call(
            functools.partial(dense_kernel, z), "dense", (1,),
            [VMEM] * NEAR, [VMEM] + [_whole(out)] * (n_far - 1),
            [_shape(out, f32)] + [_shape(out, bf16)] * (n_far - 1), [],
            2 * packed_rows * ten_dev * rank * wide, 2 * packed_rows * wide,
        )(info, *got)

    def to_far(parts):
        return [parts[0]] + [_xor(parts[j], n_dp, NEAR * j) for j in range(1, n_far)]

    def final(groups):
        wide = sum(g[0].shape[1] for g in groups)
        out = (ten_dev * rank, wide)
        total = _call(
            functools.partial(final_kernel, len(groups), n_far), "final", (1,),
            [VMEM] * (len(groups) * n_far), _whole(out), _shape(out, f32), [],
            ten_dev * rank * wide, 10 * ten_dev * rank * wide,
        )(info, *[a for g in groups for a in g])
        return total.reshape(ten_dev, rank, wide)

    half = width // 2
    sends_a = pack(info, 0, half)
    got_a = to_near(sends_a)
    sends_b = pack(_tie(info, sends_a[0]), half, half)
    got_b = to_near(sends_b)

    if shared:
        farther = _xor(_tie(shard_far, sends_b[0]), n_dp, 2)

    base_own, g_full = _call(
        functools.partial(own_kernel, z), "base_own", (1,),
        [VMEM] * 4, [VMEM, VMEM],
        [_shape((rows, cols), f32), _shape((rows, 2 * cols), bf16)], [],
        2 * rows * cols * width, 12 * rows * cols,
    )(_tie(info, sends_b[0]), tokens, base_weight, out_cotangent, cotangent_other)

    if shared:
        block = (nb * rank, quarter)
        chosen = _call(
            functools.partial(choose_kernel, z), "choose", (1,),
            [VMEM] * 4, [_whole(block)] * 4, [_shape(block, bf16)] * 4, [],
            0, 4 * shard.size,
        )(_tie(info, base_own), shard, shard_near, shard_far, farther)
        got_down = [
            chosen[0],
            _xor(chosen[1], n_dp, 1),
            _swap(chosen[2], "groups"),
            lax.ppermute(
                chosen[3],
                ("groups", "dp"),
                [(g * n_dp + d, (1 - g) * n_dp + (d ^ 1)) for g in range(2) for d in range(n_dp)],
            ),
        ]
        after_choose = chosen[0]
    else:
        every = lax.all_gather(down_t, "dp", axis=0, tiled=True)
        got_down = [jnp.take(every, slots, axis=0).reshape(nb * rank, width)]
        after_choose = base_own

    dense_a = dense(_tie(info, after_choose), got_a)
    far_a = to_far(dense_a)

    block_down, shrink_part = _call(
        functools.partial(shrink_kernel, z, n_parts), "shrink", (1,),
        [VMEM] * (1 + n_parts), [VMEM, _whole(part)],
        [_shape((nb * rank, width), bf16), _shape(part, f32)], [],
        2 * rows * width * 128, 2 * nb * rank * width,
    )(_tie(info, dense_a[1]), tokens, *got_down)
    shrink_other = _swap(shrink_part, "tensor")

    dense_b = dense(_tie(info, shrink_part), got_b)
    far_b = to_far(dense_b)

    up_sends = _call(
        functools.partial(pack_up_kernel, z, NEAR), "pack_up", (1,),
        [VMEM] * 3, [_whole((near_rows, cols))] * NEAR,
        [_shape((near_rows, cols), bf16)] * NEAR,
        [pltpu.VMEM((packed_rows, rows), bf16)],
        2 * packed_rows * rows * cols, 2 * rows * cols + 2 * packed_rows * cols,
    )(_tie(info, dense_b[1]), shrink_part, shrink_other, g_full)
    got_u = to_near(up_sends)

    step = min(1024, width // 4)
    n_steps = width // step

    def token_grads(info, first, count, so_far=None):
        return _call(
            functools.partial(tokens_kernel, z, first), "token_grads", (count,),
            [VMEM] * 5 + ([] if so_far is None else [pl.BlockSpec(memory_space=pl.ANY)]),
            pl.BlockSpec((rows, step), lambda i, *_: (0, first + i)),
            _shape((rows, width), bf16), [pltpu.VMEM((nb * rank, rows), bf16)],
            4 * rows * cols * step * count, 2 * rows * step * count,
            None if so_far is None else {6: 0},
        )(
            info, g_full, base_weight, back_part, back_other, block_down,
            *([] if so_far is None else [so_far]),
        )

    grads_1 = token_grads(_tie(info, up_sends[0]), 0, n_steps // 2)
    dense_u = dense(_tie(info, grads_1), got_u)
    far_u = to_far(dense_u)
    grad_tokens = token_grads(_tie(info, dense_u[1]), n_steps // 2, n_steps - n_steps // 2, grads_1)

    projected = _call(
        functools.partial(projected_kernel, z), "projected", (1,),
        [VMEM] * 5, _whole((rows, cols)), _shape((rows, cols), bf16),
        [pltpu.VMEM((nb * rank, rows), bf16)],
        2 * rows * cols * 128, 8 * rows * cols,
    )(_tie(info, grad_tokens), base_own, base_arrived, shrink_part, shrink_other, block_up)

    grad_up = final([far_u])
    grad_down = jnp.swapaxes(final([far_a, far_b]), 1, 2)
    return projected, grad_tokens, grad_down, grad_up


def solution(mesh):
    n_groups, n_dp = mesh.shape["groups"], mesh.shape["dp"]
    in_specs = (
        P(("groups", "dp"), "tensor"),
        P("tensor", None),
        P("dp", "tensor", None),
        P("dp", None, "tensor"),
        P(("groups", "dp"), "tensor"),
        P(("groups", "dp")),
        P(("groups", "dp")),
        P("groups"),
    )
    out_specs = (
        P(("groups", "dp"), "tensor"),
        P(("groups", "dp"), "tensor"),
        P(("groups", "dp"), "tensor", None),
        P(("groups", "dp"), None, "tensor"),
    )

    def run(*args):
        return on_device(n_groups, n_dp, *args)

    return jax.shard_map(
        run, mesh=mesh, in_specs=in_specs, out_specs=out_specs, check_vma=False
    )
```

time: 117 us -> 121 us (1.034)
  Pallas kernels: 56.5 us -> 40 us
  local copies, waits for them, and re-layouts: 3.11 us -> 15.5 us
  starting transfers between devices: 28.5 us -> 35.8 us
  waiting for transfers between devices: 25.6 us -> 27.1 us
    pallas_call x12 -> x16, Pallas kernels: 56.5 us -> 40 us  [the longest x2 14.1 us: token_grads(): _call(functools.partial(tokens_kernel, z, first), 'token_grads', (count,)...]
    unnamed x4 -> x28, local copies, waits for them, and re-layouts: 1.19 us -> 14.3 us
    ppermute x16 -> x21, starting transfers between devices: 25.3 us -> 31.8 us  [_xor(): return lax.ppermute(x, 'dp', [(i, i ^ k) for i in range(n)])]
    ppermute x16 -> x21, waiting for transfers between devices: 25.6 us -> 27.1 us  [_xor(): return lax.ppermute(x, 'dp', [(i, i ^ k) for i in range(n)])]
  transfers between devices with their start and end apart: 23 -> 28, of which waited for: 5 -> 5; matrix products, arithmetic and copies ran while one was open for 2% -> 2% of each run, Pallas kernels for 48% -> 32%
where the time goes in v3:
time: 121 us
  Pallas kernels  40 us (33%)
  starting transfers between devices  35.8 us (30%)
  waiting for transfers between devices  27.1 us (22%)
  local copies, waits for them, and re-layouts  15.5 us (13%)
  other arithmetic  1.76 us (1%)
    ppermute x21, starting transfers between devices, _xor(): return lax.ppermute(x, 'dp', [(i, i ^ k) for i in range(n)])  31.8 us
    ppermute x21, waiting for transfers between devices, _xor(): return lax.ppermute(x, 'dp', [(i, i ^ k) for i in range(n)])  27.1 us
    unnamed x28, local copies, waits for them, and re-layouts  14.3 us
    pallas_call x2, Pallas kernels, token_grads(): _call(functools.partial(tokens_kernel, z, first), 'token_grads', (count,)...  14.1 us
    pallas_call x1, Pallas kernels, on_device(): _call(functools.partial(own_kernel, z), 'base_own', (1,), [VMEM] * 4, [VM...  4.63 us
    pallas_call x1, Pallas kernels, on_device(): _call(functools.partial(other_kernel, z), 'base_other', (1,), [VMEM, VMEM...  3.96 us
    pallas_call x2, Pallas kernels, pack(): _call(functools.partial(pack_kernel, z, NEAR, start), 'pack_down', (1,),...  3.66 us
    pallas_call x3, Pallas kernels, dense(): _call(functools.partial(dense_kernel, z), 'dense', (1,), [VMEM] * NEAR, [...  3.45 us
  transfers between devices with their start and end apart: 28, of which 5 were waited for; matrix products, arithmetic and copies ran while one was open for 2% of the time, Pallas kernels for 32%

profile of v3, /device:TPU:0, one launch (start us, length us, event | category | flops | bytes accessed | tf_op | source)
XLA Modules:
  0.0 121.1 jit_solution(5251697553213252293)
XLA Ops:
  1.7 3.0 %collective-permute-start.5 = (bf16[4,16,1024]{2,1,0:T(8,128)(2,1)S(1)}, bf16[4,16,1024]{2,1,0:T(8,128)(2,1)S(1)}, u32[]{:S(2)}, u32[]{:S(2)}) collective-permute-start(bf16[4,16,1024]{2,1,0:T(8,128)(2,1)S(1)} %get-tuple-element.115), channel_id=1, source_target_pairs={{0,2},{2,0},{4,6},{6,4},{8,10},{10,8},{12,14},{14,12},{1,3},{3,1},... | collective-permute-start | bytes 393224 | tf_op jit(solution)/shard_map/ppermute | solution.py:34
  5.5 1.5 %collective-permute-start = (s32[7]{0:T(128)S(1)}, s32[7]{0:T(128)S(1)}, u32[]{:S(2)}, u32[]{:S(2)}) collective-permute-start(s32[7]{0:T(128)S(1)} %select_reduce_fusion), channel_id=1, source_target_pairs={{0,16},{16,0},{1,17},{17,1},{2,18},{18,2},{3,19},{19,3},{4,20},{20... | collective-permute-start | bytes 92 | tf_op jit(solution)/shard_map/ppermute | solution.py:30
  7.1 2.6 %collective-permute-start.1 = (bf16[4,16,512]{2,1,0:T(8,128)(2,1)}, bf16[4,16,512]{2,1,0:T(8,128)(2,1)S(1)}, u32[]{:S(2)}, u32[]{:S(2)}) collective-permute-start(bf16[4,16,512]{2,1,0:T(8,128)(2,1)} %param.15), channel_id=1, source_target_pairs={{0,8},{2,10},{4,12},{6,14},{8,0},{10,2},{12,4},{14,6},{1,9},{3,11}... | collective-permute-start | bytes 196616 | tf_op jit(solution)/shard_map/ppermute | solution.py:34
  9.9 2.6 %collective-permute-done.1 = bf16[4,16,512]{2,1,0:T(8,128)(2,1)S(1)} collective-permute-done((bf16[4,16,512]{2,1,0:T(8,128)(2,1)}, bf16[4,16,512]{2,1,0:T(8,128)(2,1)S(1)}, u32[]{:S(2)}, u32[]{:S(2)}) %collective-permute-start.1) | collective-permute-done | bytes 65568 | tf_op jit(solution)/shard_map/ppermute | solution.py:34
  13.9 2.5 %collective-permute-start.4 = (bf16[144,512]{1,0:T(8,128)(2,1)S(1)}, bf16[144,512]{1,0:T(8,128)(2,1)S(1)}, u32[]{:S(2)}, u32[]{:S(2)}) collective-permute-start(bf16[144,512]{1,0:T(8,128)(2,1)S(1)} %pad_maximum_fusion.1.refs_0_), channel_id=1, source_target_pairs={{0,6},{2,4},{4,2},{6,0},{8,14},{10,12},{12,10},{14,8},{1,7},{3,5},... | collective-permute-start | bytes 442376 | tf_op jit(solution)/shard_map/ppermute | solution.py:34
  16.9 2.8 %collective-permute-start.9 = (bf16[8,16,1024]{2,1,0:T(8,128)(2,1)S(1)}, bf16[8,16,1024]{2,1,0:T(8,128)(2,1)S(1)}, u32[]{:S(2)}, u32[]{:S(2)}) collective-permute-start(bf16[8,16,1024]{2,1,0:T(8,128)(2,1)S(1)} %pad_maximum_fusion.own_ref), channel_id=1, source_target_pairs={{0,8},{2,10},{4,12},{6,14},{8,0},{10,2},{12,4},{14,6},{1,9},{3,11}... | collective-permute-start | bytes 786440 | tf_op jit(solution)/shard_map/ppermute | solution.py:34
  19.7 3.1 %copy-done = bf16[896,4096]{1,0:T(8,128)(2,1)S(1)} copy-done((bf16[896,4096]{1,0:T(8,128)(2,1)S(1)}, bf16[896,4096]{1,0:T(8,128)(2,1)}, u32[]{:S(2)}) %copy-start) | copy-done | bytes 7340056
  22.8 3.4 %copy-done.2 = bf16[4096,1024]{1,0:T(8,128)(2,1)S(1)} copy-done((bf16[4096,1024]{1,0:T(8,128)(2,1)S(1)}, bf16[4096,1024]{1,0:T(8,128)(2,1)}, u32[]{:S(2)}) %copy-start.2) | copy-done | bytes 8388632
  26.2 4.0 %base_other.1 = bf16[896,512]{1,0:T(8,128)(2,1)S(1)} custom-call(s32[1]{0:T(128)} %bitcast.11.me, bf16[896,4096]{1,0:T(8,128)(2,1)S(1)} %copy-done, bf16[4096,1024]{1,0:T(8,128)(2,1)S(1)} %copy-done.2), custom_call_target="tpu_custom_call" | custom-call | flops 3758096384 | bytes 917504 | tf_op jit(solution)/shard_map/base_other/pallas_call | solution.py:333
  35.9 2.1 %collective-permute-start.8 = (bf16[8,16,1024]{2,1,0:T(8,128)(2,1)S(1)}, bf16[8,16,1024]{2,1,0:T(8,128)(2,1)S(1)}, u32[]{:S(2)}, u32[]{:S(2)}) collective-permute-start(bf16[8,16,1024]{2,1,0:T(8,128)(2,1)S(1)} %pad_maximum_fusion.own_ref), channel_id=1, source_target_pairs={{0,4},{2,6},{4,0},{6,2},{8,12},{10,14},{12,8},{14,10},{1,5},{3,7},... | collective-permute-start | bytes 786440 | tf_op jit(solution)/shard_map/ppermute | solution.py:34
  38.0 3.1 %copy-done.1 = bf16[896,4096]{1,0:T(8,128)(2,1)S(1)} copy-done((bf16[896,4096]{1,0:T(8,128)(2,1)S(1)}, bf16[896,4096]{1,0:T(8,128)(2,1)}, u32[]{:S(2)}) %copy-start.1) | copy-done | bytes 7340056
  41.0 1.8 %pack_down.2 = (bf16[64,2048]{1,0:T(8,128)(2,1)S(1)}, bf16[64,2048]{1,0:T(8,128)(2,1)S(1)}, bf16[64,2048]{1,0:T(8,128)(2,1)S(1)}, bf16[64,2048]{1,0:T(8,128)(2,1)S(1)}) custom-call(s32[52]{0:T(128)S(1)} %concatenate.14.info, f32[16,896]{1,0:T(8,128)S(1)} %get-tuple-element.74.mine_ref, f32[16,896]{1,0:T(8,128)S(1)} %collective-permute-done.6.other_ref, ...), custom_call_target="tpu_custom_call" | custom-call | flops 939524096 | bytes 1048576 | tf_op jit(solution)/shard_map/pack_down/pallas_call | solution.py:359
  42.9 1.8 %pack_down.3 = (bf16[64,2048]{1,0:T(8,128)(2,1)S(1)}, bf16[64,2048]{1,0:T(8,128)(2,1)S(1)}, bf16[64,2048]{1,0:T(8,128)(2,1)S(1)}, bf16[64,2048]{1,0:T(8,128)(2,1)S(1)}) custom-call(s32[52]{0:T(128)S(1)} %concatenate.14.info, f32[16,896]{1,0:T(8,128)S(1)} %get-tuple-element.74.mine_ref, f32[16,896]{1,0:T(8,128)S(1)} %collective-permute-done.6.other_ref, ...), custom_call_target="tpu_custom_call" | custom-call | flops 939524096 | bytes 1048576 | tf_op jit(solution)/shard_map/pack_down/pallas_call | solution.py:359
  46.5 1.8 %collective-permute-start.13 = (bf16[64,2048]{1,0:T(8,128)(2,1)S(1)}, bf16[64,2048]{1,0:T(8,128)(2,1)S(1)}, u32[]{:S(2)}, u32[]{:S(2)}) collective-permute-start(bf16[64,2048]{1,0:T(8,128)(2,1)S(1)} %get-tuple-element.86), channel_id=1, source_target_pairs={{0,6},{2,4},{4,2},{6,0},{8,14},{10,12},{12,10},{14,8},{1,7},{3,5},... | collective-permute-start | bytes 786440 | tf_op jit(solution)/shard_map/ppermute | solution.py:34
  48.3 1.2 collective-permute-start.10
  49.5 4.6 %base_own.1 = (f32[896,512]{1,0:T(8,128)S(1)}, bf16[896,1024]{1,0:T(8,128)(2,1)S(1)}) custom-call(s32[52]{0:T(128)S(1)} %concatenate.14.info, bf16[896,4096]{1,0:T(8,128)(2,1)S(1)} %copy-done.1, bf16[4096,1024]{1,0:T(8,128)(2,1)S(1)} %copy-done.3, bf16[896,512]{1,0:T(8,128)(2,1)S(1)} %copy-done.4, bf16[896,512]{1,0:T(8,128)(2,1)S(1)} %collective-permute-done.7.h_ref), custom_call_target="tpu_custom_call" | custom-call | flops 3758096384 | bytes 5505024 | tf_op jit(solution)/shard_map/base_own/pallas_call | solution.py:402
  54.1 10.5 %collective-permute-done.10.farther_ref = bf16[8,16,1024]{2,1,0:T(8,128)(2,1)S(1)} collective-permute-done((bf16[8,16,1024]{2,1,0:T(8,128)(2,1)S(1)}, bf16[8,16,1024]{2,1,0:T(8,128)(2,1)S(1)}, u32[]{:S(2)}, u32[]{:S(2)}) %collective-permute-start.10) | collective-permute-done | bytes 262176 | tf_op jit(solution)/shard_map/ppermute | solution.py:34
  65.5 1.6 %collective-permute-start.14 = (bf16[112,1024]{1,0:T(8,128)(2,1)S(1)}, bf16[112,1024]{1,0:T(8,128)(2,1)S(1)}, u32[]{:S(2)}, u32[]{:S(2)}) collective-permute-start(bf16[112,1024]{1,0:T(8,128)(2,1)S(1)} %get-tuple-element.89), channel_id=1, source_target_pairs={{0,2},{2,0},{4,6},{6,4},{8,10},{10,8},{12,14},{14,12},{1,3},{3,1},... | collective-permute-start | bytes 688136 | tf_op jit(solution)/shard_map/ppermute | solution.py:34
  67.6 1.4 %collective-permute-start.16 = (bf16[112,1024]{1,0:T(8,128)(2,1)S(1)}, bf16[112,1024]{1,0:T(8,128)(2,1)S(1)}, u32[]{:S(2)}, u32[]{:S(2)}) collective-permute-start(bf16[112,1024]{1,0:T(8,128)(2,1)S(1)} %get-tuple-element.91), channel_id=1, source_target_pairs={{0,18},{2,16},{4,22},{6,20},{8,26},{10,24},{12,30},{14,28},{16,2},... | collective-permute-start | bytes 688136 | tf_op jit(solution)/shard_map/ppermute | solution.py:420
  69.0 1.5 %collective-permute-start.17 = (bf16[64,2048]{1,0:T(8,128)(2,1)S(1)}, bf16[64,2048]{1,0:T(8,128)(2,1)S(1)}, u32[]{:S(2)}, u32[]{:S(2)}) collective-permute-start(bf16[64,2048]{1,0:T(8,128)(2,1)S(1)} %get-tuple-element.94), channel_id=1, source_target_pairs={{0,2},{2,0},{4,6},{6,4},{8,10},{10,8},{12,14},{14,12},{1,3},{3,1},... | collective-permute-start | bytes 786440 | tf_op jit(solution)/shard_map/ppermute | solution.py:34
  71.7 10.1 %collective-permute-done.14.refs_1_ = bf16[112,1024]{1,0:T(8,128)(2,1)S(1)} collective-permute-done((bf16[112,1024]{1,0:T(8,128)(2,1)S(1)}, bf16[112,1024]{1,0:T(8,128)(2,1)S(1)}, u32[]{:S(2)}, u32[]{:S(2)}) %collective-permute-start.14) | collective-permute-done | bytes 229408 | tf_op jit(solution)/shard_map/ppermute | solution.py:34
  81.8 2.1 %collective-permute-start.19 = (bf16[64,2048]{1,0:T(8,128)(2,1)S(1)}, bf16[64,2048]{1,0:T(8,128)(2,1)S(1)}, u32[]{:S(2)}, u32[]{:S(2)}) collective-permute-start(bf16[64,2048]{1,0:T(8,128)(2,1)S(1)} %get-tuple-element.96), channel_id=1, source_target_pairs={{0,6},{2,4},{4,2},{6,0},{8,14},{10,12},{12,10},{14,8},{1,7},{3,5},... | collective-permute-start | bytes 786440 | tf_op jit(solution)/shard_map/ppermute | solution.py:34
  83.9 1.3 %dense.3 = (f32[64,2048]{1,0:T(8,128)S(1)}, bf16[64,2048]{1,0:T(8,128)(2,1)S(1)}) custom-call(s32[52]{0:T(128)S(1)} %concatenate.14.info, bf16[64,2048]{1,0:T(8,128)(2,1)S(1)} %get-tuple-element.75.refs_0_, bf16[64,2048]{1,0:T(8,128)(2,1)S(1)} %collective-permute-done.11.refs_1_, bf16[64,2048]{1,0:T(8,128)(2,1)S(1)} %collective-permute-done.12.refs_2_, ...), custom_call_target="tpu_custom_call" | custom-call | flops 67108864 | bytes 1048576 | tf_op jit(solution)/shard_map/dense/pallas_call | solution.py:373
  85.2 2.7 %shrink.1 = (bf16[112,4096]{1,0:T(8,128)(2,1)S(1)}, f32[16,896]{1,0:T(8,128)S(1)}) custom-call(s32[52]{0:T(128)S(1)} %concatenate.14.info, bf16[896,4096]{1,0:T(8,128)(2,1)S(1)} %bitcast.36, bf16[112,1024]{1,0:T(8,128)(2,1)S(1)} %get-tuple-element.82.refs_0_, bf16[112,1024]{1,0:T(8,128)(2,1)S(1)} %collective-permute-done.14.refs_1_, ...), custom_call_target="tpu_custom_call" | custom-call | flops 939524096 | bytes 917504 | tf_op jit(solution)/shard_map/shrink/pallas_call | solution.py:435
  89.1 1.2 %dense.4 = (f32[64,2048]{1,0:T(8,128)S(1)}, bf16[64,2048]{1,0:T(8,128)(2,1)S(1)}) custom-call(s32[52]{0:T(128)S(1)} %concatenate.14.info, bf16[64,2048]{1,0:T(8,128)(2,1)S(1)} %get-tuple-element.77.refs_0_, bf16[64,2048]{1,0:T(8,128)(2,1)S(1)} %collective-permute-done.17.refs_1_, bf16[64,2048]{1,0:T(8,128)(2,1)S(1)} %collective-permute-done.18.refs_2_, ...), custom_call_target="tpu_custom_call" | custom-call | flops 67108864 | bytes 1048576 | tf_op jit(solution)/shard_map/dense/pallas_call | solution.py:373
  91.3 1.6 %collective-permute-start.21 = (bf16[64,512]{1,0:T(8,128)(2,1)S(1)}, bf16[64,512]{1,0:T(8,128)(2,1)S(1)}, u32[]{:S(2)}, u32[]{:S(2)}) collective-permute-start(bf16[64,512]{1,0:T(8,128)(2,1)S(1)} %get-tuple-element.104), channel_id=1, source_target_pairs={{0,2},{2,0},{4,6},{6,4},{8,10},{10,8},{12,14},{14,12},{1,3},{3,1},... | collective-permute-start | bytes 196616 | tf_op jit(solution)/shard_map/ppermute | solution.py:34
  94.9 7.1 %token_grads.2.refs_0_ = bf16[896,4096]{1,0:T(8,128)(2,1)} custom-call(s32[52]{0:T(128)S(1)} %concatenate.14.info, bf16[896,1024]{1,0:T(8,128)(2,1)S(1)} %get-tuple-element.99.g_ref, bf16[4096,1024]{1,0:T(8,128)(2,1)S(1)} %copy-done.3, f32[16,896]{1,0:T(8,128)S(1)} %get-tuple-element.74.mine_ref, f32[16,896]{1,0:T(8,128)S(1)} %collective-permute-done.6.other_ref, ...), custom_call_target="tpu_custom_call" | custom-call | flops 3758096384 | bytes 3670016 | tf_op jit(solution)/shard_map/token_grads/pallas_call | solution.py:459
  102.0 2.4 %collective-permute-start.26 = (bf16[64,2048]{1,0:T(8,128)(2,1)S(1)}, bf16[64,2048]{1,0:T(8,128)(2,1)S(1)}, u32[]{:S(2)}, u32[]{:S(2)}) collective-permute-start(bf16[64,2048]{1,0:T(8,128)(2,1)S(1)} %get-tuple-element.97), channel_id=1, source_target_pairs={{0,8},{2,10},{4,12},{6,14},{8,0},{10,2},{12,4},{14,6},{1,9},{3,11}... | collective-permute-start | bytes 786440 | tf_op jit(solution)/shard_map/ppermute | solution.py:34
  106.0 7.0 %token_grads.3 = bf16[896,4096]{1,0:T(8,128)(2,1)} custom-call(s32[52]{0:T(128)S(1)} %concatenate.14.info, bf16[896,1024]{1,0:T(8,128)(2,1)S(1)} %get-tuple-element.99.g_ref, bf16[4096,1024]{1,0:T(8,128)(2,1)S(1)} %copy-done.3, f32[16,896]{1,0:T(8,128)S(1)} %get-tuple-element.74.mine_ref, ...), custom_call_target="tpu_custom_call", output_to_operand_aliasing={{}: (6, {})} | custom-call | flops 3758096384 | bytes 3670016 | tf_op jit(solution)/shard_map/token_grads/pallas_call | solution.py:459
  112.9 2.0 %projected.1 = bf16[896,512]{1,0:T(8,128)(2,1)} custom-call(s32[52]{0:T(128)S(1)} %concatenate.14.info, f32[896,512]{1,0:T(8,128)S(1)} %get-tuple-element.79.base_ref, bf16[896,512]{1,0:T(8,128)(2,1)S(1)} %collective-permute-done.24.far_ref, f32[16,896]{1,0:T(8,128)S(1)} %get-tuple-element.92.mine_ref, f32[16,896]{1,0:T(8,128)S(1)} %collective-permute-done.20.other_ref, ...), custom_call_target="tpu_custom_call" | custom-call | flops 117440512 | bytes 3670016 | tf_op jit(solution)/shard_map/projected/pallas_call | solution.py:476
  115.0 3.3 %collective-permute-done.27.refs_1_ = bf16[64,512]{1,0:T(8,128)(2,1)S(1)} collective-permute-done((bf16[64,512]{1,0:T(8,128)(2,1)S(1)}, bf16[64,512]{1,0:T(8,128)(2,1)S(1)}, u32[]{:S(2)}, u32[]{:S(2)}) %collective-permute-start.27) | collective-permute-done | bytes 65568 | tf_op jit(solution)/shard_map/ppermute | solution.py:34
  119.5 1.6 %final.2 = f32[64,4096]{1,0:T(8,128)} custom-call(s32[52]{0:T(128)S(1)} %concatenate.14.info, f32[64,2048]{1,0:T(8,128)S(1)} %get-tuple-element.111.refs_0_, bf16[64,2048]{1,0:T(8,128)(2,1)S(1)} %collective-permute-done.25.refs_1_, f32[64,2048]{1,0:T(8,128)S(1)} %get-tuple-element.112.refs_2_, bf16[64,2048]{1,0:T(8,128)(2,1)S(1)} %collective-permute-done.26.refs_3_), custom_call_target="tpu_custom_call" | custom-call | flops 262144 | bytes 2621440 | tf_op jit(solution)/shard_map/final/pallas_call | solution.py:386
  (84 shorter events, 20.9 us)
Async XLA Ops:
  1.7 15.2 %collective-permute-start.5 = (bf16[4,16,1024]{2,1,0:T(8,128)(2,1)S(1)}, bf16[4,16,1024]{2,1,0:T(8,128)(2,1)S(1)}, u32[]{:S(2)}, u32[]{:S(2)}) collective-permute-start(bf16[4,16,1024]{2,1,0:T(8,128)(2,1)S(1)} %get-tuple-element.115), channel_id=1, source_target_pairs={{0,2},{2,0},{4,6},{6,4},{8,10},{10,8},{12,14},{14,12},{1,3},{3,1},... | collective-permute-start | bytes 393224 | tf_op jit(solution)/shard_map/ppermute | solution.py:34
  5.5 4.2 %collective-permute-start = (s32[7]{0:T(128)S(1)}, s32[7]{0:T(128)S(1)}, u32[]{:S(2)}, u32[]{:S(2)}) collective-permute-start(s32[7]{0:T(128)S(1)} %select_reduce_fusion), channel_id=1, source_target_pairs={{0,16},{16,0},{1,17},{17,1},{2,18},{18,2},{3,19},{19,3},{4,20},{20... | collective-permute-start | bytes 92 | tf_op jit(solution)/shard_map/ppermute | solution.py:30
  7.1 5.4 %collective-permute-start.1 = (bf16[4,16,512]{2,1,0:T(8,128)(2,1)}, bf16[4,16,512]{2,1,0:T(8,128)(2,1)S(1)}, u32[]{:S(2)}, u32[]{:S(2)}) collective-permute-start(bf16[4,16,512]{2,1,0:T(8,128)(2,1)} %param.15), channel_id=1, source_target_pairs={{0,8},{2,10},{4,12},{6,14},{8,0},{10,2},{12,4},{14,6},{1,9},{3,11}... | collective-permute-start | bytes 196616 | tf_op jit(solution)/shard_map/ppermute | solution.py:34
  9.7 38.6 %collective-permute-start.7 = (bf16[896,512]{1,0:T(8,128)(2,1)}, bf16[896,512]{1,0:T(8,128)(2,1)S(1)}, u32[]{:S(2)}, u32[]{:S(2)}) collective-permute-start(bf16[896,512]{1,0:T(8,128)(2,1)} %g_ref.3), channel_id=1, source_target_pairs={{0,1},{1,0},{2,3},{3,2},{4,5},{5,4},{6,7},{7,6},{8,9},{9,8},{10,11... | collective-permute-start | bytes 2752520 | tf_op jit(solution)/shard_map/ppermute | solution.py:30
  13.3 18.2 %collective-permute-start.2 = (bf16[144,512]{1,0:T(8,128)(2,1)S(1)}, bf16[144,512]{1,0:T(8,128)(2,1)S(1)}, u32[]{:S(2)}, u32[]{:S(2)}) collective-permute-start(bf16[144,512]{1,0:T(8,128)(2,1)S(1)} %pad_maximum_fusion.1.refs_0_), channel_id=1, source_target_pairs={{0,2},{2,0},{4,6},{6,4},{8,10},{10,8},{12,14},{14,12},{1,3},{3,1},... | collective-permute-start | bytes 442376 | tf_op jit(solution)/shard_map/ppermute | solution.py:34
  13.9 16.2 %collective-permute-start.4 = (bf16[144,512]{1,0:T(8,128)(2,1)S(1)}, bf16[144,512]{1,0:T(8,128)(2,1)S(1)}, u32[]{:S(2)}, u32[]{:S(2)}) collective-permute-start(bf16[144,512]{1,0:T(8,128)(2,1)S(1)} %pad_maximum_fusion.1.refs_0_), channel_id=1, source_target_pairs={{0,6},{2,4},{4,2},{6,0},{8,14},{10,12},{12,10},{14,8},{1,7},{3,5},... | collective-permute-start | bytes 442376 | tf_op jit(solution)/shard_map/ppermute | solution.py:34
  16.4 14.4 %collective-permute-start.3 = (bf16[144,512]{1,0:T(8,128)(2,1)S(1)}, bf16[144,512]{1,0:T(8,128)(2,1)S(1)}, u32[]{:S(2)}, u32[]{:S(2)}) collective-permute-start(bf16[144,512]{1,0:T(8,128)(2,1)S(1)} %pad_maximum_fusion.1.refs_0_), channel_id=1, source_target_pairs={{0,4},{2,6},{4,0},{6,2},{8,12},{10,14},{12,8},{14,10},{1,5},{3,7},... | collective-permute-start | bytes 442376 | tf_op jit(solution)/shard_map/ppermute | solution.py:34
  16.9 29.6 %collective-permute-start.9 = (bf16[8,16,1024]{2,1,0:T(8,128)(2,1)S(1)}, bf16[8,16,1024]{2,1,0:T(8,128)(2,1)S(1)}, u32[]{:S(2)}, u32[]{:S(2)}) collective-permute-start(bf16[8,16,1024]{2,1,0:T(8,128)(2,1)S(1)} %pad_maximum_fusion.own_ref), channel_id=1, source_target_pairs={{0,8},{2,10},{4,12},{6,14},{8,0},{10,2},{12,4},{14,6},{1,9},{3,11}... | collective-permute-start | bytes 786440 | tf_op jit(solution)/shard_map/ppermute | solution.py:34
  26.2 6.1 %copy-start.4 = (bf16[896,512]{1,0:T(8,128)(2,1)S(1)}, bf16[896,512]{1,0:T(8,128)(2,1)}, u32[]{:S(2)}) copy-start(bf16[896,512]{1,0:T(8,128)(2,1)} %g_ref.3) | copy-start | bytes 2752516
  35.9 2.1 %collective-permute-start.6 = (f32[16,896]{1,0:T(8,128)S(1)}, f32[16,896]{1,0:T(8,128)S(1)}, u32[]{:S(2)}, u32[]{:S(2)}) collective-permute-start(f32[16,896]{1,0:T(8,128)S(1)} %get-tuple-element.74.mine_ref), channel_id=1, source_target_pairs={{0,1},{1,0},{2,3},{3,2},{4,5},{5,4},{6,7},{7,6},{8,9},{9,8},{10,11... | collective-permute-start | bytes 172040 | tf_op jit(solution)/shard_map/ppermute | solution.py:30
  35.9 18.2 %collective-permute-start.8 = (bf16[8,16,1024]{2,1,0:T(8,128)(2,1)S(1)}, bf16[8,16,1024]{2,1,0:T(8,128)(2,1)S(1)}, u32[]{:S(2)}, u32[]{:S(2)}) collective-permute-start(bf16[8,16,1024]{2,1,0:T(8,128)(2,1)S(1)} %pad_maximum_fusion.own_ref), channel_id=1, source_target_pairs={{0,4},{2,6},{4,0},{6,2},{8,12},{10,14},{12,8},{14,10},{1,5},{3,7},... | collective-permute-start | bytes 786440 | tf_op jit(solution)/shard_map/ppermute | solution.py:34
  41.0 8.5 %copy-start.3 = (bf16[4096,1024]{1,0:T(8,128)(2,1)S(1)}, bf16[4096,1024]{1,0:T(8,128)(2,1)}, u32[]{:S(2)}) copy-start(bf16[4096,1024]{1,0:T(8,128)(2,1)} %w_ref.7) | copy-start | bytes 25165828
  44.7 22.9 %collective-permute-start.11 = (bf16[64,2048]{1,0:T(8,128)(2,1)S(1)}, bf16[64,2048]{1,0:T(8,128)(2,1)S(1)}, u32[]{:S(2)}, u32[]{:S(2)}) collective-permute-start(bf16[64,2048]{1,0:T(8,128)(2,1)S(1)} %get-tuple-element.84), channel_id=1, source_target_pairs={{0,2},{2,0},{4,6},{6,4},{8,10},{10,8},{12,14},{14,12},{1,3},{3,1},... | collective-permute-start | bytes 786440 | tf_op jit(solution)/shard_map/ppermute | solution.py:34
  45.3 23.7 %collective-permute-start.12 = (bf16[64,2048]{1,0:T(8,128)(2,1)S(1)}, bf16[64,2048]{1,0:T(8,128)(2,1)S(1)}, u32[]{:S(2)}, u32[]{:S(2)}) collective-permute-start(bf16[64,2048]{1,0:T(8,128)(2,1)S(1)} %get-tuple-element.85), channel_id=1, source_target_pairs={{0,4},{2,6},{4,0},{6,2},{8,12},{10,14},{12,8},{14,10},{1,5},{3,7},... | collective-permute-start | bytes 786440 | tf_op jit(solution)/shard_map/ppermute | solution.py:34
  46.5 38.7 %slice-start = ((s8[7340032]{0:T(1024)(128)(4,1)}), s8[4194304]{0:T(1024)(128)(4,1)S(1)}, s32[]{:S(2)}) async-start(s8[7340032]{0:T(1024)(128)(4,1)} %bitcast.35), calls=%async_computation | async-start | bytes 8388608
  46.5 38.7 %slice-start.1 = ((s8[7340032]{0:T(1024)(128)(4,1)}), s8[3145728]{0:T(1024)(128)(4,1)S(1)}, s32[]{:S(2)}) async-start(s8[7340032]{0:T(1024)(128)(4,1)} %bitcast.35), calls=%async_computation.1 | async-start | bytes 6291456
  46.5 24.0 %collective-permute-start.13 = (bf16[64,2048]{1,0:T(8,128)(2,1)S(1)}, bf16[64,2048]{1,0:T(8,128)(2,1)S(1)}, u32[]{:S(2)}, u32[]{:S(2)}) collective-permute-start(bf16[64,2048]{1,0:T(8,128)(2,1)S(1)} %get-tuple-element.86), channel_id=1, source_target_pairs={{0,6},{2,4},{4,2},{6,0},{8,14},{10,12},{12,10},{14,8},{1,7},{3,5},... | collective-permute-start | bytes 786440 | tf_op jit(solution)/shard_map/ppermute | solution.py:34
  48.3 16.4 %collective-permute-start.10 = (bf16[8,16,1024]{2,1,0:T(8,128)(2,1)S(1)}, bf16[8,16,1024]{2,1,0:T(8,128)(2,1)S(1)}, u32[]{:S(2)}, u32[]{:S(2)}) collective-permute-start(bf16[8,16,1024]{2,1,0:T(8,128)(2,1)S(1)} %collective-permute-done.9.far_ref), channel_id=1, source_target_pairs={{0,4},{2,6},{4,0},{6,2},{8,12},{10,14},{12,8},{14,10},{1,5},{3,7},... | collective-permute-start | bytes 786440 | tf_op jit(solution)/shard_map/ppermute | solution.py:34
  65.5 16.3 %collective-permute-start.14 = (bf16[112,1024]{1,0:T(8,128)(2,1)S(1)}, bf16[112,1024]{1,0:T(8,128)(2,1)S(1)}, u32[]{:S(2)}, u32[]{:S(2)}) collective-permute-start(bf16[112,1024]{1,0:T(8,128)(2,1)S(1)} %get-tuple-element.89), channel_id=1, source_target_pairs={{0,2},{2,0},{4,6},{6,4},{8,10},{10,8},{12,14},{14,12},{1,3},{3,1},... | collective-permute-start | bytes 688136 | tf_op jit(solution)/shard_map/ppermute | solution.py:34
  67.0 16.9 %collective-permute-start.15 = (bf16[112,1024]{1,0:T(8,128)(2,1)S(1)}, bf16[112,1024]{1,0:T(8,128)(2,1)S(1)}, u32[]{:S(2)}, u32[]{:S(2)}) collective-permute-start(bf16[112,1024]{1,0:T(8,128)(2,1)S(1)} %get-tuple-element.90), channel_id=1, source_target_pairs={{0,16},{16,0},{1,17},{17,1},{2,18},{18,2},{3,19},{19,3},{4,20},{20... | collective-permute-start | bytes 688136 | tf_op jit(solution)/shard_map/ppermute | solution.py:30
  67.6 17.6 %collective-permute-start.16 = (bf16[112,1024]{1,0:T(8,128)(2,1)S(1)}, bf16[112,1024]{1,0:T(8,128)(2,1)S(1)}, u32[]{:S(2)}, u32[]{:S(2)}) collective-permute-start(bf16[112,1024]{1,0:T(8,128)(2,1)S(1)} %get-tuple-element.91), channel_id=1, source_target_pairs={{0,18},{2,16},{4,22},{6,20},{8,26},{10,24},{12,30},{14,28},{16,2},... | collective-permute-start | bytes 688136 | tf_op jit(solution)/shard_map/ppermute | solution.py:420
  69.0 19.5 %collective-permute-start.17 = (bf16[64,2048]{1,0:T(8,128)(2,1)S(1)}, bf16[64,2048]{1,0:T(8,128)(2,1)S(1)}, u32[]{:S(2)}, u32[]{:S(2)}) collective-permute-start(bf16[64,2048]{1,0:T(8,128)(2,1)S(1)} %get-tuple-element.94), channel_id=1, source_target_pairs={{0,2},{2,0},{4,6},{6,4},{8,10},{10,8},{12,14},{14,12},{1,3},{3,1},... | collective-permute-start | bytes 786440 | tf_op jit(solution)/shard_map/ppermute | solution.py:34
  70.5 18.0 %collective-permute-start.18 = (bf16[64,2048]{1,0:T(8,128)(2,1)S(1)}, bf16[64,2048]{1,0:T(8,128)(2,1)S(1)}, u32[]{:S(2)}, u32[]{:S(2)}) collective-permute-start(bf16[64,2048]{1,0:T(8,128)(2,1)S(1)} %get-tuple-element.95), channel_id=1, source_target_pairs={{0,4},{2,6},{4,0},{6,2},{8,12},{10,14},{12,8},{14,10},{1,5},{3,7},... | collective-permute-start | bytes 786440 | tf_op jit(solution)/shard_map/ppermute | solution.py:34
  81.8 7.3 %collective-permute-start.19 = (bf16[64,2048]{1,0:T(8,128)(2,1)S(1)}, bf16[64,2048]{1,0:T(8,128)(2,1)S(1)}, u32[]{:S(2)}, u32[]{:S(2)}) collective-permute-start(bf16[64,2048]{1,0:T(8,128)(2,1)S(1)} %get-tuple-element.96), channel_id=1, source_target_pairs={{0,6},{2,4},{4,2},{6,0},{8,14},{10,12},{12,10},{14,8},{1,7},{3,5},... | collective-permute-start | bytes 786440 | tf_op jit(solution)/shard_map/ppermute | solution.py:34
  83.9 29.0 %collective-permute-start.24 = (bf16[896,512]{1,0:T(8,128)(2,1)S(1)}, bf16[896,512]{1,0:T(8,128)(2,1)S(1)}, u32[]{:S(2)}, u32[]{:S(2)}) collective-permute-start(bf16[896,512]{1,0:T(8,128)(2,1)S(1)} %base_other.1), channel_id=1, source_target_pairs={{0,1},{1,0},{2,3},{3,2},{4,5},{5,4},{6,7},{7,6},{8,9},{9,8},{10,11... | collective-permute-start | bytes 2752520 | tf_op jit(solution)/shard_map/ppermute | solution.py:30
  87.9 2.4 %collective-permute-start.20 = (f32[16,896]{1,0:T(8,128)S(1)}, f32[16,896]{1,0:T(8,128)S(1)}, u32[]{:S(2)}, u32[]{:S(2)}) collective-permute-start(f32[16,896]{1,0:T(8,128)S(1)} %get-tuple-element.92.mine_ref), channel_id=1, source_target_pairs={{0,1},{1,0},{2,3},{3,2},{4,5},{5,4},{6,7},{7,6},{8,9},{9,8},{10,11... | collective-permute-start | bytes 172040 | tf_op jit(solution)/shard_map/ppermute | solution.py:30
  88.5 31.0 %collective-permute-start.25 = (bf16[64,2048]{1,0:T(8,128)(2,1)S(1)}, bf16[64,2048]{1,0:T(8,128)(2,1)S(1)}, u32[]{:S(2)}, u32[]{:S(2)}) collective-permute-start(bf16[64,2048]{1,0:T(8,128)(2,1)S(1)} %get-tuple-element.87), channel_id=1, source_target_pairs={{0,8},{2,10},{4,12},{6,14},{8,0},{10,2},{12,4},{14,6},{1,9},{3,11}... | collective-permute-start | bytes 786440 | tf_op jit(solution)/shard_map/ppermute | solution.py:34
  91.3 10.7 %collective-permute-start.21 = (bf16[64,512]{1,0:T(8,128)(2,1)S(1)}, bf16[64,512]{1,0:T(8,128)(2,1)S(1)}, u32[]{:S(2)}, u32[]{:S(2)}) collective-permute-start(bf16[64,512]{1,0:T(8,128)(2,1)S(1)} %get-tuple-element.104), channel_id=1, source_target_pairs={{0,2},{2,0},{4,6},{6,4},{8,10},{10,8},{12,14},{14,12},{1,3},{3,1},... | collective-permute-start | bytes 196616 | tf_op jit(solution)/shard_map/ppermute | solution.py:34
  92.9 11.5 %collective-permute-start.22 = (bf16[64,512]{1,0:T(8,128)(2,1)S(1)}, bf16[64,512]{1,0:T(8,128)(2,1)S(1)}, u32[]{:S(2)}, u32[]{:S(2)}) collective-permute-start(bf16[64,512]{1,0:T(8,128)(2,1)S(1)} %get-tuple-element.105), channel_id=1, source_target_pairs={{0,4},{2,6},{4,0},{6,2},{8,12},{10,14},{12,8},{14,10},{1,5},{3,7},... | collective-permute-start | bytes 196616 | tf_op jit(solution)/shard_map/ppermute | solution.py:34
  94.1 10.3 %collective-permute-start.23 = (bf16[64,512]{1,0:T(8,128)(2,1)S(1)}, bf16[64,512]{1,0:T(8,128)(2,1)S(1)}, u32[]{:S(2)}, u32[]{:S(2)}) collective-permute-start(bf16[64,512]{1,0:T(8,128)(2,1)S(1)} %get-tuple-element.106), channel_id=1, source_target_pairs={{0,6},{2,4},{4,2},{6,0},{8,14},{10,12},{12,10},{14,8},{1,7},{3,5},... | collective-permute-start | bytes 196616 | tf_op jit(solution)/shard_map/ppermute | solution.py:34
  102.0 17.5 %collective-permute-start.26 = (bf16[64,2048]{1,0:T(8,128)(2,1)S(1)}, bf16[64,2048]{1,0:T(8,128)(2,1)S(1)}, u32[]{:S(2)}, u32[]{:S(2)}) collective-permute-start(bf16[64,2048]{1,0:T(8,128)(2,1)S(1)} %get-tuple-element.97), channel_id=1, source_target_pairs={{0,8},{2,10},{4,12},{6,14},{8,0},{10,2},{12,4},{14,6},{1,9},{3,11}... | collective-permute-start | bytes 786440 | tf_op jit(solution)/shard_map/ppermute | solution.py:34
  105.3 12.9 %collective-permute-start.27 = (bf16[64,512]{1,0:T(8,128)(2,1)S(1)}, bf16[64,512]{1,0:T(8,128)(2,1)S(1)}, u32[]{:S(2)}, u32[]{:S(2)}) collective-permute-start(bf16[64,512]{1,0:T(8,128)(2,1)S(1)} %get-tuple-element.107), channel_id=1, source_target_pairs={{0,8},{2,10},{4,12},{6,14},{8,0},{10,2},{12,4},{14,6},{1,9},{3,11}... | collective-permute-start | bytes 196616 | tf_op jit(solution)/shard_map/ppermute | solution.py:34
  (10 other events, 20.3 us)

commit v4 on v3

--- a/solution.py
+++ b/solution.py
@@ -10,7 +10,8 @@
 TENANT_BLOCK = 128
 CAP = 2
 NEAR = 4
-VMEM_LIMIT = 24 * 1024 * 1024
+VMEM_LIMIT = 16 * 1024 * 1024
+LANES = 128
 
 adapter_scale = 2.0
 f32 = jnp.float32
@@ -53,7 +54,7 @@
     return jax.ShapeDtypeStruct(shape, dtype)
 
 
-def _call(body, name, grid, in_specs, out_specs, out_shape, scratch, flops, moved, aliases=None):
+def _call(body, name, grid, in_specs, out_specs, out_shape, scratch, aliases=None):
     return pl.pallas_call(
         body,
         name=name,
@@ -67,7 +68,7 @@
         out_shape=out_shape,
         input_output_aliases=aliases or {},
         compiler_params=pltpu.CompilerParams(vmem_limit_bytes=VMEM_LIMIT),
-        cost_estimate=pl.CostEstimate(flops=flops, bytes_accessed=moved, transcendentals=0),
+        cost_estimate=pl.CostEstimate(flops=1, bytes_accessed=1, transcendentals=0),
     )
 
 
@@ -81,8 +82,7 @@
         self.rank, self.cols, self.width = rank, cols, width
         self.n_far = n_dp // NEAR
         self.rows = nb * TENANT_BLOCK
-        self.me, self.core, self.quarter = 6 * nb, 6 * nb + 1, 6 * nb + 2
-        self.valid = 6 * nb + 3
+        self.me, self.core, self.quarter = (6, 0), (6, 1), (6, 2)
 
     def block(self, b):
         return slice(b * TENANT_BLOCK, (b + 1) * TENANT_BLOCK)
@@ -91,7 +91,10 @@
         return slice(b * self.rank, (b + 1) * self.rank)
 
     def slot(self, info, which, b):
-        return info[which * self.nb + b]
+        return info[which, b]
+
+    def valid(self, info, b):
+        return info[7, b]
 
     def owner_and_order(self, info, which):
         owners = [_div(self.slot(info, which, b), self.ten_dev) for b in range(self.nb)]
@@ -118,19 +121,19 @@
     return jnp.where(row < valid, x, jnp.zeros((), x.dtype))
 
 
-def other_kernel(z, me, x_ref, w_ref, out_ref):
-    far = pl.ds(pl.multiple_of((1 - me[0]) * z.cols, z.cols), z.cols)
+def other_kernel(z, place, x_ref, w_ref, out_ref):
+    far = pl.ds(pl.multiple_of((1 - place[z.core[1]]) * z.cols, z.cols), z.cols)
     out_ref[...] = _dot(x_ref[...], w_ref[:, far], NN).astype(bf16)
 
 
-def own_kernel(z, info, x_ref, w_ref, g_ref, h_ref, out_ref, full_ref):
+def own_kernel(z, info, x_ref, w_ref, far_ref, g_ref, h_ref, out_ref, full_ref):
     own = pl.ds(pl.multiple_of(info[z.core] * z.cols, z.cols), z.cols)
     far = pl.ds(pl.multiple_of((1 - info[z.core]) * z.cols, z.cols), z.cols)
-    out_ref[...] = _dot(x_ref[...], w_ref[:, own], NN)
+    out_ref[...] = _dot(x_ref[...], w_ref[:, own], NN) + far_ref[...].astype(f32)
     for b in range(z.nb):
         cut = z.block(b)
-        full_ref[cut, own] = _masked(g_ref[cut, :], info[z.valid + b])
-        full_ref[cut, far] = _masked(h_ref[cut, :], info[z.valid + b])
+        full_ref[cut, own] = _masked(g_ref[cut, :], z.valid(info, b))
+        full_ref[cut, far] = _masked(h_ref[cut, :], z.valid(info, b))
 
 
 def back_kernel(z, info, g_ref, *refs):
@@ -145,7 +148,7 @@
         for k in range(1, NEAR):
             u = jnp.where(near == k, packets[k][at, :], u)
         up_ref[z.ranks(b), :] = u
-        g = _masked(g_ref[z.block(b), :], info[z.valid + b])
+        g = _masked(g_ref[z.block(b), :], z.valid(info, b))
         part_ref[:, z.block(b)] = _dot(u, g, NT)
 
 
@@ -249,7 +252,7 @@
         out_ref[:, z.block(b)] = total[z.block(b), :].T[z.ranks(b), :]
 
 
-def projected_kernel(z, info, base_ref, far_ref, mine_ref, other_ref, up_ref, out_ref, spread):
+def projected_kernel(z, info, base_ref, mine_ref, other_ref, up_ref, out_ref, spread):
     spread[...] = jnp.zeros_like(spread)
     for b in range(z.nb):
         cut = z.block(b)
@@ -257,8 +260,8 @@
     wide = _dot(spread[...], up_ref[...], TN)
     for b in range(z.nb):
         cut = z.block(b)
-        full = base_ref[cut, :] + far_ref[cut, :].astype(f32) + adapter_scale * wide[cut]
-        out_ref[cut, :] = _masked(full, info[z.valid + b]).astype(bf16)
+        full = base_ref[cut, :] + adapter_scale * wide[cut]
+        out_ref[cut, :] = _masked(full, z.valid(info, b)).astype(bf16)
 
 
 def tokens_kernel(z, first, info, g_ref, w_ref, mine_ref, other_ref, d_ref, *refs):
@@ -306,51 +309,58 @@
     mine_q = group * 2 + me % 2 if shared else jnp.int32(0)
     quarter = width // n_parts
 
-    far_up = [_xor(adapter_up, n_dp, NEAR * j) for j in range(1, n_far)]
     down_t = jnp.swapaxes(adapter_down, 1, 2)
     if shared:
         to_y = lax.dynamic_slice_in_dim(down_t, (mine_q ^ 1) * quarter, quarter, axis=2)
         from_y = _xor(to_y, n_dp, 1)
-    tenant_match = block_tenant[:, None] == jnp.arange(tenants, dtype=i32)[None, :]
+    far_up = [_xor(adapter_up, n_dp, NEAR * j) for j in range(1, n_far)]
+    lanes = jnp.pad(block_tenant, (0, LANES - nb))
+    tenant_match = lanes[:, None] == jnp.arange(tenants, dtype=i32)[None, :]
     slots = jnp.sum(jnp.where(tenant_match, tenant_slot[None, :], 0), axis=1).astype(i32)
+    lane = jnp.arange(LANES, dtype=i32)
+    place = jnp.where(lane == 0, me, jnp.where(lane == 1, core, mine_q))
+    slots = _tie(slots, place)
     slots_x = _swap(slots, "groups") if shared else slots
-    cotangent_other = _swap(out_cotangent, "tensor")
-
-    tag = jnp.zeros((16, cols), bf16)
-    tag = tag.at[0, :nb].set(slots.astype(bf16)).at[1, :nb].set(slots_x.astype(bf16))
+
+    line = lax.broadcasted_iota(i32, (16, LANES), 0)
+    tag = jnp.where(line == 0, slots[None, :], slots_x[None, :]).astype(bf16)
+    tag = jnp.pad(tag, ((0, 0), (0, cols - LANES)))
     ups = [u.reshape(ten_dev * rank, cols) for u in [adapter_up] + far_up]
     packet = jnp.concatenate(ups + [tag], axis=0)
     packets = [packet] + [_xor(packet, n_dp, k) for k in range(1, NEAR)]
 
-    gate = packet
     if shared:
         own = lax.dynamic_slice_in_dim(down_t, mine_q * quarter, quarter, axis=2)
-        shard = _tie(jnp.concatenate([own, from_y], axis=0), packet)
+        shard = jnp.concatenate([own, from_y], axis=0)
         shard_far = _xor(shard, n_dp, 4)
         shard_near = _xor(shard, n_dp, 2)
-        gate = shard
 
     base_other = _call(
         functools.partial(other_kernel, z), "base_other", (1,),
         [VMEM, VMEM], _whole((rows, cols)), _shape((rows, cols), bf16), [],
-        2 * rows * cols * width, 2 * rows * cols,
-    )(_tie(jnp.full((1,), core, i32), gate), tokens, base_weight)
+    )(_tie(place, shard if shared else packet), tokens, base_weight)
     base_arrived = _swap(base_other, "tensor")
-
-    tags = [p[-16:-14, :nb].astype(i32) for p in packets]
-    info = jnp.concatenate(
-        [tags[k][0] for k in range(NEAR)]
-        + [tags[0][1], tags[1][1], jnp.stack([me, core, mine_q]), block_valid]
-    ).astype(i32)
+    packets = [_tie(p, base_other) for p in packets]
+
+    line = lax.broadcasted_iota(i32, (8, LANES), 0)
+    info = jnp.where(line == 6, place[None, :], jnp.pad(block_valid, (0, LANES - nb))[None, :])
+    for k in range(NEAR):
+        info = jnp.where(line == k, packets[k][-16, :LANES].astype(i32)[None, :], info)
+    for k in range(2):
+        info = jnp.where(line == 4 + k, packets[k][-15, :LANES].astype(i32)[None, :], info)
+
+    if shared:
+        info = _tie(info, shard_far, shard_near)
+        farther = _xor(shard_far, n_dp, 2)
 
     part = (rank, rows)
     block_up, back_part = _call(
         functools.partial(back_kernel, z), "back", (1,),
         [VMEM] * (1 + NEAR), [VMEM, _whole(part)],
         [_shape((nb * rank, cols), bf16), _shape(part, f32)], [],
-        2 * rows * cols * rank * 8, 2 * rows * cols,
-    )(_tie(info, base_other), out_cotangent, *packets)
+    )(info, out_cotangent, *packets)
     back_other = _swap(back_part, "tensor")
+    cotangent_other = _swap(_tie(out_cotangent, back_part), "tensor")
 
     packed_rows = n_dp * CAP * rank
     near_rows = packed_rows // NEAR
@@ -361,7 +371,6 @@
             [VMEM] * 3, [_whole((near_rows, wide))] * NEAR,
             [_shape((near_rows, wide), bf16)] * NEAR,
             [pltpu.VMEM((packed_rows, rows), bf16)],
-            2 * packed_rows * rows * wide, 2 * packed_rows * wide,
         )(info, back_part, back_other, tokens)
 
     def to_near(sends):
@@ -374,7 +383,6 @@
             functools.partial(dense_kernel, z), "dense", (1,),
             [VMEM] * NEAR, [VMEM] + [_whole(out)] * (n_far - 1),
             [_shape(out, f32)] + [_shape(out, bf16)] * (n_far - 1), [],
-            2 * packed_rows * ten_dev * rank * wide, 2 * packed_rows * wide,
         )(info, *got)
 
     def to_far(parts):
@@ -386,99 +394,94 @@
         total = _call(
             functools.partial(final_kernel, len(groups), n_far), "final", (1,),
             [VMEM] * (len(groups) * n_far), _whole(out), _shape(out, f32), [],
-            ten_dev * rank * wide, 10 * ten_dev * rank * wide,
         )(info, *[a for g in groups for a in g])
         return total.reshape(ten_dev, rank, wide)
 
     half = width // 2
-    sends_a = pack(info, 0, half)
+    sends_a = pack(_tie(info, cotangent_other, base_arrived), 0, half)
     got_a = to_near(sends_a)
-    sends_b = pack(_tie(info, sends_a[0]), half, half)
-    got_b = to_near(sends_b)
-
-    if shared:
-        farther = _xor(_tie(shard_far, sends_b[0]), n_dp, 2)
-
-    base_own, g_full = _call(
-        functools.partial(own_kernel, z), "base_own", (1,),
-        [VMEM] * 4, [VMEM, VMEM],
-        [_shape((rows, cols), f32), _shape((rows, 2 * cols), bf16)], [],
-        2 * rows * cols * width, 12 * rows * cols,
-    )(_tie(info, sends_b[0]), tokens, base_weight, out_cotangent, cotangent_other)
 
     if shared:
         block = (nb * rank, quarter)
         chosen = _call(
             functools.partial(choose_kernel, z), "choose", (1,),
             [VMEM] * 4, [_whole(block)] * 4, [_shape(block, bf16)] * 4, [],
-            0, 4 * shard.size,
-        )(_tie(info, base_own), shard, shard_near, shard_far, farther)
-        got_down = [
-            chosen[0],
-            _xor(chosen[1], n_dp, 1),
-            _swap(chosen[2], "groups"),
-            lax.ppermute(
-                chosen[3],
-                ("groups", "dp"),
-                [(g * n_dp + d, (1 - g) * n_dp + (d ^ 1)) for g in range(2) for d in range(n_dp)],
-            ),
-        ]
+        )(_tie(info, sends_a[0]), shard, shard_near, shard_far, farther)
+        got_x = _swap(chosen[2], "groups")
+        got_d = lax.ppermute(
+            chosen[3],
+            ("groups", "dp"),
+            [(g * n_dp + d, (1 - g) * n_dp + (d ^ 1)) for g in range(2) for d in range(n_dp)],
+        )
         after_choose = chosen[0]
     else:
         every = lax.all_gather(down_t, "dp", axis=0, tiled=True)
-        got_down = [jnp.take(every, slots, axis=0).reshape(nb * rank, width)]
-        after_choose = base_own
-
-    dense_a = dense(_tie(info, after_choose), got_a)
+        got_down = [jnp.take(every, slots[:nb], axis=0).reshape(nb * rank, width)]
+        after_choose = sends_a[0]
+
+    sends_b = pack(_tie(info, after_choose), half, half)
+    got_b = to_near(sends_b)
+
+    base_own, g_full = _call(
+        functools.partial(own_kernel, z), "base_own", (1,),
+        [VMEM] * 5, [VMEM, VMEM],
+        [_shape((rows, cols), f32), _shape((rows, 2 * cols), bf16)], [],
+    )(_tie(info, sends_b[0]), tokens, base_weight, base_arrived, out_cotangent, cotangent_other)
+
+    if shared:
+        got_y = _xor(_tie(chosen[1], base_own), n_dp, 1)
+        got_down = [chosen[0], got_y, got_x, got_d]
+    dense_a = dense(_tie(info, base_own), got_a)
     far_a = to_far(dense_a)
 
     block_down, shrink_part = _call(
         functools.partial(shrink_kernel, z, n_parts), "shrink", (1,),
         [VMEM] * (1 + n_parts), [VMEM, _whole(part)],
         [_shape((nb * rank, width), bf16), _shape(part, f32)], [],
-        2 * rows * width * 128, 2 * nb * rank * width,
     )(_tie(info, dense_a[1]), tokens, *got_down)
     shrink_other = _swap(shrink_part, "tensor")
 
-    dense_b = dense(_tie(info, shrink_part), got_b)
-    far_b = to_far(dense_b)
+    step = min(512, width // 8)
+    n_calls = 4
+    per_call = width // step // n_calls
+
+    def token_grads(info, call, so_far):
+        first = call * per_call
+        return _call(
+            functools.partial(tokens_kernel, z, first), "token_grads", (per_call,),
+            [VMEM] * 5 + ([] if so_far is None else [pl.BlockSpec(memory_space=pl.ANY)]),
+            pl.BlockSpec((rows, step), lambda i, *_: (0, first + i)),
+            _shape((rows, width), bf16), [pltpu.VMEM((nb * rank, rows), bf16)],
+            None if so_far is None else {6: 0},
+        )(
+            info, g_full, base_weight, back_part, back_other, block_down,
+            *([] if so_far is None else [so_far]),
+        )
+
+    grad_tokens = token_grads(_tie(info, shrink_part), 0, None)
 
     up_sends = _call(
         functools.partial(pack_up_kernel, z, NEAR), "pack_up", (1,),
         [VMEM] * 3, [_whole((near_rows, cols))] * NEAR,
         [_shape((near_rows, cols), bf16)] * NEAR,
         [pltpu.VMEM((packed_rows, rows), bf16)],
-        2 * packed_rows * rows * cols, 2 * rows * cols + 2 * packed_rows * cols,
-    )(_tie(info, dense_b[1]), shrink_part, shrink_other, g_full)
+    )(_tie(info, grad_tokens), shrink_part, shrink_other, g_full)
     got_u = to_near(up_sends)
 
-    step = min(1024, width // 4)
-    n_steps = width // step
-
-    def token_grads(info, first, count, so_far=None):
-        return _call(
-            functools.partial(tokens_kernel, z, first), "token_grads", (count,),
-            [VMEM] * 5 + ([] if so_far is None else [pl.BlockSpec(memory_space=pl.ANY)]),
-            pl.BlockSpec((rows, step), lambda i, *_: (0, first + i)),
-            _shape((rows, width), bf16), [pltpu.VMEM((nb * rank, rows), bf16)],
-            4 * rows * cols * step * count, 2 * rows * step * count,
-            None if so_far is None else {6: 0},
-        )(
-            info, g_full, base_weight, back_part, back_other, block_down,
-            *([] if so_far is None else [so_far]),
-        )
-
-    grads_1 = token_grads(_tie(info, up_sends[0]), 0, n_steps // 2)
-    dense_u = dense(_tie(info, grads_1), got_u)
+    dense_b = dense(_tie(info, up_sends[0]), got_b)
+    far_b = to_far(dense_b)
+
+    grad_tokens = token_grads(_tie(info, dense_b[1]), 1, grad_tokens)
+    dense_u = dense(_tie(info, grad_tokens), got_u)
     far_u = to_far(dense_u)
-    grad_tokens = token_grads(_tie(info, dense_u[1]), n_steps // 2, n_steps - n_steps // 2, grads_1)
+    grad_tokens = token_grads(_tie(info, dense_u[1]), 2, grad_tokens)
+    grad_tokens = token_grads(info, 3, grad_tokens)
 
     projected = _call(
         functools.partial(projected_kernel, z), "projected", (1,),
-        [VMEM] * 5, _whole((rows, cols)), _shape((rows, cols), bf16),
+        [VMEM] * 4, _whole((rows, cols)), _shape((rows, cols), bf16),
         [pltpu.VMEM((nb * rank, rows), bf16)],
-        2 * rows * cols * 128, 8 * rows * cols,
-    )(_tie(info, grad_tokens), base_own, base_arrived, shrink_part, shrink_other, block_up)
+    )(_tie(info, grad_tokens), base_own, shrink_part, shrink_other, block_up)
 
     grad_up = final([far_u])
     grad_down = jnp.swapaxes(final([far_a, far_b]), 1, 2)

time: 121 us -> 109 us (0.901)
  waiting for transfers between devices: 27.1 us -> 12.5 us
  local copies, waits for them, and re-layouts: 15.5 us -> 8.78 us
  Pallas kernels: 40 us -> 44.5 us
  starting transfers between devices: 35.8 us -> 40.2 us
    ppermute x21, waiting for transfers between devices: 27.1 us -> 11.4 us  [_xor(): return lax.ppermute(x, 'dp', [(i, i ^ k) for i in range(n)])]
    unnamed x28 -> x12, local copies, waits for them, and re-layouts: 14.3 us -> 6.48 us
    pallas_call x3 -> x5, Pallas kernels: 18.7 us -> 22.2 us  [the longest x4 17.5 us: token_grads(): _call(functools.partial(tokens_kernel, z, first), 'token_grads', (per_cal...]
    ppermute x6, starting transfers between devices: 2.66 us -> 4.42 us  [_swap(): return lax.ppermute(x, axis, [(0, 1), (1, 0)])]
    ppermute x21, starting transfers between devices: 31.8 us -> 33.4 us  [_xor(): return lax.ppermute(x, 'dp', [(i, i ^ k) for i in range(n)])]
    pad x0 -> x2, local copies, waits for them, and re-layouts: none -> 1.32 us  [the longest x1 0.66 us: on_device(): lanes = jnp.pad(block_tenant, (0, LANES - nb))]
  transfers between devices with their start and end apart: 28 -> 28, of which waited for: 5 -> 8; matrix products, arithmetic and copies ran while one was open for 2% -> 3% of each run, Pallas kernels for 32% -> 39%
where the time goes in v4:
time: 109 us
  Pallas kernels  44.5 us (41%)
  starting transfers between devices  40.2 us (37%)
  waiting for transfers between devices  12.5 us (11%)
  local copies, waits for them, and re-layouts  8.78 us (8%)
  other arithmetic  1.82 us (2%)
    ppermute x21, starting transfers between devices, _xor(): return lax.ppermute(x, 'dp', [(i, i ^ k) for i in range(n)])  33.4 us
    pallas_call x4, Pallas kernels, token_grads(): _call(functools.partial(tokens_kernel, z, first), 'token_grads', (per_cal...  17.5 us
    ppermute x21, waiting for transfers between devices, _xor(): return lax.ppermute(x, 'dp', [(i, i ^ k) for i in range(n)])  11.4 us
    unnamed x12, local copies, waits for them, and re-layouts  6.48 us
    pallas_call x1, Pallas kernels, on_device(): _call(functools.partial(own_kernel, z), 'base_own', (1,), [VMEM] * 5, [VM...  4.69 us
    pallas_call x1, Pallas kernels, on_device(): _call(functools.partial(other_kernel, z), 'base_other', (1,), [VMEM, VMEM...  4.5 us
    ppermute x6, starting transfers between devices, _swap(): return lax.ppermute(x, axis, [(0, 1), (1, 0)])  4.42 us
    pallas_call x2, Pallas kernels, pack(): _call(functools.partial(pack_kernel, z, NEAR, start), 'pack_down', (1,),...  3.77 us
  transfers between devices with their start and end apart: 28, of which 8 were waited for; matrix products, arithmetic and copies ran while one was open for 3% of the time, Pallas kernels for 39%

profile of v4, /device:TPU:0, one launch (start us, length us, event | category | flops | bytes accessed | tf_op | source)
XLA Modules:
  0.0 108.7 jit_solution(17097453920405012383)
XLA Ops:
  2.0 3.0 %collective-permute-start.1 = (s32[128]{0:T(128)S(1)}, s32[128]{0:T(128)S(1)}, u32[]{:S(2)}, u32[]{:S(2)}) collective-permute-start(s32[128]{0:T(128)S(1)} %select_reduce_fusion), channel_id=1, source_target_pairs={{0,16},{16,0},{1,17},{17,1},{2,18},{18,2},{3,19},{19,3},{4,20},{20... | collective-permute-start | bytes 1544 | tf_op jit(solution)/shard_map/ppermute | solution.py:31
  5.0 2.6 %collective-permute-start = (bf16[4,16,512]{2,1,0:T(8,128)(2,1)}, bf16[4,16,512]{2,1,0:T(8,128)(2,1)S(1)}, u32[]{:S(2)}, u32[]{:S(2)}) collective-permute-start(bf16[4,16,512]{2,1,0:T(8,128)(2,1)} %param.11), channel_id=1, source_target_pairs={{0,8},{2,10},{4,12},{6,14},{8,0},{10,2},{12,4},{14,6},{1,9},{3,11}... | collective-permute-start | bytes 196616 | tf_op jit(solution)/shard_map/ppermute | solution.py:35
  8.6 1.6 %collective-permute-start.3 = (bf16[4,16,1024]{2,1,0:T(8,128)(2,1)S(1)}, bf16[4,16,1024]{2,1,0:T(8,128)(2,1)S(1)}, u32[]{:S(2)}, u32[]{:S(2)}) collective-permute-start(bf16[4,16,1024]{2,1,0:T(8,128)(2,1)S(1)} %get-tuple-element.105), channel_id=1, source_target_pairs={{0,2},{2,0},{4,6},{6,4},{8,10},{10,8},{12,14},{14,12},{1,3},{3,1},... | collective-permute-start | bytes 393224 | tf_op jit(solution)/shard_map/ppermute | solution.py:35
  11.6 1.3 %collective-permute-start.5 = (bf16[144,512]{1,0:T(8,128)(2,1)S(1)}, bf16[144,512]{1,0:T(8,128)(2,1)S(1)}, u32[]{:S(2)}, u32[]{:S(2)}) collective-permute-start(bf16[144,512]{1,0:T(8,128)(2,1)S(1)} %fusion.1.refs_0_), channel_id=1, source_target_pairs={{0,4},{2,6},{4,0},{6,2},{8,12},{10,14},{12,8},{14,10},{1,5},{3,7},... | collective-permute-start | bytes 442376 | tf_op jit(solution)/shard_map/ppermute | solution.py:35
  12.9 1.7 %collective-permute-start.4 = (bf16[144,512]{1,0:T(8,128)(2,1)S(1)}, bf16[144,512]{1,0:T(8,128)(2,1)S(1)}, u32[]{:S(2)}, u32[]{:S(2)}) collective-permute-start(bf16[144,512]{1,0:T(8,128)(2,1)S(1)} %fusion.1.refs_0_), channel_id=1, source_target_pairs={{0,6},{2,4},{4,2},{6,0},{8,14},{10,12},{12,10},{14,8},{1,7},{3,5},... | collective-permute-start | bytes 442376 | tf_op jit(solution)/shard_map/ppermute | solution.py:35
  15.8 1.3 %collective-permute-start.7 = (bf16[8,16,1024]{2,1,0:T(8,128)(2,1)S(1)}, bf16[8,16,1024]{2,1,0:T(8,128)(2,1)S(1)}, u32[]{:S(2)}, u32[]{:S(2)}) collective-permute-start(bf16[8,16,1024]{2,1,0:T(8,128)(2,1)S(1)} %pad_maximum_fusion.own_ref), channel_id=1, source_target_pairs={{0,4},{2,6},{4,0},{6,2},{8,12},{10,14},{12,8},{14,10},{1,5},{3,7},... | collective-permute-start | bytes 786440 | tf_op jit(solution)/shard_map/ppermute | solution.py:35
  17.2 3.2 %collective-permute-start.6 = (bf16[8,16,1024]{2,1,0:T(8,128)(2,1)S(1)}, bf16[8,16,1024]{2,1,0:T(8,128)(2,1)S(1)}, u32[]{:S(2)}, u32[]{:S(2)}) collective-permute-start(bf16[8,16,1024]{2,1,0:T(8,128)(2,1)S(1)} %pad_maximum_fusion.own_ref), channel_id=1, source_target_pairs={{0,8},{2,10},{4,12},{6,14},{8,0},{10,2},{12,4},{14,6},{1,9},{3,11}... | collective-permute-start | bytes 786440 | tf_op jit(solution)/shard_map/ppermute | solution.py:35
  20.3 3.4 %copy-done = bf16[4096,1024]{1,0:T(8,128)(2,1)S(1)} copy-done((bf16[4096,1024]{1,0:T(8,128)(2,1)S(1)}, bf16[4096,1024]{1,0:T(8,128)(2,1)}, u32[]{:S(2)}) %copy-start) | copy-done | bytes 8388632
  23.7 3.1 %copy-done.1 = bf16[896,4096]{1,0:T(8,128)(2,1)S(1)} copy-done((bf16[896,4096]{1,0:T(8,128)(2,1)S(1)}, bf16[896,4096]{1,0:T(8,128)(2,1)}, u32[]{:S(2)}) %copy-start.1) | copy-done | bytes 7340056
  26.8 4.5 %base_other.1 = bf16[896,512]{1,0:T(8,128)(2,1)S(1)} custom-call(s32[128]{0:T(128)S(1)} %compare_select_fusion.1.place, bf16[896,4096]{1,0:T(8,128)(2,1)S(1)} %copy-done.1, bf16[4096,1024]{1,0:T(8,128)(2,1)S(1)} %copy-done), custom_call_target="tpu_custom_call" | custom-call | flops 1 | bytes 1 | tf_op jit(solution)/shard_map/base_other/pallas_call | solution.py:338
  33.0 1.6 %collective-permute-start.11 = (bf16[8,16,1024]{2,1,0:T(8,128)(2,1)S(1)}, bf16[8,16,1024]{2,1,0:T(8,128)(2,1)S(1)}, u32[]{:S(2)}, u32[]{:S(2)}) collective-permute-start(bf16[8,16,1024]{2,1,0:T(8,128)(2,1)S(1)} %collective-permute-done.6.far_ref), channel_id=1, source_target_pairs={{0,4},{2,6},{4,0},{6,2},{8,12},{10,14},{12,8},{14,10},{1,5},{3,7},... | collective-permute-start | bytes 786440 | tf_op jit(solution)/shard_map/ppermute | solution.py:35
  35.9 1.9 %pack_down.2 = (bf16[64,2048]{1,0:T(8,128)(2,1)S(1)}, bf16[64,2048]{1,0:T(8,128)(2,1)S(1)}, bf16[64,2048]{1,0:T(8,128)(2,1)S(1)}, bf16[64,2048]{1,0:T(8,128)(2,1)S(1)}) custom-call(s32[8,128]{1,0:T(8,128)S(1)} %select_select_fusion.info, f32[16,896]{1,0:T(8,128)S(1)} %get-tuple-element.61.mine_ref, f32[16,896]{1,0:T(8,128)S(1)} %collective-permute-done.10.other_ref, ...), custom_call_target="tpu_custom_call" | custom-call | flops 1 | bytes 1 | tf_op jit(solution)/shard_map/pack_down/pallas_call | solution.py:369
  39.9 1.4 %collective-permute-start.14 = (bf16[64,2048]{1,0:T(8,128)(2,1)S(1)}, bf16[64,2048]{1,0:T(8,128)(2,1)S(1)}, u32[]{:S(2)}, u32[]{:S(2)}) collective-permute-start(bf16[64,2048]{1,0:T(8,128)(2,1)S(1)} %get-tuple-element.75), channel_id=1, source_target_pairs={{0,6},{2,4},{4,2},{6,0},{8,14},{10,12},{12,10},{14,8},{1,7},{3,5},... | collective-permute-start | bytes 786440 | tf_op jit(solution)/shard_map/ppermute | solution.py:35
  43.1 2.4 %collective-permute-start.17 = (bf16[112,1024]{1,0:T(8,128)(2,1)S(1)}, bf16[112,1024]{1,0:T(8,128)(2,1)S(1)}, u32[]{:S(2)}, u32[]{:S(2)}) collective-permute-start(bf16[112,1024]{1,0:T(8,128)(2,1)S(1)} %get-tuple-element.81), channel_id=1, source_target_pairs={{0,18},{2,16},{4,22},{6,20},{8,26},{10,24},{12,30},{14,28},{16,2},... | collective-permute-start | bytes 688136 | tf_op jit(solution)/shard_map/ppermute | solution.py:411
  45.5 1.9 %pack_down.3 = (bf16[64,2048]{1,0:T(8,128)(2,1)S(1)}, bf16[64,2048]{1,0:T(8,128)(2,1)S(1)}, bf16[64,2048]{1,0:T(8,128)(2,1)S(1)}, bf16[64,2048]{1,0:T(8,128)(2,1)S(1)}) custom-call(s32[8,128]{1,0:T(8,128)S(1)} %select_select_fusion.info, f32[16,896]{1,0:T(8,128)S(1)} %get-tuple-element.61.mine_ref, f32[16,896]{1,0:T(8,128)S(1)} %collective-permute-done.10.other_ref, ...), custom_call_target="tpu_custom_call" | custom-call | flops 1 | bytes 1 | tf_op jit(solution)/shard_map/pack_down/pallas_call | solution.py:369
  47.4 4.7 %base_own.1 = (f32[896,512]{1,0:T(8,128)S(1)}, bf16[896,1024]{1,0:T(8,128)(2,1)S(1)}) custom-call(s32[8,128]{1,0:T(8,128)S(1)} %select_select_fusion.info, bf16[896,4096]{1,0:T(8,128)(2,1)S(1)} %copy-done.2, bf16[4096,1024]{1,0:T(8,128)(2,1)S(1)} %bitcast.29, bf16[896,512]{1,0:T(8,128)(2,1)S(1)} %collective-permute-done.9.far_ref, ...), custom_call_target="tpu_custom_call" | custom-call | flops 1 | bytes 1 | tf_op jit(solution)/shard_map/base_own/pallas_call | solution.py:425
  52.7 1.5 %collective-permute-start.19 = (bf16[64,2048]{1,0:T(8,128)(2,1)S(1)}, bf16[64,2048]{1,0:T(8,128)(2,1)S(1)}, u32[]{:S(2)}, u32[]{:S(2)}) collective-permute-start(bf16[64,2048]{1,0:T(8,128)(2,1)S(1)} %get-tuple-element.88), channel_id=1, source_target_pairs={{0,2},{2,0},{4,6},{6,4},{8,10},{10,8},{12,14},{14,12},{1,3},{3,1},... | collective-permute-start | bytes 786440 | tf_op jit(solution)/shard_map/ppermute | solution.py:35
  54.2 1.4 %collective-permute-start.20 = (bf16[64,2048]{1,0:T(8,128)(2,1)S(1)}, bf16[64,2048]{1,0:T(8,128)(2,1)S(1)}, u32[]{:S(2)}, u32[]{:S(2)}) collective-permute-start(bf16[64,2048]{1,0:T(8,128)(2,1)S(1)} %get-tuple-element.89), channel_id=1, source_target_pairs={{0,4},{2,6},{4,0},{6,2},{8,12},{10,14},{12,8},{14,10},{1,5},{3,7},... | collective-permute-start | bytes 786440 | tf_op jit(solution)/shard_map/ppermute | solution.py:35
  55.6 2.2 %collective-permute-done.14.refs_3_ = bf16[64,2048]{1,0:T(8,128)(2,1)S(1)} collective-permute-done((bf16[64,2048]{1,0:T(8,128)(2,1)S(1)}, bf16[64,2048]{1,0:T(8,128)(2,1)S(1)}, u32[]{:S(2)}, u32[]{:S(2)}) %collective-permute-start.14) | collective-permute-done | bytes 262176 | tf_op jit(solution)/shard_map/ppermute | solution.py:35
  57.8 2.0 %collective-permute-start.21 = (bf16[64,2048]{1,0:T(8,128)(2,1)S(1)}, bf16[64,2048]{1,0:T(8,128)(2,1)S(1)}, u32[]{:S(2)}, u32[]{:S(2)}) collective-permute-start(bf16[64,2048]{1,0:T(8,128)(2,1)S(1)} %get-tuple-element.90), channel_id=1, source_target_pairs={{0,6},{2,4},{4,2},{6,0},{8,14},{10,12},{12,10},{14,8},{1,7},{3,5},... | collective-permute-start | bytes 786440 | tf_op jit(solution)/shard_map/ppermute | solution.py:35
  59.8 1.3 %dense.3 = (f32[64,2048]{1,0:T(8,128)S(1)}, bf16[64,2048]{1,0:T(8,128)(2,1)S(1)}) custom-call(s32[8,128]{1,0:T(8,128)S(1)} %select_select_fusion.info, bf16[64,2048]{1,0:T(8,128)(2,1)S(1)} %get-tuple-element.64.refs_0_, bf16[64,2048]{1,0:T(8,128)(2,1)S(1)} %collective-permute-done.12.refs_1_, bf16[64,2048]{1,0:T(8,128)(2,1)S(1)} %collective-permute-done.13.refs_2_, ...), custom_call_target="tpu_custom_call" | custom-call | flops 1 | bytes 1 | tf_op jit(solution)/shard_map/dense/pallas_call | solution.py:382
  61.1 7.5 %collective-permute-done.15.refs_1_ = bf16[112,1024]{1,0:T(8,128)(2,1)S(1)} collective-permute-done((bf16[112,1024]{1,0:T(8,128)(2,1)S(1)}, bf16[112,1024]{1,0:T(8,128)(2,1)S(1)}, u32[]{:S(2)}, u32[]{:S(2)}) %collective-permute-start.15) | collective-permute-done | bytes 229408 | tf_op jit(solution)/shard_map/ppermute | solution.py:35
  68.6 2.7 %shrink.1 = (bf16[112,4096]{1,0:T(8,128)(2,1)S(1)}, f32[16,896]{1,0:T(8,128)S(1)}) custom-call(s32[8,128]{1,0:T(8,128)S(1)} %select_select_fusion.info, bf16[896,4096]{1,0:T(8,128)(2,1)S(1)} %copy-done.2, bf16[112,1024]{1,0:T(8,128)(2,1)S(1)} %get-tuple-element.66.refs_0_, bf16[112,1024]{1,0:T(8,128)(2,1)S(1)} %collective-permute-done.15.refs_1_, ...), custom_call_target="tpu_custom_call" | custom-call | flops 1 | bytes 1 | tf_op jit(solution)/shard_map/shrink/pallas_call | solution.py:437
  71.4 1.9 %collective-permute-start.25 = (bf16[64,2048]{1,0:T(8,128)(2,1)S(1)}, bf16[64,2048]{1,0:T(8,128)(2,1)S(1)}, u32[]{:S(2)}, u32[]{:S(2)}) collective-permute-start(bf16[64,2048]{1,0:T(8,128)(2,1)S(1)} %get-tuple-element.76), channel_id=1, source_target_pairs={{0,8},{2,10},{4,12},{6,14},{8,0},{10,2},{12,4},{14,6},{1,9},{3,11}... | collective-permute-start | bytes 786440 | tf_op jit(solution)/shard_map/ppermute | solution.py:35
  73.3 4.5 %token_grads.4.refs_0_ = bf16[896,4096]{1,0:T(8,128)(2,1)} custom-call(s32[8,128]{1,0:T(8,128)S(1)} %select_select_fusion.info, bf16[896,1024]{1,0:T(8,128)(2,1)S(1)} %get-tuple-element.70.g_ref, bf16[4096,1024]{1,0:T(8,128)(2,1)S(1)} %bitcast.29, f32[16,896]{1,0:T(8,128)S(1)} %get-tuple-element.61.mine_ref, ...), custom_call_target="tpu_custom_call" | custom-call | flops 1 | bytes 1 | tf_op jit(solution)/shard_map/token_grads/pallas_call | solution.py:450
  82.6 1.8 %collective-permute-start.23 = (bf16[64,512]{1,0:T(8,128)(2,1)S(1)}, bf16[64,512]{1,0:T(8,128)(2,1)S(1)}, u32[]{:S(2)}, u32[]{:S(2)}) collective-permute-start(bf16[64,512]{1,0:T(8,128)(2,1)S(1)} %get-tuple-element.95), channel_id=1, source_target_pairs={{0,4},{2,6},{4,0},{6,2},{8,12},{10,14},{12,8},{14,10},{1,5},{3,7},... | collective-permute-start | bytes 196616 | tf_op jit(solution)/shard_map/ppermute | solution.py:35
  84.9 4.3 %token_grads.5.refs_0_ = bf16[896,4096]{1,0:T(8,128)(2,1)} custom-call(s32[8,128]{1,0:T(8,128)S(1)} %select_select_fusion.info, bf16[896,1024]{1,0:T(8,128)(2,1)S(1)} %get-tuple-element.70.g_ref, bf16[4096,1024]{1,0:T(8,128)(2,1)S(1)} %bitcast.29, f32[16,896]{1,0:T(8,128)S(1)} %get-tuple-element.61.mine_ref, ...), custom_call_target="tpu_custom_call", output_to_operand_aliasing={{}: (6, {})} | custom-call | flops 1 | bytes 1 | tf_op jit(solution)/shard_map/token_grads/pallas_call | solution.py:450
  91.1 4.0 %collective-permute-start.27 = (bf16[64,512]{1,0:T(8,128)(2,1)S(1)}, bf16[64,512]{1,0:T(8,128)(2,1)S(1)}, u32[]{:S(2)}, u32[]{:S(2)}) collective-permute-start(bf16[64,512]{1,0:T(8,128)(2,1)S(1)} %get-tuple-element.97), channel_id=1, source_target_pairs={{0,8},{2,10},{4,12},{6,14},{8,0},{10,2},{12,4},{14,6},{1,9},{3,11}... | collective-permute-start | bytes 196616 | tf_op jit(solution)/shard_map/ppermute | solution.py:35
  95.2 4.3 %token_grads.6.refs_0_ = bf16[896,4096]{1,0:T(8,128)(2,1)} custom-call(s32[8,128]{1,0:T(8,128)S(1)} %select_select_fusion.info, bf16[896,1024]{1,0:T(8,128)(2,1)S(1)} %get-tuple-element.70.g_ref, bf16[4096,1024]{1,0:T(8,128)(2,1)S(1)} %bitcast.29, f32[16,896]{1,0:T(8,128)S(1)} %get-tuple-element.61.mine_ref, ...), custom_call_target="tpu_custom_call", output_to_operand_aliasing={{}: (6, {})} | custom-call | flops 1 | bytes 1 | tf_op jit(solution)/shard_map/token_grads/pallas_call | solution.py:450
  99.5 4.3 %token_grads.7 = bf16[896,4096]{1,0:T(8,128)(2,1)} custom-call(s32[8,128]{1,0:T(8,128)S(1)} %select_select_fusion.info, bf16[896,1024]{1,0:T(8,128)(2,1)S(1)} %get-tuple-element.70.g_ref, bf16[4096,1024]{1,0:T(8,128)(2,1)S(1)} %bitcast.29, f32[16,896]{1,0:T(8,128)S(1)} %get-tuple-element.61.mine_ref, ...), custom_call_target="tpu_custom_call", output_to_operand_aliasing={{}: (6, {})} | custom-call | flops 1 | bytes 1 | tf_op jit(solution)/shard_map/token_grads/pallas_call | solution.py:450
  103.8 2.0 %projected.1 = bf16[896,512]{1,0:T(8,128)(2,1)} custom-call(s32[8,128]{1,0:T(8,128)S(1)} %select_select_fusion.info, f32[896,512]{1,0:T(8,128)S(1)} %get-tuple-element.71.base_ref, f32[16,896]{1,0:T(8,128)S(1)} %get-tuple-element.83.mine_ref, f32[16,896]{1,0:T(8,128)S(1)} %collective-permute-done.18.other_ref, bf16[112,512]{1,0:T(8,128)(2,1)S(1)} %get-tuple-element.100.up_ref), custom_call_target="tpu_custom_call" | custom-call | flops 1 | bytes 1 | tf_op jit(solution)/shard_map/projected/pallas_call | solution.py:480
  107.1 1.7 %final.2 = f32[64,4096]{1,0:T(8,128)} custom-call(s32[8,128]{1,0:T(8,128)S(1)} %select_select_fusion.info, f32[64,2048]{1,0:T(8,128)S(1)} %get-tuple-element.101.refs_0_, bf16[64,2048]{1,0:T(8,128)(2,1)S(1)} %collective-permute-done.25.refs_1_, f32[64,2048]{1,0:T(8,128)S(1)} %get-tuple-element.102.refs_2_, bf16[64,2048]{1,0:T(8,128)(2,1)S(1)} %collective-permute-done.26.refs_3_), custom_call_target="tpu_custom_call" | custom-call | flops 1 | bytes 1 | tf_op jit(solution)/shard_map/final/pallas_call | solution.py:394
  (71 shorter events, 20.8 us)
Async XLA Ops:
  2.0 8.2 %collective-permute-start.1 = (s32[128]{0:T(128)S(1)}, s32[128]{0:T(128)S(1)}, u32[]{:S(2)}, u32[]{:S(2)}) collective-permute-start(s32[128]{0:T(128)S(1)} %select_reduce_fusion), channel_id=1, source_target_pairs={{0,16},{16,0},{1,17},{17,1},{2,18},{18,2},{3,19},{19,3},{4,20},{20... | collective-permute-start | bytes 1544 | tf_op jit(solution)/shard_map/ppermute | solution.py:31
  5.0 5.7 %collective-permute-start = (bf16[4,16,512]{2,1,0:T(8,128)(2,1)}, bf16[4,16,512]{2,1,0:T(8,128)(2,1)S(1)}, u32[]{:S(2)}, u32[]{:S(2)}) collective-permute-start(bf16[4,16,512]{2,1,0:T(8,128)(2,1)} %param.11), channel_id=1, source_target_pairs={{0,8},{2,10},{4,12},{6,14},{8,0},{10,2},{12,4},{14,6},{1,9},{3,11}... | collective-permute-start | bytes 196616 | tf_op jit(solution)/shard_map/ppermute | solution.py:35
  8.6 7.2 %collective-permute-start.3 = (bf16[4,16,1024]{2,1,0:T(8,128)(2,1)S(1)}, bf16[4,16,1024]{2,1,0:T(8,128)(2,1)S(1)}, u32[]{:S(2)}, u32[]{:S(2)}) collective-permute-start(bf16[4,16,1024]{2,1,0:T(8,128)(2,1)S(1)} %get-tuple-element.105), channel_id=1, source_target_pairs={{0,2},{2,0},{4,6},{6,4},{8,10},{10,8},{12,14},{14,12},{1,3},{3,1},... | collective-permute-start | bytes 393224 | tf_op jit(solution)/shard_map/ppermute | solution.py:35
  11.6 19.8 %collective-permute-start.5 = (bf16[144,512]{1,0:T(8,128)(2,1)S(1)}, bf16[144,512]{1,0:T(8,128)(2,1)S(1)}, u32[]{:S(2)}, u32[]{:S(2)}) collective-permute-start(bf16[144,512]{1,0:T(8,128)(2,1)S(1)} %fusion.1.refs_0_), channel_id=1, source_target_pairs={{0,4},{2,6},{4,0},{6,2},{8,12},{10,14},{12,8},{14,10},{1,5},{3,7},... | collective-permute-start | bytes 442376 | tf_op jit(solution)/shard_map/ppermute | solution.py:35
  12.9 18.5 %collective-permute-start.4 = (bf16[144,512]{1,0:T(8,128)(2,1)S(1)}, bf16[144,512]{1,0:T(8,128)(2,1)S(1)}, u32[]{:S(2)}, u32[]{:S(2)}) collective-permute-start(bf16[144,512]{1,0:T(8,128)(2,1)S(1)} %fusion.1.refs_0_), channel_id=1, source_target_pairs={{0,6},{2,4},{4,2},{6,0},{8,14},{10,12},{12,10},{14,8},{1,7},{3,5},... | collective-permute-start | bytes 442376 | tf_op jit(solution)/shard_map/ppermute | solution.py:35
  14.6 16.8 %collective-permute-start.2 = (bf16[144,512]{1,0:T(8,128)(2,1)S(1)}, bf16[144,512]{1,0:T(8,128)(2,1)S(1)}, u32[]{:S(2)}, u32[]{:S(2)}) collective-permute-start(bf16[144,512]{1,0:T(8,128)(2,1)S(1)} %fusion.1.refs_0_), channel_id=1, source_target_pairs={{0,2},{2,0},{4,6},{6,4},{8,10},{10,8},{12,14},{14,12},{1,3},{3,1},... | collective-permute-start | bytes 442376 | tf_op jit(solution)/shard_map/ppermute | solution.py:35
  15.8 15.7 %collective-permute-start.7 = (bf16[8,16,1024]{2,1,0:T(8,128)(2,1)S(1)}, bf16[8,16,1024]{2,1,0:T(8,128)(2,1)S(1)}, u32[]{:S(2)}, u32[]{:S(2)}) collective-permute-start(bf16[8,16,1024]{2,1,0:T(8,128)(2,1)S(1)} %pad_maximum_fusion.own_ref), channel_id=1, source_target_pairs={{0,4},{2,6},{4,0},{6,2},{8,12},{10,14},{12,8},{14,10},{1,5},{3,7},... | collective-permute-start | bytes 786440 | tf_op jit(solution)/shard_map/ppermute | solution.py:35
  17.2 14.4 %collective-permute-start.6 = (bf16[8,16,1024]{2,1,0:T(8,128)(2,1)S(1)}, bf16[8,16,1024]{2,1,0:T(8,128)(2,1)S(1)}, u32[]{:S(2)}, u32[]{:S(2)}) collective-permute-start(bf16[8,16,1024]{2,1,0:T(8,128)(2,1)S(1)} %pad_maximum_fusion.own_ref), channel_id=1, source_target_pairs={{0,8},{2,10},{4,12},{6,14},{8,0},{10,2},{12,4},{14,6},{1,9},{3,11}... | collective-permute-start | bytes 786440 | tf_op jit(solution)/shard_map/ppermute | solution.py:35
  26.8 4.8 %copy-start.3 = (bf16[896,512]{1,0:T(8,128)(2,1)S(1)}, bf16[896,512]{1,0:T(8,128)(2,1)}, u32[]{:S(2)}) copy-start(bf16[896,512]{1,0:T(8,128)(2,1)} %g_ref.3) | copy-start | bytes 2752516
  26.8 9.1 %copy-start.2 = (bf16[896,4096]{1,0:T(8,128)(2,1)S(1)}, bf16[896,4096]{1,0:T(8,128)(2,1)}, u32[]{:S(2)}) copy-start(bf16[896,4096]{1,0:T(8,128)(2,1)} %x_ref.9) | copy-start | bytes 22020100
  31.3 3.5 %collective-permute-start.9 = (bf16[896,512]{1,0:T(8,128)(2,1)S(1)}, bf16[896,512]{1,0:T(8,128)(2,1)S(1)}, u32[]{:S(2)}, u32[]{:S(2)}) collective-permute-start(bf16[896,512]{1,0:T(8,128)(2,1)S(1)} %base_other.1), channel_id=1, source_target_pairs={{0,1},{1,0},{2,3},{3,2},{4,5},{5,4},{6,7},{7,6},{8,9},{9,8},{10,11... | collective-permute-start | bytes 2752520 | tf_op jit(solution)/shard_map/ppermute | solution.py:31
  32.5 14.9 %slice-start = ((s8[8388608]{0:T(1024)(128)(4,1)}), s8[4194304]{0:T(1024)(128)(4,1)S(1)}, s32[]{:S(2)}) async-start(s8[8388608]{0:T(1024)(128)(4,1)} %bitcast.28), calls=%async_computation | async-start | bytes 8388608
  32.5 2.7 %collective-permute-start.8 = (bf16[896,512]{1,0:T(8,128)(2,1)S(1)}, bf16[896,512]{1,0:T(8,128)(2,1)S(1)}, u32[]{:S(2)}, u32[]{:S(2)}) collective-permute-start(bf16[896,512]{1,0:T(8,128)(2,1)S(1)} %copy-done.3), channel_id=1, source_target_pairs={{0,1},{1,0},{2,3},{3,2},{4,5},{5,4},{6,7},{7,6},{8,9},{9,8},{10,11... | collective-permute-start | bytes 2752520 | tf_op jit(solution)/shard_map/ppermute | solution.py:31
  33.0 8.7 %collective-permute-start.11 = (bf16[8,16,1024]{2,1,0:T(8,128)(2,1)S(1)}, bf16[8,16,1024]{2,1,0:T(8,128)(2,1)S(1)}, u32[]{:S(2)}, u32[]{:S(2)}) collective-permute-start(bf16[8,16,1024]{2,1,0:T(8,128)(2,1)S(1)} %collective-permute-done.6.far_ref), channel_id=1, source_target_pairs={{0,4},{2,6},{4,0},{6,2},{8,12},{10,14},{12,8},{14,10},{1,5},{3,7},... | collective-permute-start | bytes 786440 | tf_op jit(solution)/shard_map/ppermute | solution.py:35
  34.6 1.2 %collective-permute-start.10 = (f32[16,896]{1,0:T(8,128)S(1)}, f32[16,896]{1,0:T(8,128)S(1)}, u32[]{:S(2)}, u32[]{:S(2)}) collective-permute-start(f32[16,896]{1,0:T(8,128)S(1)} %get-tuple-element.61.mine_ref), channel_id=1, source_target_pairs={{0,1},{1,0},{2,3},{3,2},{4,5},{5,4},{6,7},{7,6},{8,9},{9,8},{10,11... | collective-permute-start | bytes 172040 | tf_op jit(solution)/shard_map/ppermute | solution.py:31
  37.8 14.9 %collective-permute-start.12 = (bf16[64,2048]{1,0:T(8,128)(2,1)S(1)}, bf16[64,2048]{1,0:T(8,128)(2,1)S(1)}, u32[]{:S(2)}, u32[]{:S(2)}) collective-permute-start(bf16[64,2048]{1,0:T(8,128)(2,1)S(1)} %get-tuple-element.73), channel_id=1, source_target_pairs={{0,2},{2,0},{4,6},{6,4},{8,10},{10,8},{12,14},{14,12},{1,3},{3,1},... | collective-permute-start | bytes 786440 | tf_op jit(solution)/shard_map/ppermute | solution.py:35
  38.7 15.5 %collective-permute-start.13 = (bf16[64,2048]{1,0:T(8,128)(2,1)S(1)}, bf16[64,2048]{1,0:T(8,128)(2,1)S(1)}, u32[]{:S(2)}, u32[]{:S(2)}) collective-permute-start(bf16[64,2048]{1,0:T(8,128)(2,1)S(1)} %get-tuple-element.74), channel_id=1, source_target_pairs={{0,4},{2,6},{4,0},{6,2},{8,12},{10,14},{12,8},{14,10},{1,5},{3,7},... | collective-permute-start | bytes 786440 | tf_op jit(solution)/shard_map/ppermute | solution.py:35
  39.9 17.9 %collective-permute-start.14 = (bf16[64,2048]{1,0:T(8,128)(2,1)S(1)}, bf16[64,2048]{1,0:T(8,128)(2,1)S(1)}, u32[]{:S(2)}, u32[]{:S(2)}) collective-permute-start(bf16[64,2048]{1,0:T(8,128)(2,1)S(1)} %get-tuple-element.75), channel_id=1, source_target_pairs={{0,6},{2,4},{4,2},{6,0},{8,14},{10,12},{12,10},{14,8},{1,7},{3,5},... | collective-permute-start | bytes 786440 | tf_op jit(solution)/shard_map/ppermute | solution.py:35
  41.3 6.1 %slice-start.1 = ((s8[8388608]{0:T(1024)(128)(4,1)}), s8[4194304]{0:T(1024)(128)(4,1)S(1)}, s32[]{:S(2)}) async-start(s8[8388608]{0:T(1024)(128)(4,1)} %bitcast.28), calls=%async_computation.1 | async-start | bytes 8388608
  42.5 9.7 %collective-permute-start.16 = (bf16[112,1024]{1,0:T(8,128)(2,1)S(1)}, bf16[112,1024]{1,0:T(8,128)(2,1)S(1)}, u32[]{:S(2)}, u32[]{:S(2)}) collective-permute-start(bf16[112,1024]{1,0:T(8,128)(2,1)S(1)} %get-tuple-element.80), channel_id=1, source_target_pairs={{0,16},{16,0},{1,17},{17,1},{2,18},{18,2},{3,19},{19,3},{4,20},{20... | collective-permute-start | bytes 688136 | tf_op jit(solution)/shard_map/ppermute | solution.py:31
  43.1 18.0 %collective-permute-start.17 = (bf16[112,1024]{1,0:T(8,128)(2,1)S(1)}, bf16[112,1024]{1,0:T(8,128)(2,1)S(1)}, u32[]{:S(2)}, u32[]{:S(2)}) collective-permute-start(bf16[112,1024]{1,0:T(8,128)(2,1)S(1)} %get-tuple-element.81), channel_id=1, source_target_pairs={{0,18},{2,16},{4,22},{6,20},{8,26},{10,24},{12,30},{14,28},{16,2},... | collective-permute-start | bytes 688136 | tf_op jit(solution)/shard_map/ppermute | solution.py:411
  52.1 16.4 %collective-permute-start.15 = (bf16[112,1024]{1,0:T(8,128)(2,1)S(1)}, bf16[112,1024]{1,0:T(8,128)(2,1)S(1)}, u32[]{:S(2)}, u32[]{:S(2)}) collective-permute-start(bf16[112,1024]{1,0:T(8,128)(2,1)S(1)} %get-tuple-element.79), channel_id=1, source_target_pairs={{0,2},{2,0},{4,6},{6,4},{8,10},{10,8},{12,14},{14,12},{1,3},{3,1},... | collective-permute-start | bytes 688136 | tf_op jit(solution)/shard_map/ppermute | solution.py:35
  52.7 26.1 %collective-permute-start.19 = (bf16[64,2048]{1,0:T(8,128)(2,1)S(1)}, bf16[64,2048]{1,0:T(8,128)(2,1)S(1)}, u32[]{:S(2)}, u32[]{:S(2)}) collective-permute-start(bf16[64,2048]{1,0:T(8,128)(2,1)S(1)} %get-tuple-element.88), channel_id=1, source_target_pairs={{0,2},{2,0},{4,6},{6,4},{8,10},{10,8},{12,14},{14,12},{1,3},{3,1},... | collective-permute-start | bytes 786440 | tf_op jit(solution)/shard_map/ppermute | solution.py:35
  54.2 24.6 %collective-permute-start.20 = (bf16[64,2048]{1,0:T(8,128)(2,1)S(1)}, bf16[64,2048]{1,0:T(8,128)(2,1)S(1)}, u32[]{:S(2)}, u32[]{:S(2)}) collective-permute-start(bf16[64,2048]{1,0:T(8,128)(2,1)S(1)} %get-tuple-element.89), channel_id=1, source_target_pairs={{0,4},{2,6},{4,0},{6,2},{8,12},{10,14},{12,8},{14,10},{1,5},{3,7},... | collective-permute-start | bytes 786440 | tf_op jit(solution)/shard_map/ppermute | solution.py:35
  57.8 21.1 %collective-permute-start.21 = (bf16[64,2048]{1,0:T(8,128)(2,1)S(1)}, bf16[64,2048]{1,0:T(8,128)(2,1)S(1)}, u32[]{:S(2)}, u32[]{:S(2)}) collective-permute-start(bf16[64,2048]{1,0:T(8,128)(2,1)S(1)} %get-tuple-element.90), channel_id=1, source_target_pairs={{0,6},{2,4},{4,2},{6,0},{8,14},{10,12},{12,10},{14,8},{1,7},{3,5},... | collective-permute-start | bytes 786440 | tf_op jit(solution)/shard_map/ppermute | solution.py:35
  71.3 6.5 %collective-permute-start.18 = (f32[16,896]{1,0:T(8,128)S(1)}, f32[16,896]{1,0:T(8,128)S(1)}, u32[]{:S(2)}, u32[]{:S(2)}) collective-permute-start(f32[16,896]{1,0:T(8,128)S(1)} %get-tuple-element.83.mine_ref), channel_id=1, source_target_pairs={{0,1},{1,0},{2,3},{3,2},{4,5},{5,4},{6,7},{7,6},{8,9},{9,8},{10,11... | collective-permute-start | bytes 172040 | tf_op jit(solution)/shard_map/ppermute | solution.py:31
  71.4 35.7 %collective-permute-start.25 = (bf16[64,2048]{1,0:T(8,128)(2,1)S(1)}, bf16[64,2048]{1,0:T(8,128)(2,1)S(1)}, u32[]{:S(2)}, u32[]{:S(2)}) collective-permute-start(bf16[64,2048]{1,0:T(8,128)(2,1)S(1)} %get-tuple-element.76), channel_id=1, source_target_pairs={{0,8},{2,10},{4,12},{6,14},{8,0},{10,2},{12,4},{14,6},{1,9},{3,11}... | collective-permute-start | bytes 786440 | tf_op jit(solution)/shard_map/ppermute | solution.py:35
  80.2 26.9 %collective-permute-start.26 = (bf16[64,2048]{1,0:T(8,128)(2,1)S(1)}, bf16[64,2048]{1,0:T(8,128)(2,1)S(1)}, u32[]{:S(2)}, u32[]{:S(2)}) collective-permute-start(bf16[64,2048]{1,0:T(8,128)(2,1)S(1)} %get-tuple-element.91), channel_id=1, source_target_pairs={{0,8},{2,10},{4,12},{6,14},{8,0},{10,2},{12,4},{14,6},{1,9},{3,11}... | collective-permute-start | bytes 786440 | tf_op jit(solution)/shard_map/ppermute | solution.py:35
  81.4 7.8 %collective-permute-start.22 = (bf16[64,512]{1,0:T(8,128)(2,1)S(1)}, bf16[64,512]{1,0:T(8,128)(2,1)S(1)}, u32[]{:S(2)}, u32[]{:S(2)}) collective-permute-start(bf16[64,512]{1,0:T(8,128)(2,1)S(1)} %get-tuple-element.94), channel_id=1, source_target_pairs={{0,2},{2,0},{4,6},{6,4},{8,10},{10,8},{12,14},{14,12},{1,3},{3,1},... | collective-permute-start | bytes 196616 | tf_op jit(solution)/shard_map/ppermute | solution.py:35
  82.6 6.9 %collective-permute-start.23 = (bf16[64,512]{1,0:T(8,128)(2,1)S(1)}, bf16[64,512]{1,0:T(8,128)(2,1)S(1)}, u32[]{:S(2)}, u32[]{:S(2)}) collective-permute-start(bf16[64,512]{1,0:T(8,128)(2,1)S(1)} %get-tuple-element.95), channel_id=1, source_target_pairs={{0,4},{2,6},{4,0},{6,2},{8,12},{10,14},{12,8},{14,10},{1,5},{3,7},... | collective-permute-start | bytes 196616 | tf_op jit(solution)/shard_map/ppermute | solution.py:35
  84.4 5.8 %collective-permute-start.24 = (bf16[64,512]{1,0:T(8,128)(2,1)S(1)}, bf16[64,512]{1,0:T(8,128)(2,1)S(1)}, u32[]{:S(2)}, u32[]{:S(2)}) collective-permute-start(bf16[64,512]{1,0:T(8,128)(2,1)S(1)} %get-tuple-element.96), channel_id=1, source_target_pairs={{0,6},{2,4},{4,2},{6,0},{8,14},{10,12},{12,10},{14,8},{1,7},{3,5},... | collective-permute-start | bytes 196616 | tf_op jit(solution)/shard_map/ppermute | solution.py:35
  91.1 14.7 %collective-permute-start.27 = (bf16[64,512]{1,0:T(8,128)(2,1)S(1)}, bf16[64,512]{1,0:T(8,128)(2,1)S(1)}, u32[]{:S(2)}, u32[]{:S(2)}) collective-permute-start(bf16[64,512]{1,0:T(8,128)(2,1)S(1)} %get-tuple-element.97), channel_id=1, source_target_pairs={{0,8},{2,10},{4,12},{6,14},{8,0},{10,2},{12,4},{14,6},{1,9},{3,11}... | collective-permute-start | bytes 196616 | tf_op jit(solution)/shard_map/ppermute | solution.py:35
  (2 other events, 6.5 us)

commit v5 on v4

--- a/solution.py
+++ b/solution.py
@@ -11,6 +11,7 @@
 CAP = 2
 NEAR = 4
 VMEM_LIMIT = 16 * 1024 * 1024
+BIG_VMEM = 52 * 1024 * 1024
 LANES = 128
 
 adapter_scale = 2.0
@@ -54,7 +55,9 @@
     return jax.ShapeDtypeStruct(shape, dtype)
 
 
-def _call(body, name, grid, in_specs, out_specs, out_shape, scratch, aliases=None):
+def _call(
+    body, name, grid, in_specs, out_specs, out_shape, scratch, aliases=None, vmem=VMEM_LIMIT
+):
     return pl.pallas_call(
         body,
         name=name,
@@ -67,7 +70,7 @@
         ),
         out_shape=out_shape,
         input_output_aliases=aliases or {},
-        compiler_params=pltpu.CompilerParams(vmem_limit_bytes=VMEM_LIMIT),
+        compiler_params=pltpu.CompilerParams(vmem_limit_bytes=vmem),
         cost_estimate=pl.CostEstimate(flops=1, bytes_accessed=1, transcendentals=0),
     )
 
@@ -121,9 +124,24 @@
     return jnp.where(row < valid, x, jnp.zeros((), x.dtype))
 
 
-def other_kernel(z, place, x_ref, w_ref, out_ref):
+def other_kernel(z, place, x_hbm, w_hbm, out_ref, x_buf, w_buf, x_sem, w_sem):
     far = pl.ds(pl.multiple_of((1 - place[z.core[1]]) * z.cols, z.cols), z.cols)
-    out_ref[...] = _dot(x_ref[...], w_ref[:, far], NN).astype(bf16)
+    unit = z.width // 8
+    copies = []
+    for i, (first, last) in enumerate(((0, 1), (1, 2), (2, 4), (4, 6), (6, 8))):
+        cut = pl.ds(first * unit, (last - first) * unit)
+        x = pltpu.make_async_copy(x_hbm.at[:, cut], x_buf.at[:, cut], x_sem.at[i])
+        w = pltpu.make_async_copy(w_hbm.at[cut, far], w_buf.at[cut], w_sem.at[i])
+        x.start()
+        w.start()
+        copies.append((x, w, cut))
+    total = None
+    for x, w, cut in copies:
+        x.wait()
+        w.wait()
+        term = _dot(x_buf[:, cut], w_buf[cut, :], NN)
+        total = term if total is None else total + term
+    out_ref[...] = total.astype(bf16)
 
 
 def own_kernel(z, info, x_ref, w_ref, far_ref, g_ref, h_ref, out_ref, full_ref):
@@ -337,7 +355,13 @@
 
     base_other = _call(
         functools.partial(other_kernel, z), "base_other", (1,),
-        [VMEM, VMEM], _whole((rows, cols)), _shape((rows, cols), bf16), [],
+        [pl.BlockSpec(memory_space=pl.ANY)] * 2,
+        _whole((rows, cols)), _shape((rows, cols), bf16),
+        [
+            pltpu.VMEM((rows, width), bf16), pltpu.VMEM((width, cols), bf16),
+            pltpu.SemaphoreType.DMA((5,)), pltpu.SemaphoreType.DMA((5,)),
+        ],
+        vmem=BIG_VMEM,
     )(_tie(place, shard if shared else packet), tokens, base_weight)
     base_arrived = _swap(base_other, "tensor")
     packets = [_tie(p, base_other) for p in packets]
@@ -399,14 +423,20 @@
 
     half = width // 2
     sends_a = pack(_tie(info, cotangent_other, base_arrived), 0, half)
-    got_a = to_near(sends_a)
+
+    base_own, g_full = _call(
+        functools.partial(own_kernel, z), "base_own", (1,),
+        [VMEM] * 5, [VMEM, VMEM],
+        [_shape((rows, cols), f32), _shape((rows, 2 * cols), bf16)], [],
+    )(_tie(info, sends_a[0]), tokens, base_weight, base_arrived, out_cotangent, cotangent_other)
 
     if shared:
         block = (nb * rank, quarter)
         chosen = _call(
             functools.partial(choose_kernel, z), "choose", (1,),
             [VMEM] * 4, [_whole(block)] * 4, [_shape(block, bf16)] * 4, [],
-        )(_tie(info, sends_a[0]), shard, shard_near, shard_far, farther)
+        )(_tie(info, base_own), shard, shard_near, shard_far, farther)
+        got_y = _xor(chosen[1], n_dp, 1)
         got_x = _swap(chosen[2], "groups")
         got_d = lax.ppermute(
             chosen[3],
@@ -417,32 +447,27 @@
     else:
         every = lax.all_gather(down_t, "dp", axis=0, tiled=True)
         got_down = [jnp.take(every, slots[:nb], axis=0).reshape(nb * rank, width)]
-        after_choose = sends_a[0]
+        after_choose = base_own
 
     sends_b = pack(_tie(info, after_choose), half, half)
+
+    gate = [sends_b[0]] + ([got_x] if shared else [])
+    got_a = to_near([sends_a[0], _tie(sends_a[1], *gate), *sends_a[2:]])
     got_b = to_near(sends_b)
-
-    base_own, g_full = _call(
-        functools.partial(own_kernel, z), "base_own", (1,),
-        [VMEM] * 5, [VMEM, VMEM],
-        [_shape((rows, cols), f32), _shape((rows, 2 * cols), bf16)], [],
-    )(_tie(info, sends_b[0]), tokens, base_weight, base_arrived, out_cotangent, cotangent_other)
-
     if shared:
-        got_y = _xor(_tie(chosen[1], base_own), n_dp, 1)
         got_down = [chosen[0], got_y, got_x, got_d]
-    dense_a = dense(_tie(info, base_own), got_a)
-    far_a = to_far(dense_a)
-
     block_down, shrink_part = _call(
         functools.partial(shrink_kernel, z, n_parts), "shrink", (1,),
         [VMEM] * (1 + n_parts), [VMEM, _whole(part)],
         [_shape((nb * rank, width), bf16), _shape(part, f32)], [],
-    )(_tie(info, dense_a[1]), tokens, *got_down)
+    )(_tie(info, sends_b[0]), tokens, *got_down)
     shrink_other = _swap(shrink_part, "tensor")
 
-    step = min(512, width // 8)
-    n_calls = 4
+    dense_a = dense(_tie(info, shrink_part), got_a)
+    far_a = to_far(dense_a)
+
+    step = min(1024, width // 4)
+    n_calls = 2
     per_call = width // step // n_calls
 
     def token_grads(info, call, so_far):
@@ -458,7 +483,7 @@
             *([] if so_far is None else [so_far]),
         )
 
-    grad_tokens = token_grads(_tie(info, shrink_part), 0, None)
+    grad_tokens = token_grads(_tie(info, dense_a[1]), 0, None)
 
     up_sends = _call(
         functools.partial(pack_up_kernel, z, NEAR), "pack_up", (1,),
@@ -474,17 +499,15 @@
     grad_tokens = token_grads(_tie(info, dense_b[1]), 1, grad_tokens)
     dense_u = dense(_tie(info, grad_tokens), got_u)
     far_u = to_far(dense_u)
-    grad_tokens = token_grads(_tie(info, dense_u[1]), 2, grad_tokens)
-    grad_tokens = token_grads(info, 3, grad_tokens)
 
     projected = _call(
         functools.partial(projected_kernel, z), "projected", (1,),
         [VMEM] * 4, _whole((rows, cols)), _shape((rows, cols), bf16),
         [pltpu.VMEM((nb * rank, rows), bf16)],
-    )(_tie(info, grad_tokens), base_own, shrink_part, shrink_other, block_up)
-
+    )(_tie(info, dense_u[1]), base_own, shrink_part, shrink_other, block_up)
+
+    grad_down = jnp.swapaxes(final([far_a, far_b]), 1, 2)
     grad_up = final([far_u])
-    grad_down = jnp.swapaxes(final([far_a, far_b]), 1, 2)
     return projected, grad_tokens, grad_down, grad_up
 
 

time: 109 us -> 111 us (1.018)
  waiting for transfers between devices: 12.5 us -> 22.5 us
  starting transfers between devices: 40.2 us -> 36.4 us
  local copies, waits for them, and re-layouts: 8.78 us -> 5.71 us
  Pallas kernels: 44.5 us -> 43.2 us
    ppermute x21, waiting for transfers between devices: 11.4 us -> 19.3 us  [_xor(): return lax.ppermute(x, 'dp', [(i, i ^ k) for i in range(n)])]
    pallas_call x4 -> x2, Pallas kernels: 17.5 us -> 14.2 us  [token_grads(): _call(functools.partial(tokens_kernel, z, first), 'token_grads', (per_cal...]
    ppermute x21, starting transfers between devices: 33.4 us -> 30.3 us  [_xor(): return lax.ppermute(x, 'dp', [(i, i ^ k) for i in range(n)])]
    unnamed x12, local copies, waits for them, and re-layouts: 6.48 us -> 3.41 us
    ppermute x6, waiting for transfers between devices: 1.06 us -> 3.16 us  [_swap(): return lax.ppermute(x, axis, [(0, 1), (1, 0)])]
    pallas_call x1, Pallas kernels: 4.5 us -> 6.48 us  [on_device(): _call(functools.partial(other_kernel, z), 'base_other', (1,), [pl.BlockSp...]
  transfers between devices with their start and end apart: 28 -> 28, of which waited for: 8 -> 8; matrix products, arithmetic and copies ran while one was open for 3% -> 2% of each run, Pallas kernels for 39% -> 38%
where the time goes in v5:
time: 111 us; the launch traced here: 110 us
  Pallas kernels  43.2 us (39%)
  starting transfers between devices  36.4 us (33%)
  waiting for transfers between devices  22.5 us (20%)
  local copies, waits for them, and re-layouts  5.71 us (5%)
  other arithmetic  1.82 us (2%)
    ppermute x21, starting transfers between devices, _xor(): return lax.ppermute(x, 'dp', [(i, i ^ k) for i in range(n)])  30.3 us
    ppermute x21, waiting for transfers between devices, _xor(): return lax.ppermute(x, 'dp', [(i, i ^ k) for i in range(n)])  19.3 us
    pallas_call x2, Pallas kernels, token_grads(): _call(functools.partial(tokens_kernel, z, first), 'token_grads', (per_cal...  14.2 us
    pallas_call x1, Pallas kernels, on_device(): _call(functools.partial(other_kernel, z), 'base_other', (1,), [pl.BlockSp...  6.48 us
    pallas_call x1, Pallas kernels, on_device(): _call(functools.partial(own_kernel, z), 'base_own', (1,), [VMEM] * 5, [VM...  4.72 us
    ppermute x6, starting transfers between devices, _swap(): return lax.ppermute(x, axis, [(0, 1), (1, 0)])  3.93 us
    pallas_call x2, Pallas kernels, pack(): _call(functools.partial(pack_kernel, z, NEAR, start), 'pack_down', (1,),...  3.77 us
    pallas_call x3, Pallas kernels, dense(): _call(functools.partial(dense_kernel, z), 'dense', (1,), [VMEM] * NEAR, [...  3.64 us
  transfers between devices with their start and end apart: 28, of which 8 were waited for; matrix products, arithmetic and copies ran while one was open for 2% of the time, Pallas kernels for 38%

profile of v5, /device:TPU:0, one launch (start us, length us, event | category | flops | bytes accessed | tf_op | source)
XLA Modules:
  0.0 110.5 jit_solution(15568597542874829725)
XLA Ops:
  2.0 3.0 %collective-permute-start.1 = (s32[128]{0:T(128)S(1)}, s32[128]{0:T(128)S(1)}, u32[]{:S(2)}, u32[]{:S(2)}) collective-permute-start(s32[128]{0:T(128)S(1)} %select_reduce_fusion), channel_id=1, source_target_pairs={{0,16},{16,0},{1,17},{17,1},{2,18},{18,2},{3,19},{19,3},{4,20},{20... | collective-permute-start | bytes 1544 | tf_op jit(solution)/shard_map/ppermute | solution.py:32
  5.0 2.6 %collective-permute-start = (bf16[4,16,512]{2,1,0:T(8,128)(2,1)}, bf16[4,16,512]{2,1,0:T(8,128)(2,1)S(1)}, u32[]{:S(2)}, u32[]{:S(2)}) collective-permute-start(bf16[4,16,512]{2,1,0:T(8,128)(2,1)} %param.11), channel_id=1, source_target_pairs={{0,8},{2,10},{4,12},{6,14},{8,0},{10,2},{12,4},{14,6},{1,9},{3,11}... | collective-permute-start | bytes 196616 | tf_op jit(solution)/shard_map/ppermute | solution.py:36
  8.6 1.6 %collective-permute-start.3 = (bf16[4,16,1024]{2,1,0:T(8,128)(2,1)S(1)}, bf16[4,16,1024]{2,1,0:T(8,128)(2,1)S(1)}, u32[]{:S(2)}, u32[]{:S(2)}) collective-permute-start(bf16[4,16,1024]{2,1,0:T(8,128)(2,1)S(1)} %get-tuple-element.103), channel_id=1, source_target_pairs={{0,2},{2,0},{4,6},{6,4},{8,10},{10,8},{12,14},{14,12},{1,3},{3,1},... | collective-permute-start | bytes 393224 | tf_op jit(solution)/shard_map/ppermute | solution.py:36
  11.6 1.3 %collective-permute-start.5 = (bf16[144,512]{1,0:T(8,128)(2,1)S(1)}, bf16[144,512]{1,0:T(8,128)(2,1)S(1)}, u32[]{:S(2)}, u32[]{:S(2)}) collective-permute-start(bf16[144,512]{1,0:T(8,128)(2,1)S(1)} %fusion.1.refs_0_), channel_id=1, source_target_pairs={{0,4},{2,6},{4,0},{6,2},{8,12},{10,14},{12,8},{14,10},{1,5},{3,7},... | collective-permute-start | bytes 442376 | tf_op jit(solution)/shard_map/ppermute | solution.py:36
  12.9 1.7 %collective-permute-start.4 = (bf16[144,512]{1,0:T(8,128)(2,1)S(1)}, bf16[144,512]{1,0:T(8,128)(2,1)S(1)}, u32[]{:S(2)}, u32[]{:S(2)}) collective-permute-start(bf16[144,512]{1,0:T(8,128)(2,1)S(1)} %fusion.1.refs_0_), channel_id=1, source_target_pairs={{0,6},{2,4},{4,2},{6,0},{8,14},{10,12},{12,10},{14,8},{1,7},{3,5},... | collective-permute-start | bytes 442376 | tf_op jit(solution)/shard_map/ppermute | solution.py:36
  15.8 1.3 %collective-permute-start.7 = (bf16[8,16,1024]{2,1,0:T(8,128)(2,1)S(1)}, bf16[8,16,1024]{2,1,0:T(8,128)(2,1)S(1)}, u32[]{:S(2)}, u32[]{:S(2)}) collective-permute-start(bf16[8,16,1024]{2,1,0:T(8,128)(2,1)S(1)} %pad_maximum_fusion.own_ref), channel_id=1, source_target_pairs={{0,4},{2,6},{4,0},{6,2},{8,12},{10,14},{12,8},{14,10},{1,5},{3,7},... | collective-permute-start | bytes 786440 | tf_op jit(solution)/shard_map/ppermute | solution.py:36
  17.2 3.2 %collective-permute-start.6 = (bf16[8,16,1024]{2,1,0:T(8,128)(2,1)S(1)}, bf16[8,16,1024]{2,1,0:T(8,128)(2,1)S(1)}, u32[]{:S(2)}, u32[]{:S(2)}) collective-permute-start(bf16[8,16,1024]{2,1,0:T(8,128)(2,1)S(1)} %pad_maximum_fusion.own_ref), channel_id=1, source_target_pairs={{0,8},{2,10},{4,12},{6,14},{8,0},{10,2},{12,4},{14,6},{1,9},{3,11}... | collective-permute-start | bytes 786440 | tf_op jit(solution)/shard_map/ppermute | solution.py:36
  20.4 6.5 %base_other.1 = bf16[896,512]{1,0:T(8,128)(2,1)S(1)} custom-call(s32[128]{0:T(128)S(1)} %compare_select_fusion.1.place, bf16[896,4096]{1,0:T(8,128)(2,1)} %x_ref.7, bf16[4096,1024]{1,0:T(8,128)(2,1)} %w_ref.5), custom_call_target="tpu_custom_call" | custom-call | flops 1 | bytes 1 | tf_op jit(solution)/shard_map/base_other/pallas_call | solution.py:356
  26.9 1.2 %collective-permute-done.4.refs_3_ = bf16[144,512]{1,0:T(8,128)(2,1)S(1)} collective-permute-done((bf16[144,512]{1,0:T(8,128)(2,1)S(1)}, bf16[144,512]{1,0:T(8,128)(2,1)S(1)}, u32[]{:S(2)}, u32[]{:S(2)}) %collective-permute-start.4) | collective-permute-done | bytes 147488 | tf_op jit(solution)/shard_map/ppermute | solution.py:36
  28.2 2.5 %collective-permute-done.7.near_ref = bf16[8,16,1024]{2,1,0:T(8,128)(2,1)S(1)} collective-permute-done((bf16[8,16,1024]{2,1,0:T(8,128)(2,1)S(1)}, bf16[8,16,1024]{2,1,0:T(8,128)(2,1)S(1)}, u32[]{:S(2)}, u32[]{:S(2)}) %collective-permute-start.7) | collective-permute-done | bytes 262176 | tf_op jit(solution)/shard_map/ppermute | solution.py:36
  31.7 2.9 %collective-permute-start.11 = (bf16[8,16,1024]{2,1,0:T(8,128)(2,1)S(1)}, bf16[8,16,1024]{2,1,0:T(8,128)(2,1)S(1)}, u32[]{:S(2)}, u32[]{:S(2)}) collective-permute-start(bf16[8,16,1024]{2,1,0:T(8,128)(2,1)S(1)} %collective-permute-done.6.far_ref), channel_id=1, source_target_pairs={{0,4},{2,6},{4,0},{6,2},{8,12},{10,14},{12,8},{14,10},{1,5},{3,7},... | collective-permute-start | bytes 786440 | tf_op jit(solution)/shard_map/ppermute | solution.py:36
  35.9 1.9 %pack_down.2 = (bf16[64,2048]{1,0:T(8,128)(2,1)S(1)}, bf16[64,2048]{1,0:T(8,128)(2,1)S(1)}, bf16[64,2048]{1,0:T(8,128)(2,1)S(1)}, bf16[64,2048]{1,0:T(8,128)(2,1)S(1)}) custom-call(s32[8,128]{1,0:T(8,128)S(1)} %select_select_fusion.info, f32[16,896]{1,0:T(8,128)S(1)} %get-tuple-element.60.mine_ref, f32[16,896]{1,0:T(8,128)S(1)} %collective-permute-done.10.other_ref, ...), custom_call_target="tpu_custom_call" | custom-call | flops 1 | bytes 1 | tf_op jit(solution)/shard_map/pack_down/pallas_call | solution.py:393
  37.8 1.3 %collective-permute-start.16 = (bf16[64,2048]{1,0:T(8,128)(2,1)S(1)}, bf16[64,2048]{1,0:T(8,128)(2,1)S(1)}, u32[]{:S(2)}, u32[]{:S(2)}) collective-permute-start(bf16[64,2048]{1,0:T(8,128)(2,1)S(1)} %get-tuple-element.78), channel_id=1, source_target_pairs={{0,4},{2,6},{4,0},{6,2},{8,12},{10,14},{12,8},{14,10},{1,5},{3,7},... | collective-permute-start | bytes 786440 | tf_op jit(solution)/shard_map/ppermute | solution.py:36
  39.1 3.4 %copy-done = bf16[4096,1024]{1,0:T(8,128)(2,1)S(1)} copy-done((bf16[4096,1024]{1,0:T(8,128)(2,1)S(1)}, bf16[4096,1024]{1,0:T(8,128)(2,1)}, u32[]{:S(2)}) %copy-start) | copy-done | bytes 8388632
  42.5 4.7 %base_own.1 = (f32[896,512]{1,0:T(8,128)S(1)}, bf16[896,1024]{1,0:T(8,128)(2,1)S(1)}) custom-call(s32[8,128]{1,0:T(8,128)S(1)} %select_select_fusion.info, bf16[896,4096]{1,0:T(8,128)(2,1)S(1)} %bitcast.29, bf16[4096,1024]{1,0:T(8,128)(2,1)S(1)} %copy-done, bf16[896,512]{1,0:T(8,128)(2,1)S(1)} %collective-permute-done.9.far_ref, ...), custom_call_target="tpu_custom_call" | custom-call | flops 1 | bytes 1 | tf_op jit(solution)/shard_map/base_own/pallas_call | solution.py:427
  49.4 2.1 %collective-permute-start.14 = (bf16[112,1024]{1,0:T(8,128)(2,1)S(1)}, bf16[112,1024]{1,0:T(8,128)(2,1)S(1)}, u32[]{:S(2)}, u32[]{:S(2)}) collective-permute-start(bf16[112,1024]{1,0:T(8,128)(2,1)S(1)} %get-tuple-element.73), channel_id=1, source_target_pairs={{0,18},{2,16},{4,22},{6,20},{8,26},{10,24},{12,30},{14,28},{16,2},... | collective-permute-start | bytes 688136 | tf_op jit(solution)/shard_map/ppermute | solution.py:441
  52.6 1.9 %pack_down.3 = (bf16[64,2048]{1,0:T(8,128)(2,1)S(1)}, bf16[64,2048]{1,0:T(8,128)(2,1)S(1)}, bf16[64,2048]{1,0:T(8,128)(2,1)S(1)}, bf16[64,2048]{1,0:T(8,128)(2,1)S(1)}) custom-call(s32[8,128]{1,0:T(8,128)S(1)} %select_select_fusion.info, f32[16,896]{1,0:T(8,128)S(1)} %get-tuple-element.60.mine_ref, f32[16,896]{1,0:T(8,128)S(1)} %collective-permute-done.10.other_ref, ...), custom_call_target="tpu_custom_call" | custom-call | flops 1 | bytes 1 | tf_op jit(solution)/shard_map/pack_down/pallas_call | solution.py:393
  54.5 2.1 %collective-permute-done.13.refs_2_ = bf16[112,1024]{1,0:T(8,128)(2,1)S(1)} collective-permute-done((bf16[112,1024]{1,0:T(8,128)(2,1)S(1)}, bf16[112,1024]{1,0:T(8,128)(2,1)S(1)}, u32[]{:S(2)}, u32[]{:S(2)}) %collective-permute-start.13) | collective-permute-done | bytes 229408 | tf_op jit(solution)/shard_map/ppermute | solution.py:32
  57.4 10.3 %collective-permute-done.12.refs_1_ = bf16[112,1024]{1,0:T(8,128)(2,1)S(1)} collective-permute-done((bf16[112,1024]{1,0:T(8,128)(2,1)S(1)}, bf16[112,1024]{1,0:T(8,128)(2,1)S(1)}, u32[]{:S(2)}, u32[]{:S(2)}) %collective-permute-start.12) | collective-permute-done | bytes 229408 | tf_op jit(solution)/shard_map/ppermute | solution.py:36
  69.2 1.9 %collective-permute-start.21 = (bf16[64,2048]{1,0:T(8,128)(2,1)S(1)}, bf16[64,2048]{1,0:T(8,128)(2,1)S(1)}, u32[]{:S(2)}, u32[]{:S(2)}) collective-permute-start(bf16[64,2048]{1,0:T(8,128)(2,1)S(1)} %get-tuple-element.89), channel_id=1, source_target_pairs={{0,6},{2,4},{4,2},{6,0},{8,14},{10,12},{12,10},{14,8},{1,7},{3,5},... | collective-permute-start | bytes 786440 | tf_op jit(solution)/shard_map/ppermute | solution.py:36
  71.2 2.7 %shrink.1 = (bf16[112,4096]{1,0:T(8,128)(2,1)S(1)}, f32[16,896]{1,0:T(8,128)S(1)}) custom-call(s32[8,128]{1,0:T(8,128)S(1)} %select_select_fusion.info, bf16[896,4096]{1,0:T(8,128)(2,1)S(1)} %bitcast.29, bf16[112,1024]{1,0:T(8,128)(2,1)S(1)} %get-tuple-element.67.refs_0_, bf16[112,1024]{1,0:T(8,128)(2,1)S(1)} %collective-permute-done.12.refs_1_, ...), custom_call_target="tpu_custom_call" | custom-call | flops 1 | bytes 1 | tf_op jit(solution)/shard_map/shrink/pallas_call | solution.py:459
  74.0 2.1 %collective-permute-done.15.refs_1_ = bf16[64,2048]{1,0:T(8,128)(2,1)S(1)} collective-permute-done((bf16[64,2048]{1,0:T(8,128)(2,1)S(1)}, bf16[64,2048]{1,0:T(8,128)(2,1)S(1)}, u32[]{:S(2)}, u32[]{:S(2)}) %collective-permute-start.15) | collective-permute-done | bytes 262176 | tf_op jit(solution)/shard_map/ppermute | solution.py:36
  76.1 1.3 %dense.3 = (f32[64,2048]{1,0:T(8,128)S(1)}, bf16[64,2048]{1,0:T(8,128)(2,1)S(1)}) custom-call(s32[8,128]{1,0:T(8,128)S(1)} %select_select_fusion.info, bf16[64,2048]{1,0:T(8,128)(2,1)S(1)} %get-tuple-element.63.refs_0_, bf16[64,2048]{1,0:T(8,128)(2,1)S(1)} %collective-permute-done.15.refs_1_, bf16[64,2048]{1,0:T(8,128)(2,1)S(1)} %collective-permute-done.16.refs_2_, ...), custom_call_target="tpu_custom_call" | custom-call | flops 1 | bytes 1 | tf_op jit(solution)/shard_map/dense/pallas_call | solution.py:406
  78.6 7.2 %token_grads.2.refs_0_ = bf16[896,4096]{1,0:T(8,128)(2,1)} custom-call(s32[8,128]{1,0:T(8,128)S(1)} %select_select_fusion.info, bf16[896,1024]{1,0:T(8,128)(2,1)S(1)} %get-tuple-element.82.g_ref, bf16[4096,1024]{1,0:T(8,128)(2,1)S(1)} %bitcast.31, f32[16,896]{1,0:T(8,128)S(1)} %get-tuple-element.60.mine_ref, ...), custom_call_target="tpu_custom_call" | custom-call | flops 1 | bytes 1 | tf_op jit(solution)/shard_map/token_grads/pallas_call | solution.py:475
  86.9 1.3 %dense.4 = (f32[64,2048]{1,0:T(8,128)S(1)}, bf16[64,2048]{1,0:T(8,128)(2,1)S(1)}) custom-call(s32[8,128]{1,0:T(8,128)S(1)} %select_select_fusion.info, bf16[64,2048]{1,0:T(8,128)(2,1)S(1)} %get-tuple-element.69.refs_0_, bf16[64,2048]{1,0:T(8,128)(2,1)S(1)} %collective-permute-done.19.refs_1_, bf16[64,2048]{1,0:T(8,128)(2,1)S(1)} %collective-permute-done.20.refs_2_, ...), custom_call_target="tpu_custom_call" | custom-call | flops 1 | bytes 1 | tf_op jit(solution)/shard_map/dense/pallas_call | solution.py:406
  88.2 1.9 %collective-permute-start.26 = (bf16[64,2048]{1,0:T(8,128)(2,1)S(1)}, bf16[64,2048]{1,0:T(8,128)(2,1)S(1)}, u32[]{:S(2)}, u32[]{:S(2)}) collective-permute-start(bf16[64,2048]{1,0:T(8,128)(2,1)S(1)} %get-tuple-element.90), channel_id=1, source_target_pairs={{0,8},{2,10},{4,12},{6,14},{8,0},{10,2},{12,4},{14,6},{1,9},{3,11}... | collective-permute-start | bytes 786440 | tf_op jit(solution)/shard_map/ppermute | solution.py:36
  91.6 2.0 %collective-permute-start.24 = (bf16[64,512]{1,0:T(8,128)(2,1)S(1)}, bf16[64,512]{1,0:T(8,128)(2,1)S(1)}, u32[]{:S(2)}, u32[]{:S(2)}) collective-permute-start(bf16[64,512]{1,0:T(8,128)(2,1)S(1)} %get-tuple-element.95), channel_id=1, source_target_pairs={{0,6},{2,4},{4,2},{6,0},{8,14},{10,12},{12,10},{14,8},{1,7},{3,5},... | collective-permute-start | bytes 196616 | tf_op jit(solution)/shard_map/ppermute | solution.py:36
  93.6 7.0 %token_grads.3 = bf16[896,4096]{1,0:T(8,128)(2,1)} custom-call(s32[8,128]{1,0:T(8,128)S(1)} %select_select_fusion.info, bf16[896,1024]{1,0:T(8,128)(2,1)S(1)} %get-tuple-element.82.g_ref, bf16[4096,1024]{1,0:T(8,128)(2,1)S(1)} %bitcast.31, f32[16,896]{1,0:T(8,128)S(1)} %get-tuple-element.60.mine_ref, ...), custom_call_target="tpu_custom_call", output_to_operand_aliasing={{}: (6, {})} | custom-call | flops 1 | bytes 1 | tf_op jit(solution)/shard_map/token_grads/pallas_call | solution.py:475
  102.8 2.0 %projected.1 = bf16[896,512]{1,0:T(8,128)(2,1)} custom-call(s32[8,128]{1,0:T(8,128)S(1)} %select_select_fusion.info, f32[896,512]{1,0:T(8,128)S(1)} %get-tuple-element.65.base_ref, f32[16,896]{1,0:T(8,128)S(1)} %get-tuple-element.74.mine_ref, f32[16,896]{1,0:T(8,128)S(1)} %collective-permute-done.18.other_ref, bf16[112,512]{1,0:T(8,128)(2,1)S(1)} %get-tuple-element.98.up_ref), custom_call_target="tpu_custom_call" | custom-call | flops 1 | bytes 1 | tf_op jit(solution)/shard_map/projected/pallas_call | solution.py:503
  104.8 2.8 %collective-permute-done.27.refs_1_ = bf16[64,512]{1,0:T(8,128)(2,1)S(1)} collective-permute-done((bf16[64,512]{1,0:T(8,128)(2,1)S(1)}, bf16[64,512]{1,0:T(8,128)(2,1)S(1)}, u32[]{:S(2)}, u32[]{:S(2)}) %collective-permute-start.27) | collective-permute-done | bytes 65568 | tf_op jit(solution)/shard_map/ppermute | solution.py:36
  107.6 1.3 %final.3 = f32[64,512]{1,0:T(8,128)} custom-call(s32[8,128]{1,0:T(8,128)S(1)} %select_select_fusion.info, f32[64,512]{1,0:T(8,128)S(1)} %get-tuple-element.101.refs_0_, bf16[64,512]{1,0:T(8,128)(2,1)S(1)} %collective-permute-done.27.refs_1_), custom_call_target="tpu_custom_call" | custom-call | flops 1 | bytes 1 | tf_op jit(solution)/shard_map/final/pallas_call | solution.py:418
  108.8 1.7 %final.2 = f32[64,4096]{1,0:T(8,128)} custom-call(s32[8,128]{1,0:T(8,128)S(1)} %select_select_fusion.info, f32[64,2048]{1,0:T(8,128)S(1)} %get-tuple-element.99.refs_0_, bf16[64,2048]{1,0:T(8,128)(2,1)S(1)} %collective-permute-done.25.refs_1_, f32[64,2048]{1,0:T(8,128)S(1)} %get-tuple-element.100.refs_2_, bf16[64,2048]{1,0:T(8,128)(2,1)S(1)} %collective-permute-done.26.refs_3_), custom_call_target="tpu_custom_call" | custom-call | flops 1 | bytes 1 | tf_op jit(solution)/shard_map/final/pallas_call | solution.py:418
  (70 shorter events, 18.8 us)
Async XLA Ops:
  2.0 8.2 %collective-permute-start.1 = (s32[128]{0:T(128)S(1)}, s32[128]{0:T(128)S(1)}, u32[]{:S(2)}, u32[]{:S(2)}) collective-permute-start(s32[128]{0:T(128)S(1)} %select_reduce_fusion), channel_id=1, source_target_pairs={{0,16},{16,0},{1,17},{17,1},{2,18},{18,2},{3,19},{19,3},{4,20},{20... | collective-permute-start | bytes 1544 | tf_op jit(solution)/shard_map/ppermute | solution.py:32
  5.0 5.7 %collective-permute-start = (bf16[4,16,512]{2,1,0:T(8,128)(2,1)}, bf16[4,16,512]{2,1,0:T(8,128)(2,1)S(1)}, u32[]{:S(2)}, u32[]{:S(2)}) collective-permute-start(bf16[4,16,512]{2,1,0:T(8,128)(2,1)} %param.11), channel_id=1, source_target_pairs={{0,8},{2,10},{4,12},{6,14},{8,0},{10,2},{12,4},{14,6},{1,9},{3,11}... | collective-permute-start | bytes 196616 | tf_op jit(solution)/shard_map/ppermute | solution.py:36
  8.6 7.2 %collective-permute-start.3 = (bf16[4,16,1024]{2,1,0:T(8,128)(2,1)S(1)}, bf16[4,16,1024]{2,1,0:T(8,128)(2,1)S(1)}, u32[]{:S(2)}, u32[]{:S(2)}) collective-permute-start(bf16[4,16,1024]{2,1,0:T(8,128)(2,1)S(1)} %get-tuple-element.103), channel_id=1, source_target_pairs={{0,2},{2,0},{4,6},{6,4},{8,10},{10,8},{12,14},{14,12},{1,3},{3,1},... | collective-permute-start | bytes 393224 | tf_op jit(solution)/shard_map/ppermute | solution.py:36
  11.6 15.3 %collective-permute-start.5 = (bf16[144,512]{1,0:T(8,128)(2,1)S(1)}, bf16[144,512]{1,0:T(8,128)(2,1)S(1)}, u32[]{:S(2)}, u32[]{:S(2)}) collective-permute-start(bf16[144,512]{1,0:T(8,128)(2,1)S(1)} %fusion.1.refs_0_), channel_id=1, source_target_pairs={{0,4},{2,6},{4,0},{6,2},{8,12},{10,14},{12,8},{14,10},{1,5},{3,7},... | collective-permute-start | bytes 442376 | tf_op jit(solution)/shard_map/ppermute | solution.py:36
  12.9 15.2 %collective-permute-start.4 = (bf16[144,512]{1,0:T(8,128)(2,1)S(1)}, bf16[144,512]{1,0:T(8,128)(2,1)S(1)}, u32[]{:S(2)}, u32[]{:S(2)}) collective-permute-start(bf16[144,512]{1,0:T(8,128)(2,1)S(1)} %fusion.1.refs_0_), channel_id=1, source_target_pairs={{0,6},{2,4},{4,2},{6,0},{8,14},{10,12},{12,10},{14,8},{1,7},{3,5},... | collective-permute-start | bytes 442376 | tf_op jit(solution)/shard_map/ppermute | solution.py:36
  14.6 13.5 %collective-permute-start.2 = (bf16[144,512]{1,0:T(8,128)(2,1)S(1)}, bf16[144,512]{1,0:T(8,128)(2,1)S(1)}, u32[]{:S(2)}, u32[]{:S(2)}) collective-permute-start(bf16[144,512]{1,0:T(8,128)(2,1)S(1)} %fusion.1.refs_0_), channel_id=1, source_target_pairs={{0,2},{2,0},{4,6},{6,4},{8,10},{10,8},{12,14},{14,12},{1,3},{3,1},... | collective-permute-start | bytes 442376 | tf_op jit(solution)/shard_map/ppermute | solution.py:36
  15.8 20.1 %slice-start = ((s8[7340032]{0:T(1024)(128)(4,1)}), s8[4194304]{0:T(1024)(128)(4,1)S(1)}, s32[]{:S(2)}) async-start(s8[7340032]{0:T(1024)(128)(4,1)} %bitcast.28), calls=%async_computation | async-start | bytes 8388608
  15.8 14.9 %copy-start.1 = (bf16[896,512]{1,0:T(8,128)(2,1)S(1)}, bf16[896,512]{1,0:T(8,128)(2,1)}, u32[]{:S(2)}) copy-start(bf16[896,512]{1,0:T(8,128)(2,1)} %g_ref.3) | copy-start | bytes 2752516
  15.8 20.0 %slice-start.1 = ((s8[7340032]{0:T(1024)(128)(4,1)}), s8[3145728]{0:T(1024)(128)(4,1)S(1)}, s32[]{:S(2)}) async-start(s8[7340032]{0:T(1024)(128)(4,1)} %bitcast.28), calls=%async_computation.1 | async-start | bytes 6291456
  15.8 14.9 %collective-permute-start.7 = (bf16[8,16,1024]{2,1,0:T(8,128)(2,1)S(1)}, bf16[8,16,1024]{2,1,0:T(8,128)(2,1)S(1)}, u32[]{:S(2)}, u32[]{:S(2)}) collective-permute-start(bf16[8,16,1024]{2,1,0:T(8,128)(2,1)S(1)} %pad_maximum_fusion.own_ref), channel_id=1, source_target_pairs={{0,4},{2,6},{4,0},{6,2},{8,12},{10,14},{12,8},{14,10},{1,5},{3,7},... | collective-permute-start | bytes 786440 | tf_op jit(solution)/shard_map/ppermute | solution.py:36
  17.2 13.6 %collective-permute-start.6 = (bf16[8,16,1024]{2,1,0:T(8,128)(2,1)S(1)}, bf16[8,16,1024]{2,1,0:T(8,128)(2,1)S(1)}, u32[]{:S(2)}, u32[]{:S(2)}) collective-permute-start(bf16[8,16,1024]{2,1,0:T(8,128)(2,1)S(1)} %pad_maximum_fusion.own_ref), channel_id=1, source_target_pairs={{0,8},{2,10},{4,12},{6,14},{8,0},{10,2},{12,4},{14,6},{1,9},{3,11}... | collective-permute-start | bytes 786440 | tf_op jit(solution)/shard_map/ppermute | solution.py:36
  26.9 7.9 %collective-permute-start.9 = (bf16[896,512]{1,0:T(8,128)(2,1)S(1)}, bf16[896,512]{1,0:T(8,128)(2,1)S(1)}, u32[]{:S(2)}, u32[]{:S(2)}) collective-permute-start(bf16[896,512]{1,0:T(8,128)(2,1)S(1)} %base_other.1), channel_id=1, source_target_pairs={{0,1},{1,0},{2,3},{3,2},{4,5},{5,4},{6,7},{7,6},{8,9},{9,8},{10,11... | collective-permute-start | bytes 2752520 | tf_op jit(solution)/shard_map/ppermute | solution.py:32
  31.7 3.1 %collective-permute-start.8 = (bf16[896,512]{1,0:T(8,128)(2,1)S(1)}, bf16[896,512]{1,0:T(8,128)(2,1)S(1)}, u32[]{:S(2)}, u32[]{:S(2)}) collective-permute-start(bf16[896,512]{1,0:T(8,128)(2,1)S(1)} %copy-done.1), channel_id=1, source_target_pairs={{0,1},{1,0},{2,3},{3,2},{4,5},{5,4},{6,7},{7,6},{8,9},{9,8},{10,11... | collective-permute-start | bytes 2752520 | tf_op jit(solution)/shard_map/ppermute | solution.py:32
  31.7 15.5 %collective-permute-start.11 = (bf16[8,16,1024]{2,1,0:T(8,128)(2,1)S(1)}, bf16[8,16,1024]{2,1,0:T(8,128)(2,1)S(1)}, u32[]{:S(2)}, u32[]{:S(2)}) collective-permute-start(bf16[8,16,1024]{2,1,0:T(8,128)(2,1)S(1)} %collective-permute-done.6.far_ref), channel_id=1, source_target_pairs={{0,4},{2,6},{4,0},{6,2},{8,12},{10,14},{12,8},{14,10},{1,5},{3,7},... | collective-permute-start | bytes 786440 | tf_op jit(solution)/shard_map/ppermute | solution.py:36
  34.6 1.2 %collective-permute-start.10 = (f32[16,896]{1,0:T(8,128)S(1)}, f32[16,896]{1,0:T(8,128)S(1)}, u32[]{:S(2)}, u32[]{:S(2)}) collective-permute-start(f32[16,896]{1,0:T(8,128)S(1)} %get-tuple-element.60.mine_ref), channel_id=1, source_target_pairs={{0,1},{1,0},{2,3},{3,2},{4,5},{5,4},{6,7},{7,6},{8,9},{9,8},{10,11... | collective-permute-start | bytes 172040 | tf_op jit(solution)/shard_map/ppermute | solution.py:32
  37.8 31.5 %collective-permute-start.16 = (bf16[64,2048]{1,0:T(8,128)(2,1)S(1)}, bf16[64,2048]{1,0:T(8,128)(2,1)S(1)}, u32[]{:S(2)}, u32[]{:S(2)}) collective-permute-start(bf16[64,2048]{1,0:T(8,128)(2,1)S(1)} %get-tuple-element.78), channel_id=1, source_target_pairs={{0,4},{2,6},{4,0},{6,2},{8,12},{10,14},{12,8},{14,10},{1,5},{3,7},... | collective-permute-start | bytes 786440 | tf_op jit(solution)/shard_map/ppermute | solution.py:36
  48.0 8.6 %collective-permute-start.13 = (bf16[112,1024]{1,0:T(8,128)(2,1)S(1)}, bf16[112,1024]{1,0:T(8,128)(2,1)S(1)}, u32[]{:S(2)}, u32[]{:S(2)}) collective-permute-start(bf16[112,1024]{1,0:T(8,128)(2,1)S(1)} %get-tuple-element.72), channel_id=1, source_target_pairs={{0,16},{16,0},{1,17},{17,1},{2,18},{18,2},{3,19},{19,3},{4,20},{20... | collective-permute-start | bytes 688136 | tf_op jit(solution)/shard_map/ppermute | solution.py:32
  48.6 19.1 %collective-permute-start.12 = (bf16[112,1024]{1,0:T(8,128)(2,1)S(1)}, bf16[112,1024]{1,0:T(8,128)(2,1)S(1)}, u32[]{:S(2)}, u32[]{:S(2)}) collective-permute-start(bf16[112,1024]{1,0:T(8,128)(2,1)S(1)} %get-tuple-element.71), channel_id=1, source_target_pairs={{0,2},{2,0},{4,6},{6,4},{8,10},{10,8},{12,14},{14,12},{1,3},{3,1},... | collective-permute-start | bytes 688136 | tf_op jit(solution)/shard_map/ppermute | solution.py:36
  49.4 19.1 %collective-permute-start.14 = (bf16[112,1024]{1,0:T(8,128)(2,1)S(1)}, bf16[112,1024]{1,0:T(8,128)(2,1)S(1)}, u32[]{:S(2)}, u32[]{:S(2)}) collective-permute-start(bf16[112,1024]{1,0:T(8,128)(2,1)S(1)} %get-tuple-element.73), channel_id=1, source_target_pairs={{0,18},{2,16},{4,22},{6,20},{8,26},{10,24},{12,30},{14,28},{16,2},... | collective-permute-start | bytes 688136 | tf_op jit(solution)/shard_map/ppermute | solution.py:441
  51.6 22.4 %collective-permute-start.17 = (bf16[64,2048]{1,0:T(8,128)(2,1)S(1)}, bf16[64,2048]{1,0:T(8,128)(2,1)S(1)}, u32[]{:S(2)}, u32[]{:S(2)}) collective-permute-start(bf16[64,2048]{1,0:T(8,128)(2,1)S(1)} %get-tuple-element.79), channel_id=1, source_target_pairs={{0,6},{2,4},{4,2},{6,0},{8,14},{10,12},{12,10},{14,8},{1,7},{3,5},... | collective-permute-start | bytes 786440 | tf_op jit(solution)/shard_map/ppermute | solution.py:36
  52.6 26.0 %slice-start.2 = ((s8[8388608]{0:T(1024)(128)(4,1)}), s8[4194304]{0:T(1024)(128)(4,1)S(1)}, s32[]{:S(2)}) async-start(s8[8388608]{0:T(1024)(128)(4,1)} %bitcast.30), calls=%async_computation.2 | async-start | bytes 8388608
  56.6 19.5 %collective-permute-start.15 = (bf16[64,2048]{1,0:T(8,128)(2,1)S(1)}, bf16[64,2048]{1,0:T(8,128)(2,1)S(1)}, u32[]{:S(2)}, u32[]{:S(2)}) collective-permute-start(bf16[64,2048]{1,0:T(8,128)(2,1)S(1)} %get-tuple-element.77), channel_id=1, source_target_pairs={{0,2},{2,0},{4,6},{6,4},{8,10},{10,8},{12,14},{14,12},{1,3},{3,1},... | collective-permute-start | bytes 786440 | tf_op jit(solution)/shard_map/ppermute | solution.py:36
  67.7 19.2 %collective-permute-start.19 = (bf16[64,2048]{1,0:T(8,128)(2,1)S(1)}, bf16[64,2048]{1,0:T(8,128)(2,1)S(1)}, u32[]{:S(2)}, u32[]{:S(2)}) collective-permute-start(bf16[64,2048]{1,0:T(8,128)(2,1)S(1)} %get-tuple-element.87), channel_id=1, source_target_pairs={{0,2},{2,0},{4,6},{6,4},{8,10},{10,8},{12,14},{14,12},{1,3},{3,1},... | collective-permute-start | bytes 786440 | tf_op jit(solution)/shard_map/ppermute | solution.py:36
  68.5 18.4 %collective-permute-start.20 = (bf16[64,2048]{1,0:T(8,128)(2,1)S(1)}, bf16[64,2048]{1,0:T(8,128)(2,1)S(1)}, u32[]{:S(2)}, u32[]{:S(2)}) collective-permute-start(bf16[64,2048]{1,0:T(8,128)(2,1)S(1)} %get-tuple-element.88), channel_id=1, source_target_pairs={{0,4},{2,6},{4,0},{6,2},{8,12},{10,14},{12,8},{14,10},{1,5},{3,7},... | collective-permute-start | bytes 786440 | tf_op jit(solution)/shard_map/ppermute | solution.py:36
  69.2 17.6 %collective-permute-start.21 = (bf16[64,2048]{1,0:T(8,128)(2,1)S(1)}, bf16[64,2048]{1,0:T(8,128)(2,1)S(1)}, u32[]{:S(2)}, u32[]{:S(2)}) collective-permute-start(bf16[64,2048]{1,0:T(8,128)(2,1)S(1)} %get-tuple-element.89), channel_id=1, source_target_pairs={{0,6},{2,4},{4,2},{6,0},{8,14},{10,12},{12,10},{14,8},{1,7},{3,5},... | collective-permute-start | bytes 786440 | tf_op jit(solution)/shard_map/ppermute | solution.py:36
  73.9 11.8 %collective-permute-start.18 = (f32[16,896]{1,0:T(8,128)S(1)}, f32[16,896]{1,0:T(8,128)S(1)}, u32[]{:S(2)}, u32[]{:S(2)}) collective-permute-start(f32[16,896]{1,0:T(8,128)S(1)} %get-tuple-element.74.mine_ref), channel_id=1, source_target_pairs={{0,1},{1,0},{2,3},{3,2},{4,5},{5,4},{6,7},{7,6},{8,9},{9,8},{10,11... | collective-permute-start | bytes 172040 | tf_op jit(solution)/shard_map/ppermute | solution.py:32
  77.4 31.4 %collective-permute-start.25 = (bf16[64,2048]{1,0:T(8,128)(2,1)S(1)}, bf16[64,2048]{1,0:T(8,128)(2,1)S(1)}, u32[]{:S(2)}, u32[]{:S(2)}) collective-permute-start(bf16[64,2048]{1,0:T(8,128)(2,1)S(1)} %get-tuple-element.80), channel_id=1, source_target_pairs={{0,8},{2,10},{4,12},{6,14},{8,0},{10,2},{12,4},{14,6},{1,9},{3,11}... | collective-permute-start | bytes 786440 | tf_op jit(solution)/shard_map/ppermute | solution.py:36
  88.2 20.7 %collective-permute-start.26 = (bf16[64,2048]{1,0:T(8,128)(2,1)S(1)}, bf16[64,2048]{1,0:T(8,128)(2,1)S(1)}, u32[]{:S(2)}, u32[]{:S(2)}) collective-permute-start(bf16[64,2048]{1,0:T(8,128)(2,1)S(1)} %get-tuple-element.90), channel_id=1, source_target_pairs={{0,8},{2,10},{4,12},{6,14},{8,0},{10,2},{12,4},{14,6},{1,9},{3,11}... | collective-permute-start | bytes 786440 | tf_op jit(solution)/shard_map/ppermute | solution.py:36
  90.1 10.5 %collective-permute-start.22 = (bf16[64,512]{1,0:T(8,128)(2,1)S(1)}, bf16[64,512]{1,0:T(8,128)(2,1)S(1)}, u32[]{:S(2)}, u32[]{:S(2)}) collective-permute-start(bf16[64,512]{1,0:T(8,128)(2,1)S(1)} %get-tuple-element.93), channel_id=1, source_target_pairs={{0,2},{2,0},{4,6},{6,4},{8,10},{10,8},{12,14},{14,12},{1,3},{3,1},... | collective-permute-start | bytes 196616 | tf_op jit(solution)/shard_map/ppermute | solution.py:36
  90.9 9.7 %collective-permute-start.23 = (bf16[64,512]{1,0:T(8,128)(2,1)S(1)}, bf16[64,512]{1,0:T(8,128)(2,1)S(1)}, u32[]{:S(2)}, u32[]{:S(2)}) collective-permute-start(bf16[64,512]{1,0:T(8,128)(2,1)S(1)} %get-tuple-element.94), channel_id=1, source_target_pairs={{0,4},{2,6},{4,0},{6,2},{8,12},{10,14},{12,8},{14,10},{1,5},{3,7},... | collective-permute-start | bytes 196616 | tf_op jit(solution)/shard_map/ppermute | solution.py:36
  91.6 9.1 %collective-permute-start.24 = (bf16[64,512]{1,0:T(8,128)(2,1)S(1)}, bf16[64,512]{1,0:T(8,128)(2,1)S(1)}, u32[]{:S(2)}, u32[]{:S(2)}) collective-permute-start(bf16[64,512]{1,0:T(8,128)(2,1)S(1)} %get-tuple-element.95), channel_id=1, source_target_pairs={{0,6},{2,4},{4,2},{6,0},{8,14},{10,12},{12,10},{14,8},{1,7},{3,5},... | collective-permute-start | bytes 196616 | tf_op jit(solution)/shard_map/ppermute | solution.py:36
  101.6 5.9 %collective-permute-start.27 = (bf16[64,512]{1,0:T(8,128)(2,1)S(1)}, bf16[64,512]{1,0:T(8,128)(2,1)S(1)}, u32[]{:S(2)}, u32[]{:S(2)}) collective-permute-start(bf16[64,512]{1,0:T(8,128)(2,1)S(1)} %get-tuple-element.96), channel_id=1, source_target_pairs={{0,8},{2,10},{4,12},{6,14},{8,0},{10,2},{12,4},{14,6},{1,9},{3,11}... | collective-permute-start | bytes 196616 | tf_op jit(solution)/shard_map/ppermute | solution.py:36
  (2 other events, 12.7 us)

commit v6 on v5

--- a/solution.py
+++ b/solution.py
@@ -56,13 +56,14 @@
 
 
 def _call(
-    body, name, grid, in_specs, out_specs, out_shape, scratch, aliases=None, vmem=VMEM_LIMIT
+    body, name, grid, in_specs, out_specs, out_shape, scratch, aliases=None, vmem=VMEM_LIMIT,
+    n_scalars=1,
 ):
     return pl.pallas_call(
         body,
         name=name,
         grid_spec=pltpu.PrefetchScalarGridSpec(
-            num_scalar_prefetch=1,
+            num_scalar_prefetch=n_scalars,
             grid=grid,
             in_specs=in_specs,
             out_specs=out_specs,
@@ -85,7 +86,7 @@
         self.rank, self.cols, self.width = rank, cols, width
         self.n_far = n_dp // NEAR
         self.rows = nb * TENANT_BLOCK
-        self.me, self.core, self.quarter = (6, 0), (6, 1), (6, 2)
+        self.me, self.core, self.quarter = (8, 0), (8, 1), (8, 2)
 
     def block(self, b):
         return slice(b * TENANT_BLOCK, (b + 1) * TENANT_BLOCK)
@@ -94,10 +95,10 @@
         return slice(b * self.rank, (b + 1) * self.rank)
 
     def slot(self, info, which, b):
-        return info[which, b]
+        return info[6, info[which, b]]
 
     def valid(self, info, b):
-        return info[7, b]
+        return info[9, b]
 
     def owner_and_order(self, info, which):
         owners = [_div(self.slot(info, which, b), self.ten_dev) for b in range(self.nb)]
@@ -125,7 +126,7 @@
 
 
 def other_kernel(z, place, x_hbm, w_hbm, out_ref, x_buf, w_buf, x_sem, w_sem):
-    far = pl.ds(pl.multiple_of((1 - place[z.core[1]]) * z.cols, z.cols), z.cols)
+    far = pl.ds(pl.multiple_of((1 - place[z.core]) * z.cols, z.cols), z.cols)
     unit = z.width // 8
     copies = []
     for i, (first, last) in enumerate(((0, 1), (1, 2), (2, 4), (4, 6), (6, 8))):
@@ -240,11 +241,12 @@
         at += total.shape[1]
 
 
-def choose_kernel(z, info, own_ref, near_ref, far_ref, farther_ref, *outs):
+def choose_kernel(z, info, info_x, own_ref, near_ref, far_ref, farther_ref, *outs):
     sources = (own_ref, near_ref, far_ref, farther_ref)
-    for which, out in zip((0, 1, 4, 5), outs):
+    wanted = ((info, 0), (info, 1), (info_x, 0), (info_x, 1))
+    for (table, which), out in zip(wanted, outs):
         for b in range(z.nb):
-            s = z.slot(info, which, b)
+            s = z.slot(table, which, b)
             rel = _div(s, z.ten_dev) ^ info[z.me]
             at = _rem(rel, 2) * z.ten_dev + _rem(s, z.ten_dev)
             line = _div(rel, 2)
@@ -282,7 +284,14 @@
         out_ref[cut, :] = _masked(full, z.valid(info, b)).astype(bf16)
 
 
-def tokens_kernel(z, first, info, g_ref, w_ref, mine_ref, other_ref, d_ref, *refs):
+def through_kernel(info, g_ref, w_ref, out_ref):
+    half = out_ref.shape[1] // 2
+    for h in range(2):
+        cut = slice(h * half, (h + 1) * half)
+        out_ref[:, cut] = _dot(g_ref[...], w_ref[cut, :], NT)
+
+
+def tokens_kernel(z, first, ready, info, g_ref, w_ref, mine_ref, other_ref, d_ref, *refs):
     out_ref, spread = refs[-2:]
     step = pl.program_id(0)
 
@@ -296,7 +305,7 @@
 
     wide = out_ref.shape[1]
     cut = pl.ds(pl.multiple_of((first + step) * wide, wide), wide)
-    through = _dot(g_ref[...], w_ref[cut, :], NT)
+    through = g_ref[:, cut] if ready else _dot(g_ref[...], w_ref[cut, :], NT)
     out_ref[...] = (through + _dot(spread[...], d_ref[:, cut], TN)).astype(bf16)
 
 
@@ -332,16 +341,14 @@
         to_y = lax.dynamic_slice_in_dim(down_t, (mine_q ^ 1) * quarter, quarter, axis=2)
         from_y = _xor(to_y, n_dp, 1)
     far_up = [_xor(adapter_up, n_dp, NEAR * j) for j in range(1, n_far)]
-    lanes = jnp.pad(block_tenant, (0, LANES - nb))
-    tenant_match = lanes[:, None] == jnp.arange(tenants, dtype=i32)[None, :]
-    slots = jnp.sum(jnp.where(tenant_match, tenant_slot[None, :], 0), axis=1).astype(i32)
     lane = jnp.arange(LANES, dtype=i32)
-    place = jnp.where(lane == 0, me, jnp.where(lane == 1, core, mine_q))
-    slots = _tie(slots, place)
-    slots_x = _swap(slots, "groups") if shared else slots
-
-    line = lax.broadcasted_iota(i32, (16, LANES), 0)
-    tag = jnp.where(line == 0, slots[None, :], slots_x[None, :]).astype(bf16)
+
+    def spread_out(x):
+        hit = lane[:, None] == jnp.arange(x.shape[0], dtype=i32)[None, :]
+        return jnp.sum(jnp.where(hit, x[None, :], 0), axis=1).astype(i32)
+
+    own_tenants = spread_out(block_tenant)
+    tag = jnp.broadcast_to(own_tenants[None, :], (16, LANES)).astype(bf16)
     tag = jnp.pad(tag, ((0, 0), (0, cols - LANES)))
     ups = [u.reshape(ten_dev * rank, cols) for u in [adapter_up] + far_up]
     packet = jnp.concatenate(ups + [tag], axis=0)
@@ -352,6 +359,12 @@
         shard = jnp.concatenate([own, from_y], axis=0)
         shard_far = _xor(shard, n_dp, 4)
         shard_near = _xor(shard, n_dp, 2)
+
+    line = lax.broadcasted_iota(i32, (16, LANES), 0)
+    place = jnp.where(lane == 0, me, jnp.where(lane == 1, core, mine_q))
+    info = jnp.where(line == 8, place[None, :], spread_out(block_valid)[None, :])
+    info = jnp.where(line == 6, spread_out(tenant_slot)[None, :], info)
+    info = jnp.where(line == 0, own_tenants[None, :], info)
 
     base_other = _call(
         functools.partial(other_kernel, z), "base_other", (1,),
@@ -362,20 +375,17 @@
             pltpu.SemaphoreType.DMA((5,)), pltpu.SemaphoreType.DMA((5,)),
         ],
         vmem=BIG_VMEM,
-    )(_tie(place, shard if shared else packet), tokens, base_weight)
+    )(_tie(info, shard if shared else packet), tokens, base_weight)
     base_arrived = _swap(base_other, "tensor")
     packets = [_tie(p, base_other) for p in packets]
 
-    line = lax.broadcasted_iota(i32, (8, LANES), 0)
-    info = jnp.where(line == 6, place[None, :], jnp.pad(block_valid, (0, LANES - nb))[None, :])
-    for k in range(NEAR):
+    for k in range(1, NEAR):
         info = jnp.where(line == k, packets[k][-16, :LANES].astype(i32)[None, :], info)
-    for k in range(2):
-        info = jnp.where(line == 4 + k, packets[k][-15, :LANES].astype(i32)[None, :], info)
 
     if shared:
         info = _tie(info, shard_far, shard_near)
         farther = _xor(shard_far, n_dp, 2)
+        info_x = _swap(info, "groups")
 
     part = (rank, rows)
     block_up, back_part = _call(
@@ -422,20 +432,15 @@
         return total.reshape(ten_dev, rank, wide)
 
     half = width // 2
-    sends_a = pack(_tie(info, cotangent_other, base_arrived), 0, half)
-
-    base_own, g_full = _call(
-        functools.partial(own_kernel, z), "base_own", (1,),
-        [VMEM] * 5, [VMEM, VMEM],
-        [_shape((rows, cols), f32), _shape((rows, 2 * cols), bf16)], [],
-    )(_tie(info, sends_a[0]), tokens, base_weight, base_arrived, out_cotangent, cotangent_other)
+    sends_a = pack(_tie(info, cotangent_other, base_arrived, *([info_x] if shared else [])), 0, half)
 
     if shared:
         block = (nb * rank, quarter)
         chosen = _call(
             functools.partial(choose_kernel, z), "choose", (1,),
             [VMEM] * 4, [_whole(block)] * 4, [_shape(block, bf16)] * 4, [],
-        )(_tie(info, base_own), shard, shard_near, shard_far, farther)
+            n_scalars=2,
+        )(_tie(info, sends_a[0]), info_x, shard, shard_near, shard_far, farther)
         got_y = _xor(chosen[1], n_dp, 1)
         got_x = _swap(chosen[2], "groups")
         got_d = lax.ppermute(
@@ -446,12 +451,23 @@
         after_choose = chosen[0]
     else:
         every = lax.all_gather(down_t, "dp", axis=0, tiled=True)
-        got_down = [jnp.take(every, slots[:nb], axis=0).reshape(nb * rank, width)]
-        after_choose = base_own
+        slots = jnp.take(tenant_slot, block_tenant, axis=0)
+        got_down = [jnp.take(every, slots, axis=0).reshape(nb * rank, width)]
+        after_choose = sends_a[0]
 
     sends_b = pack(_tie(info, after_choose), half, half)
 
-    gate = [sends_b[0]] + ([got_x] if shared else [])
+    base_own, g_full = _call(
+        functools.partial(own_kernel, z), "base_own", (1,),
+        [VMEM] * 5, [VMEM, VMEM],
+        [_shape((rows, cols), f32), _shape((rows, 2 * cols), bf16)], [],
+    )(_tie(info, sends_b[0]), tokens, base_weight, base_arrived, out_cotangent, cotangent_other)
+
+    through = _call(
+        through_kernel, "through", (1,), [VMEM] * 2, VMEM, _shape((rows, half), f32), [],
+    )(_tie(info, base_own), g_full, base_weight)
+
+    gate = [through]
     got_a = to_near([sends_a[0], _tie(sends_a[1], *gate), *sends_a[2:]])
     got_b = to_near(sends_b)
     if shared:
@@ -460,7 +476,7 @@
         functools.partial(shrink_kernel, z, n_parts), "shrink", (1,),
         [VMEM] * (1 + n_parts), [VMEM, _whole(part)],
         [_shape((nb * rank, width), bf16), _shape(part, f32)], [],
-    )(_tie(info, sends_b[0]), tokens, *got_down)
+    )(_tie(info, through), tokens, *got_down)
     shrink_other = _swap(shrink_part, "tensor")
 
     dense_a = dense(_tie(info, shrink_part), got_a)
@@ -470,20 +486,20 @@
     n_calls = 2
     per_call = width // step // n_calls
 
-    def token_grads(info, call, so_far):
+    def token_grads(info, call, g, so_far):
         first = call * per_call
         return _call(
-            functools.partial(tokens_kernel, z, first), "token_grads", (per_call,),
+            functools.partial(tokens_kernel, z, first, so_far is None), "token_grads", (per_call,),
             [VMEM] * 5 + ([] if so_far is None else [pl.BlockSpec(memory_space=pl.ANY)]),
             pl.BlockSpec((rows, step), lambda i, *_: (0, first + i)),
             _shape((rows, width), bf16), [pltpu.VMEM((nb * rank, rows), bf16)],
             None if so_far is None else {6: 0},
         )(
-            info, g_full, base_weight, back_part, back_other, block_down,
+            info, g, g if so_far is None else base_weight, back_part, back_other, block_down,
             *([] if so_far is None else [so_far]),
         )
 
-    grad_tokens = token_grads(_tie(info, dense_a[1]), 0, None)
+    grad_tokens = token_grads(_tie(info, dense_a[1]), 0, through, None)
 
     up_sends = _call(
         functools.partial(pack_up_kernel, z, NEAR), "pack_up", (1,),
@@ -496,7 +512,7 @@
     dense_b = dense(_tie(info, up_sends[0]), got_b)
     far_b = to_far(dense_b)
 
-    grad_tokens = token_grads(_tie(info, dense_b[1]), 1, grad_tokens)
+    grad_tokens = token_grads(_tie(info, dense_b[1]), 1, g_full, grad_tokens)
     dense_u = dense(_tie(info, grad_tokens), got_u)
     far_u = to_far(dense_u)
 

time: 111 us -> 108 us (0.973)
  local copies, waits for them, and re-layouts: 5.71 us -> 1.02 us
  Pallas kernels: 43.2 us -> 45.4 us
  starting transfers between devices: 36.4 us -> 34.5 us
    unnamed x12 -> x10, local copies, waits for them, and re-layouts: 3.41 us -> 0.03 us
    ppermute x21, waiting for transfers between devices: 19.3 us -> 21.4 us  [_xor(): return lax.ppermute(x, 'dp', [(i, i ^ k) for i in range(n)])]
    pad x2, local copies, waits for them, and re-layouts: 1.32 us -> 0.01 us  [on_device(): tag = jnp.pad(tag, ((0, 0), (0, cols - LANES)))]
    pallas_call x2 -> x3, Pallas kernels: 14.2 us -> 15 us  [the longest x2 10.3 us: token_grads(): _call(functools.partial(tokens_kernel, z, first, so_far is None), 'token_...]
  transfers between devices with their start and end apart: 28 -> 28, of which waited for: 8 -> 8; matrix products, arithmetic and copies ran while one was open for 2% -> 3% of each run, Pallas kernels for 38% -> 40%
where the time goes in v6:
time: 108 us
  Pallas kernels  45.4 us (42%)
  starting transfers between devices  34.5 us (32%)
  waiting for transfers between devices  23.6 us (22%)
  other arithmetic  2.58 us (2%)
    ppermute x21, starting transfers between devices, _xor(): return lax.ppermute(x, 'dp', [(i, i ^ k) for i in range(n)])  29.7 us
    ppermute x21, waiting for transfers between devices, _xor(): return lax.ppermute(x, 'dp', [(i, i ^ k) for i in range(n)])  21.4 us
    pallas_call x2, Pallas kernels, token_grads(): _call(functools.partial(tokens_kernel, z, first, so_far is None), 'token_...  10.3 us
    pallas_call x1, Pallas kernels, on_device(): _call(functools.partial(other_kernel, z), 'base_other', (1,), [pl.BlockSp...  6.61 us
    pallas_call x1, Pallas kernels, on_device(): _call(functools.partial(own_kernel, z), 'base_own', (1,), [VMEM] * 5, [VM...  4.77 us
    pallas_call x1, Pallas kernels, on_device(): _call(through_kernel, 'through', (1,), [VMEM] * 2, VMEM, _shape((rows, ha...  4.66 us
    pallas_call x3, Pallas kernels, dense(): _call(functools.partial(dense_kernel, z), 'dense', (1,), [VMEM] * NEAR, [...  3.95 us
    pallas_call x2, Pallas kernels, pack(): _call(functools.partial(pack_kernel, z, NEAR, start), 'pack_down', (1,),...  3.94 us
  transfers between devices with their start and end apart: 28, of which 8 were waited for; matrix products, arithmetic and copies ran while one was open for 3% of the time, Pallas kernels for 40%

profile of v6, /device:TPU:0, one launch (start us, length us, event | category | flops | bytes accessed | tf_op | source)
XLA Modules:
  0.0 108.0 jit_solution(16062112232498995972)
XLA Ops:
  0.6 4.1 %collective-permute-start = (bf16[4,16,512]{2,1,0:T(8,128)(2,1)}, bf16[4,16,512]{2,1,0:T(8,128)(2,1)S(1)}, u32[]{:S(2)}, u32[]{:S(2)}) collective-permute-start(bf16[4,16,512]{2,1,0:T(8,128)(2,1)} %param.11), channel_id=1, source_target_pairs={{0,8},{2,10},{4,12},{6,14},{8,0},{10,2},{12,4},{14,6},{1,9},{3,11}... | collective-permute-start | bytes 196616 | tf_op jit(solution)/shard_map/ppermute | solution.py:36
  5.7 1.6 %collective-permute-start.2 = (bf16[4,16,1024]{2,1,0:T(8,128)(2,1)S(1)}, bf16[4,16,1024]{2,1,0:T(8,128)(2,1)S(1)}, u32[]{:S(2)}, u32[]{:S(2)}) collective-permute-start(bf16[4,16,1024]{2,1,0:T(8,128)(2,1)S(1)} %get-tuple-element.103), channel_id=1, source_target_pairs={{0,2},{2,0},{4,6},{6,4},{8,10},{10,8},{12,14},{14,12},{1,3},{3,1},... | collective-permute-start | bytes 393224 | tf_op jit(solution)/shard_map/ppermute | solution.py:36
  9.8 1.4 %collective-permute-start.4 = (bf16[144,512]{1,0:T(8,128)(2,1)S(1)}, bf16[144,512]{1,0:T(8,128)(2,1)S(1)}, u32[]{:S(2)}, u32[]{:S(2)}) collective-permute-start(bf16[144,512]{1,0:T(8,128)(2,1)S(1)} %pad_maximum_fusion.1.refs_0_), channel_id=1, source_target_pairs={{0,2},{2,0},{4,6},{6,4},{8,10},{10,8},{12,14},{14,12},{1,3},{3,1},... | collective-permute-start | bytes 442376 | tf_op jit(solution)/shard_map/ppermute | solution.py:36
  12.0 1.4 %collective-permute-start.1 = (bf16[144,512]{1,0:T(8,128)(2,1)S(1)}, bf16[144,512]{1,0:T(8,128)(2,1)S(1)}, u32[]{:S(2)}, u32[]{:S(2)}) collective-permute-start(bf16[144,512]{1,0:T(8,128)(2,1)S(1)} %pad_maximum_fusion.1.refs_0_), channel_id=1, source_target_pairs={{0,6},{2,4},{4,2},{6,0},{8,14},{10,12},{12,10},{14,8},{1,7},{3,5},... | collective-permute-start | bytes 442376 | tf_op jit(solution)/shard_map/ppermute | solution.py:36
  13.4 1.6 %collective-permute-start.6 = (bf16[8,16,1024]{2,1,0:T(8,128)(2,1)S(1)}, bf16[8,16,1024]{2,1,0:T(8,128)(2,1)S(1)}, u32[]{:S(2)}, u32[]{:S(2)}) collective-permute-start(bf16[8,16,1024]{2,1,0:T(8,128)(2,1)S(1)} %pad_maximum_fusion.own_ref), channel_id=1, source_target_pairs={{0,4},{2,6},{4,0},{6,2},{8,12},{10,14},{12,8},{14,10},{1,5},{3,7},... | collective-permute-start | bytes 786440 | tf_op jit(solution)/shard_map/ppermute | solution.py:36
  15.1 2.0 %collective-permute-start.5 = (bf16[8,16,1024]{2,1,0:T(8,128)(2,1)S(1)}, bf16[8,16,1024]{2,1,0:T(8,128)(2,1)S(1)}, u32[]{:S(2)}, u32[]{:S(2)}) collective-permute-start(bf16[8,16,1024]{2,1,0:T(8,128)(2,1)S(1)} %pad_maximum_fusion.own_ref), channel_id=1, source_target_pairs={{0,8},{2,10},{4,12},{6,14},{8,0},{10,2},{12,4},{14,6},{1,9},{3,11}... | collective-permute-start | bytes 786440 | tf_op jit(solution)/shard_map/ppermute | solution.py:36
  17.1 6.6 %base_other.1 = bf16[896,512]{1,0:T(8,128)(2,1)S(1)} custom-call(s32[16,128]{1,0:T(8,128)S(1)} %select_select_fusion.1.place, bf16[896,4096]{1,0:T(8,128)(2,1)} %x_ref.7, bf16[4096,1024]{1,0:T(8,128)(2,1)} %w_ref.5), custom_call_target="tpu_custom_call" | custom-call | flops 1 | bytes 1 | tf_op jit(solution)/shard_map/base_other/pallas_call | solution.py:369
  23.8 3.1 %collective-permute-done.1.refs_3_ = bf16[144,512]{1,0:T(8,128)(2,1)S(1)} collective-permute-done((bf16[144,512]{1,0:T(8,128)(2,1)S(1)}, bf16[144,512]{1,0:T(8,128)(2,1)S(1)}, u32[]{:S(2)}, u32[]{:S(2)}) %collective-permute-start.1) | collective-permute-done | bytes 147488 | tf_op jit(solution)/shard_map/ppermute | solution.py:36
  27.0 3.2 %collective-permute-done.6.near_ref = bf16[8,16,1024]{2,1,0:T(8,128)(2,1)S(1)} collective-permute-done((bf16[8,16,1024]{2,1,0:T(8,128)(2,1)S(1)}, bf16[8,16,1024]{2,1,0:T(8,128)(2,1)S(1)}, u32[]{:S(2)}, u32[]{:S(2)}) %collective-permute-start.6) | collective-permute-done | bytes 262176 | tf_op jit(solution)/shard_map/ppermute | solution.py:36
  31.2 2.6 %collective-permute-start.11 = (bf16[8,16,1024]{2,1,0:T(8,128)(2,1)S(1)}, bf16[8,16,1024]{2,1,0:T(8,128)(2,1)S(1)}, u32[]{:S(2)}, u32[]{:S(2)}) collective-permute-start(bf16[8,16,1024]{2,1,0:T(8,128)(2,1)S(1)} %collective-permute-done.5.far_ref), channel_id=1, source_target_pairs={{0,4},{2,6},{4,0},{6,2},{8,12},{10,14},{12,8},{14,10},{1,5},{3,7},... | collective-permute-start | bytes 786440 | tf_op jit(solution)/shard_map/ppermute | solution.py:36
  34.1 1.5 %collective-permute-start.9 = (s32[16,128]{1,0:T(8,128)S(1)}, s32[16,128]{1,0:T(8,128)S(1)}, u32[]{:S(2)}, u32[]{:S(2)}) collective-permute-start(s32[16,128]{1,0:T(8,128)S(1)} %select_select_fusion.info), channel_id=1, source_target_pairs={{0,16},{16,0},{1,17},{17,1},{2,18},{18,2},{3,19},{19,3},{4,20},{20... | collective-permute-start | bytes 24584 | tf_op jit(solution)/shard_map/ppermute | solution.py:32
  35.5 2.2 %collective-permute-done.9.info_x = s32[16,128]{1,0:T(8,128)S(1)} collective-permute-done((s32[16,128]{1,0:T(8,128)S(1)}, s32[16,128]{1,0:T(8,128)S(1)}, u32[]{:S(2)}, u32[]{:S(2)}) %collective-permute-start.9) | collective-permute-done | bytes 8224 | tf_op jit(solution)/shard_map/ppermute | solution.py:32
  37.7 2.0 %pack_down.2 = (bf16[64,2048]{1,0:T(8,128)(2,1)S(1)}, bf16[64,2048]{1,0:T(8,128)(2,1)S(1)}, bf16[64,2048]{1,0:T(8,128)(2,1)S(1)}, bf16[64,2048]{1,0:T(8,128)(2,1)S(1)}) custom-call(s32[16,128]{1,0:T(8,128)S(1)} %select_select_fusion.info, f32[16,896]{1,0:T(8,128)S(1)} %get-tuple-element.59.mine_ref, f32[16,896]{1,0:T(8,128)S(1)} %collective-permute-done.10.other_ref, ...), custom_call_target="tpu_custom_call" | custom-call | flops 1 | bytes 1 | tf_op jit(solution)/shard_map/pack_down/pallas_call | solution.py:403
  42.4 1.5 %collective-permute-start.13 = (bf16[112,1024]{1,0:T(8,128)(2,1)S(1)}, bf16[112,1024]{1,0:T(8,128)(2,1)S(1)}, u32[]{:S(2)}, u32[]{:S(2)}) collective-permute-start(bf16[112,1024]{1,0:T(8,128)(2,1)S(1)} %get-tuple-element.73), channel_id=1, source_target_pairs={{0,16},{16,0},{1,17},{17,1},{2,18},{18,2},{3,19},{19,3},{4,20},{20... | collective-permute-start | bytes 688136 | tf_op jit(solution)/shard_map/ppermute | solution.py:32
  43.9 1.5 %collective-permute-start.14 = (bf16[112,1024]{1,0:T(8,128)(2,1)S(1)}, bf16[112,1024]{1,0:T(8,128)(2,1)S(1)}, u32[]{:S(2)}, u32[]{:S(2)}) collective-permute-start(bf16[112,1024]{1,0:T(8,128)(2,1)S(1)} %get-tuple-element.74), channel_id=1, source_target_pairs={{0,18},{2,16},{4,22},{6,20},{8,26},{10,24},{12,30},{14,28},{16,2},... | collective-permute-start | bytes 688136 | tf_op jit(solution)/shard_map/ppermute | solution.py:446
  45.4 2.0 %collective-permute-start.17 = (bf16[64,2048]{1,0:T(8,128)(2,1)S(1)}, bf16[64,2048]{1,0:T(8,128)(2,1)S(1)}, u32[]{:S(2)}, u32[]{:S(2)}) collective-permute-start(bf16[64,2048]{1,0:T(8,128)(2,1)S(1)} %get-tuple-element.80), channel_id=1, source_target_pairs={{0,6},{2,4},{4,2},{6,0},{8,14},{10,12},{12,10},{14,8},{1,7},{3,5},... | collective-permute-start | bytes 786440 | tf_op jit(solution)/shard_map/ppermute | solution.py:36
  47.4 2.0 %pack_down.3 = (bf16[64,2048]{1,0:T(8,128)(2,1)S(1)}, bf16[64,2048]{1,0:T(8,128)(2,1)S(1)}, bf16[64,2048]{1,0:T(8,128)(2,1)S(1)}, bf16[64,2048]{1,0:T(8,128)(2,1)S(1)}) custom-call(s32[16,128]{1,0:T(8,128)S(1)} %select_select_fusion.info, f32[16,896]{1,0:T(8,128)S(1)} %get-tuple-element.59.mine_ref, f32[16,896]{1,0:T(8,128)S(1)} %collective-permute-done.10.other_ref, ...), custom_call_target="tpu_custom_call" | custom-call | flops 1 | bytes 1 | tf_op jit(solution)/shard_map/pack_down/pallas_call | solution.py:403
  49.4 4.8 %base_own.1 = (f32[896,512]{1,0:T(8,128)S(1)}, bf16[896,1024]{1,0:T(8,128)(2,1)S(1)}) custom-call(s32[16,128]{1,0:T(8,128)S(1)} %select_select_fusion.info, bf16[896,4096]{1,0:T(8,128)(2,1)S(1)} %bitcast.20, bf16[4096,1024]{1,0:T(8,128)(2,1)S(1)} %bitcast.22, bf16[896,512]{1,0:T(8,128)(2,1)S(1)} %collective-permute-done.8.far_ref, ...), custom_call_target="tpu_custom_call" | custom-call | flops 1 | bytes 1 | tf_op jit(solution)/shard_map/base_own/pallas_call | solution.py:460
  54.2 4.7 %through.1.g_ref.w_ref = f32[896,2048]{1,0:T(8,128)S(1)} custom-call(s32[16,128]{1,0:T(8,128)S(1)} %select_select_fusion.info, bf16[896,1024]{1,0:T(8,128)(2,1)S(1)} %get-tuple-element.70.g_ref, bf16[4096,1024]{1,0:T(8,128)(2,1)S(1)} %bitcast.22), custom_call_target="tpu_custom_call" | custom-call | flops 1 | bytes 1 | tf_op jit(solution)/shard_map/through/pallas_call | solution.py:466
  60.5 1.4 %collective-permute-start.19 = (bf16[64,2048]{1,0:T(8,128)(2,1)S(1)}, bf16[64,2048]{1,0:T(8,128)(2,1)S(1)}, u32[]{:S(2)}, u32[]{:S(2)}) collective-permute-start(bf16[64,2048]{1,0:T(8,128)(2,1)S(1)} %get-tuple-element.87), channel_id=1, source_target_pairs={{0,2},{2,0},{4,6},{6,4},{8,10},{10,8},{12,14},{14,12},{1,3},{3,1},... | collective-permute-start | bytes 786440 | tf_op jit(solution)/shard_map/ppermute | solution.py:36
  61.9 2.6 %collective-permute-start.20 = (bf16[64,2048]{1,0:T(8,128)(2,1)S(1)}, bf16[64,2048]{1,0:T(8,128)(2,1)S(1)}, u32[]{:S(2)}, u32[]{:S(2)}) collective-permute-start(bf16[64,2048]{1,0:T(8,128)(2,1)S(1)} %get-tuple-element.88), channel_id=1, source_target_pairs={{0,4},{2,6},{4,0},{6,2},{8,12},{10,14},{12,8},{14,10},{1,5},{3,7},... | collective-permute-start | bytes 786440 | tf_op jit(solution)/shard_map/ppermute | solution.py:36
  64.4 2.8 %shrink.1 = (bf16[112,4096]{1,0:T(8,128)(2,1)S(1)}, f32[16,896]{1,0:T(8,128)S(1)}) custom-call(s32[16,128]{1,0:T(8,128)S(1)} %select_select_fusion.info, bf16[896,4096]{1,0:T(8,128)(2,1)S(1)} %bitcast.20, bf16[112,1024]{1,0:T(8,128)(2,1)S(1)} %get-tuple-element.64.refs_0_, bf16[112,1024]{1,0:T(8,128)(2,1)S(1)} %collective-permute-done.12.refs_1_, ...), custom_call_target="tpu_custom_call" | custom-call | flops 1 | bytes 1 | tf_op jit(solution)/shard_map/shrink/pallas_call | solution.py:475
  67.3 7.1 %collective-permute-done.15.refs_1_ = bf16[64,2048]{1,0:T(8,128)(2,1)S(1)} collective-permute-done((bf16[64,2048]{1,0:T(8,128)(2,1)S(1)}, bf16[64,2048]{1,0:T(8,128)(2,1)S(1)}, u32[]{:S(2)}, u32[]{:S(2)}) %collective-permute-start.15) | collective-permute-done | bytes 262176 | tf_op jit(solution)/shard_map/ppermute | solution.py:36
  75.8 2.1 %collective-permute-start.25 = (bf16[64,2048]{1,0:T(8,128)(2,1)S(1)}, bf16[64,2048]{1,0:T(8,128)(2,1)S(1)}, u32[]{:S(2)}, u32[]{:S(2)}) collective-permute-start(bf16[64,2048]{1,0:T(8,128)(2,1)S(1)} %get-tuple-element.81), channel_id=1, source_target_pairs={{0,8},{2,10},{4,12},{6,14},{8,0},{10,2},{12,4},{14,6},{1,9},{3,11}... | collective-permute-start | bytes 786440 | tf_op jit(solution)/shard_map/ppermute | solution.py:36
  77.9 3.3 %token_grads.2.refs_0_ = bf16[896,4096]{1,0:T(8,128)(2,1)} custom-call(s32[16,128]{1,0:T(8,128)S(1)} %select_select_fusion.info, f32[896,2048]{1,0:T(8,128)S(1)} %through.1.g_ref.w_ref, f32[896,2048]{1,0:T(8,128)S(1)} %through.1.g_ref.w_ref, f32[16,896]{1,0:T(8,128)S(1)} %get-tuple-element.59.mine_ref, f32[16,896]{1,0:T(8,128)S(1)} %collective-permute-done.10.other_ref, ...), custom_call_target="tpu_custom_call" | custom-call | flops 1 | bytes 1 | tf_op jit(solution)/shard_map/token_grads/pallas_call | solution.py:491
  82.3 1.4 %dense.4 = (f32[64,2048]{1,0:T(8,128)S(1)}, bf16[64,2048]{1,0:T(8,128)(2,1)S(1)}) custom-call(s32[16,128]{1,0:T(8,128)S(1)} %select_select_fusion.info, bf16[64,2048]{1,0:T(8,128)(2,1)S(1)} %get-tuple-element.66.refs_0_, bf16[64,2048]{1,0:T(8,128)(2,1)S(1)} %collective-permute-done.19.refs_1_, bf16[64,2048]{1,0:T(8,128)(2,1)S(1)} %collective-permute-done.20.refs_2_, ...), custom_call_target="tpu_custom_call" | custom-call | flops 1 | bytes 1 | tf_op jit(solution)/shard_map/dense/pallas_call | solution.py:416
  85.7 2.5 %collective-permute-start.24 = (bf16[64,512]{1,0:T(8,128)(2,1)S(1)}, bf16[64,512]{1,0:T(8,128)(2,1)S(1)}, u32[]{:S(2)}, u32[]{:S(2)}) collective-permute-start(bf16[64,512]{1,0:T(8,128)(2,1)S(1)} %get-tuple-element.95), channel_id=1, source_target_pairs={{0,6},{2,4},{4,2},{6,0},{8,14},{10,12},{12,10},{14,8},{1,7},{3,5},... | collective-permute-start | bytes 196616 | tf_op jit(solution)/shard_map/ppermute | solution.py:36
  88.2 7.1 %token_grads.3 = bf16[896,4096]{1,0:T(8,128)(2,1)} custom-call(s32[16,128]{1,0:T(8,128)S(1)} %select_select_fusion.info, bf16[896,1024]{1,0:T(8,128)(2,1)S(1)} %get-tuple-element.70.g_ref, bf16[4096,1024]{1,0:T(8,128)(2,1)S(1)} %bitcast.22, f32[16,896]{1,0:T(8,128)S(1)} %get-tuple-element.59.mine_ref, ...), custom_call_target="tpu_custom_call", output_to_operand_aliasing={{}: (6, {})} | custom-call | flops 1 | bytes 1 | tf_op jit(solution)/shard_map/token_grads/pallas_call | solution.py:491
  95.3 2.5 %collective-permute-done.24.refs_3_ = bf16[64,512]{1,0:T(8,128)(2,1)S(1)} collective-permute-done((bf16[64,512]{1,0:T(8,128)(2,1)S(1)}, bf16[64,512]{1,0:T(8,128)(2,1)S(1)}, u32[]{:S(2)}, u32[]{:S(2)}) %collective-permute-start.24) | collective-permute-done | bytes 65568 | tf_op jit(solution)/shard_map/ppermute | solution.py:36
  99.1 2.0 %projected.1 = bf16[896,512]{1,0:T(8,128)(2,1)} custom-call(s32[16,128]{1,0:T(8,128)S(1)} %select_select_fusion.info, f32[896,512]{1,0:T(8,128)S(1)} %get-tuple-element.68.base_ref, f32[16,896]{1,0:T(8,128)S(1)} %get-tuple-element.75.mine_ref, f32[16,896]{1,0:T(8,128)S(1)} %collective-permute-done.18.other_ref, bf16[112,512]{1,0:T(8,128)(2,1)S(1)} %get-tuple-element.98.up_ref), custom_call_target="tpu_custom_call" | custom-call | flops 1 | bytes 1 | tf_op jit(solution)/shard_map/projected/pallas_call | solution.py:519
  101.1 3.8 %collective-permute-done.27.refs_1_ = bf16[64,512]{1,0:T(8,128)(2,1)S(1)} collective-permute-done((bf16[64,512]{1,0:T(8,128)(2,1)S(1)}, bf16[64,512]{1,0:T(8,128)(2,1)S(1)}, u32[]{:S(2)}, u32[]{:S(2)}) %collective-permute-start.27) | collective-permute-done | bytes 65568 | tf_op jit(solution)/shard_map/ppermute | solution.py:36
  106.3 1.7 %final.2 = f32[64,4096]{1,0:T(8,128)} custom-call(s32[16,128]{1,0:T(8,128)S(1)} %select_select_fusion.info, f32[64,2048]{1,0:T(8,128)S(1)} %get-tuple-element.99.refs_0_, bf16[64,2048]{1,0:T(8,128)(2,1)S(1)} %collective-permute-done.25.refs_1_, f32[64,2048]{1,0:T(8,128)S(1)} %get-tuple-element.100.refs_2_, bf16[64,2048]{1,0:T(8,128)(2,1)S(1)} %collective-permute-done.26.refs_3_), custom_call_target="tpu_custom_call" | custom-call | flops 1 | bytes 1 | tf_op jit(solution)/shard_map/final/pallas_call | solution.py:428
  (70 shorter events, 17.0 us)
Async XLA Ops:
  0.6 8.3 %collective-permute-start = (bf16[4,16,512]{2,1,0:T(8,128)(2,1)}, bf16[4,16,512]{2,1,0:T(8,128)(2,1)S(1)}, u32[]{:S(2)}, u32[]{:S(2)}) collective-permute-start(bf16[4,16,512]{2,1,0:T(8,128)(2,1)} %param.11), channel_id=1, source_target_pairs={{0,8},{2,10},{4,12},{6,14},{8,0},{10,2},{12,4},{14,6},{1,9},{3,11}... | collective-permute-start | bytes 196616 | tf_op jit(solution)/shard_map/ppermute | solution.py:36
  5.7 7.7 %collective-permute-start.2 = (bf16[4,16,1024]{2,1,0:T(8,128)(2,1)S(1)}, bf16[4,16,1024]{2,1,0:T(8,128)(2,1)S(1)}, u32[]{:S(2)}, u32[]{:S(2)}) collective-permute-start(bf16[4,16,1024]{2,1,0:T(8,128)(2,1)S(1)} %get-tuple-element.103), channel_id=1, source_target_pairs={{0,2},{2,0},{4,6},{6,4},{8,10},{10,8},{12,14},{14,12},{1,3},{3,1},... | collective-permute-start | bytes 393224 | tf_op jit(solution)/shard_map/ppermute | solution.py:36
  9.8 13.9 %collective-permute-start.4 = (bf16[144,512]{1,0:T(8,128)(2,1)S(1)}, bf16[144,512]{1,0:T(8,128)(2,1)S(1)}, u32[]{:S(2)}, u32[]{:S(2)}) collective-permute-start(bf16[144,512]{1,0:T(8,128)(2,1)S(1)} %pad_maximum_fusion.1.refs_0_), channel_id=1, source_target_pairs={{0,2},{2,0},{4,6},{6,4},{8,10},{10,8},{12,14},{14,12},{1,3},{3,1},... | collective-permute-start | bytes 442376 | tf_op jit(solution)/shard_map/ppermute | solution.py:36
  11.2 12.6 %collective-permute-start.3 = (bf16[144,512]{1,0:T(8,128)(2,1)S(1)}, bf16[144,512]{1,0:T(8,128)(2,1)S(1)}, u32[]{:S(2)}, u32[]{:S(2)}) collective-permute-start(bf16[144,512]{1,0:T(8,128)(2,1)S(1)} %pad_maximum_fusion.1.refs_0_), channel_id=1, source_target_pairs={{0,4},{2,6},{4,0},{6,2},{8,12},{10,14},{12,8},{14,10},{1,5},{3,7},... | collective-permute-start | bytes 442376 | tf_op jit(solution)/shard_map/ppermute | solution.py:36
  12.0 14.9 %collective-permute-start.1 = (bf16[144,512]{1,0:T(8,128)(2,1)S(1)}, bf16[144,512]{1,0:T(8,128)(2,1)S(1)}, u32[]{:S(2)}, u32[]{:S(2)}) collective-permute-start(bf16[144,512]{1,0:T(8,128)(2,1)S(1)} %pad_maximum_fusion.1.refs_0_), channel_id=1, source_target_pairs={{0,6},{2,4},{4,2},{6,0},{8,14},{10,12},{12,10},{14,8},{1,7},{3,5},... | collective-permute-start | bytes 442376 | tf_op jit(solution)/shard_map/ppermute | solution.py:36
  13.4 24.3 %slice-start = ((s8[7340032]{0:T(1024)(128)(4,1)}), s8[4194304]{0:T(1024)(128)(4,1)S(1)}, s32[]{:S(2)}) async-start(s8[7340032]{0:T(1024)(128)(4,1)} %bitcast.19), calls=%async_computation | async-start | bytes 8388608
  13.4 16.8 %copy-start = (bf16[896,512]{1,0:T(8,128)(2,1)S(1)}, bf16[896,512]{1,0:T(8,128)(2,1)}, u32[]{:S(2)}) copy-start(bf16[896,512]{1,0:T(8,128)(2,1)} %g_ref.3) | copy-start | bytes 2752516
  13.4 24.3 %slice-start.1 = ((s8[7340032]{0:T(1024)(128)(4,1)}), s8[3145728]{0:T(1024)(128)(4,1)S(1)}, s32[]{:S(2)}) async-start(s8[7340032]{0:T(1024)(128)(4,1)} %bitcast.19), calls=%async_computation.1 | async-start | bytes 6291456
  13.4 16.8 %collective-permute-start.6 = (bf16[8,16,1024]{2,1,0:T(8,128)(2,1)S(1)}, bf16[8,16,1024]{2,1,0:T(8,128)(2,1)S(1)}, u32[]{:S(2)}, u32[]{:S(2)}) collective-permute-start(bf16[8,16,1024]{2,1,0:T(8,128)(2,1)S(1)} %pad_maximum_fusion.own_ref), channel_id=1, source_target_pairs={{0,4},{2,6},{4,0},{6,2},{8,12},{10,14},{12,8},{14,10},{1,5},{3,7},... | collective-permute-start | bytes 786440 | tf_op jit(solution)/shard_map/ppermute | solution.py:36
  15.1 15.1 %collective-permute-start.5 = (bf16[8,16,1024]{2,1,0:T(8,128)(2,1)S(1)}, bf16[8,16,1024]{2,1,0:T(8,128)(2,1)S(1)}, u32[]{:S(2)}, u32[]{:S(2)}) collective-permute-start(bf16[8,16,1024]{2,1,0:T(8,128)(2,1)S(1)} %pad_maximum_fusion.own_ref), channel_id=1, source_target_pairs={{0,8},{2,10},{4,12},{6,14},{8,0},{10,2},{12,4},{14,6},{1,9},{3,11}... | collective-permute-start | bytes 786440 | tf_op jit(solution)/shard_map/ppermute | solution.py:36
  23.7 14.0 %collective-permute-start.8 = (bf16[896,512]{1,0:T(8,128)(2,1)S(1)}, bf16[896,512]{1,0:T(8,128)(2,1)S(1)}, u32[]{:S(2)}, u32[]{:S(2)}) collective-permute-start(bf16[896,512]{1,0:T(8,128)(2,1)S(1)} %base_other.1), channel_id=1, source_target_pairs={{0,1},{1,0},{2,3},{3,2},{4,5},{5,4},{6,7},{7,6},{8,9},{9,8},{10,11... | collective-permute-start | bytes 2752520 | tf_op jit(solution)/shard_map/ppermute | solution.py:32
  31.2 18.2 %slice-start.2 = ((s8[8388608]{0:T(1024)(128)(4,1)}), s8[4194304]{0:T(1024)(128)(4,1)S(1)}, s32[]{:S(2)}) async-start(s8[8388608]{0:T(1024)(128)(4,1)} %bitcast.21), calls=%async_computation.2 | async-start | bytes 8388608
  31.2 6.5 %collective-permute-start.7 = (bf16[896,512]{1,0:T(8,128)(2,1)S(1)}, bf16[896,512]{1,0:T(8,128)(2,1)S(1)}, u32[]{:S(2)}, u32[]{:S(2)}) collective-permute-start(bf16[896,512]{1,0:T(8,128)(2,1)S(1)} %copy-done), channel_id=1, source_target_pairs={{0,1},{1,0},{2,3},{3,2},{4,5},{5,4},{6,7},{7,6},{8,9},{9,8},{10,11... | collective-permute-start | bytes 2752520 | tf_op jit(solution)/shard_map/ppermute | solution.py:32
  31.2 9.6 %collective-permute-start.11 = (bf16[8,16,1024]{2,1,0:T(8,128)(2,1)S(1)}, bf16[8,16,1024]{2,1,0:T(8,128)(2,1)S(1)}, u32[]{:S(2)}, u32[]{:S(2)}) collective-permute-start(bf16[8,16,1024]{2,1,0:T(8,128)(2,1)S(1)} %collective-permute-done.5.far_ref), channel_id=1, source_target_pairs={{0,4},{2,6},{4,0},{6,2},{8,12},{10,14},{12,8},{14,10},{1,5},{3,7},... | collective-permute-start | bytes 786440 | tf_op jit(solution)/shard_map/ppermute | solution.py:36
  33.9 3.8 %collective-permute-start.10 = (f32[16,896]{1,0:T(8,128)S(1)}, f32[16,896]{1,0:T(8,128)S(1)}, u32[]{:S(2)}, u32[]{:S(2)}) collective-permute-start(f32[16,896]{1,0:T(8,128)S(1)} %get-tuple-element.59.mine_ref), channel_id=1, source_target_pairs={{0,1},{1,0},{2,3},{3,2},{4,5},{5,4},{6,7},{7,6},{8,9},{9,8},{10,11... | collective-permute-start | bytes 172040 | tf_op jit(solution)/shard_map/ppermute | solution.py:32
  34.1 3.7 %collective-permute-start.9 = (s32[16,128]{1,0:T(8,128)S(1)}, s32[16,128]{1,0:T(8,128)S(1)}, u32[]{:S(2)}, u32[]{:S(2)}) collective-permute-start(s32[16,128]{1,0:T(8,128)S(1)} %select_select_fusion.info), channel_id=1, source_target_pairs={{0,16},{16,0},{1,17},{17,1},{2,18},{18,2},{3,19},{19,3},{4,20},{20... | collective-permute-start | bytes 24584 | tf_op jit(solution)/shard_map/ppermute | solution.py:32
  39.7 24.7 %collective-permute-start.16 = (bf16[64,2048]{1,0:T(8,128)(2,1)S(1)}, bf16[64,2048]{1,0:T(8,128)(2,1)S(1)}, u32[]{:S(2)}, u32[]{:S(2)}) collective-permute-start(bf16[64,2048]{1,0:T(8,128)(2,1)S(1)} %get-tuple-element.79), channel_id=1, source_target_pairs={{0,4},{2,6},{4,0},{6,2},{8,12},{10,14},{12,8},{14,10},{1,5},{3,7},... | collective-permute-start | bytes 786440 | tf_op jit(solution)/shard_map/ppermute | solution.py:36
  41.8 18.0 %collective-permute-start.12 = (bf16[112,1024]{1,0:T(8,128)(2,1)S(1)}, bf16[112,1024]{1,0:T(8,128)(2,1)S(1)}, u32[]{:S(2)}, u32[]{:S(2)}) collective-permute-start(bf16[112,1024]{1,0:T(8,128)(2,1)S(1)} %get-tuple-element.72), channel_id=1, source_target_pairs={{0,2},{2,0},{4,6},{6,4},{8,10},{10,8},{12,14},{14,12},{1,3},{3,1},... | collective-permute-start | bytes 688136 | tf_op jit(solution)/shard_map/ppermute | solution.py:36
  42.4 18.0 %collective-permute-start.13 = (bf16[112,1024]{1,0:T(8,128)(2,1)S(1)}, bf16[112,1024]{1,0:T(8,128)(2,1)S(1)}, u32[]{:S(2)}, u32[]{:S(2)}) collective-permute-start(bf16[112,1024]{1,0:T(8,128)(2,1)S(1)} %get-tuple-element.73), channel_id=1, source_target_pairs={{0,16},{16,0},{1,17},{17,1},{2,18},{18,2},{3,19},{19,3},{4,20},{20... | collective-permute-start | bytes 688136 | tf_op jit(solution)/shard_map/ppermute | solution.py:32
  43.9 18.0 %collective-permute-start.14 = (bf16[112,1024]{1,0:T(8,128)(2,1)S(1)}, bf16[112,1024]{1,0:T(8,128)(2,1)S(1)}, u32[]{:S(2)}, u32[]{:S(2)}) collective-permute-start(bf16[112,1024]{1,0:T(8,128)(2,1)S(1)} %get-tuple-element.74), channel_id=1, source_target_pairs={{0,18},{2,16},{4,22},{6,20},{8,26},{10,24},{12,30},{14,28},{16,2},... | collective-permute-start | bytes 688136 | tf_op jit(solution)/shard_map/ppermute | solution.py:446
  45.4 21.9 %collective-permute-start.17 = (bf16[64,2048]{1,0:T(8,128)(2,1)S(1)}, bf16[64,2048]{1,0:T(8,128)(2,1)S(1)}, u32[]{:S(2)}, u32[]{:S(2)}) collective-permute-start(bf16[64,2048]{1,0:T(8,128)(2,1)S(1)} %get-tuple-element.80), channel_id=1, source_target_pairs={{0,6},{2,4},{4,2},{6,0},{8,14},{10,12},{12,10},{14,8},{1,7},{3,5},... | collective-permute-start | bytes 786440 | tf_op jit(solution)/shard_map/ppermute | solution.py:36
  59.8 14.6 %collective-permute-start.15 = (bf16[64,2048]{1,0:T(8,128)(2,1)S(1)}, bf16[64,2048]{1,0:T(8,128)(2,1)S(1)}, u32[]{:S(2)}, u32[]{:S(2)}) collective-permute-start(bf16[64,2048]{1,0:T(8,128)(2,1)S(1)} %get-tuple-element.78), channel_id=1, source_target_pairs={{0,2},{2,0},{4,6},{6,4},{8,10},{10,8},{12,14},{14,12},{1,3},{3,1},... | collective-permute-start | bytes 786440 | tf_op jit(solution)/shard_map/ppermute | solution.py:36
  60.5 21.9 %collective-permute-start.19 = (bf16[64,2048]{1,0:T(8,128)(2,1)S(1)}, bf16[64,2048]{1,0:T(8,128)(2,1)S(1)}, u32[]{:S(2)}, u32[]{:S(2)}) collective-permute-start(bf16[64,2048]{1,0:T(8,128)(2,1)S(1)} %get-tuple-element.87), channel_id=1, source_target_pairs={{0,2},{2,0},{4,6},{6,4},{8,10},{10,8},{12,14},{14,12},{1,3},{3,1},... | collective-permute-start | bytes 786440 | tf_op jit(solution)/shard_map/ppermute | solution.py:36
  61.9 20.5 %collective-permute-start.20 = (bf16[64,2048]{1,0:T(8,128)(2,1)S(1)}, bf16[64,2048]{1,0:T(8,128)(2,1)S(1)}, u32[]{:S(2)}, u32[]{:S(2)}) collective-permute-start(bf16[64,2048]{1,0:T(8,128)(2,1)S(1)} %get-tuple-element.88), channel_id=1, source_target_pairs={{0,4},{2,6},{4,0},{6,2},{8,12},{10,14},{12,8},{14,10},{1,5},{3,7},... | collective-permute-start | bytes 786440 | tf_op jit(solution)/shard_map/ppermute | solution.py:36
  64.4 17.9 %collective-permute-start.21 = (bf16[64,2048]{1,0:T(8,128)(2,1)S(1)}, bf16[64,2048]{1,0:T(8,128)(2,1)S(1)}, u32[]{:S(2)}, u32[]{:S(2)}) collective-permute-start(bf16[64,2048]{1,0:T(8,128)(2,1)S(1)} %get-tuple-element.89), channel_id=1, source_target_pairs={{0,6},{2,4},{4,2},{6,0},{8,14},{10,12},{12,10},{14,8},{1,7},{3,5},... | collective-permute-start | bytes 786440 | tf_op jit(solution)/shard_map/ppermute | solution.py:36
  67.3 13.9 %collective-permute-start.18 = (f32[16,896]{1,0:T(8,128)S(1)}, f32[16,896]{1,0:T(8,128)S(1)}, u32[]{:S(2)}, u32[]{:S(2)}) collective-permute-start(f32[16,896]{1,0:T(8,128)S(1)} %get-tuple-element.75.mine_ref), channel_id=1, source_target_pairs={{0,1},{1,0},{2,3},{3,2},{4,5},{5,4},{6,7},{7,6},{8,9},{9,8},{10,11... | collective-permute-start | bytes 172040 | tf_op jit(solution)/shard_map/ppermute | solution.py:32
  75.8 30.4 %collective-permute-start.25 = (bf16[64,2048]{1,0:T(8,128)(2,1)S(1)}, bf16[64,2048]{1,0:T(8,128)(2,1)S(1)}, u32[]{:S(2)}, u32[]{:S(2)}) collective-permute-start(bf16[64,2048]{1,0:T(8,128)(2,1)S(1)} %get-tuple-element.81), channel_id=1, source_target_pairs={{0,8},{2,10},{4,12},{6,14},{8,0},{10,2},{12,4},{14,6},{1,9},{3,11}... | collective-permute-start | bytes 786440 | tf_op jit(solution)/shard_map/ppermute | solution.py:36
  83.7 22.5 %collective-permute-start.26 = (bf16[64,2048]{1,0:T(8,128)(2,1)S(1)}, bf16[64,2048]{1,0:T(8,128)(2,1)S(1)}, u32[]{:S(2)}, u32[]{:S(2)}) collective-permute-start(bf16[64,2048]{1,0:T(8,128)(2,1)S(1)} %get-tuple-element.90), channel_id=1, source_target_pairs={{0,8},{2,10},{4,12},{6,14},{8,0},{10,2},{12,4},{14,6},{1,9},{3,11}... | collective-permute-start | bytes 786440 | tf_op jit(solution)/shard_map/ppermute | solution.py:36
  84.7 10.6 %collective-permute-start.22 = (bf16[64,512]{1,0:T(8,128)(2,1)S(1)}, bf16[64,512]{1,0:T(8,128)(2,1)S(1)}, u32[]{:S(2)}, u32[]{:S(2)}) collective-permute-start(bf16[64,512]{1,0:T(8,128)(2,1)S(1)} %get-tuple-element.93), channel_id=1, source_target_pairs={{0,2},{2,0},{4,6},{6,4},{8,10},{10,8},{12,14},{14,12},{1,3},{3,1},... | collective-permute-start | bytes 196616 | tf_op jit(solution)/shard_map/ppermute | solution.py:36
  84.7 10.6 %collective-permute-start.23 = (bf16[64,512]{1,0:T(8,128)(2,1)S(1)}, bf16[64,512]{1,0:T(8,128)(2,1)S(1)}, u32[]{:S(2)}, u32[]{:S(2)}) collective-permute-start(bf16[64,512]{1,0:T(8,128)(2,1)S(1)} %get-tuple-element.94), channel_id=1, source_target_pairs={{0,4},{2,6},{4,0},{6,2},{8,12},{10,14},{12,8},{14,10},{1,5},{3,7},... | collective-permute-start | bytes 196616 | tf_op jit(solution)/shard_map/ppermute | solution.py:36
  85.7 12.1 %collective-permute-start.24 = (bf16[64,512]{1,0:T(8,128)(2,1)S(1)}, bf16[64,512]{1,0:T(8,128)(2,1)S(1)}, u32[]{:S(2)}, u32[]{:S(2)}) collective-permute-start(bf16[64,512]{1,0:T(8,128)(2,1)S(1)} %get-tuple-element.95), channel_id=1, source_target_pairs={{0,6},{2,4},{4,2},{6,0},{8,14},{10,12},{12,10},{14,8},{1,7},{3,5},... | collective-permute-start | bytes 196616 | tf_op jit(solution)/shard_map/ppermute | solution.py:36
  99.0 5.9 %collective-permute-start.27 = (bf16[64,512]{1,0:T(8,128)(2,1)S(1)}, bf16[64,512]{1,0:T(8,128)(2,1)S(1)}, u32[]{:S(2)}, u32[]{:S(2)}) collective-permute-start(bf16[64,512]{1,0:T(8,128)(2,1)S(1)} %get-tuple-element.96), channel_id=1, source_target_pairs={{0,8},{2,10},{4,12},{6,14},{8,0},{10,2},{12,4},{14,6},{1,9},{3,11}... | collective-permute-start | bytes 196616 | tf_op jit(solution)/shard_map/ppermute | solution.py:36
  (1 other events, 9.3 us)

commit v7 on v6

--- a/solution.py
+++ b/solution.py
@@ -358,7 +358,6 @@
         own = lax.dynamic_slice_in_dim(down_t, mine_q * quarter, quarter, axis=2)
         shard = jnp.concatenate([own, from_y], axis=0)
         shard_far = _xor(shard, n_dp, 4)
-        shard_near = _xor(shard, n_dp, 2)
 
     line = lax.broadcasted_iota(i32, (16, LANES), 0)
     place = jnp.where(lane == 0, me, jnp.where(lane == 1, core, mine_q))
@@ -383,9 +382,8 @@
         info = jnp.where(line == k, packets[k][-16, :LANES].astype(i32)[None, :], info)
 
     if shared:
-        info = _tie(info, shard_far, shard_near)
+        info = _tie(info, shard_far)
         farther = _xor(shard_far, n_dp, 2)
-        info_x = _swap(info, "groups")
 
     part = (rank, rows)
     block_up, back_part = _call(
@@ -395,6 +393,10 @@
     )(info, out_cotangent, *packets)
     back_other = _swap(back_part, "tensor")
     cotangent_other = _swap(_tie(out_cotangent, back_part), "tensor")
+    ready = [cotangent_other, base_arrived]
+    if shared:
+        shard_near = _xor(_tie(shard, base_other), n_dp, 2)
+        info_x = _swap(info, "groups")
 
     packed_rows = n_dp * CAP * rank
     near_rows = packed_rows // NEAR
@@ -428,11 +430,12 @@
         total = _call(
             functools.partial(final_kernel, len(groups), n_far), "final", (1,),
             [VMEM] * (len(groups) * n_far), _whole(out), _shape(out, f32), [],
-        )(info, *[a for g in groups for a in g])
+        )(_tie(info, grad_tokens), *[a for g in groups for a in g])
         return total.reshape(ten_dev, rank, wide)
 
     half = width // 2
-    sends_a = pack(_tie(info, cotangent_other, base_arrived, *([info_x] if shared else [])), 0, half)
+    sends_a = pack(_tie(info, *ready), 0, half)
+    got_a = to_near(sends_a)
 
     if shared:
         block = (nb * rank, quarter)
@@ -441,7 +444,7 @@
             [VMEM] * 4, [_whole(block)] * 4, [_shape(block, bf16)] * 4, [],
             n_scalars=2,
         )(_tie(info, sends_a[0]), info_x, shard, shard_near, shard_far, farther)
-        got_y = _xor(chosen[1], n_dp, 1)
+        got_y = _xor(_tie(chosen[1], got_a[2]), n_dp, 1)
         got_x = _swap(chosen[2], "groups")
         got_d = lax.ppermute(
             chosen[3],
@@ -463,13 +466,18 @@
         [_shape((rows, cols), f32), _shape((rows, 2 * cols), bf16)], [],
     )(_tie(info, sends_b[0]), tokens, base_weight, base_arrived, out_cotangent, cotangent_other)
 
+    dense_a = dense(_tie(info, base_own), got_a)
+    far_a = to_far(dense_a)
+
+    gate = [dense_a[1]] + ([got_y] if shared else [])
+    got_b = to_near(
+        [_tie(b, *gate) if k in (1, 3) else _tie(b, dense_a[1]) for k, b in enumerate(sends_b)]
+    )
+
     through = _call(
         through_kernel, "through", (1,), [VMEM] * 2, VMEM, _shape((rows, half), f32), [],
-    )(_tie(info, base_own), g_full, base_weight)
-
-    gate = [through]
-    got_a = to_near([sends_a[0], _tie(sends_a[1], *gate), *sends_a[2:]])
-    got_b = to_near(sends_b)
+    )(_tie(info, dense_a[1]), g_full, base_weight)
+
     if shared:
         got_down = [chosen[0], got_y, got_x, got_d]
     block_down, shrink_part = _call(
@@ -479,17 +487,10 @@
     )(_tie(info, through), tokens, *got_down)
     shrink_other = _swap(shrink_part, "tensor")
 
-    dense_a = dense(_tie(info, shrink_part), got_a)
-    far_a = to_far(dense_a)
-
-    step = min(1024, width // 4)
-    n_calls = 2
-    per_call = width // step // n_calls
-
-    def token_grads(info, call, g, so_far):
-        first = call * per_call
+    def token_grads(info, start, wide, step, g, so_far):
+        first = start // step
         return _call(
-            functools.partial(tokens_kernel, z, first, so_far is None), "token_grads", (per_call,),
+            functools.partial(tokens_kernel, z, first, so_far is None), "token_grads", (wide // step,),
             [VMEM] * 5 + ([] if so_far is None else [pl.BlockSpec(memory_space=pl.ANY)]),
             pl.BlockSpec((rows, step), lambda i, *_: (0, first + i)),
             _shape((rows, width), bf16), [pltpu.VMEM((nb * rank, rows), bf16)],
@@ -499,7 +500,7 @@
             *([] if so_far is None else [so_far]),
         )
 
-    grad_tokens = token_grads(_tie(info, dense_a[1]), 0, through, None)
+    grad_tokens = token_grads(_tie(info, shrink_part), 0, half, half // 2, through, None)
 
     up_sends = _call(
         functools.partial(pack_up_kernel, z, NEAR), "pack_up", (1,),
@@ -512,15 +513,21 @@
     dense_b = dense(_tie(info, up_sends[0]), got_b)
     far_b = to_far(dense_b)
 
-    grad_tokens = token_grads(_tie(info, dense_b[1]), 1, g_full, grad_tokens)
-    dense_u = dense(_tie(info, grad_tokens), got_u)
-    far_u = to_far(dense_u)
-
+    rest = (width - half) // 2
+    grad_tokens = token_grads(
+        _tie(info, dense_b[1]), half, rest, rest // 2, g_full, grad_tokens
+    )
     projected = _call(
         functools.partial(projected_kernel, z), "projected", (1,),
         [VMEM] * 4, _whole((rows, cols)), _shape((rows, cols), bf16),
         [pltpu.VMEM((nb * rank, rows), bf16)],
-    )(_tie(info, dense_u[1]), base_own, shrink_part, shrink_other, block_up)
+    )(_tie(info, grad_tokens), base_own, shrink_part, shrink_other, block_up)
+    dense_u = dense(_tie(info, projected), got_u)
+    far_u = to_far(dense_u)
+    grad_tokens = token_grads(
+        _tie(info, dense_u[1]), half + rest, rest, rest // 2, g_full, grad_tokens
+    )
+
 
     grad_down = jnp.swapaxes(final([far_a, far_b]), 1, 2)
     grad_up = final([far_u])

time: 108 us -> 107 us (level)
  waiting for transfers between devices: 23.6 us -> 19.8 us
  Pallas kernels: 45.4 us -> 47.3 us
    ppermute x21, waiting for transfers between devices: 21.4 us -> 17.6 us  [_xor(): return lax.ppermute(x, 'dp', [(i, i ^ k) for i in range(n)])]
    pallas_call x2 -> x3, Pallas kernels: 10.3 us -> 12.1 us  [token_grads(): _call(functools.partial(tokens_kernel, z, first, so_far is None), 'token_...]
  transfers between devices with their start and end apart: 28 -> 28, of which waited for: 8 -> 9; matrix products, arithmetic and copies ran while one was open for 3% -> 3% of each run, Pallas kernels for 40% -> 43%
where the time goes in v7:
time: 107 us
  Pallas kernels  47.3 us (44%)
  starting transfers between devices  35.2 us (33%)
  waiting for transfers between devices  19.8 us (19%)
  other arithmetic  2.58 us (2%)
    ppermute x21, starting transfers between devices, _xor(): return lax.ppermute(x, 'dp', [(i, i ^ k) for i in range(n)])  30.6 us
    ppermute x21, waiting for transfers between devices, _xor(): return lax.ppermute(x, 'dp', [(i, i ^ k) for i in range(n)])  17.6 us
    pallas_call x3, Pallas kernels, token_grads(): _call(functools.partial(tokens_kernel, z, first, so_far is None), 'token_...  12.1 us
    pallas_call x1, Pallas kernels, on_device(): _call(functools.partial(other_kernel, z), 'base_other', (1,), [pl.BlockSp...  6.63 us
    pallas_call x1, Pallas kernels, on_device(): _call(through_kernel, 'through', (1,), [VMEM] * 2, VMEM, _shape((rows, ha...  4.85 us
    pallas_call x1, Pallas kernels, on_device(): _call(functools.partial(own_kernel, z), 'base_own', (1,), [VMEM] * 5, [VM...  4.77 us
    pallas_call x3, Pallas kernels, dense(): _call(functools.partial(dense_kernel, z), 'dense', (1,), [VMEM] * NEAR, [...  3.95 us
    pallas_call x2, Pallas kernels, pack(): _call(functools.partial(pack_kernel, z, NEAR, start), 'pack_down', (1,),...  3.94 us
  transfers between devices with their start and end apart: 28, of which 9 were waited for; matrix products, arithmetic and copies ran while one was open for 3% of the time, Pallas kernels for 43%

profile of v7, /device:TPU:0, one launch (start us, length us, event | category | flops | bytes accessed | tf_op | source)
XLA Modules:
  0.0 106.8 jit_solution(4933527098919904043)
XLA Ops:
  0.6 4.1 %collective-permute-start = (bf16[4,16,512]{2,1,0:T(8,128)(2,1)}, bf16[4,16,512]{2,1,0:T(8,128)(2,1)S(1)}, u32[]{:S(2)}, u32[]{:S(2)}) collective-permute-start(bf16[4,16,512]{2,1,0:T(8,128)(2,1)} %param.11), channel_id=1, source_target_pairs={{0,8},{2,10},{4,12},{6,14},{8,0},{10,2},{12,4},{14,6},{1,9},{3,11}... | collective-permute-start | bytes 196616 | tf_op jit(solution)/shard_map/ppermute | solution.py:36
  5.7 1.6 %collective-permute-start.2 = (bf16[4,16,1024]{2,1,0:T(8,128)(2,1)S(1)}, bf16[4,16,1024]{2,1,0:T(8,128)(2,1)S(1)}, u32[]{:S(2)}, u32[]{:S(2)}) collective-permute-start(bf16[4,16,1024]{2,1,0:T(8,128)(2,1)S(1)} %get-tuple-element.117), channel_id=1, source_target_pairs={{0,2},{2,0},{4,6},{6,4},{8,10},{10,8},{12,14},{14,12},{1,3},{3,1},... | collective-permute-start | bytes 393224 | tf_op jit(solution)/shard_map/ppermute | solution.py:36
  9.8 1.4 %collective-permute-start.4 = (bf16[144,512]{1,0:T(8,128)(2,1)S(1)}, bf16[144,512]{1,0:T(8,128)(2,1)S(1)}, u32[]{:S(2)}, u32[]{:S(2)}) collective-permute-start(bf16[144,512]{1,0:T(8,128)(2,1)S(1)} %pad_maximum_fusion.1.refs_0_), channel_id=1, source_target_pairs={{0,2},{2,0},{4,6},{6,4},{8,10},{10,8},{12,14},{14,12},{1,3},{3,1},... | collective-permute-start | bytes 442376 | tf_op jit(solution)/shard_map/ppermute | solution.py:36
  12.0 1.4 %collective-permute-start.1 = (bf16[144,512]{1,0:T(8,128)(2,1)S(1)}, bf16[144,512]{1,0:T(8,128)(2,1)S(1)}, u32[]{:S(2)}, u32[]{:S(2)}) collective-permute-start(bf16[144,512]{1,0:T(8,128)(2,1)S(1)} %pad_maximum_fusion.1.refs_0_), channel_id=1, source_target_pairs={{0,6},{2,4},{4,2},{6,0},{8,14},{10,12},{12,10},{14,8},{1,7},{3,5},... | collective-permute-start | bytes 442376 | tf_op jit(solution)/shard_map/ppermute | solution.py:36
  13.4 1.7 %collective-permute-start.5 = (bf16[8,16,1024]{2,1,0:T(8,128)(2,1)S(1)}, bf16[8,16,1024]{2,1,0:T(8,128)(2,1)S(1)}, u32[]{:S(2)}, u32[]{:S(2)}) collective-permute-start(bf16[8,16,1024]{2,1,0:T(8,128)(2,1)S(1)} %pad_maximum_fusion.own_ref), channel_id=1, source_target_pairs={{0,8},{2,10},{4,12},{6,14},{8,0},{10,2},{12,4},{14,6},{1,9},{3,11}... | collective-permute-start | bytes 786440 | tf_op jit(solution)/shard_map/ppermute | solution.py:36
  15.1 6.6 %base_other.1 = bf16[896,512]{1,0:T(8,128)(2,1)S(1)} custom-call(s32[16,128]{1,0:T(8,128)S(1)} %select_select_fusion.1.place, bf16[896,4096]{1,0:T(8,128)(2,1)} %x_ref.7, bf16[4096,1024]{1,0:T(8,128)(2,1)} %w_ref.7), custom_call_target="tpu_custom_call" | custom-call | flops 1 | bytes 1 | tf_op jit(solution)/shard_map/base_other/pallas_call | solution.py:368
  24.3 2.4 %collective-permute-done.5.far_ref = bf16[8,16,1024]{2,1,0:T(8,128)(2,1)S(1)} collective-permute-done((bf16[8,16,1024]{2,1,0:T(8,128)(2,1)S(1)}, bf16[8,16,1024]{2,1,0:T(8,128)(2,1)S(1)}, u32[]{:S(2)}, u32[]{:S(2)}) %collective-permute-start.5) | collective-permute-done | bytes 262176 | tf_op jit(solution)/shard_map/ppermute | solution.py:36
  28.8 1.5 %collective-permute-start.11 = (bf16[8,16,1024]{2,1,0:T(8,128)(2,1)S(1)}, bf16[8,16,1024]{2,1,0:T(8,128)(2,1)S(1)}, u32[]{:S(2)}, u32[]{:S(2)}) collective-permute-start(bf16[8,16,1024]{2,1,0:T(8,128)(2,1)S(1)} %collective-permute-done.5.far_ref), channel_id=1, source_target_pairs={{0,4},{2,6},{4,0},{6,2},{8,12},{10,14},{12,8},{14,10},{1,5},{3,7},... | collective-permute-start | bytes 786440 | tf_op jit(solution)/shard_map/ppermute | solution.py:36
  30.3 2.0 %pack_down.2 = (bf16[64,2048]{1,0:T(8,128)(2,1)S(1)}, bf16[64,2048]{1,0:T(8,128)(2,1)S(1)}, bf16[64,2048]{1,0:T(8,128)(2,1)S(1)}, bf16[64,2048]{1,0:T(8,128)(2,1)S(1)}) custom-call(s32[16,128]{1,0:T(8,128)S(1)} %select_select_fusion.info, f32[16,896]{1,0:T(8,128)S(1)} %get-tuple-element.66.mine_ref, f32[16,896]{1,0:T(8,128)S(1)} %collective-permute-done.8.other_ref, ...), custom_call_target="tpu_custom_call" | custom-call | flops 1 | bytes 1 | tf_op jit(solution)/shard_map/pack_down/pallas_call | solution.py:405
  32.9 1.5 %collective-permute-start.12 = (bf16[64,2048]{1,0:T(8,128)(2,1)S(1)}, bf16[64,2048]{1,0:T(8,128)(2,1)S(1)}, u32[]{:S(2)}, u32[]{:S(2)}) collective-permute-start(bf16[64,2048]{1,0:T(8,128)(2,1)S(1)} %get-tuple-element.78), channel_id=1, source_target_pairs={{0,2},{2,0},{4,6},{6,4},{8,10},{10,8},{12,14},{14,12},{1,3},{3,1},... | collective-permute-start | bytes 786440 | tf_op jit(solution)/shard_map/ppermute | solution.py:36
  34.5 1.4 %collective-permute-start.14 = (bf16[64,2048]{1,0:T(8,128)(2,1)S(1)}, bf16[64,2048]{1,0:T(8,128)(2,1)S(1)}, u32[]{:S(2)}, u32[]{:S(2)}) collective-permute-start(bf16[64,2048]{1,0:T(8,128)(2,1)S(1)} %get-tuple-element.80), channel_id=1, source_target_pairs={{0,6},{2,4},{4,2},{6,0},{8,14},{10,12},{12,10},{14,8},{1,7},{3,5},... | collective-permute-start | bytes 786440 | tf_op jit(solution)/shard_map/ppermute | solution.py:36
  35.9 1.6 %collective-permute-done.10.near_ref = bf16[8,16,1024]{2,1,0:T(8,128)(2,1)S(1)} collective-permute-done((bf16[8,16,1024]{2,1,0:T(8,128)(2,1)S(1)}, bf16[8,16,1024]{2,1,0:T(8,128)(2,1)S(1)}, u32[]{:S(2)}, u32[]{:S(2)}) %collective-permute-start.10) | collective-permute-done | bytes 262176 | tf_op jit(solution)/shard_map/ppermute | solution.py:36
  37.4 1.5 %collective-permute-start.9 = (s32[16,128]{1,0:T(8,128)S(1)}, s32[16,128]{1,0:T(8,128)S(1)}, u32[]{:S(2)}, u32[]{:S(2)}) collective-permute-start(s32[16,128]{1,0:T(8,128)S(1)} %select_select_fusion.info), channel_id=1, source_target_pairs={{0,16},{16,0},{1,17},{17,1},{2,18},{18,2},{3,19},{19,3},{4,20},{20... | collective-permute-start | bytes 24584 | tf_op jit(solution)/shard_map/ppermute | solution.py:32
  38.9 2.2 %collective-permute-done.9.info_x = s32[16,128]{1,0:T(8,128)S(1)} collective-permute-done((s32[16,128]{1,0:T(8,128)S(1)}, s32[16,128]{1,0:T(8,128)S(1)}, u32[]{:S(2)}, u32[]{:S(2)}) %collective-permute-start.9) | collective-permute-done | bytes 8224 | tf_op jit(solution)/shard_map/ppermute | solution.py:32
  41.1 2.0 %collective-permute-done.11.farther_ref = bf16[8,16,1024]{2,1,0:T(8,128)(2,1)S(1)} collective-permute-done((bf16[8,16,1024]{2,1,0:T(8,128)(2,1)S(1)}, bf16[8,16,1024]{2,1,0:T(8,128)(2,1)S(1)}, u32[]{:S(2)}, u32[]{:S(2)}) %collective-permute-start.11) | collective-permute-done | bytes 262176 | tf_op jit(solution)/shard_map/ppermute | solution.py:36
  44.1 4.6 %collective-permute-done.13.refs_2_ = bf16[64,2048]{1,0:T(8,128)(2,1)S(1)} collective-permute-done((bf16[64,2048]{1,0:T(8,128)(2,1)S(1)}, bf16[64,2048]{1,0:T(8,128)(2,1)S(1)}, u32[]{:S(2)}, u32[]{:S(2)}) %collective-permute-start.13) | collective-permute-done | bytes 262176 | tf_op jit(solution)/shard_map/ppermute | solution.py:36
  49.8 1.5 %collective-permute-start.16 = (bf16[112,1024]{1,0:T(8,128)(2,1)S(1)}, bf16[112,1024]{1,0:T(8,128)(2,1)S(1)}, u32[]{:S(2)}, u32[]{:S(2)}) collective-permute-start(bf16[112,1024]{1,0:T(8,128)(2,1)S(1)} %get-tuple-element.87), channel_id=1, source_target_pairs={{0,16},{16,0},{1,17},{17,1},{2,18},{18,2},{3,19},{19,3},{4,20},{20... | collective-permute-start | bytes 688136 | tf_op jit(solution)/shard_map/ppermute | solution.py:32
  52.2 2.0 %pack_down.3 = (bf16[64,2048]{1,0:T(8,128)(2,1)S(1)}, bf16[64,2048]{1,0:T(8,128)(2,1)S(1)}, bf16[64,2048]{1,0:T(8,128)(2,1)S(1)}, bf16[64,2048]{1,0:T(8,128)(2,1)S(1)}) custom-call(s32[16,128]{1,0:T(8,128)S(1)} %select_select_fusion.info, f32[16,896]{1,0:T(8,128)S(1)} %get-tuple-element.66.mine_ref, f32[16,896]{1,0:T(8,128)S(1)} %collective-permute-done.8.other_ref, ...), custom_call_target="tpu_custom_call" | custom-call | flops 1 | bytes 1 | tf_op jit(solution)/shard_map/pack_down/pallas_call | solution.py:405
  54.2 4.8 %base_own.1 = (f32[896,512]{1,0:T(8,128)S(1)}, bf16[896,1024]{1,0:T(8,128)(2,1)S(1)}) custom-call(s32[16,128]{1,0:T(8,128)S(1)} %select_select_fusion.info, bf16[896,4096]{1,0:T(8,128)(2,1)S(1)} %bitcast.22, bf16[4096,1024]{1,0:T(8,128)(2,1)S(1)} %bitcast.20, bf16[896,512]{1,0:T(8,128)(2,1)S(1)} %collective-permute-done.7.far_ref, ...), custom_call_target="tpu_custom_call" | custom-call | flops 1 | bytes 1 | tf_op jit(solution)/shard_map/base_own/pallas_call | solution.py:463
  61.0 2.8 %collective-permute-done.15.refs_1_ = bf16[112,1024]{1,0:T(8,128)(2,1)S(1)} collective-permute-done((bf16[112,1024]{1,0:T(8,128)(2,1)S(1)}, bf16[112,1024]{1,0:T(8,128)(2,1)S(1)}, u32[]{:S(2)}, u32[]{:S(2)}) %collective-permute-start.15) | collective-permute-done | bytes 229408 | tf_op jit(solution)/shard_map/ppermute | solution.py:36
  64.7 1.5 %collective-permute-start.21 = (bf16[64,2048]{1,0:T(8,128)(2,1)S(1)}, bf16[64,2048]{1,0:T(8,128)(2,1)S(1)}, u32[]{:S(2)}, u32[]{:S(2)}) collective-permute-start(bf16[64,2048]{1,0:T(8,128)(2,1)S(1)} %get-tuple-element.101), channel_id=1, source_target_pairs={{0,6},{2,4},{4,2},{6,0},{8,14},{10,12},{12,10},{14,8},{1,7},{3,5},... | collective-permute-start | bytes 786440 | tf_op jit(solution)/shard_map/ppermute | solution.py:36
  66.1 4.9 %through.1.g_ref.w_ref = f32[896,2048]{1,0:T(8,128)S(1)} custom-call(s32[16,128]{1,0:T(8,128)S(1)} %select_select_fusion.info, bf16[896,1024]{1,0:T(8,128)(2,1)S(1)} %get-tuple-element.83.g_ref, bf16[4096,1024]{1,0:T(8,128)(2,1)S(1)} %bitcast.20), custom_call_target="tpu_custom_call" | custom-call | flops 1 | bytes 1 | tf_op jit(solution)/shard_map/through/pallas_call | solution.py:477
  71.0 2.8 %shrink.1 = (bf16[112,4096]{1,0:T(8,128)(2,1)S(1)}, f32[16,896]{1,0:T(8,128)S(1)}) custom-call(s32[16,128]{1,0:T(8,128)S(1)} %select_select_fusion.info, bf16[896,4096]{1,0:T(8,128)(2,1)S(1)} %bitcast.22, bf16[112,1024]{1,0:T(8,128)(2,1)S(1)} %get-tuple-element.72.refs_0_, bf16[112,1024]{1,0:T(8,128)(2,1)S(1)} %collective-permute-done.15.refs_1_, ...), custom_call_target="tpu_custom_call" | custom-call | flops 1 | bytes 1 | tf_op jit(solution)/shard_map/shrink/pallas_call | solution.py:483
  73.9 3.4 %collective-permute-start.25 = (bf16[64,2048]{1,0:T(8,128)(2,1)S(1)}, bf16[64,2048]{1,0:T(8,128)(2,1)S(1)}, u32[]{:S(2)}, u32[]{:S(2)}) collective-permute-start(bf16[64,2048]{1,0:T(8,128)(2,1)S(1)} %get-tuple-element.81), channel_id=1, source_target_pairs={{0,8},{2,10},{4,12},{6,14},{8,0},{10,2},{12,4},{14,6},{1,9},{3,11}... | collective-permute-start | bytes 786440 | tf_op jit(solution)/shard_map/ppermute | solution.py:36
  77.4 3.3 %token_grads.3.refs_0_ = bf16[896,4096]{1,0:T(8,128)(2,1)} custom-call(s32[16,128]{1,0:T(8,128)S(1)} %select_select_fusion.info, f32[896,2048]{1,0:T(8,128)S(1)} %through.1.g_ref.w_ref, f32[896,2048]{1,0:T(8,128)S(1)} %through.1.g_ref.w_ref, f32[16,896]{1,0:T(8,128)S(1)} %get-tuple-element.66.mine_ref, f32[16,896]{1,0:T(8,128)S(1)} %collective-permute-done.8.other_ref, ...), custom_call_target="tpu_custom_call" | custom-call | flops 1 | bytes 1 | tf_op jit(solution)/shard_map/token_grads/pallas_call | solution.py:492
  84.8 2.0 %collective-permute-start.24 = (bf16[64,512]{1,0:T(8,128)(2,1)S(1)}, bf16[64,512]{1,0:T(8,128)(2,1)S(1)}, u32[]{:S(2)}, u32[]{:S(2)}) collective-permute-start(bf16[64,512]{1,0:T(8,128)(2,1)S(1)} %get-tuple-element.109), channel_id=1, source_target_pairs={{0,6},{2,4},{4,2},{6,0},{8,14},{10,12},{12,10},{14,8},{1,7},{3,5},... | collective-permute-start | bytes 196616 | tf_op jit(solution)/shard_map/ppermute | solution.py:36
  86.8 4.4 %token_grads.4.refs_0_ = bf16[896,4096]{1,0:T(8,128)(2,1)} custom-call(s32[16,128]{1,0:T(8,128)S(1)} %select_select_fusion.info, bf16[896,1024]{1,0:T(8,128)(2,1)S(1)} %get-tuple-element.83.g_ref, bf16[4096,1024]{1,0:T(8,128)(2,1)S(1)} %bitcast.20, f32[16,896]{1,0:T(8,128)S(1)} %get-tuple-element.66.mine_ref, ...), custom_call_target="tpu_custom_call", output_to_operand_aliasing={{}: (6, {})} | custom-call | flops 1 | bytes 1 | tf_op jit(solution)/shard_map/token_grads/pallas_call | solution.py:492
  91.2 2.0 %projected.1 = bf16[896,512]{1,0:T(8,128)(2,1)} custom-call(s32[16,128]{1,0:T(8,128)S(1)} %select_select_fusion.info, f32[896,512]{1,0:T(8,128)S(1)} %get-tuple-element.76.base_ref, f32[16,896]{1,0:T(8,128)S(1)} %get-tuple-element.89.mine_ref, f32[16,896]{1,0:T(8,128)S(1)} %collective-permute-done.18.other_ref, bf16[112,512]{1,0:T(8,128)(2,1)S(1)} %get-tuple-element.105.up_ref), custom_call_target="tpu_custom_call" | custom-call | flops 1 | bytes 1 | tf_op jit(solution)/shard_map/projected/pallas_call | solution.py:520
  94.5 2.9 %collective-permute-start.27 = (bf16[64,512]{1,0:T(8,128)(2,1)S(1)}, bf16[64,512]{1,0:T(8,128)(2,1)S(1)}, u32[]{:S(2)}, u32[]{:S(2)}) collective-permute-start(bf16[64,512]{1,0:T(8,128)(2,1)S(1)} %get-tuple-element.110), channel_id=1, source_target_pairs={{0,8},{2,10},{4,12},{6,14},{8,0},{10,2},{12,4},{14,6},{1,9},{3,11}... | collective-permute-start | bytes 196616 | tf_op jit(solution)/shard_map/ppermute | solution.py:36
  97.4 4.4 %token_grads.5 = bf16[896,4096]{1,0:T(8,128)(2,1)} custom-call(s32[16,128]{1,0:T(8,128)S(1)} %select_select_fusion.info, bf16[896,1024]{1,0:T(8,128)(2,1)S(1)} %get-tuple-element.83.g_ref, bf16[4096,1024]{1,0:T(8,128)(2,1)S(1)} %bitcast.20, f32[16,896]{1,0:T(8,128)S(1)} %get-tuple-element.66.mine_ref, ...), custom_call_target="tpu_custom_call", output_to_operand_aliasing={{}: (6, {})} | custom-call | flops 1 | bytes 1 | tf_op jit(solution)/shard_map/token_grads/pallas_call | solution.py:492
  101.8 2.0 %collective-permute-done.27.refs_1_ = bf16[64,512]{1,0:T(8,128)(2,1)S(1)} collective-permute-done((bf16[64,512]{1,0:T(8,128)(2,1)S(1)}, bf16[64,512]{1,0:T(8,128)(2,1)S(1)}, u32[]{:S(2)}, u32[]{:S(2)}) %collective-permute-start.27) | collective-permute-done | bytes 65568 | tf_op jit(solution)/shard_map/ppermute | solution.py:36
  105.1 1.7 %final.2 = f32[64,4096]{1,0:T(8,128)} custom-call(s32[16,128]{1,0:T(8,128)S(1)} %select_select_fusion.info, f32[64,2048]{1,0:T(8,128)S(1)} %get-tuple-element.113.refs_0_, bf16[64,2048]{1,0:T(8,128)(2,1)S(1)} %collective-permute-done.25.refs_1_, f32[64,2048]{1,0:T(8,128)S(1)} %get-tuple-element.114.refs_2_, bf16[64,2048]{1,0:T(8,128)(2,1)S(1)} %collective-permute-done.26.refs_3_), custom_call_target="tpu_custom_call" | custom-call | flops 1 | bytes 1 | tf_op jit(solution)/shard_map/final/pallas_call | solution.py:430
  (71 shorter events, 22.2 us)
Async XLA Ops:
  0.6 8.3 %collective-permute-start = (bf16[4,16,512]{2,1,0:T(8,128)(2,1)}, bf16[4,16,512]{2,1,0:T(8,128)(2,1)S(1)}, u32[]{:S(2)}, u32[]{:S(2)}) collective-permute-start(bf16[4,16,512]{2,1,0:T(8,128)(2,1)} %param.11), channel_id=1, source_target_pairs={{0,8},{2,10},{4,12},{6,14},{8,0},{10,2},{12,4},{14,6},{1,9},{3,11}... | collective-permute-start | bytes 196616 | tf_op jit(solution)/shard_map/ppermute | solution.py:36
  5.7 7.7 %collective-permute-start.2 = (bf16[4,16,1024]{2,1,0:T(8,128)(2,1)S(1)}, bf16[4,16,1024]{2,1,0:T(8,128)(2,1)S(1)}, u32[]{:S(2)}, u32[]{:S(2)}) collective-permute-start(bf16[4,16,1024]{2,1,0:T(8,128)(2,1)S(1)} %get-tuple-element.117), channel_id=1, source_target_pairs={{0,2},{2,0},{4,6},{6,4},{8,10},{10,8},{12,14},{14,12},{1,3},{3,1},... | collective-permute-start | bytes 393224 | tf_op jit(solution)/shard_map/ppermute | solution.py:36
  9.8 12.1 %collective-permute-start.4 = (bf16[144,512]{1,0:T(8,128)(2,1)S(1)}, bf16[144,512]{1,0:T(8,128)(2,1)S(1)}, u32[]{:S(2)}, u32[]{:S(2)}) collective-permute-start(bf16[144,512]{1,0:T(8,128)(2,1)S(1)} %pad_maximum_fusion.1.refs_0_), channel_id=1, source_target_pairs={{0,2},{2,0},{4,6},{6,4},{8,10},{10,8},{12,14},{14,12},{1,3},{3,1},... | collective-permute-start | bytes 442376 | tf_op jit(solution)/shard_map/ppermute | solution.py:36
  11.2 11.7 %collective-permute-start.3 = (bf16[144,512]{1,0:T(8,128)(2,1)S(1)}, bf16[144,512]{1,0:T(8,128)(2,1)S(1)}, u32[]{:S(2)}, u32[]{:S(2)}) collective-permute-start(bf16[144,512]{1,0:T(8,128)(2,1)S(1)} %pad_maximum_fusion.1.refs_0_), channel_id=1, source_target_pairs={{0,4},{2,6},{4,0},{6,2},{8,12},{10,14},{12,8},{14,10},{1,5},{3,7},... | collective-permute-start | bytes 442376 | tf_op jit(solution)/shard_map/ppermute | solution.py:36
  12.0 12.3 %collective-permute-start.1 = (bf16[144,512]{1,0:T(8,128)(2,1)S(1)}, bf16[144,512]{1,0:T(8,128)(2,1)S(1)}, u32[]{:S(2)}, u32[]{:S(2)}) collective-permute-start(bf16[144,512]{1,0:T(8,128)(2,1)S(1)} %pad_maximum_fusion.1.refs_0_), channel_id=1, source_target_pairs={{0,6},{2,4},{4,2},{6,0},{8,14},{10,12},{12,10},{14,8},{1,7},{3,5},... | collective-permute-start | bytes 442376 | tf_op jit(solution)/shard_map/ppermute | solution.py:36
  13.4 16.9 %slice-start.2 = ((s8[7340032]{0:T(1024)(128)(4,1)}), s8[4194304]{0:T(1024)(128)(4,1)S(1)}, s32[]{:S(2)}) async-start(s8[7340032]{0:T(1024)(128)(4,1)} %bitcast.21), calls=%async_computation.2 | async-start | bytes 8388608
  13.4 16.9 %slice-start.3 = ((s8[7340032]{0:T(1024)(128)(4,1)}), s8[3145728]{0:T(1024)(128)(4,1)S(1)}, s32[]{:S(2)}) async-start(s8[7340032]{0:T(1024)(128)(4,1)} %bitcast.21), calls=%async_computation.3 | async-start | bytes 6291456
  13.4 13.3 %collective-permute-start.5 = (bf16[8,16,1024]{2,1,0:T(8,128)(2,1)S(1)}, bf16[8,16,1024]{2,1,0:T(8,128)(2,1)S(1)}, u32[]{:S(2)}, u32[]{:S(2)}) collective-permute-start(bf16[8,16,1024]{2,1,0:T(8,128)(2,1)S(1)} %pad_maximum_fusion.own_ref), channel_id=1, source_target_pairs={{0,8},{2,10},{4,12},{6,14},{8,0},{10,2},{12,4},{14,6},{1,9},{3,11}... | collective-permute-start | bytes 786440 | tf_op jit(solution)/shard_map/ppermute | solution.py:36
  21.8 8.5 %collective-permute-start.7 = (bf16[896,512]{1,0:T(8,128)(2,1)S(1)}, bf16[896,512]{1,0:T(8,128)(2,1)S(1)}, u32[]{:S(2)}, u32[]{:S(2)}) collective-permute-start(bf16[896,512]{1,0:T(8,128)(2,1)S(1)} %base_other.1), channel_id=1, source_target_pairs={{0,1},{1,0},{2,3},{3,2},{4,5},{5,4},{6,7},{7,6},{8,9},{9,8},{10,11... | collective-permute-start | bytes 2752520 | tf_op jit(solution)/shard_map/ppermute | solution.py:32
  27.7 26.4 %slice-start = ((s8[8388608]{0:T(1024)(128)(4,1)}), s8[4194304]{0:T(1024)(128)(4,1)S(1)}, s32[]{:S(2)}) async-start(s8[8388608]{0:T(1024)(128)(4,1)} %bitcast.19), calls=%async_computation | async-start | bytes 8388608
  27.7 2.6 %collective-permute-start.6 = (bf16[896,512]{1,0:T(8,128)(2,1)S(1)}, bf16[896,512]{1,0:T(8,128)(2,1)S(1)}, u32[]{:S(2)}, u32[]{:S(2)}) collective-permute-start(bf16[896,512]{1,0:T(8,128)(2,1)S(1)} %copy-done), channel_id=1, source_target_pairs={{0,1},{1,0},{2,3},{3,2},{4,5},{5,4},{6,7},{7,6},{8,9},{9,8},{10,11... | collective-permute-start | bytes 2752520 | tf_op jit(solution)/shard_map/ppermute | solution.py:32
  27.7 2.6 %collective-permute-start.8 = (f32[16,896]{1,0:T(8,128)S(1)}, f32[16,896]{1,0:T(8,128)S(1)}, u32[]{:S(2)}, u32[]{:S(2)}) collective-permute-start(f32[16,896]{1,0:T(8,128)S(1)} %get-tuple-element.66.mine_ref), channel_id=1, source_target_pairs={{0,1},{1,0},{2,3},{3,2},{4,5},{5,4},{6,7},{7,6},{8,9},{9,8},{10,11... | collective-permute-start | bytes 172040 | tf_op jit(solution)/shard_map/ppermute | solution.py:32
  28.3 9.2 %collective-permute-start.10 = (bf16[8,16,1024]{2,1,0:T(8,128)(2,1)S(1)}, bf16[8,16,1024]{2,1,0:T(8,128)(2,1)S(1)}, u32[]{:S(2)}, u32[]{:S(2)}) collective-permute-start(bf16[8,16,1024]{2,1,0:T(8,128)(2,1)S(1)} %pad_maximum_fusion.own_ref), channel_id=1, source_target_pairs={{0,4},{2,6},{4,0},{6,2},{8,12},{10,14},{12,8},{14,10},{1,5},{3,7},... | collective-permute-start | bytes 786440 | tf_op jit(solution)/shard_map/ppermute | solution.py:36
  28.8 14.2 %collective-permute-start.11 = (bf16[8,16,1024]{2,1,0:T(8,128)(2,1)S(1)}, bf16[8,16,1024]{2,1,0:T(8,128)(2,1)S(1)}, u32[]{:S(2)}, u32[]{:S(2)}) collective-permute-start(bf16[8,16,1024]{2,1,0:T(8,128)(2,1)S(1)} %collective-permute-done.5.far_ref), channel_id=1, source_target_pairs={{0,4},{2,6},{4,0},{6,2},{8,12},{10,14},{12,8},{14,10},{1,5},{3,7},... | collective-permute-start | bytes 786440 | tf_op jit(solution)/shard_map/ppermute | solution.py:36
  32.3 16.4 %collective-permute-start.13 = (bf16[64,2048]{1,0:T(8,128)(2,1)S(1)}, bf16[64,2048]{1,0:T(8,128)(2,1)S(1)}, u32[]{:S(2)}, u32[]{:S(2)}) collective-permute-start(bf16[64,2048]{1,0:T(8,128)(2,1)S(1)} %get-tuple-element.79), channel_id=1, source_target_pairs={{0,4},{2,6},{4,0},{6,2},{8,12},{10,14},{12,8},{14,10},{1,5},{3,7},... | collective-permute-start | bytes 786440 | tf_op jit(solution)/shard_map/ppermute | solution.py:36
  32.9 26.0 %collective-permute-start.12 = (bf16[64,2048]{1,0:T(8,128)(2,1)S(1)}, bf16[64,2048]{1,0:T(8,128)(2,1)S(1)}, u32[]{:S(2)}, u32[]{:S(2)}) collective-permute-start(bf16[64,2048]{1,0:T(8,128)(2,1)S(1)} %get-tuple-element.78), channel_id=1, source_target_pairs={{0,2},{2,0},{4,6},{6,4},{8,10},{10,8},{12,14},{14,12},{1,3},{3,1},... | collective-permute-start | bytes 786440 | tf_op jit(solution)/shard_map/ppermute | solution.py:36
  34.5 24.5 %collective-permute-start.14 = (bf16[64,2048]{1,0:T(8,128)(2,1)S(1)}, bf16[64,2048]{1,0:T(8,128)(2,1)S(1)}, u32[]{:S(2)}, u32[]{:S(2)}) collective-permute-start(bf16[64,2048]{1,0:T(8,128)(2,1)S(1)} %get-tuple-element.80), channel_id=1, source_target_pairs={{0,6},{2,4},{4,2},{6,0},{8,14},{10,12},{12,10},{14,8},{1,7},{3,5},... | collective-permute-start | bytes 786440 | tf_op jit(solution)/shard_map/ppermute | solution.py:36
  37.4 3.7 %collective-permute-start.9 = (s32[16,128]{1,0:T(8,128)S(1)}, s32[16,128]{1,0:T(8,128)S(1)}, u32[]{:S(2)}, u32[]{:S(2)}) collective-permute-start(s32[16,128]{1,0:T(8,128)S(1)} %select_select_fusion.info), channel_id=1, source_target_pairs={{0,16},{16,0},{1,17},{17,1},{2,18},{18,2},{3,19},{19,3},{4,20},{20... | collective-permute-start | bytes 24584 | tf_op jit(solution)/shard_map/ppermute | solution.py:32
  38.9 15.2 %slice-start.1 = ((s8[8388608]{0:T(1024)(128)(4,1)}), s8[4194304]{0:T(1024)(128)(4,1)S(1)}, s32[]{:S(2)}) async-start(s8[8388608]{0:T(1024)(128)(4,1)} %bitcast.19), calls=%async_computation.1 | async-start | bytes 8388608
  48.7 15.1 %collective-permute-start.15 = (bf16[112,1024]{1,0:T(8,128)(2,1)S(1)}, bf16[112,1024]{1,0:T(8,128)(2,1)S(1)}, u32[]{:S(2)}, u32[]{:S(2)}) collective-permute-start(bf16[112,1024]{1,0:T(8,128)(2,1)S(1)} %get-tuple-element.86), channel_id=1, source_target_pairs={{0,2},{2,0},{4,6},{6,4},{8,10},{10,8},{12,14},{14,12},{1,3},{3,1},... | collective-permute-start | bytes 688136 | tf_op jit(solution)/shard_map/ppermute | solution.py:36
  49.8 21.2 %collective-permute-start.16 = (bf16[112,1024]{1,0:T(8,128)(2,1)S(1)}, bf16[112,1024]{1,0:T(8,128)(2,1)S(1)}, u32[]{:S(2)}, u32[]{:S(2)}) collective-permute-start(bf16[112,1024]{1,0:T(8,128)(2,1)S(1)} %get-tuple-element.87), channel_id=1, source_target_pairs={{0,16},{16,0},{1,17},{17,1},{2,18},{18,2},{3,19},{19,3},{4,20},{20... | collective-permute-start | bytes 688136 | tf_op jit(solution)/shard_map/ppermute | solution.py:32
  51.3 19.7 %collective-permute-start.17 = (bf16[112,1024]{1,0:T(8,128)(2,1)S(1)}, bf16[112,1024]{1,0:T(8,128)(2,1)S(1)}, u32[]{:S(2)}, u32[]{:S(2)}) collective-permute-start(bf16[112,1024]{1,0:T(8,128)(2,1)S(1)} %get-tuple-element.88), channel_id=1, source_target_pairs={{0,18},{2,16},{4,22},{6,20},{8,26},{10,24},{12,30},{14,28},{16,2},... | collective-permute-start | bytes 688136 | tf_op jit(solution)/shard_map/ppermute | solution.py:449
  60.4 21.4 %collective-permute-start.20 = (bf16[64,2048]{1,0:T(8,128)(2,1)S(1)}, bf16[64,2048]{1,0:T(8,128)(2,1)S(1)}, u32[]{:S(2)}, u32[]{:S(2)}) collective-permute-start(bf16[64,2048]{1,0:T(8,128)(2,1)S(1)} %get-tuple-element.99), channel_id=1, source_target_pairs={{0,4},{2,6},{4,0},{6,2},{8,12},{10,14},{12,8},{14,10},{1,5},{3,7},... | collective-permute-start | bytes 786440 | tf_op jit(solution)/shard_map/ppermute | solution.py:36
  63.8 18.0 %collective-permute-start.19 = (bf16[64,2048]{1,0:T(8,128)(2,1)S(1)}, bf16[64,2048]{1,0:T(8,128)(2,1)S(1)}, u32[]{:S(2)}, u32[]{:S(2)}) collective-permute-start(bf16[64,2048]{1,0:T(8,128)(2,1)S(1)} %get-tuple-element.97), channel_id=1, source_target_pairs={{0,2},{2,0},{4,6},{6,4},{8,10},{10,8},{12,14},{14,12},{1,3},{3,1},... | collective-permute-start | bytes 786440 | tf_op jit(solution)/shard_map/ppermute | solution.py:36
  64.7 17.1 %collective-permute-start.21 = (bf16[64,2048]{1,0:T(8,128)(2,1)S(1)}, bf16[64,2048]{1,0:T(8,128)(2,1)S(1)}, u32[]{:S(2)}, u32[]{:S(2)}) collective-permute-start(bf16[64,2048]{1,0:T(8,128)(2,1)S(1)} %get-tuple-element.101), channel_id=1, source_target_pairs={{0,6},{2,4},{4,2},{6,0},{8,14},{10,12},{12,10},{14,8},{1,7},{3,5},... | collective-permute-start | bytes 786440 | tf_op jit(solution)/shard_map/ppermute | solution.py:36
  73.8 6.8 %collective-permute-start.18 = (f32[16,896]{1,0:T(8,128)S(1)}, f32[16,896]{1,0:T(8,128)S(1)}, u32[]{:S(2)}, u32[]{:S(2)}) collective-permute-start(f32[16,896]{1,0:T(8,128)S(1)} %get-tuple-element.89.mine_ref), channel_id=1, source_target_pairs={{0,1},{1,0},{2,3},{3,2},{4,5},{5,4},{6,7},{7,6},{8,9},{9,8},{10,11... | collective-permute-start | bytes 172040 | tf_op jit(solution)/shard_map/ppermute | solution.py:32
  73.9 31.2 %collective-permute-start.25 = (bf16[64,2048]{1,0:T(8,128)(2,1)S(1)}, bf16[64,2048]{1,0:T(8,128)(2,1)S(1)}, u32[]{:S(2)}, u32[]{:S(2)}) collective-permute-start(bf16[64,2048]{1,0:T(8,128)(2,1)S(1)} %get-tuple-element.81), channel_id=1, source_target_pairs={{0,8},{2,10},{4,12},{6,14},{8,0},{10,2},{12,4},{14,6},{1,9},{3,11}... | collective-permute-start | bytes 786440 | tf_op jit(solution)/shard_map/ppermute | solution.py:36
  83.2 21.9 %collective-permute-start.26 = (bf16[64,2048]{1,0:T(8,128)(2,1)S(1)}, bf16[64,2048]{1,0:T(8,128)(2,1)S(1)}, u32[]{:S(2)}, u32[]{:S(2)}) collective-permute-start(bf16[64,2048]{1,0:T(8,128)(2,1)S(1)} %get-tuple-element.102), channel_id=1, source_target_pairs={{0,8},{2,10},{4,12},{6,14},{8,0},{10,2},{12,4},{14,6},{1,9},{3,11}... | collective-permute-start | bytes 786440 | tf_op jit(solution)/shard_map/ppermute | solution.py:36
  83.3 10.0 %collective-permute-start.22 = (bf16[64,512]{1,0:T(8,128)(2,1)S(1)}, bf16[64,512]{1,0:T(8,128)(2,1)S(1)}, u32[]{:S(2)}, u32[]{:S(2)}) collective-permute-start(bf16[64,512]{1,0:T(8,128)(2,1)S(1)} %get-tuple-element.107), channel_id=1, source_target_pairs={{0,2},{2,0},{4,6},{6,4},{8,10},{10,8},{12,14},{14,12},{1,3},{3,1},... | collective-permute-start | bytes 196616 | tf_op jit(solution)/shard_map/ppermute | solution.py:36
  83.9 9.4 %collective-permute-start.23 = (bf16[64,512]{1,0:T(8,128)(2,1)S(1)}, bf16[64,512]{1,0:T(8,128)(2,1)S(1)}, u32[]{:S(2)}, u32[]{:S(2)}) collective-permute-start(bf16[64,512]{1,0:T(8,128)(2,1)S(1)} %get-tuple-element.108), channel_id=1, source_target_pairs={{0,4},{2,6},{4,0},{6,2},{8,12},{10,14},{12,8},{14,10},{1,5},{3,7},... | collective-permute-start | bytes 196616 | tf_op jit(solution)/shard_map/ppermute | solution.py:36
  84.8 8.4 %collective-permute-start.24 = (bf16[64,512]{1,0:T(8,128)(2,1)S(1)}, bf16[64,512]{1,0:T(8,128)(2,1)S(1)}, u32[]{:S(2)}, u32[]{:S(2)}) collective-permute-start(bf16[64,512]{1,0:T(8,128)(2,1)S(1)} %get-tuple-element.109), channel_id=1, source_target_pairs={{0,6},{2,4},{4,2},{6,0},{8,14},{10,12},{12,10},{14,8},{1,7},{3,5},... | collective-permute-start | bytes 196616 | tf_op jit(solution)/shard_map/ppermute | solution.py:36
  94.5 9.3 %collective-permute-start.27 = (bf16[64,512]{1,0:T(8,128)(2,1)S(1)}, bf16[64,512]{1,0:T(8,128)(2,1)S(1)}, u32[]{:S(2)}, u32[]{:S(2)}) collective-permute-start(bf16[64,512]{1,0:T(8,128)(2,1)S(1)} %get-tuple-element.110), channel_id=1, source_target_pairs={{0,8},{2,10},{4,12},{6,14},{8,0},{10,2},{12,4},{14,6},{1,9},{3,11}... | collective-permute-start | bytes 196616 | tf_op jit(solution)/shard_map/ppermute | solution.py:36
  (1 other events, 13.3 us)

commit v8 on v7

--- a/solution.py
+++ b/solution.py
@@ -10,8 +10,8 @@
 TENANT_BLOCK = 128
 CAP = 2
 NEAR = 4
-VMEM_LIMIT = 16 * 1024 * 1024
-BIG_VMEM = 52 * 1024 * 1024
+VMEM_LIMIT = 9 * 1024 * 1024
+BIG_VMEM = 36 * 1024 * 1024
 LANES = 128
 
 adapter_scale = 2.0
@@ -125,34 +125,29 @@
     return jnp.where(row < valid, x, jnp.zeros((), x.dtype))
 
 
-def other_kernel(z, place, x_hbm, w_hbm, out_ref, x_buf, w_buf, x_sem, w_sem):
-    far = pl.ds(pl.multiple_of((1 - place[z.core]) * z.cols, z.cols), z.cols)
+def base_kernel(
+    z, info, x_hbm, w_hbm, g_ref, h_ref, far_ref, own_ref, full_ref, x_ref, w_ref, x_sem, w_sem
+):
+    own = pl.ds(pl.multiple_of(info[z.core] * z.cols, z.cols), z.cols)
+    far = pl.ds(pl.multiple_of((1 - info[z.core]) * z.cols, z.cols), z.cols)
     unit = z.width // 8
     copies = []
     for i, (first, last) in enumerate(((0, 1), (1, 2), (2, 4), (4, 6), (6, 8))):
         cut = pl.ds(first * unit, (last - first) * unit)
-        x = pltpu.make_async_copy(x_hbm.at[:, cut], x_buf.at[:, cut], x_sem.at[i])
-        w = pltpu.make_async_copy(w_hbm.at[cut, far], w_buf.at[cut], w_sem.at[i])
+        x = pltpu.make_async_copy(x_hbm.at[:, cut], x_ref.at[:, cut], x_sem.at[i])
+        w = pltpu.make_async_copy(w_hbm.at[cut], w_ref.at[cut], w_sem.at[i])
         x.start()
         w.start()
         copies.append((x, w, cut))
-    total = None
-    for x, w, cut in copies:
-        x.wait()
-        w.wait()
-        term = _dot(x_buf[:, cut], w_buf[cut, :], NN)
-        total = term if total is None else total + term
-    out_ref[...] = total.astype(bf16)
-
-
-def own_kernel(z, info, x_ref, w_ref, far_ref, g_ref, h_ref, out_ref, full_ref):
-    own = pl.ds(pl.multiple_of(info[z.core] * z.cols, z.cols), z.cols)
-    far = pl.ds(pl.multiple_of((1 - info[z.core]) * z.cols, z.cols), z.cols)
-    out_ref[...] = _dot(x_ref[...], w_ref[:, own], NN) + far_ref[...].astype(f32)
     for b in range(z.nb):
         cut = z.block(b)
         full_ref[cut, own] = _masked(g_ref[cut, :], z.valid(info, b))
         full_ref[cut, far] = _masked(h_ref[cut, :], z.valid(info, b))
+    for x, w, cut in copies:
+        x.wait()
+        w.wait()
+    far_ref[...] = _dot(x_ref[...], w_ref[:, far], NN).astype(bf16)
+    own_ref[...] = _dot(x_ref[...], w_ref[:, own], NN)
 
 
 def back_kernel(z, info, g_ref, *refs):
@@ -198,8 +193,7 @@
         outs[k][...] = res[k * each : (k + 1) * each]
 
 
-def dense_kernel(z, info, *refs):
-    got, near_ref, far_refs = refs[:NEAR], refs[NEAR], refs[NEAR + 1 :]
+def one_hot_sums(z, info, sums_ref):
     n = CAP * z.rank
     shape = (z.ten_dev * z.rank, n)
     row = lax.broadcasted_iota(i32, shape, 0)
@@ -209,7 +203,7 @@
     tables = [z.owner_and_order(info, k) for k in range(NEAR)]
     for j in range(z.n_far):
         holder = info[z.me] ^ (NEAR * j)
-        total = None
+        parts = []
         for k in range(NEAR):
             owners, orders = tables[k]
             local = []
@@ -220,29 +214,39 @@
                     found = jnp.where(hit, _rem(z.slot(info, k, b), z.ten_dev), found)
                 local.append(found)
             wanted = jnp.where(col < z.rank, local[0], local[1])
-            one_hot = jnp.where(same & (row_slot == wanted), 1.0, 0.0).astype(bf16)
-            term = _dot(one_hot, got[k][j * n : (j + 1) * n, :], NN)
-            total = term if total is None else total + term
+            parts.append(jnp.where(same & (row_slot == wanted), 1.0, 0.0))
+        sums_ref[j] = jnp.concatenate(parts, axis=1).astype(bf16)
+
+
+def dense_kernel(z, info, sums_ref, *refs):
+    got, near_ref, far_refs = refs[:NEAR], refs[NEAR], refs[NEAR + 1 :]
+    n = CAP * z.rank
+    for j in range(z.n_far):
+        stacked = jnp.concatenate([g[j * n : (j + 1) * n, :] for g in got], axis=0)
+        total = _dot(sums_ref[j], stacked, NN)
         if j == 0:
             near_ref[...] = total
         else:
             far_refs[j - 1][...] = total.astype(bf16)
 
 
-def final_kernel(n_parts, n_far, info, *refs):
-    out = refs[-1]
-    at = 0
-    for p in range(n_parts):
-        near, far = refs[p * n_far], refs[p * n_far + 1 : (p + 1) * n_far]
-        total = near[...]
-        for r in far:
-            total = total + r[...].astype(f32)
-        out[:, at : at + total.shape[1]] = total
-        at += total.shape[1]
-
-
-def choose_kernel(z, info, info_x, own_ref, near_ref, far_ref, farther_ref, *outs):
-    sources = (own_ref, near_ref, far_ref, farther_ref)
+def final_kernel(parts, n_far, info, *refs):
+    outs = refs[len(refs) - len(parts) :]
+    i = 0
+    for n, out in zip(parts, outs):
+        at = 0
+        for _ in range(n):
+            total = refs[i][...]
+            for r in refs[i + 1 : i + n_far]:
+                total = total + r[...].astype(f32)
+            out[:, at : at + total.shape[1]] = total
+            at += total.shape[1]
+            i += n_far
+
+
+def choose_kernel(z, info, info_x, own_ref, far_ref, pair_ref, *outs):
+    half = own_ref.shape[0]
+    sources = (own_ref, pair_ref.at[:half], far_ref, pair_ref.at[half:])
     wanted = ((info, 0), (info, 1), (info_x, 0), (info_x, 1))
     for (table, which), out in zip(wanted, outs):
         for b in range(z.nb):
@@ -272,7 +276,7 @@
         out_ref[:, z.block(b)] = total[z.block(b), :].T[z.ranks(b), :]
 
 
-def projected_kernel(z, info, base_ref, mine_ref, other_ref, up_ref, out_ref, spread):
+def projected_kernel(z, info, base_ref, far_ref, mine_ref, other_ref, up_ref, out_ref, spread):
     spread[...] = jnp.zeros_like(spread)
     for b in range(z.nb):
         cut = z.block(b)
@@ -280,20 +284,24 @@
     wide = _dot(spread[...], up_ref[...], TN)
     for b in range(z.nb):
         cut = z.block(b)
-        full = base_ref[cut, :] + adapter_scale * wide[cut]
+        full = base_ref[cut, :] + far_ref[cut, :].astype(f32) + adapter_scale * wide[cut]
         out_ref[cut, :] = _masked(full, z.valid(info, b)).astype(bf16)
 
 
-def through_kernel(info, g_ref, w_ref, out_ref):
-    half = out_ref.shape[1] // 2
-    for h in range(2):
-        cut = slice(h * half, (h + 1) * half)
-        out_ref[:, cut] = _dot(g_ref[...], w_ref[cut, :], NT)
-
-
-def tokens_kernel(z, first, ready, info, g_ref, w_ref, mine_ref, other_ref, d_ref, *refs):
-    out_ref, spread = refs[-2:]
+def through_kernel(z, first, info, g_ref, w_ref, out_ref, *sums):
+    step = out_ref.shape[1] // 4
+    for h in range(4):
+        cut = slice(h * step, (h + 1) * step)
+        rows = slice(first + h * step, first + (h + 1) * step)
+        out_ref[:, cut] = _dot(g_ref[...], w_ref[rows, :], NT)
+    for s in sums:
+        one_hot_sums(z, info, s)
+
+
+def tokens_kernel(z, info, low_ref, high_ref, mine_ref, other_ref, d_ref, out_ref, spread):
     step = pl.program_id(0)
+    wide = out_ref.shape[1]
+    per_half = low_ref.shape[1] // wide
 
     @pl.when(step == 0)
     def _():
@@ -303,10 +311,14 @@
             v = (mine_ref[:, cut] + other_ref[:, cut]) * adapter_scale
             spread[z.ranks(b), cut] = v.astype(bf16)
 
-    wide = out_ref.shape[1]
-    cut = pl.ds(pl.multiple_of((first + step) * wide, wide), wide)
-    through = g_ref[:, cut] if ready else _dot(g_ref[...], w_ref[cut, :], NT)
-    out_ref[...] = (through + _dot(spread[...], d_ref[:, cut], TN)).astype(bf16)
+    cut = pl.ds(pl.multiple_of(step * wide, wide), wide)
+    added = _dot(spread[...], d_ref[:, cut], TN)
+    for half, through in enumerate((low_ref, high_ref)):
+
+        @pl.when(step // per_half == half)
+        def _():
+            here = pl.ds(pl.multiple_of((step - half * per_half) * wide, wide), wide)
+            out_ref[...] = (through[:, here] + added).astype(bf16)
 
 
 def on_device(
@@ -336,6 +348,8 @@
     mine_q = group * 2 + me % 2 if shared else jnp.int32(0)
     quarter = width // n_parts
 
+    cotangent_other = _swap(out_cotangent, "tensor")
+
     down_t = jnp.swapaxes(adapter_down, 1, 2)
     if shared:
         to_y = lax.dynamic_slice_in_dim(down_t, (mine_q ^ 1) * quarter, quarter, axis=2)
@@ -365,16 +379,21 @@
     info = jnp.where(line == 6, spread_out(tenant_slot)[None, :], info)
     info = jnp.where(line == 0, own_tenants[None, :], info)
 
-    base_other = _call(
-        functools.partial(other_kernel, z), "base_other", (1,),
-        [pl.BlockSpec(memory_space=pl.ANY)] * 2,
-        _whole((rows, cols)), _shape((rows, cols), bf16),
+    base_other, base_own, g_full, x_in, w_in = _call(
+        functools.partial(base_kernel, z), "base", (1,),
+        [pl.BlockSpec(memory_space=pl.ANY)] * 2 + [VMEM] * 2,
+        [_whole((rows, cols))] + [VMEM] * 4,
         [
-            pltpu.VMEM((rows, width), bf16), pltpu.VMEM((width, cols), bf16),
-            pltpu.SemaphoreType.DMA((5,)), pltpu.SemaphoreType.DMA((5,)),
+            _shape((rows, cols), bf16), _shape((rows, cols), f32),
+            _shape((rows, 2 * cols), bf16), _shape(tokens.shape, bf16),
+            _shape(base_weight.shape, bf16),
         ],
+        [pltpu.SemaphoreType.DMA((5,)), pltpu.SemaphoreType.DMA((5,))],
         vmem=BIG_VMEM,
-    )(_tie(info, shard if shared else packet), tokens, base_weight)
+    )(
+        _tie(info, shard if shared else packet),
+        tokens, base_weight, out_cotangent, cotangent_other,
+    )
     base_arrived = _swap(base_other, "tensor")
     packets = [_tie(p, base_other) for p in packets]
 
@@ -382,8 +401,9 @@
         info = jnp.where(line == k, packets[k][-16, :LANES].astype(i32)[None, :], info)
 
     if shared:
+        shard_far = _tie(shard_far, base_other)
         info = _tie(info, shard_far)
-        farther = _xor(shard_far, n_dp, 2)
+        farther = _xor(jnp.concatenate([shard, shard_far], axis=0), n_dp, 2)
 
     part = (rank, rows)
     block_up, back_part = _call(
@@ -392,11 +412,10 @@
         [_shape((nb * rank, cols), bf16), _shape(part, f32)], [],
     )(info, out_cotangent, *packets)
     back_other = _swap(back_part, "tensor")
-    cotangent_other = _swap(_tie(out_cotangent, back_part), "tensor")
-    ready = [cotangent_other, base_arrived]
+    ready = [base_arrived]
     if shared:
-        shard_near = _xor(_tie(shard, base_other), n_dp, 2)
         info_x = _swap(info, "groups")
+        ready.append(info_x)
 
     packed_rows = n_dp * CAP * rank
     near_rows = packed_rows // NEAR
@@ -407,7 +426,7 @@
             [VMEM] * 3, [_whole((near_rows, wide))] * NEAR,
             [_shape((near_rows, wide), bf16)] * NEAR,
             [pltpu.VMEM((packed_rows, rows), bf16)],
-        )(info, back_part, back_other, tokens)
+        )(info, back_part, back_other, x_in)
 
     def to_near(sends):
         return [sends[0]] + [_xor(sends[k], n_dp, k) for k in range(1, NEAR)]
@@ -417,33 +436,34 @@
         out = (ten_dev * rank, wide)
         return _call(
             functools.partial(dense_kernel, z), "dense", (1,),
-            [VMEM] * NEAR, [VMEM] + [_whole(out)] * (n_far - 1),
+            [VMEM] * (1 + NEAR), [VMEM] + [_whole(out)] * (n_far - 1),
             [_shape(out, f32)] + [_shape(out, bf16)] * (n_far - 1), [],
-        )(info, *got)
+        )(info, sums, *got)
 
     def to_far(parts):
         return [parts[0]] + [_xor(parts[j], n_dp, NEAR * j) for j in range(1, n_far)]
 
-    def final(groups):
-        wide = sum(g[0].shape[1] for g in groups)
-        out = (ten_dev * rank, wide)
-        total = _call(
-            functools.partial(final_kernel, len(groups), n_far), "final", (1,),
-            [VMEM] * (len(groups) * n_far), _whole(out), _shape(out, f32), [],
-        )(_tie(info, grad_tokens), *[a for g in groups for a in g])
-        return total.reshape(ten_dev, rank, wide)
+    def through(info, first, wide, with_sums):
+        sums = _shape((n_far, ten_dev * rank, NEAR * CAP * rank), bf16)
+        return _call(
+            functools.partial(through_kernel, z, first), "through", (1,), [VMEM] * 2,
+            [VMEM] * (1 + with_sums), [_shape((rows, wide), f32)] + [sums] * with_sums, [],
+        )(info, g_full, w_in)
 
     half = width // 2
-    sends_a = pack(_tie(info, *ready), 0, half)
+    wide_a = width * 5 // 8
+    sends_a = pack(_tie(info, *ready), 0, wide_a)
     got_a = to_near(sends_a)
+
+    low, sums = through(_tie(info, sends_a[0]), 0, half, 1)
 
     if shared:
         block = (nb * rank, quarter)
         chosen = _call(
             functools.partial(choose_kernel, z), "choose", (1,),
-            [VMEM] * 4, [_whole(block)] * 4, [_shape(block, bf16)] * 4, [],
+            [VMEM] * 3, [_whole(block)] * 4, [_shape(block, bf16)] * 4, [],
             n_scalars=2,
-        )(_tie(info, sends_a[0]), info_x, shard, shard_near, shard_far, farther)
+        )(_tie(info, low), info_x, shard, shard_far, farther)
         got_y = _xor(_tie(chosen[1], got_a[2]), n_dp, 1)
         got_x = _swap(chosen[2], "groups")
         got_d = lax.ppermute(
@@ -456,17 +476,11 @@
         every = lax.all_gather(down_t, "dp", axis=0, tiled=True)
         slots = jnp.take(tenant_slot, block_tenant, axis=0)
         got_down = [jnp.take(every, slots, axis=0).reshape(nb * rank, width)]
-        after_choose = sends_a[0]
-
-    sends_b = pack(_tie(info, after_choose), half, half)
-
-    base_own, g_full = _call(
-        functools.partial(own_kernel, z), "base_own", (1,),
-        [VMEM] * 5, [VMEM, VMEM],
-        [_shape((rows, cols), f32), _shape((rows, 2 * cols), bf16)], [],
-    )(_tie(info, sends_b[0]), tokens, base_weight, base_arrived, out_cotangent, cotangent_other)
-
-    dense_a = dense(_tie(info, base_own), got_a)
+        after_choose = low
+
+    sends_b = pack(_tie(info, after_choose), wide_a, width - wide_a)
+
+    dense_a = dense(_tie(info, sends_b[0]), got_a)
     far_a = to_far(dense_a)
 
     gate = [dense_a[1]] + ([got_y] if shared else [])
@@ -474,9 +488,7 @@
         [_tie(b, *gate) if k in (1, 3) else _tie(b, dense_a[1]) for k, b in enumerate(sends_b)]
     )
 
-    through = _call(
-        through_kernel, "through", (1,), [VMEM] * 2, VMEM, _shape((rows, half), f32), [],
-    )(_tie(info, dense_a[1]), g_full, base_weight)
+    (high,) = through(_tie(info, dense_a[1]), half, width - half, 0)
 
     if shared:
         got_down = [chosen[0], got_y, got_x, got_d]
@@ -484,23 +496,15 @@
         functools.partial(shrink_kernel, z, n_parts), "shrink", (1,),
         [VMEM] * (1 + n_parts), [VMEM, _whole(part)],
         [_shape((nb * rank, width), bf16), _shape(part, f32)], [],
-    )(_tie(info, through), tokens, *got_down)
+    )(_tie(info, high), x_in, *got_down)
     shrink_other = _swap(shrink_part, "tensor")
 
-    def token_grads(info, start, wide, step, g, so_far):
-        first = start // step
-        return _call(
-            functools.partial(tokens_kernel, z, first, so_far is None), "token_grads", (wide // step,),
-            [VMEM] * 5 + ([] if so_far is None else [pl.BlockSpec(memory_space=pl.ANY)]),
-            pl.BlockSpec((rows, step), lambda i, *_: (0, first + i)),
-            _shape((rows, width), bf16), [pltpu.VMEM((nb * rank, rows), bf16)],
-            None if so_far is None else {6: 0},
-        )(
-            info, g, g if so_far is None else base_weight, back_part, back_other, block_down,
-            *([] if so_far is None else [so_far]),
-        )
-
-    grad_tokens = token_grads(_tie(info, shrink_part), 0, half, half // 2, through, None)
+    step = min(512, width // 8)
+    grad_tokens = _call(
+        functools.partial(tokens_kernel, z), "token_grads", (width // step,),
+        [VMEM] * 5, pl.BlockSpec((rows, step), lambda i, *_: (0, i)),
+        _shape((rows, width), bf16), [pltpu.VMEM((nb * rank, rows), bf16)],
+    )(_tie(info, shrink_part), low, high, back_part, back_other, block_down)
 
     up_sends = _call(
         functools.partial(pack_up_kernel, z, NEAR), "pack_up", (1,),
@@ -513,25 +517,24 @@
     dense_b = dense(_tie(info, up_sends[0]), got_b)
     far_b = to_far(dense_b)
 
-    rest = (width - half) // 2
-    grad_tokens = token_grads(
-        _tie(info, dense_b[1]), half, rest, rest // 2, g_full, grad_tokens
-    )
     projected = _call(
         functools.partial(projected_kernel, z), "projected", (1,),
-        [VMEM] * 4, _whole((rows, cols)), _shape((rows, cols), bf16),
+        [VMEM] * 5, _whole((rows, cols)), _shape((rows, cols), bf16),
         [pltpu.VMEM((nb * rank, rows), bf16)],
-    )(_tie(info, grad_tokens), base_own, shrink_part, shrink_other, block_up)
+    )(
+        _tie(info, dense_b[1]),
+        base_own, base_arrived, shrink_part, shrink_other, block_up,
+    )
     dense_u = dense(_tie(info, projected), got_u)
     far_u = to_far(dense_u)
-    grad_tokens = token_grads(
-        _tie(info, dense_u[1]), half + rest, rest, rest // 2, g_full, grad_tokens
-    )
-
-
-    grad_down = jnp.swapaxes(final([far_a, far_b]), 1, 2)
-    grad_up = final([far_u])
-    return projected, grad_tokens, grad_down, grad_up
+
+    outs = [(ten_dev * rank, width), (ten_dev * rank, cols)]
+    grad_down, grad_up = _call(
+        functools.partial(final_kernel, (2, 1), n_far), "final", (1,),
+        [VMEM] * (3 * n_far), [_whole(o) for o in outs], [_shape(o, f32) for o in outs], [],
+    )(info, *far_a, *far_b, *far_u)
+    grad_down = jnp.swapaxes(grad_down.reshape(ten_dev, rank, width), 1, 2)
+    return projected, grad_tokens, grad_down, grad_up.reshape(ten_dev, rank, cols)
 
 
 def solution(mesh):

time: 107 us -> 111 us (1.037)
  waiting for transfers between devices: 19.8 us -> 22.2 us
  local copies, waits for them, and re-layouts: 1.02 us -> 2.17 us
    ppermute x21 -> x20, waiting for transfers between devices: 17.6 us -> 20 us  [_xor(): return lax.ppermute(x, 'dp', [(i, i ^ k) for i in range(n)])]
    unnamed x10 -> x4, local copies, waits for them, and re-layouts: 0.03 us -> 1.18 us
    pallas_call x12 -> x9, Pallas kernels: 36.4 us -> 37 us  [the longest x1 14.1 us: on_device(): _call(functools.partial(base_kernel, z), 'base', (1,), [pl.BlockSpec(memo...]
    ppermute x21 -> x20, starting transfers between devices: 30.6 us -> 31 us  [_xor(): return lax.ppermute(x, 'dp', [(i, i ^ k) for i in range(n)])]
  transfers between devices with their start and end apart: 28 -> 27, of which waited for: 9 -> 8; matrix products, arithmetic and copies ran while one was open for 3% -> 3% of each run, Pallas kernels for 43% -> 42%
where the time goes in v8:
time: 111 us
  Pallas kernels  48 us (43%)
  starting transfers between devices  34.8 us (31%)
  waiting for transfers between devices  22.2 us (20%)
  other arithmetic  2.63 us (2%)
  local copies, waits for them, and re-layouts  2.17 us (2%)
    ppermute x20, starting transfers between devices, _xor(): return lax.ppermute(x, 'dp', [(i, i ^ k) for i in range(n)])  31 us
    ppermute x20, waiting for transfers between devices, _xor(): return lax.ppermute(x, 'dp', [(i, i ^ k) for i in range(n)])  20 us
    pallas_call x1, Pallas kernels, on_device(): _call(functools.partial(base_kernel, z), 'base', (1,), [pl.BlockSpec(memo...  14.1 us
    pallas_call x2, Pallas kernels, through(): _call(functools.partial(through_kernel, z, first), 'through', (1,), [VMEM...  9.59 us
    pallas_call x1, Pallas kernels, on_device(): _call(functools.partial(tokens_kernel, z), 'token_grads', (width // step,...  7.7 us
    pallas_call x2, Pallas kernels, pack(): _call(functools.partial(pack_kernel, z, NEAR, start), 'pack_down', (1,),...  3.96 us
    ppermute x6, starting transfers between devices, _swap(): return lax.ppermute(x, axis, [(0, 1), (1, 0)])  3.35 us
    pallas_call x1, Pallas kernels, on_device(): _call(functools.partial(shrink_kernel, z, n_parts), 'shrink', (1,), [VMEM...  2.81 us
  transfers between devices with their start and end apart: 27, of which 8 were waited for; matrix products, arithmetic and copies ran while one was open for 3% of the time, Pallas kernels for 42%

profile of v8, /device:TPU:0, one launch (start us, length us, event | category | flops | bytes accessed | tf_op | source)
XLA Modules:
  0.0 110.7 jit_solution(14746660309280241716)
XLA Ops:
  0.6 4.1 %collective-permute-start = (bf16[4,16,512]{2,1,0:T(8,128)(2,1)}, bf16[4,16,512]{2,1,0:T(8,128)(2,1)S(1)}, u32[]{:S(2)}, u32[]{:S(2)}) collective-permute-start(bf16[4,16,512]{2,1,0:T(8,128)(2,1)} %param.11), channel_id=1, source_target_pairs={{0,8},{2,10},{4,12},{6,14},{8,0},{10,2},{12,4},{14,6},{1,9},{3,11}... | collective-permute-start | bytes 196616 | tf_op jit(solution)/shard_map/ppermute | solution.py:36
  5.7 1.6 %collective-permute-start.2 = (bf16[4,16,1024]{2,1,0:T(8,128)(2,1)S(1)}, bf16[4,16,1024]{2,1,0:T(8,128)(2,1)S(1)}, u32[]{:S(2)}, u32[]{:S(2)}) collective-permute-start(bf16[4,16,1024]{2,1,0:T(8,128)(2,1)S(1)} %get-tuple-element.123), channel_id=1, source_target_pairs={{0,2},{2,0},{4,6},{6,4},{8,10},{10,8},{12,14},{14,12},{1,3},{3,1},... | collective-permute-start | bytes 393224 | tf_op jit(solution)/shard_map/ppermute | solution.py:36
  8.9 1.8 %collective-permute-done.2 = bf16[4,16,1024]{2,1,0:T(8,128)(2,1)S(1)} collective-permute-done((bf16[4,16,1024]{2,1,0:T(8,128)(2,1)S(1)}, bf16[4,16,1024]{2,1,0:T(8,128)(2,1)S(1)}, u32[]{:S(2)}, u32[]{:S(2)}) %collective-permute-start.2) | collective-permute-done | bytes 131104 | tf_op jit(solution)/shard_map/ppermute | solution.py:36
  12.0 1.6 %collective-permute-start.5 = (bf16[144,512]{1,0:T(8,128)(2,1)S(1)}, bf16[144,512]{1,0:T(8,128)(2,1)S(1)}, u32[]{:S(2)}, u32[]{:S(2)}) collective-permute-start(bf16[144,512]{1,0:T(8,128)(2,1)S(1)} %pad_maximum_fusion.2.refs_0_), channel_id=1, source_target_pairs={{0,2},{2,0},{4,6},{6,4},{8,10},{10,8},{12,14},{14,12},{1,3},{3,1},... | collective-permute-start | bytes 442376 | tf_op jit(solution)/shard_map/ppermute | solution.py:36
  13.6 1.6 %collective-permute-start.4 = (bf16[144,512]{1,0:T(8,128)(2,1)S(1)}, bf16[144,512]{1,0:T(8,128)(2,1)S(1)}, u32[]{:S(2)}, u32[]{:S(2)}) collective-permute-start(bf16[144,512]{1,0:T(8,128)(2,1)S(1)} %pad_maximum_fusion.2.refs_0_), channel_id=1, source_target_pairs={{0,4},{2,6},{4,0},{6,2},{8,12},{10,14},{12,8},{14,10},{1,5},{3,7},... | collective-permute-start | bytes 442376 | tf_op jit(solution)/shard_map/ppermute | solution.py:36
  15.6 1.2 %copy-done.1 = bf16[896,512]{1,0:T(8,128)(2,1)S(1)} copy-done((bf16[896,512]{1,0:T(8,128)(2,1)S(1)}, bf16[896,512]{1,0:T(8,128)(2,1)}, u32[]{:S(2)}) %copy-start.1) | copy-done | bytes 917528
  16.8 14.1 %base.1 = (bf16[896,512]{1,0:T(8,128)(2,1)S(1)}, f32[896,512]{1,0:T(8,128)S(1)}, bf16[896,1024]{1,0:T(8,128)(2,1)S(1)}, bf16[896,4096]{1,0:T(8,128)(2,1)S(1)}, bf16[4096,1024]{1,0:T(8,128)(2,1)}) custom-call(s32[16,128]{1,0:T(8,128)S(1)} %select_select_fusion.1.info, bf16[896,4096]{1,0:T(8,128)(2,1)} %x_hbm.1, bf16[4096,1024]{1,0:T(8,128)(2,1)} %w_hbm.1, ...), custom_call_target="tpu_custom_call" | custom-call | flops 1 | bytes 1 | tf_op jit(solution)/shard_map/base/pallas_call | solution.py:382
  31.1 1.7 %collective-permute-start.10 = (bf16[16,16,1024]{2,1,0:T(8,128)(2,1)S(1)}, bf16[16,16,1024]{2,1,0:T(8,128)(2,1)S(1)}, u32[]{:S(2)}, u32[]{:S(2)}) collective-permute-start(bf16[16,16,1024]{2,1,0:T(8,128)(2,1)S(1)} %pad_maximum_fusion), channel_id=1, source_target_pairs={{0,4},{2,6},{4,0},{6,2},{8,12},{10,14},{12,8},{14,10},{1,5},{3,7},... | collective-permute-start | bytes 1572872 | tf_op jit(solution)/shard_map/ppermute | solution.py:36
  34.1 1.5 %collective-permute-start.8 = (s32[16,128]{1,0:T(8,128)S(1)}, s32[16,128]{1,0:T(8,128)S(1)}, u32[]{:S(2)}, u32[]{:S(2)}) collective-permute-start(s32[16,128]{1,0:T(8,128)S(1)} %select_select_fusion.info), channel_id=1, source_target_pairs={{0,16},{16,0},{1,17},{17,1},{2,18},{18,2},{3,19},{19,3},{4,20},{20... | collective-permute-start | bytes 24584 | tf_op jit(solution)/shard_map/ppermute | solution.py:32
  35.6 2.2 %collective-permute-done.8.info_x = s32[16,128]{1,0:T(8,128)S(1)} collective-permute-done((s32[16,128]{1,0:T(8,128)S(1)}, s32[16,128]{1,0:T(8,128)S(1)}, u32[]{:S(2)}, u32[]{:S(2)}) %collective-permute-start.8) | collective-permute-done | bytes 8224 | tf_op jit(solution)/shard_map/ppermute | solution.py:32
  37.8 2.2 %pack_down.2 = (bf16[64,2560]{1,0:T(8,128)(2,1)S(1)}, bf16[64,2560]{1,0:T(8,128)(2,1)S(1)}, bf16[64,2560]{1,0:T(8,128)(2,1)S(1)}, bf16[64,2560]{1,0:T(8,128)(2,1)S(1)}) custom-call(s32[16,128]{1,0:T(8,128)S(1)} %select_select_fusion.info, f32[16,896]{1,0:T(8,128)S(1)} %get-tuple-element.72.mine_ref, f32[16,896]{1,0:T(8,128)S(1)} %collective-permute-done.9.other_ref, ...), custom_call_target="tpu_custom_call" | custom-call | flops 1 | bytes 1 | tf_op jit(solution)/shard_map/pack_down/pallas_call | solution.py:424
  40.5 1.5 %collective-permute-start.11 = (bf16[64,2560]{1,0:T(8,128)(2,1)S(1)}, bf16[64,2560]{1,0:T(8,128)(2,1)S(1)}, u32[]{:S(2)}, u32[]{:S(2)}) collective-permute-start(bf16[64,2560]{1,0:T(8,128)(2,1)S(1)} %get-tuple-element.85), channel_id=1, source_target_pairs={{0,2},{2,0},{4,6},{6,4},{8,10},{10,8},{12,14},{14,12},{1,3},{3,1},... | collective-permute-start | bytes 983048 | tf_op jit(solution)/shard_map/ppermute | solution.py:36
  42.1 1.5 %collective-permute-start.13 = (bf16[64,2560]{1,0:T(8,128)(2,1)S(1)}, bf16[64,2560]{1,0:T(8,128)(2,1)S(1)}, u32[]{:S(2)}, u32[]{:S(2)}) collective-permute-start(bf16[64,2560]{1,0:T(8,128)(2,1)S(1)} %get-tuple-element.87), channel_id=1, source_target_pairs={{0,6},{2,4},{4,2},{6,0},{8,14},{10,12},{12,10},{14,8},{1,7},{3,5},... | collective-permute-start | bytes 983048 | tf_op jit(solution)/shard_map/ppermute | solution.py:36
  43.6 4.7 %through.2 = (f32[896,2048]{1,0:T(8,128)S(1)}, bf16[2,64,128]{2,1,0:T(8,128)(2,1)S(1)}) custom-call(s32[16,128]{1,0:T(8,128)S(1)} %select_select_fusion.info, bf16[896,1024]{1,0:T(8,128)(2,1)S(1)} %get-tuple-element.76.g_ref, bf16[4096,1024]{1,0:T(8,128)(2,1)S(1)} %copy-done), custom_call_target="tpu_custom_call" | custom-call | flops 1 | bytes 1 | tf_op jit(solution)/shard_map/through/pallas_call | solution.py:448
  49.4 3.5 %collective-permute-done.12.refs_2_ = bf16[64,2560]{1,0:T(8,128)(2,1)S(1)} collective-permute-done((bf16[64,2560]{1,0:T(8,128)(2,1)S(1)}, bf16[64,2560]{1,0:T(8,128)(2,1)S(1)}, u32[]{:S(2)}, u32[]{:S(2)}) %collective-permute-start.12) | collective-permute-done | bytes 327712 | tf_op jit(solution)/shard_map/ppermute | solution.py:36
  52.9 1.5 %collective-permute-start.14 = (bf16[112,1024]{1,0:T(8,128)(2,1)S(1)}, bf16[112,1024]{1,0:T(8,128)(2,1)S(1)}, u32[]{:S(2)}, u32[]{:S(2)}) collective-permute-start(bf16[112,1024]{1,0:T(8,128)(2,1)S(1)} %get-tuple-element.92), channel_id=1, source_target_pairs={{0,2},{2,0},{4,6},{6,4},{8,10},{10,8},{12,14},{14,12},{1,3},{3,1},... | collective-permute-start | bytes 688136 | tf_op jit(solution)/shard_map/ppermute | solution.py:36
  54.5 1.5 %collective-permute-start.15 = (bf16[112,1024]{1,0:T(8,128)(2,1)S(1)}, bf16[112,1024]{1,0:T(8,128)(2,1)S(1)}, u32[]{:S(2)}, u32[]{:S(2)}) collective-permute-start(bf16[112,1024]{1,0:T(8,128)(2,1)S(1)} %get-tuple-element.93), channel_id=1, source_target_pairs={{0,16},{16,0},{1,17},{17,1},{2,18},{18,2},{3,19},{19,3},{4,20},{20... | collective-permute-start | bytes 688136 | tf_op jit(solution)/shard_map/ppermute | solution.py:32
  56.4 1.7 %pack_down.3 = (bf16[64,1536]{1,0:T(8,128)(2,1)S(1)}, bf16[64,1536]{1,0:T(8,128)(2,1)S(1)}, bf16[64,1536]{1,0:T(8,128)(2,1)S(1)}, bf16[64,1536]{1,0:T(8,128)(2,1)S(1)}) custom-call(s32[16,128]{1,0:T(8,128)S(1)} %select_select_fusion.info, f32[16,896]{1,0:T(8,128)S(1)} %get-tuple-element.72.mine_ref, f32[16,896]{1,0:T(8,128)S(1)} %collective-permute-done.9.other_ref, ...), custom_call_target="tpu_custom_call" | custom-call | flops 1 | bytes 1 | tf_op jit(solution)/shard_map/pack_down/pallas_call | solution.py:424
  58.1 3.5 %collective-permute-done.13.refs_3_ = bf16[64,2560]{1,0:T(8,128)(2,1)S(1)} collective-permute-done((bf16[64,2560]{1,0:T(8,128)(2,1)S(1)}, bf16[64,2560]{1,0:T(8,128)(2,1)S(1)}, u32[]{:S(2)}, u32[]{:S(2)}) %collective-permute-start.13) | collective-permute-done | bytes 327712 | tf_op jit(solution)/shard_map/ppermute | solution.py:36
  62.6 1.6 %collective-permute-start.19 = (bf16[64,1536]{1,0:T(8,128)(2,1)S(1)}, bf16[64,1536]{1,0:T(8,128)(2,1)S(1)}, u32[]{:S(2)}, u32[]{:S(2)}) collective-permute-start(bf16[64,1536]{1,0:T(8,128)(2,1)S(1)} %get-tuple-element.105), channel_id=1, source_target_pairs={{0,4},{2,6},{4,0},{6,2},{8,12},{10,14},{12,8},{14,10},{1,5},{3,7},... | collective-permute-start | bytes 589832 | tf_op jit(solution)/shard_map/ppermute | solution.py:36
  64.3 6.1 %collective-permute-done.14.refs_1_ = bf16[112,1024]{1,0:T(8,128)(2,1)S(1)} collective-permute-done((bf16[112,1024]{1,0:T(8,128)(2,1)S(1)}, bf16[112,1024]{1,0:T(8,128)(2,1)S(1)}, u32[]{:S(2)}, u32[]{:S(2)}) %collective-permute-start.14) | collective-permute-done | bytes 229408 | tf_op jit(solution)/shard_map/ppermute | solution.py:36
  70.8 2.6 %collective-permute-start.20 = (bf16[64,1536]{1,0:T(8,128)(2,1)S(1)}, bf16[64,1536]{1,0:T(8,128)(2,1)S(1)}, u32[]{:S(2)}, u32[]{:S(2)}) collective-permute-start(bf16[64,1536]{1,0:T(8,128)(2,1)S(1)} %get-tuple-element.107), channel_id=1, source_target_pairs={{0,6},{2,4},{4,2},{6,0},{8,14},{10,12},{12,10},{14,8},{1,7},{3,5},... | collective-permute-start | bytes 589832 | tf_op jit(solution)/shard_map/ppermute | solution.py:36
  73.4 2.6 %collective-permute-start.21 = (bf16[64,2560]{1,0:T(8,128)(2,1)S(1)}, bf16[64,2560]{1,0:T(8,128)(2,1)S(1)}, u32[]{:S(2)}, u32[]{:S(2)}) collective-permute-start(bf16[64,2560]{1,0:T(8,128)(2,1)S(1)} %get-tuple-element.88), channel_id=1, source_target_pairs={{0,8},{2,10},{4,12},{6,14},{8,0},{10,2},{12,4},{14,6},{1,9},{3,11}... | collective-permute-start | bytes 983048 | tf_op jit(solution)/shard_map/ppermute | solution.py:36
  76.0 4.9 %through.3.high_ref = f32[896,2048]{1,0:T(8,128)S(1)} custom-call(s32[16,128]{1,0:T(8,128)S(1)} %select_select_fusion.info, bf16[896,1024]{1,0:T(8,128)(2,1)S(1)} %get-tuple-element.76.g_ref, bf16[4096,1024]{1,0:T(8,128)(2,1)S(1)} %copy-done), custom_call_target="tpu_custom_call" | custom-call | flops 1 | bytes 1 | tf_op jit(solution)/shard_map/through/pallas_call | solution.py:448
  80.8 2.8 %shrink.1 = (bf16[112,4096]{1,0:T(8,128)(2,1)S(1)}, f32[16,896]{1,0:T(8,128)S(1)}) custom-call(s32[16,128]{1,0:T(8,128)S(1)} %select_select_fusion.info, bf16[896,4096]{1,0:T(8,128)(2,1)S(1)} %get-tuple-element.73.x_ref, bf16[112,1024]{1,0:T(8,128)(2,1)S(1)} %get-tuple-element.80.refs_0_, bf16[112,1024]{1,0:T(8,128)(2,1)S(1)} %collective-permute-done.14.refs_1_, ...), custom_call_target="tpu_custom_call" | custom-call | flops 1 | bytes 1 | tf_op jit(solution)/shard_map/shrink/pallas_call | solution.py:495
  83.7 7.7 %token_grads.1 = bf16[896,4096]{1,0:T(8,128)(2,1)} custom-call(s32[16,128]{1,0:T(8,128)S(1)} %select_select_fusion.info, f32[896,2048]{1,0:T(8,128)S(1)} %get-tuple-element.78.low_ref, f32[896,2048]{1,0:T(8,128)S(1)} %through.3.high_ref, f32[16,896]{1,0:T(8,128)S(1)} %get-tuple-element.72.mine_ref, f32[16,896]{1,0:T(8,128)S(1)} %collective-permute-done.9.other_ref, ...), custom_call_target="tpu_custom_call" | custom-call | flops 1 | bytes 1 | tf_op jit(solution)/shard_map/token_grads/pallas_call | solution.py:503
  91.4 1.1 %pack_up.1 = (bf16[64,512]{1,0:T(8,128)(2,1)S(1)}, bf16[64,512]{1,0:T(8,128)(2,1)S(1)}, bf16[64,512]{1,0:T(8,128)(2,1)S(1)}, bf16[64,512]{1,0:T(8,128)(2,1)S(1)}) custom-call(s32[16,128]{1,0:T(8,128)S(1)} %select_select_fusion.info, f32[16,896]{1,0:T(8,128)S(1)} %get-tuple-element.95.mine_ref, f32[16,896]{1,0:T(8,128)S(1)} %collective-permute-done.17.other_ref, ...), custom_call_target="tpu_custom_call" | custom-call | flops 1 | bytes 1 | tf_op jit(solution)/shard_map/pack_up/pallas_call | solution.py:509
  94.9 2.6 %collective-permute-start.25 = (bf16[64,512]{1,0:T(8,128)(2,1)S(1)}, bf16[64,512]{1,0:T(8,128)(2,1)S(1)}, u32[]{:S(2)}, u32[]{:S(2)}) collective-permute-start(bf16[64,512]{1,0:T(8,128)(2,1)S(1)} %get-tuple-element.117), channel_id=1, source_target_pairs={{0,6},{2,4},{4,2},{6,0},{8,14},{10,12},{12,10},{14,8},{1,7},{3,5},... | collective-permute-start | bytes 196616 | tf_op jit(solution)/shard_map/ppermute | solution.py:36
  97.4 2.1 %projected.1 = bf16[896,512]{1,0:T(8,128)(2,1)} custom-call(s32[16,128]{1,0:T(8,128)S(1)} %select_select_fusion.info, f32[896,512]{1,0:T(8,128)S(1)} %get-tuple-element.110.base_ref, bf16[896,512]{1,0:T(8,128)(2,1)S(1)} %collective-permute-done.7.far_ref, f32[16,896]{1,0:T(8,128)S(1)} %get-tuple-element.95.mine_ref, ...), custom_call_target="tpu_custom_call" | custom-call | flops 1 | bytes 1 | tf_op jit(solution)/shard_map/projected/pallas_call | solution.py:520
  102.5 3.5 %collective-permute-start.26 = (bf16[64,512]{1,0:T(8,128)(2,1)S(1)}, bf16[64,512]{1,0:T(8,128)(2,1)S(1)}, u32[]{:S(2)}, u32[]{:S(2)}) collective-permute-start(bf16[64,512]{1,0:T(8,128)(2,1)S(1)} %get-tuple-element.119), channel_id=1, source_target_pairs={{0,8},{2,10},{4,12},{6,14},{8,0},{10,2},{12,4},{14,6},{1,9},{3,11}... | collective-permute-start | bytes 196616 | tf_op jit(solution)/shard_map/ppermute | solution.py:36
  106.0 2.9 %collective-permute-done.26.refs_5_ = bf16[64,512]{1,0:T(8,128)(2,1)S(1)} collective-permute-done((bf16[64,512]{1,0:T(8,128)(2,1)S(1)}, bf16[64,512]{1,0:T(8,128)(2,1)S(1)}, u32[]{:S(2)}, u32[]{:S(2)}) %collective-permute-start.26) | collective-permute-done | bytes 65568 | tf_op jit(solution)/shard_map/ppermute | solution.py:36
  108.9 1.8 %final.1 = (f32[64,4096]{1,0:T(8,128)}, f32[64,512]{1,0:T(8,128)}) custom-call(s32[16,128]{1,0:T(8,128)S(1)} %select_select_fusion.info, f32[64,2560]{1,0:T(8,128)S(1)} %get-tuple-element.112.refs_0_, bf16[64,2560]{1,0:T(8,128)(2,1)S(1)} %collective-permute-done.21.refs_1_, f32[64,1536]{1,0:T(8,128)S(1)} %get-tuple-element.113.refs_2_, ...), custom_call_target="tpu_custom_call" | custom-call | flops 1 | bytes 1 | tf_op jit(solution)/shard_map/final/pallas_call | solution.py:532
  (60 shorter events, 14.4 us)
Async XLA Ops:
  0.6 10.5 %collective-permute-start = (bf16[4,16,512]{2,1,0:T(8,128)(2,1)}, bf16[4,16,512]{2,1,0:T(8,128)(2,1)S(1)}, u32[]{:S(2)}, u32[]{:S(2)}) collective-permute-start(bf16[4,16,512]{2,1,0:T(8,128)(2,1)} %param.11), channel_id=1, source_target_pairs={{0,8},{2,10},{4,12},{6,14},{8,0},{10,2},{12,4},{14,6},{1,9},{3,11}... | collective-permute-start | bytes 196616 | tf_op jit(solution)/shard_map/ppermute | solution.py:36
  5.7 5.0 %collective-permute-start.2 = (bf16[4,16,1024]{2,1,0:T(8,128)(2,1)S(1)}, bf16[4,16,1024]{2,1,0:T(8,128)(2,1)S(1)}, u32[]{:S(2)}, u32[]{:S(2)}) collective-permute-start(bf16[4,16,1024]{2,1,0:T(8,128)(2,1)S(1)} %get-tuple-element.123), channel_id=1, source_target_pairs={{0,2},{2,0},{4,6},{6,4},{8,10},{10,8},{12,14},{14,12},{1,3},{3,1},... | collective-permute-start | bytes 393224 | tf_op jit(solution)/shard_map/ppermute | solution.py:36
  7.3 8.3 %collective-permute-start.3 = (bf16[896,512]{1,0:T(8,128)(2,1)}, bf16[896,512]{1,0:T(8,128)(2,1)S(1)}, u32[]{:S(2)}, u32[]{:S(2)}) collective-permute-start(bf16[896,512]{1,0:T(8,128)(2,1)} %g_ref.3), channel_id=1, source_target_pairs={{0,1},{1,0},{2,3},{3,2},{4,5},{5,4},{6,7},{7,6},{8,9},{9,8},{10,11... | collective-permute-start | bytes 2752520 | tf_op jit(solution)/shard_map/ppermute | solution.py:32
  10.8 20.2 %collective-permute-start.6 = (bf16[8,16,1024]{2,1,0:T(8,128)(2,1)S(1)}, bf16[8,16,1024]{2,1,0:T(8,128)(2,1)S(1)}, u32[]{:S(2)}, u32[]{:S(2)}) collective-permute-start(bf16[8,16,1024]{2,1,0:T(8,128)(2,1)S(1)} %pad_maximum_fusion.1.own_ref), channel_id=1, source_target_pairs={{0,8},{2,10},{4,12},{6,14},{8,0},{10,2},{12,4},{14,6},{1,9},{3,11}... | collective-permute-start | bytes 786440 | tf_op jit(solution)/shard_map/ppermute | solution.py:36
  12.0 19.0 %collective-permute-start.5 = (bf16[144,512]{1,0:T(8,128)(2,1)S(1)}, bf16[144,512]{1,0:T(8,128)(2,1)S(1)}, u32[]{:S(2)}, u32[]{:S(2)}) collective-permute-start(bf16[144,512]{1,0:T(8,128)(2,1)S(1)} %pad_maximum_fusion.2.refs_0_), channel_id=1, source_target_pairs={{0,2},{2,0},{4,6},{6,4},{8,10},{10,8},{12,14},{14,12},{1,3},{3,1},... | collective-permute-start | bytes 442376 | tf_op jit(solution)/shard_map/ppermute | solution.py:36
  13.6 17.4 %collective-permute-start.4 = (bf16[144,512]{1,0:T(8,128)(2,1)S(1)}, bf16[144,512]{1,0:T(8,128)(2,1)S(1)}, u32[]{:S(2)}, u32[]{:S(2)}) collective-permute-start(bf16[144,512]{1,0:T(8,128)(2,1)S(1)} %pad_maximum_fusion.2.refs_0_), channel_id=1, source_target_pairs={{0,4},{2,6},{4,0},{6,2},{8,12},{10,14},{12,8},{14,10},{1,5},{3,7},... | collective-permute-start | bytes 442376 | tf_op jit(solution)/shard_map/ppermute | solution.py:36
  15.2 15.8 %collective-permute-start.1 = (bf16[144,512]{1,0:T(8,128)(2,1)S(1)}, bf16[144,512]{1,0:T(8,128)(2,1)S(1)}, u32[]{:S(2)}, u32[]{:S(2)}) collective-permute-start(bf16[144,512]{1,0:T(8,128)(2,1)S(1)} %pad_maximum_fusion.2.refs_0_), channel_id=1, source_target_pairs={{0,6},{2,4},{4,2},{6,0},{8,14},{10,12},{12,10},{14,8},{1,7},{3,5},... | collective-permute-start | bytes 442376 | tf_op jit(solution)/shard_map/ppermute | solution.py:36
  15.6 1.2 %copy-start.1 = (bf16[896,512]{1,0:T(8,128)(2,1)S(1)}, bf16[896,512]{1,0:T(8,128)(2,1)}, u32[]{:S(2)}) copy-start(bf16[896,512]{1,0:T(8,128)(2,1)} %g_ref.3) | copy-start | bytes 2752516
  30.9 12.7 %copy-start = (bf16[4096,1024]{1,0:T(8,128)(2,1)S(1)}, bf16[4096,1024]{1,0:T(8,128)(2,1)}, u32[]{:S(2)}) copy-start(bf16[4096,1024]{1,0:T(8,128)(2,1)} %get-tuple-element.77.w_ref) | copy-start | bytes 25165828
  30.9 6.8 %collective-permute-start.7 = (bf16[896,512]{1,0:T(8,128)(2,1)S(1)}, bf16[896,512]{1,0:T(8,128)(2,1)S(1)}, u32[]{:S(2)}, u32[]{:S(2)}) collective-permute-start(bf16[896,512]{1,0:T(8,128)(2,1)S(1)} %get-tuple-element.64), channel_id=1, source_target_pairs={{0,1},{1,0},{2,3},{3,2},{4,5},{5,4},{6,7},{7,6},{8,9},{9,8},{10,11... | collective-permute-start | bytes 2752520 | tf_op jit(solution)/shard_map/ppermute | solution.py:32
  31.1 17.2 %collective-permute-start.10 = (bf16[16,16,1024]{2,1,0:T(8,128)(2,1)S(1)}, bf16[16,16,1024]{2,1,0:T(8,128)(2,1)S(1)}, u32[]{:S(2)}, u32[]{:S(2)}) collective-permute-start(bf16[16,16,1024]{2,1,0:T(8,128)(2,1)S(1)} %pad_maximum_fusion), channel_id=1, source_target_pairs={{0,4},{2,6},{4,0},{6,2},{8,12},{10,14},{12,8},{14,10},{1,5},{3,7},... | collective-permute-start | bytes 1572872 | tf_op jit(solution)/shard_map/ppermute | solution.py:36
  33.9 3.9 %collective-permute-start.9 = (f32[16,896]{1,0:T(8,128)S(1)}, f32[16,896]{1,0:T(8,128)S(1)}, u32[]{:S(2)}, u32[]{:S(2)}) collective-permute-start(f32[16,896]{1,0:T(8,128)S(1)} %get-tuple-element.72.mine_ref), channel_id=1, source_target_pairs={{0,1},{1,0},{2,3},{3,2},{4,5},{5,4},{6,7},{7,6},{8,9},{9,8},{10,11... | collective-permute-start | bytes 172040 | tf_op jit(solution)/shard_map/ppermute | solution.py:32
  34.1 3.7 %collective-permute-start.8 = (s32[16,128]{1,0:T(8,128)S(1)}, s32[16,128]{1,0:T(8,128)S(1)}, u32[]{:S(2)}, u32[]{:S(2)}) collective-permute-start(s32[16,128]{1,0:T(8,128)S(1)} %select_select_fusion.info), channel_id=1, source_target_pairs={{0,16},{16,0},{1,17},{17,1},{2,18},{18,2},{3,19},{19,3},{4,20},{20... | collective-permute-start | bytes 24584 | tf_op jit(solution)/shard_map/ppermute | solution.py:32
  40.0 12.9 %collective-permute-start.12 = (bf16[64,2560]{1,0:T(8,128)(2,1)S(1)}, bf16[64,2560]{1,0:T(8,128)(2,1)S(1)}, u32[]{:S(2)}, u32[]{:S(2)}) collective-permute-start(bf16[64,2560]{1,0:T(8,128)(2,1)S(1)} %get-tuple-element.86), channel_id=1, source_target_pairs={{0,4},{2,6},{4,0},{6,2},{8,12},{10,14},{12,8},{14,10},{1,5},{3,7},... | collective-permute-start | bytes 983048 | tf_op jit(solution)/shard_map/ppermute | solution.py:36
  40.5 17.6 %collective-permute-start.11 = (bf16[64,2560]{1,0:T(8,128)(2,1)S(1)}, bf16[64,2560]{1,0:T(8,128)(2,1)S(1)}, u32[]{:S(2)}, u32[]{:S(2)}) collective-permute-start(bf16[64,2560]{1,0:T(8,128)(2,1)S(1)} %get-tuple-element.85), channel_id=1, source_target_pairs={{0,2},{2,0},{4,6},{6,4},{8,10},{10,8},{12,14},{14,12},{1,3},{3,1},... | collective-permute-start | bytes 983048 | tf_op jit(solution)/shard_map/ppermute | solution.py:36
  42.1 19.6 %collective-permute-start.13 = (bf16[64,2560]{1,0:T(8,128)(2,1)S(1)}, bf16[64,2560]{1,0:T(8,128)(2,1)S(1)}, u32[]{:S(2)}, u32[]{:S(2)}) collective-permute-start(bf16[64,2560]{1,0:T(8,128)(2,1)S(1)} %get-tuple-element.87), channel_id=1, source_target_pairs={{0,6},{2,4},{4,2},{6,0},{8,14},{10,12},{12,10},{14,8},{1,7},{3,5},... | collective-permute-start | bytes 983048 | tf_op jit(solution)/shard_map/ppermute | solution.py:36
  52.9 17.4 %collective-permute-start.14 = (bf16[112,1024]{1,0:T(8,128)(2,1)S(1)}, bf16[112,1024]{1,0:T(8,128)(2,1)S(1)}, u32[]{:S(2)}, u32[]{:S(2)}) collective-permute-start(bf16[112,1024]{1,0:T(8,128)(2,1)S(1)} %get-tuple-element.92), channel_id=1, source_target_pairs={{0,2},{2,0},{4,6},{6,4},{8,10},{10,8},{12,14},{14,12},{1,3},{3,1},... | collective-permute-start | bytes 688136 | tf_op jit(solution)/shard_map/ppermute | solution.py:36
  54.5 18.9 %collective-permute-start.15 = (bf16[112,1024]{1,0:T(8,128)(2,1)S(1)}, bf16[112,1024]{1,0:T(8,128)(2,1)S(1)}, u32[]{:S(2)}, u32[]{:S(2)}) collective-permute-start(bf16[112,1024]{1,0:T(8,128)(2,1)S(1)} %get-tuple-element.93), channel_id=1, source_target_pairs={{0,16},{16,0},{1,17},{17,1},{2,18},{18,2},{3,19},{19,3},{4,20},{20... | collective-permute-start | bytes 688136 | tf_op jit(solution)/shard_map/ppermute | solution.py:32
  56.0 24.9 %collective-permute-start.16 = (bf16[112,1024]{1,0:T(8,128)(2,1)S(1)}, bf16[112,1024]{1,0:T(8,128)(2,1)S(1)}, u32[]{:S(2)}, u32[]{:S(2)}) collective-permute-start(bf16[112,1024]{1,0:T(8,128)(2,1)S(1)} %get-tuple-element.94), channel_id=1, source_target_pairs={{0,18},{2,16},{4,22},{6,20},{8,26},{10,24},{12,30},{14,28},{16,2},... | collective-permute-start | bytes 688136 | tf_op jit(solution)/shard_map/ppermute | solution.py:469
  62.6 29.9 %collective-permute-start.19 = (bf16[64,1536]{1,0:T(8,128)(2,1)S(1)}, bf16[64,1536]{1,0:T(8,128)(2,1)S(1)}, u32[]{:S(2)}, u32[]{:S(2)}) collective-permute-start(bf16[64,1536]{1,0:T(8,128)(2,1)S(1)} %get-tuple-element.105), channel_id=1, source_target_pairs={{0,4},{2,6},{4,0},{6,2},{8,12},{10,14},{12,8},{14,10},{1,5},{3,7},... | collective-permute-start | bytes 589832 | tf_op jit(solution)/shard_map/ppermute | solution.py:36
  70.4 22.2 %collective-permute-start.18 = (bf16[64,1536]{1,0:T(8,128)(2,1)S(1)}, bf16[64,1536]{1,0:T(8,128)(2,1)S(1)}, u32[]{:S(2)}, u32[]{:S(2)}) collective-permute-start(bf16[64,1536]{1,0:T(8,128)(2,1)S(1)} %get-tuple-element.103), channel_id=1, source_target_pairs={{0,2},{2,0},{4,6},{6,4},{8,10},{10,8},{12,14},{14,12},{1,3},{3,1},... | collective-permute-start | bytes 589832 | tf_op jit(solution)/shard_map/ppermute | solution.py:36
  70.8 21.8 %collective-permute-start.20 = (bf16[64,1536]{1,0:T(8,128)(2,1)S(1)}, bf16[64,1536]{1,0:T(8,128)(2,1)S(1)}, u32[]{:S(2)}, u32[]{:S(2)}) collective-permute-start(bf16[64,1536]{1,0:T(8,128)(2,1)S(1)} %get-tuple-element.107), channel_id=1, source_target_pairs={{0,6},{2,4},{4,2},{6,0},{8,14},{10,12},{12,10},{14,8},{1,7},{3,5},... | collective-permute-start | bytes 589832 | tf_op jit(solution)/shard_map/ppermute | solution.py:36
  73.4 32.6 %collective-permute-start.21 = (bf16[64,2560]{1,0:T(8,128)(2,1)S(1)}, bf16[64,2560]{1,0:T(8,128)(2,1)S(1)}, u32[]{:S(2)}, u32[]{:S(2)}) collective-permute-start(bf16[64,2560]{1,0:T(8,128)(2,1)S(1)} %get-tuple-element.88), channel_id=1, source_target_pairs={{0,8},{2,10},{4,12},{6,14},{8,0},{10,2},{12,4},{14,6},{1,9},{3,11}... | collective-permute-start | bytes 983048 | tf_op jit(solution)/shard_map/ppermute | solution.py:36
  83.7 7.8 %collective-permute-start.17 = (f32[16,896]{1,0:T(8,128)S(1)}, f32[16,896]{1,0:T(8,128)S(1)}, u32[]{:S(2)}, u32[]{:S(2)}) collective-permute-start(f32[16,896]{1,0:T(8,128)S(1)} %get-tuple-element.95.mine_ref), channel_id=1, source_target_pairs={{0,1},{1,0},{2,3},{3,2},{4,5},{5,4},{6,7},{7,6},{8,9},{9,8},{10,11... | collective-permute-start | bytes 172040 | tf_op jit(solution)/shard_map/ppermute | solution.py:32
  93.5 15.4 %collective-permute-start.22 = (bf16[64,1536]{1,0:T(8,128)(2,1)S(1)}, bf16[64,1536]{1,0:T(8,128)(2,1)S(1)}, u32[]{:S(2)}, u32[]{:S(2)}) collective-permute-start(bf16[64,1536]{1,0:T(8,128)(2,1)S(1)} %get-tuple-element.108), channel_id=1, source_target_pairs={{0,8},{2,10},{4,12},{6,14},{8,0},{10,2},{12,4},{14,6},{1,9},{3,11}... | collective-permute-start | bytes 589832 | tf_op jit(solution)/shard_map/ppermute | solution.py:36
  93.9 5.6 %collective-permute-start.23 = (bf16[64,512]{1,0:T(8,128)(2,1)S(1)}, bf16[64,512]{1,0:T(8,128)(2,1)S(1)}, u32[]{:S(2)}, u32[]{:S(2)}) collective-permute-start(bf16[64,512]{1,0:T(8,128)(2,1)S(1)} %get-tuple-element.115), channel_id=1, source_target_pairs={{0,2},{2,0},{4,6},{6,4},{8,10},{10,8},{12,14},{14,12},{1,3},{3,1},... | collective-permute-start | bytes 196616 | tf_op jit(solution)/shard_map/ppermute | solution.py:36
  94.4 6.2 %collective-permute-start.24 = (bf16[64,512]{1,0:T(8,128)(2,1)S(1)}, bf16[64,512]{1,0:T(8,128)(2,1)S(1)}, u32[]{:S(2)}, u32[]{:S(2)}) collective-permute-start(bf16[64,512]{1,0:T(8,128)(2,1)S(1)} %get-tuple-element.116), channel_id=1, source_target_pairs={{0,4},{2,6},{4,0},{6,2},{8,12},{10,14},{12,8},{14,10},{1,5},{3,7},... | collective-permute-start | bytes 196616 | tf_op jit(solution)/shard_map/ppermute | solution.py:36
  94.9 6.7 %collective-permute-start.25 = (bf16[64,512]{1,0:T(8,128)(2,1)S(1)}, bf16[64,512]{1,0:T(8,128)(2,1)S(1)}, u32[]{:S(2)}, u32[]{:S(2)}) collective-permute-start(bf16[64,512]{1,0:T(8,128)(2,1)S(1)} %get-tuple-element.117), channel_id=1, source_target_pairs={{0,6},{2,4},{4,2},{6,0},{8,14},{10,12},{12,10},{14,8},{1,7},{3,5},... | collective-permute-start | bytes 196616 | tf_op jit(solution)/shard_map/ppermute | solution.py:36
  102.5 6.4 %collective-permute-start.26 = (bf16[64,512]{1,0:T(8,128)(2,1)S(1)}, bf16[64,512]{1,0:T(8,128)(2,1)S(1)}, u32[]{:S(2)}, u32[]{:S(2)}) collective-permute-start(bf16[64,512]{1,0:T(8,128)(2,1)S(1)} %get-tuple-element.119), channel_id=1, source_target_pairs={{0,8},{2,10},{4,12},{6,14},{8,0},{10,2},{12,4},{14,6},{1,9},{3,11}... | collective-permute-start | bytes 196616 | tf_op jit(solution)/shard_map/ppermute | solution.py:36

commit v9 on v8

--- a/solution.py
+++ b/solution.py
@@ -126,13 +126,13 @@
 
 
 def base_kernel(
-    z, info, x_hbm, w_hbm, g_ref, h_ref, far_ref, own_ref, full_ref, x_ref, w_ref, x_sem, w_sem
+    z, info, x_hbm, w_hbm, g_ref, h_ref, far_ref, full_ref, x_ref, w_ref, x_sem, w_sem
 ):
     own = pl.ds(pl.multiple_of(info[z.core] * z.cols, z.cols), z.cols)
     far = pl.ds(pl.multiple_of((1 - info[z.core]) * z.cols, z.cols), z.cols)
     unit = z.width // 8
     copies = []
-    for i, (first, last) in enumerate(((0, 1), (1, 2), (2, 4), (4, 6), (6, 8))):
+    for i, (first, last) in enumerate(((0, 1), (1, 3), (3, 5), (5, 7), (7, 8))):
         cut = pl.ds(first * unit, (last - first) * unit)
         x = pltpu.make_async_copy(x_hbm.at[:, cut], x_ref.at[:, cut], x_sem.at[i])
         w = pltpu.make_async_copy(w_hbm.at[cut], w_ref.at[cut], w_sem.at[i])
@@ -143,11 +143,18 @@
         cut = z.block(b)
         full_ref[cut, own] = _masked(g_ref[cut, :], z.valid(info, b))
         full_ref[cut, far] = _masked(h_ref[cut, :], z.valid(info, b))
+    total = None
     for x, w, cut in copies:
         x.wait()
         w.wait()
-    far_ref[...] = _dot(x_ref[...], w_ref[:, far], NN).astype(bf16)
-    own_ref[...] = _dot(x_ref[...], w_ref[:, own], NN)
+        term = _dot(x_ref[:, cut], w_ref[cut, far], NN)
+        total = term if total is None else total + term
+    far_ref[...] = total.astype(bf16)
+
+
+def own_kernel(z, info, x_ref, w_ref, far_ref, out_ref):
+    own = pl.ds(pl.multiple_of(info[z.core] * z.cols, z.cols), z.cols)
+    out_ref[...] = _dot(x_ref[...], w_ref[:, own], NN) + far_ref[...].astype(f32)
 
 
 def back_kernel(z, info, g_ref, *refs):
@@ -276,7 +283,7 @@
         out_ref[:, z.block(b)] = total[z.block(b), :].T[z.ranks(b), :]
 
 
-def projected_kernel(z, info, base_ref, far_ref, mine_ref, other_ref, up_ref, out_ref, spread):
+def projected_kernel(z, info, base_ref, mine_ref, other_ref, up_ref, out_ref, spread):
     spread[...] = jnp.zeros_like(spread)
     for b in range(z.nb):
         cut = z.block(b)
@@ -284,7 +291,7 @@
     wide = _dot(spread[...], up_ref[...], TN)
     for b in range(z.nb):
         cut = z.block(b)
-        full = base_ref[cut, :] + far_ref[cut, :].astype(f32) + adapter_scale * wide[cut]
+        full = base_ref[cut, :] + adapter_scale * wide[cut]
         out_ref[cut, :] = _masked(full, z.valid(info, b)).astype(bf16)
 
 
@@ -379,13 +386,12 @@
     info = jnp.where(line == 6, spread_out(tenant_slot)[None, :], info)
     info = jnp.where(line == 0, own_tenants[None, :], info)
 
-    base_other, base_own, g_full, x_in, w_in = _call(
+    base_other, g_full, x_in, w_in = _call(
         functools.partial(base_kernel, z), "base", (1,),
         [pl.BlockSpec(memory_space=pl.ANY)] * 2 + [VMEM] * 2,
-        [_whole((rows, cols))] + [VMEM] * 4,
+        [_whole((rows, cols))] + [VMEM] * 3,
         [
-            _shape((rows, cols), bf16), _shape((rows, cols), f32),
-            _shape((rows, 2 * cols), bf16), _shape(tokens.shape, bf16),
+            _shape((rows, cols), bf16), _shape((rows, 2 * cols), bf16), _shape(tokens.shape, bf16),
             _shape(base_weight.shape, bf16),
         ],
         [pltpu.SemaphoreType.DMA((5,)), pltpu.SemaphoreType.DMA((5,))],
@@ -415,7 +421,6 @@
     ready = [base_arrived]
     if shared:
         info_x = _swap(info, "groups")
-        ready.append(info_x)
 
     packed_rows = n_dp * CAP * rank
     near_rows = packed_rows // NEAR
@@ -451,10 +456,8 @@
         )(info, g_full, w_in)
 
     half = width // 2
-    wide_a = width * 5 // 8
+    wide_a = half
     sends_a = pack(_tie(info, *ready), 0, wide_a)
-    got_a = to_near(sends_a)
-
     low, sums = through(_tie(info, sends_a[0]), 0, half, 1)
 
     if shared:
@@ -464,7 +467,7 @@
             [VMEM] * 3, [_whole(block)] * 4, [_shape(block, bf16)] * 4, [],
             n_scalars=2,
         )(_tie(info, low), info_x, shard, shard_far, farther)
-        got_y = _xor(_tie(chosen[1], got_a[2]), n_dp, 1)
+        got_y = _xor(chosen[1], n_dp, 1)
         got_x = _swap(chosen[2], "groups")
         got_d = lax.ppermute(
             chosen[3],
@@ -480,15 +483,14 @@
 
     sends_b = pack(_tie(info, after_choose), wide_a, width - wide_a)
 
-    dense_a = dense(_tie(info, sends_b[0]), got_a)
-    far_a = to_far(dense_a)
-
-    gate = [dense_a[1]] + ([got_y] if shared else [])
-    got_b = to_near(
-        [_tie(b, *gate) if k in (1, 3) else _tie(b, dense_a[1]) for k, b in enumerate(sends_b)]
-    )
-
-    (high,) = through(_tie(info, dense_a[1]), half, width - half, 0)
+    got_a = [sends_a[0], None] + [_xor(sends_a[k], n_dp, k) for k in range(2, NEAR)]
+    got_a[1] = _xor(_tie(sends_a[1], sends_b[0], got_a[2]), n_dp, 1)
+
+    base_own = _call(
+        functools.partial(own_kernel, z), "base_own", (1,),
+        [VMEM] * 3, VMEM, _shape((rows, cols), f32), [],
+    )(_tie(info, sends_b[0]), x_in, w_in, base_arrived)
+    (high,) = through(_tie(info, base_own), half, width - half, 0)
 
     if shared:
         got_down = [chosen[0], got_y, got_x, got_d]
@@ -499,12 +501,16 @@
     )(_tie(info, high), x_in, *got_down)
     shrink_other = _swap(shrink_part, "tensor")
 
+    dense_a = dense(_tie(info, shrink_part), got_a)
+    far_a = to_far(dense_a)
+    got_b = to_near([_tie(b, shrink_part) for b in sends_b])
+
     step = min(512, width // 8)
     grad_tokens = _call(
         functools.partial(tokens_kernel, z), "token_grads", (width // step,),
         [VMEM] * 5, pl.BlockSpec((rows, step), lambda i, *_: (0, i)),
         _shape((rows, width), bf16), [pltpu.VMEM((nb * rank, rows), bf16)],
-    )(_tie(info, shrink_part), low, high, back_part, back_other, block_down)
+    )(_tie(info, dense_a[1]), low, high, back_part, back_other, block_down)
 
     up_sends = _call(
         functools.partial(pack_up_kernel, z, NEAR), "pack_up", (1,),
@@ -519,11 +525,11 @@
 
     projected = _call(
         functools.partial(projected_kernel, z), "projected", (1,),
-        [VMEM] * 5, _whole((rows, cols)), _shape((rows, cols), bf16),
+        [VMEM] * 4, _whole((rows, cols)), _shape((rows, cols), bf16),
         [pltpu.VMEM((nb * rank, rows), bf16)],
     )(
         _tie(info, dense_b[1]),
-        base_own, base_arrived, shrink_part, shrink_other, block_up,
+        base_own, shrink_part, shrink_other, block_up,
     )
     dense_u = dense(_tie(info, projected), got_u)
     far_u = to_far(dense_u)

time: 111 us -> 106 us (0.955)
  the two profiles are of different devices: /device:TPU:0 before, /device:TPU:26 now
where the time goes in v9:
time: 106 us
  Pallas kernels  50.2 us (47%)
  starting transfers between devices  27.4 us (26%)
  waiting for transfers between devices  22.9 us (22%)
  other arithmetic  2.63 us (2%)
  local copies, waits for them, and re-layouts  2.17 us (2%)
    ppermute x20, starting transfers between devices, _xor(): return lax.ppermute(x, 'dp', [(i, i ^ k) for i in range(n)])  24.6 us
    ppermute x20, waiting for transfers between devices, _xor(): return lax.ppermute(x, 'dp', [(i, i ^ k) for i in range(n)])  21.9 us
    pallas_call x1, Pallas kernels, on_device(): _call(functools.partial(base_kernel, z), 'base', (1,), [pl.BlockSpec(memo...  11.8 us
    pallas_call x2, Pallas kernels, through(): _call(functools.partial(through_kernel, z, first), 'through', (1,), [VMEM...  9.58 us
    pallas_call x1, Pallas kernels, on_device(): _call(functools.partial(tokens_kernel, z), 'token_grads', (width // step,...  7.7 us
    pallas_call x1, Pallas kernels, on_device(): _call(functools.partial(own_kernel, z), 'base_own', (1,), [VMEM] * 3, VME...  4.61 us
    pallas_call x2, Pallas kernels, pack(): _call(functools.partial(pack_kernel, z, NEAR, start), 'pack_down', (1,),...  3.93 us
    pallas_call x1, Pallas kernels, on_device(): _call(functools.partial(shrink_kernel, z, n_parts), 'shrink', (1,), [VMEM...  2.81 us
  transfers between devices with their start and end apart: 27, of which 8 were waited for; matrix products, arithmetic and copies ran while one was open for 3% of the time, Pallas kernels for 46%

profile of v9, /device:TPU:26, one launch (start us, length us, event | category | flops | bytes accessed | tf_op | source)
XLA Modules:
  0.0 106.2 jit_solution(14574536359037716746)
XLA Ops:
  1.0 1.0 dynamic-slice_bitcast_fusion.1
  2.0 1.6 %collective-permute-start.2 = (bf16[4,16,1024]{2,1,0:T(8,128)(2,1)S(1)}, bf16[4,16,1024]{2,1,0:T(8,128)(2,1)S(1)}, u32[]{:S(2)}, u32[]{:S(2)}) collective-permute-start(bf16[4,16,1024]{2,1,0:T(8,128)(2,1)S(1)} %get-tuple-element.123), channel_id=1, source_target_pairs={{0,2},{2,0},{4,6},{6,4},{8,10},{10,8},{12,14},{14,12},{1,3},{3,1},... | collective-permute-start | bytes 393224 | tf_op jit(solution)/shard_map/ppermute | solution.py:36
  5.2 1.8 %collective-permute-done.2 = bf16[4,16,1024]{2,1,0:T(8,128)(2,1)S(1)} collective-permute-done((bf16[4,16,1024]{2,1,0:T(8,128)(2,1)S(1)}, bf16[4,16,1024]{2,1,0:T(8,128)(2,1)S(1)}, u32[]{:S(2)}, u32[]{:S(2)}) %collective-permute-start.2) | collective-permute-done | bytes 131104 | tf_op jit(solution)/shard_map/ppermute | solution.py:36
  7.1 2.7 %collective-permute-start.6 = (bf16[8,16,1024]{2,1,0:T(8,128)(2,1)S(1)}, bf16[8,16,1024]{2,1,0:T(8,128)(2,1)S(1)}, u32[]{:S(2)}, u32[]{:S(2)}) collective-permute-start(bf16[8,16,1024]{2,1,0:T(8,128)(2,1)S(1)} %pad_maximum_fusion.1.own_ref), channel_id=1, source_target_pairs={{0,8},{2,10},{4,12},{6,14},{8,0},{10,2},{12,4},{14,6},{1,9},{3,11}... | collective-permute-start | bytes 786440 | tf_op jit(solution)/shard_map/ppermute | solution.py:36
  10.6 1.6 %collective-permute-start.5 = (bf16[144,512]{1,0:T(8,128)(2,1)S(1)}, bf16[144,512]{1,0:T(8,128)(2,1)S(1)}, u32[]{:S(2)}, u32[]{:S(2)}) collective-permute-start(bf16[144,512]{1,0:T(8,128)(2,1)S(1)} %pad_maximum_fusion.2.refs_0_), channel_id=1, source_target_pairs={{0,2},{2,0},{4,6},{6,4},{8,10},{10,8},{12,14},{14,12},{1,3},{3,1},... | collective-permute-start | bytes 442376 | tf_op jit(solution)/shard_map/ppermute | solution.py:36
  12.6 1.5 %collective-permute-start.1 = (bf16[144,512]{1,0:T(8,128)(2,1)S(1)}, bf16[144,512]{1,0:T(8,128)(2,1)S(1)}, u32[]{:S(2)}, u32[]{:S(2)}) collective-permute-start(bf16[144,512]{1,0:T(8,128)(2,1)S(1)} %pad_maximum_fusion.2.refs_0_), channel_id=1, source_target_pairs={{0,6},{2,4},{4,2},{6,0},{8,14},{10,12},{12,10},{14,8},{1,7},{3,5},... | collective-permute-start | bytes 442376 | tf_op jit(solution)/shard_map/ppermute | solution.py:36
  14.2 1.2 %copy-done.1 = bf16[896,512]{1,0:T(8,128)(2,1)S(1)} copy-done((bf16[896,512]{1,0:T(8,128)(2,1)S(1)}, bf16[896,512]{1,0:T(8,128)(2,1)}, u32[]{:S(2)}) %copy-start.1) | copy-done | bytes 917528
  15.4 11.8 %base.1 = (bf16[896,512]{1,0:T(8,128)(2,1)S(1)}, bf16[896,1024]{1,0:T(8,128)(2,1)S(1)}, bf16[896,4096]{1,0:T(8,128)(2,1)S(1)}, bf16[4096,1024]{1,0:T(8,128)(2,1)}) custom-call(s32[16,128]{1,0:T(8,128)S(1)} %select_select_fusion.1.info, bf16[896,4096]{1,0:T(8,128)(2,1)} %x_hbm.1, bf16[4096,1024]{1,0:T(8,128)(2,1)} %w_hbm.1, bf16[896,512]{1,0:T(8,128)(2,1)S(1)} %copy-done.1, ...), custom_call_target="tpu_custom_call" | custom-call | flops 1 | bytes 1 | tf_op jit(solution)/shard_map/base/pallas_call | solution.py:389
  28.0 1.0 back.1
  30.3 2.0 %pack_down.2 = (bf16[64,2048]{1,0:T(8,128)(2,1)S(1)}, bf16[64,2048]{1,0:T(8,128)(2,1)S(1)}, bf16[64,2048]{1,0:T(8,128)(2,1)S(1)}, bf16[64,2048]{1,0:T(8,128)(2,1)S(1)}) custom-call(s32[16,128]{1,0:T(8,128)S(1)} %select_select_fusion.info, f32[16,896]{1,0:T(8,128)S(1)} %get-tuple-element.72.mine_ref, f32[16,896]{1,0:T(8,128)S(1)} %collective-permute-done.8.other_ref, ...), custom_call_target="tpu_custom_call" | custom-call | flops 1 | bytes 1 | tf_op jit(solution)/shard_map/pack_down/pallas_call | solution.py:429
  32.3 1.7 %collective-permute-start.14 = (bf16[64,2048]{1,0:T(8,128)(2,1)S(1)}, bf16[64,2048]{1,0:T(8,128)(2,1)S(1)}, u32[]{:S(2)}, u32[]{:S(2)}) collective-permute-start(bf16[64,2048]{1,0:T(8,128)(2,1)S(1)} %get-tuple-element.93), channel_id=1, source_target_pairs={{0,4},{2,6},{4,0},{6,2},{8,12},{10,14},{12,8},{14,10},{1,5},{3,7},... | collective-permute-start | bytes 786440 | tf_op jit(solution)/shard_map/ppermute | solution.py:36
  34.4 4.7 %through.2 = (f32[896,2048]{1,0:T(8,128)S(1)}, bf16[2,64,128]{2,1,0:T(8,128)(2,1)S(1)}) custom-call(s32[16,128]{1,0:T(8,128)S(1)} %select_select_fusion.info, bf16[896,1024]{1,0:T(8,128)(2,1)S(1)} %get-tuple-element.76.g_ref, bf16[4096,1024]{1,0:T(8,128)(2,1)S(1)} %copy-done), custom_call_target="tpu_custom_call" | custom-call | flops 1 | bytes 1 | tf_op jit(solution)/shard_map/through/pallas_call | solution.py:453
  39.2 3.0 %collective-permute-done.10.pair_ref = bf16[16,16,1024]{2,1,0:T(8,128)(2,1)S(1)} collective-permute-done((bf16[16,16,1024]{2,1,0:T(8,128)(2,1)S(1)}, bf16[16,16,1024]{2,1,0:T(8,128)(2,1)S(1)}, u32[]{:S(2)}, u32[]{:S(2)}) %collective-permute-start.10) | collective-permute-done | bytes 524320 | tf_op jit(solution)/shard_map/ppermute | solution.py:36
  42.2 1.0 choose.1
  43.2 1.6 %collective-permute-start.11 = (bf16[112,1024]{1,0:T(8,128)(2,1)S(1)}, bf16[112,1024]{1,0:T(8,128)(2,1)S(1)}, u32[]{:S(2)}, u32[]{:S(2)}) collective-permute-start(bf16[112,1024]{1,0:T(8,128)(2,1)S(1)} %get-tuple-element.86), channel_id=1, source_target_pairs={{0,2},{2,0},{4,6},{6,4},{8,10},{10,8},{12,14},{14,12},{1,3},{3,1},... | collective-permute-start | bytes 688136 | tf_op jit(solution)/shard_map/ppermute | solution.py:36
  45.3 1.4 %collective-permute-start.13 = (bf16[112,1024]{1,0:T(8,128)(2,1)S(1)}, bf16[112,1024]{1,0:T(8,128)(2,1)S(1)}, u32[]{:S(2)}, u32[]{:S(2)}) collective-permute-start(bf16[112,1024]{1,0:T(8,128)(2,1)S(1)} %get-tuple-element.88), channel_id=1, source_target_pairs={{0,18},{2,16},{4,22},{6,20},{8,26},{10,24},{12,30},{14,28},{16,2},... | collective-permute-start | bytes 688136 | tf_op jit(solution)/shard_map/ppermute | solution.py:472
  46.8 1.4 %collective-permute-start.16 = (bf16[64,2048]{1,0:T(8,128)(2,1)S(1)}, bf16[64,2048]{1,0:T(8,128)(2,1)S(1)}, u32[]{:S(2)}, u32[]{:S(2)}) collective-permute-start(bf16[64,2048]{1,0:T(8,128)(2,1)S(1)} %get-tuple-element.95), channel_id=1, source_target_pairs={{0,6},{2,4},{4,2},{6,0},{8,14},{10,12},{12,10},{14,8},{1,7},{3,5},... | collective-permute-start | bytes 786440 | tf_op jit(solution)/shard_map/ppermute | solution.py:36
  48.2 2.0 %pack_down.3 = (bf16[64,2048]{1,0:T(8,128)(2,1)S(1)}, bf16[64,2048]{1,0:T(8,128)(2,1)S(1)}, bf16[64,2048]{1,0:T(8,128)(2,1)S(1)}, bf16[64,2048]{1,0:T(8,128)(2,1)S(1)}) custom-call(s32[16,128]{1,0:T(8,128)S(1)} %select_select_fusion.info, f32[16,896]{1,0:T(8,128)S(1)} %get-tuple-element.72.mine_ref, f32[16,896]{1,0:T(8,128)S(1)} %collective-permute-done.8.other_ref, ...), custom_call_target="tpu_custom_call" | custom-call | flops 1 | bytes 1 | tf_op jit(solution)/shard_map/pack_down/pallas_call | solution.py:429
  50.1 4.6 %base_own.1.base_ref = f32[896,512]{1,0:T(8,128)S(1)} custom-call(s32[16,128]{1,0:T(8,128)S(1)} %select_select_fusion.info, bf16[896,4096]{1,0:T(8,128)(2,1)S(1)} %get-tuple-element.73.x_ref, bf16[4096,1024]{1,0:T(8,128)(2,1)S(1)} %copy-done, bf16[896,512]{1,0:T(8,128)(2,1)S(1)} %collective-permute-done.7.far_ref), custom_call_target="tpu_custom_call" | custom-call | flops 1 | bytes 1 | tf_op jit(solution)/shard_map/base_own/pallas_call | solution.py:489
  54.7 4.8 %through.3.high_ref = f32[896,2048]{1,0:T(8,128)S(1)} custom-call(s32[16,128]{1,0:T(8,128)S(1)} %select_select_fusion.info, bf16[896,1024]{1,0:T(8,128)(2,1)S(1)} %get-tuple-element.76.g_ref, bf16[4096,1024]{1,0:T(8,128)(2,1)S(1)} %copy-done), custom_call_target="tpu_custom_call" | custom-call | flops 1 | bytes 1 | tf_op jit(solution)/shard_map/through/pallas_call | solution.py:453
  60.7 2.8 %shrink.1 = (bf16[112,4096]{1,0:T(8,128)(2,1)S(1)}, f32[16,896]{1,0:T(8,128)S(1)}) custom-call(s32[16,128]{1,0:T(8,128)S(1)} %select_select_fusion.info, bf16[896,4096]{1,0:T(8,128)(2,1)S(1)} %get-tuple-element.73.x_ref, bf16[112,1024]{1,0:T(8,128)(2,1)S(1)} %get-tuple-element.80.refs_0_, bf16[112,1024]{1,0:T(8,128)(2,1)S(1)} %collective-permute-done.11.refs_1_, ...), custom_call_target="tpu_custom_call" | custom-call | flops 1 | bytes 1 | tf_op jit(solution)/shard_map/shrink/pallas_call | solution.py:497
  63.5 2.5 %collective-permute-start.18 = (bf16[64,2048]{1,0:T(8,128)(2,1)S(1)}, bf16[64,2048]{1,0:T(8,128)(2,1)S(1)}, u32[]{:S(2)}, u32[]{:S(2)}) collective-permute-start(bf16[64,2048]{1,0:T(8,128)(2,1)S(1)} %get-tuple-element.104), channel_id=1, source_target_pairs={{0,2},{2,0},{4,6},{6,4},{8,10},{10,8},{12,14},{14,12},{1,3},{3,1},... | collective-permute-start | bytes 786440 | tf_op jit(solution)/shard_map/ppermute | solution.py:36
  66.2 1.5 %collective-permute-start.20 = (bf16[64,2048]{1,0:T(8,128)(2,1)S(1)}, bf16[64,2048]{1,0:T(8,128)(2,1)S(1)}, u32[]{:S(2)}, u32[]{:S(2)}) collective-permute-start(bf16[64,2048]{1,0:T(8,128)(2,1)S(1)} %get-tuple-element.108), channel_id=1, source_target_pairs={{0,6},{2,4},{4,2},{6,0},{8,14},{10,12},{12,10},{14,8},{1,7},{3,5},... | collective-permute-start | bytes 786440 | tf_op jit(solution)/shard_map/ppermute | solution.py:36
  67.6 4.0 %collective-permute-done.15.refs_1_ = bf16[64,2048]{1,0:T(8,128)(2,1)S(1)} collective-permute-done((bf16[64,2048]{1,0:T(8,128)(2,1)S(1)}, bf16[64,2048]{1,0:T(8,128)(2,1)S(1)}, u32[]{:S(2)}, u32[]{:S(2)}) %collective-permute-start.15) | collective-permute-done | bytes 262176 | tf_op jit(solution)/shard_map/ppermute | solution.py:36
  73.0 7.7 %token_grads.1 = bf16[896,4096]{1,0:T(8,128)(2,1)} custom-call(s32[16,128]{1,0:T(8,128)S(1)} %select_select_fusion.info, f32[896,2048]{1,0:T(8,128)S(1)} %get-tuple-element.78.low_ref, f32[896,2048]{1,0:T(8,128)S(1)} %through.3.high_ref, f32[16,896]{1,0:T(8,128)S(1)} %get-tuple-element.72.mine_ref, f32[16,896]{1,0:T(8,128)S(1)} %collective-permute-done.8.other_ref, ...), custom_call_target="tpu_custom_call" | custom-call | flops 1 | bytes 1 | tf_op jit(solution)/shard_map/token_grads/pallas_call | solution.py:509
  80.7 1.1 %pack_up.1 = (bf16[64,512]{1,0:T(8,128)(2,1)S(1)}, bf16[64,512]{1,0:T(8,128)(2,1)S(1)}, bf16[64,512]{1,0:T(8,128)(2,1)S(1)}, bf16[64,512]{1,0:T(8,128)(2,1)S(1)}) custom-call(s32[16,128]{1,0:T(8,128)S(1)} %select_select_fusion.info, f32[16,896]{1,0:T(8,128)S(1)} %get-tuple-element.89.mine_ref, f32[16,896]{1,0:T(8,128)S(1)} %collective-permute-done.17.other_ref, ...), custom_call_target="tpu_custom_call" | custom-call | flops 1 | bytes 1 | tf_op jit(solution)/shard_map/pack_up/pallas_call | solution.py:515
  82.8 2.7 %collective-permute-start.22 = (bf16[64,2048]{1,0:T(8,128)(2,1)S(1)}, bf16[64,2048]{1,0:T(8,128)(2,1)S(1)}, u32[]{:S(2)}, u32[]{:S(2)}) collective-permute-start(bf16[64,2048]{1,0:T(8,128)(2,1)S(1)} %get-tuple-element.109), channel_id=1, source_target_pairs={{0,8},{2,10},{4,12},{6,14},{8,0},{10,2},{12,4},{14,6},{1,9},{3,11}... | collective-permute-start | bytes 786440 | tf_op jit(solution)/shard_map/ppermute | solution.py:36
  86.1 3.0 %collective-permute-start.25 = (bf16[64,512]{1,0:T(8,128)(2,1)S(1)}, bf16[64,512]{1,0:T(8,128)(2,1)S(1)}, u32[]{:S(2)}, u32[]{:S(2)}) collective-permute-start(bf16[64,512]{1,0:T(8,128)(2,1)S(1)} %get-tuple-element.117), channel_id=1, source_target_pairs={{0,6},{2,4},{4,2},{6,0},{8,14},{10,12},{12,10},{14,8},{1,7},{3,5},... | collective-permute-start | bytes 196616 | tf_op jit(solution)/shard_map/ppermute | solution.py:36
  89.0 2.0 %projected.1 = bf16[896,512]{1,0:T(8,128)(2,1)} custom-call(s32[16,128]{1,0:T(8,128)S(1)} %select_select_fusion.info, f32[896,512]{1,0:T(8,128)S(1)} %base_own.1.base_ref, f32[16,896]{1,0:T(8,128)S(1)} %get-tuple-element.89.mine_ref, f32[16,896]{1,0:T(8,128)S(1)} %collective-permute-done.17.other_ref, bf16[112,512]{1,0:T(8,128)(2,1)S(1)} %get-tuple-element.111.up_ref), custom_call_target="tpu_custom_call" | custom-call | flops 1 | bytes 1 | tf_op jit(solution)/shard_map/projected/pallas_call | solution.py:526
  91.1 7.3 %collective-permute-done.25.refs_3_ = bf16[64,512]{1,0:T(8,128)(2,1)S(1)} collective-permute-done((bf16[64,512]{1,0:T(8,128)(2,1)S(1)}, bf16[64,512]{1,0:T(8,128)(2,1)S(1)}, u32[]{:S(2)}, u32[]{:S(2)}) %collective-permute-start.25) | collective-permute-done | bytes 65568 | tf_op jit(solution)/shard_map/ppermute | solution.py:36
  99.3 5.2 %collective-permute-done.26.refs_5_ = bf16[64,512]{1,0:T(8,128)(2,1)S(1)} collective-permute-done((bf16[64,512]{1,0:T(8,128)(2,1)S(1)}, bf16[64,512]{1,0:T(8,128)(2,1)S(1)}, u32[]{:S(2)}, u32[]{:S(2)}) %collective-permute-start.26) | collective-permute-done | bytes 65568 | tf_op jit(solution)/shard_map/ppermute | solution.py:36
  104.4 1.8 %final.1 = (f32[64,4096]{1,0:T(8,128)}, f32[64,512]{1,0:T(8,128)}) custom-call(s32[16,128]{1,0:T(8,128)S(1)} %select_select_fusion.info, f32[64,2048]{1,0:T(8,128)S(1)} %get-tuple-element.112.refs_0_, bf16[64,2048]{1,0:T(8,128)(2,1)S(1)} %collective-permute-done.21.refs_1_, f32[64,2048]{1,0:T(8,128)S(1)} %get-tuple-element.113.refs_2_, ...), custom_call_target="tpu_custom_call" | custom-call | flops 1 | bytes 1 | tf_op jit(solution)/shard_map/final/pallas_call | solution.py:538
  (61 shorter events, 11.4 us)
Async XLA Ops:
  0.6 9.1 %collective-permute-start = (bf16[4,16,512]{2,1,0:T(8,128)(2,1)}, bf16[4,16,512]{2,1,0:T(8,128)(2,1)S(1)}, u32[]{:S(2)}, u32[]{:S(2)}) collective-permute-start(bf16[4,16,512]{2,1,0:T(8,128)(2,1)} %param.11), channel_id=1, source_target_pairs={{0,8},{2,10},{4,12},{6,14},{8,0},{10,2},{12,4},{14,6},{1,9},{3,11}... | collective-permute-start | bytes 196616 | tf_op jit(solution)/shard_map/ppermute | solution.py:36
  2.0 5.0 %collective-permute-start.2 = (bf16[4,16,1024]{2,1,0:T(8,128)(2,1)S(1)}, bf16[4,16,1024]{2,1,0:T(8,128)(2,1)S(1)}, u32[]{:S(2)}, u32[]{:S(2)}) collective-permute-start(bf16[4,16,1024]{2,1,0:T(8,128)(2,1)S(1)} %get-tuple-element.123), channel_id=1, source_target_pairs={{0,2},{2,0},{4,6},{6,4},{8,10},{10,8},{12,14},{14,12},{1,3},{3,1},... | collective-permute-start | bytes 393224 | tf_op jit(solution)/shard_map/ppermute | solution.py:36
  3.6 10.6 %collective-permute-start.3 = (bf16[896,512]{1,0:T(8,128)(2,1)}, bf16[896,512]{1,0:T(8,128)(2,1)S(1)}, u32[]{:S(2)}, u32[]{:S(2)}) collective-permute-start(bf16[896,512]{1,0:T(8,128)(2,1)} %g_ref.3), channel_id=1, source_target_pairs={{0,1},{1,0},{2,3},{3,2},{4,5},{5,4},{6,7},{7,6},{8,9},{9,8},{10,11... | collective-permute-start | bytes 2752520 | tf_op jit(solution)/shard_map/ppermute | solution.py:32
  7.1 20.2 %collective-permute-start.6 = (bf16[8,16,1024]{2,1,0:T(8,128)(2,1)S(1)}, bf16[8,16,1024]{2,1,0:T(8,128)(2,1)S(1)}, u32[]{:S(2)}, u32[]{:S(2)}) collective-permute-start(bf16[8,16,1024]{2,1,0:T(8,128)(2,1)S(1)} %pad_maximum_fusion.1.own_ref), channel_id=1, source_target_pairs={{0,8},{2,10},{4,12},{6,14},{8,0},{10,2},{12,4},{14,6},{1,9},{3,11}... | collective-permute-start | bytes 786440 | tf_op jit(solution)/shard_map/ppermute | solution.py:36
  10.6 16.7 %collective-permute-start.5 = (bf16[144,512]{1,0:T(8,128)(2,1)S(1)}, bf16[144,512]{1,0:T(8,128)(2,1)S(1)}, u32[]{:S(2)}, u32[]{:S(2)}) collective-permute-start(bf16[144,512]{1,0:T(8,128)(2,1)S(1)} %pad_maximum_fusion.2.refs_0_), channel_id=1, source_target_pairs={{0,2},{2,0},{4,6},{6,4},{8,10},{10,8},{12,14},{14,12},{1,3},{3,1},... | collective-permute-start | bytes 442376 | tf_op jit(solution)/shard_map/ppermute | solution.py:36
  12.2 15.1 %collective-permute-start.4 = (bf16[144,512]{1,0:T(8,128)(2,1)S(1)}, bf16[144,512]{1,0:T(8,128)(2,1)S(1)}, u32[]{:S(2)}, u32[]{:S(2)}) collective-permute-start(bf16[144,512]{1,0:T(8,128)(2,1)S(1)} %pad_maximum_fusion.2.refs_0_), channel_id=1, source_target_pairs={{0,4},{2,6},{4,0},{6,2},{8,12},{10,14},{12,8},{14,10},{1,5},{3,7},... | collective-permute-start | bytes 442376 | tf_op jit(solution)/shard_map/ppermute | solution.py:36
  12.6 14.7 %collective-permute-start.1 = (bf16[144,512]{1,0:T(8,128)(2,1)S(1)}, bf16[144,512]{1,0:T(8,128)(2,1)S(1)}, u32[]{:S(2)}, u32[]{:S(2)}) collective-permute-start(bf16[144,512]{1,0:T(8,128)(2,1)S(1)} %pad_maximum_fusion.2.refs_0_), channel_id=1, source_target_pairs={{0,6},{2,4},{4,2},{6,0},{8,14},{10,12},{12,10},{14,8},{1,7},{3,5},... | collective-permute-start | bytes 442376 | tf_op jit(solution)/shard_map/ppermute | solution.py:36
  14.2 1.2 %copy-start.1 = (bf16[896,512]{1,0:T(8,128)(2,1)S(1)}, bf16[896,512]{1,0:T(8,128)(2,1)}, u32[]{:S(2)}) copy-start(bf16[896,512]{1,0:T(8,128)(2,1)} %g_ref.3) | copy-start | bytes 2752516
  27.2 7.2 %copy-start = (bf16[4096,1024]{1,0:T(8,128)(2,1)S(1)}, bf16[4096,1024]{1,0:T(8,128)(2,1)}, u32[]{:S(2)}) copy-start(bf16[4096,1024]{1,0:T(8,128)(2,1)} %get-tuple-element.77.w_ref) | copy-start | bytes 25165828
  27.2 2.5 %collective-permute-start.7 = (bf16[896,512]{1,0:T(8,128)(2,1)S(1)}, bf16[896,512]{1,0:T(8,128)(2,1)S(1)}, u32[]{:S(2)}, u32[]{:S(2)}) collective-permute-start(bf16[896,512]{1,0:T(8,128)(2,1)S(1)} %get-tuple-element.64), channel_id=1, source_target_pairs={{0,1},{1,0},{2,3},{3,2},{4,5},{5,4},{6,7},{7,6},{8,9},{9,8},{10,11... | collective-permute-start | bytes 2752520 | tf_op jit(solution)/shard_map/ppermute | solution.py:32
  27.4 14.8 %collective-permute-start.10 = (bf16[16,16,1024]{2,1,0:T(8,128)(2,1)S(1)}, bf16[16,16,1024]{2,1,0:T(8,128)(2,1)S(1)}, u32[]{:S(2)}, u32[]{:S(2)}) collective-permute-start(bf16[16,16,1024]{2,1,0:T(8,128)(2,1)S(1)} %pad_maximum_fusion), channel_id=1, source_target_pairs={{0,4},{2,6},{4,0},{6,2},{8,12},{10,14},{12,8},{14,10},{1,5},{3,7},... | collective-permute-start | bytes 1572872 | tf_op jit(solution)/shard_map/ppermute | solution.py:36
  29.0 1.3 %collective-permute-start.8 = (f32[16,896]{1,0:T(8,128)S(1)}, f32[16,896]{1,0:T(8,128)S(1)}, u32[]{:S(2)}, u32[]{:S(2)}) collective-permute-start(f32[16,896]{1,0:T(8,128)S(1)} %get-tuple-element.72.mine_ref), channel_id=1, source_target_pairs={{0,1},{1,0},{2,3},{3,2},{4,5},{5,4},{6,7},{7,6},{8,9},{9,8},{10,11... | collective-permute-start | bytes 172040 | tf_op jit(solution)/shard_map/ppermute | solution.py:32
  32.3 27.3 %collective-permute-start.14 = (bf16[64,2048]{1,0:T(8,128)(2,1)S(1)}, bf16[64,2048]{1,0:T(8,128)(2,1)S(1)}, u32[]{:S(2)}, u32[]{:S(2)}) collective-permute-start(bf16[64,2048]{1,0:T(8,128)(2,1)S(1)} %get-tuple-element.93), channel_id=1, source_target_pairs={{0,4},{2,6},{4,0},{6,2},{8,12},{10,14},{12,8},{14,10},{1,5},{3,7},... | collective-permute-start | bytes 786440 | tf_op jit(solution)/shard_map/ppermute | solution.py:36
  33.9 5.3 %collective-permute-start.9 = (s32[16,128]{1,0:T(8,128)S(1)}, s32[16,128]{1,0:T(8,128)S(1)}, u32[]{:S(2)}, u32[]{:S(2)}) collective-permute-start(s32[16,128]{1,0:T(8,128)S(1)} %select_select_fusion.info), channel_id=1, source_target_pairs={{0,16},{16,0},{1,17},{17,1},{2,18},{18,2},{3,19},{19,3},{4,20},{20... | collective-permute-start | bytes 24584 | tf_op jit(solution)/shard_map/ppermute | solution.py:32
  43.2 17.5 %collective-permute-start.11 = (bf16[112,1024]{1,0:T(8,128)(2,1)S(1)}, bf16[112,1024]{1,0:T(8,128)(2,1)S(1)}, u32[]{:S(2)}, u32[]{:S(2)}) collective-permute-start(bf16[112,1024]{1,0:T(8,128)(2,1)S(1)} %get-tuple-element.86), channel_id=1, source_target_pairs={{0,2},{2,0},{4,6},{6,4},{8,10},{10,8},{12,14},{14,12},{1,3},{3,1},... | collective-permute-start | bytes 688136 | tf_op jit(solution)/shard_map/ppermute | solution.py:36
  44.8 15.9 %collective-permute-start.12 = (bf16[112,1024]{1,0:T(8,128)(2,1)S(1)}, bf16[112,1024]{1,0:T(8,128)(2,1)S(1)}, u32[]{:S(2)}, u32[]{:S(2)}) collective-permute-start(bf16[112,1024]{1,0:T(8,128)(2,1)S(1)} %get-tuple-element.87), channel_id=1, source_target_pairs={{0,16},{16,0},{1,17},{17,1},{2,18},{18,2},{3,19},{19,3},{4,20},{20... | collective-permute-start | bytes 688136 | tf_op jit(solution)/shard_map/ppermute | solution.py:32
  45.3 15.4 %collective-permute-start.13 = (bf16[112,1024]{1,0:T(8,128)(2,1)S(1)}, bf16[112,1024]{1,0:T(8,128)(2,1)S(1)}, u32[]{:S(2)}, u32[]{:S(2)}) collective-permute-start(bf16[112,1024]{1,0:T(8,128)(2,1)S(1)} %get-tuple-element.88), channel_id=1, source_target_pairs={{0,18},{2,16},{4,22},{6,20},{8,26},{10,24},{12,30},{14,28},{16,2},... | collective-permute-start | bytes 688136 | tf_op jit(solution)/shard_map/ppermute | solution.py:472
  46.8 20.9 %collective-permute-start.16 = (bf16[64,2048]{1,0:T(8,128)(2,1)S(1)}, bf16[64,2048]{1,0:T(8,128)(2,1)S(1)}, u32[]{:S(2)}, u32[]{:S(2)}) collective-permute-start(bf16[64,2048]{1,0:T(8,128)(2,1)S(1)} %get-tuple-element.95), channel_id=1, source_target_pairs={{0,6},{2,4},{4,2},{6,0},{8,14},{10,12},{12,10},{14,8},{1,7},{3,5},... | collective-permute-start | bytes 786440 | tf_op jit(solution)/shard_map/ppermute | solution.py:36
  59.6 12.1 %collective-permute-start.15 = (bf16[64,2048]{1,0:T(8,128)(2,1)S(1)}, bf16[64,2048]{1,0:T(8,128)(2,1)S(1)}, u32[]{:S(2)}, u32[]{:S(2)}) collective-permute-start(bf16[64,2048]{1,0:T(8,128)(2,1)S(1)} %get-tuple-element.94), channel_id=1, source_target_pairs={{0,2},{2,0},{4,6},{6,4},{8,10},{10,8},{12,14},{14,12},{1,3},{3,1},... | collective-permute-start | bytes 786440 | tf_op jit(solution)/shard_map/ppermute | solution.py:36
  63.5 18.3 %collective-permute-start.18 = (bf16[64,2048]{1,0:T(8,128)(2,1)S(1)}, bf16[64,2048]{1,0:T(8,128)(2,1)S(1)}, u32[]{:S(2)}, u32[]{:S(2)}) collective-permute-start(bf16[64,2048]{1,0:T(8,128)(2,1)S(1)} %get-tuple-element.104), channel_id=1, source_target_pairs={{0,2},{2,0},{4,6},{6,4},{8,10},{10,8},{12,14},{14,12},{1,3},{3,1},... | collective-permute-start | bytes 786440 | tf_op jit(solution)/shard_map/ppermute | solution.py:36
  66.1 15.8 %collective-permute-start.19 = (bf16[64,2048]{1,0:T(8,128)(2,1)S(1)}, bf16[64,2048]{1,0:T(8,128)(2,1)S(1)}, u32[]{:S(2)}, u32[]{:S(2)}) collective-permute-start(bf16[64,2048]{1,0:T(8,128)(2,1)S(1)} %get-tuple-element.106), channel_id=1, source_target_pairs={{0,4},{2,6},{4,0},{6,2},{8,12},{10,14},{12,8},{14,10},{1,5},{3,7},... | collective-permute-start | bytes 786440 | tf_op jit(solution)/shard_map/ppermute | solution.py:36
  66.2 15.7 %collective-permute-start.20 = (bf16[64,2048]{1,0:T(8,128)(2,1)S(1)}, bf16[64,2048]{1,0:T(8,128)(2,1)S(1)}, u32[]{:S(2)}, u32[]{:S(2)}) collective-permute-start(bf16[64,2048]{1,0:T(8,128)(2,1)S(1)} %get-tuple-element.108), channel_id=1, source_target_pairs={{0,6},{2,4},{4,2},{6,0},{8,14},{10,12},{12,10},{14,8},{1,7},{3,5},... | collective-permute-start | bytes 786440 | tf_op jit(solution)/shard_map/ppermute | solution.py:36
  67.6 13.1 %collective-permute-start.17 = (f32[16,896]{1,0:T(8,128)S(1)}, f32[16,896]{1,0:T(8,128)S(1)}, u32[]{:S(2)}, u32[]{:S(2)}) collective-permute-start(f32[16,896]{1,0:T(8,128)S(1)} %get-tuple-element.89.mine_ref), channel_id=1, source_target_pairs={{0,1},{1,0},{2,3},{3,2},{4,5},{5,4},{6,7},{7,6},{8,9},{9,8},{10,11... | collective-permute-start | bytes 172040 | tf_op jit(solution)/shard_map/ppermute | solution.py:32
  72.6 31.8 %collective-permute-start.21 = (bf16[64,2048]{1,0:T(8,128)(2,1)S(1)}, bf16[64,2048]{1,0:T(8,128)(2,1)S(1)}, u32[]{:S(2)}, u32[]{:S(2)}) collective-permute-start(bf16[64,2048]{1,0:T(8,128)(2,1)S(1)} %get-tuple-element.96), channel_id=1, source_target_pairs={{0,8},{2,10},{4,12},{6,14},{8,0},{10,2},{12,4},{14,6},{1,9},{3,11}... | collective-permute-start | bytes 786440 | tf_op jit(solution)/shard_map/ppermute | solution.py:36
  82.8 21.6 %collective-permute-start.22 = (bf16[64,2048]{1,0:T(8,128)(2,1)S(1)}, bf16[64,2048]{1,0:T(8,128)(2,1)S(1)}, u32[]{:S(2)}, u32[]{:S(2)}) collective-permute-start(bf16[64,2048]{1,0:T(8,128)(2,1)S(1)} %get-tuple-element.109), channel_id=1, source_target_pairs={{0,8},{2,10},{4,12},{6,14},{8,0},{10,2},{12,4},{14,6},{1,9},{3,11}... | collective-permute-start | bytes 786440 | tf_op jit(solution)/shard_map/ppermute | solution.py:36
  85.5 5.5 %collective-permute-start.23 = (bf16[64,512]{1,0:T(8,128)(2,1)S(1)}, bf16[64,512]{1,0:T(8,128)(2,1)S(1)}, u32[]{:S(2)}, u32[]{:S(2)}) collective-permute-start(bf16[64,512]{1,0:T(8,128)(2,1)S(1)} %get-tuple-element.115), channel_id=1, source_target_pairs={{0,2},{2,0},{4,6},{6,4},{8,10},{10,8},{12,14},{14,12},{1,3},{3,1},... | collective-permute-start | bytes 196616 | tf_op jit(solution)/shard_map/ppermute | solution.py:36
  85.7 5.4 %collective-permute-start.24 = (bf16[64,512]{1,0:T(8,128)(2,1)S(1)}, bf16[64,512]{1,0:T(8,128)(2,1)S(1)}, u32[]{:S(2)}, u32[]{:S(2)}) collective-permute-start(bf16[64,512]{1,0:T(8,128)(2,1)S(1)} %get-tuple-element.116), channel_id=1, source_target_pairs={{0,4},{2,6},{4,0},{6,2},{8,12},{10,14},{12,8},{14,10},{1,5},{3,7},... | collective-permute-start | bytes 196616 | tf_op jit(solution)/shard_map/ppermute | solution.py:36
  86.1 12.3 %collective-permute-start.25 = (bf16[64,512]{1,0:T(8,128)(2,1)S(1)}, bf16[64,512]{1,0:T(8,128)(2,1)S(1)}, u32[]{:S(2)}, u32[]{:S(2)}) collective-permute-start(bf16[64,512]{1,0:T(8,128)(2,1)S(1)} %get-tuple-element.117), channel_id=1, source_target_pairs={{0,6},{2,4},{4,2},{6,0},{8,14},{10,12},{12,10},{14,8},{1,7},{3,5},... | collective-permute-start | bytes 196616 | tf_op jit(solution)/shard_map/ppermute | solution.py:36
  99.2 5.2 %collective-permute-start.26 = (bf16[64,512]{1,0:T(8,128)(2,1)S(1)}, bf16[64,512]{1,0:T(8,128)(2,1)S(1)}, u32[]{:S(2)}, u32[]{:S(2)}) collective-permute-start(bf16[64,512]{1,0:T(8,128)(2,1)S(1)} %get-tuple-element.119), channel_id=1, source_target_pairs={{0,8},{2,10},{4,12},{6,14},{8,0},{10,2},{12,4},{14,6},{1,9},{3,11}... | collective-permute-start | bytes 196616 | tf_op jit(solution)/shard_map/ppermute | solution.py:36

commit v10 on v9

--- a/solution.py
+++ b/solution.py
@@ -135,7 +135,7 @@
     for i, (first, last) in enumerate(((0, 1), (1, 3), (3, 5), (5, 7), (7, 8))):
         cut = pl.ds(first * unit, (last - first) * unit)
         x = pltpu.make_async_copy(x_hbm.at[:, cut], x_ref.at[:, cut], x_sem.at[i])
-        w = pltpu.make_async_copy(w_hbm.at[cut], w_ref.at[cut], w_sem.at[i])
+        w = pltpu.make_async_copy(w_hbm.at[cut, far], w_ref.at[cut], w_sem.at[i])
         x.start()
         w.start()
         copies.append((x, w, cut))
@@ -147,7 +147,7 @@
     for x, w, cut in copies:
         x.wait()
         w.wait()
-        term = _dot(x_ref[:, cut], w_ref[cut, far], NN)
+        term = _dot(x_ref[:, cut], w_ref[cut, :], NN)
         total = term if total is None else total + term
     far_ref[...] = total.astype(bf16)
 
@@ -386,15 +386,17 @@
     info = jnp.where(line == 6, spread_out(tenant_slot)[None, :], info)
     info = jnp.where(line == 0, own_tenants[None, :], info)
 
-    base_other, g_full, x_in, w_in = _call(
+    base_other, g_full, x_in = _call(
         functools.partial(base_kernel, z), "base", (1,),
         [pl.BlockSpec(memory_space=pl.ANY)] * 2 + [VMEM] * 2,
-        [_whole((rows, cols))] + [VMEM] * 3,
+        [_whole((rows, cols))] + [VMEM] * 2,
         [
             _shape((rows, cols), bf16), _shape((rows, 2 * cols), bf16), _shape(tokens.shape, bf16),
-            _shape(base_weight.shape, bf16),
         ],
-        [pltpu.SemaphoreType.DMA((5,)), pltpu.SemaphoreType.DMA((5,))],
+        [
+            pltpu.VMEM((width, cols), bf16),
+            pltpu.SemaphoreType.DMA((5,)), pltpu.SemaphoreType.DMA((5,)),
+        ],
         vmem=BIG_VMEM,
     )(
         _tie(info, shard if shared else packet),
@@ -453,11 +455,12 @@
         return _call(
             functools.partial(through_kernel, z, first), "through", (1,), [VMEM] * 2,
             [VMEM] * (1 + with_sums), [_shape((rows, wide), f32)] + [sums] * with_sums, [],
-        )(info, g_full, w_in)
+        )(info, g_full, base_weight)
 
     half = width // 2
     wide_a = half
     sends_a = pack(_tie(info, *ready), 0, wide_a)
+    got_a = to_near(sends_a)
     low, sums = through(_tie(info, sends_a[0]), 0, half, 1)
 
     if shared:
@@ -467,7 +470,7 @@
             [VMEM] * 3, [_whole(block)] * 4, [_shape(block, bf16)] * 4, [],
             n_scalars=2,
         )(_tie(info, low), info_x, shard, shard_far, farther)
-        got_y = _xor(chosen[1], n_dp, 1)
+        got_y = _xor(_tie(chosen[1], got_a[2]), n_dp, 1)
         got_x = _swap(chosen[2], "groups")
         got_d = lax.ppermute(
             chosen[3],
@@ -483,14 +486,18 @@
 
     sends_b = pack(_tie(info, after_choose), wide_a, width - wide_a)
 
-    got_a = [sends_a[0], None] + [_xor(sends_a[k], n_dp, k) for k in range(2, NEAR)]
-    got_a[1] = _xor(_tie(sends_a[1], sends_b[0], got_a[2]), n_dp, 1)
-
     base_own = _call(
         functools.partial(own_kernel, z), "base_own", (1,),
         [VMEM] * 3, VMEM, _shape((rows, cols), f32), [],
-    )(_tie(info, sends_b[0]), x_in, w_in, base_arrived)
-    (high,) = through(_tie(info, base_own), half, width - half, 0)
+    )(_tie(info, sends_b[0]), x_in, base_weight, base_arrived)
+    dense_a = dense(_tie(info, base_own), got_a)
+    far_a = to_far(dense_a)
+
+    gate = [dense_a[1]] + ([got_y] if shared else [])
+    got_b = to_near(
+        [_tie(b, *gate) if k in (1, 3) else _tie(b, dense_a[1]) for k, b in enumerate(sends_b)]
+    )
+    (high,) = through(_tie(info, dense_a[1]), half, width - half, 0)
 
     if shared:
         got_down = [chosen[0], got_y, got_x, got_d]
@@ -501,16 +508,13 @@
     )(_tie(info, high), x_in, *got_down)
     shrink_other = _swap(shrink_part, "tensor")
 
-    dense_a = dense(_tie(info, shrink_part), got_a)
-    far_a = to_far(dense_a)
-    got_b = to_near([_tie(b, shrink_part) for b in sends_b])
 
     step = min(512, width // 8)
     grad_tokens = _call(
         functools.partial(tokens_kernel, z), "token_grads", (width // step,),
         [VMEM] * 5, pl.BlockSpec((rows, step), lambda i, *_: (0, i)),
         _shape((rows, width), bf16), [pltpu.VMEM((nb * rank, rows), bf16)],
-    )(_tie(info, dense_a[1]), low, high, back_part, back_other, block_down)
+    )(_tie(info, shrink_part), low, high, back_part, back_other, block_down)
 
     up_sends = _call(
         functools.partial(pack_up_kernel, z, NEAR), "pack_up", (1,),

time: 106 us -> 103 us (0.972)
  the two profiles are of different devices: /device:TPU:26 before, /device:TPU:0 now
where the time goes in v10:
time: 103 us
  Pallas kernels  46.1 us (45%)
  starting transfers between devices  33.2 us (32%)
  waiting for transfers between devices  17.6 us (17%)
  other arithmetic  2.63 us (3%)
  local copies, waits for them, and re-layouts  2.33 us (2%)
    ppermute x20, starting transfers between devices, _xor(): return lax.ppermute(x, 'dp', [(i, i ^ k) for i in range(n)])  28.9 us
    ppermute x20, waiting for transfers between devices, _xor(): return lax.ppermute(x, 'dp', [(i, i ^ k) for i in range(n)])  16.5 us
    pallas_call x2, Pallas kernels, through(): _call(functools.partial(through_kernel, z, first), 'through', (1,), [VMEM...  9.57 us
    pallas_call x1, Pallas kernels, on_device(): _call(functools.partial(base_kernel, z), 'base', (1,), [pl.BlockSpec(memo...  7.77 us
    pallas_call x1, Pallas kernels, on_device(): _call(functools.partial(tokens_kernel, z), 'token_grads', (width // step,...  7.7 us
    pallas_call x1, Pallas kernels, on_device(): _call(functools.partial(own_kernel, z), 'base_own', (1,), [VMEM] * 3, VME...  4.61 us
    pallas_call x2, Pallas kernels, pack(): _call(functools.partial(pack_kernel, z, NEAR, start), 'pack_down', (1,),...  3.93 us
    ppermute x6, starting transfers between devices, _swap(): return lax.ppermute(x, axis, [(0, 1), (1, 0)])  3.34 us
  transfers between devices with their start and end apart: 27, of which 8 were waited for; matrix products, arithmetic and copies ran while one was open for 4% of the time, Pallas kernels for 43%

profile of v10, /device:TPU:0, one launch (start us, length us, event | category | flops | bytes accessed | tf_op | source)
XLA Modules:
  0.0 102.9 jit_solution(18405025746321428241)
XLA Ops:
  0.6 4.1 %collective-permute-start = (bf16[4,16,512]{2,1,0:T(8,128)(2,1)}, bf16[4,16,512]{2,1,0:T(8,128)(2,1)S(1)}, u32[]{:S(2)}, u32[]{:S(2)}) collective-permute-start(bf16[4,16,512]{2,1,0:T(8,128)(2,1)} %param.11), channel_id=1, source_target_pairs={{0,8},{2,10},{4,12},{6,14},{8,0},{10,2},{12,4},{14,6},{1,9},{3,11}... | collective-permute-start | bytes 196616 | tf_op jit(solution)/shard_map/ppermute | solution.py:36
  5.7 1.6 %collective-permute-start.2 = (bf16[4,16,1024]{2,1,0:T(8,128)(2,1)S(1)}, bf16[4,16,1024]{2,1,0:T(8,128)(2,1)S(1)}, u32[]{:S(2)}, u32[]{:S(2)}) collective-permute-start(bf16[4,16,1024]{2,1,0:T(8,128)(2,1)S(1)} %get-tuple-element.121), channel_id=1, source_target_pairs={{0,2},{2,0},{4,6},{6,4},{8,10},{10,8},{12,14},{14,12},{1,3},{3,1},... | collective-permute-start | bytes 393224 | tf_op jit(solution)/shard_map/ppermute | solution.py:36
  8.9 1.8 %collective-permute-done.2 = bf16[4,16,1024]{2,1,0:T(8,128)(2,1)S(1)} collective-permute-done((bf16[4,16,1024]{2,1,0:T(8,128)(2,1)S(1)}, bf16[4,16,1024]{2,1,0:T(8,128)(2,1)S(1)}, u32[]{:S(2)}, u32[]{:S(2)}) %collective-permute-start.2) | collective-permute-done | bytes 131104 | tf_op jit(solution)/shard_map/ppermute | solution.py:36
  12.0 1.6 %collective-permute-start.5 = (bf16[144,512]{1,0:T(8,128)(2,1)S(1)}, bf16[144,512]{1,0:T(8,128)(2,1)S(1)}, u32[]{:S(2)}, u32[]{:S(2)}) collective-permute-start(bf16[144,512]{1,0:T(8,128)(2,1)S(1)} %pad_maximum_fusion.2.refs_0_), channel_id=1, source_target_pairs={{0,2},{2,0},{4,6},{6,4},{8,10},{10,8},{12,14},{14,12},{1,3},{3,1},... | collective-permute-start | bytes 442376 | tf_op jit(solution)/shard_map/ppermute | solution.py:36
  13.6 1.6 %collective-permute-start.4 = (bf16[144,512]{1,0:T(8,128)(2,1)S(1)}, bf16[144,512]{1,0:T(8,128)(2,1)S(1)}, u32[]{:S(2)}, u32[]{:S(2)}) collective-permute-start(bf16[144,512]{1,0:T(8,128)(2,1)S(1)} %pad_maximum_fusion.2.refs_0_), channel_id=1, source_target_pairs={{0,4},{2,6},{4,0},{6,2},{8,12},{10,14},{12,8},{14,10},{1,5},{3,7},... | collective-permute-start | bytes 442376 | tf_op jit(solution)/shard_map/ppermute | solution.py:36
  15.6 1.3 %copy-done = bf16[896,512]{1,0:T(8,128)(2,1)S(1)} copy-done((bf16[896,512]{1,0:T(8,128)(2,1)S(1)}, bf16[896,512]{1,0:T(8,128)(2,1)}, u32[]{:S(2)}) %copy-start) | copy-done | bytes 917528
  17.0 7.8 %base.1 = (bf16[896,512]{1,0:T(8,128)(2,1)S(1)}, bf16[896,1024]{1,0:T(8,128)(2,1)S(1)}, bf16[896,4096]{1,0:T(8,128)(2,1)S(1)}) custom-call(s32[16,128]{1,0:T(8,128)S(1)} %select_select_fusion.1.info, bf16[896,4096]{1,0:T(8,128)(2,1)} %x_hbm.1, bf16[4096,1024]{1,0:T(8,128)(2,1)} %w_ref.5, bf16[896,512]{1,0:T(8,128)(2,1)S(1)} %copy-done, ...), custom_call_target="tpu_custom_call" | custom-call | flops 1 | bytes 1 | tf_op jit(solution)/shard_map/base/pallas_call | solution.py:389
  27.9 1.0 %collective-permute-done.8.other_ref = f32[16,896]{1,0:T(8,128)S(1)} collective-permute-done((f32[16,896]{1,0:T(8,128)S(1)}, f32[16,896]{1,0:T(8,128)S(1)}, u32[]{:S(2)}, u32[]{:S(2)}) %collective-permute-start.8) | collective-permute-done | bytes 57376 | tf_op jit(solution)/shard_map/ppermute | solution.py:32
  29.0 2.0 %pack_down.2 = (bf16[64,2048]{1,0:T(8,128)(2,1)S(1)}, bf16[64,2048]{1,0:T(8,128)(2,1)S(1)}, bf16[64,2048]{1,0:T(8,128)(2,1)S(1)}, bf16[64,2048]{1,0:T(8,128)(2,1)S(1)}) custom-call(s32[16,128]{1,0:T(8,128)S(1)} %select_select_fusion.info, f32[16,896]{1,0:T(8,128)S(1)} %get-tuple-element.71.mine_ref, f32[16,896]{1,0:T(8,128)S(1)} %collective-permute-done.8.other_ref, ...), custom_call_target="tpu_custom_call" | custom-call | flops 1 | bytes 1 | tf_op jit(solution)/shard_map/pack_down/pallas_call | solution.py:431
  30.9 1.3 %collective-permute-start.12 = (bf16[64,2048]{1,0:T(8,128)(2,1)S(1)}, bf16[64,2048]{1,0:T(8,128)(2,1)S(1)}, u32[]{:S(2)}, u32[]{:S(2)}) collective-permute-start(bf16[64,2048]{1,0:T(8,128)(2,1)S(1)} %get-tuple-element.85), channel_id=1, source_target_pairs={{0,4},{2,6},{4,0},{6,2},{8,12},{10,14},{12,8},{14,10},{1,5},{3,7},... | collective-permute-start | bytes 786440 | tf_op jit(solution)/shard_map/ppermute | solution.py:36
  32.2 1.1 %collective-permute-start.11 = (bf16[64,2048]{1,0:T(8,128)(2,1)S(1)}, bf16[64,2048]{1,0:T(8,128)(2,1)S(1)}, u32[]{:S(2)}, u32[]{:S(2)}) collective-permute-start(bf16[64,2048]{1,0:T(8,128)(2,1)S(1)} %get-tuple-element.84), channel_id=1, source_target_pairs={{0,2},{2,0},{4,6},{6,4},{8,10},{10,8},{12,14},{14,12},{1,3},{3,1},... | collective-permute-start | bytes 786440 | tf_op jit(solution)/shard_map/ppermute | solution.py:36
  33.3 1.2 %collective-permute-start.13 = (bf16[64,2048]{1,0:T(8,128)(2,1)S(1)}, bf16[64,2048]{1,0:T(8,128)(2,1)S(1)}, u32[]{:S(2)}, u32[]{:S(2)}) collective-permute-start(bf16[64,2048]{1,0:T(8,128)(2,1)S(1)} %get-tuple-element.86), channel_id=1, source_target_pairs={{0,6},{2,4},{4,2},{6,0},{8,14},{10,12},{12,10},{14,8},{1,7},{3,5},... | collective-permute-start | bytes 786440 | tf_op jit(solution)/shard_map/ppermute | solution.py:36
  34.5 1.5 %collective-permute-start.9 = (s32[16,128]{1,0:T(8,128)S(1)}, s32[16,128]{1,0:T(8,128)S(1)}, u32[]{:S(2)}, u32[]{:S(2)}) collective-permute-start(s32[16,128]{1,0:T(8,128)S(1)} %select_select_fusion.info), channel_id=1, source_target_pairs={{0,16},{16,0},{1,17},{17,1},{2,18},{18,2},{3,19},{19,3},{4,20},{20... | collective-permute-start | bytes 24584 | tf_op jit(solution)/shard_map/ppermute | solution.py:32
  36.0 4.7 %through.2 = (f32[896,2048]{1,0:T(8,128)S(1)}, bf16[2,64,128]{2,1,0:T(8,128)(2,1)S(1)}) custom-call(s32[16,128]{1,0:T(8,128)S(1)} %select_select_fusion.info, bf16[896,1024]{1,0:T(8,128)(2,1)S(1)} %get-tuple-element.75.g_ref, bf16[4096,1024]{1,0:T(8,128)(2,1)S(1)} %bitcast.20), custom_call_target="tpu_custom_call" | custom-call | flops 1 | bytes 1 | tf_op jit(solution)/shard_map/through/pallas_call | solution.py:455
  40.8 1.0 %choose.1 = (bf16[112,1024]{1,0:T(8,128)(2,1)S(1)}, bf16[112,1024]{1,0:T(8,128)(2,1)S(1)}, bf16[112,1024]{1,0:T(8,128)(2,1)S(1)}, bf16[112,1024]{1,0:T(8,128)(2,1)S(1)}) custom-call(s32[16,128]{1,0:T(8,128)S(1)} %select_select_fusion.info, s32[16,128]{1,0:T(8,128)S(1)} %collective-permute-done.9.info_x, bf16[8,16,1024]{2,1,0:T(8,128)(2,1)S(1)} %pad_maximum_fusion.1.own_ref, ...), custom_call_target="tpu_custom_call" | custom-call | flops 1 | bytes 1 | tf_op jit(solution)/shard_map/choose/pallas_call | solution.py:468
  41.8 4.4 %collective-permute-done.12.refs_2_ = bf16[64,2048]{1,0:T(8,128)(2,1)S(1)} collective-permute-done((bf16[64,2048]{1,0:T(8,128)(2,1)S(1)}, bf16[64,2048]{1,0:T(8,128)(2,1)S(1)}, u32[]{:S(2)}, u32[]{:S(2)}) %collective-permute-start.12) | collective-permute-done | bytes 262176 | tf_op jit(solution)/shard_map/ppermute | solution.py:36
  47.2 1.5 %collective-permute-start.15 = (bf16[112,1024]{1,0:T(8,128)(2,1)S(1)}, bf16[112,1024]{1,0:T(8,128)(2,1)S(1)}, u32[]{:S(2)}, u32[]{:S(2)}) collective-permute-start(bf16[112,1024]{1,0:T(8,128)(2,1)S(1)} %get-tuple-element.92), channel_id=1, source_target_pairs={{0,16},{16,0},{1,17},{17,1},{2,18},{18,2},{3,19},{19,3},{4,20},{20... | collective-permute-start | bytes 688136 | tf_op jit(solution)/shard_map/ppermute | solution.py:32
  49.7 2.0 %pack_down.3 = (bf16[64,2048]{1,0:T(8,128)(2,1)S(1)}, bf16[64,2048]{1,0:T(8,128)(2,1)S(1)}, bf16[64,2048]{1,0:T(8,128)(2,1)S(1)}, bf16[64,2048]{1,0:T(8,128)(2,1)S(1)}) custom-call(s32[16,128]{1,0:T(8,128)S(1)} %select_select_fusion.info, f32[16,896]{1,0:T(8,128)S(1)} %get-tuple-element.71.mine_ref, f32[16,896]{1,0:T(8,128)S(1)} %collective-permute-done.8.other_ref, ...), custom_call_target="tpu_custom_call" | custom-call | flops 1 | bytes 1 | tf_op jit(solution)/shard_map/pack_down/pallas_call | solution.py:431
  51.7 4.6 %base_own.1.base_ref = f32[896,512]{1,0:T(8,128)S(1)} custom-call(s32[16,128]{1,0:T(8,128)S(1)} %select_select_fusion.info, bf16[896,4096]{1,0:T(8,128)(2,1)S(1)} %get-tuple-element.72.x_ref, bf16[4096,1024]{1,0:T(8,128)(2,1)S(1)} %bitcast.20, bf16[896,512]{1,0:T(8,128)(2,1)S(1)} %collective-permute-done.7.far_ref), custom_call_target="tpu_custom_call" | custom-call | flops 1 | bytes 1 | tf_op jit(solution)/shard_map/base_own/pallas_call | solution.py:489
  58.1 3.3 %collective-permute-done.14.refs_1_ = bf16[112,1024]{1,0:T(8,128)(2,1)S(1)} collective-permute-done((bf16[112,1024]{1,0:T(8,128)(2,1)S(1)}, bf16[112,1024]{1,0:T(8,128)(2,1)S(1)}, u32[]{:S(2)}, u32[]{:S(2)}) %collective-permute-start.14) | collective-permute-done | bytes 229408 | tf_op jit(solution)/shard_map/ppermute | solution.py:36
  61.8 2.5 %collective-permute-start.20 = (bf16[64,2048]{1,0:T(8,128)(2,1)S(1)}, bf16[64,2048]{1,0:T(8,128)(2,1)S(1)}, u32[]{:S(2)}, u32[]{:S(2)}) collective-permute-start(bf16[64,2048]{1,0:T(8,128)(2,1)S(1)} %get-tuple-element.106), channel_id=1, source_target_pairs={{0,6},{2,4},{4,2},{6,0},{8,14},{10,12},{12,10},{14,8},{1,7},{3,5},... | collective-permute-start | bytes 786440 | tf_op jit(solution)/shard_map/ppermute | solution.py:36
  64.4 4.8 %through.3.high_ref = f32[896,2048]{1,0:T(8,128)S(1)} custom-call(s32[16,128]{1,0:T(8,128)S(1)} %select_select_fusion.info, bf16[896,1024]{1,0:T(8,128)(2,1)S(1)} %get-tuple-element.75.g_ref, bf16[4096,1024]{1,0:T(8,128)(2,1)S(1)} %bitcast.20), custom_call_target="tpu_custom_call" | custom-call | flops 1 | bytes 1 | tf_op jit(solution)/shard_map/through/pallas_call | solution.py:455
  69.2 2.8 %shrink.1 = (bf16[112,4096]{1,0:T(8,128)(2,1)S(1)}, f32[16,896]{1,0:T(8,128)S(1)}) custom-call(s32[16,128]{1,0:T(8,128)S(1)} %select_select_fusion.info, bf16[896,4096]{1,0:T(8,128)(2,1)S(1)} %get-tuple-element.72.x_ref, bf16[112,1024]{1,0:T(8,128)(2,1)S(1)} %get-tuple-element.78.refs_0_, bf16[112,1024]{1,0:T(8,128)(2,1)S(1)} %collective-permute-done.14.refs_1_, ...), custom_call_target="tpu_custom_call" | custom-call | flops 1 | bytes 1 | tf_op jit(solution)/shard_map/shrink/pallas_call | solution.py:504
  72.1 2.0 %collective-permute-start.21 = (bf16[64,2048]{1,0:T(8,128)(2,1)S(1)}, bf16[64,2048]{1,0:T(8,128)(2,1)S(1)}, u32[]{:S(2)}, u32[]{:S(2)}) collective-permute-start(bf16[64,2048]{1,0:T(8,128)(2,1)S(1)} %get-tuple-element.87), channel_id=1, source_target_pairs={{0,8},{2,10},{4,12},{6,14},{8,0},{10,2},{12,4},{14,6},{1,9},{3,11}... | collective-permute-start | bytes 786440 | tf_op jit(solution)/shard_map/ppermute | solution.py:36
  74.2 7.7 %token_grads.1 = bf16[896,4096]{1,0:T(8,128)(2,1)} custom-call(s32[16,128]{1,0:T(8,128)S(1)} %select_select_fusion.info, f32[896,2048]{1,0:T(8,128)S(1)} %get-tuple-element.76.low_ref, f32[896,2048]{1,0:T(8,128)S(1)} %through.3.high_ref, f32[16,896]{1,0:T(8,128)S(1)} %get-tuple-element.71.mine_ref, f32[16,896]{1,0:T(8,128)S(1)} %collective-permute-done.8.other_ref, ...), custom_call_target="tpu_custom_call" | custom-call | flops 1 | bytes 1 | tf_op jit(solution)/shard_map/token_grads/pallas_call | solution.py:513
  81.9 1.1 %pack_up.1 = (bf16[64,512]{1,0:T(8,128)(2,1)S(1)}, bf16[64,512]{1,0:T(8,128)(2,1)S(1)}, bf16[64,512]{1,0:T(8,128)(2,1)S(1)}, bf16[64,512]{1,0:T(8,128)(2,1)S(1)}) custom-call(s32[16,128]{1,0:T(8,128)S(1)} %select_select_fusion.info, f32[16,896]{1,0:T(8,128)S(1)} %get-tuple-element.94.mine_ref, f32[16,896]{1,0:T(8,128)S(1)} %collective-permute-done.17.other_ref, ...), custom_call_target="tpu_custom_call" | custom-call | flops 1 | bytes 1 | tf_op jit(solution)/shard_map/pack_up/pallas_call | solution.py:519
  86.0 2.5 %collective-permute-start.25 = (bf16[64,512]{1,0:T(8,128)(2,1)S(1)}, bf16[64,512]{1,0:T(8,128)(2,1)S(1)}, u32[]{:S(2)}, u32[]{:S(2)}) collective-permute-start(bf16[64,512]{1,0:T(8,128)(2,1)S(1)} %get-tuple-element.115), channel_id=1, source_target_pairs={{0,6},{2,4},{4,2},{6,0},{8,14},{10,12},{12,10},{14,8},{1,7},{3,5},... | collective-permute-start | bytes 196616 | tf_op jit(solution)/shard_map/ppermute | solution.py:36
  88.5 2.0 %projected.1 = bf16[896,512]{1,0:T(8,128)(2,1)} custom-call(s32[16,128]{1,0:T(8,128)S(1)} %select_select_fusion.info, f32[896,512]{1,0:T(8,128)S(1)} %base_own.1.base_ref, f32[16,896]{1,0:T(8,128)S(1)} %get-tuple-element.94.mine_ref, f32[16,896]{1,0:T(8,128)S(1)} %collective-permute-done.17.other_ref, bf16[112,512]{1,0:T(8,128)(2,1)S(1)} %get-tuple-element.109.up_ref), custom_call_target="tpu_custom_call" | custom-call | flops 1 | bytes 1 | tf_op jit(solution)/shard_map/projected/pallas_call | solution.py:530
  90.6 2.5 %collective-permute-done.24.refs_2_ = bf16[64,512]{1,0:T(8,128)(2,1)S(1)} collective-permute-done((bf16[64,512]{1,0:T(8,128)(2,1)S(1)}, bf16[64,512]{1,0:T(8,128)(2,1)S(1)}, u32[]{:S(2)}, u32[]{:S(2)}) %collective-permute-start.24) | collective-permute-done | bytes 65568 | tf_op jit(solution)/shard_map/ppermute | solution.py:36
  94.6 3.5 %collective-permute-start.26 = (bf16[64,512]{1,0:T(8,128)(2,1)S(1)}, bf16[64,512]{1,0:T(8,128)(2,1)S(1)}, u32[]{:S(2)}, u32[]{:S(2)}) collective-permute-start(bf16[64,512]{1,0:T(8,128)(2,1)S(1)} %get-tuple-element.117), channel_id=1, source_target_pairs={{0,8},{2,10},{4,12},{6,14},{8,0},{10,2},{12,4},{14,6},{1,9},{3,11}... | collective-permute-start | bytes 196616 | tf_op jit(solution)/shard_map/ppermute | solution.py:36
  98.1 3.0 %collective-permute-done.26.refs_5_ = bf16[64,512]{1,0:T(8,128)(2,1)S(1)} collective-permute-done((bf16[64,512]{1,0:T(8,128)(2,1)S(1)}, bf16[64,512]{1,0:T(8,128)(2,1)S(1)}, u32[]{:S(2)}, u32[]{:S(2)}) %collective-permute-start.26) | collective-permute-done | bytes 65568 | tf_op jit(solution)/shard_map/ppermute | solution.py:36
  101.1 1.8 %final.1 = (f32[64,4096]{1,0:T(8,128)}, f32[64,512]{1,0:T(8,128)}) custom-call(s32[16,128]{1,0:T(8,128)S(1)} %select_select_fusion.info, f32[64,2048]{1,0:T(8,128)S(1)} %get-tuple-element.110.refs_0_, bf16[64,2048]{1,0:T(8,128)(2,1)S(1)} %collective-permute-done.21.refs_1_, f32[64,2048]{1,0:T(8,128)S(1)} %get-tuple-element.111.refs_2_, ...), custom_call_target="tpu_custom_call" | custom-call | flops 1 | bytes 1 | tf_op jit(solution)/shard_map/final/pallas_call | solution.py:542
  (64 shorter events, 16.2 us)
Async XLA Ops:
  0.6 10.5 %collective-permute-start = (bf16[4,16,512]{2,1,0:T(8,128)(2,1)}, bf16[4,16,512]{2,1,0:T(8,128)(2,1)S(1)}, u32[]{:S(2)}, u32[]{:S(2)}) collective-permute-start(bf16[4,16,512]{2,1,0:T(8,128)(2,1)} %param.11), channel_id=1, source_target_pairs={{0,8},{2,10},{4,12},{6,14},{8,0},{10,2},{12,4},{14,6},{1,9},{3,11}... | collective-permute-start | bytes 196616 | tf_op jit(solution)/shard_map/ppermute | solution.py:36
  5.7 5.0 %collective-permute-start.2 = (bf16[4,16,1024]{2,1,0:T(8,128)(2,1)S(1)}, bf16[4,16,1024]{2,1,0:T(8,128)(2,1)S(1)}, u32[]{:S(2)}, u32[]{:S(2)}) collective-permute-start(bf16[4,16,1024]{2,1,0:T(8,128)(2,1)S(1)} %get-tuple-element.121), channel_id=1, source_target_pairs={{0,2},{2,0},{4,6},{6,4},{8,10},{10,8},{12,14},{14,12},{1,3},{3,1},... | collective-permute-start | bytes 393224 | tf_op jit(solution)/shard_map/ppermute | solution.py:36
  7.3 8.3 %collective-permute-start.3 = (bf16[896,512]{1,0:T(8,128)(2,1)}, bf16[896,512]{1,0:T(8,128)(2,1)S(1)}, u32[]{:S(2)}, u32[]{:S(2)}) collective-permute-start(bf16[896,512]{1,0:T(8,128)(2,1)} %g_ref.3), channel_id=1, source_target_pairs={{0,1},{1,0},{2,3},{3,2},{4,5},{5,4},{6,7},{7,6},{8,9},{9,8},{10,11... | collective-permute-start | bytes 2752520 | tf_op jit(solution)/shard_map/ppermute | solution.py:32
  10.8 14.0 %collective-permute-start.6 = (bf16[8,16,1024]{2,1,0:T(8,128)(2,1)S(1)}, bf16[8,16,1024]{2,1,0:T(8,128)(2,1)S(1)}, u32[]{:S(2)}, u32[]{:S(2)}) collective-permute-start(bf16[8,16,1024]{2,1,0:T(8,128)(2,1)S(1)} %pad_maximum_fusion.1.own_ref), channel_id=1, source_target_pairs={{0,8},{2,10},{4,12},{6,14},{8,0},{10,2},{12,4},{14,6},{1,9},{3,11}... | collective-permute-start | bytes 786440 | tf_op jit(solution)/shard_map/ppermute | solution.py:36
  12.0 12.8 %collective-permute-start.5 = (bf16[144,512]{1,0:T(8,128)(2,1)S(1)}, bf16[144,512]{1,0:T(8,128)(2,1)S(1)}, u32[]{:S(2)}, u32[]{:S(2)}) collective-permute-start(bf16[144,512]{1,0:T(8,128)(2,1)S(1)} %pad_maximum_fusion.2.refs_0_), channel_id=1, source_target_pairs={{0,2},{2,0},{4,6},{6,4},{8,10},{10,8},{12,14},{14,12},{1,3},{3,1},... | collective-permute-start | bytes 442376 | tf_op jit(solution)/shard_map/ppermute | solution.py:36
  13.6 11.2 %collective-permute-start.4 = (bf16[144,512]{1,0:T(8,128)(2,1)S(1)}, bf16[144,512]{1,0:T(8,128)(2,1)S(1)}, u32[]{:S(2)}, u32[]{:S(2)}) collective-permute-start(bf16[144,512]{1,0:T(8,128)(2,1)S(1)} %pad_maximum_fusion.2.refs_0_), channel_id=1, source_target_pairs={{0,4},{2,6},{4,0},{6,2},{8,12},{10,14},{12,8},{14,10},{1,5},{3,7},... | collective-permute-start | bytes 442376 | tf_op jit(solution)/shard_map/ppermute | solution.py:36
  15.2 10.4 %collective-permute-start.1 = (bf16[144,512]{1,0:T(8,128)(2,1)S(1)}, bf16[144,512]{1,0:T(8,128)(2,1)S(1)}, u32[]{:S(2)}, u32[]{:S(2)}) collective-permute-start(bf16[144,512]{1,0:T(8,128)(2,1)S(1)} %pad_maximum_fusion.2.refs_0_), channel_id=1, source_target_pairs={{0,6},{2,4},{4,2},{6,0},{8,14},{10,12},{12,10},{14,8},{1,7},{3,5},... | collective-permute-start | bytes 442376 | tf_op jit(solution)/shard_map/ppermute | solution.py:36
  15.6 20.4 %slice-start = ((s8[8388608]{0:T(1024)(128)(4,1)}), s8[4194304]{0:T(1024)(128)(4,1)S(1)}, s32[]{:S(2)}) async-start(s8[8388608]{0:T(1024)(128)(4,1)} %bitcast.19), calls=%async_computation | async-start | bytes 8388608
  15.6 20.4 %slice-start.1 = ((s8[8388608]{0:T(1024)(128)(4,1)}), s8[4194304]{0:T(1024)(128)(4,1)S(1)}, s32[]{:S(2)}) async-start(s8[8388608]{0:T(1024)(128)(4,1)} %bitcast.19), calls=%async_computation.1 | async-start | bytes 8388608
  15.6 1.3 %copy-start = (bf16[896,512]{1,0:T(8,128)(2,1)S(1)}, bf16[896,512]{1,0:T(8,128)(2,1)}, u32[]{:S(2)}) copy-start(bf16[896,512]{1,0:T(8,128)(2,1)} %g_ref.3) | copy-start | bytes 2752516
  24.7 3.2 %collective-permute-start.7 = (bf16[896,512]{1,0:T(8,128)(2,1)S(1)}, bf16[896,512]{1,0:T(8,128)(2,1)S(1)}, u32[]{:S(2)}, u32[]{:S(2)}) collective-permute-start(bf16[896,512]{1,0:T(8,128)(2,1)S(1)} %get-tuple-element.63), channel_id=1, source_target_pairs={{0,1},{1,0},{2,3},{3,2},{4,5},{5,4},{6,7},{7,6},{8,9},{9,8},{10,11... | collective-permute-start | bytes 2752520 | tf_op jit(solution)/shard_map/ppermute | solution.py:32
  25.7 15.0 %collective-permute-start.10 = (bf16[16,16,1024]{2,1,0:T(8,128)(2,1)S(1)}, bf16[16,16,1024]{2,1,0:T(8,128)(2,1)S(1)}, u32[]{:S(2)}, u32[]{:S(2)}) collective-permute-start(bf16[16,16,1024]{2,1,0:T(8,128)(2,1)S(1)} %pad_maximum_fusion), channel_id=1, source_target_pairs={{0,4},{2,6},{4,0},{6,2},{8,12},{10,14},{12,8},{14,10},{1,5},{3,7},... | collective-permute-start | bytes 1572872 | tf_op jit(solution)/shard_map/ppermute | solution.py:36
  27.7 1.3 %collective-permute-start.8 = (f32[16,896]{1,0:T(8,128)S(1)}, f32[16,896]{1,0:T(8,128)S(1)}, u32[]{:S(2)}, u32[]{:S(2)}) collective-permute-start(f32[16,896]{1,0:T(8,128)S(1)} %get-tuple-element.71.mine_ref), channel_id=1, source_target_pairs={{0,1},{1,0},{2,3},{3,2},{4,5},{5,4},{6,7},{7,6},{8,9},{9,8},{10,11... | collective-permute-start | bytes 172040 | tf_op jit(solution)/shard_map/ppermute | solution.py:32
  30.9 15.3 %collective-permute-start.12 = (bf16[64,2048]{1,0:T(8,128)(2,1)S(1)}, bf16[64,2048]{1,0:T(8,128)(2,1)S(1)}, u32[]{:S(2)}, u32[]{:S(2)}) collective-permute-start(bf16[64,2048]{1,0:T(8,128)(2,1)S(1)} %get-tuple-element.85), channel_id=1, source_target_pairs={{0,4},{2,6},{4,0},{6,2},{8,12},{10,14},{12,8},{14,10},{1,5},{3,7},... | collective-permute-start | bytes 786440 | tf_op jit(solution)/shard_map/ppermute | solution.py:36
  32.2 24.1 %collective-permute-start.11 = (bf16[64,2048]{1,0:T(8,128)(2,1)S(1)}, bf16[64,2048]{1,0:T(8,128)(2,1)S(1)}, u32[]{:S(2)}, u32[]{:S(2)}) collective-permute-start(bf16[64,2048]{1,0:T(8,128)(2,1)S(1)} %get-tuple-element.84), channel_id=1, source_target_pairs={{0,2},{2,0},{4,6},{6,4},{8,10},{10,8},{12,14},{14,12},{1,3},{3,1},... | collective-permute-start | bytes 786440 | tf_op jit(solution)/shard_map/ppermute | solution.py:36
  33.3 23.0 %collective-permute-start.13 = (bf16[64,2048]{1,0:T(8,128)(2,1)S(1)}, bf16[64,2048]{1,0:T(8,128)(2,1)S(1)}, u32[]{:S(2)}, u32[]{:S(2)}) collective-permute-start(bf16[64,2048]{1,0:T(8,128)(2,1)S(1)} %get-tuple-element.86), channel_id=1, source_target_pairs={{0,6},{2,4},{4,2},{6,0},{8,14},{10,12},{12,10},{14,8},{1,7},{3,5},... | collective-permute-start | bytes 786440 | tf_op jit(solution)/shard_map/ppermute | solution.py:36
  34.5 6.2 %collective-permute-start.9 = (s32[16,128]{1,0:T(8,128)S(1)}, s32[16,128]{1,0:T(8,128)S(1)}, u32[]{:S(2)}, u32[]{:S(2)}) collective-permute-start(s32[16,128]{1,0:T(8,128)S(1)} %select_select_fusion.info), channel_id=1, source_target_pairs={{0,16},{16,0},{1,17},{17,1},{2,18},{18,2},{3,19},{19,3},{4,20},{20... | collective-permute-start | bytes 24584 | tf_op jit(solution)/shard_map/ppermute | solution.py:32
  46.2 15.1 %collective-permute-start.14 = (bf16[112,1024]{1,0:T(8,128)(2,1)S(1)}, bf16[112,1024]{1,0:T(8,128)(2,1)S(1)}, u32[]{:S(2)}, u32[]{:S(2)}) collective-permute-start(bf16[112,1024]{1,0:T(8,128)(2,1)S(1)} %get-tuple-element.91), channel_id=1, source_target_pairs={{0,2},{2,0},{4,6},{6,4},{8,10},{10,8},{12,14},{14,12},{1,3},{3,1},... | collective-permute-start | bytes 688136 | tf_op jit(solution)/shard_map/ppermute | solution.py:36
  47.2 22.0 %collective-permute-start.15 = (bf16[112,1024]{1,0:T(8,128)(2,1)S(1)}, bf16[112,1024]{1,0:T(8,128)(2,1)S(1)}, u32[]{:S(2)}, u32[]{:S(2)}) collective-permute-start(bf16[112,1024]{1,0:T(8,128)(2,1)S(1)} %get-tuple-element.92), channel_id=1, source_target_pairs={{0,16},{16,0},{1,17},{17,1},{2,18},{18,2},{3,19},{19,3},{4,20},{20... | collective-permute-start | bytes 688136 | tf_op jit(solution)/shard_map/ppermute | solution.py:32
  48.7 20.5 %collective-permute-start.16 = (bf16[112,1024]{1,0:T(8,128)(2,1)S(1)}, bf16[112,1024]{1,0:T(8,128)(2,1)S(1)}, u32[]{:S(2)}, u32[]{:S(2)}) collective-permute-start(bf16[112,1024]{1,0:T(8,128)(2,1)S(1)} %get-tuple-element.93), channel_id=1, source_target_pairs={{0,18},{2,16},{4,22},{6,20},{8,26},{10,24},{12,30},{14,28},{16,2},... | collective-permute-start | bytes 688136 | tf_op jit(solution)/shard_map/ppermute | solution.py:475
  57.3 25.7 %collective-permute-start.19 = (bf16[64,2048]{1,0:T(8,128)(2,1)S(1)}, bf16[64,2048]{1,0:T(8,128)(2,1)S(1)}, u32[]{:S(2)}, u32[]{:S(2)}) collective-permute-start(bf16[64,2048]{1,0:T(8,128)(2,1)S(1)} %get-tuple-element.104), channel_id=1, source_target_pairs={{0,4},{2,6},{4,0},{6,2},{8,12},{10,14},{12,8},{14,10},{1,5},{3,7},... | collective-permute-start | bytes 786440 | tf_op jit(solution)/shard_map/ppermute | solution.py:36
  61.3 21.7 %collective-permute-start.18 = (bf16[64,2048]{1,0:T(8,128)(2,1)S(1)}, bf16[64,2048]{1,0:T(8,128)(2,1)S(1)}, u32[]{:S(2)}, u32[]{:S(2)}) collective-permute-start(bf16[64,2048]{1,0:T(8,128)(2,1)S(1)} %get-tuple-element.102), channel_id=1, source_target_pairs={{0,2},{2,0},{4,6},{6,4},{8,10},{10,8},{12,14},{14,12},{1,3},{3,1},... | collective-permute-start | bytes 786440 | tf_op jit(solution)/shard_map/ppermute | solution.py:36
  61.8 21.2 %collective-permute-start.20 = (bf16[64,2048]{1,0:T(8,128)(2,1)S(1)}, bf16[64,2048]{1,0:T(8,128)(2,1)S(1)}, u32[]{:S(2)}, u32[]{:S(2)}) collective-permute-start(bf16[64,2048]{1,0:T(8,128)(2,1)S(1)} %get-tuple-element.106), channel_id=1, source_target_pairs={{0,6},{2,4},{4,2},{6,0},{8,14},{10,12},{12,10},{14,8},{1,7},{3,5},... | collective-permute-start | bytes 786440 | tf_op jit(solution)/shard_map/ppermute | solution.py:36
  72.1 9.8 %collective-permute-start.17 = (f32[16,896]{1,0:T(8,128)S(1)}, f32[16,896]{1,0:T(8,128)S(1)}, u32[]{:S(2)}, u32[]{:S(2)}) collective-permute-start(f32[16,896]{1,0:T(8,128)S(1)} %get-tuple-element.94.mine_ref), channel_id=1, source_target_pairs={{0,1},{1,0},{2,3},{3,2},{4,5},{5,4},{6,7},{7,6},{8,9},{9,8},{10,11... | collective-permute-start | bytes 172040 | tf_op jit(solution)/shard_map/ppermute | solution.py:32
  72.1 26.0 %collective-permute-start.21 = (bf16[64,2048]{1,0:T(8,128)(2,1)S(1)}, bf16[64,2048]{1,0:T(8,128)(2,1)S(1)}, u32[]{:S(2)}, u32[]{:S(2)}) collective-permute-start(bf16[64,2048]{1,0:T(8,128)(2,1)S(1)} %get-tuple-element.87), channel_id=1, source_target_pairs={{0,8},{2,10},{4,12},{6,14},{8,0},{10,2},{12,4},{14,6},{1,9},{3,11}... | collective-permute-start | bytes 786440 | tf_op jit(solution)/shard_map/ppermute | solution.py:36
  84.0 17.1 %collective-permute-start.22 = (bf16[64,2048]{1,0:T(8,128)(2,1)S(1)}, bf16[64,2048]{1,0:T(8,128)(2,1)S(1)}, u32[]{:S(2)}, u32[]{:S(2)}) collective-permute-start(bf16[64,2048]{1,0:T(8,128)(2,1)S(1)} %get-tuple-element.107), channel_id=1, source_target_pairs={{0,8},{2,10},{4,12},{6,14},{8,0},{10,2},{12,4},{14,6},{1,9},{3,11}... | collective-permute-start | bytes 786440 | tf_op jit(solution)/shard_map/ppermute | solution.py:36
  85.0 5.5 %collective-permute-start.23 = (bf16[64,512]{1,0:T(8,128)(2,1)S(1)}, bf16[64,512]{1,0:T(8,128)(2,1)S(1)}, u32[]{:S(2)}, u32[]{:S(2)}) collective-permute-start(bf16[64,512]{1,0:T(8,128)(2,1)S(1)} %get-tuple-element.113), channel_id=1, source_target_pairs={{0,2},{2,0},{4,6},{6,4},{8,10},{10,8},{12,14},{14,12},{1,3},{3,1},... | collective-permute-start | bytes 196616 | tf_op jit(solution)/shard_map/ppermute | solution.py:36
  85.5 7.6 %collective-permute-start.24 = (bf16[64,512]{1,0:T(8,128)(2,1)S(1)}, bf16[64,512]{1,0:T(8,128)(2,1)S(1)}, u32[]{:S(2)}, u32[]{:S(2)}) collective-permute-start(bf16[64,512]{1,0:T(8,128)(2,1)S(1)} %get-tuple-element.114), channel_id=1, source_target_pairs={{0,4},{2,6},{4,0},{6,2},{8,12},{10,14},{12,8},{14,10},{1,5},{3,7},... | collective-permute-start | bytes 196616 | tf_op jit(solution)/shard_map/ppermute | solution.py:36
  86.0 7.8 %collective-permute-start.25 = (bf16[64,512]{1,0:T(8,128)(2,1)S(1)}, bf16[64,512]{1,0:T(8,128)(2,1)S(1)}, u32[]{:S(2)}, u32[]{:S(2)}) collective-permute-start(bf16[64,512]{1,0:T(8,128)(2,1)S(1)} %get-tuple-element.115), channel_id=1, source_target_pairs={{0,6},{2,4},{4,2},{6,0},{8,14},{10,12},{12,10},{14,8},{1,7},{3,5},... | collective-permute-start | bytes 196616 | tf_op jit(solution)/shard_map/ppermute | solution.py:36
  94.6 6.5 %collective-permute-start.26 = (bf16[64,512]{1,0:T(8,128)(2,1)S(1)}, bf16[64,512]{1,0:T(8,128)(2,1)S(1)}, u32[]{:S(2)}, u32[]{:S(2)}) collective-permute-start(bf16[64,512]{1,0:T(8,128)(2,1)S(1)} %get-tuple-element.117), channel_id=1, source_target_pairs={{0,8},{2,10},{4,12},{6,14},{8,0},{10,2},{12,4},{14,6},{1,9},{3,11}... | collective-permute-start | bytes 196616 | tf_op jit(solution)/shard_map/ppermute | solution.py:36

commit v11 on v10

--- a/solution.py
+++ b/solution.py
@@ -126,11 +126,13 @@
 
 
 def base_kernel(
-    z, info, x_hbm, w_hbm, g_ref, h_ref, far_ref, full_ref, x_ref, w_ref, x_sem, w_sem
+    z, info, x_hbm, w_hbm, g_hbm, h_ref, far_ref, full_ref, x_ref, w_ref, g_ref, x_sem, w_sem, g_sem
 ):
     own = pl.ds(pl.multiple_of(info[z.core] * z.cols, z.cols), z.cols)
     far = pl.ds(pl.multiple_of((1 - info[z.core]) * z.cols, z.cols), z.cols)
     unit = z.width // 8
+    g = pltpu.make_async_copy(g_hbm, g_ref, g_sem)
+    g.start()
     copies = []
     for i, (first, last) in enumerate(((0, 1), (1, 3), (3, 5), (5, 7), (7, 8))):
         cut = pl.ds(first * unit, (last - first) * unit)
@@ -139,6 +141,7 @@
         x.start()
         w.start()
         copies.append((x, w, cut))
+    g.wait()
     for b in range(z.nb):
         cut = z.block(b)
         full_ref[cut, own] = _masked(g_ref[cut, :], z.valid(info, b))
@@ -159,6 +162,7 @@
 
 def back_kernel(z, info, g_ref, *refs):
     packets, (up_ref, part_ref) = refs[:NEAR], refs[NEAR:]
+    own = pl.ds(pl.multiple_of(info[z.core] * z.cols, z.cols), z.cols)
     for b in range(z.nb):
         s = z.slot(info, 0, b)
         rel = _div(s, z.ten_dev) ^ info[z.me]
@@ -169,8 +173,7 @@
         for k in range(1, NEAR):
             u = jnp.where(near == k, packets[k][at, :], u)
         up_ref[z.ranks(b), :] = u
-        g = _masked(g_ref[z.block(b), :], z.valid(info, b))
-        part_ref[:, z.block(b)] = _dot(u, g, NT)
+        part_ref[:, z.block(b)] = _dot(u, g_ref[z.block(b), own], NT)
 
 
 def pack_kernel(z, n_out, start, info, mine_ref, other_ref, x_ref, *refs):
@@ -305,10 +308,10 @@
         one_hot_sums(z, info, s)
 
 
-def tokens_kernel(z, info, low_ref, high_ref, mine_ref, other_ref, d_ref, out_ref, spread):
+def tokens_kernel(z, first, info, through_ref, mine_ref, other_ref, d_ref, *refs):
+    out_ref, spread = refs[-2:]
     step = pl.program_id(0)
     wide = out_ref.shape[1]
-    per_half = low_ref.shape[1] // wide
 
     @pl.when(step == 0)
     def _():
@@ -318,14 +321,10 @@
             v = (mine_ref[:, cut] + other_ref[:, cut]) * adapter_scale
             spread[z.ranks(b), cut] = v.astype(bf16)
 
-    cut = pl.ds(pl.multiple_of(step * wide, wide), wide)
+    here = pl.ds(pl.multiple_of(step * wide, wide), wide)
+    cut = pl.ds(pl.multiple_of((first + step) * wide, wide), wide)
     added = _dot(spread[...], d_ref[:, cut], TN)
-    for half, through in enumerate((low_ref, high_ref)):
-
-        @pl.when(step // per_half == half)
-        def _():
-            here = pl.ds(pl.multiple_of((step - half * per_half) * wide, wide), wide)
-            out_ref[...] = (through[:, here] + added).astype(bf16)
+    out_ref[...] = (through_ref[:, here] + added).astype(bf16)
 
 
 def on_device(
@@ -388,14 +387,15 @@
 
     base_other, g_full, x_in = _call(
         functools.partial(base_kernel, z), "base", (1,),
-        [pl.BlockSpec(memory_space=pl.ANY)] * 2 + [VMEM] * 2,
+        [pl.BlockSpec(memory_space=pl.ANY)] * 3 + [VMEM],
         [_whole((rows, cols))] + [VMEM] * 2,
         [
             _shape((rows, cols), bf16), _shape((rows, 2 * cols), bf16), _shape(tokens.shape, bf16),
         ],
         [
-            pltpu.VMEM((width, cols), bf16),
+            pltpu.VMEM((width, cols), bf16), pltpu.VMEM((rows, cols), bf16),
             pltpu.SemaphoreType.DMA((5,)), pltpu.SemaphoreType.DMA((5,)),
+            pltpu.SemaphoreType.DMA,
         ],
         vmem=BIG_VMEM,
     )(
@@ -418,7 +418,7 @@
         functools.partial(back_kernel, z), "back", (1,),
         [VMEM] * (1 + NEAR), [VMEM, _whole(part)],
         [_shape((nb * rank, cols), bf16), _shape(part, f32)], [],
-    )(info, out_cotangent, *packets)
+    )(info, g_full, *packets)
     back_other = _swap(back_part, "tensor")
     ready = [base_arrived]
     if shared:
@@ -470,21 +470,19 @@
             [VMEM] * 3, [_whole(block)] * 4, [_shape(block, bf16)] * 4, [],
             n_scalars=2,
         )(_tie(info, low), info_x, shard, shard_far, farther)
-        got_y = _xor(_tie(chosen[1], got_a[2]), n_dp, 1)
-        got_x = _swap(chosen[2], "groups")
+        sends_b = pack(_tie(info, chosen[0]), wide_a, width - wide_a)
+        got_y = _xor(_tie(chosen[1], got_a[2], sends_b[0]), n_dp, 1)
+        got_x = _swap(_tie(chosen[2], sends_b[0]), "groups")
         got_d = lax.ppermute(
-            chosen[3],
+            _tie(chosen[3], sends_b[0]),
             ("groups", "dp"),
             [(g * n_dp + d, (1 - g) * n_dp + (d ^ 1)) for g in range(2) for d in range(n_dp)],
         )
-        after_choose = chosen[0]
     else:
         every = lax.all_gather(down_t, "dp", axis=0, tiled=True)
         slots = jnp.take(tenant_slot, block_tenant, axis=0)
         got_down = [jnp.take(every, slots, axis=0).reshape(nb * rank, width)]
-        after_choose = low
-
-    sends_b = pack(_tie(info, after_choose), wide_a, width - wide_a)
+        sends_b = pack(_tie(info, low), wide_a, width - wide_a)
 
     base_own = _call(
         functools.partial(own_kernel, z), "base_own", (1,),
@@ -493,11 +491,11 @@
     dense_a = dense(_tie(info, base_own), got_a)
     far_a = to_far(dense_a)
 
-    gate = [dense_a[1]] + ([got_y] if shared else [])
+    (high,) = through(_tie(info, dense_a[1]), half, width - half, 0)
+    gate = [high] + ([got_y] if shared else [])
     got_b = to_near(
         [_tie(b, *gate) if k in (1, 3) else _tie(b, dense_a[1]) for k, b in enumerate(sends_b)]
     )
-    (high,) = through(_tie(info, dense_a[1]), half, width - half, 0)
 
     if shared:
         got_down = [chosen[0], got_y, got_x, got_d]
@@ -510,11 +508,18 @@
 
 
     step = min(512, width // 8)
-    grad_tokens = _call(
-        functools.partial(tokens_kernel, z), "token_grads", (width // step,),
-        [VMEM] * 5, pl.BlockSpec((rows, step), lambda i, *_: (0, i)),
-        _shape((rows, width), bf16), [pltpu.VMEM((nb * rank, rows), bf16)],
-    )(_tie(info, shrink_part), low, high, back_part, back_other, block_down)
+
+    def token_grads(info, product, first, so_far):
+        steps = product.shape[1] // step
+        return _call(
+            functools.partial(tokens_kernel, z, first), "token_grads", (steps,),
+            [VMEM] * 4 + [pl.BlockSpec(memory_space=pl.ANY)] * len(so_far),
+            pl.BlockSpec((rows, step), lambda i, *_: (0, first + i)),
+            _shape((rows, width), bf16), [pltpu.VMEM((nb * rank, rows), bf16)],
+            {5: 0} if so_far else None,
+        )(info, product, back_part, back_other, block_down, *so_far)
+
+    grad_tokens = token_grads(_tie(info, shrink_part), low, 0, [])
 
     up_sends = _call(
         functools.partial(pack_up_kernel, z, NEAR), "pack_up", (1,),
@@ -527,16 +532,18 @@
     dense_b = dense(_tie(info, up_sends[0]), got_b)
     far_b = to_far(dense_b)
 
+    grad_tokens = token_grads(_tie(info, dense_b[1]), high, half // step, [grad_tokens])
+    dense_u = dense(_tie(info, grad_tokens), got_u)
+    far_u = to_far(dense_u)
+
     projected = _call(
         functools.partial(projected_kernel, z), "projected", (1,),
         [VMEM] * 4, _whole((rows, cols)), _shape((rows, cols), bf16),
         [pltpu.VMEM((nb * rank, rows), bf16)],
     )(
-        _tie(info, dense_b[1]),
+        _tie(info, dense_u[1]),
         base_own, shrink_part, shrink_other, block_up,
     )
-    dense_u = dense(_tie(info, projected), got_u)
-    far_u = to_far(dense_u)
 
     outs = [(ten_dev * rank, width), (ten_dev * rank, cols)]
     grad_down, grad_up = _call(

time: 103 us -> 98.5 us (0.956)
  waiting for transfers between devices: 17.6 us -> 10.8 us
  starting transfers between devices: 33.2 us -> 35.5 us
    ppermute x20, waiting for transfers between devices: 16.5 us -> 9.71 us  [_xor(): return lax.ppermute(x, 'dp', [(i, i ^ k) for i in range(n)])]
    ppermute x20, starting transfers between devices: 28.9 us -> 31.2 us  [_xor(): return lax.ppermute(x, 'dp', [(i, i ^ k) for i in range(n)])]
    pallas_call x1 -> x2, Pallas kernels: 7.7 us -> 7.72 us  [token_grads(): _call(functools.partial(tokens_kernel, z, first), 'token_grads', (steps,)...]
  transfers between devices with their start and end apart: 27 -> 27, of which waited for: 8 -> 7; matrix products, arithmetic and copies ran while one was open for 4% -> 4% of each run, Pallas kernels for 43% -> 45%
where the time goes in v11:
time: 98.5 us; the launch traced here: 98.3 us
  Pallas kernels  46.2 us (47%)
  starting transfers between devices  35.5 us (36%)
  waiting for transfers between devices  10.8 us (11%)
  other arithmetic  2.63 us (3%)
  local copies, waits for them, and re-layouts  2.33 us (2%)
    ppermute x20, starting transfers between devices, _xor(): return lax.ppermute(x, 'dp', [(i, i ^ k) for i in range(n)])  31.2 us
    ppermute x20, waiting for transfers between devices, _xor(): return lax.ppermute(x, 'dp', [(i, i ^ k) for i in range(n)])  9.71 us
    pallas_call x2, Pallas kernels, through(): _call(functools.partial(through_kernel, z, first), 'through', (1,), [VMEM...  9.59 us
    pallas_call x1, Pallas kernels, on_device(): _call(functools.partial(base_kernel, z), 'base', (1,), [pl.BlockSpec(memo...  7.78 us
    pallas_call x2, Pallas kernels, token_grads(): _call(functools.partial(tokens_kernel, z, first), 'token_grads', (steps,)...  7.72 us
    pallas_call x1, Pallas kernels, on_device(): _call(functools.partial(own_kernel, z), 'base_own', (1,), [VMEM] * 3, VME...  4.61 us
    pallas_call x2, Pallas kernels, pack(): _call(functools.partial(pack_kernel, z, NEAR, start), 'pack_down', (1,),...  3.94 us
    ppermute x6, starting transfers between devices, _swap(): return lax.ppermute(x, axis, [(0, 1), (1, 0)])  3.35 us
  transfers between devices with their start and end apart: 27, of which 7 were waited for; matrix products, arithmetic and copies ran while one was open for 4% of the time, Pallas kernels for 45%

profile of v11, /device:TPU:0, one launch (start us, length us, event | category | flops | bytes accessed | tf_op | source)
XLA Modules:
  0.0 98.3 jit_solution(1448363740717788434)
XLA Ops:
  0.6 4.1 %collective-permute-start = (bf16[4,16,512]{2,1,0:T(8,128)(2,1)}, bf16[4,16,512]{2,1,0:T(8,128)(2,1)S(1)}, u32[]{:S(2)}, u32[]{:S(2)}) collective-permute-start(bf16[4,16,512]{2,1,0:T(8,128)(2,1)} %param.11), channel_id=1, source_target_pairs={{0,8},{2,10},{4,12},{6,14},{8,0},{10,2},{12,4},{14,6},{1,9},{3,11}... | collective-permute-start | bytes 196616 | tf_op jit(solution)/shard_map/ppermute | solution.py:36
  5.7 1.6 %collective-permute-start.2 = (bf16[4,16,1024]{2,1,0:T(8,128)(2,1)S(1)}, bf16[4,16,1024]{2,1,0:T(8,128)(2,1)S(1)}, u32[]{:S(2)}, u32[]{:S(2)}) collective-permute-start(bf16[4,16,1024]{2,1,0:T(8,128)(2,1)S(1)} %get-tuple-element.127), channel_id=1, source_target_pairs={{0,2},{2,0},{4,6},{6,4},{8,10},{10,8},{12,14},{14,12},{1,3},{3,1},... | collective-permute-start | bytes 393224 | tf_op jit(solution)/shard_map/ppermute | solution.py:36
  8.9 1.8 %collective-permute-done.2 = bf16[4,16,1024]{2,1,0:T(8,128)(2,1)S(1)} collective-permute-done((bf16[4,16,1024]{2,1,0:T(8,128)(2,1)S(1)}, bf16[4,16,1024]{2,1,0:T(8,128)(2,1)S(1)}, u32[]{:S(2)}, u32[]{:S(2)}) %collective-permute-start.2) | collective-permute-done | bytes 131104 | tf_op jit(solution)/shard_map/ppermute | solution.py:36
  12.0 1.6 %collective-permute-start.5 = (bf16[144,512]{1,0:T(8,128)(2,1)S(1)}, bf16[144,512]{1,0:T(8,128)(2,1)S(1)}, u32[]{:S(2)}, u32[]{:S(2)}) collective-permute-start(bf16[144,512]{1,0:T(8,128)(2,1)S(1)} %pad_maximum_fusion.2.refs_0_), channel_id=1, source_target_pairs={{0,2},{2,0},{4,6},{6,4},{8,10},{10,8},{12,14},{14,12},{1,3},{3,1},... | collective-permute-start | bytes 442376 | tf_op jit(solution)/shard_map/ppermute | solution.py:36
  13.6 1.6 %collective-permute-start.4 = (bf16[144,512]{1,0:T(8,128)(2,1)S(1)}, bf16[144,512]{1,0:T(8,128)(2,1)S(1)}, u32[]{:S(2)}, u32[]{:S(2)}) collective-permute-start(bf16[144,512]{1,0:T(8,128)(2,1)S(1)} %pad_maximum_fusion.2.refs_0_), channel_id=1, source_target_pairs={{0,4},{2,6},{4,0},{6,2},{8,12},{10,14},{12,8},{14,10},{1,5},{3,7},... | collective-permute-start | bytes 442376 | tf_op jit(solution)/shard_map/ppermute | solution.py:36
  15.6 1.3 %copy-done = bf16[896,512]{1,0:T(8,128)(2,1)S(1)} copy-done((bf16[896,512]{1,0:T(8,128)(2,1)S(1)}, bf16[896,512]{1,0:T(8,128)(2,1)}, u32[]{:S(2)}) %copy-start) | copy-done | bytes 917528
  17.0 7.8 %base.1 = (bf16[896,512]{1,0:T(8,128)(2,1)S(1)}, bf16[896,1024]{1,0:T(8,128)(2,1)S(1)}, bf16[896,4096]{1,0:T(8,128)(2,1)S(1)}) custom-call(s32[16,128]{1,0:T(8,128)S(1)} %select_select_fusion.1.info, bf16[896,4096]{1,0:T(8,128)(2,1)} %x_hbm.1, bf16[4096,1024]{1,0:T(8,128)(2,1)} %w_ref.5, bf16[896,512]{1,0:T(8,128)(2,1)S(1)} %copy-done, ...), custom_call_target="tpu_custom_call" | custom-call | flops 1 | bytes 1 | tf_op jit(solution)/shard_map/base/pallas_call | solution.py:388
  29.0 2.0 %pack_down.2 = (bf16[64,2048]{1,0:T(8,128)(2,1)S(1)}, bf16[64,2048]{1,0:T(8,128)(2,1)S(1)}, bf16[64,2048]{1,0:T(8,128)(2,1)S(1)}, bf16[64,2048]{1,0:T(8,128)(2,1)S(1)}) custom-call(s32[16,128]{1,0:T(8,128)S(1)} %select_select_fusion.info, f32[16,896]{1,0:T(8,128)S(1)} %get-tuple-element.75.mine_ref, f32[16,896]{1,0:T(8,128)S(1)} %collective-permute-done.8.other_ref, ...), custom_call_target="tpu_custom_call" | custom-call | flops 1 | bytes 1 | tf_op jit(solution)/shard_map/pack_down/pallas_call | solution.py:431
  30.9 1.3 %collective-permute-start.12 = (bf16[64,2048]{1,0:T(8,128)(2,1)S(1)}, bf16[64,2048]{1,0:T(8,128)(2,1)S(1)}, u32[]{:S(2)}, u32[]{:S(2)}) collective-permute-start(bf16[64,2048]{1,0:T(8,128)(2,1)S(1)} %get-tuple-element.88), channel_id=1, source_target_pairs={{0,4},{2,6},{4,0},{6,2},{8,12},{10,14},{12,8},{14,10},{1,5},{3,7},... | collective-permute-start | bytes 786440 | tf_op jit(solution)/shard_map/ppermute | solution.py:36
  32.2 1.1 %collective-permute-start.11 = (bf16[64,2048]{1,0:T(8,128)(2,1)S(1)}, bf16[64,2048]{1,0:T(8,128)(2,1)S(1)}, u32[]{:S(2)}, u32[]{:S(2)}) collective-permute-start(bf16[64,2048]{1,0:T(8,128)(2,1)S(1)} %get-tuple-element.87), channel_id=1, source_target_pairs={{0,2},{2,0},{4,6},{6,4},{8,10},{10,8},{12,14},{14,12},{1,3},{3,1},... | collective-permute-start | bytes 786440 | tf_op jit(solution)/shard_map/ppermute | solution.py:36
  33.3 1.2 %collective-permute-start.13 = (bf16[64,2048]{1,0:T(8,128)(2,1)S(1)}, bf16[64,2048]{1,0:T(8,128)(2,1)S(1)}, u32[]{:S(2)}, u32[]{:S(2)}) collective-permute-start(bf16[64,2048]{1,0:T(8,128)(2,1)S(1)} %get-tuple-element.89), channel_id=1, source_target_pairs={{0,6},{2,4},{4,2},{6,0},{8,14},{10,12},{12,10},{14,8},{1,7},{3,5},... | collective-permute-start | bytes 786440 | tf_op jit(solution)/shard_map/ppermute | solution.py:36
  34.5 1.5 %collective-permute-start.9 = (s32[16,128]{1,0:T(8,128)S(1)}, s32[16,128]{1,0:T(8,128)S(1)}, u32[]{:S(2)}, u32[]{:S(2)}) collective-permute-start(s32[16,128]{1,0:T(8,128)S(1)} %select_select_fusion.info), channel_id=1, source_target_pairs={{0,16},{16,0},{1,17},{17,1},{2,18},{18,2},{3,19},{19,3},{4,20},{20... | collective-permute-start | bytes 24584 | tf_op jit(solution)/shard_map/ppermute | solution.py:32
  36.0 4.7 %through.2 = (f32[896,2048]{1,0:T(8,128)S(1)}, bf16[2,64,128]{2,1,0:T(8,128)(2,1)S(1)}) custom-call(s32[16,128]{1,0:T(8,128)S(1)} %select_select_fusion.info, bf16[896,1024]{1,0:T(8,128)(2,1)S(1)} %get-tuple-element.73.g_ref, bf16[4096,1024]{1,0:T(8,128)(2,1)S(1)} %bitcast.20), custom_call_target="tpu_custom_call" | custom-call | flops 1 | bytes 1 | tf_op jit(solution)/shard_map/through/pallas_call | solution.py:455
  41.8 2.0 %pack_down.3 = (bf16[64,2048]{1,0:T(8,128)(2,1)S(1)}, bf16[64,2048]{1,0:T(8,128)(2,1)S(1)}, bf16[64,2048]{1,0:T(8,128)(2,1)S(1)}, bf16[64,2048]{1,0:T(8,128)(2,1)S(1)}) custom-call(s32[16,128]{1,0:T(8,128)S(1)} %select_select_fusion.info, f32[16,896]{1,0:T(8,128)S(1)} %get-tuple-element.75.mine_ref, f32[16,896]{1,0:T(8,128)S(1)} %collective-permute-done.8.other_ref, ...), custom_call_target="tpu_custom_call" | custom-call | flops 1 | bytes 1 | tf_op jit(solution)/shard_map/pack_down/pallas_call | solution.py:431
  43.8 2.4 %collective-permute-done.12.refs_2_ = bf16[64,2048]{1,0:T(8,128)(2,1)S(1)} collective-permute-done((bf16[64,2048]{1,0:T(8,128)(2,1)S(1)}, bf16[64,2048]{1,0:T(8,128)(2,1)S(1)}, u32[]{:S(2)}, u32[]{:S(2)}) %collective-permute-start.12) | collective-permute-done | bytes 262176 | tf_op jit(solution)/shard_map/ppermute | solution.py:36
  47.2 1.5 %collective-permute-start.15 = (bf16[112,1024]{1,0:T(8,128)(2,1)S(1)}, bf16[112,1024]{1,0:T(8,128)(2,1)S(1)}, u32[]{:S(2)}, u32[]{:S(2)}) collective-permute-start(bf16[112,1024]{1,0:T(8,128)(2,1)S(1)} %get-tuple-element.96), channel_id=1, source_target_pairs={{0,16},{16,0},{1,17},{17,1},{2,18},{18,2},{3,19},{19,3},{4,20},{20... | collective-permute-start | bytes 688136 | tf_op jit(solution)/shard_map/ppermute | solution.py:32
  49.7 4.6 %base_own.1.base_ref = f32[896,512]{1,0:T(8,128)S(1)} custom-call(s32[16,128]{1,0:T(8,128)S(1)} %select_select_fusion.info, bf16[896,4096]{1,0:T(8,128)(2,1)S(1)} %get-tuple-element.76.x_ref, bf16[4096,1024]{1,0:T(8,128)(2,1)S(1)} %bitcast.20, bf16[896,512]{1,0:T(8,128)(2,1)S(1)} %collective-permute-done.7.far_ref), custom_call_target="tpu_custom_call" | custom-call | flops 1 | bytes 1 | tf_op jit(solution)/shard_map/base_own/pallas_call | solution.py:487
  56.1 4.9 %through.3.through_ref = f32[896,2048]{1,0:T(8,128)S(1)} custom-call(s32[16,128]{1,0:T(8,128)S(1)} %select_select_fusion.info, bf16[896,1024]{1,0:T(8,128)(2,1)S(1)} %get-tuple-element.73.g_ref, bf16[4096,1024]{1,0:T(8,128)(2,1)S(1)} %bitcast.20), custom_call_target="tpu_custom_call" | custom-call | flops 1 | bytes 1 | tf_op jit(solution)/shard_map/through/pallas_call | solution.py:455
  61.3 1.2 %collective-permute-start.18 = (bf16[64,2048]{1,0:T(8,128)(2,1)S(1)}, bf16[64,2048]{1,0:T(8,128)(2,1)S(1)}, u32[]{:S(2)}, u32[]{:S(2)}) collective-permute-start(bf16[64,2048]{1,0:T(8,128)(2,1)S(1)} %get-tuple-element.107), channel_id=1, source_target_pairs={{0,2},{2,0},{4,6},{6,4},{8,10},{10,8},{12,14},{14,12},{1,3},{3,1},... | collective-permute-start | bytes 786440 | tf_op jit(solution)/shard_map/ppermute | solution.py:36
  62.5 1.8 %collective-permute-start.20 = (bf16[64,2048]{1,0:T(8,128)(2,1)S(1)}, bf16[64,2048]{1,0:T(8,128)(2,1)S(1)}, u32[]{:S(2)}, u32[]{:S(2)}) collective-permute-start(bf16[64,2048]{1,0:T(8,128)(2,1)S(1)} %get-tuple-element.111), channel_id=1, source_target_pairs={{0,6},{2,4},{4,2},{6,0},{8,14},{10,12},{12,10},{14,8},{1,7},{3,5},... | collective-permute-start | bytes 786440 | tf_op jit(solution)/shard_map/ppermute | solution.py:36
  64.4 2.8 %shrink.1 = (bf16[112,4096]{1,0:T(8,128)(2,1)S(1)}, f32[16,896]{1,0:T(8,128)S(1)}) custom-call(s32[16,128]{1,0:T(8,128)S(1)} %select_select_fusion.info, bf16[896,4096]{1,0:T(8,128)(2,1)S(1)} %get-tuple-element.76.x_ref, bf16[112,1024]{1,0:T(8,128)(2,1)S(1)} %get-tuple-element.81.refs_0_, bf16[112,1024]{1,0:T(8,128)(2,1)S(1)} %collective-permute-done.14.refs_1_, ...), custom_call_target="tpu_custom_call" | custom-call | flops 1 | bytes 1 | tf_op jit(solution)/shard_map/shrink/pallas_call | solution.py:502
  67.3 2.1 %collective-permute-start.24 = (bf16[64,2048]{1,0:T(8,128)(2,1)S(1)}, bf16[64,2048]{1,0:T(8,128)(2,1)S(1)}, u32[]{:S(2)}, u32[]{:S(2)}) collective-permute-start(bf16[64,2048]{1,0:T(8,128)(2,1)S(1)} %get-tuple-element.90), channel_id=1, source_target_pairs={{0,8},{2,10},{4,12},{6,14},{8,0},{10,2},{12,4},{14,6},{1,9},{3,11}... | collective-permute-start | bytes 786440 | tf_op jit(solution)/shard_map/ppermute | solution.py:36
  69.3 3.9 %token_grads.2.refs_0_ = bf16[896,4096]{1,0:T(8,128)(2,1)} custom-call(s32[16,128]{1,0:T(8,128)S(1)} %select_select_fusion.info, f32[896,2048]{1,0:T(8,128)S(1)} %get-tuple-element.79.through_ref, f32[16,896]{1,0:T(8,128)S(1)} %get-tuple-element.75.mine_ref, f32[16,896]{1,0:T(8,128)S(1)} %collective-permute-done.8.other_ref, ...), custom_call_target="tpu_custom_call" | custom-call | flops 1 | bytes 1 | tf_op jit(solution)/shard_map/token_grads/pallas_call | solution.py:514
  73.2 1.1 %pack_up.1 = (bf16[64,512]{1,0:T(8,128)(2,1)S(1)}, bf16[64,512]{1,0:T(8,128)(2,1)S(1)}, bf16[64,512]{1,0:T(8,128)(2,1)S(1)}, bf16[64,512]{1,0:T(8,128)(2,1)S(1)}) custom-call(s32[16,128]{1,0:T(8,128)S(1)} %select_select_fusion.info, f32[16,896]{1,0:T(8,128)S(1)} %get-tuple-element.99.mine_ref, f32[16,896]{1,0:T(8,128)S(1)} %collective-permute-done.17.other_ref, ...), custom_call_target="tpu_custom_call" | custom-call | flops 1 | bytes 1 | tf_op jit(solution)/shard_map/pack_up/pallas_call | solution.py:524
  76.2 2.4 %collective-permute-start.25 = (bf16[64,2048]{1,0:T(8,128)(2,1)S(1)}, bf16[64,2048]{1,0:T(8,128)(2,1)S(1)}, u32[]{:S(2)}, u32[]{:S(2)}) collective-permute-start(bf16[64,2048]{1,0:T(8,128)(2,1)S(1)} %get-tuple-element.112), channel_id=1, source_target_pairs={{0,8},{2,10},{4,12},{6,14},{8,0},{10,2},{12,4},{14,6},{1,9},{3,11}... | collective-permute-start | bytes 786440 | tf_op jit(solution)/shard_map/ppermute | solution.py:36
  79.3 1.3 %collective-permute-start.22 = (bf16[64,512]{1,0:T(8,128)(2,1)S(1)}, bf16[64,512]{1,0:T(8,128)(2,1)S(1)}, u32[]{:S(2)}, u32[]{:S(2)}) collective-permute-start(bf16[64,512]{1,0:T(8,128)(2,1)S(1)} %get-tuple-element.116), channel_id=1, source_target_pairs={{0,4},{2,6},{4,0},{6,2},{8,12},{10,14},{12,8},{14,10},{1,5},{3,7},... | collective-permute-start | bytes 196616 | tf_op jit(solution)/shard_map/ppermute | solution.py:36
  80.7 1.4 %collective-permute-start.23 = (bf16[64,512]{1,0:T(8,128)(2,1)S(1)}, bf16[64,512]{1,0:T(8,128)(2,1)S(1)}, u32[]{:S(2)}, u32[]{:S(2)}) collective-permute-start(bf16[64,512]{1,0:T(8,128)(2,1)S(1)} %get-tuple-element.117), channel_id=1, source_target_pairs={{0,6},{2,4},{4,2},{6,0},{8,14},{10,12},{12,10},{14,8},{1,7},{3,5},... | collective-permute-start | bytes 196616 | tf_op jit(solution)/shard_map/ppermute | solution.py:36
  82.1 3.9 %token_grads.3 = bf16[896,4096]{1,0:T(8,128)(2,1)} custom-call(s32[16,128]{1,0:T(8,128)S(1)} %select_select_fusion.info, f32[896,2048]{1,0:T(8,128)S(1)} %through.3.through_ref, f32[16,896]{1,0:T(8,128)S(1)} %get-tuple-element.75.mine_ref, f32[16,896]{1,0:T(8,128)S(1)} %collective-permute-done.8.other_ref, ...), custom_call_target="tpu_custom_call", output_to_operand_aliasing={{}: (5, {})} | custom-call | flops 1 | bytes 1 | tf_op jit(solution)/shard_map/token_grads/pallas_call | solution.py:514
  86.8 4.3 %collective-permute-start.26 = (bf16[64,512]{1,0:T(8,128)(2,1)S(1)}, bf16[64,512]{1,0:T(8,128)(2,1)S(1)}, u32[]{:S(2)}, u32[]{:S(2)}) collective-permute-start(bf16[64,512]{1,0:T(8,128)(2,1)S(1)} %get-tuple-element.118), channel_id=1, source_target_pairs={{0,8},{2,10},{4,12},{6,14},{8,0},{10,2},{12,4},{14,6},{1,9},{3,11}... | collective-permute-start | bytes 196616 | tf_op jit(solution)/shard_map/ppermute | solution.py:36
  91.1 2.0 %projected.1 = bf16[896,512]{1,0:T(8,128)(2,1)} custom-call(s32[16,128]{1,0:T(8,128)S(1)} %select_select_fusion.info, f32[896,512]{1,0:T(8,128)S(1)} %base_own.1.base_ref, f32[16,896]{1,0:T(8,128)S(1)} %get-tuple-element.99.mine_ref, f32[16,896]{1,0:T(8,128)S(1)} %collective-permute-done.17.other_ref, bf16[112,512]{1,0:T(8,128)(2,1)S(1)} %get-tuple-element.120.up_ref), custom_call_target="tpu_custom_call" | custom-call | flops 1 | bytes 1 | tf_op jit(solution)/shard_map/projected/pallas_call | solution.py:539
  93.1 3.4 %collective-permute-done.26.refs_5_ = bf16[64,512]{1,0:T(8,128)(2,1)S(1)} collective-permute-done((bf16[64,512]{1,0:T(8,128)(2,1)S(1)}, bf16[64,512]{1,0:T(8,128)(2,1)S(1)}, u32[]{:S(2)}, u32[]{:S(2)}) %collective-permute-start.26) | collective-permute-done | bytes 65568 | tf_op jit(solution)/shard_map/ppermute | solution.py:36
  96.6 1.8 %final.1 = (f32[64,4096]{1,0:T(8,128)}, f32[64,512]{1,0:T(8,128)}) custom-call(s32[16,128]{1,0:T(8,128)S(1)} %select_select_fusion.info, f32[64,2048]{1,0:T(8,128)S(1)} %get-tuple-element.121.refs_0_, bf16[64,2048]{1,0:T(8,128)(2,1)S(1)} %collective-permute-done.24.refs_1_, f32[64,2048]{1,0:T(8,128)S(1)} %get-tuple-element.122.refs_2_, ...), custom_call_target="tpu_custom_call" | custom-call | flops 1 | bytes 1 | tf_op jit(solution)/shard_map/final/pallas_call | solution.py:549
  (65 shorter events, 17.0 us)
Async XLA Ops:
  0.6 10.5 %collective-permute-start = (bf16[4,16,512]{2,1,0:T(8,128)(2,1)}, bf16[4,16,512]{2,1,0:T(8,128)(2,1)S(1)}, u32[]{:S(2)}, u32[]{:S(2)}) collective-permute-start(bf16[4,16,512]{2,1,0:T(8,128)(2,1)} %param.11), channel_id=1, source_target_pairs={{0,8},{2,10},{4,12},{6,14},{8,0},{10,2},{12,4},{14,6},{1,9},{3,11}... | collective-permute-start | bytes 196616 | tf_op jit(solution)/shard_map/ppermute | solution.py:36
  5.7 5.0 %collective-permute-start.2 = (bf16[4,16,1024]{2,1,0:T(8,128)(2,1)S(1)}, bf16[4,16,1024]{2,1,0:T(8,128)(2,1)S(1)}, u32[]{:S(2)}, u32[]{:S(2)}) collective-permute-start(bf16[4,16,1024]{2,1,0:T(8,128)(2,1)S(1)} %get-tuple-element.127), channel_id=1, source_target_pairs={{0,2},{2,0},{4,6},{6,4},{8,10},{10,8},{12,14},{14,12},{1,3},{3,1},... | collective-permute-start | bytes 393224 | tf_op jit(solution)/shard_map/ppermute | solution.py:36
  7.3 8.3 %collective-permute-start.3 = (bf16[896,512]{1,0:T(8,128)(2,1)}, bf16[896,512]{1,0:T(8,128)(2,1)S(1)}, u32[]{:S(2)}, u32[]{:S(2)}) collective-permute-start(bf16[896,512]{1,0:T(8,128)(2,1)} %g_hbm.1), channel_id=1, source_target_pairs={{0,1},{1,0},{2,3},{3,2},{4,5},{5,4},{6,7},{7,6},{8,9},{9,8},{10,11... | collective-permute-start | bytes 2752520 | tf_op jit(solution)/shard_map/ppermute | solution.py:32
  10.8 14.0 %collective-permute-start.6 = (bf16[8,16,1024]{2,1,0:T(8,128)(2,1)S(1)}, bf16[8,16,1024]{2,1,0:T(8,128)(2,1)S(1)}, u32[]{:S(2)}, u32[]{:S(2)}) collective-permute-start(bf16[8,16,1024]{2,1,0:T(8,128)(2,1)S(1)} %pad_maximum_fusion.1.own_ref), channel_id=1, source_target_pairs={{0,8},{2,10},{4,12},{6,14},{8,0},{10,2},{12,4},{14,6},{1,9},{3,11}... | collective-permute-start | bytes 786440 | tf_op jit(solution)/shard_map/ppermute | solution.py:36
  12.0 12.8 %collective-permute-start.5 = (bf16[144,512]{1,0:T(8,128)(2,1)S(1)}, bf16[144,512]{1,0:T(8,128)(2,1)S(1)}, u32[]{:S(2)}, u32[]{:S(2)}) collective-permute-start(bf16[144,512]{1,0:T(8,128)(2,1)S(1)} %pad_maximum_fusion.2.refs_0_), channel_id=1, source_target_pairs={{0,2},{2,0},{4,6},{6,4},{8,10},{10,8},{12,14},{14,12},{1,3},{3,1},... | collective-permute-start | bytes 442376 | tf_op jit(solution)/shard_map/ppermute | solution.py:36
  13.6 11.2 %collective-permute-start.4 = (bf16[144,512]{1,0:T(8,128)(2,1)S(1)}, bf16[144,512]{1,0:T(8,128)(2,1)S(1)}, u32[]{:S(2)}, u32[]{:S(2)}) collective-permute-start(bf16[144,512]{1,0:T(8,128)(2,1)S(1)} %pad_maximum_fusion.2.refs_0_), channel_id=1, source_target_pairs={{0,4},{2,6},{4,0},{6,2},{8,12},{10,14},{12,8},{14,10},{1,5},{3,7},... | collective-permute-start | bytes 442376 | tf_op jit(solution)/shard_map/ppermute | solution.py:36
  15.2 10.4 %collective-permute-start.1 = (bf16[144,512]{1,0:T(8,128)(2,1)S(1)}, bf16[144,512]{1,0:T(8,128)(2,1)S(1)}, u32[]{:S(2)}, u32[]{:S(2)}) collective-permute-start(bf16[144,512]{1,0:T(8,128)(2,1)S(1)} %pad_maximum_fusion.2.refs_0_), channel_id=1, source_target_pairs={{0,6},{2,4},{4,2},{6,0},{8,14},{10,12},{12,10},{14,8},{1,7},{3,5},... | collective-permute-start | bytes 442376 | tf_op jit(solution)/shard_map/ppermute | solution.py:36
  15.6 20.4 %slice-start = ((s8[8388608]{0:T(1024)(128)(4,1)}), s8[4194304]{0:T(1024)(128)(4,1)S(1)}, s32[]{:S(2)}) async-start(s8[8388608]{0:T(1024)(128)(4,1)} %bitcast.19), calls=%async_computation | async-start | bytes 8388608
  15.6 20.4 %slice-start.1 = ((s8[8388608]{0:T(1024)(128)(4,1)}), s8[4194304]{0:T(1024)(128)(4,1)S(1)}, s32[]{:S(2)}) async-start(s8[8388608]{0:T(1024)(128)(4,1)} %bitcast.19), calls=%async_computation.1 | async-start | bytes 8388608
  15.6 1.3 %copy-start = (bf16[896,512]{1,0:T(8,128)(2,1)S(1)}, bf16[896,512]{1,0:T(8,128)(2,1)}, u32[]{:S(2)}) copy-start(bf16[896,512]{1,0:T(8,128)(2,1)} %g_hbm.1) | copy-start | bytes 2752516
  24.7 3.2 %collective-permute-start.7 = (bf16[896,512]{1,0:T(8,128)(2,1)S(1)}, bf16[896,512]{1,0:T(8,128)(2,1)S(1)}, u32[]{:S(2)}, u32[]{:S(2)}) collective-permute-start(bf16[896,512]{1,0:T(8,128)(2,1)S(1)} %get-tuple-element.66), channel_id=1, source_target_pairs={{0,1},{1,0},{2,3},{3,2},{4,5},{5,4},{6,7},{7,6},{8,9},{9,8},{10,11... | collective-permute-start | bytes 2752520 | tf_op jit(solution)/shard_map/ppermute | solution.py:32
  25.7 15.0 %collective-permute-start.10 = (bf16[16,16,1024]{2,1,0:T(8,128)(2,1)S(1)}, bf16[16,16,1024]{2,1,0:T(8,128)(2,1)S(1)}, u32[]{:S(2)}, u32[]{:S(2)}) collective-permute-start(bf16[16,16,1024]{2,1,0:T(8,128)(2,1)S(1)} %pad_maximum_fusion), channel_id=1, source_target_pairs={{0,4},{2,6},{4,0},{6,2},{8,12},{10,14},{12,8},{14,10},{1,5},{3,7},... | collective-permute-start | bytes 1572872 | tf_op jit(solution)/shard_map/ppermute | solution.py:36
  27.7 1.3 %collective-permute-start.8 = (f32[16,896]{1,0:T(8,128)S(1)}, f32[16,896]{1,0:T(8,128)S(1)}, u32[]{:S(2)}, u32[]{:S(2)}) collective-permute-start(f32[16,896]{1,0:T(8,128)S(1)} %get-tuple-element.75.mine_ref), channel_id=1, source_target_pairs={{0,1},{1,0},{2,3},{3,2},{4,5},{5,4},{6,7},{7,6},{8,9},{9,8},{10,11... | collective-permute-start | bytes 172040 | tf_op jit(solution)/shard_map/ppermute | solution.py:32
  30.9 15.3 %collective-permute-start.12 = (bf16[64,2048]{1,0:T(8,128)(2,1)S(1)}, bf16[64,2048]{1,0:T(8,128)(2,1)S(1)}, u32[]{:S(2)}, u32[]{:S(2)}) collective-permute-start(bf16[64,2048]{1,0:T(8,128)(2,1)S(1)} %get-tuple-element.88), channel_id=1, source_target_pairs={{0,4},{2,6},{4,0},{6,2},{8,12},{10,14},{12,8},{14,10},{1,5},{3,7},... | collective-permute-start | bytes 786440 | tf_op jit(solution)/shard_map/ppermute | solution.py:36
  32.2 22.1 %collective-permute-start.11 = (bf16[64,2048]{1,0:T(8,128)(2,1)S(1)}, bf16[64,2048]{1,0:T(8,128)(2,1)S(1)}, u32[]{:S(2)}, u32[]{:S(2)}) collective-permute-start(bf16[64,2048]{1,0:T(8,128)(2,1)S(1)} %get-tuple-element.87), channel_id=1, source_target_pairs={{0,2},{2,0},{4,6},{6,4},{8,10},{10,8},{12,14},{14,12},{1,3},{3,1},... | collective-permute-start | bytes 786440 | tf_op jit(solution)/shard_map/ppermute | solution.py:36
  33.3 21.1 %collective-permute-start.13 = (bf16[64,2048]{1,0:T(8,128)(2,1)S(1)}, bf16[64,2048]{1,0:T(8,128)(2,1)S(1)}, u32[]{:S(2)}, u32[]{:S(2)}) collective-permute-start(bf16[64,2048]{1,0:T(8,128)(2,1)S(1)} %get-tuple-element.89), channel_id=1, source_target_pairs={{0,6},{2,4},{4,2},{6,0},{8,14},{10,12},{12,10},{14,8},{1,7},{3,5},... | collective-permute-start | bytes 786440 | tf_op jit(solution)/shard_map/ppermute | solution.py:36
  34.5 6.2 %collective-permute-start.9 = (s32[16,128]{1,0:T(8,128)S(1)}, s32[16,128]{1,0:T(8,128)S(1)}, u32[]{:S(2)}, u32[]{:S(2)}) collective-permute-start(s32[16,128]{1,0:T(8,128)S(1)} %select_select_fusion.info), channel_id=1, source_target_pairs={{0,16},{16,0},{1,17},{17,1},{2,18},{18,2},{3,19},{19,3},{4,20},{20... | collective-permute-start | bytes 24584 | tf_op jit(solution)/shard_map/ppermute | solution.py:32
  46.2 15.1 %collective-permute-start.14 = (bf16[112,1024]{1,0:T(8,128)(2,1)S(1)}, bf16[112,1024]{1,0:T(8,128)(2,1)S(1)}, u32[]{:S(2)}, u32[]{:S(2)}) collective-permute-start(bf16[112,1024]{1,0:T(8,128)(2,1)S(1)} %get-tuple-element.94), channel_id=1, source_target_pairs={{0,2},{2,0},{4,6},{6,4},{8,10},{10,8},{12,14},{14,12},{1,3},{3,1},... | collective-permute-start | bytes 688136 | tf_op jit(solution)/shard_map/ppermute | solution.py:36
  47.2 17.2 %collective-permute-start.15 = (bf16[112,1024]{1,0:T(8,128)(2,1)S(1)}, bf16[112,1024]{1,0:T(8,128)(2,1)S(1)}, u32[]{:S(2)}, u32[]{:S(2)}) collective-permute-start(bf16[112,1024]{1,0:T(8,128)(2,1)S(1)} %get-tuple-element.96), channel_id=1, source_target_pairs={{0,16},{16,0},{1,17},{17,1},{2,18},{18,2},{3,19},{19,3},{4,20},{20... | collective-permute-start | bytes 688136 | tf_op jit(solution)/shard_map/ppermute | solution.py:32
  48.7 15.7 %collective-permute-start.16 = (bf16[112,1024]{1,0:T(8,128)(2,1)S(1)}, bf16[112,1024]{1,0:T(8,128)(2,1)S(1)}, u32[]{:S(2)}, u32[]{:S(2)}) collective-permute-start(bf16[112,1024]{1,0:T(8,128)(2,1)S(1)} %get-tuple-element.98), channel_id=1, source_target_pairs={{0,18},{2,16},{4,22},{6,20},{8,26},{10,24},{12,30},{14,28},{16,2},... | collective-permute-start | bytes 688136 | tf_op jit(solution)/shard_map/ppermute | solution.py:476
  55.3 19.0 %collective-permute-start.19 = (bf16[64,2048]{1,0:T(8,128)(2,1)S(1)}, bf16[64,2048]{1,0:T(8,128)(2,1)S(1)}, u32[]{:S(2)}, u32[]{:S(2)}) collective-permute-start(bf16[64,2048]{1,0:T(8,128)(2,1)S(1)} %get-tuple-element.109), channel_id=1, source_target_pairs={{0,4},{2,6},{4,0},{6,2},{8,12},{10,14},{12,8},{14,10},{1,5},{3,7},... | collective-permute-start | bytes 786440 | tf_op jit(solution)/shard_map/ppermute | solution.py:36
  61.3 13.8 %collective-permute-start.18 = (bf16[64,2048]{1,0:T(8,128)(2,1)S(1)}, bf16[64,2048]{1,0:T(8,128)(2,1)S(1)}, u32[]{:S(2)}, u32[]{:S(2)}) collective-permute-start(bf16[64,2048]{1,0:T(8,128)(2,1)S(1)} %get-tuple-element.107), channel_id=1, source_target_pairs={{0,2},{2,0},{4,6},{6,4},{8,10},{10,8},{12,14},{14,12},{1,3},{3,1},... | collective-permute-start | bytes 786440 | tf_op jit(solution)/shard_map/ppermute | solution.py:36
  62.5 12.6 %collective-permute-start.20 = (bf16[64,2048]{1,0:T(8,128)(2,1)S(1)}, bf16[64,2048]{1,0:T(8,128)(2,1)S(1)}, u32[]{:S(2)}, u32[]{:S(2)}) collective-permute-start(bf16[64,2048]{1,0:T(8,128)(2,1)S(1)} %get-tuple-element.111), channel_id=1, source_target_pairs={{0,6},{2,4},{4,2},{6,0},{8,14},{10,12},{12,10},{14,8},{1,7},{3,5},... | collective-permute-start | bytes 786440 | tf_op jit(solution)/shard_map/ppermute | solution.py:36
  67.2 6.0 %collective-permute-start.17 = (f32[16,896]{1,0:T(8,128)S(1)}, f32[16,896]{1,0:T(8,128)S(1)}, u32[]{:S(2)}, u32[]{:S(2)}) collective-permute-start(f32[16,896]{1,0:T(8,128)S(1)} %get-tuple-element.99.mine_ref), channel_id=1, source_target_pairs={{0,1},{1,0},{2,3},{3,2},{4,5},{5,4},{6,7},{7,6},{8,9},{9,8},{10,11... | collective-permute-start | bytes 172040 | tf_op jit(solution)/shard_map/ppermute | solution.py:32
  67.3 25.8 %collective-permute-start.24 = (bf16[64,2048]{1,0:T(8,128)(2,1)S(1)}, bf16[64,2048]{1,0:T(8,128)(2,1)S(1)}, u32[]{:S(2)}, u32[]{:S(2)}) collective-permute-start(bf16[64,2048]{1,0:T(8,128)(2,1)S(1)} %get-tuple-element.90), channel_id=1, source_target_pairs={{0,8},{2,10},{4,12},{6,14},{8,0},{10,2},{12,4},{14,6},{1,9},{3,11}... | collective-permute-start | bytes 786440 | tf_op jit(solution)/shard_map/ppermute | solution.py:36
  76.2 20.4 %collective-permute-start.25 = (bf16[64,2048]{1,0:T(8,128)(2,1)S(1)}, bf16[64,2048]{1,0:T(8,128)(2,1)S(1)}, u32[]{:S(2)}, u32[]{:S(2)}) collective-permute-start(bf16[64,2048]{1,0:T(8,128)(2,1)S(1)} %get-tuple-element.112), channel_id=1, source_target_pairs={{0,8},{2,10},{4,12},{6,14},{8,0},{10,2},{12,4},{14,6},{1,9},{3,11}... | collective-permute-start | bytes 786440 | tf_op jit(solution)/shard_map/ppermute | solution.py:36
  78.6 7.4 %collective-permute-start.21 = (bf16[64,512]{1,0:T(8,128)(2,1)S(1)}, bf16[64,512]{1,0:T(8,128)(2,1)S(1)}, u32[]{:S(2)}, u32[]{:S(2)}) collective-permute-start(bf16[64,512]{1,0:T(8,128)(2,1)S(1)} %get-tuple-element.115), channel_id=1, source_target_pairs={{0,2},{2,0},{4,6},{6,4},{8,10},{10,8},{12,14},{14,12},{1,3},{3,1},... | collective-permute-start | bytes 196616 | tf_op jit(solution)/shard_map/ppermute | solution.py:36
  79.3 6.6 %collective-permute-start.22 = (bf16[64,512]{1,0:T(8,128)(2,1)S(1)}, bf16[64,512]{1,0:T(8,128)(2,1)S(1)}, u32[]{:S(2)}, u32[]{:S(2)}) collective-permute-start(bf16[64,512]{1,0:T(8,128)(2,1)S(1)} %get-tuple-element.116), channel_id=1, source_target_pairs={{0,4},{2,6},{4,0},{6,2},{8,12},{10,14},{12,8},{14,10},{1,5},{3,7},... | collective-permute-start | bytes 196616 | tf_op jit(solution)/shard_map/ppermute | solution.py:36
  80.7 5.3 %collective-permute-start.23 = (bf16[64,512]{1,0:T(8,128)(2,1)S(1)}, bf16[64,512]{1,0:T(8,128)(2,1)S(1)}, u32[]{:S(2)}, u32[]{:S(2)}) collective-permute-start(bf16[64,512]{1,0:T(8,128)(2,1)S(1)} %get-tuple-element.117), channel_id=1, source_target_pairs={{0,6},{2,4},{4,2},{6,0},{8,14},{10,12},{12,10},{14,8},{1,7},{3,5},... | collective-permute-start | bytes 196616 | tf_op jit(solution)/shard_map/ppermute | solution.py:36
  86.8 9.7 %collective-permute-start.26 = (bf16[64,512]{1,0:T(8,128)(2,1)S(1)}, bf16[64,512]{1,0:T(8,128)(2,1)S(1)}, u32[]{:S(2)}, u32[]{:S(2)}) collective-permute-start(bf16[64,512]{1,0:T(8,128)(2,1)S(1)} %get-tuple-element.118), channel_id=1, source_target_pairs={{0,8},{2,10},{4,12},{6,14},{8,0},{10,2},{12,4},{14,6},{1,9},{3,11}... | collective-permute-start | bytes 196616 | tf_op jit(solution)/shard_map/ppermute | solution.py:36

commit v12 on v11

--- a/solution.py
+++ b/solution.py
@@ -458,7 +458,7 @@
         )(info, g_full, base_weight)
 
     half = width // 2
-    wide_a = half
+    wide_a = width * 5 // 8
     sends_a = pack(_tie(info, *ready), 0, wide_a)
     got_a = to_near(sends_a)
     low, sums = through(_tie(info, sends_a[0]), 0, half, 1)
@@ -492,9 +492,9 @@
     far_a = to_far(dense_a)
 
     (high,) = through(_tie(info, dense_a[1]), half, width - half, 0)
-    gate = [high] + ([got_y] if shared else [])
+    gate = [high] + ([got_y, got_x, got_d] if shared else [])
     got_b = to_near(
-        [_tie(b, *gate) if k in (1, 3) else _tie(b, dense_a[1]) for k, b in enumerate(sends_b)]
+        [_tie(b, *gate) for k, b in enumerate(sends_b)]
     )
 
     if shared:
@@ -526,7 +526,7 @@
         [VMEM] * 3, [_whole((near_rows, cols))] * NEAR,
         [_shape((near_rows, cols), bf16)] * NEAR,
         [pltpu.VMEM((packed_rows, rows), bf16)],
-    )(_tie(info, grad_tokens), shrink_part, shrink_other, g_full)
+    )(_tie(info, grad_tokens, far_a[1]), shrink_part, shrink_other, g_full)
     got_u = to_near(up_sends)
 
     dense_b = dense(_tie(info, up_sends[0]), got_b)

time: 98.5 us -> 103 us (1.046)
  waiting for transfers between devices: 10.8 us -> 16.2 us
    ppermute x20, waiting for transfers between devices: 9.71 us -> 15.2 us  [_xor(): return lax.ppermute(x, 'dp', [(i, i ^ k) for i in range(n)])]
    ppermute x20, starting transfers between devices: 31.2 us -> 29.8 us  [_xor(): return lax.ppermute(x, 'dp', [(i, i ^ k) for i in range(n)])]
  transfers between devices with their start and end apart: 27 -> 27, of which waited for: 7 -> 9; matrix products, arithmetic and copies ran while one was open for 4% -> 4% of each run, Pallas kernels for 45% -> 42%
where the time goes in v12:
time: 103 us
  Pallas kernels  46.2 us (45%)
  starting transfers between devices  34.7 us (34%)
  waiting for transfers between devices  16.2 us (16%)
  other arithmetic  2.63 us (3%)
  local copies, waits for them, and re-layouts  2.33 us (2%)
    ppermute x20, starting transfers between devices, _xor(): return lax.ppermute(x, 'dp', [(i, i ^ k) for i in range(n)])  29.8 us
    ppermute x20, waiting for transfers between devices, _xor(): return lax.ppermute(x, 'dp', [(i, i ^ k) for i in range(n)])  15.2 us
    pallas_call x2, Pallas kernels, through(): _call(functools.partial(through_kernel, z, first), 'through', (1,), [VMEM...  9.59 us
    pallas_call x1, Pallas kernels, on_device(): _call(functools.partial(base_kernel, z), 'base', (1,), [pl.BlockSpec(memo...  7.78 us
    pallas_call x2, Pallas kernels, token_grads(): _call(functools.partial(tokens_kernel, z, first), 'token_grads', (steps,)...  7.73 us
    pallas_call x1, Pallas kernels, on_device(): _call(functools.partial(own_kernel, z), 'base_own', (1,), [VMEM] * 3, VME...  4.61 us
    pallas_call x2, Pallas kernels, pack(): _call(functools.partial(pack_kernel, z, NEAR, start), 'pack_down', (1,),...  3.95 us
    ppermute x6, starting transfers between devices, _swap(): return lax.ppermute(x, axis, [(0, 1), (1, 0)])  2.98 us
  transfers between devices with their start and end apart: 27, of which 9 were waited for; matrix products, arithmetic and copies ran while one was open for 4% of the time, Pallas kernels for 42%

profile of v12, /device:TPU:0, one launch (start us, length us, event | category | flops | bytes accessed | tf_op | source)
XLA Modules:
  0.0 103.0 jit_solution(8362687877191592939)
XLA Ops:
  0.6 4.1 %collective-permute-start = (bf16[4,16,512]{2,1,0:T(8,128)(2,1)}, bf16[4,16,512]{2,1,0:T(8,128)(2,1)S(1)}, u32[]{:S(2)}, u32[]{:S(2)}) collective-permute-start(bf16[4,16,512]{2,1,0:T(8,128)(2,1)} %param.11), channel_id=1, source_target_pairs={{0,8},{2,10},{4,12},{6,14},{8,0},{10,2},{12,4},{14,6},{1,9},{3,11}... | collective-permute-start | bytes 196616 | tf_op jit(solution)/shard_map/ppermute | solution.py:36
  5.7 1.6 %collective-permute-start.2 = (bf16[4,16,1024]{2,1,0:T(8,128)(2,1)S(1)}, bf16[4,16,1024]{2,1,0:T(8,128)(2,1)S(1)}, u32[]{:S(2)}, u32[]{:S(2)}) collective-permute-start(bf16[4,16,1024]{2,1,0:T(8,128)(2,1)S(1)} %get-tuple-element.127), channel_id=1, source_target_pairs={{0,2},{2,0},{4,6},{6,4},{8,10},{10,8},{12,14},{14,12},{1,3},{3,1},... | collective-permute-start | bytes 393224 | tf_op jit(solution)/shard_map/ppermute | solution.py:36
  8.9 1.8 %collective-permute-done.2 = bf16[4,16,1024]{2,1,0:T(8,128)(2,1)S(1)} collective-permute-done((bf16[4,16,1024]{2,1,0:T(8,128)(2,1)S(1)}, bf16[4,16,1024]{2,1,0:T(8,128)(2,1)S(1)}, u32[]{:S(2)}, u32[]{:S(2)}) %collective-permute-start.2) | collective-permute-done | bytes 131104 | tf_op jit(solution)/shard_map/ppermute | solution.py:36
  12.0 1.6 %collective-permute-start.5 = (bf16[144,512]{1,0:T(8,128)(2,1)S(1)}, bf16[144,512]{1,0:T(8,128)(2,1)S(1)}, u32[]{:S(2)}, u32[]{:S(2)}) collective-permute-start(bf16[144,512]{1,0:T(8,128)(2,1)S(1)} %pad_maximum_fusion.2.refs_0_), channel_id=1, source_target_pairs={{0,2},{2,0},{4,6},{6,4},{8,10},{10,8},{12,14},{14,12},{1,3},{3,1},... | collective-permute-start | bytes 442376 | tf_op jit(solution)/shard_map/ppermute | solution.py:36
  13.6 1.6 %collective-permute-start.4 = (bf16[144,512]{1,0:T(8,128)(2,1)S(1)}, bf16[144,512]{1,0:T(8,128)(2,1)S(1)}, u32[]{:S(2)}, u32[]{:S(2)}) collective-permute-start(bf16[144,512]{1,0:T(8,128)(2,1)S(1)} %pad_maximum_fusion.2.refs_0_), channel_id=1, source_target_pairs={{0,4},{2,6},{4,0},{6,2},{8,12},{10,14},{12,8},{14,10},{1,5},{3,7},... | collective-permute-start | bytes 442376 | tf_op jit(solution)/shard_map/ppermute | solution.py:36
  15.6 1.3 %copy-done = bf16[896,512]{1,0:T(8,128)(2,1)S(1)} copy-done((bf16[896,512]{1,0:T(8,128)(2,1)S(1)}, bf16[896,512]{1,0:T(8,128)(2,1)}, u32[]{:S(2)}) %copy-start) | copy-done | bytes 917528
  17.0 7.8 %base.1 = (bf16[896,512]{1,0:T(8,128)(2,1)S(1)}, bf16[896,1024]{1,0:T(8,128)(2,1)S(1)}, bf16[896,4096]{1,0:T(8,128)(2,1)S(1)}) custom-call(s32[16,128]{1,0:T(8,128)S(1)} %select_select_fusion.1.info, bf16[896,4096]{1,0:T(8,128)(2,1)} %x_hbm.1, bf16[4096,1024]{1,0:T(8,128)(2,1)} %w_ref.5, bf16[896,512]{1,0:T(8,128)(2,1)S(1)} %copy-done, ...), custom_call_target="tpu_custom_call" | custom-call | flops 1 | bytes 1 | tf_op jit(solution)/shard_map/base/pallas_call | solution.py:388
  29.0 2.2 %pack_down.2 = (bf16[64,2560]{1,0:T(8,128)(2,1)S(1)}, bf16[64,2560]{1,0:T(8,128)(2,1)S(1)}, bf16[64,2560]{1,0:T(8,128)(2,1)S(1)}, bf16[64,2560]{1,0:T(8,128)(2,1)S(1)}) custom-call(s32[16,128]{1,0:T(8,128)S(1)} %select_select_fusion.info, f32[16,896]{1,0:T(8,128)S(1)} %get-tuple-element.75.mine_ref, f32[16,896]{1,0:T(8,128)S(1)} %collective-permute-done.8.other_ref, ...), custom_call_target="tpu_custom_call" | custom-call | flops 1 | bytes 1 | tf_op jit(solution)/shard_map/pack_down/pallas_call | solution.py:431
  31.2 1.3 %collective-permute-start.12 = (bf16[64,2560]{1,0:T(8,128)(2,1)S(1)}, bf16[64,2560]{1,0:T(8,128)(2,1)S(1)}, u32[]{:S(2)}, u32[]{:S(2)}) collective-permute-start(bf16[64,2560]{1,0:T(8,128)(2,1)S(1)} %get-tuple-element.88), channel_id=1, source_target_pairs={{0,4},{2,6},{4,0},{6,2},{8,12},{10,14},{12,8},{14,10},{1,5},{3,7},... | collective-permute-start | bytes 983048 | tf_op jit(solution)/shard_map/ppermute | solution.py:36
  33.5 1.2 %collective-permute-start.13 = (bf16[64,2560]{1,0:T(8,128)(2,1)S(1)}, bf16[64,2560]{1,0:T(8,128)(2,1)S(1)}, u32[]{:S(2)}, u32[]{:S(2)}) collective-permute-start(bf16[64,2560]{1,0:T(8,128)(2,1)S(1)} %get-tuple-element.89), channel_id=1, source_target_pairs={{0,6},{2,4},{4,2},{6,0},{8,14},{10,12},{12,10},{14,8},{1,7},{3,5},... | collective-permute-start | bytes 983048 | tf_op jit(solution)/shard_map/ppermute | solution.py:36
  34.8 1.5 %collective-permute-start.9 = (s32[16,128]{1,0:T(8,128)S(1)}, s32[16,128]{1,0:T(8,128)S(1)}, u32[]{:S(2)}, u32[]{:S(2)}) collective-permute-start(s32[16,128]{1,0:T(8,128)S(1)} %select_select_fusion.info), channel_id=1, source_target_pairs={{0,16},{16,0},{1,17},{17,1},{2,18},{18,2},{3,19},{19,3},{4,20},{20... | collective-permute-start | bytes 24584 | tf_op jit(solution)/shard_map/ppermute | solution.py:32
  36.3 4.7 %through.2 = (f32[896,2048]{1,0:T(8,128)S(1)}, bf16[2,64,128]{2,1,0:T(8,128)(2,1)S(1)}) custom-call(s32[16,128]{1,0:T(8,128)S(1)} %select_select_fusion.info, bf16[896,1024]{1,0:T(8,128)(2,1)S(1)} %get-tuple-element.73.g_ref, bf16[4096,1024]{1,0:T(8,128)(2,1)S(1)} %bitcast.20), custom_call_target="tpu_custom_call" | custom-call | flops 1 | bytes 1 | tf_op jit(solution)/shard_map/through/pallas_call | solution.py:455
  42.1 1.7 %pack_down.3 = (bf16[64,1536]{1,0:T(8,128)(2,1)S(1)}, bf16[64,1536]{1,0:T(8,128)(2,1)S(1)}, bf16[64,1536]{1,0:T(8,128)(2,1)S(1)}, bf16[64,1536]{1,0:T(8,128)(2,1)S(1)}) custom-call(s32[16,128]{1,0:T(8,128)S(1)} %select_select_fusion.info, f32[16,896]{1,0:T(8,128)S(1)} %get-tuple-element.75.mine_ref, f32[16,896]{1,0:T(8,128)S(1)} %collective-permute-done.8.other_ref, ...), custom_call_target="tpu_custom_call" | custom-call | flops 1 | bytes 1 | tf_op jit(solution)/shard_map/pack_down/pallas_call | solution.py:431
  43.8 1.1 %collective-permute-start.15 = (bf16[112,1024]{1,0:T(8,128)(2,1)S(1)}, bf16[112,1024]{1,0:T(8,128)(2,1)S(1)}, u32[]{:S(2)}, u32[]{:S(2)}) collective-permute-start(bf16[112,1024]{1,0:T(8,128)(2,1)S(1)} %get-tuple-element.96), channel_id=1, source_target_pairs={{0,16},{16,0},{1,17},{17,1},{2,18},{18,2},{3,19},{19,3},{4,20},{20... | collective-permute-start | bytes 688136 | tf_op jit(solution)/shard_map/ppermute | solution.py:32
  44.9 1.9 %collective-permute-start.16 = (bf16[112,1024]{1,0:T(8,128)(2,1)S(1)}, bf16[112,1024]{1,0:T(8,128)(2,1)S(1)}, u32[]{:S(2)}, u32[]{:S(2)}) collective-permute-start(bf16[112,1024]{1,0:T(8,128)(2,1)S(1)} %get-tuple-element.98), channel_id=1, source_target_pairs={{0,18},{2,16},{4,22},{6,20},{8,26},{10,24},{12,30},{14,28},{16,2},... | collective-permute-start | bytes 688136 | tf_op jit(solution)/shard_map/ppermute | solution.py:476
  48.6 4.6 %base_own.1.base_ref = f32[896,512]{1,0:T(8,128)S(1)} custom-call(s32[16,128]{1,0:T(8,128)S(1)} %select_select_fusion.info, bf16[896,4096]{1,0:T(8,128)(2,1)S(1)} %get-tuple-element.76.x_ref, bf16[4096,1024]{1,0:T(8,128)(2,1)S(1)} %bitcast.20, bf16[896,512]{1,0:T(8,128)(2,1)S(1)} %collective-permute-done.7.far_ref), custom_call_target="tpu_custom_call" | custom-call | flops 1 | bytes 1 | tf_op jit(solution)/shard_map/base_own/pallas_call | solution.py:487
  53.2 5.4 %collective-permute-done.13.refs_3_ = bf16[64,2560]{1,0:T(8,128)(2,1)S(1)} collective-permute-done((bf16[64,2560]{1,0:T(8,128)(2,1)S(1)}, bf16[64,2560]{1,0:T(8,128)(2,1)S(1)}, u32[]{:S(2)}, u32[]{:S(2)}) %collective-permute-start.13) | collective-permute-done | bytes 327712 | tf_op jit(solution)/shard_map/ppermute | solution.py:36
  59.6 1.8 %collective-permute-start.17 = (bf16[64,2560]{1,0:T(8,128)(2,1)S(1)}, bf16[64,2560]{1,0:T(8,128)(2,1)S(1)}, u32[]{:S(2)}, u32[]{:S(2)}) collective-permute-start(bf16[64,2560]{1,0:T(8,128)(2,1)S(1)} %get-tuple-element.90), channel_id=1, source_target_pairs={{0,8},{2,10},{4,12},{6,14},{8,0},{10,2},{12,4},{14,6},{1,9},{3,11}... | collective-permute-start | bytes 983048 | tf_op jit(solution)/shard_map/ppermute | solution.py:36
  61.3 4.8 %through.3.through_ref = f32[896,2048]{1,0:T(8,128)S(1)} custom-call(s32[16,128]{1,0:T(8,128)S(1)} %select_select_fusion.info, bf16[896,1024]{1,0:T(8,128)(2,1)S(1)} %get-tuple-element.73.g_ref, bf16[4096,1024]{1,0:T(8,128)(2,1)S(1)} %bitcast.20), custom_call_target="tpu_custom_call" | custom-call | flops 1 | bytes 1 | tf_op jit(solution)/shard_map/through/pallas_call | solution.py:455
  66.7 2.8 %collective-permute-start.20 = (bf16[64,1536]{1,0:T(8,128)(2,1)S(1)}, bf16[64,1536]{1,0:T(8,128)(2,1)S(1)}, u32[]{:S(2)}, u32[]{:S(2)}) collective-permute-start(bf16[64,1536]{1,0:T(8,128)(2,1)S(1)} %get-tuple-element.109), channel_id=1, source_target_pairs={{0,4},{2,6},{4,0},{6,2},{8,12},{10,14},{12,8},{14,10},{1,5},{3,7},... | collective-permute-start | bytes 589832 | tf_op jit(solution)/shard_map/ppermute | solution.py:36
  70.4 2.8 %shrink.1 = (bf16[112,4096]{1,0:T(8,128)(2,1)S(1)}, f32[16,896]{1,0:T(8,128)S(1)}) custom-call(s32[16,128]{1,0:T(8,128)S(1)} %select_select_fusion.info, bf16[896,4096]{1,0:T(8,128)(2,1)S(1)} %get-tuple-element.76.x_ref, bf16[112,1024]{1,0:T(8,128)(2,1)S(1)} %get-tuple-element.81.refs_0_, bf16[112,1024]{1,0:T(8,128)(2,1)S(1)} %collective-permute-done.14.refs_1_, ...), custom_call_target="tpu_custom_call" | custom-call | flops 1 | bytes 1 | tf_op jit(solution)/shard_map/shrink/pallas_call | solution.py:502
  73.3 3.9 %token_grads.2.refs_0_ = bf16[896,4096]{1,0:T(8,128)(2,1)} custom-call(s32[16,128]{1,0:T(8,128)S(1)} %select_select_fusion.info, f32[896,2048]{1,0:T(8,128)S(1)} %get-tuple-element.79.through_ref, f32[16,896]{1,0:T(8,128)S(1)} %get-tuple-element.75.mine_ref, f32[16,896]{1,0:T(8,128)S(1)} %collective-permute-done.8.other_ref, ...), custom_call_target="tpu_custom_call" | custom-call | flops 1 | bytes 1 | tf_op jit(solution)/shard_map/token_grads/pallas_call | solution.py:514
  77.2 1.1 %pack_up.1 = (bf16[64,512]{1,0:T(8,128)(2,1)S(1)}, bf16[64,512]{1,0:T(8,128)(2,1)S(1)}, bf16[64,512]{1,0:T(8,128)(2,1)S(1)}, bf16[64,512]{1,0:T(8,128)(2,1)S(1)}) custom-call(s32[16,128]{1,0:T(8,128)S(1)} %select_select_fusion.info, f32[16,896]{1,0:T(8,128)S(1)} %get-tuple-element.99.mine_ref, f32[16,896]{1,0:T(8,128)S(1)} %collective-permute-done.18.other_ref, ...), custom_call_target="tpu_custom_call" | custom-call | flops 1 | bytes 1 | tf_op jit(solution)/shard_map/pack_up/pallas_call | solution.py:524
  78.4 2.9 %collective-permute-done.21.refs_3_ = bf16[64,1536]{1,0:T(8,128)(2,1)S(1)} collective-permute-done((bf16[64,1536]{1,0:T(8,128)(2,1)S(1)}, bf16[64,1536]{1,0:T(8,128)(2,1)S(1)}, u32[]{:S(2)}, u32[]{:S(2)}) %collective-permute-start.21) | collective-permute-done | bytes 196640 | tf_op jit(solution)/shard_map/ppermute | solution.py:36
  82.2 3.0 %collective-permute-start.25 = (bf16[64,1536]{1,0:T(8,128)(2,1)S(1)}, bf16[64,1536]{1,0:T(8,128)(2,1)S(1)}, u32[]{:S(2)}, u32[]{:S(2)}) collective-permute-start(bf16[64,1536]{1,0:T(8,128)(2,1)S(1)} %get-tuple-element.112), channel_id=1, source_target_pairs={{0,8},{2,10},{4,12},{6,14},{8,0},{10,2},{12,4},{14,6},{1,9},{3,11}... | collective-permute-start | bytes 589832 | tf_op jit(solution)/shard_map/ppermute | solution.py:36
  85.2 3.9 %collective-permute-start.23 = (bf16[64,512]{1,0:T(8,128)(2,1)S(1)}, bf16[64,512]{1,0:T(8,128)(2,1)S(1)}, u32[]{:S(2)}, u32[]{:S(2)}) collective-permute-start(bf16[64,512]{1,0:T(8,128)(2,1)S(1)} %get-tuple-element.116), channel_id=1, source_target_pairs={{0,4},{2,6},{4,0},{6,2},{8,12},{10,14},{12,8},{14,10},{1,5},{3,7},... | collective-permute-start | bytes 196616 | tf_op jit(solution)/shard_map/ppermute | solution.py:36
  89.1 3.9 %token_grads.3 = bf16[896,4096]{1,0:T(8,128)(2,1)} custom-call(s32[16,128]{1,0:T(8,128)S(1)} %select_select_fusion.info, f32[896,2048]{1,0:T(8,128)S(1)} %through.3.through_ref, f32[16,896]{1,0:T(8,128)S(1)} %get-tuple-element.75.mine_ref, f32[16,896]{1,0:T(8,128)S(1)} %collective-permute-done.8.other_ref, ...), custom_call_target="tpu_custom_call", output_to_operand_aliasing={{}: (5, {})} | custom-call | flops 1 | bytes 1 | tf_op jit(solution)/shard_map/token_grads/pallas_call | solution.py:514
  93.0 1.4 %collective-permute-done.23.refs_2_ = bf16[64,512]{1,0:T(8,128)(2,1)S(1)} collective-permute-done((bf16[64,512]{1,0:T(8,128)(2,1)S(1)}, bf16[64,512]{1,0:T(8,128)(2,1)S(1)}, u32[]{:S(2)}, u32[]{:S(2)}) %collective-permute-start.23) | collective-permute-done | bytes 65568 | tf_op jit(solution)/shard_map/ppermute | solution.py:36
  95.3 1.9 %collective-permute-start.26 = (bf16[64,512]{1,0:T(8,128)(2,1)S(1)}, bf16[64,512]{1,0:T(8,128)(2,1)S(1)}, u32[]{:S(2)}, u32[]{:S(2)}) collective-permute-start(bf16[64,512]{1,0:T(8,128)(2,1)S(1)} %get-tuple-element.118), channel_id=1, source_target_pairs={{0,8},{2,10},{4,12},{6,14},{8,0},{10,2},{12,4},{14,6},{1,9},{3,11}... | collective-permute-start | bytes 196616 | tf_op jit(solution)/shard_map/ppermute | solution.py:36
  97.2 2.0 %projected.1 = bf16[896,512]{1,0:T(8,128)(2,1)} custom-call(s32[16,128]{1,0:T(8,128)S(1)} %select_select_fusion.info, f32[896,512]{1,0:T(8,128)S(1)} %base_own.1.base_ref, f32[16,896]{1,0:T(8,128)S(1)} %get-tuple-element.99.mine_ref, f32[16,896]{1,0:T(8,128)S(1)} %collective-permute-done.18.other_ref, bf16[112,512]{1,0:T(8,128)(2,1)S(1)} %get-tuple-element.120.up_ref), custom_call_target="tpu_custom_call" | custom-call | flops 1 | bytes 1 | tf_op jit(solution)/shard_map/projected/pallas_call | solution.py:539
  99.2 2.0 %collective-permute-done.26.refs_5_ = bf16[64,512]{1,0:T(8,128)(2,1)S(1)} collective-permute-done((bf16[64,512]{1,0:T(8,128)(2,1)S(1)}, bf16[64,512]{1,0:T(8,128)(2,1)S(1)}, u32[]{:S(2)}, u32[]{:S(2)}) %collective-permute-start.26) | collective-permute-done | bytes 65568 | tf_op jit(solution)/shard_map/ppermute | solution.py:36
  101.2 1.8 %final.1 = (f32[64,4096]{1,0:T(8,128)}, f32[64,512]{1,0:T(8,128)}) custom-call(s32[16,128]{1,0:T(8,128)S(1)} %select_select_fusion.info, f32[64,2560]{1,0:T(8,128)S(1)} %get-tuple-element.121.refs_0_, bf16[64,2560]{1,0:T(8,128)(2,1)S(1)} %collective-permute-done.17.refs_1_, f32[64,1536]{1,0:T(8,128)S(1)} %get-tuple-element.122.refs_2_, ...), custom_call_target="tpu_custom_call" | custom-call | flops 1 | bytes 1 | tf_op jit(solution)/shard_map/final/pallas_call | solution.py:549
  (65 shorter events, 16.6 us)
Async XLA Ops:
  0.6 10.5 %collective-permute-start = (bf16[4,16,512]{2,1,0:T(8,128)(2,1)}, bf16[4,16,512]{2,1,0:T(8,128)(2,1)S(1)}, u32[]{:S(2)}, u32[]{:S(2)}) collective-permute-start(bf16[4,16,512]{2,1,0:T(8,128)(2,1)} %param.11), channel_id=1, source_target_pairs={{0,8},{2,10},{4,12},{6,14},{8,0},{10,2},{12,4},{14,6},{1,9},{3,11}... | collective-permute-start | bytes 196616 | tf_op jit(solution)/shard_map/ppermute | solution.py:36
  5.7 5.0 %collective-permute-start.2 = (bf16[4,16,1024]{2,1,0:T(8,128)(2,1)S(1)}, bf16[4,16,1024]{2,1,0:T(8,128)(2,1)S(1)}, u32[]{:S(2)}, u32[]{:S(2)}) collective-permute-start(bf16[4,16,1024]{2,1,0:T(8,128)(2,1)S(1)} %get-tuple-element.127), channel_id=1, source_target_pairs={{0,2},{2,0},{4,6},{6,4},{8,10},{10,8},{12,14},{14,12},{1,3},{3,1},... | collective-permute-start | bytes 393224 | tf_op jit(solution)/shard_map/ppermute | solution.py:36
  7.3 8.3 %collective-permute-start.3 = (bf16[896,512]{1,0:T(8,128)(2,1)}, bf16[896,512]{1,0:T(8,128)(2,1)S(1)}, u32[]{:S(2)}, u32[]{:S(2)}) collective-permute-start(bf16[896,512]{1,0:T(8,128)(2,1)} %g_hbm.1), channel_id=1, source_target_pairs={{0,1},{1,0},{2,3},{3,2},{4,5},{5,4},{6,7},{7,6},{8,9},{9,8},{10,11... | collective-permute-start | bytes 2752520 | tf_op jit(solution)/shard_map/ppermute | solution.py:32
  10.8 14.0 %collective-permute-start.6 = (bf16[8,16,1024]{2,1,0:T(8,128)(2,1)S(1)}, bf16[8,16,1024]{2,1,0:T(8,128)(2,1)S(1)}, u32[]{:S(2)}, u32[]{:S(2)}) collective-permute-start(bf16[8,16,1024]{2,1,0:T(8,128)(2,1)S(1)} %pad_maximum_fusion.1.own_ref), channel_id=1, source_target_pairs={{0,8},{2,10},{4,12},{6,14},{8,0},{10,2},{12,4},{14,6},{1,9},{3,11}... | collective-permute-start | bytes 786440 | tf_op jit(solution)/shard_map/ppermute | solution.py:36
  12.0 12.8 %collective-permute-start.5 = (bf16[144,512]{1,0:T(8,128)(2,1)S(1)}, bf16[144,512]{1,0:T(8,128)(2,1)S(1)}, u32[]{:S(2)}, u32[]{:S(2)}) collective-permute-start(bf16[144,512]{1,0:T(8,128)(2,1)S(1)} %pad_maximum_fusion.2.refs_0_), channel_id=1, source_target_pairs={{0,2},{2,0},{4,6},{6,4},{8,10},{10,8},{12,14},{14,12},{1,3},{3,1},... | collective-permute-start | bytes 442376 | tf_op jit(solution)/shard_map/ppermute | solution.py:36
  13.6 11.2 %collective-permute-start.4 = (bf16[144,512]{1,0:T(8,128)(2,1)S(1)}, bf16[144,512]{1,0:T(8,128)(2,1)S(1)}, u32[]{:S(2)}, u32[]{:S(2)}) collective-permute-start(bf16[144,512]{1,0:T(8,128)(2,1)S(1)} %pad_maximum_fusion.2.refs_0_), channel_id=1, source_target_pairs={{0,4},{2,6},{4,0},{6,2},{8,12},{10,14},{12,8},{14,10},{1,5},{3,7},... | collective-permute-start | bytes 442376 | tf_op jit(solution)/shard_map/ppermute | solution.py:36
  15.2 10.4 %collective-permute-start.1 = (bf16[144,512]{1,0:T(8,128)(2,1)S(1)}, bf16[144,512]{1,0:T(8,128)(2,1)S(1)}, u32[]{:S(2)}, u32[]{:S(2)}) collective-permute-start(bf16[144,512]{1,0:T(8,128)(2,1)S(1)} %pad_maximum_fusion.2.refs_0_), channel_id=1, source_target_pairs={{0,6},{2,4},{4,2},{6,0},{8,14},{10,12},{12,10},{14,8},{1,7},{3,5},... | collective-permute-start | bytes 442376 | tf_op jit(solution)/shard_map/ppermute | solution.py:36
  15.6 20.7 %slice-start = ((s8[8388608]{0:T(1024)(128)(4,1)}), s8[4194304]{0:T(1024)(128)(4,1)S(1)}, s32[]{:S(2)}) async-start(s8[8388608]{0:T(1024)(128)(4,1)} %bitcast.19), calls=%async_computation | async-start | bytes 8388608
  15.6 20.7 %slice-start.1 = ((s8[8388608]{0:T(1024)(128)(4,1)}), s8[4194304]{0:T(1024)(128)(4,1)S(1)}, s32[]{:S(2)}) async-start(s8[8388608]{0:T(1024)(128)(4,1)} %bitcast.19), calls=%async_computation.1 | async-start | bytes 8388608
  15.6 1.3 %copy-start = (bf16[896,512]{1,0:T(8,128)(2,1)S(1)}, bf16[896,512]{1,0:T(8,128)(2,1)}, u32[]{:S(2)}) copy-start(bf16[896,512]{1,0:T(8,128)(2,1)} %g_hbm.1) | copy-start | bytes 2752516
  24.7 3.2 %collective-permute-start.7 = (bf16[896,512]{1,0:T(8,128)(2,1)S(1)}, bf16[896,512]{1,0:T(8,128)(2,1)S(1)}, u32[]{:S(2)}, u32[]{:S(2)}) collective-permute-start(bf16[896,512]{1,0:T(8,128)(2,1)S(1)} %get-tuple-element.66), channel_id=1, source_target_pairs={{0,1},{1,0},{2,3},{3,2},{4,5},{5,4},{6,7},{7,6},{8,9},{9,8},{10,11... | collective-permute-start | bytes 2752520 | tf_op jit(solution)/shard_map/ppermute | solution.py:32
  25.7 15.3 %collective-permute-start.10 = (bf16[16,16,1024]{2,1,0:T(8,128)(2,1)S(1)}, bf16[16,16,1024]{2,1,0:T(8,128)(2,1)S(1)}, u32[]{:S(2)}, u32[]{:S(2)}) collective-permute-start(bf16[16,16,1024]{2,1,0:T(8,128)(2,1)S(1)} %pad_maximum_fusion), channel_id=1, source_target_pairs={{0,4},{2,6},{4,0},{6,2},{8,12},{10,14},{12,8},{14,10},{1,5},{3,7},... | collective-permute-start | bytes 1572872 | tf_op jit(solution)/shard_map/ppermute | solution.py:36
  27.7 1.3 %collective-permute-start.8 = (f32[16,896]{1,0:T(8,128)S(1)}, f32[16,896]{1,0:T(8,128)S(1)}, u32[]{:S(2)}, u32[]{:S(2)}) collective-permute-start(f32[16,896]{1,0:T(8,128)S(1)} %get-tuple-element.75.mine_ref), channel_id=1, source_target_pairs={{0,1},{1,0},{2,3},{3,2},{4,5},{5,4},{6,7},{7,6},{8,9},{9,8},{10,11... | collective-permute-start | bytes 172040 | tf_op jit(solution)/shard_map/ppermute | solution.py:32
  31.2 16.4 %collective-permute-start.12 = (bf16[64,2560]{1,0:T(8,128)(2,1)S(1)}, bf16[64,2560]{1,0:T(8,128)(2,1)S(1)}, u32[]{:S(2)}, u32[]{:S(2)}) collective-permute-start(bf16[64,2560]{1,0:T(8,128)(2,1)S(1)} %get-tuple-element.88), channel_id=1, source_target_pairs={{0,4},{2,6},{4,0},{6,2},{8,12},{10,14},{12,8},{14,10},{1,5},{3,7},... | collective-permute-start | bytes 983048 | tf_op jit(solution)/shard_map/ppermute | solution.py:36
  32.5 20.7 %collective-permute-start.11 = (bf16[64,2560]{1,0:T(8,128)(2,1)S(1)}, bf16[64,2560]{1,0:T(8,128)(2,1)S(1)}, u32[]{:S(2)}, u32[]{:S(2)}) collective-permute-start(bf16[64,2560]{1,0:T(8,128)(2,1)S(1)} %get-tuple-element.87), channel_id=1, source_target_pairs={{0,2},{2,0},{4,6},{6,4},{8,10},{10,8},{12,14},{14,12},{1,3},{3,1},... | collective-permute-start | bytes 983048 | tf_op jit(solution)/shard_map/ppermute | solution.py:36
  33.5 25.0 %collective-permute-start.13 = (bf16[64,2560]{1,0:T(8,128)(2,1)S(1)}, bf16[64,2560]{1,0:T(8,128)(2,1)S(1)}, u32[]{:S(2)}, u32[]{:S(2)}) collective-permute-start(bf16[64,2560]{1,0:T(8,128)(2,1)S(1)} %get-tuple-element.89), channel_id=1, source_target_pairs={{0,6},{2,4},{4,2},{6,0},{8,14},{10,12},{12,10},{14,8},{1,7},{3,5},... | collective-permute-start | bytes 983048 | tf_op jit(solution)/shard_map/ppermute | solution.py:36
  34.8 6.2 %collective-permute-start.9 = (s32[16,128]{1,0:T(8,128)S(1)}, s32[16,128]{1,0:T(8,128)S(1)}, u32[]{:S(2)}, u32[]{:S(2)}) collective-permute-start(s32[16,128]{1,0:T(8,128)S(1)} %select_select_fusion.info), channel_id=1, source_target_pairs={{0,16},{16,0},{1,17},{17,1},{2,18},{18,2},{3,19},{19,3},{4,20},{20... | collective-permute-start | bytes 24584 | tf_op jit(solution)/shard_map/ppermute | solution.py:32
  43.8 22.4 %collective-permute-start.15 = (bf16[112,1024]{1,0:T(8,128)(2,1)S(1)}, bf16[112,1024]{1,0:T(8,128)(2,1)S(1)}, u32[]{:S(2)}, u32[]{:S(2)}) collective-permute-start(bf16[112,1024]{1,0:T(8,128)(2,1)S(1)} %get-tuple-element.96), channel_id=1, source_target_pairs={{0,16},{16,0},{1,17},{17,1},{2,18},{18,2},{3,19},{19,3},{4,20},{20... | collective-permute-start | bytes 688136 | tf_op jit(solution)/shard_map/ppermute | solution.py:32
  44.9 21.3 %collective-permute-start.16 = (bf16[112,1024]{1,0:T(8,128)(2,1)S(1)}, bf16[112,1024]{1,0:T(8,128)(2,1)S(1)}, u32[]{:S(2)}, u32[]{:S(2)}) collective-permute-start(bf16[112,1024]{1,0:T(8,128)(2,1)S(1)} %get-tuple-element.98), channel_id=1, source_target_pairs={{0,18},{2,16},{4,22},{6,20},{8,26},{10,24},{12,30},{14,28},{16,2},... | collective-permute-start | bytes 688136 | tf_op jit(solution)/shard_map/ppermute | solution.py:476
  47.6 18.6 %collective-permute-start.14 = (bf16[112,1024]{1,0:T(8,128)(2,1)S(1)}, bf16[112,1024]{1,0:T(8,128)(2,1)S(1)}, u32[]{:S(2)}, u32[]{:S(2)}) collective-permute-start(bf16[112,1024]{1,0:T(8,128)(2,1)S(1)} %get-tuple-element.94), channel_id=1, source_target_pairs={{0,2},{2,0},{4,6},{6,4},{8,10},{10,8},{12,14},{14,12},{1,3},{3,1},... | collective-permute-start | bytes 688136 | tf_op jit(solution)/shard_map/ppermute | solution.py:36
  59.6 17.6 %collective-permute-start.17 = (bf16[64,2560]{1,0:T(8,128)(2,1)S(1)}, bf16[64,2560]{1,0:T(8,128)(2,1)S(1)}, u32[]{:S(2)}, u32[]{:S(2)}) collective-permute-start(bf16[64,2560]{1,0:T(8,128)(2,1)S(1)} %get-tuple-element.90), channel_id=1, source_target_pairs={{0,8},{2,10},{4,12},{6,14},{8,0},{10,2},{12,4},{14,6},{1,9},{3,11}... | collective-permute-start | bytes 983048 | tf_op jit(solution)/shard_map/ppermute | solution.py:36
  66.2 12.1 %collective-permute-start.19 = (bf16[64,1536]{1,0:T(8,128)(2,1)S(1)}, bf16[64,1536]{1,0:T(8,128)(2,1)S(1)}, u32[]{:S(2)}, u32[]{:S(2)}) collective-permute-start(bf16[64,1536]{1,0:T(8,128)(2,1)S(1)} %get-tuple-element.107), channel_id=1, source_target_pairs={{0,2},{2,0},{4,6},{6,4},{8,10},{10,8},{12,14},{14,12},{1,3},{3,1},... | collective-permute-start | bytes 589832 | tf_op jit(solution)/shard_map/ppermute | solution.py:36
  66.7 11.7 %collective-permute-start.20 = (bf16[64,1536]{1,0:T(8,128)(2,1)S(1)}, bf16[64,1536]{1,0:T(8,128)(2,1)S(1)}, u32[]{:S(2)}, u32[]{:S(2)}) collective-permute-start(bf16[64,1536]{1,0:T(8,128)(2,1)S(1)} %get-tuple-element.109), channel_id=1, source_target_pairs={{0,4},{2,6},{4,0},{6,2},{8,12},{10,14},{12,8},{14,10},{1,5},{3,7},... | collective-permute-start | bytes 589832 | tf_op jit(solution)/shard_map/ppermute | solution.py:36
  69.5 11.7 %collective-permute-start.21 = (bf16[64,1536]{1,0:T(8,128)(2,1)S(1)}, bf16[64,1536]{1,0:T(8,128)(2,1)S(1)}, u32[]{:S(2)}, u32[]{:S(2)}) collective-permute-start(bf16[64,1536]{1,0:T(8,128)(2,1)S(1)} %get-tuple-element.111), channel_id=1, source_target_pairs={{0,6},{2,4},{4,2},{6,0},{8,14},{10,12},{12,10},{14,8},{1,7},{3,5},... | collective-permute-start | bytes 589832 | tf_op jit(solution)/shard_map/ppermute | solution.py:36
  73.3 4.0 %collective-permute-start.18 = (f32[16,896]{1,0:T(8,128)S(1)}, f32[16,896]{1,0:T(8,128)S(1)}, u32[]{:S(2)}, u32[]{:S(2)}) collective-permute-start(f32[16,896]{1,0:T(8,128)S(1)} %get-tuple-element.99.mine_ref), channel_id=1, source_target_pairs={{0,1},{1,0},{2,3},{3,2},{4,5},{5,4},{6,7},{7,6},{8,9},{9,8},{10,11... | collective-permute-start | bytes 172040 | tf_op jit(solution)/shard_map/ppermute | solution.py:32
  82.2 19.1 %collective-permute-start.25 = (bf16[64,1536]{1,0:T(8,128)(2,1)S(1)}, bf16[64,1536]{1,0:T(8,128)(2,1)S(1)}, u32[]{:S(2)}, u32[]{:S(2)}) collective-permute-start(bf16[64,1536]{1,0:T(8,128)(2,1)S(1)} %get-tuple-element.112), channel_id=1, source_target_pairs={{0,8},{2,10},{4,12},{6,14},{8,0},{10,2},{12,4},{14,6},{1,9},{3,11}... | collective-permute-start | bytes 589832 | tf_op jit(solution)/shard_map/ppermute | solution.py:36
  85.2 7.8 %collective-permute-start.22 = (bf16[64,512]{1,0:T(8,128)(2,1)S(1)}, bf16[64,512]{1,0:T(8,128)(2,1)S(1)}, u32[]{:S(2)}, u32[]{:S(2)}) collective-permute-start(bf16[64,512]{1,0:T(8,128)(2,1)S(1)} %get-tuple-element.115), channel_id=1, source_target_pairs={{0,2},{2,0},{4,6},{6,4},{8,10},{10,8},{12,14},{14,12},{1,3},{3,1},... | collective-permute-start | bytes 196616 | tf_op jit(solution)/shard_map/ppermute | solution.py:36
  85.2 9.2 %collective-permute-start.23 = (bf16[64,512]{1,0:T(8,128)(2,1)S(1)}, bf16[64,512]{1,0:T(8,128)(2,1)S(1)}, u32[]{:S(2)}, u32[]{:S(2)}) collective-permute-start(bf16[64,512]{1,0:T(8,128)(2,1)S(1)} %get-tuple-element.116), channel_id=1, source_target_pairs={{0,4},{2,6},{4,0},{6,2},{8,12},{10,14},{12,8},{14,10},{1,5},{3,7},... | collective-permute-start | bytes 196616 | tf_op jit(solution)/shard_map/ppermute | solution.py:36
  89.1 5.4 %collective-permute-start.24 = (bf16[64,512]{1,0:T(8,128)(2,1)S(1)}, bf16[64,512]{1,0:T(8,128)(2,1)S(1)}, u32[]{:S(2)}, u32[]{:S(2)}) collective-permute-start(bf16[64,512]{1,0:T(8,128)(2,1)S(1)} %get-tuple-element.117), channel_id=1, source_target_pairs={{0,6},{2,4},{4,2},{6,0},{8,14},{10,12},{12,10},{14,8},{1,7},{3,5},... | collective-permute-start | bytes 196616 | tf_op jit(solution)/shard_map/ppermute | solution.py:36
  95.3 5.9 %collective-permute-start.26 = (bf16[64,512]{1,0:T(8,128)(2,1)S(1)}, bf16[64,512]{1,0:T(8,128)(2,1)S(1)}, u32[]{:S(2)}, u32[]{:S(2)}) collective-permute-start(bf16[64,512]{1,0:T(8,128)(2,1)S(1)} %get-tuple-element.118), channel_id=1, source_target_pairs={{0,8},{2,10},{4,12},{6,14},{8,0},{10,2},{12,4},{14,6},{1,9},{3,11}... | collective-permute-start | bytes 196616 | tf_op jit(solution)/shard_map/ppermute | solution.py:36

commit v13 on v11

--- a/solution.py
+++ b/solution.py
@@ -526,7 +526,7 @@
         [VMEM] * 3, [_whole((near_rows, cols))] * NEAR,
         [_shape((near_rows, cols), bf16)] * NEAR,
         [pltpu.VMEM((packed_rows, rows), bf16)],
-    )(_tie(info, grad_tokens), shrink_part, shrink_other, g_full)
+    )(_tie(info, grad_tokens, far_a[1]), shrink_part, shrink_other, g_full)
     got_u = to_near(up_sends)
 
     dense_b = dense(_tie(info, up_sends[0]), got_b)

time: 98.5 us -> 96 us (0.975)
  waiting for transfers between devices: 10.8 us -> 8.87 us
    ppermute x20, waiting for transfers between devices: 9.71 us -> 7.82 us  [_xor(): return lax.ppermute(x, 'dp', [(i, i ^ k) for i in range(n)])]
  transfers between devices with their start and end apart: 27 -> 27, of which waited for: 7 -> 6; matrix products, arithmetic and copies ran while one was open for 4% -> 4% of each run, Pallas kernels for 45% -> 45%
where the time goes in v13:
time: 96 us; the launch traced here: 95.8 us
  Pallas kernels  46.2 us (48%)
  starting transfers between devices  34.9 us (36%)
  waiting for transfers between devices  8.87 us (9%)
  other arithmetic  2.63 us (3%)
  local copies, waits for them, and re-layouts  2.33 us (2%)
    ppermute x20, starting transfers between devices, _xor(): return lax.ppermute(x, 'dp', [(i, i ^ k) for i in range(n)])  30.5 us
    pallas_call x2, Pallas kernels, through(): _call(functools.partial(through_kernel, z, first), 'through', (1,), [VMEM...  9.59 us
    ppermute x20, waiting for transfers between devices, _xor(): return lax.ppermute(x, 'dp', [(i, i ^ k) for i in range(n)])  7.82 us
    pallas_call x1, Pallas kernels, on_device(): _call(functools.partial(base_kernel, z), 'base', (1,), [pl.BlockSpec(memo...  7.78 us
    pallas_call x2, Pallas kernels, token_grads(): _call(functools.partial(tokens_kernel, z, first), 'token_grads', (steps,)...  7.73 us
    pallas_call x1, Pallas kernels, on_device(): _call(functools.partial(own_kernel, z), 'base_own', (1,), [VMEM] * 3, VME...  4.61 us
    pallas_call x2, Pallas kernels, pack(): _call(functools.partial(pack_kernel, z, NEAR, start), 'pack_down', (1,),...  3.94 us
    ppermute x6, starting transfers between devices, _swap(): return lax.ppermute(x, axis, [(0, 1), (1, 0)])  3.35 us
  transfers between devices with their start and end apart: 27, of which 6 were waited for; matrix products, arithmetic and copies ran while one was open for 4% of the time, Pallas kernels for 45%

profile of v13, /device:TPU:0, one launch (start us, length us, event | category | flops | bytes accessed | tf_op | source)
XLA Modules:
  0.0 95.8 jit_solution(5181397901768597936)
XLA Ops:
  0.6 4.1 %collective-permute-start = (bf16[4,16,512]{2,1,0:T(8,128)(2,1)}, bf16[4,16,512]{2,1,0:T(8,128)(2,1)S(1)}, u32[]{:S(2)}, u32[]{:S(2)}) collective-permute-start(bf16[4,16,512]{2,1,0:T(8,128)(2,1)} %param.11), channel_id=1, source_target_pairs={{0,8},{2,10},{4,12},{6,14},{8,0},{10,2},{12,4},{14,6},{1,9},{3,11}... | collective-permute-start | bytes 196616 | tf_op jit(solution)/shard_map/ppermute | solution.py:36
  5.7 1.6 %collective-permute-start.2 = (bf16[4,16,1024]{2,1,0:T(8,128)(2,1)S(1)}, bf16[4,16,1024]{2,1,0:T(8,128)(2,1)S(1)}, u32[]{:S(2)}, u32[]{:S(2)}) collective-permute-start(bf16[4,16,1024]{2,1,0:T(8,128)(2,1)S(1)} %get-tuple-element.127), channel_id=1, source_target_pairs={{0,2},{2,0},{4,6},{6,4},{8,10},{10,8},{12,14},{14,12},{1,3},{3,1},... | collective-permute-start | bytes 393224 | tf_op jit(solution)/shard_map/ppermute | solution.py:36
  8.9 1.8 %collective-permute-done.2 = bf16[4,16,1024]{2,1,0:T(8,128)(2,1)S(1)} collective-permute-done((bf16[4,16,1024]{2,1,0:T(8,128)(2,1)S(1)}, bf16[4,16,1024]{2,1,0:T(8,128)(2,1)S(1)}, u32[]{:S(2)}, u32[]{:S(2)}) %collective-permute-start.2) | collective-permute-done | bytes 131104 | tf_op jit(solution)/shard_map/ppermute | solution.py:36
  12.0 1.6 %collective-permute-start.5 = (bf16[144,512]{1,0:T(8,128)(2,1)S(1)}, bf16[144,512]{1,0:T(8,128)(2,1)S(1)}, u32[]{:S(2)}, u32[]{:S(2)}) collective-permute-start(bf16[144,512]{1,0:T(8,128)(2,1)S(1)} %pad_maximum_fusion.2.refs_0_), channel_id=1, source_target_pairs={{0,2},{2,0},{4,6},{6,4},{8,10},{10,8},{12,14},{14,12},{1,3},{3,1},... | collective-permute-start | bytes 442376 | tf_op jit(solution)/shard_map/ppermute | solution.py:36
  13.6 1.6 %collective-permute-start.4 = (bf16[144,512]{1,0:T(8,128)(2,1)S(1)}, bf16[144,512]{1,0:T(8,128)(2,1)S(1)}, u32[]{:S(2)}, u32[]{:S(2)}) collective-permute-start(bf16[144,512]{1,0:T(8,128)(2,1)S(1)} %pad_maximum_fusion.2.refs_0_), channel_id=1, source_target_pairs={{0,4},{2,6},{4,0},{6,2},{8,12},{10,14},{12,8},{14,10},{1,5},{3,7},... | collective-permute-start | bytes 442376 | tf_op jit(solution)/shard_map/ppermute | solution.py:36
  15.6 1.3 %copy-done = bf16[896,512]{1,0:T(8,128)(2,1)S(1)} copy-done((bf16[896,512]{1,0:T(8,128)(2,1)S(1)}, bf16[896,512]{1,0:T(8,128)(2,1)}, u32[]{:S(2)}) %copy-start) | copy-done | bytes 917528
  17.0 7.8 %base.1 = (bf16[896,512]{1,0:T(8,128)(2,1)S(1)}, bf16[896,1024]{1,0:T(8,128)(2,1)S(1)}, bf16[896,4096]{1,0:T(8,128)(2,1)S(1)}) custom-call(s32[16,128]{1,0:T(8,128)S(1)} %select_select_fusion.1.info, bf16[896,4096]{1,0:T(8,128)(2,1)} %x_hbm.1, bf16[4096,1024]{1,0:T(8,128)(2,1)} %w_ref.5, bf16[896,512]{1,0:T(8,128)(2,1)S(1)} %copy-done, ...), custom_call_target="tpu_custom_call" | custom-call | flops 1 | bytes 1 | tf_op jit(solution)/shard_map/base/pallas_call | solution.py:388
  29.0 2.0 %pack_down.2 = (bf16[64,2048]{1,0:T(8,128)(2,1)S(1)}, bf16[64,2048]{1,0:T(8,128)(2,1)S(1)}, bf16[64,2048]{1,0:T(8,128)(2,1)S(1)}, bf16[64,2048]{1,0:T(8,128)(2,1)S(1)}) custom-call(s32[16,128]{1,0:T(8,128)S(1)} %select_select_fusion.info, f32[16,896]{1,0:T(8,128)S(1)} %get-tuple-element.75.mine_ref, f32[16,896]{1,0:T(8,128)S(1)} %collective-permute-done.8.other_ref, ...), custom_call_target="tpu_custom_call" | custom-call | flops 1 | bytes 1 | tf_op jit(solution)/shard_map/pack_down/pallas_call | solution.py:431
  30.9 1.3 %collective-permute-start.12 = (bf16[64,2048]{1,0:T(8,128)(2,1)S(1)}, bf16[64,2048]{1,0:T(8,128)(2,1)S(1)}, u32[]{:S(2)}, u32[]{:S(2)}) collective-permute-start(bf16[64,2048]{1,0:T(8,128)(2,1)S(1)} %get-tuple-element.88), channel_id=1, source_target_pairs={{0,4},{2,6},{4,0},{6,2},{8,12},{10,14},{12,8},{14,10},{1,5},{3,7},... | collective-permute-start | bytes 786440 | tf_op jit(solution)/shard_map/ppermute | solution.py:36
  32.2 1.1 %collective-permute-start.11 = (bf16[64,2048]{1,0:T(8,128)(2,1)S(1)}, bf16[64,2048]{1,0:T(8,128)(2,1)S(1)}, u32[]{:S(2)}, u32[]{:S(2)}) collective-permute-start(bf16[64,2048]{1,0:T(8,128)(2,1)S(1)} %get-tuple-element.87), channel_id=1, source_target_pairs={{0,2},{2,0},{4,6},{6,4},{8,10},{10,8},{12,14},{14,12},{1,3},{3,1},... | collective-permute-start | bytes 786440 | tf_op jit(solution)/shard_map/ppermute | solution.py:36
  33.3 1.2 %collective-permute-start.13 = (bf16[64,2048]{1,0:T(8,128)(2,1)S(1)}, bf16[64,2048]{1,0:T(8,128)(2,1)S(1)}, u32[]{:S(2)}, u32[]{:S(2)}) collective-permute-start(bf16[64,2048]{1,0:T(8,128)(2,1)S(1)} %get-tuple-element.89), channel_id=1, source_target_pairs={{0,6},{2,4},{4,2},{6,0},{8,14},{10,12},{12,10},{14,8},{1,7},{3,5},... | collective-permute-start | bytes 786440 | tf_op jit(solution)/shard_map/ppermute | solution.py:36
  34.5 1.5 %collective-permute-start.9 = (s32[16,128]{1,0:T(8,128)S(1)}, s32[16,128]{1,0:T(8,128)S(1)}, u32[]{:S(2)}, u32[]{:S(2)}) collective-permute-start(s32[16,128]{1,0:T(8,128)S(1)} %select_select_fusion.info), channel_id=1, source_target_pairs={{0,16},{16,0},{1,17},{17,1},{2,18},{18,2},{3,19},{19,3},{4,20},{20... | collective-permute-start | bytes 24584 | tf_op jit(solution)/shard_map/ppermute | solution.py:32
  36.0 4.7 %through.2 = (f32[896,2048]{1,0:T(8,128)S(1)}, bf16[2,64,128]{2,1,0:T(8,128)(2,1)S(1)}) custom-call(s32[16,128]{1,0:T(8,128)S(1)} %select_select_fusion.info, bf16[896,1024]{1,0:T(8,128)(2,1)S(1)} %get-tuple-element.73.g_ref, bf16[4096,1024]{1,0:T(8,128)(2,1)S(1)} %bitcast.20), custom_call_target="tpu_custom_call" | custom-call | flops 1 | bytes 1 | tf_op jit(solution)/shard_map/through/pallas_call | solution.py:455
  41.8 2.0 %pack_down.3 = (bf16[64,2048]{1,0:T(8,128)(2,1)S(1)}, bf16[64,2048]{1,0:T(8,128)(2,1)S(1)}, bf16[64,2048]{1,0:T(8,128)(2,1)S(1)}, bf16[64,2048]{1,0:T(8,128)(2,1)S(1)}) custom-call(s32[16,128]{1,0:T(8,128)S(1)} %select_select_fusion.info, f32[16,896]{1,0:T(8,128)S(1)} %get-tuple-element.75.mine_ref, f32[16,896]{1,0:T(8,128)S(1)} %collective-permute-done.8.other_ref, ...), custom_call_target="tpu_custom_call" | custom-call | flops 1 | bytes 1 | tf_op jit(solution)/shard_map/pack_down/pallas_call | solution.py:431
  43.8 2.4 %collective-permute-done.12.refs_2_ = bf16[64,2048]{1,0:T(8,128)(2,1)S(1)} collective-permute-done((bf16[64,2048]{1,0:T(8,128)(2,1)S(1)}, bf16[64,2048]{1,0:T(8,128)(2,1)S(1)}, u32[]{:S(2)}, u32[]{:S(2)}) %collective-permute-start.12) | collective-permute-done | bytes 262176 | tf_op jit(solution)/shard_map/ppermute | solution.py:36
  47.2 1.5 %collective-permute-start.15 = (bf16[112,1024]{1,0:T(8,128)(2,1)S(1)}, bf16[112,1024]{1,0:T(8,128)(2,1)S(1)}, u32[]{:S(2)}, u32[]{:S(2)}) collective-permute-start(bf16[112,1024]{1,0:T(8,128)(2,1)S(1)} %get-tuple-element.96), channel_id=1, source_target_pairs={{0,16},{16,0},{1,17},{17,1},{2,18},{18,2},{3,19},{19,3},{4,20},{20... | collective-permute-start | bytes 688136 | tf_op jit(solution)/shard_map/ppermute | solution.py:32
  49.7 4.6 %base_own.1.base_ref = f32[896,512]{1,0:T(8,128)S(1)} custom-call(s32[16,128]{1,0:T(8,128)S(1)} %select_select_fusion.info, bf16[896,4096]{1,0:T(8,128)(2,1)S(1)} %get-tuple-element.76.x_ref, bf16[4096,1024]{1,0:T(8,128)(2,1)S(1)} %bitcast.20, bf16[896,512]{1,0:T(8,128)(2,1)S(1)} %collective-permute-done.7.far_ref), custom_call_target="tpu_custom_call" | custom-call | flops 1 | bytes 1 | tf_op jit(solution)/shard_map/base_own/pallas_call | solution.py:487
  55.3 2.5 %collective-permute-start.17 = (bf16[64,2048]{1,0:T(8,128)(2,1)S(1)}, bf16[64,2048]{1,0:T(8,128)(2,1)S(1)}, u32[]{:S(2)}, u32[]{:S(2)}) collective-permute-start(bf16[64,2048]{1,0:T(8,128)(2,1)S(1)} %get-tuple-element.90), channel_id=1, source_target_pairs={{0,8},{2,10},{4,12},{6,14},{8,0},{10,2},{12,4},{14,6},{1,9},{3,11}... | collective-permute-start | bytes 786440 | tf_op jit(solution)/shard_map/ppermute | solution.py:36
  57.8 2.1 %collective-permute-start.20 = (bf16[64,2048]{1,0:T(8,128)(2,1)S(1)}, bf16[64,2048]{1,0:T(8,128)(2,1)S(1)}, u32[]{:S(2)}, u32[]{:S(2)}) collective-permute-start(bf16[64,2048]{1,0:T(8,128)(2,1)S(1)} %get-tuple-element.109), channel_id=1, source_target_pairs={{0,4},{2,6},{4,0},{6,2},{8,12},{10,14},{12,8},{14,10},{1,5},{3,7},... | collective-permute-start | bytes 786440 | tf_op jit(solution)/shard_map/ppermute | solution.py:36
  59.9 4.9 %through.3.through_ref = f32[896,2048]{1,0:T(8,128)S(1)} custom-call(s32[16,128]{1,0:T(8,128)S(1)} %select_select_fusion.info, bf16[896,1024]{1,0:T(8,128)(2,1)S(1)} %get-tuple-element.73.g_ref, bf16[4096,1024]{1,0:T(8,128)(2,1)S(1)} %bitcast.20), custom_call_target="tpu_custom_call" | custom-call | flops 1 | bytes 1 | tf_op jit(solution)/shard_map/through/pallas_call | solution.py:455
  64.8 1.3 %collective-permute-start.19 = (bf16[64,2048]{1,0:T(8,128)(2,1)S(1)}, bf16[64,2048]{1,0:T(8,128)(2,1)S(1)}, u32[]{:S(2)}, u32[]{:S(2)}) collective-permute-start(bf16[64,2048]{1,0:T(8,128)(2,1)S(1)} %get-tuple-element.107), channel_id=1, source_target_pairs={{0,2},{2,0},{4,6},{6,4},{8,10},{10,8},{12,14},{14,12},{1,3},{3,1},... | collective-permute-start | bytes 786440 | tf_op jit(solution)/shard_map/ppermute | solution.py:36
  66.3 2.8 %shrink.1 = (bf16[112,4096]{1,0:T(8,128)(2,1)S(1)}, f32[16,896]{1,0:T(8,128)S(1)}) custom-call(s32[16,128]{1,0:T(8,128)S(1)} %select_select_fusion.info, bf16[896,4096]{1,0:T(8,128)(2,1)S(1)} %get-tuple-element.76.x_ref, bf16[112,1024]{1,0:T(8,128)(2,1)S(1)} %get-tuple-element.81.refs_0_, bf16[112,1024]{1,0:T(8,128)(2,1)S(1)} %collective-permute-done.14.refs_1_, ...), custom_call_target="tpu_custom_call" | custom-call | flops 1 | bytes 1 | tf_op jit(solution)/shard_map/shrink/pallas_call | solution.py:502
  69.2 3.9 %token_grads.2.refs_0_ = bf16[896,4096]{1,0:T(8,128)(2,1)} custom-call(s32[16,128]{1,0:T(8,128)S(1)} %select_select_fusion.info, f32[896,2048]{1,0:T(8,128)S(1)} %get-tuple-element.79.through_ref, f32[16,896]{1,0:T(8,128)S(1)} %get-tuple-element.75.mine_ref, f32[16,896]{1,0:T(8,128)S(1)} %collective-permute-done.8.other_ref, ...), custom_call_target="tpu_custom_call" | custom-call | flops 1 | bytes 1 | tf_op jit(solution)/shard_map/token_grads/pallas_call | solution.py:514
  73.1 1.1 %pack_up.1 = (bf16[64,512]{1,0:T(8,128)(2,1)S(1)}, bf16[64,512]{1,0:T(8,128)(2,1)S(1)}, bf16[64,512]{1,0:T(8,128)(2,1)S(1)}, bf16[64,512]{1,0:T(8,128)(2,1)S(1)}) custom-call(s32[16,128]{1,0:T(8,128)S(1)} %select_select_fusion.info, f32[16,896]{1,0:T(8,128)S(1)} %get-tuple-element.99.mine_ref, f32[16,896]{1,0:T(8,128)S(1)} %collective-permute-done.18.other_ref, ...), custom_call_target="tpu_custom_call" | custom-call | flops 1 | bytes 1 | tf_op jit(solution)/shard_map/pack_up/pallas_call | solution.py:524
  74.2 2.1 %collective-permute-done.19.refs_1_ = bf16[64,2048]{1,0:T(8,128)(2,1)S(1)} collective-permute-done((bf16[64,2048]{1,0:T(8,128)(2,1)S(1)}, bf16[64,2048]{1,0:T(8,128)(2,1)S(1)}, u32[]{:S(2)}, u32[]{:S(2)}) %collective-permute-start.19) | collective-permute-done | bytes 262176 | tf_op jit(solution)/shard_map/ppermute | solution.py:36
  77.3 1.3 %collective-permute-start.25 = (bf16[64,2048]{1,0:T(8,128)(2,1)S(1)}, bf16[64,2048]{1,0:T(8,128)(2,1)S(1)}, u32[]{:S(2)}, u32[]{:S(2)}) collective-permute-start(bf16[64,2048]{1,0:T(8,128)(2,1)S(1)} %get-tuple-element.112), channel_id=1, source_target_pairs={{0,8},{2,10},{4,12},{6,14},{8,0},{10,2},{12,4},{14,6},{1,9},{3,11}... | collective-permute-start | bytes 786440 | tf_op jit(solution)/shard_map/ppermute | solution.py:36
  79.3 1.3 %collective-permute-start.23 = (bf16[64,512]{1,0:T(8,128)(2,1)S(1)}, bf16[64,512]{1,0:T(8,128)(2,1)S(1)}, u32[]{:S(2)}, u32[]{:S(2)}) collective-permute-start(bf16[64,512]{1,0:T(8,128)(2,1)S(1)} %get-tuple-element.116), channel_id=1, source_target_pairs={{0,4},{2,6},{4,0},{6,2},{8,12},{10,14},{12,8},{14,10},{1,5},{3,7},... | collective-permute-start | bytes 196616 | tf_op jit(solution)/shard_map/ppermute | solution.py:36
  80.7 1.4 %collective-permute-start.24 = (bf16[64,512]{1,0:T(8,128)(2,1)S(1)}, bf16[64,512]{1,0:T(8,128)(2,1)S(1)}, u32[]{:S(2)}, u32[]{:S(2)}) collective-permute-start(bf16[64,512]{1,0:T(8,128)(2,1)S(1)} %get-tuple-element.117), channel_id=1, source_target_pairs={{0,6},{2,4},{4,2},{6,0},{8,14},{10,12},{12,10},{14,8},{1,7},{3,5},... | collective-permute-start | bytes 196616 | tf_op jit(solution)/shard_map/ppermute | solution.py:36
  82.1 3.9 %token_grads.3 = bf16[896,4096]{1,0:T(8,128)(2,1)} custom-call(s32[16,128]{1,0:T(8,128)S(1)} %select_select_fusion.info, f32[896,2048]{1,0:T(8,128)S(1)} %through.3.through_ref, f32[16,896]{1,0:T(8,128)S(1)} %get-tuple-element.75.mine_ref, f32[16,896]{1,0:T(8,128)S(1)} %collective-permute-done.8.other_ref, ...), custom_call_target="tpu_custom_call", output_to_operand_aliasing={{}: (5, {})} | custom-call | flops 1 | bytes 1 | tf_op jit(solution)/shard_map/token_grads/pallas_call | solution.py:514
  86.8 4.6 %collective-permute-start.26 = (bf16[64,512]{1,0:T(8,128)(2,1)S(1)}, bf16[64,512]{1,0:T(8,128)(2,1)S(1)}, u32[]{:S(2)}, u32[]{:S(2)}) collective-permute-start(bf16[64,512]{1,0:T(8,128)(2,1)S(1)} %get-tuple-element.118), channel_id=1, source_target_pairs={{0,8},{2,10},{4,12},{6,14},{8,0},{10,2},{12,4},{14,6},{1,9},{3,11}... | collective-permute-start | bytes 196616 | tf_op jit(solution)/shard_map/ppermute | solution.py:36
  91.4 2.0 %projected.1 = bf16[896,512]{1,0:T(8,128)(2,1)} custom-call(s32[16,128]{1,0:T(8,128)S(1)} %select_select_fusion.info, f32[896,512]{1,0:T(8,128)S(1)} %base_own.1.base_ref, f32[16,896]{1,0:T(8,128)S(1)} %get-tuple-element.99.mine_ref, f32[16,896]{1,0:T(8,128)S(1)} %collective-permute-done.18.other_ref, bf16[112,512]{1,0:T(8,128)(2,1)S(1)} %get-tuple-element.120.up_ref), custom_call_target="tpu_custom_call" | custom-call | flops 1 | bytes 1 | tf_op jit(solution)/shard_map/projected/pallas_call | solution.py:539
  94.0 1.8 %final.1 = (f32[64,4096]{1,0:T(8,128)}, f32[64,512]{1,0:T(8,128)}) custom-call(s32[16,128]{1,0:T(8,128)S(1)} %select_select_fusion.info, f32[64,2048]{1,0:T(8,128)S(1)} %get-tuple-element.121.refs_0_, bf16[64,2048]{1,0:T(8,128)(2,1)S(1)} %collective-permute-done.17.refs_1_, f32[64,2048]{1,0:T(8,128)S(1)} %get-tuple-element.122.refs_2_, ...), custom_call_target="tpu_custom_call" | custom-call | flops 1 | bytes 1 | tf_op jit(solution)/shard_map/final/pallas_call | solution.py:549
  (65 shorter events, 15.9 us)
Async XLA Ops:
  0.6 10.5 %collective-permute-start = (bf16[4,16,512]{2,1,0:T(8,128)(2,1)}, bf16[4,16,512]{2,1,0:T(8,128)(2,1)S(1)}, u32[]{:S(2)}, u32[]{:S(2)}) collective-permute-start(bf16[4,16,512]{2,1,0:T(8,128)(2,1)} %param.11), channel_id=1, source_target_pairs={{0,8},{2,10},{4,12},{6,14},{8,0},{10,2},{12,4},{14,6},{1,9},{3,11}... | collective-permute-start | bytes 196616 | tf_op jit(solution)/shard_map/ppermute | solution.py:36
  5.7 5.0 %collective-permute-start.2 = (bf16[4,16,1024]{2,1,0:T(8,128)(2,1)S(1)}, bf16[4,16,1024]{2,1,0:T(8,128)(2,1)S(1)}, u32[]{:S(2)}, u32[]{:S(2)}) collective-permute-start(bf16[4,16,1024]{2,1,0:T(8,128)(2,1)S(1)} %get-tuple-element.127), channel_id=1, source_target_pairs={{0,2},{2,0},{4,6},{6,4},{8,10},{10,8},{12,14},{14,12},{1,3},{3,1},... | collective-permute-start | bytes 393224 | tf_op jit(solution)/shard_map/ppermute | solution.py:36
  7.3 8.3 %collective-permute-start.3 = (bf16[896,512]{1,0:T(8,128)(2,1)}, bf16[896,512]{1,0:T(8,128)(2,1)S(1)}, u32[]{:S(2)}, u32[]{:S(2)}) collective-permute-start(bf16[896,512]{1,0:T(8,128)(2,1)} %g_hbm.1), channel_id=1, source_target_pairs={{0,1},{1,0},{2,3},{3,2},{4,5},{5,4},{6,7},{7,6},{8,9},{9,8},{10,11... | collective-permute-start | bytes 2752520 | tf_op jit(solution)/shard_map/ppermute | solution.py:32
  10.8 14.0 %collective-permute-start.6 = (bf16[8,16,1024]{2,1,0:T(8,128)(2,1)S(1)}, bf16[8,16,1024]{2,1,0:T(8,128)(2,1)S(1)}, u32[]{:S(2)}, u32[]{:S(2)}) collective-permute-start(bf16[8,16,1024]{2,1,0:T(8,128)(2,1)S(1)} %pad_maximum_fusion.1.own_ref), channel_id=1, source_target_pairs={{0,8},{2,10},{4,12},{6,14},{8,0},{10,2},{12,4},{14,6},{1,9},{3,11}... | collective-permute-start | bytes 786440 | tf_op jit(solution)/shard_map/ppermute | solution.py:36
  12.0 12.8 %collective-permute-start.5 = (bf16[144,512]{1,0:T(8,128)(2,1)S(1)}, bf16[144,512]{1,0:T(8,128)(2,1)S(1)}, u32[]{:S(2)}, u32[]{:S(2)}) collective-permute-start(bf16[144,512]{1,0:T(8,128)(2,1)S(1)} %pad_maximum_fusion.2.refs_0_), channel_id=1, source_target_pairs={{0,2},{2,0},{4,6},{6,4},{8,10},{10,8},{12,14},{14,12},{1,3},{3,1},... | collective-permute-start | bytes 442376 | tf_op jit(solution)/shard_map/ppermute | solution.py:36
  13.6 11.2 %collective-permute-start.4 = (bf16[144,512]{1,0:T(8,128)(2,1)S(1)}, bf16[144,512]{1,0:T(8,128)(2,1)S(1)}, u32[]{:S(2)}, u32[]{:S(2)}) collective-permute-start(bf16[144,512]{1,0:T(8,128)(2,1)S(1)} %pad_maximum_fusion.2.refs_0_), channel_id=1, source_target_pairs={{0,4},{2,6},{4,0},{6,2},{8,12},{10,14},{12,8},{14,10},{1,5},{3,7},... | collective-permute-start | bytes 442376 | tf_op jit(solution)/shard_map/ppermute | solution.py:36
  15.2 10.4 %collective-permute-start.1 = (bf16[144,512]{1,0:T(8,128)(2,1)S(1)}, bf16[144,512]{1,0:T(8,128)(2,1)S(1)}, u32[]{:S(2)}, u32[]{:S(2)}) collective-permute-start(bf16[144,512]{1,0:T(8,128)(2,1)S(1)} %pad_maximum_fusion.2.refs_0_), channel_id=1, source_target_pairs={{0,6},{2,4},{4,2},{6,0},{8,14},{10,12},{12,10},{14,8},{1,7},{3,5},... | collective-permute-start | bytes 442376 | tf_op jit(solution)/shard_map/ppermute | solution.py:36
  15.6 20.4 %slice-start = ((s8[8388608]{0:T(1024)(128)(4,1)}), s8[4194304]{0:T(1024)(128)(4,1)S(1)}, s32[]{:S(2)}) async-start(s8[8388608]{0:T(1024)(128)(4,1)} %bitcast.19), calls=%async_computation | async-start | bytes 8388608
  15.6 20.4 %slice-start.1 = ((s8[8388608]{0:T(1024)(128)(4,1)}), s8[4194304]{0:T(1024)(128)(4,1)S(1)}, s32[]{:S(2)}) async-start(s8[8388608]{0:T(1024)(128)(4,1)} %bitcast.19), calls=%async_computation.1 | async-start | bytes 8388608
  15.6 1.3 %copy-start = (bf16[896,512]{1,0:T(8,128)(2,1)S(1)}, bf16[896,512]{1,0:T(8,128)(2,1)}, u32[]{:S(2)}) copy-start(bf16[896,512]{1,0:T(8,128)(2,1)} %g_hbm.1) | copy-start | bytes 2752516
  24.7 3.2 %collective-permute-start.7 = (bf16[896,512]{1,0:T(8,128)(2,1)S(1)}, bf16[896,512]{1,0:T(8,128)(2,1)S(1)}, u32[]{:S(2)}, u32[]{:S(2)}) collective-permute-start(bf16[896,512]{1,0:T(8,128)(2,1)S(1)} %get-tuple-element.66), channel_id=1, source_target_pairs={{0,1},{1,0},{2,3},{3,2},{4,5},{5,4},{6,7},{7,6},{8,9},{9,8},{10,11... | collective-permute-start | bytes 2752520 | tf_op jit(solution)/shard_map/ppermute | solution.py:32
  25.7 15.0 %collective-permute-start.10 = (bf16[16,16,1024]{2,1,0:T(8,128)(2,1)S(1)}, bf16[16,16,1024]{2,1,0:T(8,128)(2,1)S(1)}, u32[]{:S(2)}, u32[]{:S(2)}) collective-permute-start(bf16[16,16,1024]{2,1,0:T(8,128)(2,1)S(1)} %pad_maximum_fusion), channel_id=1, source_target_pairs={{0,4},{2,6},{4,0},{6,2},{8,12},{10,14},{12,8},{14,10},{1,5},{3,7},... | collective-permute-start | bytes 1572872 | tf_op jit(solution)/shard_map/ppermute | solution.py:36
  27.7 1.3 %collective-permute-start.8 = (f32[16,896]{1,0:T(8,128)S(1)}, f32[16,896]{1,0:T(8,128)S(1)}, u32[]{:S(2)}, u32[]{:S(2)}) collective-permute-start(f32[16,896]{1,0:T(8,128)S(1)} %get-tuple-element.75.mine_ref), channel_id=1, source_target_pairs={{0,1},{1,0},{2,3},{3,2},{4,5},{5,4},{6,7},{7,6},{8,9},{9,8},{10,11... | collective-permute-start | bytes 172040 | tf_op jit(solution)/shard_map/ppermute | solution.py:32
  30.9 15.3 %collective-permute-start.12 = (bf16[64,2048]{1,0:T(8,128)(2,1)S(1)}, bf16[64,2048]{1,0:T(8,128)(2,1)S(1)}, u32[]{:S(2)}, u32[]{:S(2)}) collective-permute-start(bf16[64,2048]{1,0:T(8,128)(2,1)S(1)} %get-tuple-element.88), channel_id=1, source_target_pairs={{0,4},{2,6},{4,0},{6,2},{8,12},{10,14},{12,8},{14,10},{1,5},{3,7},... | collective-permute-start | bytes 786440 | tf_op jit(solution)/shard_map/ppermute | solution.py:36
  32.2 22.1 %collective-permute-start.11 = (bf16[64,2048]{1,0:T(8,128)(2,1)S(1)}, bf16[64,2048]{1,0:T(8,128)(2,1)S(1)}, u32[]{:S(2)}, u32[]{:S(2)}) collective-permute-start(bf16[64,2048]{1,0:T(8,128)(2,1)S(1)} %get-tuple-element.87), channel_id=1, source_target_pairs={{0,2},{2,0},{4,6},{6,4},{8,10},{10,8},{12,14},{14,12},{1,3},{3,1},... | collective-permute-start | bytes 786440 | tf_op jit(solution)/shard_map/ppermute | solution.py:36
  33.3 21.1 %collective-permute-start.13 = (bf16[64,2048]{1,0:T(8,128)(2,1)S(1)}, bf16[64,2048]{1,0:T(8,128)(2,1)S(1)}, u32[]{:S(2)}, u32[]{:S(2)}) collective-permute-start(bf16[64,2048]{1,0:T(8,128)(2,1)S(1)} %get-tuple-element.89), channel_id=1, source_target_pairs={{0,6},{2,4},{4,2},{6,0},{8,14},{10,12},{12,10},{14,8},{1,7},{3,5},... | collective-permute-start | bytes 786440 | tf_op jit(solution)/shard_map/ppermute | solution.py:36
  34.5 6.2 %collective-permute-start.9 = (s32[16,128]{1,0:T(8,128)S(1)}, s32[16,128]{1,0:T(8,128)S(1)}, u32[]{:S(2)}, u32[]{:S(2)}) collective-permute-start(s32[16,128]{1,0:T(8,128)S(1)} %select_select_fusion.info), channel_id=1, source_target_pairs={{0,16},{16,0},{1,17},{17,1},{2,18},{18,2},{3,19},{19,3},{4,20},{20... | collective-permute-start | bytes 24584 | tf_op jit(solution)/shard_map/ppermute | solution.py:32
  46.2 18.6 %collective-permute-start.14 = (bf16[112,1024]{1,0:T(8,128)(2,1)S(1)}, bf16[112,1024]{1,0:T(8,128)(2,1)S(1)}, u32[]{:S(2)}, u32[]{:S(2)}) collective-permute-start(bf16[112,1024]{1,0:T(8,128)(2,1)S(1)} %get-tuple-element.94), channel_id=1, source_target_pairs={{0,2},{2,0},{4,6},{6,4},{8,10},{10,8},{12,14},{14,12},{1,3},{3,1},... | collective-permute-start | bytes 688136 | tf_op jit(solution)/shard_map/ppermute | solution.py:36
  47.2 18.9 %collective-permute-start.15 = (bf16[112,1024]{1,0:T(8,128)(2,1)S(1)}, bf16[112,1024]{1,0:T(8,128)(2,1)S(1)}, u32[]{:S(2)}, u32[]{:S(2)}) collective-permute-start(bf16[112,1024]{1,0:T(8,128)(2,1)S(1)} %get-tuple-element.96), channel_id=1, source_target_pairs={{0,16},{16,0},{1,17},{17,1},{2,18},{18,2},{3,19},{19,3},{4,20},{20... | collective-permute-start | bytes 688136 | tf_op jit(solution)/shard_map/ppermute | solution.py:32
  48.7 17.6 %collective-permute-start.16 = (bf16[112,1024]{1,0:T(8,128)(2,1)S(1)}, bf16[112,1024]{1,0:T(8,128)(2,1)S(1)}, u32[]{:S(2)}, u32[]{:S(2)}) collective-permute-start(bf16[112,1024]{1,0:T(8,128)(2,1)S(1)} %get-tuple-element.98), channel_id=1, source_target_pairs={{0,18},{2,16},{4,22},{6,20},{8,26},{10,24},{12,30},{14,28},{16,2},... | collective-permute-start | bytes 688136 | tf_op jit(solution)/shard_map/ppermute | solution.py:476
  55.3 17.8 %collective-permute-start.17 = (bf16[64,2048]{1,0:T(8,128)(2,1)S(1)}, bf16[64,2048]{1,0:T(8,128)(2,1)S(1)}, u32[]{:S(2)}, u32[]{:S(2)}) collective-permute-start(bf16[64,2048]{1,0:T(8,128)(2,1)S(1)} %get-tuple-element.90), channel_id=1, source_target_pairs={{0,8},{2,10},{4,12},{6,14},{8,0},{10,2},{12,4},{14,6},{1,9},{3,11}... | collective-permute-start | bytes 786440 | tf_op jit(solution)/shard_map/ppermute | solution.py:36
  57.8 16.4 %collective-permute-start.20 = (bf16[64,2048]{1,0:T(8,128)(2,1)S(1)}, bf16[64,2048]{1,0:T(8,128)(2,1)S(1)}, u32[]{:S(2)}, u32[]{:S(2)}) collective-permute-start(bf16[64,2048]{1,0:T(8,128)(2,1)S(1)} %get-tuple-element.109), channel_id=1, source_target_pairs={{0,4},{2,6},{4,0},{6,2},{8,12},{10,14},{12,8},{14,10},{1,5},{3,7},... | collective-permute-start | bytes 786440 | tf_op jit(solution)/shard_map/ppermute | solution.py:36
  64.8 11.6 %collective-permute-start.19 = (bf16[64,2048]{1,0:T(8,128)(2,1)S(1)}, bf16[64,2048]{1,0:T(8,128)(2,1)S(1)}, u32[]{:S(2)}, u32[]{:S(2)}) collective-permute-start(bf16[64,2048]{1,0:T(8,128)(2,1)S(1)} %get-tuple-element.107), channel_id=1, source_target_pairs={{0,2},{2,0},{4,6},{6,4},{8,10},{10,8},{12,14},{14,12},{1,3},{3,1},... | collective-permute-start | bytes 786440 | tf_op jit(solution)/shard_map/ppermute | solution.py:36
  66.1 10.2 %collective-permute-start.21 = (bf16[64,2048]{1,0:T(8,128)(2,1)S(1)}, bf16[64,2048]{1,0:T(8,128)(2,1)S(1)}, u32[]{:S(2)}, u32[]{:S(2)}) collective-permute-start(bf16[64,2048]{1,0:T(8,128)(2,1)S(1)} %get-tuple-element.111), channel_id=1, source_target_pairs={{0,6},{2,4},{4,2},{6,0},{8,14},{10,12},{12,10},{14,8},{1,7},{3,5},... | collective-permute-start | bytes 786440 | tf_op jit(solution)/shard_map/ppermute | solution.py:36
  69.1 4.0 %collective-permute-start.18 = (f32[16,896]{1,0:T(8,128)S(1)}, f32[16,896]{1,0:T(8,128)S(1)}, u32[]{:S(2)}, u32[]{:S(2)}) collective-permute-start(f32[16,896]{1,0:T(8,128)S(1)} %get-tuple-element.99.mine_ref), channel_id=1, source_target_pairs={{0,1},{1,0},{2,3},{3,2},{4,5},{5,4},{6,7},{7,6},{8,9},{9,8},{10,11... | collective-permute-start | bytes 172040 | tf_op jit(solution)/shard_map/ppermute | solution.py:32
  77.3 16.7 %collective-permute-start.25 = (bf16[64,2048]{1,0:T(8,128)(2,1)S(1)}, bf16[64,2048]{1,0:T(8,128)(2,1)S(1)}, u32[]{:S(2)}, u32[]{:S(2)}) collective-permute-start(bf16[64,2048]{1,0:T(8,128)(2,1)S(1)} %get-tuple-element.112), channel_id=1, source_target_pairs={{0,8},{2,10},{4,12},{6,14},{8,0},{10,2},{12,4},{14,6},{1,9},{3,11}... | collective-permute-start | bytes 786440 | tf_op jit(solution)/shard_map/ppermute | solution.py:36
  78.6 7.4 %collective-permute-start.22 = (bf16[64,512]{1,0:T(8,128)(2,1)S(1)}, bf16[64,512]{1,0:T(8,128)(2,1)S(1)}, u32[]{:S(2)}, u32[]{:S(2)}) collective-permute-start(bf16[64,512]{1,0:T(8,128)(2,1)S(1)} %get-tuple-element.115), channel_id=1, source_target_pairs={{0,2},{2,0},{4,6},{6,4},{8,10},{10,8},{12,14},{14,12},{1,3},{3,1},... | collective-permute-start | bytes 196616 | tf_op jit(solution)/shard_map/ppermute | solution.py:36
  79.3 6.6 %collective-permute-start.23 = (bf16[64,512]{1,0:T(8,128)(2,1)S(1)}, bf16[64,512]{1,0:T(8,128)(2,1)S(1)}, u32[]{:S(2)}, u32[]{:S(2)}) collective-permute-start(bf16[64,512]{1,0:T(8,128)(2,1)S(1)} %get-tuple-element.116), channel_id=1, source_target_pairs={{0,4},{2,6},{4,0},{6,2},{8,12},{10,14},{12,8},{14,10},{1,5},{3,7},... | collective-permute-start | bytes 196616 | tf_op jit(solution)/shard_map/ppermute | solution.py:36
  80.7 5.3 %collective-permute-start.24 = (bf16[64,512]{1,0:T(8,128)(2,1)S(1)}, bf16[64,512]{1,0:T(8,128)(2,1)S(1)}, u32[]{:S(2)}, u32[]{:S(2)}) collective-permute-start(bf16[64,512]{1,0:T(8,128)(2,1)S(1)} %get-tuple-element.117), channel_id=1, source_target_pairs={{0,6},{2,4},{4,2},{6,0},{8,14},{10,12},{12,10},{14,8},{1,7},{3,5},... | collective-permute-start | bytes 196616 | tf_op jit(solution)/shard_map/ppermute | solution.py:36
  86.8 7.2 %collective-permute-start.26 = (bf16[64,512]{1,0:T(8,128)(2,1)S(1)}, bf16[64,512]{1,0:T(8,128)(2,1)S(1)}, u32[]{:S(2)}, u32[]{:S(2)}) collective-permute-start(bf16[64,512]{1,0:T(8,128)(2,1)S(1)} %get-tuple-element.118), channel_id=1, source_target_pairs={{0,8},{2,10},{4,12},{6,14},{8,0},{10,2},{12,4},{14,6},{1,9},{3,11}... | collective-permute-start | bytes 196616 | tf_op jit(solution)/shard_map/ppermute | solution.py:36

commit v14 on v13

--- a/solution.py
+++ b/solution.py
@@ -458,7 +458,7 @@
         )(info, g_full, base_weight)
 
     half = width // 2
-    wide_a = half
+    wide_a = width * 9 // 16
     sends_a = pack(_tie(info, *ready), 0, wide_a)
     got_a = to_near(sends_a)
     low, sums = through(_tie(info, sends_a[0]), 0, half, 1)

time: 96 us -> 95.6 us (level)
  transfers between devices with their start and end apart: 27 -> 27, of which waited for: 6 -> 6; matrix products, arithmetic and copies ran while one was open for 4% -> 4% of each run, Pallas kernels for 45% -> 46%
where the time goes in v14:
time: 95.6 us; the launch traced here: 95.4 us
  Pallas kernels  46.2 us (48%)
  starting transfers between devices  34.7 us (36%)
  waiting for transfers between devices  8.58 us (9%)
  other arithmetic  2.63 us (3%)
  local copies, waits for them, and re-layouts  2.33 us (2%)
    ppermute x20, starting transfers between devices, _xor(): return lax.ppermute(x, 'dp', [(i, i ^ k) for i in range(n)])  30.8 us
    pallas_call x2, Pallas kernels, through(): _call(functools.partial(through_kernel, z, first), 'through', (1,), [VMEM...  9.57 us
    pallas_call x1, Pallas kernels, on_device(): _call(functools.partial(base_kernel, z), 'base', (1,), [pl.BlockSpec(memo...  7.78 us
    pallas_call x2, Pallas kernels, token_grads(): _call(functools.partial(tokens_kernel, z, first), 'token_grads', (steps,)...  7.73 us
    ppermute x20, waiting for transfers between devices, _xor(): return lax.ppermute(x, 'dp', [(i, i ^ k) for i in range(n)])  7.52 us
    pallas_call x1, Pallas kernels, on_device(): _call(functools.partial(own_kernel, z), 'base_own', (1,), [VMEM] * 3, VME...  4.61 us
    pallas_call x2, Pallas kernels, pack(): _call(functools.partial(pack_kernel, z, NEAR, start), 'pack_down', (1,),...  3.96 us
    ppermute x6, starting transfers between devices, _swap(): return lax.ppermute(x, axis, [(0, 1), (1, 0)])  3.35 us
  transfers between devices with their start and end apart: 27, of which 6 were waited for; matrix products, arithmetic and copies ran while one was open for 4% of the time, Pallas kernels for 46%

profile of v14, /device:TPU:0, one launch (start us, length us, event | category | flops | bytes accessed | tf_op | source)
XLA Modules:
  0.0 95.4 jit_solution(11480124478685872029)
XLA Ops:
  0.6 4.1 %collective-permute-start = (bf16[4,16,512]{2,1,0:T(8,128)(2,1)}, bf16[4,16,512]{2,1,0:T(8,128)(2,1)S(1)}, u32[]{:S(2)}, u32[]{:S(2)}) collective-permute-start(bf16[4,16,512]{2,1,0:T(8,128)(2,1)} %param.11), channel_id=1, source_target_pairs={{0,8},{2,10},{4,12},{6,14},{8,0},{10,2},{12,4},{14,6},{1,9},{3,11}... | collective-permute-start | bytes 196616 | tf_op jit(solution)/shard_map/ppermute | solution.py:36
  5.7 1.6 %collective-permute-start.2 = (bf16[4,16,1024]{2,1,0:T(8,128)(2,1)S(1)}, bf16[4,16,1024]{2,1,0:T(8,128)(2,1)S(1)}, u32[]{:S(2)}, u32[]{:S(2)}) collective-permute-start(bf16[4,16,1024]{2,1,0:T(8,128)(2,1)S(1)} %get-tuple-element.127), channel_id=1, source_target_pairs={{0,2},{2,0},{4,6},{6,4},{8,10},{10,8},{12,14},{14,12},{1,3},{3,1},... | collective-permute-start | bytes 393224 | tf_op jit(solution)/shard_map/ppermute | solution.py:36
  8.9 1.8 %collective-permute-done.2 = bf16[4,16,1024]{2,1,0:T(8,128)(2,1)S(1)} collective-permute-done((bf16[4,16,1024]{2,1,0:T(8,128)(2,1)S(1)}, bf16[4,16,1024]{2,1,0:T(8,128)(2,1)S(1)}, u32[]{:S(2)}, u32[]{:S(2)}) %collective-permute-start.2) | collective-permute-done | bytes 131104 | tf_op jit(solution)/shard_map/ppermute | solution.py:36
  12.0 1.6 %collective-permute-start.5 = (bf16[144,512]{1,0:T(8,128)(2,1)S(1)}, bf16[144,512]{1,0:T(8,128)(2,1)S(1)}, u32[]{:S(2)}, u32[]{:S(2)}) collective-permute-start(bf16[144,512]{1,0:T(8,128)(2,1)S(1)} %pad_maximum_fusion.2.refs_0_), channel_id=1, source_target_pairs={{0,2},{2,0},{4,6},{6,4},{8,10},{10,8},{12,14},{14,12},{1,3},{3,1},... | collective-permute-start | bytes 442376 | tf_op jit(solution)/shard_map/ppermute | solution.py:36
  13.6 1.6 %collective-permute-start.4 = (bf16[144,512]{1,0:T(8,128)(2,1)S(1)}, bf16[144,512]{1,0:T(8,128)(2,1)S(1)}, u32[]{:S(2)}, u32[]{:S(2)}) collective-permute-start(bf16[144,512]{1,0:T(8,128)(2,1)S(1)} %pad_maximum_fusion.2.refs_0_), channel_id=1, source_target_pairs={{0,4},{2,6},{4,0},{6,2},{8,12},{10,14},{12,8},{14,10},{1,5},{3,7},... | collective-permute-start | bytes 442376 | tf_op jit(solution)/shard_map/ppermute | solution.py:36
  15.6 1.3 %copy-done = bf16[896,512]{1,0:T(8,128)(2,1)S(1)} copy-done((bf16[896,512]{1,0:T(8,128)(2,1)S(1)}, bf16[896,512]{1,0:T(8,128)(2,1)}, u32[]{:S(2)}) %copy-start) | copy-done | bytes 917528
  17.0 7.8 %base.1 = (bf16[896,512]{1,0:T(8,128)(2,1)S(1)}, bf16[896,1024]{1,0:T(8,128)(2,1)S(1)}, bf16[896,4096]{1,0:T(8,128)(2,1)S(1)}) custom-call(s32[16,128]{1,0:T(8,128)S(1)} %select_select_fusion.1.info, bf16[896,4096]{1,0:T(8,128)(2,1)} %x_hbm.1, bf16[4096,1024]{1,0:T(8,128)(2,1)} %w_ref.5, bf16[896,512]{1,0:T(8,128)(2,1)S(1)} %copy-done, ...), custom_call_target="tpu_custom_call" | custom-call | flops 1 | bytes 1 | tf_op jit(solution)/shard_map/base/pallas_call | solution.py:388
  29.0 2.1 %pack_down.2 = (bf16[64,2304]{1,0:T(8,128)(2,1)S(1)}, bf16[64,2304]{1,0:T(8,128)(2,1)S(1)}, bf16[64,2304]{1,0:T(8,128)(2,1)S(1)}, bf16[64,2304]{1,0:T(8,128)(2,1)S(1)}) custom-call(s32[16,128]{1,0:T(8,128)S(1)} %select_select_fusion.info, f32[16,896]{1,0:T(8,128)S(1)} %get-tuple-element.75.mine_ref, f32[16,896]{1,0:T(8,128)S(1)} %collective-permute-done.8.other_ref, ...), custom_call_target="tpu_custom_call" | custom-call | flops 1 | bytes 1 | tf_op jit(solution)/shard_map/pack_down/pallas_call | solution.py:431
  31.1 1.3 %collective-permute-start.12 = (bf16[64,2304]{1,0:T(8,128)(2,1)S(1)}, bf16[64,2304]{1,0:T(8,128)(2,1)S(1)}, u32[]{:S(2)}, u32[]{:S(2)}) collective-permute-start(bf16[64,2304]{1,0:T(8,128)(2,1)S(1)} %get-tuple-element.88), channel_id=1, source_target_pairs={{0,4},{2,6},{4,0},{6,2},{8,12},{10,14},{12,8},{14,10},{1,5},{3,7},... | collective-permute-start | bytes 884744 | tf_op jit(solution)/shard_map/ppermute | solution.py:36
  32.4 1.1 %collective-permute-start.11 = (bf16[64,2304]{1,0:T(8,128)(2,1)S(1)}, bf16[64,2304]{1,0:T(8,128)(2,1)S(1)}, u32[]{:S(2)}, u32[]{:S(2)}) collective-permute-start(bf16[64,2304]{1,0:T(8,128)(2,1)S(1)} %get-tuple-element.87), channel_id=1, source_target_pairs={{0,2},{2,0},{4,6},{6,4},{8,10},{10,8},{12,14},{14,12},{1,3},{3,1},... | collective-permute-start | bytes 884744 | tf_op jit(solution)/shard_map/ppermute | solution.py:36
  33.4 1.2 %collective-permute-start.13 = (bf16[64,2304]{1,0:T(8,128)(2,1)S(1)}, bf16[64,2304]{1,0:T(8,128)(2,1)S(1)}, u32[]{:S(2)}, u32[]{:S(2)}) collective-permute-start(bf16[64,2304]{1,0:T(8,128)(2,1)S(1)} %get-tuple-element.89), channel_id=1, source_target_pairs={{0,6},{2,4},{4,2},{6,0},{8,14},{10,12},{12,10},{14,8},{1,7},{3,5},... | collective-permute-start | bytes 884744 | tf_op jit(solution)/shard_map/ppermute | solution.py:36
  34.6 1.5 %collective-permute-start.9 = (s32[16,128]{1,0:T(8,128)S(1)}, s32[16,128]{1,0:T(8,128)S(1)}, u32[]{:S(2)}, u32[]{:S(2)}) collective-permute-start(s32[16,128]{1,0:T(8,128)S(1)} %select_select_fusion.info), channel_id=1, source_target_pairs={{0,16},{16,0},{1,17},{17,1},{2,18},{18,2},{3,19},{19,3},{4,20},{20... | collective-permute-start | bytes 24584 | tf_op jit(solution)/shard_map/ppermute | solution.py:32
  36.1 4.7 %through.2 = (f32[896,2048]{1,0:T(8,128)S(1)}, bf16[2,64,128]{2,1,0:T(8,128)(2,1)S(1)}) custom-call(s32[16,128]{1,0:T(8,128)S(1)} %select_select_fusion.info, bf16[896,1024]{1,0:T(8,128)(2,1)S(1)} %get-tuple-element.73.g_ref, bf16[4096,1024]{1,0:T(8,128)(2,1)S(1)} %bitcast.20), custom_call_target="tpu_custom_call" | custom-call | flops 1 | bytes 1 | tf_op jit(solution)/shard_map/through/pallas_call | solution.py:455
  41.9 1.8 %pack_down.3 = (bf16[64,1792]{1,0:T(8,128)(2,1)S(1)}, bf16[64,1792]{1,0:T(8,128)(2,1)S(1)}, bf16[64,1792]{1,0:T(8,128)(2,1)S(1)}, bf16[64,1792]{1,0:T(8,128)(2,1)S(1)}) custom-call(s32[16,128]{1,0:T(8,128)S(1)} %select_select_fusion.info, f32[16,896]{1,0:T(8,128)S(1)} %get-tuple-element.75.mine_ref, f32[16,896]{1,0:T(8,128)S(1)} %collective-permute-done.8.other_ref, ...), custom_call_target="tpu_custom_call" | custom-call | flops 1 | bytes 1 | tf_op jit(solution)/shard_map/pack_down/pallas_call | solution.py:431
  43.8 3.1 %collective-permute-done.12.refs_2_ = bf16[64,2304]{1,0:T(8,128)(2,1)S(1)} collective-permute-done((bf16[64,2304]{1,0:T(8,128)(2,1)S(1)}, bf16[64,2304]{1,0:T(8,128)(2,1)S(1)}, u32[]{:S(2)}, u32[]{:S(2)}) %collective-permute-start.12) | collective-permute-done | bytes 294944 | tf_op jit(solution)/shard_map/ppermute | solution.py:36
  47.9 1.5 %collective-permute-start.15 = (bf16[112,1024]{1,0:T(8,128)(2,1)S(1)}, bf16[112,1024]{1,0:T(8,128)(2,1)S(1)}, u32[]{:S(2)}, u32[]{:S(2)}) collective-permute-start(bf16[112,1024]{1,0:T(8,128)(2,1)S(1)} %get-tuple-element.96), channel_id=1, source_target_pairs={{0,16},{16,0},{1,17},{17,1},{2,18},{18,2},{3,19},{19,3},{4,20},{20... | collective-permute-start | bytes 688136 | tf_op jit(solution)/shard_map/ppermute | solution.py:32
  49.4 4.6 %base_own.1.base_ref = f32[896,512]{1,0:T(8,128)S(1)} custom-call(s32[16,128]{1,0:T(8,128)S(1)} %select_select_fusion.info, bf16[896,4096]{1,0:T(8,128)(2,1)S(1)} %get-tuple-element.76.x_ref, bf16[4096,1024]{1,0:T(8,128)(2,1)S(1)} %bitcast.20, bf16[896,512]{1,0:T(8,128)(2,1)S(1)} %collective-permute-done.7.far_ref), custom_call_target="tpu_custom_call" | custom-call | flops 1 | bytes 1 | tf_op jit(solution)/shard_map/base_own/pallas_call | solution.py:487
  55.0 2.9 %collective-permute-start.17 = (bf16[64,2304]{1,0:T(8,128)(2,1)S(1)}, bf16[64,2304]{1,0:T(8,128)(2,1)S(1)}, u32[]{:S(2)}, u32[]{:S(2)}) collective-permute-start(bf16[64,2304]{1,0:T(8,128)(2,1)S(1)} %get-tuple-element.90), channel_id=1, source_target_pairs={{0,8},{2,10},{4,12},{6,14},{8,0},{10,2},{12,4},{14,6},{1,9},{3,11}... | collective-permute-start | bytes 884744 | tf_op jit(solution)/shard_map/ppermute | solution.py:36
  58.5 2.1 %collective-permute-start.20 = (bf16[64,1792]{1,0:T(8,128)(2,1)S(1)}, bf16[64,1792]{1,0:T(8,128)(2,1)S(1)}, u32[]{:S(2)}, u32[]{:S(2)}) collective-permute-start(bf16[64,1792]{1,0:T(8,128)(2,1)S(1)} %get-tuple-element.109), channel_id=1, source_target_pairs={{0,4},{2,6},{4,0},{6,2},{8,12},{10,14},{12,8},{14,10},{1,5},{3,7},... | collective-permute-start | bytes 688136 | tf_op jit(solution)/shard_map/ppermute | solution.py:36
  60.6 4.8 %through.3.through_ref = f32[896,2048]{1,0:T(8,128)S(1)} custom-call(s32[16,128]{1,0:T(8,128)S(1)} %select_select_fusion.info, bf16[896,1024]{1,0:T(8,128)(2,1)S(1)} %get-tuple-element.73.g_ref, bf16[4096,1024]{1,0:T(8,128)(2,1)S(1)} %bitcast.20), custom_call_target="tpu_custom_call" | custom-call | flops 1 | bytes 1 | tf_op jit(solution)/shard_map/through/pallas_call | solution.py:455
  65.5 1.3 %collective-permute-start.19 = (bf16[64,1792]{1,0:T(8,128)(2,1)S(1)}, bf16[64,1792]{1,0:T(8,128)(2,1)S(1)}, u32[]{:S(2)}, u32[]{:S(2)}) collective-permute-start(bf16[64,1792]{1,0:T(8,128)(2,1)S(1)} %get-tuple-element.107), channel_id=1, source_target_pairs={{0,2},{2,0},{4,6},{6,4},{8,10},{10,8},{12,14},{14,12},{1,3},{3,1},... | collective-permute-start | bytes 688136 | tf_op jit(solution)/shard_map/ppermute | solution.py:36
  67.0 2.8 %shrink.1 = (bf16[112,4096]{1,0:T(8,128)(2,1)S(1)}, f32[16,896]{1,0:T(8,128)S(1)}) custom-call(s32[16,128]{1,0:T(8,128)S(1)} %select_select_fusion.info, bf16[896,4096]{1,0:T(8,128)(2,1)S(1)} %get-tuple-element.76.x_ref, bf16[112,1024]{1,0:T(8,128)(2,1)S(1)} %get-tuple-element.81.refs_0_, bf16[112,1024]{1,0:T(8,128)(2,1)S(1)} %collective-permute-done.14.refs_1_, ...), custom_call_target="tpu_custom_call" | custom-call | flops 1 | bytes 1 | tf_op jit(solution)/shard_map/shrink/pallas_call | solution.py:502
  69.9 3.9 %token_grads.2.refs_0_ = bf16[896,4096]{1,0:T(8,128)(2,1)} custom-call(s32[16,128]{1,0:T(8,128)S(1)} %select_select_fusion.info, f32[896,2048]{1,0:T(8,128)S(1)} %get-tuple-element.79.through_ref, f32[16,896]{1,0:T(8,128)S(1)} %get-tuple-element.75.mine_ref, f32[16,896]{1,0:T(8,128)S(1)} %collective-permute-done.8.other_ref, ...), custom_call_target="tpu_custom_call" | custom-call | flops 1 | bytes 1 | tf_op jit(solution)/shard_map/token_grads/pallas_call | solution.py:514
  73.8 1.1 %pack_up.1 = (bf16[64,512]{1,0:T(8,128)(2,1)S(1)}, bf16[64,512]{1,0:T(8,128)(2,1)S(1)}, bf16[64,512]{1,0:T(8,128)(2,1)S(1)}, bf16[64,512]{1,0:T(8,128)(2,1)S(1)}) custom-call(s32[16,128]{1,0:T(8,128)S(1)} %select_select_fusion.info, f32[16,896]{1,0:T(8,128)S(1)} %get-tuple-element.99.mine_ref, f32[16,896]{1,0:T(8,128)S(1)} %collective-permute-done.18.other_ref, ...), custom_call_target="tpu_custom_call" | custom-call | flops 1 | bytes 1 | tf_op jit(solution)/shard_map/pack_up/pallas_call | solution.py:524
  74.9 1.5 %collective-permute-done.19.refs_1_ = bf16[64,1792]{1,0:T(8,128)(2,1)S(1)} collective-permute-done((bf16[64,1792]{1,0:T(8,128)(2,1)S(1)}, bf16[64,1792]{1,0:T(8,128)(2,1)S(1)}, u32[]{:S(2)}, u32[]{:S(2)}) %collective-permute-start.19) | collective-permute-done | bytes 229408 | tf_op jit(solution)/shard_map/ppermute | solution.py:36
  77.4 1.2 %collective-permute-start.25 = (bf16[64,1792]{1,0:T(8,128)(2,1)S(1)}, bf16[64,1792]{1,0:T(8,128)(2,1)S(1)}, u32[]{:S(2)}, u32[]{:S(2)}) collective-permute-start(bf16[64,1792]{1,0:T(8,128)(2,1)S(1)} %get-tuple-element.112), channel_id=1, source_target_pairs={{0,8},{2,10},{4,12},{6,14},{8,0},{10,2},{12,4},{14,6},{1,9},{3,11}... | collective-permute-start | bytes 688136 | tf_op jit(solution)/shard_map/ppermute | solution.py:36
  78.8 1.1 %collective-permute-start.23 = (bf16[64,512]{1,0:T(8,128)(2,1)S(1)}, bf16[64,512]{1,0:T(8,128)(2,1)S(1)}, u32[]{:S(2)}, u32[]{:S(2)}) collective-permute-start(bf16[64,512]{1,0:T(8,128)(2,1)S(1)} %get-tuple-element.116), channel_id=1, source_target_pairs={{0,4},{2,6},{4,0},{6,2},{8,12},{10,14},{12,8},{14,10},{1,5},{3,7},... | collective-permute-start | bytes 196616 | tf_op jit(solution)/shard_map/ppermute | solution.py:36
  79.9 2.1 %collective-permute-start.24 = (bf16[64,512]{1,0:T(8,128)(2,1)S(1)}, bf16[64,512]{1,0:T(8,128)(2,1)S(1)}, u32[]{:S(2)}, u32[]{:S(2)}) collective-permute-start(bf16[64,512]{1,0:T(8,128)(2,1)S(1)} %get-tuple-element.117), channel_id=1, source_target_pairs={{0,6},{2,4},{4,2},{6,0},{8,14},{10,12},{12,10},{14,8},{1,7},{3,5},... | collective-permute-start | bytes 196616 | tf_op jit(solution)/shard_map/ppermute | solution.py:36
  82.1 3.9 %token_grads.3 = bf16[896,4096]{1,0:T(8,128)(2,1)} custom-call(s32[16,128]{1,0:T(8,128)S(1)} %select_select_fusion.info, f32[896,2048]{1,0:T(8,128)S(1)} %through.3.through_ref, f32[16,896]{1,0:T(8,128)S(1)} %get-tuple-element.75.mine_ref, f32[16,896]{1,0:T(8,128)S(1)} %collective-permute-done.8.other_ref, ...), custom_call_target="tpu_custom_call", output_to_operand_aliasing={{}: (5, {})} | custom-call | flops 1 | bytes 1 | tf_op jit(solution)/shard_map/token_grads/pallas_call | solution.py:514
  86.8 4.6 %collective-permute-start.26 = (bf16[64,512]{1,0:T(8,128)(2,1)S(1)}, bf16[64,512]{1,0:T(8,128)(2,1)S(1)}, u32[]{:S(2)}, u32[]{:S(2)}) collective-permute-start(bf16[64,512]{1,0:T(8,128)(2,1)S(1)} %get-tuple-element.118), channel_id=1, source_target_pairs={{0,8},{2,10},{4,12},{6,14},{8,0},{10,2},{12,4},{14,6},{1,9},{3,11}... | collective-permute-start | bytes 196616 | tf_op jit(solution)/shard_map/ppermute | solution.py:36
  91.3 2.0 %projected.1 = bf16[896,512]{1,0:T(8,128)(2,1)} custom-call(s32[16,128]{1,0:T(8,128)S(1)} %select_select_fusion.info, f32[896,512]{1,0:T(8,128)S(1)} %base_own.1.base_ref, f32[16,896]{1,0:T(8,128)S(1)} %get-tuple-element.99.mine_ref, f32[16,896]{1,0:T(8,128)S(1)} %collective-permute-done.18.other_ref, bf16[112,512]{1,0:T(8,128)(2,1)S(1)} %get-tuple-element.120.up_ref), custom_call_target="tpu_custom_call" | custom-call | flops 1 | bytes 1 | tf_op jit(solution)/shard_map/projected/pallas_call | solution.py:539
  93.6 1.8 %final.1 = (f32[64,4096]{1,0:T(8,128)}, f32[64,512]{1,0:T(8,128)}) custom-call(s32[16,128]{1,0:T(8,128)S(1)} %select_select_fusion.info, f32[64,2304]{1,0:T(8,128)S(1)} %get-tuple-element.121.refs_0_, bf16[64,2304]{1,0:T(8,128)(2,1)S(1)} %collective-permute-done.17.refs_1_, f32[64,1792]{1,0:T(8,128)S(1)} %get-tuple-element.122.refs_2_, ...), custom_call_target="tpu_custom_call" | custom-call | flops 1 | bytes 1 | tf_op jit(solution)/shard_map/final/pallas_call | solution.py:549
  (65 shorter events, 14.6 us)
Async XLA Ops:
  0.6 10.5 %collective-permute-start = (bf16[4,16,512]{2,1,0:T(8,128)(2,1)}, bf16[4,16,512]{2,1,0:T(8,128)(2,1)S(1)}, u32[]{:S(2)}, u32[]{:S(2)}) collective-permute-start(bf16[4,16,512]{2,1,0:T(8,128)(2,1)} %param.11), channel_id=1, source_target_pairs={{0,8},{2,10},{4,12},{6,14},{8,0},{10,2},{12,4},{14,6},{1,9},{3,11}... | collective-permute-start | bytes 196616 | tf_op jit(solution)/shard_map/ppermute | solution.py:36
  5.7 5.0 %collective-permute-start.2 = (bf16[4,16,1024]{2,1,0:T(8,128)(2,1)S(1)}, bf16[4,16,1024]{2,1,0:T(8,128)(2,1)S(1)}, u32[]{:S(2)}, u32[]{:S(2)}) collective-permute-start(bf16[4,16,1024]{2,1,0:T(8,128)(2,1)S(1)} %get-tuple-element.127), channel_id=1, source_target_pairs={{0,2},{2,0},{4,6},{6,4},{8,10},{10,8},{12,14},{14,12},{1,3},{3,1},... | collective-permute-start | bytes 393224 | tf_op jit(solution)/shard_map/ppermute | solution.py:36
  7.3 8.3 %collective-permute-start.3 = (bf16[896,512]{1,0:T(8,128)(2,1)}, bf16[896,512]{1,0:T(8,128)(2,1)S(1)}, u32[]{:S(2)}, u32[]{:S(2)}) collective-permute-start(bf16[896,512]{1,0:T(8,128)(2,1)} %g_hbm.1), channel_id=1, source_target_pairs={{0,1},{1,0},{2,3},{3,2},{4,5},{5,4},{6,7},{7,6},{8,9},{9,8},{10,11... | collective-permute-start | bytes 2752520 | tf_op jit(solution)/shard_map/ppermute | solution.py:32
  10.8 14.0 %collective-permute-start.6 = (bf16[8,16,1024]{2,1,0:T(8,128)(2,1)S(1)}, bf16[8,16,1024]{2,1,0:T(8,128)(2,1)S(1)}, u32[]{:S(2)}, u32[]{:S(2)}) collective-permute-start(bf16[8,16,1024]{2,1,0:T(8,128)(2,1)S(1)} %pad_maximum_fusion.1.own_ref), channel_id=1, source_target_pairs={{0,8},{2,10},{4,12},{6,14},{8,0},{10,2},{12,4},{14,6},{1,9},{3,11}... | collective-permute-start | bytes 786440 | tf_op jit(solution)/shard_map/ppermute | solution.py:36
  12.0 12.8 %collective-permute-start.5 = (bf16[144,512]{1,0:T(8,128)(2,1)S(1)}, bf16[144,512]{1,0:T(8,128)(2,1)S(1)}, u32[]{:S(2)}, u32[]{:S(2)}) collective-permute-start(bf16[144,512]{1,0:T(8,128)(2,1)S(1)} %pad_maximum_fusion.2.refs_0_), channel_id=1, source_target_pairs={{0,2},{2,0},{4,6},{6,4},{8,10},{10,8},{12,14},{14,12},{1,3},{3,1},... | collective-permute-start | bytes 442376 | tf_op jit(solution)/shard_map/ppermute | solution.py:36
  13.6 11.2 %collective-permute-start.4 = (bf16[144,512]{1,0:T(8,128)(2,1)S(1)}, bf16[144,512]{1,0:T(8,128)(2,1)S(1)}, u32[]{:S(2)}, u32[]{:S(2)}) collective-permute-start(bf16[144,512]{1,0:T(8,128)(2,1)S(1)} %pad_maximum_fusion.2.refs_0_), channel_id=1, source_target_pairs={{0,4},{2,6},{4,0},{6,2},{8,12},{10,14},{12,8},{14,10},{1,5},{3,7},... | collective-permute-start | bytes 442376 | tf_op jit(solution)/shard_map/ppermute | solution.py:36
  15.2 10.4 %collective-permute-start.1 = (bf16[144,512]{1,0:T(8,128)(2,1)S(1)}, bf16[144,512]{1,0:T(8,128)(2,1)S(1)}, u32[]{:S(2)}, u32[]{:S(2)}) collective-permute-start(bf16[144,512]{1,0:T(8,128)(2,1)S(1)} %pad_maximum_fusion.2.refs_0_), channel_id=1, source_target_pairs={{0,6},{2,4},{4,2},{6,0},{8,14},{10,12},{12,10},{14,8},{1,7},{3,5},... | collective-permute-start | bytes 442376 | tf_op jit(solution)/shard_map/ppermute | solution.py:36
  15.6 20.5 %slice-start = ((s8[8388608]{0:T(1024)(128)(4,1)}), s8[4194304]{0:T(1024)(128)(4,1)S(1)}, s32[]{:S(2)}) async-start(s8[8388608]{0:T(1024)(128)(4,1)} %bitcast.19), calls=%async_computation | async-start | bytes 8388608
  15.6 20.5 %slice-start.1 = ((s8[8388608]{0:T(1024)(128)(4,1)}), s8[4194304]{0:T(1024)(128)(4,1)S(1)}, s32[]{:S(2)}) async-start(s8[8388608]{0:T(1024)(128)(4,1)} %bitcast.19), calls=%async_computation.1 | async-start | bytes 8388608
  15.6 1.3 %copy-start = (bf16[896,512]{1,0:T(8,128)(2,1)S(1)}, bf16[896,512]{1,0:T(8,128)(2,1)}, u32[]{:S(2)}) copy-start(bf16[896,512]{1,0:T(8,128)(2,1)} %g_hbm.1) | copy-start | bytes 2752516
  24.7 3.2 %collective-permute-start.7 = (bf16[896,512]{1,0:T(8,128)(2,1)S(1)}, bf16[896,512]{1,0:T(8,128)(2,1)S(1)}, u32[]{:S(2)}, u32[]{:S(2)}) collective-permute-start(bf16[896,512]{1,0:T(8,128)(2,1)S(1)} %get-tuple-element.66), channel_id=1, source_target_pairs={{0,1},{1,0},{2,3},{3,2},{4,5},{5,4},{6,7},{7,6},{8,9},{9,8},{10,11... | collective-permute-start | bytes 2752520 | tf_op jit(solution)/shard_map/ppermute | solution.py:32
  25.7 15.2 %collective-permute-start.10 = (bf16[16,16,1024]{2,1,0:T(8,128)(2,1)S(1)}, bf16[16,16,1024]{2,1,0:T(8,128)(2,1)S(1)}, u32[]{:S(2)}, u32[]{:S(2)}) collective-permute-start(bf16[16,16,1024]{2,1,0:T(8,128)(2,1)S(1)} %pad_maximum_fusion), channel_id=1, source_target_pairs={{0,4},{2,6},{4,0},{6,2},{8,12},{10,14},{12,8},{14,10},{1,5},{3,7},... | collective-permute-start | bytes 1572872 | tf_op jit(solution)/shard_map/ppermute | solution.py:36
  27.7 1.3 %collective-permute-start.8 = (f32[16,896]{1,0:T(8,128)S(1)}, f32[16,896]{1,0:T(8,128)S(1)}, u32[]{:S(2)}, u32[]{:S(2)}) collective-permute-start(f32[16,896]{1,0:T(8,128)S(1)} %get-tuple-element.75.mine_ref), channel_id=1, source_target_pairs={{0,1},{1,0},{2,3},{3,2},{4,5},{5,4},{6,7},{7,6},{8,9},{9,8},{10,11... | collective-permute-start | bytes 172040 | tf_op jit(solution)/shard_map/ppermute | solution.py:32
  31.1 15.8 %collective-permute-start.12 = (bf16[64,2304]{1,0:T(8,128)(2,1)S(1)}, bf16[64,2304]{1,0:T(8,128)(2,1)S(1)}, u32[]{:S(2)}, u32[]{:S(2)}) collective-permute-start(bf16[64,2304]{1,0:T(8,128)(2,1)S(1)} %get-tuple-element.88), channel_id=1, source_target_pairs={{0,4},{2,6},{4,0},{6,2},{8,12},{10,14},{12,8},{14,10},{1,5},{3,7},... | collective-permute-start | bytes 884744 | tf_op jit(solution)/shard_map/ppermute | solution.py:36
  32.4 21.7 %collective-permute-start.11 = (bf16[64,2304]{1,0:T(8,128)(2,1)S(1)}, bf16[64,2304]{1,0:T(8,128)(2,1)S(1)}, u32[]{:S(2)}, u32[]{:S(2)}) collective-permute-start(bf16[64,2304]{1,0:T(8,128)(2,1)S(1)} %get-tuple-element.87), channel_id=1, source_target_pairs={{0,2},{2,0},{4,6},{6,4},{8,10},{10,8},{12,14},{14,12},{1,3},{3,1},... | collective-permute-start | bytes 884744 | tf_op jit(solution)/shard_map/ppermute | solution.py:36
  33.4 20.6 %collective-permute-start.13 = (bf16[64,2304]{1,0:T(8,128)(2,1)S(1)}, bf16[64,2304]{1,0:T(8,128)(2,1)S(1)}, u32[]{:S(2)}, u32[]{:S(2)}) collective-permute-start(bf16[64,2304]{1,0:T(8,128)(2,1)S(1)} %get-tuple-element.89), channel_id=1, source_target_pairs={{0,6},{2,4},{4,2},{6,0},{8,14},{10,12},{12,10},{14,8},{1,7},{3,5},... | collective-permute-start | bytes 884744 | tf_op jit(solution)/shard_map/ppermute | solution.py:36
  34.6 6.2 %collective-permute-start.9 = (s32[16,128]{1,0:T(8,128)S(1)}, s32[16,128]{1,0:T(8,128)S(1)}, u32[]{:S(2)}, u32[]{:S(2)}) collective-permute-start(s32[16,128]{1,0:T(8,128)S(1)} %select_select_fusion.info), channel_id=1, source_target_pairs={{0,16},{16,0},{1,17},{17,1},{2,18},{18,2},{3,19},{19,3},{4,20},{20... | collective-permute-start | bytes 24584 | tf_op jit(solution)/shard_map/ppermute | solution.py:32
  46.9 18.5 %collective-permute-start.14 = (bf16[112,1024]{1,0:T(8,128)(2,1)S(1)}, bf16[112,1024]{1,0:T(8,128)(2,1)S(1)}, u32[]{:S(2)}, u32[]{:S(2)}) collective-permute-start(bf16[112,1024]{1,0:T(8,128)(2,1)S(1)} %get-tuple-element.94), channel_id=1, source_target_pairs={{0,2},{2,0},{4,6},{6,4},{8,10},{10,8},{12,14},{14,12},{1,3},{3,1},... | collective-permute-start | bytes 688136 | tf_op jit(solution)/shard_map/ppermute | solution.py:36
  47.9 18.9 %collective-permute-start.15 = (bf16[112,1024]{1,0:T(8,128)(2,1)S(1)}, bf16[112,1024]{1,0:T(8,128)(2,1)S(1)}, u32[]{:S(2)}, u32[]{:S(2)}) collective-permute-start(bf16[112,1024]{1,0:T(8,128)(2,1)S(1)} %get-tuple-element.96), channel_id=1, source_target_pairs={{0,16},{16,0},{1,17},{17,1},{2,18},{18,2},{3,19},{19,3},{4,20},{20... | collective-permute-start | bytes 688136 | tf_op jit(solution)/shard_map/ppermute | solution.py:32
  55.0 18.7 %collective-permute-start.17 = (bf16[64,2304]{1,0:T(8,128)(2,1)S(1)}, bf16[64,2304]{1,0:T(8,128)(2,1)S(1)}, u32[]{:S(2)}, u32[]{:S(2)}) collective-permute-start(bf16[64,2304]{1,0:T(8,128)(2,1)S(1)} %get-tuple-element.90), channel_id=1, source_target_pairs={{0,8},{2,10},{4,12},{6,14},{8,0},{10,2},{12,4},{14,6},{1,9},{3,11}... | collective-permute-start | bytes 884744 | tf_op jit(solution)/shard_map/ppermute | solution.py:36
  57.9 9.1 %collective-permute-start.16 = (bf16[112,1024]{1,0:T(8,128)(2,1)S(1)}, bf16[112,1024]{1,0:T(8,128)(2,1)S(1)}, u32[]{:S(2)}, u32[]{:S(2)}) collective-permute-start(bf16[112,1024]{1,0:T(8,128)(2,1)S(1)} %get-tuple-element.98), channel_id=1, source_target_pairs={{0,18},{2,16},{4,22},{6,20},{8,26},{10,24},{12,30},{14,28},{16,2},... | collective-permute-start | bytes 688136 | tf_op jit(solution)/shard_map/ppermute | solution.py:476
  58.5 16.4 %collective-permute-start.20 = (bf16[64,1792]{1,0:T(8,128)(2,1)S(1)}, bf16[64,1792]{1,0:T(8,128)(2,1)S(1)}, u32[]{:S(2)}, u32[]{:S(2)}) collective-permute-start(bf16[64,1792]{1,0:T(8,128)(2,1)S(1)} %get-tuple-element.109), channel_id=1, source_target_pairs={{0,4},{2,6},{4,0},{6,2},{8,12},{10,14},{12,8},{14,10},{1,5},{3,7},... | collective-permute-start | bytes 688136 | tf_op jit(solution)/shard_map/ppermute | solution.py:36
  65.5 11.0 %collective-permute-start.19 = (bf16[64,1792]{1,0:T(8,128)(2,1)S(1)}, bf16[64,1792]{1,0:T(8,128)(2,1)S(1)}, u32[]{:S(2)}, u32[]{:S(2)}) collective-permute-start(bf16[64,1792]{1,0:T(8,128)(2,1)S(1)} %get-tuple-element.107), channel_id=1, source_target_pairs={{0,2},{2,0},{4,6},{6,4},{8,10},{10,8},{12,14},{14,12},{1,3},{3,1},... | collective-permute-start | bytes 688136 | tf_op jit(solution)/shard_map/ppermute | solution.py:36
  66.8 9.7 %collective-permute-start.21 = (bf16[64,1792]{1,0:T(8,128)(2,1)S(1)}, bf16[64,1792]{1,0:T(8,128)(2,1)S(1)}, u32[]{:S(2)}, u32[]{:S(2)}) collective-permute-start(bf16[64,1792]{1,0:T(8,128)(2,1)S(1)} %get-tuple-element.111), channel_id=1, source_target_pairs={{0,6},{2,4},{4,2},{6,0},{8,14},{10,12},{12,10},{14,8},{1,7},{3,5},... | collective-permute-start | bytes 688136 | tf_op jit(solution)/shard_map/ppermute | solution.py:36
  69.8 4.0 %collective-permute-start.18 = (f32[16,896]{1,0:T(8,128)S(1)}, f32[16,896]{1,0:T(8,128)S(1)}, u32[]{:S(2)}, u32[]{:S(2)}) collective-permute-start(f32[16,896]{1,0:T(8,128)S(1)} %get-tuple-element.99.mine_ref), channel_id=1, source_target_pairs={{0,1},{1,0},{2,3},{3,2},{4,5},{5,4},{6,7},{7,6},{8,9},{9,8},{10,11... | collective-permute-start | bytes 172040 | tf_op jit(solution)/shard_map/ppermute | solution.py:32
  77.4 16.2 %collective-permute-start.25 = (bf16[64,1792]{1,0:T(8,128)(2,1)S(1)}, bf16[64,1792]{1,0:T(8,128)(2,1)S(1)}, u32[]{:S(2)}, u32[]{:S(2)}) collective-permute-start(bf16[64,1792]{1,0:T(8,128)(2,1)S(1)} %get-tuple-element.112), channel_id=1, source_target_pairs={{0,8},{2,10},{4,12},{6,14},{8,0},{10,2},{12,4},{14,6},{1,9},{3,11}... | collective-permute-start | bytes 688136 | tf_op jit(solution)/shard_map/ppermute | solution.py:36
  78.6 7.4 %collective-permute-start.22 = (bf16[64,512]{1,0:T(8,128)(2,1)S(1)}, bf16[64,512]{1,0:T(8,128)(2,1)S(1)}, u32[]{:S(2)}, u32[]{:S(2)}) collective-permute-start(bf16[64,512]{1,0:T(8,128)(2,1)S(1)} %get-tuple-element.115), channel_id=1, source_target_pairs={{0,2},{2,0},{4,6},{6,4},{8,10},{10,8},{12,14},{14,12},{1,3},{3,1},... | collective-permute-start | bytes 196616 | tf_op jit(solution)/shard_map/ppermute | solution.py:36
  78.8 7.1 %collective-permute-start.23 = (bf16[64,512]{1,0:T(8,128)(2,1)S(1)}, bf16[64,512]{1,0:T(8,128)(2,1)S(1)}, u32[]{:S(2)}, u32[]{:S(2)}) collective-permute-start(bf16[64,512]{1,0:T(8,128)(2,1)S(1)} %get-tuple-element.116), channel_id=1, source_target_pairs={{0,4},{2,6},{4,0},{6,2},{8,12},{10,14},{12,8},{14,10},{1,5},{3,7},... | collective-permute-start | bytes 196616 | tf_op jit(solution)/shard_map/ppermute | solution.py:36
  79.9 6.0 %collective-permute-start.24 = (bf16[64,512]{1,0:T(8,128)(2,1)S(1)}, bf16[64,512]{1,0:T(8,128)(2,1)S(1)}, u32[]{:S(2)}, u32[]{:S(2)}) collective-permute-start(bf16[64,512]{1,0:T(8,128)(2,1)S(1)} %get-tuple-element.117), channel_id=1, source_target_pairs={{0,6},{2,4},{4,2},{6,0},{8,14},{10,12},{12,10},{14,8},{1,7},{3,5},... | collective-permute-start | bytes 196616 | tf_op jit(solution)/shard_map/ppermute | solution.py:36
  86.8 6.8 %collective-permute-start.26 = (bf16[64,512]{1,0:T(8,128)(2,1)S(1)}, bf16[64,512]{1,0:T(8,128)(2,1)S(1)}, u32[]{:S(2)}, u32[]{:S(2)}) collective-permute-start(bf16[64,512]{1,0:T(8,128)(2,1)S(1)} %get-tuple-element.118), channel_id=1, source_target_pairs={{0,8},{2,10},{4,12},{6,14},{8,0},{10,2},{12,4},{14,6},{1,9},{3,11}... | collective-permute-start | bytes 196616 | tf_op jit(solution)/shard_map/ppermute | solution.py:36

commit v15 on v14

--- a/solution.py
+++ b/solution.py
@@ -461,7 +461,8 @@
     wide_a = width * 9 // 16
     sends_a = pack(_tie(info, *ready), 0, wide_a)
     got_a = to_near(sends_a)
-    low, sums = through(_tie(info, sends_a[0]), 0, half, 1)
+    wide_low = width * 5 // 8
+    low, sums = through(_tie(info, sends_a[0]), 0, wide_low, 1)
 
     if shared:
         block = (nb * rank, quarter)
@@ -491,7 +492,7 @@
     dense_a = dense(_tie(info, base_own), got_a)
     far_a = to_far(dense_a)
 
-    (high,) = through(_tie(info, dense_a[1]), half, width - half, 0)
+    (high,) = through(_tie(info, dense_a[1]), wide_low, width - wide_low, 0)
     gate = [high] + ([got_y] if shared else [])
     got_b = to_near(
         [_tie(b, *gate) if k in (1, 3) else _tie(b, dense_a[1]) for k, b in enumerate(sends_b)]
@@ -532,7 +533,7 @@
     dense_b = dense(_tie(info, up_sends[0]), got_b)
     far_b = to_far(dense_b)
 
-    grad_tokens = token_grads(_tie(info, dense_b[1]), high, half // step, [grad_tokens])
+    grad_tokens = token_grads(_tie(info, dense_b[1]), high, wide_low // step, [grad_tokens])
     dense_u = dense(_tie(info, grad_tokens), got_u)
     far_u = to_far(dense_u)
 

time: 95.6 us -> 96.4 us (level)
  waiting for transfers between devices: 8.58 us -> 5.64 us
  Pallas kernels: 46.2 us -> 48.5 us
  starting transfers between devices: 34.7 us -> 36.2 us
    ppermute x20, waiting for transfers between devices: 7.52 us -> 4.58 us  [_xor(): return lax.ppermute(x, 'dp', [(i, i ^ k) for i in range(n)])]
    pallas_call x2, Pallas kernels: 9.57 us -> 11.3 us  [through(): _call(functools.partial(through_kernel, z, first), 'through', (1,), [VMEM...]
    ppermute x20, starting transfers between devices: 30.8 us -> 32.2 us  [_xor(): return lax.ppermute(x, 'dp', [(i, i ^ k) for i in range(n)])]
  transfers between devices with their start and end apart: 27 -> 27, of which waited for: 6 -> 6; matrix products, arithmetic and copies ran while one was open for 4% -> 4% of each run, Pallas kernels for 46% -> 48%
where the time goes in v15:
time: 96.4 us; the launch traced here: 96.2 us
  Pallas kernels  48.5 us (50%)
  starting transfers between devices  36.2 us (38%)
  waiting for transfers between devices  5.64 us (6%)
  other arithmetic  2.63 us (3%)
  local copies, waits for them, and re-layouts  2.33 us (2%)
    ppermute x20, starting transfers between devices, _xor(): return lax.ppermute(x, 'dp', [(i, i ^ k) for i in range(n)])  32.2 us
    pallas_call x2, Pallas kernels, through(): _call(functools.partial(through_kernel, z, first), 'through', (1,), [VMEM...  11.3 us
    pallas_call x2, Pallas kernels, token_grads(): _call(functools.partial(tokens_kernel, z, first), 'token_grads', (steps,)...  8.19 us
    pallas_call x1, Pallas kernels, on_device(): _call(functools.partial(base_kernel, z), 'base', (1,), [pl.BlockSpec(memo...  7.78 us
    pallas_call x1, Pallas kernels, on_device(): _call(functools.partial(own_kernel, z), 'base_own', (1,), [VMEM] * 3, VME...  4.78 us
    ppermute x20, waiting for transfers between devices, _xor(): return lax.ppermute(x, 'dp', [(i, i ^ k) for i in range(n)])  4.58 us
    pallas_call x2, Pallas kernels, pack(): _call(functools.partial(pack_kernel, z, NEAR, start), 'pack_down', (1,),...  3.97 us
    ppermute x6, starting transfers between devices, _swap(): return lax.ppermute(x, axis, [(0, 1), (1, 0)])  3.35 us
  transfers between devices with their start and end apart: 27, of which 6 were waited for; matrix products, arithmetic and copies ran while one was open for 4% of the time, Pallas kernels for 48%

profile of v15, /device:TPU:0, one launch (start us, length us, event | category | flops | bytes accessed | tf_op | source)
XLA Modules:
  0.0 96.2 jit_solution(10330166474720399457)
XLA Ops:
  0.6 4.1 %collective-permute-start = (bf16[4,16,512]{2,1,0:T(8,128)(2,1)}, bf16[4,16,512]{2,1,0:T(8,128)(2,1)S(1)}, u32[]{:S(2)}, u32[]{:S(2)}) collective-permute-start(bf16[4,16,512]{2,1,0:T(8,128)(2,1)} %param.11), channel_id=1, source_target_pairs={{0,8},{2,10},{4,12},{6,14},{8,0},{10,2},{12,4},{14,6},{1,9},{3,11}... | collective-permute-start | bytes 196616 | tf_op jit(solution)/shard_map/ppermute | solution.py:36
  5.7 1.6 %collective-permute-start.2 = (bf16[4,16,1024]{2,1,0:T(8,128)(2,1)S(1)}, bf16[4,16,1024]{2,1,0:T(8,128)(2,1)S(1)}, u32[]{:S(2)}, u32[]{:S(2)}) collective-permute-start(bf16[4,16,1024]{2,1,0:T(8,128)(2,1)S(1)} %get-tuple-element.127), channel_id=1, source_target_pairs={{0,2},{2,0},{4,6},{6,4},{8,10},{10,8},{12,14},{14,12},{1,3},{3,1},... | collective-permute-start | bytes 393224 | tf_op jit(solution)/shard_map/ppermute | solution.py:36
  8.9 1.8 %collective-permute-done.2 = bf16[4,16,1024]{2,1,0:T(8,128)(2,1)S(1)} collective-permute-done((bf16[4,16,1024]{2,1,0:T(8,128)(2,1)S(1)}, bf16[4,16,1024]{2,1,0:T(8,128)(2,1)S(1)}, u32[]{:S(2)}, u32[]{:S(2)}) %collective-permute-start.2) | collective-permute-done | bytes 131104 | tf_op jit(solution)/shard_map/ppermute | solution.py:36
  12.0 1.6 %collective-permute-start.5 = (bf16[144,512]{1,0:T(8,128)(2,1)S(1)}, bf16[144,512]{1,0:T(8,128)(2,1)S(1)}, u32[]{:S(2)}, u32[]{:S(2)}) collective-permute-start(bf16[144,512]{1,0:T(8,128)(2,1)S(1)} %pad_maximum_fusion.2.refs_0_), channel_id=1, source_target_pairs={{0,2},{2,0},{4,6},{6,4},{8,10},{10,8},{12,14},{14,12},{1,3},{3,1},... | collective-permute-start | bytes 442376 | tf_op jit(solution)/shard_map/ppermute | solution.py:36
  13.6 1.6 %collective-permute-start.4 = (bf16[144,512]{1,0:T(8,128)(2,1)S(1)}, bf16[144,512]{1,0:T(8,128)(2,1)S(1)}, u32[]{:S(2)}, u32[]{:S(2)}) collective-permute-start(bf16[144,512]{1,0:T(8,128)(2,1)S(1)} %pad_maximum_fusion.2.refs_0_), channel_id=1, source_target_pairs={{0,4},{2,6},{4,0},{6,2},{8,12},{10,14},{12,8},{14,10},{1,5},{3,7},... | collective-permute-start | bytes 442376 | tf_op jit(solution)/shard_map/ppermute | solution.py:36
  15.6 1.3 %copy-done = bf16[896,512]{1,0:T(8,128)(2,1)S(1)} copy-done((bf16[896,512]{1,0:T(8,128)(2,1)S(1)}, bf16[896,512]{1,0:T(8,128)(2,1)}, u32[]{:S(2)}) %copy-start) | copy-done | bytes 917528
  17.0 7.8 %base.1 = (bf16[896,512]{1,0:T(8,128)(2,1)S(1)}, bf16[896,1024]{1,0:T(8,128)(2,1)S(1)}, bf16[896,4096]{1,0:T(8,128)(2,1)S(1)}) custom-call(s32[16,128]{1,0:T(8,128)S(1)} %select_select_fusion.1.info, bf16[896,4096]{1,0:T(8,128)(2,1)} %x_hbm.1, bf16[4096,1024]{1,0:T(8,128)(2,1)} %w_ref.5, bf16[896,512]{1,0:T(8,128)(2,1)S(1)} %copy-done, ...), custom_call_target="tpu_custom_call" | custom-call | flops 1 | bytes 1 | tf_op jit(solution)/shard_map/base/pallas_call | solution.py:388
  27.9 1.0 %collective-permute-done.8.other_ref = f32[16,896]{1,0:T(8,128)S(1)} collective-permute-done((f32[16,896]{1,0:T(8,128)S(1)}, f32[16,896]{1,0:T(8,128)S(1)}, u32[]{:S(2)}, u32[]{:S(2)}) %collective-permute-start.8) | collective-permute-done | bytes 57376 | tf_op jit(solution)/shard_map/ppermute | solution.py:32
  29.0 2.1 %pack_down.2 = (bf16[64,2304]{1,0:T(8,128)(2,1)S(1)}, bf16[64,2304]{1,0:T(8,128)(2,1)S(1)}, bf16[64,2304]{1,0:T(8,128)(2,1)S(1)}, bf16[64,2304]{1,0:T(8,128)(2,1)S(1)}) custom-call(s32[16,128]{1,0:T(8,128)S(1)} %select_select_fusion.info, f32[16,896]{1,0:T(8,128)S(1)} %get-tuple-element.75.mine_ref, f32[16,896]{1,0:T(8,128)S(1)} %collective-permute-done.8.other_ref, ...), custom_call_target="tpu_custom_call" | custom-call | flops 1 | bytes 1 | tf_op jit(solution)/shard_map/pack_down/pallas_call | solution.py:431
  31.1 1.3 %collective-permute-start.12 = (bf16[64,2304]{1,0:T(8,128)(2,1)S(1)}, bf16[64,2304]{1,0:T(8,128)(2,1)S(1)}, u32[]{:S(2)}, u32[]{:S(2)}) collective-permute-start(bf16[64,2304]{1,0:T(8,128)(2,1)S(1)} %get-tuple-element.88), channel_id=1, source_target_pairs={{0,4},{2,6},{4,0},{6,2},{8,12},{10,14},{12,8},{14,10},{1,5},{3,7},... | collective-permute-start | bytes 884744 | tf_op jit(solution)/shard_map/ppermute | solution.py:36
  32.4 1.1 %collective-permute-start.11 = (bf16[64,2304]{1,0:T(8,128)(2,1)S(1)}, bf16[64,2304]{1,0:T(8,128)(2,1)S(1)}, u32[]{:S(2)}, u32[]{:S(2)}) collective-permute-start(bf16[64,2304]{1,0:T(8,128)(2,1)S(1)} %get-tuple-element.87), channel_id=1, source_target_pairs={{0,2},{2,0},{4,6},{6,4},{8,10},{10,8},{12,14},{14,12},{1,3},{3,1},... | collective-permute-start | bytes 884744 | tf_op jit(solution)/shard_map/ppermute | solution.py:36
  33.4 1.2 %collective-permute-start.13 = (bf16[64,2304]{1,0:T(8,128)(2,1)S(1)}, bf16[64,2304]{1,0:T(8,128)(2,1)S(1)}, u32[]{:S(2)}, u32[]{:S(2)}) collective-permute-start(bf16[64,2304]{1,0:T(8,128)(2,1)S(1)} %get-tuple-element.89), channel_id=1, source_target_pairs={{0,6},{2,4},{4,2},{6,0},{8,14},{10,12},{12,10},{14,8},{1,7},{3,5},... | collective-permute-start | bytes 884744 | tf_op jit(solution)/shard_map/ppermute | solution.py:36
  34.6 1.5 %collective-permute-start.9 = (s32[16,128]{1,0:T(8,128)S(1)}, s32[16,128]{1,0:T(8,128)S(1)}, u32[]{:S(2)}, u32[]{:S(2)}) collective-permute-start(s32[16,128]{1,0:T(8,128)S(1)} %select_select_fusion.info), channel_id=1, source_target_pairs={{0,16},{16,0},{1,17},{17,1},{2,18},{18,2},{3,19},{19,3},{4,20},{20... | collective-permute-start | bytes 24584 | tf_op jit(solution)/shard_map/ppermute | solution.py:32
  36.1 6.6 %through.2 = (f32[896,2560]{1,0:T(8,128)S(1)}, bf16[2,64,128]{2,1,0:T(8,128)(2,1)S(1)}) custom-call(s32[16,128]{1,0:T(8,128)S(1)} %select_select_fusion.info, bf16[896,1024]{1,0:T(8,128)(2,1)S(1)} %get-tuple-element.73.g_ref, bf16[4096,1024]{1,0:T(8,128)(2,1)S(1)} %bitcast.20), custom_call_target="tpu_custom_call" | custom-call | flops 1 | bytes 1 | tf_op jit(solution)/shard_map/through/pallas_call | solution.py:455
  43.8 1.8 %pack_down.3 = (bf16[64,1792]{1,0:T(8,128)(2,1)S(1)}, bf16[64,1792]{1,0:T(8,128)(2,1)S(1)}, bf16[64,1792]{1,0:T(8,128)(2,1)S(1)}, bf16[64,1792]{1,0:T(8,128)(2,1)S(1)}) custom-call(s32[16,128]{1,0:T(8,128)S(1)} %select_select_fusion.info, f32[16,896]{1,0:T(8,128)S(1)} %get-tuple-element.75.mine_ref, f32[16,896]{1,0:T(8,128)S(1)} %collective-permute-done.8.other_ref, ...), custom_call_target="tpu_custom_call" | custom-call | flops 1 | bytes 1 | tf_op jit(solution)/shard_map/pack_down/pallas_call | solution.py:431
  45.7 1.2 %collective-permute-done.12.refs_2_ = bf16[64,2304]{1,0:T(8,128)(2,1)S(1)} collective-permute-done((bf16[64,2304]{1,0:T(8,128)(2,1)S(1)}, bf16[64,2304]{1,0:T(8,128)(2,1)S(1)}, u32[]{:S(2)}, u32[]{:S(2)}) %collective-permute-start.12) | collective-permute-done | bytes 294944 | tf_op jit(solution)/shard_map/ppermute | solution.py:36
  47.9 1.5 %collective-permute-start.15 = (bf16[112,1024]{1,0:T(8,128)(2,1)S(1)}, bf16[112,1024]{1,0:T(8,128)(2,1)S(1)}, u32[]{:S(2)}, u32[]{:S(2)}) collective-permute-start(bf16[112,1024]{1,0:T(8,128)(2,1)S(1)} %get-tuple-element.96), channel_id=1, source_target_pairs={{0,16},{16,0},{1,17},{17,1},{2,18},{18,2},{3,19},{19,3},{4,20},{20... | collective-permute-start | bytes 688136 | tf_op jit(solution)/shard_map/ppermute | solution.py:32
  49.4 4.8 %base_own.1.base_ref = f32[896,512]{1,0:T(8,128)S(1)} custom-call(s32[16,128]{1,0:T(8,128)S(1)} %select_select_fusion.info, bf16[896,4096]{1,0:T(8,128)(2,1)S(1)} %get-tuple-element.76.x_ref, bf16[4096,1024]{1,0:T(8,128)(2,1)S(1)} %bitcast.20, bf16[896,512]{1,0:T(8,128)(2,1)S(1)} %collective-permute-done.7.far_ref), custom_call_target="tpu_custom_call" | custom-call | flops 1 | bytes 1 | tf_op jit(solution)/shard_map/base_own/pallas_call | solution.py:488
  55.2 2.9 %collective-permute-start.17 = (bf16[64,2304]{1,0:T(8,128)(2,1)S(1)}, bf16[64,2304]{1,0:T(8,128)(2,1)S(1)}, u32[]{:S(2)}, u32[]{:S(2)}) collective-permute-start(bf16[64,2304]{1,0:T(8,128)(2,1)S(1)} %get-tuple-element.90), channel_id=1, source_target_pairs={{0,8},{2,10},{4,12},{6,14},{8,0},{10,2},{12,4},{14,6},{1,9},{3,11}... | collective-permute-start | bytes 884744 | tf_op jit(solution)/shard_map/ppermute | solution.py:36
  58.8 2.0 %collective-permute-start.20 = (bf16[64,1792]{1,0:T(8,128)(2,1)S(1)}, bf16[64,1792]{1,0:T(8,128)(2,1)S(1)}, u32[]{:S(2)}, u32[]{:S(2)}) collective-permute-start(bf16[64,1792]{1,0:T(8,128)(2,1)S(1)} %get-tuple-element.109), channel_id=1, source_target_pairs={{0,4},{2,6},{4,0},{6,2},{8,12},{10,14},{12,8},{14,10},{1,5},{3,7},... | collective-permute-start | bytes 688136 | tf_op jit(solution)/shard_map/ppermute | solution.py:36
  60.8 4.6 %through.3.through_ref = f32[896,1536]{1,0:T(8,128)S(1)} custom-call(s32[16,128]{1,0:T(8,128)S(1)} %select_select_fusion.info, bf16[896,1024]{1,0:T(8,128)(2,1)S(1)} %get-tuple-element.73.g_ref, bf16[4096,1024]{1,0:T(8,128)(2,1)S(1)} %bitcast.20), custom_call_target="tpu_custom_call" | custom-call | flops 1 | bytes 1 | tf_op jit(solution)/shard_map/through/pallas_call | solution.py:455
  65.4 1.3 %collective-permute-start.19 = (bf16[64,1792]{1,0:T(8,128)(2,1)S(1)}, bf16[64,1792]{1,0:T(8,128)(2,1)S(1)}, u32[]{:S(2)}, u32[]{:S(2)}) collective-permute-start(bf16[64,1792]{1,0:T(8,128)(2,1)S(1)} %get-tuple-element.107), channel_id=1, source_target_pairs={{0,2},{2,0},{4,6},{6,4},{8,10},{10,8},{12,14},{14,12},{1,3},{3,1},... | collective-permute-start | bytes 688136 | tf_op jit(solution)/shard_map/ppermute | solution.py:36
  67.0 2.8 %shrink.1 = (bf16[112,4096]{1,0:T(8,128)(2,1)S(1)}, f32[16,896]{1,0:T(8,128)S(1)}) custom-call(s32[16,128]{1,0:T(8,128)S(1)} %select_select_fusion.info, bf16[896,4096]{1,0:T(8,128)(2,1)S(1)} %get-tuple-element.76.x_ref, bf16[112,1024]{1,0:T(8,128)(2,1)S(1)} %get-tuple-element.81.refs_0_, bf16[112,1024]{1,0:T(8,128)(2,1)S(1)} %collective-permute-done.14.refs_1_, ...), custom_call_target="tpu_custom_call" | custom-call | flops 1 | bytes 1 | tf_op jit(solution)/shard_map/shrink/pallas_call | solution.py:503
  69.9 4.8 %token_grads.2.refs_0_ = bf16[896,4096]{1,0:T(8,128)(2,1)} custom-call(s32[16,128]{1,0:T(8,128)S(1)} %select_select_fusion.info, f32[896,2560]{1,0:T(8,128)S(1)} %get-tuple-element.79.through_ref, f32[16,896]{1,0:T(8,128)S(1)} %get-tuple-element.75.mine_ref, f32[16,896]{1,0:T(8,128)S(1)} %collective-permute-done.8.other_ref, ...), custom_call_target="tpu_custom_call" | custom-call | flops 1 | bytes 1 | tf_op jit(solution)/shard_map/token_grads/pallas_call | solution.py:515
  74.7 1.1 %pack_up.1 = (bf16[64,512]{1,0:T(8,128)(2,1)S(1)}, bf16[64,512]{1,0:T(8,128)(2,1)S(1)}, bf16[64,512]{1,0:T(8,128)(2,1)S(1)}, bf16[64,512]{1,0:T(8,128)(2,1)S(1)}) custom-call(s32[16,128]{1,0:T(8,128)S(1)} %select_select_fusion.info, f32[16,896]{1,0:T(8,128)S(1)} %get-tuple-element.99.mine_ref, f32[16,896]{1,0:T(8,128)S(1)} %collective-permute-done.18.other_ref, ...), custom_call_target="tpu_custom_call" | custom-call | flops 1 | bytes 1 | tf_op jit(solution)/shard_map/pack_up/pallas_call | solution.py:525
  77.3 1.5 %collective-permute-start.25 = (bf16[64,1792]{1,0:T(8,128)(2,1)S(1)}, bf16[64,1792]{1,0:T(8,128)(2,1)S(1)}, u32[]{:S(2)}, u32[]{:S(2)}) collective-permute-start(bf16[64,1792]{1,0:T(8,128)(2,1)S(1)} %get-tuple-element.112), channel_id=1, source_target_pairs={{0,8},{2,10},{4,12},{6,14},{8,0},{10,2},{12,4},{14,6},{1,9},{3,11}... | collective-permute-start | bytes 688136 | tf_op jit(solution)/shard_map/ppermute | solution.py:36
  79.1 1.1 %collective-permute-start.23 = (bf16[64,512]{1,0:T(8,128)(2,1)S(1)}, bf16[64,512]{1,0:T(8,128)(2,1)S(1)}, u32[]{:S(2)}, u32[]{:S(2)}) collective-permute-start(bf16[64,512]{1,0:T(8,128)(2,1)S(1)} %get-tuple-element.116), channel_id=1, source_target_pairs={{0,4},{2,6},{4,0},{6,2},{8,12},{10,14},{12,8},{14,10},{1,5},{3,7},... | collective-permute-start | bytes 196616 | tf_op jit(solution)/shard_map/ppermute | solution.py:36
  80.2 2.1 %collective-permute-start.24 = (bf16[64,512]{1,0:T(8,128)(2,1)S(1)}, bf16[64,512]{1,0:T(8,128)(2,1)S(1)}, u32[]{:S(2)}, u32[]{:S(2)}) collective-permute-start(bf16[64,512]{1,0:T(8,128)(2,1)S(1)} %get-tuple-element.117), channel_id=1, source_target_pairs={{0,6},{2,4},{4,2},{6,0},{8,14},{10,12},{12,10},{14,8},{1,7},{3,5},... | collective-permute-start | bytes 196616 | tf_op jit(solution)/shard_map/ppermute | solution.py:36
  82.3 3.4 %token_grads.3 = bf16[896,4096]{1,0:T(8,128)(2,1)} custom-call(s32[16,128]{1,0:T(8,128)S(1)} %select_select_fusion.info, f32[896,1536]{1,0:T(8,128)S(1)} %through.3.through_ref, f32[16,896]{1,0:T(8,128)S(1)} %get-tuple-element.75.mine_ref, f32[16,896]{1,0:T(8,128)S(1)} %collective-permute-done.8.other_ref, ...), custom_call_target="tpu_custom_call", output_to_operand_aliasing={{}: (5, {})} | custom-call | flops 1 | bytes 1 | tf_op jit(solution)/shard_map/token_grads/pallas_call | solution.py:515
  86.6 5.6 %collective-permute-start.26 = (bf16[64,512]{1,0:T(8,128)(2,1)S(1)}, bf16[64,512]{1,0:T(8,128)(2,1)S(1)}, u32[]{:S(2)}, u32[]{:S(2)}) collective-permute-start(bf16[64,512]{1,0:T(8,128)(2,1)S(1)} %get-tuple-element.118), channel_id=1, source_target_pairs={{0,8},{2,10},{4,12},{6,14},{8,0},{10,2},{12,4},{14,6},{1,9},{3,11}... | collective-permute-start | bytes 196616 | tf_op jit(solution)/shard_map/ppermute | solution.py:36
  92.2 2.0 %projected.1 = bf16[896,512]{1,0:T(8,128)(2,1)} custom-call(s32[16,128]{1,0:T(8,128)S(1)} %select_select_fusion.info, f32[896,512]{1,0:T(8,128)S(1)} %base_own.1.base_ref, f32[16,896]{1,0:T(8,128)S(1)} %get-tuple-element.99.mine_ref, f32[16,896]{1,0:T(8,128)S(1)} %collective-permute-done.18.other_ref, bf16[112,512]{1,0:T(8,128)(2,1)S(1)} %get-tuple-element.120.up_ref), custom_call_target="tpu_custom_call" | custom-call | flops 1 | bytes 1 | tf_op jit(solution)/shard_map/projected/pallas_call | solution.py:540
  94.4 1.8 %final.1 = (f32[64,4096]{1,0:T(8,128)}, f32[64,512]{1,0:T(8,128)}) custom-call(s32[16,128]{1,0:T(8,128)S(1)} %select_select_fusion.info, f32[64,2304]{1,0:T(8,128)S(1)} %get-tuple-element.121.refs_0_, bf16[64,2304]{1,0:T(8,128)(2,1)S(1)} %collective-permute-done.17.refs_1_, f32[64,1792]{1,0:T(8,128)S(1)} %get-tuple-element.122.refs_2_, ...), custom_call_target="tpu_custom_call" | custom-call | flops 1 | bytes 1 | tf_op jit(solution)/shard_map/final/pallas_call | solution.py:550
  (65 shorter events, 14.2 us)
Async XLA Ops:
  0.6 10.5 %collective-permute-start = (bf16[4,16,512]{2,1,0:T(8,128)(2,1)}, bf16[4,16,512]{2,1,0:T(8,128)(2,1)S(1)}, u32[]{:S(2)}, u32[]{:S(2)}) collective-permute-start(bf16[4,16,512]{2,1,0:T(8,128)(2,1)} %param.11), channel_id=1, source_target_pairs={{0,8},{2,10},{4,12},{6,14},{8,0},{10,2},{12,4},{14,6},{1,9},{3,11}... | collective-permute-start | bytes 196616 | tf_op jit(solution)/shard_map/ppermute | solution.py:36
  5.7 5.0 %collective-permute-start.2 = (bf16[4,16,1024]{2,1,0:T(8,128)(2,1)S(1)}, bf16[4,16,1024]{2,1,0:T(8,128)(2,1)S(1)}, u32[]{:S(2)}, u32[]{:S(2)}) collective-permute-start(bf16[4,16,1024]{2,1,0:T(8,128)(2,1)S(1)} %get-tuple-element.127), channel_id=1, source_target_pairs={{0,2},{2,0},{4,6},{6,4},{8,10},{10,8},{12,14},{14,12},{1,3},{3,1},... | collective-permute-start | bytes 393224 | tf_op jit(solution)/shard_map/ppermute | solution.py:36
  7.3 8.3 %collective-permute-start.3 = (bf16[896,512]{1,0:T(8,128)(2,1)}, bf16[896,512]{1,0:T(8,128)(2,1)S(1)}, u32[]{:S(2)}, u32[]{:S(2)}) collective-permute-start(bf16[896,512]{1,0:T(8,128)(2,1)} %g_hbm.1), channel_id=1, source_target_pairs={{0,1},{1,0},{2,3},{3,2},{4,5},{5,4},{6,7},{7,6},{8,9},{9,8},{10,11... | collective-permute-start | bytes 2752520 | tf_op jit(solution)/shard_map/ppermute | solution.py:32
  10.8 14.0 %collective-permute-start.6 = (bf16[8,16,1024]{2,1,0:T(8,128)(2,1)S(1)}, bf16[8,16,1024]{2,1,0:T(8,128)(2,1)S(1)}, u32[]{:S(2)}, u32[]{:S(2)}) collective-permute-start(bf16[8,16,1024]{2,1,0:T(8,128)(2,1)S(1)} %pad_maximum_fusion.1.own_ref), channel_id=1, source_target_pairs={{0,8},{2,10},{4,12},{6,14},{8,0},{10,2},{12,4},{14,6},{1,9},{3,11}... | collective-permute-start | bytes 786440 | tf_op jit(solution)/shard_map/ppermute | solution.py:36
  12.0 12.8 %collective-permute-start.5 = (bf16[144,512]{1,0:T(8,128)(2,1)S(1)}, bf16[144,512]{1,0:T(8,128)(2,1)S(1)}, u32[]{:S(2)}, u32[]{:S(2)}) collective-permute-start(bf16[144,512]{1,0:T(8,128)(2,1)S(1)} %pad_maximum_fusion.2.refs_0_), channel_id=1, source_target_pairs={{0,2},{2,0},{4,6},{6,4},{8,10},{10,8},{12,14},{14,12},{1,3},{3,1},... | collective-permute-start | bytes 442376 | tf_op jit(solution)/shard_map/ppermute | solution.py:36
  13.6 11.2 %collective-permute-start.4 = (bf16[144,512]{1,0:T(8,128)(2,1)S(1)}, bf16[144,512]{1,0:T(8,128)(2,1)S(1)}, u32[]{:S(2)}, u32[]{:S(2)}) collective-permute-start(bf16[144,512]{1,0:T(8,128)(2,1)S(1)} %pad_maximum_fusion.2.refs_0_), channel_id=1, source_target_pairs={{0,4},{2,6},{4,0},{6,2},{8,12},{10,14},{12,8},{14,10},{1,5},{3,7},... | collective-permute-start | bytes 442376 | tf_op jit(solution)/shard_map/ppermute | solution.py:36
  15.2 10.4 %collective-permute-start.1 = (bf16[144,512]{1,0:T(8,128)(2,1)S(1)}, bf16[144,512]{1,0:T(8,128)(2,1)S(1)}, u32[]{:S(2)}, u32[]{:S(2)}) collective-permute-start(bf16[144,512]{1,0:T(8,128)(2,1)S(1)} %pad_maximum_fusion.2.refs_0_), channel_id=1, source_target_pairs={{0,6},{2,4},{4,2},{6,0},{8,14},{10,12},{12,10},{14,8},{1,7},{3,5},... | collective-permute-start | bytes 442376 | tf_op jit(solution)/shard_map/ppermute | solution.py:36
  15.6 20.5 %slice-start = ((s8[8388608]{0:T(1024)(128)(4,1)}), s8[4194304]{0:T(1024)(128)(4,1)S(1)}, s32[]{:S(2)}) async-start(s8[8388608]{0:T(1024)(128)(4,1)} %bitcast.19), calls=%async_computation | async-start | bytes 8388608
  15.6 20.5 %slice-start.1 = ((s8[8388608]{0:T(1024)(128)(4,1)}), s8[4194304]{0:T(1024)(128)(4,1)S(1)}, s32[]{:S(2)}) async-start(s8[8388608]{0:T(1024)(128)(4,1)} %bitcast.19), calls=%async_computation.1 | async-start | bytes 8388608
  15.6 1.3 %copy-start = (bf16[896,512]{1,0:T(8,128)(2,1)S(1)}, bf16[896,512]{1,0:T(8,128)(2,1)}, u32[]{:S(2)}) copy-start(bf16[896,512]{1,0:T(8,128)(2,1)} %g_hbm.1) | copy-start | bytes 2752516
  24.7 3.2 %collective-permute-start.7 = (bf16[896,512]{1,0:T(8,128)(2,1)S(1)}, bf16[896,512]{1,0:T(8,128)(2,1)S(1)}, u32[]{:S(2)}, u32[]{:S(2)}) collective-permute-start(bf16[896,512]{1,0:T(8,128)(2,1)S(1)} %get-tuple-element.66), channel_id=1, source_target_pairs={{0,1},{1,0},{2,3},{3,2},{4,5},{5,4},{6,7},{7,6},{8,9},{9,8},{10,11... | collective-permute-start | bytes 2752520 | tf_op jit(solution)/shard_map/ppermute | solution.py:32
  25.7 17.1 %collective-permute-start.10 = (bf16[16,16,1024]{2,1,0:T(8,128)(2,1)S(1)}, bf16[16,16,1024]{2,1,0:T(8,128)(2,1)S(1)}, u32[]{:S(2)}, u32[]{:S(2)}) collective-permute-start(bf16[16,16,1024]{2,1,0:T(8,128)(2,1)S(1)} %pad_maximum_fusion), channel_id=1, source_target_pairs={{0,4},{2,6},{4,0},{6,2},{8,12},{10,14},{12,8},{14,10},{1,5},{3,7},... | collective-permute-start | bytes 1572872 | tf_op jit(solution)/shard_map/ppermute | solution.py:36
  27.7 1.3 %collective-permute-start.8 = (f32[16,896]{1,0:T(8,128)S(1)}, f32[16,896]{1,0:T(8,128)S(1)}, u32[]{:S(2)}, u32[]{:S(2)}) collective-permute-start(f32[16,896]{1,0:T(8,128)S(1)} %get-tuple-element.75.mine_ref), channel_id=1, source_target_pairs={{0,1},{1,0},{2,3},{3,2},{4,5},{5,4},{6,7},{7,6},{8,9},{9,8},{10,11... | collective-permute-start | bytes 172040 | tf_op jit(solution)/shard_map/ppermute | solution.py:32
  31.1 15.8 %collective-permute-start.12 = (bf16[64,2304]{1,0:T(8,128)(2,1)S(1)}, bf16[64,2304]{1,0:T(8,128)(2,1)S(1)}, u32[]{:S(2)}, u32[]{:S(2)}) collective-permute-start(bf16[64,2304]{1,0:T(8,128)(2,1)S(1)} %get-tuple-element.88), channel_id=1, source_target_pairs={{0,4},{2,6},{4,0},{6,2},{8,12},{10,14},{12,8},{14,10},{1,5},{3,7},... | collective-permute-start | bytes 884744 | tf_op jit(solution)/shard_map/ppermute | solution.py:36
  32.4 21.8 %collective-permute-start.11 = (bf16[64,2304]{1,0:T(8,128)(2,1)S(1)}, bf16[64,2304]{1,0:T(8,128)(2,1)S(1)}, u32[]{:S(2)}, u32[]{:S(2)}) collective-permute-start(bf16[64,2304]{1,0:T(8,128)(2,1)S(1)} %get-tuple-element.87), channel_id=1, source_target_pairs={{0,2},{2,0},{4,6},{6,4},{8,10},{10,8},{12,14},{14,12},{1,3},{3,1},... | collective-permute-start | bytes 884744 | tf_op jit(solution)/shard_map/ppermute | solution.py:36
  33.4 20.8 %collective-permute-start.13 = (bf16[64,2304]{1,0:T(8,128)(2,1)S(1)}, bf16[64,2304]{1,0:T(8,128)(2,1)S(1)}, u32[]{:S(2)}, u32[]{:S(2)}) collective-permute-start(bf16[64,2304]{1,0:T(8,128)(2,1)S(1)} %get-tuple-element.89), channel_id=1, source_target_pairs={{0,6},{2,4},{4,2},{6,0},{8,14},{10,12},{12,10},{14,8},{1,7},{3,5},... | collective-permute-start | bytes 884744 | tf_op jit(solution)/shard_map/ppermute | solution.py:36
  34.6 8.1 %collective-permute-start.9 = (s32[16,128]{1,0:T(8,128)S(1)}, s32[16,128]{1,0:T(8,128)S(1)}, u32[]{:S(2)}, u32[]{:S(2)}) collective-permute-start(s32[16,128]{1,0:T(8,128)S(1)} %select_select_fusion.info), channel_id=1, source_target_pairs={{0,16},{16,0},{1,17},{17,1},{2,18},{18,2},{3,19},{19,3},{4,20},{20... | collective-permute-start | bytes 24584 | tf_op jit(solution)/shard_map/ppermute | solution.py:32
  46.9 18.5 %collective-permute-start.14 = (bf16[112,1024]{1,0:T(8,128)(2,1)S(1)}, bf16[112,1024]{1,0:T(8,128)(2,1)S(1)}, u32[]{:S(2)}, u32[]{:S(2)}) collective-permute-start(bf16[112,1024]{1,0:T(8,128)(2,1)S(1)} %get-tuple-element.94), channel_id=1, source_target_pairs={{0,2},{2,0},{4,6},{6,4},{8,10},{10,8},{12,14},{14,12},{1,3},{3,1},... | collective-permute-start | bytes 688136 | tf_op jit(solution)/shard_map/ppermute | solution.py:36
  47.9 18.8 %collective-permute-start.15 = (bf16[112,1024]{1,0:T(8,128)(2,1)S(1)}, bf16[112,1024]{1,0:T(8,128)(2,1)S(1)}, u32[]{:S(2)}, u32[]{:S(2)}) collective-permute-start(bf16[112,1024]{1,0:T(8,128)(2,1)S(1)} %get-tuple-element.96), channel_id=1, source_target_pairs={{0,16},{16,0},{1,17},{17,1},{2,18},{18,2},{3,19},{19,3},{4,20},{20... | collective-permute-start | bytes 688136 | tf_op jit(solution)/shard_map/ppermute | solution.py:32
  55.2 19.5 %collective-permute-start.17 = (bf16[64,2304]{1,0:T(8,128)(2,1)S(1)}, bf16[64,2304]{1,0:T(8,128)(2,1)S(1)}, u32[]{:S(2)}, u32[]{:S(2)}) collective-permute-start(bf16[64,2304]{1,0:T(8,128)(2,1)S(1)} %get-tuple-element.90), channel_id=1, source_target_pairs={{0,8},{2,10},{4,12},{6,14},{8,0},{10,2},{12,4},{14,6},{1,9},{3,11}... | collective-permute-start | bytes 884744 | tf_op jit(solution)/shard_map/ppermute | solution.py:36
  58.1 8.9 %collective-permute-start.16 = (bf16[112,1024]{1,0:T(8,128)(2,1)S(1)}, bf16[112,1024]{1,0:T(8,128)(2,1)S(1)}, u32[]{:S(2)}, u32[]{:S(2)}) collective-permute-start(bf16[112,1024]{1,0:T(8,128)(2,1)S(1)} %get-tuple-element.98), channel_id=1, source_target_pairs={{0,18},{2,16},{4,22},{6,20},{8,26},{10,24},{12,30},{14,28},{16,2},... | collective-permute-start | bytes 688136 | tf_op jit(solution)/shard_map/ppermute | solution.py:477
  58.8 17.0 %collective-permute-start.20 = (bf16[64,1792]{1,0:T(8,128)(2,1)S(1)}, bf16[64,1792]{1,0:T(8,128)(2,1)S(1)}, u32[]{:S(2)}, u32[]{:S(2)}) collective-permute-start(bf16[64,1792]{1,0:T(8,128)(2,1)S(1)} %get-tuple-element.109), channel_id=1, source_target_pairs={{0,4},{2,6},{4,0},{6,2},{8,12},{10,14},{12,8},{14,10},{1,5},{3,7},... | collective-permute-start | bytes 688136 | tf_op jit(solution)/shard_map/ppermute | solution.py:36
  65.4 10.9 %collective-permute-start.19 = (bf16[64,1792]{1,0:T(8,128)(2,1)S(1)}, bf16[64,1792]{1,0:T(8,128)(2,1)S(1)}, u32[]{:S(2)}, u32[]{:S(2)}) collective-permute-start(bf16[64,1792]{1,0:T(8,128)(2,1)S(1)} %get-tuple-element.107), channel_id=1, source_target_pairs={{0,2},{2,0},{4,6},{6,4},{8,10},{10,8},{12,14},{14,12},{1,3},{3,1},... | collective-permute-start | bytes 688136 | tf_op jit(solution)/shard_map/ppermute | solution.py:36
  66.7 9.6 %collective-permute-start.21 = (bf16[64,1792]{1,0:T(8,128)(2,1)S(1)}, bf16[64,1792]{1,0:T(8,128)(2,1)S(1)}, u32[]{:S(2)}, u32[]{:S(2)}) collective-permute-start(bf16[64,1792]{1,0:T(8,128)(2,1)S(1)} %get-tuple-element.111), channel_id=1, source_target_pairs={{0,6},{2,4},{4,2},{6,0},{8,14},{10,12},{12,10},{14,8},{1,7},{3,5},... | collective-permute-start | bytes 688136 | tf_op jit(solution)/shard_map/ppermute | solution.py:36
  69.8 4.9 %collective-permute-start.18 = (f32[16,896]{1,0:T(8,128)S(1)}, f32[16,896]{1,0:T(8,128)S(1)}, u32[]{:S(2)}, u32[]{:S(2)}) collective-permute-start(f32[16,896]{1,0:T(8,128)S(1)} %get-tuple-element.99.mine_ref), channel_id=1, source_target_pairs={{0,1},{1,0},{2,3},{3,2},{4,5},{5,4},{6,7},{7,6},{8,9},{9,8},{10,11... | collective-permute-start | bytes 172040 | tf_op jit(solution)/shard_map/ppermute | solution.py:32
  77.3 17.2 %collective-permute-start.25 = (bf16[64,1792]{1,0:T(8,128)(2,1)S(1)}, bf16[64,1792]{1,0:T(8,128)(2,1)S(1)}, u32[]{:S(2)}, u32[]{:S(2)}) collective-permute-start(bf16[64,1792]{1,0:T(8,128)(2,1)S(1)} %get-tuple-element.112), channel_id=1, source_target_pairs={{0,8},{2,10},{4,12},{6,14},{8,0},{10,2},{12,4},{14,6},{1,9},{3,11}... | collective-permute-start | bytes 688136 | tf_op jit(solution)/shard_map/ppermute | solution.py:36
  78.8 6.9 %collective-permute-start.22 = (bf16[64,512]{1,0:T(8,128)(2,1)S(1)}, bf16[64,512]{1,0:T(8,128)(2,1)S(1)}, u32[]{:S(2)}, u32[]{:S(2)}) collective-permute-start(bf16[64,512]{1,0:T(8,128)(2,1)S(1)} %get-tuple-element.115), channel_id=1, source_target_pairs={{0,2},{2,0},{4,6},{6,4},{8,10},{10,8},{12,14},{14,12},{1,3},{3,1},... | collective-permute-start | bytes 196616 | tf_op jit(solution)/shard_map/ppermute | solution.py:36
  79.1 6.6 %collective-permute-start.23 = (bf16[64,512]{1,0:T(8,128)(2,1)S(1)}, bf16[64,512]{1,0:T(8,128)(2,1)S(1)}, u32[]{:S(2)}, u32[]{:S(2)}) collective-permute-start(bf16[64,512]{1,0:T(8,128)(2,1)S(1)} %get-tuple-element.116), channel_id=1, source_target_pairs={{0,4},{2,6},{4,0},{6,2},{8,12},{10,14},{12,8},{14,10},{1,5},{3,7},... | collective-permute-start | bytes 196616 | tf_op jit(solution)/shard_map/ppermute | solution.py:36
  80.2 5.5 %collective-permute-start.24 = (bf16[64,512]{1,0:T(8,128)(2,1)S(1)}, bf16[64,512]{1,0:T(8,128)(2,1)S(1)}, u32[]{:S(2)}, u32[]{:S(2)}) collective-permute-start(bf16[64,512]{1,0:T(8,128)(2,1)S(1)} %get-tuple-element.117), channel_id=1, source_target_pairs={{0,6},{2,4},{4,2},{6,0},{8,14},{10,12},{12,10},{14,8},{1,7},{3,5},... | collective-permute-start | bytes 196616 | tf_op jit(solution)/shard_map/ppermute | solution.py:36
  86.6 7.9 %collective-permute-start.26 = (bf16[64,512]{1,0:T(8,128)(2,1)S(1)}, bf16[64,512]{1,0:T(8,128)(2,1)S(1)}, u32[]{:S(2)}, u32[]{:S(2)}) collective-permute-start(bf16[64,512]{1,0:T(8,128)(2,1)S(1)} %get-tuple-element.118), channel_id=1, source_target_pairs={{0,8},{2,10},{4,12},{6,14},{8,0},{10,2},{12,4},{14,6},{1,9},{3,11}... | collective-permute-start | bytes 196616 | tf_op jit(solution)/shard_map/ppermute | solution.py:36

commit v16 on v14

--- a/solution.py
+++ b/solution.py
@@ -492,7 +492,7 @@
     far_a = to_far(dense_a)
 
     (high,) = through(_tie(info, dense_a[1]), half, width - half, 0)
-    gate = [high] + ([got_y] if shared else [])
+    gate = [high] + ([got_y, got_x, got_d] if shared else [])
     got_b = to_near(
         [_tie(b, *gate) if k in (1, 3) else _tie(b, dense_a[1]) for k, b in enumerate(sends_b)]
     )

time: 95.6 us -> 98.7 us (1.032)
  waiting for transfers between devices: 8.58 us -> 14.5 us
  starting transfers between devices: 34.7 us -> 31.9 us
    ppermute x20, waiting for transfers between devices: 7.52 us -> 13.5 us  [_xor(): return lax.ppermute(x, 'dp', [(i, i ^ k) for i in range(n)])]
    ppermute x20, starting transfers between devices: 30.8 us -> 27 us  [_xor(): return lax.ppermute(x, 'dp', [(i, i ^ k) for i in range(n)])]
    ppermute x1, starting transfers between devices: 0.6 us -> 1.8 us  [on_device(): lax.ppermute(_tie(chosen[3], sends_b[0]), ('groups', 'dp'), [(g * n_dp +...]
  transfers between devices with their start and end apart: 27 -> 27, of which waited for: 6 -> 8; matrix products, arithmetic and copies ran while one was open for 4% -> 4% of each run, Pallas kernels for 46% -> 44%
where the time goes in v16:
time: 98.7 us; the launch traced here: 98.5 us
  Pallas kernels  46.2 us (47%)
  starting transfers between devices  31.9 us (32%)
  waiting for transfers between devices  14.5 us (15%)
  other arithmetic  2.63 us (3%)
  local copies, waits for them, and re-layouts  2.33 us (2%)
    ppermute x20, starting transfers between devices, _xor(): return lax.ppermute(x, 'dp', [(i, i ^ k) for i in range(n)])  27 us
    ppermute x20, waiting for transfers between devices, _xor(): return lax.ppermute(x, 'dp', [(i, i ^ k) for i in range(n)])  13.5 us
    pallas_call x2, Pallas kernels, through(): _call(functools.partial(through_kernel, z, first), 'through', (1,), [VMEM...  9.57 us
    pallas_call x1, Pallas kernels, on_device(): _call(functools.partial(base_kernel, z), 'base', (1,), [pl.BlockSpec(memo...  7.78 us
    pallas_call x2, Pallas kernels, token_grads(): _call(functools.partial(tokens_kernel, z, first), 'token_grads', (steps,)...  7.73 us
    pallas_call x1, Pallas kernels, on_device(): _call(functools.partial(own_kernel, z), 'base_own', (1,), [VMEM] * 3, VME...  4.61 us
    pallas_call x2, Pallas kernels, pack(): _call(functools.partial(pack_kernel, z, NEAR, start), 'pack_down', (1,),...  3.96 us
    ppermute x6, starting transfers between devices, _swap(): return lax.ppermute(x, axis, [(0, 1), (1, 0)])  3.11 us
  transfers between devices with their start and end apart: 27, of which 8 were waited for; matrix products, arithmetic and copies ran while one was open for 4% of the time, Pallas kernels for 44%

profile of v16, /device:TPU:0, one launch (start us, length us, event | category | flops | bytes accessed | tf_op | source)
XLA Modules:
  0.0 98.5 jit_solution(8273397157539055606)
XLA Ops:
  0.6 4.1 %collective-permute-start = (bf16[4,16,512]{2,1,0:T(8,128)(2,1)}, bf16[4,16,512]{2,1,0:T(8,128)(2,1)S(1)}, u32[]{:S(2)}, u32[]{:S(2)}) collective-permute-start(bf16[4,16,512]{2,1,0:T(8,128)(2,1)} %param.11), channel_id=1, source_target_pairs={{0,8},{2,10},{4,12},{6,14},{8,0},{10,2},{12,4},{14,6},{1,9},{3,11}... | collective-permute-start | bytes 196616 | tf_op jit(solution)/shard_map/ppermute | solution.py:36
  5.7 1.6 %collective-permute-start.2 = (bf16[4,16,1024]{2,1,0:T(8,128)(2,1)S(1)}, bf16[4,16,1024]{2,1,0:T(8,128)(2,1)S(1)}, u32[]{:S(2)}, u32[]{:S(2)}) collective-permute-start(bf16[4,16,1024]{2,1,0:T(8,128)(2,1)S(1)} %get-tuple-element.127), channel_id=1, source_target_pairs={{0,2},{2,0},{4,6},{6,4},{8,10},{10,8},{12,14},{14,12},{1,3},{3,1},... | collective-permute-start | bytes 393224 | tf_op jit(solution)/shard_map/ppermute | solution.py:36
  8.9 1.8 %collective-permute-done.2 = bf16[4,16,1024]{2,1,0:T(8,128)(2,1)S(1)} collective-permute-done((bf16[4,16,1024]{2,1,0:T(8,128)(2,1)S(1)}, bf16[4,16,1024]{2,1,0:T(8,128)(2,1)S(1)}, u32[]{:S(2)}, u32[]{:S(2)}) %collective-permute-start.2) | collective-permute-done | bytes 131104 | tf_op jit(solution)/shard_map/ppermute | solution.py:36
  12.0 1.6 %collective-permute-start.5 = (bf16[144,512]{1,0:T(8,128)(2,1)S(1)}, bf16[144,512]{1,0:T(8,128)(2,1)S(1)}, u32[]{:S(2)}, u32[]{:S(2)}) collective-permute-start(bf16[144,512]{1,0:T(8,128)(2,1)S(1)} %pad_maximum_fusion.2.refs_0_), channel_id=1, source_target_pairs={{0,2},{2,0},{4,6},{6,4},{8,10},{10,8},{12,14},{14,12},{1,3},{3,1},... | collective-permute-start | bytes 442376 | tf_op jit(solution)/shard_map/ppermute | solution.py:36
  13.6 1.6 %collective-permute-start.4 = (bf16[144,512]{1,0:T(8,128)(2,1)S(1)}, bf16[144,512]{1,0:T(8,128)(2,1)S(1)}, u32[]{:S(2)}, u32[]{:S(2)}) collective-permute-start(bf16[144,512]{1,0:T(8,128)(2,1)S(1)} %pad_maximum_fusion.2.refs_0_), channel_id=1, source_target_pairs={{0,4},{2,6},{4,0},{6,2},{8,12},{10,14},{12,8},{14,10},{1,5},{3,7},... | collective-permute-start | bytes 442376 | tf_op jit(solution)/shard_map/ppermute | solution.py:36
  15.6 1.3 %copy-done = bf16[896,512]{1,0:T(8,128)(2,1)S(1)} copy-done((bf16[896,512]{1,0:T(8,128)(2,1)S(1)}, bf16[896,512]{1,0:T(8,128)(2,1)}, u32[]{:S(2)}) %copy-start) | copy-done | bytes 917528
  17.0 7.8 %base.1 = (bf16[896,512]{1,0:T(8,128)(2,1)S(1)}, bf16[896,1024]{1,0:T(8,128)(2,1)S(1)}, bf16[896,4096]{1,0:T(8,128)(2,1)S(1)}) custom-call(s32[16,128]{1,0:T(8,128)S(1)} %select_select_fusion.1.info, bf16[896,4096]{1,0:T(8,128)(2,1)} %x_hbm.1, bf16[4096,1024]{1,0:T(8,128)(2,1)} %w_ref.5, bf16[896,512]{1,0:T(8,128)(2,1)S(1)} %copy-done, ...), custom_call_target="tpu_custom_call" | custom-call | flops 1 | bytes 1 | tf_op jit(solution)/shard_map/base/pallas_call | solution.py:388
  29.0 2.1 %pack_down.2 = (bf16[64,2304]{1,0:T(8,128)(2,1)S(1)}, bf16[64,2304]{1,0:T(8,128)(2,1)S(1)}, bf16[64,2304]{1,0:T(8,128)(2,1)S(1)}, bf16[64,2304]{1,0:T(8,128)(2,1)S(1)}) custom-call(s32[16,128]{1,0:T(8,128)S(1)} %select_select_fusion.info, f32[16,896]{1,0:T(8,128)S(1)} %get-tuple-element.75.mine_ref, f32[16,896]{1,0:T(8,128)S(1)} %collective-permute-done.8.other_ref, ...), custom_call_target="tpu_custom_call" | custom-call | flops 1 | bytes 1 | tf_op jit(solution)/shard_map/pack_down/pallas_call | solution.py:431
  31.1 1.3 %collective-permute-start.12 = (bf16[64,2304]{1,0:T(8,128)(2,1)S(1)}, bf16[64,2304]{1,0:T(8,128)(2,1)S(1)}, u32[]{:S(2)}, u32[]{:S(2)}) collective-permute-start(bf16[64,2304]{1,0:T(8,128)(2,1)S(1)} %get-tuple-element.88), channel_id=1, source_target_pairs={{0,4},{2,6},{4,0},{6,2},{8,12},{10,14},{12,8},{14,10},{1,5},{3,7},... | collective-permute-start | bytes 884744 | tf_op jit(solution)/shard_map/ppermute | solution.py:36
  32.4 1.1 %collective-permute-start.11 = (bf16[64,2304]{1,0:T(8,128)(2,1)S(1)}, bf16[64,2304]{1,0:T(8,128)(2,1)S(1)}, u32[]{:S(2)}, u32[]{:S(2)}) collective-permute-start(bf16[64,2304]{1,0:T(8,128)(2,1)S(1)} %get-tuple-element.87), channel_id=1, source_target_pairs={{0,2},{2,0},{4,6},{6,4},{8,10},{10,8},{12,14},{14,12},{1,3},{3,1},... | collective-permute-start | bytes 884744 | tf_op jit(solution)/shard_map/ppermute | solution.py:36
  33.4 1.2 %collective-permute-start.13 = (bf16[64,2304]{1,0:T(8,128)(2,1)S(1)}, bf16[64,2304]{1,0:T(8,128)(2,1)S(1)}, u32[]{:S(2)}, u32[]{:S(2)}) collective-permute-start(bf16[64,2304]{1,0:T(8,128)(2,1)S(1)} %get-tuple-element.89), channel_id=1, source_target_pairs={{0,6},{2,4},{4,2},{6,0},{8,14},{10,12},{12,10},{14,8},{1,7},{3,5},... | collective-permute-start | bytes 884744 | tf_op jit(solution)/shard_map/ppermute | solution.py:36
  34.6 1.5 %collective-permute-start.9 = (s32[16,128]{1,0:T(8,128)S(1)}, s32[16,128]{1,0:T(8,128)S(1)}, u32[]{:S(2)}, u32[]{:S(2)}) collective-permute-start(s32[16,128]{1,0:T(8,128)S(1)} %select_select_fusion.info), channel_id=1, source_target_pairs={{0,16},{16,0},{1,17},{17,1},{2,18},{18,2},{3,19},{19,3},{4,20},{20... | collective-permute-start | bytes 24584 | tf_op jit(solution)/shard_map/ppermute | solution.py:32
  36.1 4.7 %through.2 = (f32[896,2048]{1,0:T(8,128)S(1)}, bf16[2,64,128]{2,1,0:T(8,128)(2,1)S(1)}) custom-call(s32[16,128]{1,0:T(8,128)S(1)} %select_select_fusion.info, bf16[896,1024]{1,0:T(8,128)(2,1)S(1)} %get-tuple-element.73.g_ref, bf16[4096,1024]{1,0:T(8,128)(2,1)S(1)} %bitcast.20), custom_call_target="tpu_custom_call" | custom-call | flops 1 | bytes 1 | tf_op jit(solution)/shard_map/through/pallas_call | solution.py:455
  41.9 1.8 %pack_down.3 = (bf16[64,1792]{1,0:T(8,128)(2,1)S(1)}, bf16[64,1792]{1,0:T(8,128)(2,1)S(1)}, bf16[64,1792]{1,0:T(8,128)(2,1)S(1)}, bf16[64,1792]{1,0:T(8,128)(2,1)S(1)}) custom-call(s32[16,128]{1,0:T(8,128)S(1)} %select_select_fusion.info, f32[16,896]{1,0:T(8,128)S(1)} %get-tuple-element.75.mine_ref, f32[16,896]{1,0:T(8,128)S(1)} %collective-permute-done.8.other_ref, ...), custom_call_target="tpu_custom_call" | custom-call | flops 1 | bytes 1 | tf_op jit(solution)/shard_map/pack_down/pallas_call | solution.py:431
  43.8 1.2 %collective-permute-start.15 = (bf16[112,1024]{1,0:T(8,128)(2,1)S(1)}, bf16[112,1024]{1,0:T(8,128)(2,1)S(1)}, u32[]{:S(2)}, u32[]{:S(2)}) collective-permute-start(bf16[112,1024]{1,0:T(8,128)(2,1)S(1)} %get-tuple-element.96), channel_id=1, source_target_pairs={{0,16},{16,0},{1,17},{17,1},{2,18},{18,2},{3,19},{19,3},{4,20},{20... | collective-permute-start | bytes 688136 | tf_op jit(solution)/shard_map/ppermute | solution.py:32
  45.0 1.8 %collective-permute-start.16 = (bf16[112,1024]{1,0:T(8,128)(2,1)S(1)}, bf16[112,1024]{1,0:T(8,128)(2,1)S(1)}, u32[]{:S(2)}, u32[]{:S(2)}) collective-permute-start(bf16[112,1024]{1,0:T(8,128)(2,1)S(1)} %get-tuple-element.98), channel_id=1, source_target_pairs={{0,18},{2,16},{4,22},{6,20},{8,26},{10,24},{12,30},{14,28},{16,2},... | collective-permute-start | bytes 688136 | tf_op jit(solution)/shard_map/ppermute | solution.py:476
  47.9 4.6 %base_own.1.base_ref = f32[896,512]{1,0:T(8,128)S(1)} custom-call(s32[16,128]{1,0:T(8,128)S(1)} %select_select_fusion.info, bf16[896,4096]{1,0:T(8,128)(2,1)S(1)} %get-tuple-element.76.x_ref, bf16[4096,1024]{1,0:T(8,128)(2,1)S(1)} %bitcast.20, bf16[896,512]{1,0:T(8,128)(2,1)S(1)} %collective-permute-done.7.far_ref), custom_call_target="tpu_custom_call" | custom-call | flops 1 | bytes 1 | tf_op jit(solution)/shard_map/base_own/pallas_call | solution.py:487
  52.5 3.2 %collective-permute-done.13.refs_3_ = bf16[64,2304]{1,0:T(8,128)(2,1)S(1)} collective-permute-done((bf16[64,2304]{1,0:T(8,128)(2,1)S(1)}, bf16[64,2304]{1,0:T(8,128)(2,1)S(1)}, u32[]{:S(2)}, u32[]{:S(2)}) %collective-permute-start.13) | collective-permute-done | bytes 294944 | tf_op jit(solution)/shard_map/ppermute | solution.py:36
  56.7 1.7 %collective-permute-start.17 = (bf16[64,2304]{1,0:T(8,128)(2,1)S(1)}, bf16[64,2304]{1,0:T(8,128)(2,1)S(1)}, u32[]{:S(2)}, u32[]{:S(2)}) collective-permute-start(bf16[64,2304]{1,0:T(8,128)(2,1)S(1)} %get-tuple-element.90), channel_id=1, source_target_pairs={{0,8},{2,10},{4,12},{6,14},{8,0},{10,2},{12,4},{14,6},{1,9},{3,11}... | collective-permute-start | bytes 884744 | tf_op jit(solution)/shard_map/ppermute | solution.py:36
  58.4 2.9 %collective-permute-start.20 = (bf16[64,1792]{1,0:T(8,128)(2,1)S(1)}, bf16[64,1792]{1,0:T(8,128)(2,1)S(1)}, u32[]{:S(2)}, u32[]{:S(2)}) collective-permute-start(bf16[64,1792]{1,0:T(8,128)(2,1)S(1)} %get-tuple-element.109), channel_id=1, source_target_pairs={{0,4},{2,6},{4,0},{6,2},{8,12},{10,14},{12,8},{14,10},{1,5},{3,7},... | collective-permute-start | bytes 688136 | tf_op jit(solution)/shard_map/ppermute | solution.py:36
  61.3 4.8 %through.3.through_ref = f32[896,2048]{1,0:T(8,128)S(1)} custom-call(s32[16,128]{1,0:T(8,128)S(1)} %select_select_fusion.info, bf16[896,1024]{1,0:T(8,128)(2,1)S(1)} %get-tuple-element.73.g_ref, bf16[4096,1024]{1,0:T(8,128)(2,1)S(1)} %bitcast.20), custom_call_target="tpu_custom_call" | custom-call | flops 1 | bytes 1 | tf_op jit(solution)/shard_map/through/pallas_call | solution.py:455
  67.7 2.8 %shrink.1 = (bf16[112,4096]{1,0:T(8,128)(2,1)S(1)}, f32[16,896]{1,0:T(8,128)S(1)}) custom-call(s32[16,128]{1,0:T(8,128)S(1)} %select_select_fusion.info, bf16[896,4096]{1,0:T(8,128)(2,1)S(1)} %get-tuple-element.76.x_ref, bf16[112,1024]{1,0:T(8,128)(2,1)S(1)} %get-tuple-element.81.refs_0_, bf16[112,1024]{1,0:T(8,128)(2,1)S(1)} %collective-permute-done.14.refs_1_, ...), custom_call_target="tpu_custom_call" | custom-call | flops 1 | bytes 1 | tf_op jit(solution)/shard_map/shrink/pallas_call | solution.py:502
  70.6 3.9 %token_grads.2.refs_0_ = bf16[896,4096]{1,0:T(8,128)(2,1)} custom-call(s32[16,128]{1,0:T(8,128)S(1)} %select_select_fusion.info, f32[896,2048]{1,0:T(8,128)S(1)} %get-tuple-element.79.through_ref, f32[16,896]{1,0:T(8,128)S(1)} %get-tuple-element.75.mine_ref, f32[16,896]{1,0:T(8,128)S(1)} %collective-permute-done.8.other_ref, ...), custom_call_target="tpu_custom_call" | custom-call | flops 1 | bytes 1 | tf_op jit(solution)/shard_map/token_grads/pallas_call | solution.py:514
  74.5 1.1 %pack_up.1 = (bf16[64,512]{1,0:T(8,128)(2,1)S(1)}, bf16[64,512]{1,0:T(8,128)(2,1)S(1)}, bf16[64,512]{1,0:T(8,128)(2,1)S(1)}, bf16[64,512]{1,0:T(8,128)(2,1)S(1)}) custom-call(s32[16,128]{1,0:T(8,128)S(1)} %select_select_fusion.info, f32[16,896]{1,0:T(8,128)S(1)} %get-tuple-element.99.mine_ref, f32[16,896]{1,0:T(8,128)S(1)} %collective-permute-done.18.other_ref, ...), custom_call_target="tpu_custom_call" | custom-call | flops 1 | bytes 1 | tf_op jit(solution)/shard_map/pack_up/pallas_call | solution.py:524
  76.8 2.2 %collective-permute-start.25 = (bf16[64,1792]{1,0:T(8,128)(2,1)S(1)}, bf16[64,1792]{1,0:T(8,128)(2,1)S(1)}, u32[]{:S(2)}, u32[]{:S(2)}) collective-permute-start(bf16[64,1792]{1,0:T(8,128)(2,1)S(1)} %get-tuple-element.112), channel_id=1, source_target_pairs={{0,8},{2,10},{4,12},{6,14},{8,0},{10,2},{12,4},{14,6},{1,9},{3,11}... | collective-permute-start | bytes 688136 | tf_op jit(solution)/shard_map/ppermute | solution.py:36
  79.0 1.4 %collective-permute-start.22 = (bf16[64,512]{1,0:T(8,128)(2,1)S(1)}, bf16[64,512]{1,0:T(8,128)(2,1)S(1)}, u32[]{:S(2)}, u32[]{:S(2)}) collective-permute-start(bf16[64,512]{1,0:T(8,128)(2,1)S(1)} %get-tuple-element.115), channel_id=1, source_target_pairs={{0,2},{2,0},{4,6},{6,4},{8,10},{10,8},{12,14},{14,12},{1,3},{3,1},... | collective-permute-start | bytes 196616 | tf_op jit(solution)/shard_map/ppermute | solution.py:36
  80.4 1.6 %collective-permute-start.23 = (bf16[64,512]{1,0:T(8,128)(2,1)S(1)}, bf16[64,512]{1,0:T(8,128)(2,1)S(1)}, u32[]{:S(2)}, u32[]{:S(2)}) collective-permute-start(bf16[64,512]{1,0:T(8,128)(2,1)S(1)} %get-tuple-element.116), channel_id=1, source_target_pairs={{0,4},{2,6},{4,0},{6,2},{8,12},{10,14},{12,8},{14,10},{1,5},{3,7},... | collective-permute-start | bytes 196616 | tf_op jit(solution)/shard_map/ppermute | solution.py:36
  82.5 3.9 %token_grads.3 = bf16[896,4096]{1,0:T(8,128)(2,1)} custom-call(s32[16,128]{1,0:T(8,128)S(1)} %select_select_fusion.info, f32[896,2048]{1,0:T(8,128)S(1)} %through.3.through_ref, f32[16,896]{1,0:T(8,128)S(1)} %get-tuple-element.75.mine_ref, f32[16,896]{1,0:T(8,128)S(1)} %collective-permute-done.8.other_ref, ...), custom_call_target="tpu_custom_call", output_to_operand_aliasing={{}: (5, {})} | custom-call | flops 1 | bytes 1 | tf_op jit(solution)/shard_map/token_grads/pallas_call | solution.py:514
  86.4 4.2 %collective-permute-done.24.refs_3_ = bf16[64,512]{1,0:T(8,128)(2,1)S(1)} collective-permute-done((bf16[64,512]{1,0:T(8,128)(2,1)S(1)}, bf16[64,512]{1,0:T(8,128)(2,1)S(1)}, u32[]{:S(2)}, u32[]{:S(2)}) %collective-permute-start.24) | collective-permute-done | bytes 65568 | tf_op jit(solution)/shard_map/ppermute | solution.py:36
  91.5 2.0 %projected.1 = bf16[896,512]{1,0:T(8,128)(2,1)} custom-call(s32[16,128]{1,0:T(8,128)S(1)} %select_select_fusion.info, f32[896,512]{1,0:T(8,128)S(1)} %base_own.1.base_ref, f32[16,896]{1,0:T(8,128)S(1)} %get-tuple-element.99.mine_ref, f32[16,896]{1,0:T(8,128)S(1)} %collective-permute-done.18.other_ref, bf16[112,512]{1,0:T(8,128)(2,1)S(1)} %get-tuple-element.120.up_ref), custom_call_target="tpu_custom_call" | custom-call | flops 1 | bytes 1 | tf_op jit(solution)/shard_map/projected/pallas_call | solution.py:539
  93.6 3.1 %collective-permute-done.26.refs_5_ = bf16[64,512]{1,0:T(8,128)(2,1)S(1)} collective-permute-done((bf16[64,512]{1,0:T(8,128)(2,1)S(1)}, bf16[64,512]{1,0:T(8,128)(2,1)S(1)}, u32[]{:S(2)}, u32[]{:S(2)}) %collective-permute-start.26) | collective-permute-done | bytes 65568 | tf_op jit(solution)/shard_map/ppermute | solution.py:36
  96.7 1.8 %final.1 = (f32[64,4096]{1,0:T(8,128)}, f32[64,512]{1,0:T(8,128)}) custom-call(s32[16,128]{1,0:T(8,128)S(1)} %select_select_fusion.info, f32[64,2304]{1,0:T(8,128)S(1)} %get-tuple-element.121.refs_0_, bf16[64,2304]{1,0:T(8,128)(2,1)S(1)} %collective-permute-done.17.refs_1_, f32[64,1792]{1,0:T(8,128)S(1)} %get-tuple-element.122.refs_2_, ...), custom_call_target="tpu_custom_call" | custom-call | flops 1 | bytes 1 | tf_op jit(solution)/shard_map/final/pallas_call | solution.py:549
  (65 shorter events, 15.7 us)
Async XLA Ops:
  0.6 10.5 %collective-permute-start = (bf16[4,16,512]{2,1,0:T(8,128)(2,1)}, bf16[4,16,512]{2,1,0:T(8,128)(2,1)S(1)}, u32[]{:S(2)}, u32[]{:S(2)}) collective-permute-start(bf16[4,16,512]{2,1,0:T(8,128)(2,1)} %param.11), channel_id=1, source_target_pairs={{0,8},{2,10},{4,12},{6,14},{8,0},{10,2},{12,4},{14,6},{1,9},{3,11}... | collective-permute-start | bytes 196616 | tf_op jit(solution)/shard_map/ppermute | solution.py:36
  5.7 5.0 %collective-permute-start.2 = (bf16[4,16,1024]{2,1,0:T(8,128)(2,1)S(1)}, bf16[4,16,1024]{2,1,0:T(8,128)(2,1)S(1)}, u32[]{:S(2)}, u32[]{:S(2)}) collective-permute-start(bf16[4,16,1024]{2,1,0:T(8,128)(2,1)S(1)} %get-tuple-element.127), channel_id=1, source_target_pairs={{0,2},{2,0},{4,6},{6,4},{8,10},{10,8},{12,14},{14,12},{1,3},{3,1},... | collective-permute-start | bytes 393224 | tf_op jit(solution)/shard_map/ppermute | solution.py:36
  7.3 8.3 %collective-permute-start.3 = (bf16[896,512]{1,0:T(8,128)(2,1)}, bf16[896,512]{1,0:T(8,128)(2,1)S(1)}, u32[]{:S(2)}, u32[]{:S(2)}) collective-permute-start(bf16[896,512]{1,0:T(8,128)(2,1)} %g_hbm.1), channel_id=1, source_target_pairs={{0,1},{1,0},{2,3},{3,2},{4,5},{5,4},{6,7},{7,6},{8,9},{9,8},{10,11... | collective-permute-start | bytes 2752520 | tf_op jit(solution)/shard_map/ppermute | solution.py:32
  10.8 14.0 %collective-permute-start.6 = (bf16[8,16,1024]{2,1,0:T(8,128)(2,1)S(1)}, bf16[8,16,1024]{2,1,0:T(8,128)(2,1)S(1)}, u32[]{:S(2)}, u32[]{:S(2)}) collective-permute-start(bf16[8,16,1024]{2,1,0:T(8,128)(2,1)S(1)} %pad_maximum_fusion.1.own_ref), channel_id=1, source_target_pairs={{0,8},{2,10},{4,12},{6,14},{8,0},{10,2},{12,4},{14,6},{1,9},{3,11}... | collective-permute-start | bytes 786440 | tf_op jit(solution)/shard_map/ppermute | solution.py:36
  12.0 12.8 %collective-permute-start.5 = (bf16[144,512]{1,0:T(8,128)(2,1)S(1)}, bf16[144,512]{1,0:T(8,128)(2,1)S(1)}, u32[]{:S(2)}, u32[]{:S(2)}) collective-permute-start(bf16[144,512]{1,0:T(8,128)(2,1)S(1)} %pad_maximum_fusion.2.refs_0_), channel_id=1, source_target_pairs={{0,2},{2,0},{4,6},{6,4},{8,10},{10,8},{12,14},{14,12},{1,3},{3,1},... | collective-permute-start | bytes 442376 | tf_op jit(solution)/shard_map/ppermute | solution.py:36
  13.6 11.2 %collective-permute-start.4 = (bf16[144,512]{1,0:T(8,128)(2,1)S(1)}, bf16[144,512]{1,0:T(8,128)(2,1)S(1)}, u32[]{:S(2)}, u32[]{:S(2)}) collective-permute-start(bf16[144,512]{1,0:T(8,128)(2,1)S(1)} %pad_maximum_fusion.2.refs_0_), channel_id=1, source_target_pairs={{0,4},{2,6},{4,0},{6,2},{8,12},{10,14},{12,8},{14,10},{1,5},{3,7},... | collective-permute-start | bytes 442376 | tf_op jit(solution)/shard_map/ppermute | solution.py:36
  15.2 10.4 %collective-permute-start.1 = (bf16[144,512]{1,0:T(8,128)(2,1)S(1)}, bf16[144,512]{1,0:T(8,128)(2,1)S(1)}, u32[]{:S(2)}, u32[]{:S(2)}) collective-permute-start(bf16[144,512]{1,0:T(8,128)(2,1)S(1)} %pad_maximum_fusion.2.refs_0_), channel_id=1, source_target_pairs={{0,6},{2,4},{4,2},{6,0},{8,14},{10,12},{12,10},{14,8},{1,7},{3,5},... | collective-permute-start | bytes 442376 | tf_op jit(solution)/shard_map/ppermute | solution.py:36
  15.6 20.5 %slice-start = ((s8[8388608]{0:T(1024)(128)(4,1)}), s8[4194304]{0:T(1024)(128)(4,1)S(1)}, s32[]{:S(2)}) async-start(s8[8388608]{0:T(1024)(128)(4,1)} %bitcast.19), calls=%async_computation | async-start | bytes 8388608
  15.6 20.5 %slice-start.1 = ((s8[8388608]{0:T(1024)(128)(4,1)}), s8[4194304]{0:T(1024)(128)(4,1)S(1)}, s32[]{:S(2)}) async-start(s8[8388608]{0:T(1024)(128)(4,1)} %bitcast.19), calls=%async_computation.1 | async-start | bytes 8388608
  15.6 1.3 %copy-start = (bf16[896,512]{1,0:T(8,128)(2,1)S(1)}, bf16[896,512]{1,0:T(8,128)(2,1)}, u32[]{:S(2)}) copy-start(bf16[896,512]{1,0:T(8,128)(2,1)} %g_hbm.1) | copy-start | bytes 2752516
  24.7 3.2 %collective-permute-start.7 = (bf16[896,512]{1,0:T(8,128)(2,1)S(1)}, bf16[896,512]{1,0:T(8,128)(2,1)S(1)}, u32[]{:S(2)}, u32[]{:S(2)}) collective-permute-start(bf16[896,512]{1,0:T(8,128)(2,1)S(1)} %get-tuple-element.66), channel_id=1, source_target_pairs={{0,1},{1,0},{2,3},{3,2},{4,5},{5,4},{6,7},{7,6},{8,9},{9,8},{10,11... | collective-permute-start | bytes 2752520 | tf_op jit(solution)/shard_map/ppermute | solution.py:32
  25.7 15.2 %collective-permute-start.10 = (bf16[16,16,1024]{2,1,0:T(8,128)(2,1)S(1)}, bf16[16,16,1024]{2,1,0:T(8,128)(2,1)S(1)}, u32[]{:S(2)}, u32[]{:S(2)}) collective-permute-start(bf16[16,16,1024]{2,1,0:T(8,128)(2,1)S(1)} %pad_maximum_fusion), channel_id=1, source_target_pairs={{0,4},{2,6},{4,0},{6,2},{8,12},{10,14},{12,8},{14,10},{1,5},{3,7},... | collective-permute-start | bytes 1572872 | tf_op jit(solution)/shard_map/ppermute | solution.py:36
  27.7 1.3 %collective-permute-start.8 = (f32[16,896]{1,0:T(8,128)S(1)}, f32[16,896]{1,0:T(8,128)S(1)}, u32[]{:S(2)}, u32[]{:S(2)}) collective-permute-start(f32[16,896]{1,0:T(8,128)S(1)} %get-tuple-element.75.mine_ref), channel_id=1, source_target_pairs={{0,1},{1,0},{2,3},{3,2},{4,5},{5,4},{6,7},{7,6},{8,9},{9,8},{10,11... | collective-permute-start | bytes 172040 | tf_op jit(solution)/shard_map/ppermute | solution.py:32
  31.1 15.8 %collective-permute-start.12 = (bf16[64,2304]{1,0:T(8,128)(2,1)S(1)}, bf16[64,2304]{1,0:T(8,128)(2,1)S(1)}, u32[]{:S(2)}, u32[]{:S(2)}) collective-permute-start(bf16[64,2304]{1,0:T(8,128)(2,1)S(1)} %get-tuple-element.88), channel_id=1, source_target_pairs={{0,4},{2,6},{4,0},{6,2},{8,12},{10,14},{12,8},{14,10},{1,5},{3,7},... | collective-permute-start | bytes 884744 | tf_op jit(solution)/shard_map/ppermute | solution.py:36
  32.4 20.2 %collective-permute-start.11 = (bf16[64,2304]{1,0:T(8,128)(2,1)S(1)}, bf16[64,2304]{1,0:T(8,128)(2,1)S(1)}, u32[]{:S(2)}, u32[]{:S(2)}) collective-permute-start(bf16[64,2304]{1,0:T(8,128)(2,1)S(1)} %get-tuple-element.87), channel_id=1, source_target_pairs={{0,2},{2,0},{4,6},{6,4},{8,10},{10,8},{12,14},{14,12},{1,3},{3,1},... | collective-permute-start | bytes 884744 | tf_op jit(solution)/shard_map/ppermute | solution.py:36
  33.4 22.3 %collective-permute-start.13 = (bf16[64,2304]{1,0:T(8,128)(2,1)S(1)}, bf16[64,2304]{1,0:T(8,128)(2,1)S(1)}, u32[]{:S(2)}, u32[]{:S(2)}) collective-permute-start(bf16[64,2304]{1,0:T(8,128)(2,1)S(1)} %get-tuple-element.89), channel_id=1, source_target_pairs={{0,6},{2,4},{4,2},{6,0},{8,14},{10,12},{12,10},{14,8},{1,7},{3,5},... | collective-permute-start | bytes 884744 | tf_op jit(solution)/shard_map/ppermute | solution.py:36
  34.6 6.2 %collective-permute-start.9 = (s32[16,128]{1,0:T(8,128)S(1)}, s32[16,128]{1,0:T(8,128)S(1)}, u32[]{:S(2)}, u32[]{:S(2)}) collective-permute-start(s32[16,128]{1,0:T(8,128)S(1)} %select_select_fusion.info), channel_id=1, source_target_pairs={{0,16},{16,0},{1,17},{17,1},{2,18},{18,2},{3,19},{19,3},{4,20},{20... | collective-permute-start | bytes 24584 | tf_op jit(solution)/shard_map/ppermute | solution.py:32
  43.8 22.4 %collective-permute-start.15 = (bf16[112,1024]{1,0:T(8,128)(2,1)S(1)}, bf16[112,1024]{1,0:T(8,128)(2,1)S(1)}, u32[]{:S(2)}, u32[]{:S(2)}) collective-permute-start(bf16[112,1024]{1,0:T(8,128)(2,1)S(1)} %get-tuple-element.96), channel_id=1, source_target_pairs={{0,16},{16,0},{1,17},{17,1},{2,18},{18,2},{3,19},{19,3},{4,20},{20... | collective-permute-start | bytes 688136 | tf_op jit(solution)/shard_map/ppermute | solution.py:32
  45.0 21.1 %collective-permute-start.16 = (bf16[112,1024]{1,0:T(8,128)(2,1)S(1)}, bf16[112,1024]{1,0:T(8,128)(2,1)S(1)}, u32[]{:S(2)}, u32[]{:S(2)}) collective-permute-start(bf16[112,1024]{1,0:T(8,128)(2,1)S(1)} %get-tuple-element.98), channel_id=1, source_target_pairs={{0,18},{2,16},{4,22},{6,20},{8,26},{10,24},{12,30},{14,28},{16,2},... | collective-permute-start | bytes 688136 | tf_op jit(solution)/shard_map/ppermute | solution.py:476
  46.9 19.3 %collective-permute-start.14 = (bf16[112,1024]{1,0:T(8,128)(2,1)S(1)}, bf16[112,1024]{1,0:T(8,128)(2,1)S(1)}, u32[]{:S(2)}, u32[]{:S(2)}) collective-permute-start(bf16[112,1024]{1,0:T(8,128)(2,1)S(1)} %get-tuple-element.94), channel_id=1, source_target_pairs={{0,2},{2,0},{4,6},{6,4},{8,10},{10,8},{12,14},{14,12},{1,3},{3,1},... | collective-permute-start | bytes 688136 | tf_op jit(solution)/shard_map/ppermute | solution.py:36
  56.7 17.8 %collective-permute-start.17 = (bf16[64,2304]{1,0:T(8,128)(2,1)S(1)}, bf16[64,2304]{1,0:T(8,128)(2,1)S(1)}, u32[]{:S(2)}, u32[]{:S(2)}) collective-permute-start(bf16[64,2304]{1,0:T(8,128)(2,1)S(1)} %get-tuple-element.90), channel_id=1, source_target_pairs={{0,8},{2,10},{4,12},{6,14},{8,0},{10,2},{12,4},{14,6},{1,9},{3,11}... | collective-permute-start | bytes 884744 | tf_op jit(solution)/shard_map/ppermute | solution.py:36
  58.4 17.2 %collective-permute-start.20 = (bf16[64,1792]{1,0:T(8,128)(2,1)S(1)}, bf16[64,1792]{1,0:T(8,128)(2,1)S(1)}, u32[]{:S(2)}, u32[]{:S(2)}) collective-permute-start(bf16[64,1792]{1,0:T(8,128)(2,1)S(1)} %get-tuple-element.109), channel_id=1, source_target_pairs={{0,4},{2,6},{4,0},{6,2},{8,12},{10,14},{12,8},{14,10},{1,5},{3,7},... | collective-permute-start | bytes 688136 | tf_op jit(solution)/shard_map/ppermute | solution.py:36
  66.2 9.7 %collective-permute-start.19 = (bf16[64,1792]{1,0:T(8,128)(2,1)S(1)}, bf16[64,1792]{1,0:T(8,128)(2,1)S(1)}, u32[]{:S(2)}, u32[]{:S(2)}) collective-permute-start(bf16[64,1792]{1,0:T(8,128)(2,1)S(1)} %get-tuple-element.107), channel_id=1, source_target_pairs={{0,2},{2,0},{4,6},{6,4},{8,10},{10,8},{12,14},{14,12},{1,3},{3,1},... | collective-permute-start | bytes 688136 | tf_op jit(solution)/shard_map/ppermute | solution.py:36
  66.8 9.1 %collective-permute-start.21 = (bf16[64,1792]{1,0:T(8,128)(2,1)S(1)}, bf16[64,1792]{1,0:T(8,128)(2,1)S(1)}, u32[]{:S(2)}, u32[]{:S(2)}) collective-permute-start(bf16[64,1792]{1,0:T(8,128)(2,1)S(1)} %get-tuple-element.111), channel_id=1, source_target_pairs={{0,6},{2,4},{4,2},{6,0},{8,14},{10,12},{12,10},{14,8},{1,7},{3,5},... | collective-permute-start | bytes 688136 | tf_op jit(solution)/shard_map/ppermute | solution.py:36
  70.5 4.0 %collective-permute-start.18 = (f32[16,896]{1,0:T(8,128)S(1)}, f32[16,896]{1,0:T(8,128)S(1)}, u32[]{:S(2)}, u32[]{:S(2)}) collective-permute-start(f32[16,896]{1,0:T(8,128)S(1)} %get-tuple-element.99.mine_ref), channel_id=1, source_target_pairs={{0,1},{1,0},{2,3},{3,2},{4,5},{5,4},{6,7},{7,6},{8,9},{9,8},{10,11... | collective-permute-start | bytes 172040 | tf_op jit(solution)/shard_map/ppermute | solution.py:32
  76.8 19.9 %collective-permute-start.25 = (bf16[64,1792]{1,0:T(8,128)(2,1)S(1)}, bf16[64,1792]{1,0:T(8,128)(2,1)S(1)}, u32[]{:S(2)}, u32[]{:S(2)}) collective-permute-start(bf16[64,1792]{1,0:T(8,128)(2,1)S(1)} %get-tuple-element.112), channel_id=1, source_target_pairs={{0,8},{2,10},{4,12},{6,14},{8,0},{10,2},{12,4},{14,6},{1,9},{3,11}... | collective-permute-start | bytes 688136 | tf_op jit(solution)/shard_map/ppermute | solution.py:36
  79.0 7.4 %collective-permute-start.22 = (bf16[64,512]{1,0:T(8,128)(2,1)S(1)}, bf16[64,512]{1,0:T(8,128)(2,1)S(1)}, u32[]{:S(2)}, u32[]{:S(2)}) collective-permute-start(bf16[64,512]{1,0:T(8,128)(2,1)S(1)} %get-tuple-element.115), channel_id=1, source_target_pairs={{0,2},{2,0},{4,6},{6,4},{8,10},{10,8},{12,14},{14,12},{1,3},{3,1},... | collective-permute-start | bytes 196616 | tf_op jit(solution)/shard_map/ppermute | solution.py:36
  80.4 5.9 %collective-permute-start.23 = (bf16[64,512]{1,0:T(8,128)(2,1)S(1)}, bf16[64,512]{1,0:T(8,128)(2,1)S(1)}, u32[]{:S(2)}, u32[]{:S(2)}) collective-permute-start(bf16[64,512]{1,0:T(8,128)(2,1)S(1)} %get-tuple-element.116), channel_id=1, source_target_pairs={{0,4},{2,6},{4,0},{6,2},{8,12},{10,14},{12,8},{14,10},{1,5},{3,7},... | collective-permute-start | bytes 196616 | tf_op jit(solution)/shard_map/ppermute | solution.py:36
  82.0 8.6 %collective-permute-start.24 = (bf16[64,512]{1,0:T(8,128)(2,1)S(1)}, bf16[64,512]{1,0:T(8,128)(2,1)S(1)}, u32[]{:S(2)}, u32[]{:S(2)}) collective-permute-start(bf16[64,512]{1,0:T(8,128)(2,1)S(1)} %get-tuple-element.117), channel_id=1, source_target_pairs={{0,6},{2,4},{4,2},{6,0},{8,14},{10,12},{12,10},{14,8},{1,7},{3,5},... | collective-permute-start | bytes 196616 | tf_op jit(solution)/shard_map/ppermute | solution.py:36
  91.5 5.2 %collective-permute-start.26 = (bf16[64,512]{1,0:T(8,128)(2,1)S(1)}, bf16[64,512]{1,0:T(8,128)(2,1)S(1)}, u32[]{:S(2)}, u32[]{:S(2)}) collective-permute-start(bf16[64,512]{1,0:T(8,128)(2,1)S(1)} %get-tuple-element.118), channel_id=1, source_target_pairs={{0,8},{2,10},{4,12},{6,14},{8,0},{10,2},{12,4},{14,6},{1,9},{3,11}... | collective-permute-start | bytes 196616 | tf_op jit(solution)/shard_map/ppermute | solution.py:36
